TPU v7x, 32 devices: a whole 2x2x4 slice. The times are simulated.
32 devices in a mesh: groups: 1, subtree: 32 (over z, y, x, core).
Axes of the slice: x: 2, y: 2, z: 4, core: 2. Of those that a mesh axis runs over, the one named last changes fastest.
Arguments:
- composition: bfloat16 [196608, 128], P(('groups', 'subtree')), may hold values from -6 to 6
- leaf_basis: bfloat16 [384, 64, 512], P('subtree'), may hold values from -0.25 to 0.25
- transfer: bfloat16 [384, 64, 64], P('subtree'), may hold values from -0.21875 to 0.21875
- coupling: bfloat16 [384, 16, 64, 64], P('subtree'), may hold values from -0.375 to 0.375
- top_coupling: bfloat16 [32, 32, 64, 64], P('subtree'), may hold values from -0.75 to 0.75
- admissible_owner: int32 [384, 16], P(('groups', 'subtree')), may hold values from 0 to 31, all different within a row; in each aligned block of 12 rows (0 to 11, 12 to 23, ...) at most 12 rows name the same one
- admissible_leaf: int32 [384, 16], P(('groups', 'subtree')), may hold values from 0 to 11
- near_list: int32 [384, 2], P(('groups', 'subtree')), may hold values 0 or 1
- leaf_order: int32 [384, 512], P(('groups', 'subtree')), may hold values from 0 to 511, each once within a row
Outputs:
- potential: bfloat16 [196608, 128], P(('groups', 'subtree'))
Inputs may be any that keep to these rules, and one draw needn't show every extreme that they name: `admissible_owner`: each row names 16 different owners; among the rows of one device no owner is named more than 12 times, a bound that some block reaches. `leaf_order`: each row holds every number of 0 to 511 once.
All inputs are finite; a program needn't handle non-finite values. No bound on the sum of `near_list` on one device may be relied on, other than what follows from the above.
Results may differ from a plain program's by a relative error of at most 0.0053.
Values may be sent and summed in bfloat16 or wider, within the bound.
No kernel may reach another device: no remote copies, remote signals or barrier semaphores. Data moves between devices by JAX's collectives and lax.ppermute only.
A program may use at most 128 MiB of HBM per device.

v0:
```python
import jax
import jax.numpy as jnp
from jax import lax
from jax.sharding import PartitionSpec as P

COULOMB_SCALE = 0.15
SOFTENING = 0.25


def padded_2(block, sides, width):
    for axis, dim in sides:
        count = lax.axis_size(axis)
        forward = [(i, i + 1) for i in range(count - 1)]
        backward = [(target, source) for source, target in forward]
        low = lax.ppermute(
            lax.slice_in_dim(block, block.shape[dim] - width, None, axis=dim), axis, forward
        )
        high = lax.ppermute(lax.slice_in_dim(block, 0, width, axis=dim), axis, backward)
        block = jnp.concatenate([low, block, high], axis=dim)
    return block


def near_tables(leaf_len):
    cells = jnp.arange(leaf_len)
    along = (cells // 64).astype(jnp.float32)
    across = (cells // 8 % 8).astype(jnp.float32)
    height = (cells % 8).astype(jnp.float32)
    extent = leaf_len // 64
    tables = []
    for offset in (-1, 0, 1):
        delta_x = along[:, None] - along[None, :] - float(offset * extent)
        delta_y = across[:, None] - across[None, :]
        delta_z = height[:, None] - height[None, :]
        square = delta_x * delta_x + delta_y * delta_y + delta_z * delta_z
        tables.append((COULOMB_SCALE / jnp.sqrt(square + SOFTENING)).astype(jnp.bfloat16))
    return jnp.stack(tables)


def on_device(
    composition,
    leaf_basis,
    transfer,
    coupling,
    top_coupling,
    admissible_owner,
    admissible_leaf,
    near_list,
    leaf_order,
):
    highest = lax.Precision.HIGHEST
    leaf_dev = leaf_basis.shape[0]
    rank_dim = leaf_basis.shape[1]
    leaf_len = leaf_basis.shape[2]
    fields = composition.shape[1]
    adm_count = coupling.shape[1]
    my_index = lax.axis_index("subtree")
    on_grid = composition.reshape(leaf_dev, leaf_len, fields)
    leaf_hot = (
        leaf_order[:, :, None] == jnp.arange(leaf_len, dtype=jnp.int32)[None, None, :]
    ).astype(jnp.bfloat16)
    ordered = jnp.einsum(
        "lij,ljv->liv", leaf_hot, on_grid, preferred_element_type=jnp.float32
    ).astype(jnp.bfloat16)
    skeleton = jnp.einsum(
        "lrc,lcv->lrv", leaf_basis, ordered, preferred_element_type=jnp.float32
    ).astype(jnp.bfloat16)
    root_part = jnp.einsum(
        "lab,lbv->av", transfer, skeleton, preferred_element_type=jnp.float32
    ).astype(jnp.bfloat16)
    segment = lax.all_gather(root_part[None], "subtree", axis=0, tiled=True)
    rows_here = segment.shape[0]
    blocks = top_coupling[0]
    sources = jnp.arange(rows_here, dtype=jnp.int32)
    distant = jnp.abs(sources - my_index) >= 2
    blocks = jnp.where(distant[:, None, None], blocks, jnp.zeros_like(blocks))
    root_local = jnp.einsum("jab,jbv->av", blocks, segment, preferred_element_type=jnp.float32)
    flat_owner = admissible_owner.reshape(-1)
    flat_leaf = admissible_leaf.reshape(-1)
    wanted = flat_owner * leaf_dev + flat_leaf
    every_skeleton = lax.all_gather(skeleton, "subtree", axis=0, tiled=True)
    chosen = every_skeleton[wanted].reshape(leaf_dev, adm_count, rank_dim, fields)
    far_part = jnp.einsum("lkab,lkbv->lav", coupling, chosen, preferred_element_type=jnp.float32)
    far_part = far_part + jnp.einsum(
        "lba,bv->lav", transfer.astype(jnp.float32), root_local, precision=highest
    )
    leaf_local = far_part.astype(jnp.bfloat16)
    padded = padded_2(ordered.reshape(leaf_dev * leaf_len, fields), (("subtree", 0),), leaf_len)
    padded = padded.reshape(leaf_dev + 2, leaf_len, fields)
    tables = near_tables(leaf_len)
    masks = near_list.astype(jnp.float32)
    near = jnp.einsum("ij,ljv->liv", tables[1], ordered, preferred_element_type=jnp.float32)
    near = near + masks[:, 0][:, None, None] * jnp.einsum(
        "ij,ljv->liv", tables[0], padded[:-2], preferred_element_type=jnp.float32
    )
    near = near + masks[:, 1][:, None, None] * jnp.einsum(
        "ij,ljv->liv", tables[2], padded[2:], preferred_element_type=jnp.float32
    )
    field = near + jnp.einsum(
        "lrc,lrv->lcv", leaf_basis, leaf_local, preferred_element_type=jnp.float32
    )
    rounded = field.astype(jnp.bfloat16)
    placed = jnp.einsum("lij,liv->ljv", leaf_hot, rounded, preferred_element_type=jnp.float32)
    return placed.astype(jnp.bfloat16).reshape(leaf_dev * leaf_len, fields)


def solution(mesh):
    placed = (
        P(("groups", "subtree"), None),
        P("subtree", None, None),
        P("subtree", None, None),
        P("subtree", None, None, None),
        P("subtree", None, None, None),
        P(("groups", "subtree"), None),
        P(("groups", "subtree"), None),
        P(("groups", "subtree"), None),
        P(("groups", "subtree"), None),
    )
    return jax.shard_map(
        on_device,
        mesh=mesh,
        in_specs=placed,
        out_specs=P(("groups", "subtree"), None),
        check_vma=False,
    )
```

profile of v0, /device:TPU:0, one launch (start us, length us, event | category | flops | bytes accessed | tf_op | source)
XLA Modules:
  0.0 116.8 jit_solution(7760283460423925961)
XLA Ops:
  6.5 5.1 %fusion.4 = bf16[12,512,128]{2,1,0:T(8,128)(2,1)S(1)} fusion(bf16[12,512,128]{2,1,0:T(8,128)(2,1)} %bitcast.72, s32[12,512]{1,0:T(8,128)} %param.17), kind=kOutput, calls=%fused_computation.10 | convolution fusion | flops 809238528 | bytes 3170304 | tf_op jit(solution)/shard_map/lij,ljv->liv/dot_general | solution.py:61
  11.6 0.0 copy-start.1
  11.6 1.1 copy-done.1
  12.8 0.0 copy-start.5
  12.8 1.1 fusion.8
  13.9 0.0 all-gather.3.cloned.1.call-update
  13.9 1.7 %slice_bitcast_fusion = (bf16[512,128]{1,0:T(8,128)(2,1)}, bf16[512,128]{1,0:T(8,128)(2,1)}) fusion(bf16[12,512,128]{2,1,0:T(8,128)(2,1)} %copy-done.1), kind=kLoop, calls=%fused_computation.80 | loop fusion | bytes 524288 | tf_op jit(solution)/shard_map/slice | solution.py:18
  15.6 1.3 %collective-permute-start.1 = (bf16[512,128]{1,0:T(8,128)(2,1)}, bf16[512,128]{1,0:T(8,128)(2,1)S(1)}, u32[]{:S(2)}, u32[]{:S(2)}) collective-permute-start(bf16[512,128]{1,0:T(8,128)(2,1)} %get-tuple-element.7), channel_id=1, source_target_pairs={{1,0},{2,1},{3,2},{4,3},{5,4},{6,5},{7,6},{8,7},{9,8},{10,9},{11,1... | collective-permute-start | bytes 393224 | tf_op jit(solution)/shard_map/ppermute | solution.py:18
  16.9 3.7 %collective-permute-start = (bf16[512,128]{1,0:T(8,128)(2,1)}, bf16[512,128]{1,0:T(8,128)(2,1)}, u32[]{:S(2)}, u32[]{:S(2)}) collective-permute-start(bf16[512,128]{1,0:T(8,128)(2,1)} %get-tuple-element.8), channel_id=1, source_target_pairs={{0,1},{1,2},{2,3},{3,4},{4,5},{5,6},{6,7},{7,8},{8,9},{9,10},{10,1... | collective-permute-start | bytes 393224 | tf_op jit(solution)/shard_map/ppermute | solution.py:15
  20.6 0.1 add.138
  20.7 1.1 fusion.10
  21.9 44.8 %all-gather = bf16[2048,128]{1,0:T(8,128)(2,1)S(1)} all-gather(bf16[64,128]{1,0:T(8,128)(2,1)S(1)} %fusion.10), channel_id=2, replica_groups=mesh['groups'=1,'subtree'=32] {'subtree'}, dimensions={0}, use_global_device_ids=true | all-gather | bytes 540672 | tf_op jit(solution)/shard_map/all_gather | solution.py:70
  66.7 1.4 %fusion.40 = f32[64,128,1]{1,0,2:T(8,128)S(1)} fusion(bf16[32,64,128]{2,1,0:T(8,128)(2,1)S(1)} %bitcast.70, bf16[1,32,64,64]{3,2,1,0:T(8,128)(2,1)} %param.13, pred[32]{0:T(512)(128)(4,1)S(1)} %abs_compare_fusion), kind=kOutput, calls=%fused_computation.51 | convolution fusion | flops 33685504 | bytes 819232 | tf_op jit(solution)/shard_map/jab,jbv->av/dot_general | solution.py:76
  68.1 0.0 copy-start.2
  68.1 4.6 %fusion.38 = f32[12,128,512]{2,1,0:T(8,128)} fusion(bf16[12,512,128]{2,1,0:T(8,128)(2,1)} %copy-done.1, f32[512]{0:T(512)S(1)} %fusion.83, f32[512]{0:T(512)S(1)} %get-tuple-element.12, f32[512]{0:T(512)S(1)} %get-tuple-element.11), kind=kOutput, calls=%fused_computation.49 | convolution fusion | flops 808189952 | bytes 4724736 | tf_op jit(solution)/shard_map/ij,ljv->liv/dot_general | solution.py:91
  72.8 2.3 %pad_maximum_fusion = (bf16[6144,128]{1,0:T(8,128)(2,1)}, bf16[6144,128]{1,0:T(8,128)(2,1)S(1)}) fusion(bf16[512,128]{1,0:T(8,128)(2,1)S(1)} %collective-permute-done.1, bf16[6144,128]{1,0:T(8,128)(2,1)S(1)} %bitcast.66, bf16[512,128]{1,0:T(8,128)(2,1)} %collective-permute-done), kind=kLoop, calls=%fused_computation.12 | loop fusion | flops 6291456 | bytes 4980736 | tf_op jit(solution)/shard_map/concatenate | solution.py:19
  75.1 3.1 %fusion.35 = f32[12,128,512]{2,1,0:T(8,128)} fusion(bf16[12,512,128]{2,1,0:T(8,128)(2,1)S(1)} %bitcast.69, f32[512]{0:T(512)S(1)} %fusion.83, f32[512]{0:T(512)S(1)} %get-tuple-element.12, f32[512]{0:T(512)S(1)} %get-tuple-element.11), kind=kOutput, calls=%fused_computation.47 | convolution fusion | flops 808452096 | bytes 4724736 | tf_op jit(solution)/shard_map/ij,ljv->liv/dot_general | solution.py:92
  78.1 10.3 %all-gather.3.cloned.1.call-done = bf16[384,64,128]{2,1,0:T(8,128)(2,1)} async-done(((bf16[12,64,128]{2,1,0:T(8,128)(2,1)}), bf16[384,64,128]{2,1,0:T(8,128)(2,1)}) %all-gather.3.cloned.1.call-update) | async-done | bytes 6291472 | tf_op jit(solution)/shard_map/all_gather | solution.py:80
  88.4 5.5 %gather_fusion = bf16[192,64,128]{2,1,0:T(8,128)(2,1)} fusion(bf16[384,64,128]{2,1,0:T(8,128)(2,1)} %all-gather.3.cloned.1.call-done, s32[1024]{0:T(1024)S(1)} %pad_clamp_fusion), kind=kCustom, calls=%fused_computation | custom fusion | bytes 6292224 | tf_op jit(solution)/shard_map/gather | solution.py:81
  93.9 3.9 %convolution_bitcast_fusion = f32[12,64,128]{1,2,0:T(8,128)S(1)} fusion(bf16[12,16,64,128]{3,2,1,0:T(8,128)(2,1)} %bitcast.67, bf16[12,16,64,64]{3,2,1,0:T(8,128)(2,1)S(1)} %copy-done), kind=kOutput, calls=%fused_computation.14 | convolution fusion | flops 201326592 | bytes 5111808 | tf_op jit(solution)/shard_map/lkab,lkbv->lav/dot_general | solution.py:82
  97.8 0.0 copy-start.9
  97.8 0.5 fusion.7
  98.4 2.2 %fusion.100 = f32[12,128,512]{2,1,0:T(8,128)} fusion(bf16[12,64,128]{1,2,0:T(8,128)(2,1)S(1)} %fusion.7, bf16[12,64,512]{2,1,0:T(8,128)(2,1)S(1)} %copy-done.4), kind=kOutput, calls=%fused_computation.118 | convolution fusion | flops 100663296 | bytes 4128768 | tf_op jit(solution)/shard_map/lrc,lrv->lcv/dot_general | solution.py:98
  100.6 9.4 %fusion.5 = bf16[12,512,128]{2,1,0:T(8,128)(2,1)} fusion(s32[12,512]{1,0:T(8,128)S(1)} %copy-done.9, f32[12,128,512]{2,1,0:T(8,128)} %fusion.100, f32[12,128,512]{2,1,0:T(8,128)} %fusion.38, f32[12,128,512]{2,1,0:T(8,128)} %fusion.35, bf16[12,512,128]{2,1,0:T(8,128)(2,1)} %bitcast.68, f32[12]{0:T(128)S(1)} %get-tuple-element.10, ...), kind=kOutput, calls=%fused_computation.11 | convolution fusion | flops 1622409216 | bytes 12613728 | tf_op jit(solution)/shard_map/lij,liv->ljv/dot_general | solution.py:102
  (26 shorter events, 0.1 us)
Async XLA Ops:
  6.5 87.3 %copy-start = (bf16[12,16,64,64]{3,2,1,0:T(8,128)(2,1)S(1)}, bf16[12,16,64,64]{3,2,1,0:T(8,128)(2,1)}, u32[]{:S(2)}) copy-start(bf16[12,16,64,64]{3,2,1,0:T(8,128)(2,1)} %param.12) | copy-start | bytes 4718596
  6.5 81.8 %all-gather.3.cloned.1.call-start = ((), (), s32[]{:S(2)}) async-start(), calls=%async_computation | async-start | bytes 6488064 | tf_op jit(solution)/shard_map/all_gather | solution.py:80
  6.5 6.2 %copy-start.3 = (bf16[12,64,512]{2,1,0:T(8,128)(2,1)S(1)}, bf16[12,64,512]{2,1,0:T(8,128)(2,1)}, u32[]{:S(2)}) copy-start(bf16[12,64,512]{2,1,0:T(8,128)(2,1)} %param.10) | copy-start | bytes 2359300
  11.6 1.1 copy-start.1
  12.8 7.8 %copy-start.8 = (s32[12,2]{0,1:T(2,128)S(1)}, s32[12,2]{0,1:T(2,128)}, u32[]{:S(2)}) copy-start(s32[12,2]{0,1:T(2,128)} %param.16) | copy-start | bytes 292
  12.8 7.8 %copy-start.6 = (s32[12,16]{1,0:T(8,128)S(1)}, s32[12,16]{1,0:T(8,128)}, u32[]{:S(2)}) copy-start(s32[12,16]{1,0:T(8,128)} %param.15) | copy-start | bytes 2308
  12.8 7.8 %copy-start.7 = (s32[12,16]{1,0:T(8,128)S(1)}, s32[12,16]{1,0:T(8,128)}, u32[]{:S(2)}) copy-start(s32[12,16]{1,0:T(8,128)} %param.14) | copy-start | bytes 2308
  12.8 8.0 %copy-start.5 = (bf16[12,64,64]{2,1,0:T(8,128)(2,1)S(1)}, bf16[12,64,64]{2,1,0:T(8,128)(2,1)}, u32[]{:S(2)}) copy-start(bf16[12,64,64]{2,1,0:T(8,128)(2,1)} %param.11) | copy-start | bytes 294916
  15.6 57.2 %collective-permute-start.1 = (bf16[512,128]{1,0:T(8,128)(2,1)}, bf16[512,128]{1,0:T(8,128)(2,1)S(1)}, u32[]{:S(2)}, u32[]{:S(2)}) collective-permute-start(bf16[512,128]{1,0:T(8,128)(2,1)} %get-tuple-element.7), channel_id=1, source_target_pairs={{1,0},{2,1},{3,2},{4,3},{5,4},{6,5},{7,6},{8,7},{9,8},{10,9},{11,1... | collective-permute-start | bytes 393224 | tf_op jit(solution)/shard_map/ppermute | solution.py:18
  16.9 55.9 %collective-permute-start = (bf16[512,128]{1,0:T(8,128)(2,1)}, bf16[512,128]{1,0:T(8,128)(2,1)}, u32[]{:S(2)}, u32[]{:S(2)}) collective-permute-start(bf16[512,128]{1,0:T(8,128)(2,1)} %get-tuple-element.8), channel_id=1, source_target_pairs={{0,1},{1,2},{2,3},{3,4},{4,5},{5,6},{6,7},{7,8},{8,9},{9,10},{10,1... | collective-permute-start | bytes 393224 | tf_op jit(solution)/shard_map/ppermute | solution.py:15
  68.1 4.7 %copy-start.2 = (bf16[12,512,128]{2,1,0:T(8,128)(2,1)S(1)}, bf16[12,512,128]{2,1,0:T(8,128)(2,1)}, u32[]{:S(2)}) copy-start(bf16[12,512,128]{2,1,0:T(8,128)(2,1)} %copy-done.1) | copy-start | bytes 4718596
  93.9 4.5 %copy-start.4 = (bf16[12,64,512]{2,1,0:T(8,128)(2,1)S(1)}, bf16[12,64,512]{2,1,0:T(8,128)(2,1)}, u32[]{:S(2)}) copy-start(bf16[12,64,512]{2,1,0:T(8,128)(2,1)} %param.10) | copy-start | bytes 2359300
  97.8 2.8 %copy-start.9 = (s32[12,512]{1,0:T(8,128)S(1)}, s32[12,512]{1,0:T(8,128)}, u32[]{:S(2)}) copy-start(s32[12,512]{1,0:T(8,128)} %param.17) | copy-start | bytes 73732
Sparse Core Ops, SparseCore 0:
  14.0 74.3 all-gather.2
where the time goes:
time: 117 us
  blocking collectives  44.8 us (38%)
  matrix products  32.4 us (28%)
  between operations  13.5 us (12%)
  waiting for transfers between devices  10.3 us (9%)
  local copies, waits for them, and re-layouts  8.45 us (7%)
  starting transfers between devices  4.98 us (4%)
  other arithmetic  2.29 us (2%)
    all_gather x1, blocking collectives, on_device(): segment = lax.all_gather(root_part[None], 'subtree', axis=0, tiled=True)  44.8 us
    all_gather x1, waiting for transfers between devices, on_device(): every_skeleton = lax.all_gather(skeleton, 'subtree', axis=0, tiled=True)  10.3 us
    dot_general x1, matrix products, on_device(): jnp.einsum('lij,liv->ljv', leaf_hot, rounded, preferred_element_type=jnp....  9.39 us
    gather x1, local copies, waits for them, and re-layouts, on_device(): every_skeleton[wanted].reshape(leaf_dev, adm_count, rank_dim, fields)  5.49 us
    dot_general x1, matrix products, on_device(): jnp.einsum('lij,ljv->liv', leaf_hot, on_grid, preferred_element_type=jnp....  5.06 us
    dot_general x1, matrix products, on_device(): jnp.einsum('ij,ljv->liv', tables[1], ordered, preferred_element_type=jnp....  4.62 us
    dot_general x1, matrix products, on_device(): jnp.einsum('lkab,lkbv->lav', coupling, chosen, preferred_element_type=jnp...  3.92 us
    ppermute x1, starting transfers between devices, padded_2(): lax.ppermute(lax.slice_in_dim(block, block.shape[dim] - width, None, axis...  3.7 us
  transfers between devices with their start and end apart: 3, of which 1 were waited for; matrix products, arithmetic and copies ran while one was open for 12% of the time, Pallas kernels for 0%

commit v1 on v0

--- a/solution.py
+++ b/solution.py
@@ -5,19 +5,6 @@
 
 COULOMB_SCALE = 0.15
 SOFTENING = 0.25
-
-
-def padded_2(block, sides, width):
-    for axis, dim in sides:
-        count = lax.axis_size(axis)
-        forward = [(i, i + 1) for i in range(count - 1)]
-        backward = [(target, source) for source, target in forward]
-        low = lax.ppermute(
-            lax.slice_in_dim(block, block.shape[dim] - width, None, axis=dim), axis, forward
-        )
-        high = lax.ppermute(lax.slice_in_dim(block, 0, width, axis=dim), axis, backward)
-        block = jnp.concatenate([low, block, high], axis=dim)
-    return block
 
 
 def near_tables(leaf_len):
@@ -34,6 +21,37 @@
         square = delta_x * delta_x + delta_y * delta_y + delta_z * delta_z
         tables.append((COULOMB_SCALE / jnp.sqrt(square + SOFTENING)).astype(jnp.bfloat16))
     return jnp.stack(tables)
+
+
+def ring_order(layers):
+    return [0] + list(range(1, layers, 2)) + list(range(layers - 2, 0, -2))
+
+
+def send(block, target):
+    count = lax.axis_size("subtree")
+    return lax.ppermute(block, "subtree", [(d, target(d)) for d in range(count)])
+
+
+def plane_gather(mine):
+    half = mine.shape[0] // 2
+    from_x = send(mine, lambda d: d ^ 2)
+    from_y = send(mine, lambda d: d ^ 4)
+    low = send(from_y[:half], lambda d: d ^ 2)
+    high = send(from_x[half:], lambda d: d ^ 4)
+    return [mine, from_x, from_y, jnp.concatenate([low, high], axis=0)]
+
+
+def line_gather(mine, layers):
+    order = ring_order(layers)
+    following = {order[i]: order[(i + 1) % layers] for i in range(layers)}
+    parts = [mine]
+    for _ in range(layers - 1):
+        parts.append(send(parts[-1], lambda d: following[d // 8] * 8 + d % 8))
+    return parts
+
+
+def both_cores(parts):
+    return parts + [send(part, lambda d: d ^ 1) for part in parts]
 
 
 def on_device(
@@ -53,6 +71,8 @@
     leaf_len = leaf_basis.shape[2]
     fields = composition.shape[1]
     adm_count = coupling.shape[1]
+    count = lax.axis_size("subtree")
+    layers = count // 8
     my_index = lax.axis_index("subtree")
     on_grid = composition.reshape(leaf_dev, leaf_len, fields)
     leaf_hot = (
@@ -67,25 +87,47 @@
     root_part = jnp.einsum(
         "lab,lbv->av", transfer, skeleton, preferred_element_type=jnp.float32
     ).astype(jnp.bfloat16)
-    segment = lax.all_gather(root_part[None], "subtree", axis=0, tiled=True)
-    rows_here = segment.shape[0]
+
+    shared = jnp.concatenate([root_part[None], skeleton], axis=0)
+    first = leaf_dev // 3
+    second = leaf_dev + 1 - first
+    plane = plane_gather(shared[:first])
+    line = line_gather(jnp.concatenate(plane, axis=0), layers)
+    tall = line_gather(shared[first:], layers)
+    wide = plane_gather(jnp.concatenate(tall, axis=0))
+    low_blocks = jnp.concatenate(both_cores(line), axis=0)
+    high_blocks = jnp.concatenate(both_cores(wide), axis=0)
+    every = jnp.concatenate([low_blocks, high_blocks], axis=0)
+
+    order = ring_order(layers)
+    position = jnp.zeros((layers,), jnp.int32).at[jnp.array(order)].set(
+        jnp.arange(layers, dtype=jnp.int32)
+    )
+
+    def place_of(owner, block):
+        layer = (position[my_index // 8] - position[owner // 8]) % layers
+        chip = (owner // 2 % 4) ^ (my_index // 2 % 4)
+        core = (owner % 2) ^ (my_index % 2)
+        low = ((core * layers + layer) * 4 + chip) * first + block
+        high = count * first + ((core * 4 + chip) * layers + layer) * second + block - first
+        return jnp.where(block < first, low, high)
+
+    sources = jnp.arange(count, dtype=jnp.int32)
+    segment = every[place_of(sources, jnp.zeros_like(sources))]
     blocks = top_coupling[0]
-    sources = jnp.arange(rows_here, dtype=jnp.int32)
     distant = jnp.abs(sources - my_index) >= 2
     blocks = jnp.where(distant[:, None, None], blocks, jnp.zeros_like(blocks))
     root_local = jnp.einsum("jab,jbv->av", blocks, segment, preferred_element_type=jnp.float32)
-    flat_owner = admissible_owner.reshape(-1)
-    flat_leaf = admissible_leaf.reshape(-1)
-    wanted = flat_owner * leaf_dev + flat_leaf
-    every_skeleton = lax.all_gather(skeleton, "subtree", axis=0, tiled=True)
-    chosen = every_skeleton[wanted].reshape(leaf_dev, adm_count, rank_dim, fields)
+    wanted = place_of(admissible_owner.reshape(-1), admissible_leaf.reshape(-1) + 1)
+    chosen = every[wanted].reshape(leaf_dev, adm_count, rank_dim, fields)
     far_part = jnp.einsum("lkab,lkbv->lav", coupling, chosen, preferred_element_type=jnp.float32)
     far_part = far_part + jnp.einsum(
         "lba,bv->lav", transfer.astype(jnp.float32), root_local, precision=highest
     )
     leaf_local = far_part.astype(jnp.bfloat16)
-    padded = padded_2(ordered.reshape(leaf_dev * leaf_len, fields), (("subtree", 0),), leaf_len)
-    padded = padded.reshape(leaf_dev + 2, leaf_len, fields)
+    before = lax.ppermute(ordered[-1:], "subtree", [(d, d + 1) for d in range(count - 1)])
+    after = lax.ppermute(ordered[:1], "subtree", [(d + 1, d) for d in range(count - 1)])
+    padded = jnp.concatenate([before, ordered, after], axis=0)
     tables = near_tables(leaf_len)
     masks = near_list.astype(jnp.float32)
     near = jnp.einsum("ij,ljv->liv", tables[1], ordered, preferred_element_type=jnp.float32)

time: 117 us -> 126 us (1.077)
  blocking collectives: 44.8 us -> 0 us
  local copies, waits for them, and re-layouts: 8.45 us -> 33.3 us
  starting transfers between devices: 4.98 us -> 26 us
  waiting for transfers between devices: 10.3 us -> 31.1 us
  between operations: 13.5 us -> 0.25 us
    all_gather x1 -> x0, blocking collectives: 44.8 us -> none  [on_device(): segment = lax.all_gather(root_part[None], 'subtree', axis=0, tiled=True)]
    ppermute x2 -> x24, waiting for transfers between devices: 0.01 us -> 31.1 us  [the longest x22 31.1 us: send(): lax.ppermute(block, 'subtree', [(d, target(d)) for d in range(count)])]
    ppermute x2 -> x24, starting transfers between devices: 4.98 us -> 26 us  [the longest x22 22.7 us: send(): lax.ppermute(block, 'subtree', [(d, target(d)) for d in range(count)])]
    unnamed x20 -> x51, local copies, waits for them, and re-layouts: 1.18 us -> 18.4 us
    all_gather x1 -> x0, waiting for transfers between devices: 10.3 us -> none  [on_device(): every_skeleton = lax.all_gather(skeleton, 'subtree', axis=0, tiled=True)]
    gather x1 -> x2, local copies, waits for them, and re-layouts: 5.49 us -> 9.95 us  [the longest x1 5.61 us: on_device(): chosen = every[wanted].reshape(leaf_dev, adm_count, rank_dim, fields)]
    dot_general x1, matrix products: 2.2 us -> 6.24 us  [on_device(): jnp.einsum('lrc,lrv->lcv', leaf_basis, leaf_local, preferred_element_type...]
    dot_general x1 -> x0, matrix products: 3.92 us -> none  [on_device(): jnp.einsum('lkab,lkbv->lav', coupling, chosen, preferred_element_type=jnp...]
  transfers between devices with their start and end apart: 3 -> 24, of which waited for: 1 -> 11; matrix products, arithmetic and copies ran while one was open for 12% -> 42% of each run, Pallas kernels for 0% -> 0%
where the time goes in v1:
time: 126 us; the launch traced here: 125 us
  local copies, waits for them, and re-layouts  33.3 us (26%)
  matrix products  32 us (25%)
  waiting for transfers between devices  31.1 us (25%)
  starting transfers between devices  26 us (21%)
  other arithmetic  2.73 us (2%)
    ppermute x22, waiting for transfers between devices, send(): lax.ppermute(block, 'subtree', [(d, target(d)) for d in range(count)])  31.1 us
    ppermute x22, starting transfers between devices, send(): lax.ppermute(block, 'subtree', [(d, target(d)) for d in range(count)])  22.7 us
    unnamed x51, local copies, waits for them, and re-layouts  18.4 us
    dot_general x1, matrix products, on_device(): jnp.einsum('lij,liv->ljv', leaf_hot, rounded, preferred_element_type=jnp....  9.41 us
    dot_general x1, matrix products, on_device(): jnp.einsum('lrc,lrv->lcv', leaf_basis, leaf_local, preferred_element_type...  6.24 us
    gather x1, local copies, waits for them, and re-layouts, on_device(): chosen = every[wanted].reshape(leaf_dev, adm_count, rank_dim, fields)  5.61 us
    dot_general x1, matrix products, on_device(): jnp.einsum('lij,ljv->liv', leaf_hot, on_grid, preferred_element_type=jnp....  5.06 us
    dot_general x1, matrix products, on_device(): jnp.einsum('ij,ljv->liv', tables[0], padded[:-2], preferred_element_type=...  4.64 us
  transfers between devices with their start and end apart: 24, of which 11 were waited for; matrix products, arithmetic and copies ran while one was open for 42% of the time, Pallas kernels for 0%

profile of v1, /device:TPU:0, one launch (start us, length us, event | category | flops | bytes accessed | tf_op | source)
XLA Modules:
  0.0 125.4 jit_solution(16397650115785160538)
XLA Ops:
  0.0 5.1 %fusion.11 = bf16[12,512,128]{2,1,0:T(8,128)(2,1)S(1)} fusion(bf16[12,512,128]{2,1,0:T(8,128)(2,1)} %bitcast.64, s32[12,512]{1,0:T(8,128)} %param.18), kind=kOutput, calls=%fused_computation.18 | convolution fusion | flops 809238528 | bytes 3170304 | tf_op jit(solution)/shard_map/lij,ljv->liv/dot_general | solution.py:81
  5.8 3.0 %collective-permute-start.2 = (bf16[4,64,128]{2,1,0:T(8,128)(2,1)S(1)}, bf16[4,64,128]{2,1,0:T(8,128)(2,1)S(1)}, u32[]{:S(2)}, u32[]{:S(2)}) collective-permute-start(bf16[4,64,128]{2,1,0:T(8,128)(2,1)S(1)} %get-tuple-element.6), channel_id=1, source_target_pairs={{0,2},{1,3},{2,0},{3,1},{4,6},{5,7},{6,4},{7,5},{8,10},{9,11},{10,... | collective-permute-start | bytes 196616 | tf_op jit(solution)/shard_map/ppermute | solution.py:32
  11.0 2.1 %collective-permute-done.3 = bf16[4,64,128]{2,1,0:T(8,128)(2,1)S(1)} collective-permute-done((bf16[4,64,128]{2,1,0:T(8,128)(2,1)S(1)}, bf16[4,64,128]{2,1,0:T(8,128)(2,1)S(1)}, u32[]{:S(2)}, u32[]{:S(2)}) %collective-permute-start.3) | collective-permute-done | bytes 65568 | tf_op jit(solution)/shard_map/ppermute | solution.py:32
  13.2 2.0 %collective-permute-start.5 = (bf16[2,64,128]{2,1,0:T(8,128)(2,1)S(1)}, bf16[2,64,128]{2,1,0:T(8,128)(2,1)S(1)}, u32[]{:S(2)}, u32[]{:S(2)}) collective-permute-start(bf16[2,64,128]{2,1,0:T(8,128)(2,1)S(1)} %slice.67), channel_id=1, source_target_pairs={{0,4},{1,5},{2,6},{3,7},{4,0},{5,1},{6,2},{7,3},{8,12},{9,13},{10,... | collective-permute-start | bytes 98312 | tf_op jit(solution)/shard_map/ppermute | solution.py:32
  20.5 1.9 %collective-permute-start = (bf16[1,512,128]{2,1,0:T(8,128)(2,1)}, bf16[1,512,128]{2,1,0:T(8,128)(2,1)}, u32[]{:S(2)}, u32[]{:S(2)}) collective-permute-start(bf16[1,512,128]{2,1,0:T(8,128)(2,1)} %get-tuple-element.8), channel_id=1, source_target_pairs={{0,1},{1,2},{2,3},{3,4},{4,5},{5,6},{6,7},{7,8},{8,9},{9,10},{10,1... | collective-permute-start | bytes 393224 | tf_op jit(solution)/shard_map/ppermute | solution.py:128
  23.8 1.7 %collective-permute-done.6 = bf16[16,64,128]{2,1,0:T(8,128)(2,1)S(1)} collective-permute-done((bf16[16,64,128]{2,1,0:T(8,128)(2,1)S(1)}, bf16[16,64,128]{2,1,0:T(8,128)(2,1)S(1)}, u32[]{:S(2)}, u32[]{:S(2)}) %collective-permute-start.6) | collective-permute-done | bytes 262176 | tf_op jit(solution)/shard_map/ppermute | solution.py:32
  25.5 5.1 %collective-permute-start.7 = (bf16[16,64,128]{2,1,0:T(8,128)(2,1)S(1)}, bf16[16,64,128]{2,1,0:T(8,128)(2,1)}, u32[]{:S(2)}, u32[]{:S(2)}) collective-permute-start(bf16[16,64,128]{2,1,0:T(8,128)(2,1)S(1)} %collective-permute-done.6), channel_id=1, source_target_pairs={{0,8},{1,9},{2,10},{3,11},{4,12},{5,13},{6,14},{7,15},{8,24},{9,25... | collective-permute-start | bytes 786440 | tf_op jit(solution)/shard_map/ppermute | solution.py:32
  30.6 3.1 %fusion.47 = f32[12,128,512]{2,1,0:T(8,128)} fusion(bf16[12,512,128]{2,1,0:T(8,128)(2,1)S(1)} %fusion.11, f32[512]{0:T(512)S(1)} %fusion.92, f32[512]{0:T(512)S(1)} %get-tuple-element.24, f32[512]{0:T(512)S(1)} %get-tuple-element.23), kind=kOutput, calls=%fused_computation.57 | convolution fusion | flops 808189952 | bytes 4724736 | tf_op jit(solution)/shard_map/ij,ljv->liv/dot_general | solution.py:133
  33.7 3.0 %collective-permute-done.7 = bf16[16,64,128]{2,1,0:T(8,128)(2,1)} collective-permute-done((bf16[16,64,128]{2,1,0:T(8,128)(2,1)S(1)}, bf16[16,64,128]{2,1,0:T(8,128)(2,1)}, u32[]{:S(2)}, u32[]{:S(2)}) %collective-permute-start.7) | collective-permute-done | bytes 262176 | tf_op jit(solution)/shard_map/ppermute | solution.py:32
  40.5 1.7 %constant_dynamic-update-slice_fusion.23 = bf16[416,64,128]{2,1,0:T(8,128)(2,1)} fusion(bf16[416,64,128]{2,1,0:T(8,128)(2,1)} %get-tuple-element.16, bf16[16,64,128]{2,1,0:T(8,128)(2,1)} %copy-done.4), kind=kLoop, calls=%fused_computation.112 | loop fusion | bytes 524288
  42.2 1.7 %constant_dynamic-update-slice_fusion.22 = bf16[416,64,128]{2,1,0:T(8,128)(2,1)} fusion(bf16[416,64,128]{2,1,0:T(8,128)(2,1)} %constant_dynamic-update-slice_fusion.23, bf16[16,64,128]{2,1,0:T(8,128)(2,1)} %collective-permute-done.7), kind=kLoop, calls=%fused_computation.111 | loop fusion | bytes 524288
  44.4 1.7 %constant_dynamic-update-slice_fusion.21 = bf16[416,64,128]{2,1,0:T(8,128)(2,1)} fusion(bf16[416,64,128]{2,1,0:T(8,128)(2,1)} %constant_dynamic-update-slice_fusion.22, bf16[16,64,128]{2,1,0:T(8,128)(2,1)} %collective-permute-done.8), kind=kLoop, calls=%fused_computation.110 | loop fusion | bytes 524288
  52.2 4.7 %collective-permute-done.13 = bf16[9,64,128]{2,1,0:T(8,128)(2,1)S(1)} collective-permute-done((bf16[9,64,128]{2,1,0:T(8,128)(2,1)S(1)}, bf16[9,64,128]{2,1,0:T(8,128)(2,1)S(1)}, u32[]{:S(2)}, u32[]{:S(2)}) %collective-permute-start.13) | collective-permute-done | bytes 147488 | tf_op jit(solution)/shard_map/ppermute | solution.py:32
  56.9 6.0 %collective-permute-done.14 = bf16[9,64,128]{2,1,0:T(8,128)(2,1)S(1)} collective-permute-done((bf16[9,64,128]{2,1,0:T(8,128)(2,1)S(1)}, bf16[9,64,128]{2,1,0:T(8,128)(2,1)S(1)}, u32[]{:S(2)}, u32[]{:S(2)}) %collective-permute-start.14) | collective-permute-done | bytes 147488 | tf_op jit(solution)/shard_map/ppermute | solution.py:32
  63.5 5.4 %collective-permute-done.15 = bf16[9,64,128]{2,1,0:T(8,128)(2,1)S(1)} collective-permute-done((bf16[9,64,128]{2,1,0:T(8,128)(2,1)S(1)}, bf16[9,64,128]{2,1,0:T(8,128)(2,1)S(1)}, u32[]{:S(2)}, u32[]{:S(2)}) %collective-permute-start.15) | collective-permute-done | bytes 147488 | tf_op jit(solution)/shard_map/ppermute | solution.py:32
  70.1 3.5 %collective-permute-start.17 = (bf16[36,64,128]{2,1,0:T(8,128)(2,1)S(1)}, bf16[36,64,128]{2,1,0:T(8,128)(2,1)S(1)}, u32[]{:S(2)}, u32[]{:S(2)}) collective-permute-start(bf16[36,64,128]{2,1,0:T(8,128)(2,1)S(1)} %pad_maximum_fusion), channel_id=1, source_target_pairs={{0,4},{1,5},{2,6},{3,7},{4,0},{5,1},{6,2},{7,3},{8,12},{9,13},{10,... | collective-permute-start | bytes 1769480 | tf_op jit(solution)/shard_map/ppermute | solution.py:32
  73.7 4.6 %fusion.4 = f32[12,128,512]{2,1,0:T(8,128)} fusion(bf16[12,512,128]{2,1,0:T(8,128)(2,1)} %copy-done.2, bf16[1,512,128]{2,1,0:T(8,128)(2,1)} %collective-permute-done, f32[512]{0:T(512)} %copy-done.8, f32[512]{0:T(512)} %copy-done.12, f32[512]{0:T(512)} %copy-done.10), kind=kOutput, calls=%fused_computation.11 | convolution fusion | flops 811859968 | bytes 4855808 | tf_op jit(solution)/shard_map/ij,ljv->liv/dot_general | solution.py:134
  79.7 4.7 %collective-permute-done.17 = bf16[36,64,128]{2,1,0:T(8,128)(2,1)S(1)} collective-permute-done((bf16[36,64,128]{2,1,0:T(8,128)(2,1)S(1)}, bf16[36,64,128]{2,1,0:T(8,128)(2,1)S(1)}, u32[]{:S(2)}, u32[]{:S(2)}) %collective-permute-start.17) | collective-permute-done | bytes 589856 | tf_op jit(solution)/shard_map/ppermute | solution.py:32
  84.5 2.3 %collective-permute-start.19 = (bf16[18,64,128]{2,1,0:T(8,128)(2,1)S(1)}, bf16[18,64,128]{2,1,0:T(8,128)(2,1)S(1)}, u32[]{:S(2)}, u32[]{:S(2)}) collective-permute-start(bf16[18,64,128]{2,1,0:T(8,128)(2,1)S(1)} %slice.70), channel_id=1, source_target_pairs={{0,4},{1,5},{2,6},{3,7},{4,0},{5,1},{6,2},{7,3},{8,12},{9,13},{10,... | collective-permute-start | bytes 884744 | tf_op jit(solution)/shard_map/ppermute | solution.py:32
  89.2 2.0 %collective-permute-done.18 = bf16[18,64,128]{2,1,0:T(8,128)(2,1)S(1)} collective-permute-done((bf16[18,64,128]{2,1,0:T(8,128)(2,1)S(1)}, bf16[18,64,128]{2,1,0:T(8,128)(2,1)S(1)}, u32[]{:S(2)}, u32[]{:S(2)}) %collective-permute-start.18) | collective-permute-done | bytes 294944 | tf_op jit(solution)/shard_map/ppermute | solution.py:32
  96.8 4.3 %gather_fusion.1 = bf16[32,64,128]{2,1,0:T(8,128)(2,1)} fusion(bf16[416,64,128]{2,1,0:T(8,128)(2,1)} %constant_dynamic-update-slice_fusion.5, s32[1024]{0:T(1024)S(1)} %get-tuple-element.21), kind=kCustom, calls=%fused_computation.1 | custom fusion | bytes 1048704 | tf_op jit(solution)/shard_map/gather | solution.py:116
  104.1 5.6 %gather_fusion = bf16[192,64,128]{2,1,0:T(8,128)(2,1)} fusion(bf16[416,64,128]{2,1,0:T(8,128)(2,1)} %constant_dynamic-update-slice_fusion.5, s32[1024]{0:T(1024)S(1)} %get-tuple-element.22), kind=kCustom, calls=%fused_computation | custom fusion | bytes 6292224 | tf_op jit(solution)/shard_map/gather | solution.py:122
  109.7 6.2 %fusion.15 = f32[12,128,512]{2,1,0:T(8,128)} fusion(bf16[12,64,512]{2,1,0:T(8,128)(2,1)} %param.11, f32[12,64,128]{1,2,0:T(8,128)} %convolution_bitcast_fusion.1, bf16[12,16,64,128]{3,2,1,0:T(8,128)(2,1)} %bitcast.62, bf16[12,16,64,64]{3,2,1,0:T(8,128)(2,1)S(1)} %copy-done), kind=kOutput, calls=%fused_computation.24 | convolution fusion | flops 302186496 | bytes 9043968 | tf_op jit(solution)/shard_map/lrc,lrv->lcv/dot_general | solution.py:140
  116.0 9.4 %fusion.12 = bf16[12,512,128]{2,1,0:T(8,128)(2,1)} fusion(s32[12,512]{1,0:T(8,128)S(1)} %copy-done.14, f32[12,128,512]{2,1,0:T(8,128)} %fusion.15, f32[12,128,512]{2,1,0:T(8,128)} %fusion.47, f32[12,128,512]{2,1,0:T(8,128)} %fusion.4, bf16[1,512,128]{2,1,0:T(8,128)(2,1)} %collective-permute-done.1, bf16[12,512,128]{2,1,0:T(8,128)(2,1)} %copy-done.2, ...), kind=kOutput, calls=%fused_computation.19 | convolution fusion | flops 1625817088 | bytes 12744800 | tf_op jit(solution)/shard_map/lij,liv->ljv/dot_general | solution.py:144
  (109 shorter events, 34.1 us)
Async XLA Ops:
  5.8 7.4 %collective-permute-start.2 = (bf16[4,64,128]{2,1,0:T(8,128)(2,1)S(1)}, bf16[4,64,128]{2,1,0:T(8,128)(2,1)S(1)}, u32[]{:S(2)}, u32[]{:S(2)}) collective-permute-start(bf16[4,64,128]{2,1,0:T(8,128)(2,1)S(1)} %get-tuple-element.6), channel_id=1, source_target_pairs={{0,2},{1,3},{2,0},{3,1},{4,6},{5,7},{6,4},{7,5},{8,10},{9,11},{10,... | collective-permute-start | bytes 196616 | tf_op jit(solution)/shard_map/ppermute | solution.py:32
  8.8 4.3 %collective-permute-start.3 = (bf16[4,64,128]{2,1,0:T(8,128)(2,1)S(1)}, bf16[4,64,128]{2,1,0:T(8,128)(2,1)S(1)}, u32[]{:S(2)}, u32[]{:S(2)}) collective-permute-start(bf16[4,64,128]{2,1,0:T(8,128)(2,1)S(1)} %get-tuple-element.6), channel_id=1, source_target_pairs={{0,4},{1,5},{2,6},{3,7},{4,0},{5,1},{6,2},{7,3},{8,12},{9,13},{10,... | collective-permute-start | bytes 196616 | tf_op jit(solution)/shard_map/ppermute | solution.py:32
  13.1 3.9 %collective-permute-start.4 = (bf16[2,64,128]{2,1,0:T(8,128)(2,1)S(1)}, bf16[2,64,128]{2,1,0:T(8,128)(2,1)S(1)}, u32[]{:S(2)}, u32[]{:S(2)}) collective-permute-start(bf16[2,64,128]{2,1,0:T(8,128)(2,1)S(1)} %slice.66), channel_id=1, source_target_pairs={{0,2},{1,3},{2,0},{3,1},{4,6},{5,7},{6,4},{7,5},{8,10},{9,11},{10,... | collective-permute-start | bytes 98312 | tf_op jit(solution)/shard_map/ppermute | solution.py:32
  13.2 4.5 %collective-permute-start.5 = (bf16[2,64,128]{2,1,0:T(8,128)(2,1)S(1)}, bf16[2,64,128]{2,1,0:T(8,128)(2,1)S(1)}, u32[]{:S(2)}, u32[]{:S(2)}) collective-permute-start(bf16[2,64,128]{2,1,0:T(8,128)(2,1)S(1)} %slice.67), channel_id=1, source_target_pairs={{0,4},{1,5},{2,6},{3,7},{4,0},{5,1},{6,2},{7,3},{8,12},{9,13},{10,... | collective-permute-start | bytes 98312 | tf_op jit(solution)/shard_map/ppermute | solution.py:32
  18.2 7.3 %collective-permute-start.6 = (bf16[16,64,128]{2,1,0:T(8,128)(2,1)S(1)}, bf16[16,64,128]{2,1,0:T(8,128)(2,1)S(1)}, u32[]{:S(2)}, u32[]{:S(2)}) collective-permute-start(bf16[16,64,128]{2,1,0:T(8,128)(2,1)S(1)} %get-tuple-element.15), channel_id=1, source_target_pairs={{0,8},{1,9},{2,10},{3,11},{4,12},{5,13},{6,14},{7,15},{8,24},{9,25... | collective-permute-start | bytes 786440 | tf_op jit(solution)/shard_map/ppermute | solution.py:32
  20.5 53.1 %collective-permute-start = (bf16[1,512,128]{2,1,0:T(8,128)(2,1)}, bf16[1,512,128]{2,1,0:T(8,128)(2,1)}, u32[]{:S(2)}, u32[]{:S(2)}) collective-permute-start(bf16[1,512,128]{2,1,0:T(8,128)(2,1)} %get-tuple-element.8), channel_id=1, source_target_pairs={{0,1},{1,2},{2,3},{3,4},{4,5},{5,6},{6,7},{7,8},{8,9},{9,10},{10,1... | collective-permute-start | bytes 393224 | tf_op jit(solution)/shard_map/ppermute | solution.py:128
  22.5 93.5 %collective-permute-start.1 = (bf16[1,512,128]{2,1,0:T(8,128)(2,1)}, bf16[1,512,128]{2,1,0:T(8,128)(2,1)}, u32[]{:S(2)}, u32[]{:S(2)}) collective-permute-start(bf16[1,512,128]{2,1,0:T(8,128)(2,1)} %get-tuple-element.7), channel_id=1, source_target_pairs={{1,0},{2,1},{3,2},{4,3},{5,4},{6,5},{7,6},{8,7},{9,8},{10,9},{11,1... | collective-permute-start | bytes 393224 | tf_op jit(solution)/shard_map/ppermute | solution.py:129
  25.5 11.2 %collective-permute-start.7 = (bf16[16,64,128]{2,1,0:T(8,128)(2,1)S(1)}, bf16[16,64,128]{2,1,0:T(8,128)(2,1)}, u32[]{:S(2)}, u32[]{:S(2)}) collective-permute-start(bf16[16,64,128]{2,1,0:T(8,128)(2,1)S(1)} %collective-permute-done.6), channel_id=1, source_target_pairs={{0,8},{1,9},{2,10},{3,11},{4,12},{5,13},{6,14},{7,15},{8,24},{9,25... | collective-permute-start | bytes 786440 | tf_op jit(solution)/shard_map/ppermute | solution.py:32
  36.8 7.6 %collective-permute-start.8 = (bf16[16,64,128]{2,1,0:T(8,128)(2,1)}, bf16[16,64,128]{2,1,0:T(8,128)(2,1)}, u32[]{:S(2)}, u32[]{:S(2)}) collective-permute-start(bf16[16,64,128]{2,1,0:T(8,128)(2,1)} %collective-permute-done.7), channel_id=1, source_target_pairs={{0,8},{1,9},{2,10},{3,11},{4,12},{5,13},{6,14},{7,15},{8,24},{9,25... | collective-permute-start | bytes 786440 | tf_op jit(solution)/shard_map/ppermute | solution.py:32
  40.0 6.1 %collective-permute-start.9 = (bf16[16,64,128]{2,1,0:T(8,128)(2,1)}, bf16[16,64,128]{2,1,0:T(8,128)(2,1)S(1)}, u32[]{:S(2)}, u32[]{:S(2)}) collective-permute-start(bf16[16,64,128]{2,1,0:T(8,128)(2,1)} %copy-done.5), channel_id=1, source_target_pairs={{0,1},{1,0},{2,3},{3,2},{4,5},{5,4},{6,7},{7,6},{8,9},{9,8},{10,11... | collective-permute-start | bytes 786440 | tf_op jit(solution)/shard_map/ppermute | solution.py:32
  40.0 7.3 %collective-permute-start.10 = (bf16[16,64,128]{2,1,0:T(8,128)(2,1)}, bf16[16,64,128]{2,1,0:T(8,128)(2,1)S(1)}, u32[]{:S(2)}, u32[]{:S(2)}) collective-permute-start(bf16[16,64,128]{2,1,0:T(8,128)(2,1)} %copy-done.4), channel_id=1, source_target_pairs={{0,1},{1,0},{2,3},{3,2},{4,5},{5,4},{6,7},{7,6},{8,9},{9,8},{10,11... | collective-permute-start | bytes 786440 | tf_op jit(solution)/shard_map/ppermute | solution.py:32
  44.4 3.7 %collective-permute-start.11 = (bf16[16,64,128]{2,1,0:T(8,128)(2,1)}, bf16[16,64,128]{2,1,0:T(8,128)(2,1)S(1)}, u32[]{:S(2)}, u32[]{:S(2)}) collective-permute-start(bf16[16,64,128]{2,1,0:T(8,128)(2,1)} %collective-permute-done.7), channel_id=1, source_target_pairs={{0,1},{1,0},{2,3},{3,2},{4,5},{5,4},{6,7},{7,6},{8,9},{9,8},{10,11... | collective-permute-start | bytes 786440 | tf_op jit(solution)/shard_map/ppermute | solution.py:32
  46.0 2.7 %collective-permute-start.12 = (bf16[16,64,128]{2,1,0:T(8,128)(2,1)}, bf16[16,64,128]{2,1,0:T(8,128)(2,1)S(1)}, u32[]{:S(2)}, u32[]{:S(2)}) collective-permute-start(bf16[16,64,128]{2,1,0:T(8,128)(2,1)} %collective-permute-done.8), channel_id=1, source_target_pairs={{0,1},{1,0},{2,3},{3,2},{4,5},{5,4},{6,7},{7,6},{8,9},{9,8},{10,11... | collective-permute-start | bytes 786440 | tf_op jit(solution)/shard_map/ppermute | solution.py:32
  50.2 6.7 %collective-permute-start.13 = (bf16[9,64,128]{2,1,0:T(8,128)(2,1)S(1)}, bf16[9,64,128]{2,1,0:T(8,128)(2,1)S(1)}, u32[]{:S(2)}, u32[]{:S(2)}) collective-permute-start(bf16[9,64,128]{2,1,0:T(8,128)(2,1)S(1)} %get-tuple-element.9), channel_id=1, source_target_pairs={{0,8},{1,9},{2,10},{3,11},{4,12},{5,13},{6,14},{7,15},{8,24},{9,25... | collective-permute-start | bytes 442376 | tf_op jit(solution)/shard_map/ppermute | solution.py:32
  56.9 6.0 %collective-permute-start.14 = (bf16[9,64,128]{2,1,0:T(8,128)(2,1)S(1)}, bf16[9,64,128]{2,1,0:T(8,128)(2,1)S(1)}, u32[]{:S(2)}, u32[]{:S(2)}) collective-permute-start(bf16[9,64,128]{2,1,0:T(8,128)(2,1)S(1)} %collective-permute-done.13), channel_id=1, source_target_pairs={{0,8},{1,9},{2,10},{3,11},{4,12},{5,13},{6,14},{7,15},{8,24},{9,25... | collective-permute-start | bytes 442376 | tf_op jit(solution)/shard_map/ppermute | solution.py:32
  62.9 6.0 %collective-permute-start.15 = (bf16[9,64,128]{2,1,0:T(8,128)(2,1)S(1)}, bf16[9,64,128]{2,1,0:T(8,128)(2,1)S(1)}, u32[]{:S(2)}, u32[]{:S(2)}) collective-permute-start(bf16[9,64,128]{2,1,0:T(8,128)(2,1)S(1)} %collective-permute-done.14), channel_id=1, source_target_pairs={{0,8},{1,9},{2,10},{3,11},{4,12},{5,13},{6,14},{7,15},{8,24},{9,25... | collective-permute-start | bytes 442376 | tf_op jit(solution)/shard_map/ppermute | solution.py:32
  69.0 15.5 %collective-permute-start.16 = (bf16[36,64,128]{2,1,0:T(8,128)(2,1)S(1)}, bf16[36,64,128]{2,1,0:T(8,128)(2,1)S(1)}, u32[]{:S(2)}, u32[]{:S(2)}) collective-permute-start(bf16[36,64,128]{2,1,0:T(8,128)(2,1)S(1)} %pad_maximum_fusion), channel_id=1, source_target_pairs={{0,2},{1,3},{2,0},{3,1},{4,6},{5,7},{6,4},{7,5},{8,10},{9,11},{10,... | collective-permute-start | bytes 1769480 | tf_op jit(solution)/shard_map/ppermute | solution.py:32
  70.1 14.3 %collective-permute-start.17 = (bf16[36,64,128]{2,1,0:T(8,128)(2,1)S(1)}, bf16[36,64,128]{2,1,0:T(8,128)(2,1)S(1)}, u32[]{:S(2)}, u32[]{:S(2)}) collective-permute-start(bf16[36,64,128]{2,1,0:T(8,128)(2,1)S(1)} %pad_maximum_fusion), channel_id=1, source_target_pairs={{0,4},{1,5},{2,6},{3,7},{4,0},{5,1},{6,2},{7,3},{8,12},{9,13},{10,... | collective-permute-start | bytes 1769480 | tf_op jit(solution)/shard_map/ppermute | solution.py:32
  79.7 13.7 %collective-permute-start.20 = (bf16[36,64,128]{2,1,0:T(8,128)(2,1)S(1)}, bf16[36,64,128]{2,1,0:T(8,128)(2,1)S(1)}, u32[]{:S(2)}, u32[]{:S(2)}) collective-permute-start(bf16[36,64,128]{2,1,0:T(8,128)(2,1)S(1)} %pad_maximum_fusion), channel_id=1, source_target_pairs={{0,1},{1,0},{2,3},{3,2},{4,5},{5,4},{6,7},{7,6},{8,9},{9,8},{10,11... | collective-permute-start | bytes 1769480 | tf_op jit(solution)/shard_map/ppermute | solution.py:32
  84.4 6.8 %collective-permute-start.18 = (bf16[18,64,128]{2,1,0:T(8,128)(2,1)S(1)}, bf16[18,64,128]{2,1,0:T(8,128)(2,1)S(1)}, u32[]{:S(2)}, u32[]{:S(2)}) collective-permute-start(bf16[18,64,128]{2,1,0:T(8,128)(2,1)S(1)} %slice.69), channel_id=1, source_target_pairs={{0,2},{1,3},{2,0},{3,1},{4,6},{5,7},{6,4},{7,5},{8,10},{9,11},{10,... | collective-permute-start | bytes 884744 | tf_op jit(solution)/shard_map/ppermute | solution.py:32
  84.5 7.0 %collective-permute-start.19 = (bf16[18,64,128]{2,1,0:T(8,128)(2,1)S(1)}, bf16[18,64,128]{2,1,0:T(8,128)(2,1)S(1)}, u32[]{:S(2)}, u32[]{:S(2)}) collective-permute-start(bf16[18,64,128]{2,1,0:T(8,128)(2,1)S(1)} %slice.70), channel_id=1, source_target_pairs={{0,4},{1,5},{2,6},{3,7},{4,0},{5,1},{6,2},{7,3},{8,12},{9,13},{10,... | collective-permute-start | bytes 884744 | tf_op jit(solution)/shard_map/ppermute | solution.py:32
  87.5 6.7 %collective-permute-start.21 = (bf16[36,64,128]{2,1,0:T(8,128)(2,1)S(1)}, bf16[36,64,128]{2,1,0:T(8,128)(2,1)S(1)}, u32[]{:S(2)}, u32[]{:S(2)}) collective-permute-start(bf16[36,64,128]{2,1,0:T(8,128)(2,1)S(1)} %collective-permute-done.16), channel_id=1, source_target_pairs={{0,1},{1,0},{2,3},{3,2},{4,5},{5,4},{6,7},{7,6},{8,9},{9,8},{10,11... | collective-permute-start | bytes 1769480 | tf_op jit(solution)/shard_map/ppermute | solution.py:32
  91.2 3.9 %collective-permute-start.22 = (bf16[36,64,128]{2,1,0:T(8,128)(2,1)S(1)}, bf16[36,64,128]{2,1,0:T(8,128)(2,1)S(1)}, u32[]{:S(2)}, u32[]{:S(2)}) collective-permute-start(bf16[36,64,128]{2,1,0:T(8,128)(2,1)S(1)} %collective-permute-done.17), channel_id=1, source_target_pairs={{0,1},{1,0},{2,3},{3,2},{4,5},{5,4},{6,7},{7,6},{8,9},{9,8},{10,11... | collective-permute-start | bytes 1769480 | tf_op jit(solution)/shard_map/ppermute | solution.py:32
  91.6 4.4 %collective-permute-start.23 = (bf16[36,64,128]{2,1,0:T(8,128)(2,1)S(1)}, bf16[36,64,128]{2,1,0:T(8,128)(2,1)S(1)}, u32[]{:S(2)}, u32[]{:S(2)}) collective-permute-start(bf16[36,64,128]{2,1,0:T(8,128)(2,1)S(1)} %pad_maximum_fusion.1), channel_id=1, source_target_pairs={{0,1},{1,0},{2,3},{3,2},{4,5},{5,4},{6,7},{7,6},{8,9},{9,8},{10,11... | collective-permute-start | bytes 1769480 | tf_op jit(solution)/shard_map/ppermute | solution.py:32
  (15 other events, 291.0 us)

commit v2 on v0

v2 whole, which is shorter than its diff:
```python
import functools

import jax
import jax.numpy as jnp
import ml_dtypes
import numpy as np
from jax import lax
from jax.experimental import pallas as pl
from jax.experimental.pallas import tpu as pltpu
from jax.sharding import PartitionSpec as P

COULOMB_SCALE = 0.15
SOFTENING = 0.25
BF = jnp.bfloat16
F32 = jnp.float32
VMEM_LIMIT = 48 * 1024 * 1024


def near_tables(leaf_len):
    cells = np.arange(leaf_len)
    along = (cells // 64).astype(np.float32)
    across = (cells // 8 % 8).astype(np.float32)
    height = (cells % 8).astype(np.float32)
    extent = leaf_len // 64
    tables = []
    for offset in (-1, 0, 1):
        delta_x = along[:, None] - along[None, :] - np.float32(offset * extent)
        delta_y = across[:, None] - across[None, :]
        delta_z = height[:, None] - height[None, :]
        square = delta_x * delta_x + delta_y * delta_y + delta_z * delta_z
        value = np.float32(COULOMB_SCALE) / np.sqrt(square + np.float32(SOFTENING))
        tables.append(value.astype(ml_dtypes.bfloat16))
    return np.concatenate(tables, axis=1)


def ring_order(layers):
    return [0] + list(range(1, layers, 2)) + list(range(layers - 2, 0, -2))


def owner_table(count):
    layers = count // 8
    order = ring_order(layers)
    position = {layer: at for at, layer in enumerate(order)}
    table = np.zeros((count, 2, layers * 4), np.int32)
    for device in range(count):
        layer, chip, core = device // 8, device // 2 % 4, device % 2
        for plane in range(2):
            for step in range(layers):
                source = order[(position[layer] - step) % layers]
                for side in range(4):
                    table[device, plane, step * 4 + side] = (
                        source * 8 + (chip ^ side) * 2 + (core ^ plane)
                    )
    return table


def send(block, target):
    count = lax.axis_size("subtree")
    return lax.ppermute(block, "subtree", [(d, target(d)) for d in range(count)])


def over_core(block):
    return send(block, lambda d: d ^ 1)


def over_x(block):
    return send(block, lambda d: d ^ 2)


def over_y(block):
    return send(block, lambda d: d ^ 4)


def along_z(block):
    layers = lax.axis_size("subtree") // 8
    order = ring_order(layers)
    following = {order[i]: order[(i + 1) % layers] for i in range(layers)}
    return send(block, lambda d: following[d // 8] * 8 + d % 8)


def params():
    return pltpu.CompilerParams(vmem_limit_bytes=VMEM_LIMIT)


def cost(flops, moved):
    return pl.CostEstimate(flops=flops, bytes_accessed=moved, transcendentals=0)


def whole():
    return pl.BlockSpec(memory_space=pltpu.VMEM)


def scalars():
    return pl.BlockSpec(memory_space=pltpu.SMEM)


def dot(a, b):
    return jnp.dot(a, b, preferred_element_type=F32)


def skeleton_kernel(per, order_ref, comp_ref, basis_ref, transfer_ref,
                    ordered_ref, shared_ref, first_ref, last_ref, root_ref):
    step = pl.program_id(0)
    leaf_len = basis_ref.shape[2]

    @pl.when(step == 0)
    def _():
        root_ref[...] = jnp.zeros_like(root_ref)

    for i in range(per):
        leaf = step * per + i
        row = order_ref[pl.ds(leaf, 1), :]
        column = jnp.broadcast_to(row, (128, leaf_len)).T
        lanes = lax.broadcasted_iota(jnp.int32, (leaf_len, 128), 1)
        hot = jnp.concatenate(
            [
                jnp.where(column == lanes + 128 * t, 1.0, 0.0).astype(BF)
                for t in range(leaf_len // 128)
            ],
            axis=1,
        )
        ordered = dot(hot, comp_ref[pl.ds(i * leaf_len, leaf_len), :]).astype(BF)
        ordered_ref[pl.ds(i * leaf_len, leaf_len), :] = ordered
        skeleton = dot(basis_ref[i], ordered).astype(BF)
        shared_ref[pl.ds(leaf + 1, 1)] = skeleton[None]
        root_ref[...] += dot(transfer_ref[i], skeleton)
        if i == 0:
            @pl.when(step == 0)
            def _():
                first_ref[...] = ordered
        if i == per - 1:
            @pl.when(step == pl.num_programs(0) - 1)
            def _():
                last_ref[...] = ordered

    @pl.when(step == pl.num_programs(0) - 1)
    def _():
        shared_ref[pl.ds(0, 1)] = root_ref[...].astype(BF)[None]


def skeletons(leaf_order, composition, leaf_basis, transfer, per=4):
    leaves, rank, leaf_len = leaf_basis.shape
    fields = composition.shape[1]
    return pl.pallas_call(
        functools.partial(skeleton_kernel, per),
        name="order_and_skeleton",
        grid=(leaves // per,),
        in_specs=[
            pl.BlockSpec((leaves, leaf_len), lambda s: (0, 0)),
            pl.BlockSpec((per * leaf_len, fields), lambda s: (s, 0)),
            pl.BlockSpec((per, rank, leaf_len), lambda s: (s, 0, 0)),
            pl.BlockSpec((per, rank, rank), lambda s: (s, 0, 0)),
        ],
        out_specs=[
            pl.BlockSpec((per * leaf_len, fields), lambda s: (s, 0)),
            pl.BlockSpec((leaves + 1, rank, fields), lambda s: (0, 0, 0)),
            pl.BlockSpec((leaf_len, fields), lambda s: (0, 0)),
            pl.BlockSpec((leaf_len, fields), lambda s: (0, 0)),
        ],
        out_shape=[
            jax.ShapeDtypeStruct((leaves * leaf_len, fields), BF),
            jax.ShapeDtypeStruct((leaves + 1, rank, fields), BF),
            jax.ShapeDtypeStruct((leaf_len, fields), BF),
            jax.ShapeDtypeStruct((leaf_len, fields), BF),
        ],
        scratch_shapes=[pltpu.VMEM((rank, fields), F32)],
        compiler_params=params(),
        cost_estimate=cost(leaves * leaf_len * leaf_len * fields * 2, 8 << 20),
    )(leaf_order, composition, leaf_basis, transfer)


def dense_kernel(slot_ref, owner_ref, far_ref, coupling_ref, top_ref, own_ref, other_ref):
    leaves, entries, rank, _ = coupling_ref.shape
    slots = own_ref.shape[2] // rank

    def block_of(plane, leaf, slot):
        entry = slot_ref[plane, leaf, slot]
        block = coupling_ref[leaf, jnp.minimum(entry, entries - 1)]
        return jnp.where(entry < entries, block, jnp.zeros_like(block))

    def top_of(plane, slot):
        block = top_ref[0, owner_ref[plane, slot]]
        return jnp.where(far_ref[plane, slot] > 0, block, jnp.zeros_like(block))

    for plane, out_ref in ((0, own_ref), (1, other_ref)):

        def body(leaf, carry, plane=plane, out_ref=out_ref):
            for slot in range(0, slots, 2):
                pair = [block_of(plane, leaf, slot), block_of(plane, leaf, slot + 1)]
                out_ref[leaf + 1, :, slot * rank:(slot + 2) * rank] = jnp.concatenate(pair, axis=1)
            return carry

        lax.fori_loop(0, leaves, body, 0)
        for slot in range(0, slots, 2):
            pair = [top_of(plane, slot), top_of(plane, slot + 1)]
            out_ref[0, :, slot * rank:(slot + 2) * rank] = jnp.concatenate(pair, axis=1)


def dense_couplings(slot_entry, owners, far, coupling, top_coupling):
    leaves, _, rank, _ = coupling.shape
    slots = owners.shape[1]
    shape = jax.ShapeDtypeStruct((leaves + 1, rank, slots * rank), BF)
    return pl.pallas_call(
        dense_kernel,
        name="couplings_by_owner",
        in_specs=[scalars(), scalars(), scalars(), whole(), whole()],
        out_specs=[whole(), whole()],
        out_shape=[shape, shape],
        compiler_params=params(),
        cost_estimate=cost(0, 8 << 20),
    )(slot_entry, owners, far, coupling, top_coupling)


def round_kernel(first, step, own_at, other_at, line_ref, x_ref, y_ref, low_ref, high_ref,
                 own_ref, other_ref, *refs):
    if first:
        own_out, other_out, diagonal = refs
    else:
        own_in, other_in, own_out, other_out, diagonal = refs
    cut = low_ref.shape[0]
    diagonal[:cut] = low_ref[...]
    diagonal[cut:] = high_ref[...]
    targets = own_ref.shape[0]
    sides = (line_ref, x_ref, y_ref, diagonal)
    for at_ref, blocks_ref, out in ((own_at, own_ref, own_out), (other_at, other_ref, other_out)):
        for target in range(targets):
            chosen = jnp.concatenate(
                [side[at_ref[target, step * 4 + q]] for q, side in enumerate(sides)], axis=0
            )
            value = dot(blocks_ref[target], chosen)
            if not first:
                value = value + (own_in if out is own_out else other_in)[target]
            out[target] = value


def far_round(step, own_at, other_at, parts, own_blocks, other_blocks, sums):
    targets, rank, _ = own_blocks.shape
    fields = parts[0].shape[2]
    first = sums is None
    sum_shape = jax.ShapeDtypeStruct((targets, rank, fields), F32)
    blocks = pl.BlockSpec((targets, rank, 4 * rank), lambda s: (0, 0, step))
    full = [pl.BlockSpec(p.shape, lambda s: (0, 0, 0)) for p in parts]
    total = pl.BlockSpec((targets, rank, fields), lambda s: (0, 0, 0))
    return pl.pallas_call(
        functools.partial(round_kernel, first, step),
        name=f"far_round_{step}",
        grid=(1,),
        in_specs=[scalars(), scalars()] + full + [blocks, blocks] + ([] if first else [total, total]),
        out_specs=[total, total],
        out_shape=[sum_shape, sum_shape],
        scratch_shapes=[pltpu.VMEM((targets, rank, fields), BF)],
        compiler_params=params(),
        cost_estimate=cost(2 * targets * rank * 4 * rank * fields * 2, 4 << 20),
    )(own_at, other_at, *parts, own_blocks, other_blocks, *([] if first else sums))


def near_kernel(edges, pair_of, last_pair, mask_ref, order_ref, table_ref, basis_ref,
                prev_ref, cur_ref, next_ref, *refs):
    if edges:
        before_ref, after_ref, _, _, near_ref, turned_ref = refs
    else:
        near_ref, turned_ref = refs
    pair = pair_of(pl.program_id(0))
    leaf_len = basis_ref.shape[2]
    low, high = cur_ref[:leaf_len, :], cur_ref[leaf_len:, :]
    prev, following = prev_ref[...], next_ref[...]
    if edges:
        prev = jnp.where(pair == 0, before_ref[...], prev)
        following = jnp.where(pair == last_pair, after_ref[...], following)

    def masked(leaf, side, value):
        return jnp.where(mask_ref[leaf, side] > 0, value, jnp.zeros_like(value))

    left = jnp.concatenate(
        [masked(2 * pair, 0, prev), low, masked(2 * pair, 1, high)], axis=0
    )
    right = jnp.concatenate(
        [masked(2 * pair + 1, 0, low), high, masked(2 * pair + 1, 1, following)], axis=0
    )
    near = dot(table_ref[...], jnp.concatenate([left, right], axis=1))
    fields = cur_ref.shape[1]
    rows = lax.broadcasted_iota(jnp.int32, (leaf_len, leaf_len), 0)
    for i in range(2):
        value = near[:, i * fields:(i + 1) * fields]
        coarse = value.astype(BF)
        fine = (value - coarse.astype(F32)).astype(BF)
        row = order_ref[pl.ds(2 * pair + i, 1), :]
        hot = jnp.where(rows == row, 1.0, 0.0).astype(BF)
        placed = dot(hot, jnp.concatenate([coarse, fine], axis=1))
        at = pl.ds(i * leaf_len, leaf_len)
        near_ref[at, :] = placed[:, :fields] + placed[:, fields:]
        turned_ref[at, :] = lax.dot_general(
            hot, basis_ref[i], (((1,), (1,)), ((), ())), preferred_element_type=F32
        ).astype(BF)


def near_field(pairs, near_list, leaf_order, tables, leaf_basis, ordered, edges=None):
    leaves, rank, leaf_len = leaf_basis.shape
    fields = ordered.shape[1]
    last = leaves // 2 - 1
    gap = pairs[1] - pairs[0] if len(pairs) > 1 else 1

    def pair_of(step):
        return pairs[0] + gap * step

    in_specs = [
        scalars(),
        pl.BlockSpec((leaves, leaf_len), lambda s: (0, 0)),
        pl.BlockSpec(tables.shape, lambda s: (0, 0)),
        pl.BlockSpec((2, rank, leaf_len), lambda s: (pair_of(s), 0, 0)),
        pl.BlockSpec((leaf_len, fields), lambda s: (jnp.maximum(2 * pair_of(s) - 1, 0), 0)),
        pl.BlockSpec((2 * leaf_len, fields), lambda s: (pair_of(s), 0)),
        pl.BlockSpec((leaf_len, fields), lambda s: (jnp.minimum(2 * pair_of(s) + 2, leaves - 1), 0)),
    ]
    args = [near_list, leaf_order, tables, leaf_basis, ordered, ordered, ordered]
    aliases = {}
    if edges is not None:
        before, after, near, turned = edges
        edge = pl.BlockSpec((leaf_len, fields), lambda s: (0, 0))
        in_specs += [edge, edge, pl.BlockSpec(memory_space=pl.ANY), pl.BlockSpec(memory_space=pl.ANY)]
        args += [before, after, near, turned]
        aliases = {9: 0, 10: 1}
    return pl.pallas_call(
        functools.partial(near_kernel, edges is not None, pair_of, last),
        name="near_and_turn",
        grid=(len(pairs),),
        in_specs=in_specs,
        out_specs=[
            pl.BlockSpec((2 * leaf_len, fields), lambda s: (pair_of(s), 0)),
            pl.BlockSpec((2 * leaf_len, rank), lambda s: (pair_of(s), 0)),
        ],
        out_shape=[
            jax.ShapeDtypeStruct((leaves * leaf_len, fields), F32),
            jax.ShapeDtypeStruct((leaves * leaf_len, rank), BF),
        ],
        input_output_aliases=aliases,
        compiler_params=params(),
        cost_estimate=cost(len(pairs) * 2 * leaf_len * leaf_len * fields * 12, len(pairs) << 20),
    )(*args)


def field_kernel(per, own_ref, other_ref, turned_transfer_ref, near_ref, turned_ref, out_ref):
    step = pl.program_id(0)
    leaf_len = near_ref.shape[0] // per
    local = own_ref[0] + other_ref[0]
    coarse = local.astype(BF)
    fine = (local - coarse.astype(F32)).astype(BF)
    both = jnp.concatenate([coarse, fine], axis=1)
    fields = local.shape[1]
    for i in range(per):
        leaf = step * per + i
        down = dot(turned_transfer_ref[i], both)
        value = own_ref[leaf + 1] + other_ref[leaf + 1] + (down[:, :fields] + down[:, fields:])
        at = pl.ds(i * leaf_len, leaf_len)
        far = dot(turned_ref[at, :], value.astype(BF))
        out_ref[at, :] = (near_ref[at, :] + far).astype(BF)


def field(own, other, turned_transfer, near, turned, per=2):
    leaves, rank, _ = turned_transfer.shape
    fields = near.shape[1]
    leaf_len = near.shape[0] // leaves
    total = pl.BlockSpec(own.shape, lambda s: (0, 0, 0))
    return pl.pallas_call(
        functools.partial(field_kernel, per),
        name="local_and_field",
        grid=(leaves // per,),
        in_specs=[
            total,
            total,
            pl.BlockSpec((per, rank, rank), lambda s: (s, 0, 0)),
            pl.BlockSpec((per * leaf_len, fields), lambda s: (s, 0)),
            pl.BlockSpec((per * leaf_len, rank), lambda s: (s, 0)),
        ],
        out_specs=pl.BlockSpec((per * leaf_len, fields), lambda s: (s, 0)),
        out_shape=jax.ShapeDtypeStruct(near.shape, BF),
        compiler_params=params(),
        cost_estimate=cost(leaves * leaf_len * rank * fields * 2, 6 << 20),
    )(own, other, turned_transfer, near, turned)


def on_device(
    composition,
    leaf_basis,
    transfer,
    coupling,
    top_coupling,
    admissible_owner,
    admissible_leaf,
    near_list,
    leaf_order,
):
    leaves, rank, leaf_len = leaf_basis.shape
    entries = coupling.shape[1]
    count = lax.axis_size("subtree")
    layers = count // 8
    my_index = lax.axis_index("subtree")

    ordered, shared, first, last = skeletons(leaf_order, composition, leaf_basis, transfer)

    owners = jnp.asarray(owner_table(count))[my_index]
    named = admissible_owner[None, :, None, :] == owners[:, None, :, None]
    entry = jnp.arange(entries, dtype=jnp.int32)
    slot_entry = jnp.min(jnp.where(named, entry, entries), axis=-1).astype(jnp.int32)
    slot_block = jnp.sum(
        jnp.where(named, admissible_leaf[None, :, None, :] + 1, 0), axis=-1
    ).astype(jnp.int32)
    slot_block = jnp.concatenate([jnp.zeros_like(slot_block[:, :1]), slot_block], axis=1)
    far = (jnp.abs(owners - my_index) >= 2).astype(jnp.int32)
    own_blocks, my_other = dense_couplings(slot_entry, owners, far, coupling, top_coupling)

    cut = (leaves + 2) // 2
    line = shared
    rounds = []
    for step in range(layers):
        from_x, from_y = over_x(line), over_y(line)
        following = along_z(line) if step < layers - 1 else None
        rounds.append([line, from_x, from_y, over_x(from_y[:cut]), over_y(from_x[cut:])])
        line = following

    before = lax.ppermute(last, "subtree", [(d, d + 1) for d in range(count - 1)])
    after = lax.ppermute(first, "subtree", [(d + 1, d) for d in range(count - 1)])
    other_blocks = over_core(my_other)
    other_at = over_core(slot_block[1])
    own_at = slot_block[0]

    tables = jnp.asarray(near_tables(leaf_len))
    near_args = (near_list, leaf_order, tables, leaf_basis, ordered)
    pairs = leaves // 2
    near, turned = near_field(list(range(1, pairs - 1)), *near_args)
    near, turned = near_field([0, pairs - 1], *near_args, edges=(before, after, near, turned))

    sums = None
    for step, parts in enumerate(rounds):
        sums = far_round(step, own_at, other_at, parts, own_blocks, other_blocks, sums)
    own_sum, other_sum = sums
    received = over_core(other_sum)
    return field(own_sum, received, transfer.transpose(0, 2, 1), near, turned)


def solution(mesh):
    placed = (
        P(("groups", "subtree"), None),
        P("subtree", None, None),
        P("subtree", None, None),
        P("subtree", None, None, None),
        P("subtree", None, None, None),
        P(("groups", "subtree"), None),
        P(("groups", "subtree"), None),
        P(("groups", "subtree"), None),
        P(("groups", "subtree"), None),
    )
    return jax.shard_map(
        on_device,
        mesh=mesh,
        in_specs=placed,
        out_specs=P(("groups", "subtree"), None),
        check_vma=False,
    )
```

time: 117 us -> 109 us (0.932)
  the two profiles are of different devices: /device:TPU:0 before, /device:TPU:9 now
where the time goes in v2:
time: 109 us; the launch traced here: 108 us
  Pallas kernels  37.1 us (34%)
  starting transfers between devices  36.9 us (34%)
  local copies, waits for them, and re-layouts  24.5 us (22%)
  waiting for transfers between devices  6.35 us (6%)
  other arithmetic  3.03 us (3%)
    ppermute x22, starting transfers between devices, send(): lax.ppermute(block, 'subtree', [(d, target(d)) for d in range(count)])  27.4 us
    unnamed x96, local copies, waits for them, and re-layouts  20.5 us
    pallas_call x2, Pallas kernels, near_field(): pl.pallas_call(functools.partial(near_kernel, edges is not None, pair_of,...  13.7 us
    pallas_call x1, Pallas kernels, skeletons(): pl.pallas_call(functools.partial(skeleton_kernel, per), name='order_and_s...  7.67 us
    ppermute x1, starting transfers between devices, on_device(): lax.ppermute(last, 'subtree', [(d, d + 1) for d in range(count - 1)])  7.56 us
    ppermute x22, waiting for transfers between devices, send(): lax.ppermute(block, 'subtree', [(d, target(d)) for d in range(count)])  6.35 us
    pallas_call x4, Pallas kernels, far_round(): pl.pallas_call(functools.partial(round_kernel, first, step), name=f'far_r...  6.33 us
    pallas_call x1, Pallas kernels, dense_couplings(): pl.pallas_call(dense_kernel, name='couplings_by_owner', in_specs=[scalars...  4.87 us
  transfers between devices with their start and end apart: 24, of which 5 were waited for; matrix products, arithmetic and copies ran while one was open for 3% of the time, Pallas kernels for 26%

profile of v2, /device:TPU:9, one launch (start us, length us, event | category | flops | bytes accessed | tf_op | source)
XLA Modules:
  0.0 108.3 jit_solution(15862121004756531232)
XLA Ops:
  2.1 1.6 %fusion.1 = (s32[2,12,16]{2,1,0:T(8,128)S(1)}, s32[2,12,16]{2,1,0:T(8,128)S(1)}) fusion(s32[2,16]{1,0:T(2,128)S(1)} %dynamic-slice_bitcast_fusion.owner_ref, s32[12,16]{1,0:T(8,128)} %param.16, s32[12,16]{1,0:T(8,128)S(1)} %broadcast_add_fusion), kind=kLoop, calls=%fused_computation.3 | loop fusion | flops 29952 | bytes 4736 | tf_op jit(solution)/shard_map/reduce_min | solution.py:404
  4.8 4.9 %couplings_by_owner.1 = (bf16[13,64,1024]{2,1,0:T(8,128)(2,1)S(1)}, bf16[13,64,1024]{2,1,0:T(8,128)(2,1)S(1)}) custom-call(s32[2,12,16]{2,1,0:T(8,128)S(1)} %get-tuple-element.41.slot_ref, s32[2,16]{1,0:T(2,128)S(1)} %dynamic-slice_bitcast_fusion.owner_ref, s32[2,16]{1,0:T(2,128)S(1)} %compare_convert_fusion.far_ref, bf16[12,16,64,64]{3,2,1,0:T(8,128)(2,1)} %coupling_ref.1, ...), custom_call_target="tpu_custom_call" | custom-call | bytes 8388608 | tf_op jit(solution)/shard_map/couplings_by_owner/pallas_call | solution.py:203
  10.4 7.7 %order_and_skeleton.1 = (bf16[6144,128]{1,0:T(8,128)(2,1)S(1)}, bf16[13,64,128]{2,1,0:T(8,128)(2,1)S(1)}, bf16[512,128]{1,0:T(8,128)(2,1)}, bf16[512,128]{1,0:T(8,128)(2,1)}) custom-call(s32[12,512]{1,0:T(8,128)S(1)} %copy-done.42, bf16[6144,128]{1,0:T(8,128)(2,1)S(1)} %copy-done.45, bf16[12,64,512]{2,1,0:T(8,128)(2,1)S(1)} %copy-done.6, ...), custom_call_target="tpu_custom_call" | custom-call | flops 805306368 | bytes 8388608 | tf_op jit(solution)/shard_map/order_and_skeleton/pallas_call | solution.py:144
  18.1 2.3 %collective-permute-start.1 = (bf16[13,64,128]{2,1,0:T(8,128)(2,1)S(1)}, bf16[13,64,128]{2,1,0:T(8,128)(2,1)S(1)}, u32[]{:S(2)}, u32[]{:S(2)}) collective-permute-start(bf16[13,64,128]{2,1,0:T(8,128)(2,1)S(1)} %get-tuple-element.23.line_ref), channel_id=1, source_target_pairs={{0,8},{1,9},{2,10},{3,11},{4,12},{5,13},{6,14},{7,15},{8,24},{9,25... | collective-permute-start | bytes 638984 | tf_op jit(solution)/shard_map/ppermute | solution.py:59
  20.4 1.2 %collective-permute-start.18 = (bf16[13,64,128]{2,1,0:T(8,128)(2,1)S(1)}, bf16[13,64,128]{2,1,0:T(8,128)(2,1)S(1)}, u32[]{:S(2)}, u32[]{:S(2)}) collective-permute-start(bf16[13,64,128]{2,1,0:T(8,128)(2,1)S(1)} %get-tuple-element.23.line_ref), channel_id=1, source_target_pairs={{0,4},{1,5},{2,6},{3,7},{4,0},{5,1},{6,2},{7,3},{8,12},{9,13},{10,... | collective-permute-start | bytes 638984 | tf_op jit(solution)/shard_map/ppermute | solution.py:59
  23.5 1.5 %collective-permute-done.1.line_ref = bf16[13,64,128]{2,1,0:T(8,128)(2,1)S(1)} collective-permute-done((bf16[13,64,128]{2,1,0:T(8,128)(2,1)S(1)}, bf16[13,64,128]{2,1,0:T(8,128)(2,1)S(1)}, u32[]{:S(2)}, u32[]{:S(2)}) %collective-permute-start.1) | collective-permute-done | bytes 213024 | tf_op jit(solution)/shard_map/ppermute | solution.py:59
  25.0 3.1 %collective-permute-start.2 = (bf16[13,64,128]{2,1,0:T(8,128)(2,1)S(1)}, bf16[13,64,128]{2,1,0:T(8,128)(2,1)S(1)}, u32[]{:S(2)}, u32[]{:S(2)}) collective-permute-start(bf16[13,64,128]{2,1,0:T(8,128)(2,1)S(1)} %collective-permute-done.1.line_ref), channel_id=1, source_target_pairs={{0,8},{1,9},{2,10},{3,11},{4,12},{5,13},{6,14},{7,15},{8,24},{9,25... | collective-permute-start | bytes 638984 | tf_op jit(solution)/shard_map/ppermute | solution.py:59
  31.9 3.1 %collective-permute-start.3 = (bf16[13,64,128]{2,1,0:T(8,128)(2,1)S(1)}, bf16[13,64,128]{2,1,0:T(8,128)(2,1)S(1)}, u32[]{:S(2)}, u32[]{:S(2)}) collective-permute-start(bf16[13,64,128]{2,1,0:T(8,128)(2,1)S(1)} %collective-permute-done.2.line_ref), channel_id=1, source_target_pairs={{0,8},{1,9},{2,10},{3,11},{4,12},{5,13},{6,14},{7,15},{8,24},{9,25... | collective-permute-start | bytes 638984 | tf_op jit(solution)/shard_map/ppermute | solution.py:59
  40.5 1.9 %collective-permute-done.20.high_ref = bf16[6,64,128]{2,1,0:T(8,128)(2,1)S(1)} collective-permute-done((bf16[6,64,128]{2,1,0:T(8,128)(2,1)S(1)}, bf16[6,64,128]{2,1,0:T(8,128)(2,1)S(1)}, u32[]{:S(2)}, u32[]{:S(2)}) %collective-permute-start.20) | collective-permute-done | bytes 98336 | tf_op jit(solution)/shard_map/ppermute | solution.py:59
  45.2 1.2 %collective-permute-start.9 = (bf16[13,64,128]{2,1,0:T(8,128)(2,1)S(1)}, bf16[13,64,128]{2,1,0:T(8,128)(2,1)S(1)}, u32[]{:S(2)}, u32[]{:S(2)}) collective-permute-start(bf16[13,64,128]{2,1,0:T(8,128)(2,1)S(1)} %collective-permute-done.2.line_ref), channel_id=1, source_target_pairs={{0,2},{1,3},{2,0},{3,1},{4,6},{5,7},{6,4},{7,5},{8,10},{9,11},{10,... | collective-permute-start | bytes 638984 | tf_op jit(solution)/shard_map/ppermute | solution.py:59
  52.6 1.4 %collective-permute-done.5.y_ref = bf16[13,64,128]{2,1,0:T(8,128)(2,1)S(1)} collective-permute-done((bf16[13,64,128]{2,1,0:T(8,128)(2,1)S(1)}, bf16[13,64,128]{2,1,0:T(8,128)(2,1)S(1)}, u32[]{:S(2)}, u32[]{:S(2)}) %collective-permute-start.5) | collective-permute-done | bytes 213024 | tf_op jit(solution)/shard_map/ppermute | solution.py:59
  54.0 1.2 %collective-permute-start.11 = (bf16[7,64,128]{2,1,0:T(8,128)(2,1)}, bf16[7,64,128]{2,1,0:T(8,128)(2,1)}, u32[]{:S(2)}, u32[]{:S(2)}) collective-permute-start(bf16[7,64,128]{2,1,0:T(8,128)(2,1)} %slice.42), channel_id=1, source_target_pairs={{0,2},{1,3},{2,0},{3,1},{4,6},{5,7},{6,4},{7,5},{8,10},{9,11},{10,... | collective-permute-start | bytes 344072 | tf_op jit(solution)/shard_map/ppermute | solution.py:59
  59.7 1.2 %collective-permute-start.7 = (bf16[6,64,128]{2,1,0:T(8,128)(2,1)}, bf16[6,64,128]{2,1,0:T(8,128)(2,1)}, u32[]{:S(2)}, u32[]{:S(2)}) collective-permute-start(bf16[6,64,128]{2,1,0:T(8,128)(2,1)} %slice.41), channel_id=1, source_target_pairs={{0,4},{1,5},{2,6},{3,7},{4,0},{5,1},{6,2},{7,3},{8,12},{9,13},{10,... | collective-permute-start | bytes 294920 | tf_op jit(solution)/shard_map/ppermute | solution.py:59
  65.9 7.6 %collective-permute-start.22 = (bf16[512,128]{1,0:T(8,128)(2,1)}, bf16[512,128]{1,0:T(8,128)(2,1)}, u32[]{:S(2)}, u32[]{:S(2)}) collective-permute-start(bf16[512,128]{1,0:T(8,128)(2,1)} %get-tuple-element.35), channel_id=1, source_target_pairs={{0,1},{1,2},{2,3},{3,4},{4,5},{5,6},{6,7},{7,8},{8,9},{9,10},{10,1... | collective-permute-start | bytes 393224 | tf_op jit(solution)/shard_map/ppermute | solution.py:421
  73.6 1.4 %far_round_1.1 = (f32[13,64,128]{2,1,0:T(8,128)S(1)}, f32[13,64,128]{2,1,0:T(8,128)S(1)}) custom-call(s32[13,16]{1,0:T(8,128)S(1)} %get-tuple-element.44.own_at, s32[13,16]{1,0:T(8,128)S(1)} %collective-permute-done.other_at, bf16[13,64,128]{2,1,0:T(8,128)(2,1)S(1)} %copy-done.33, bf16[13,64,128]{2,1,0:T(8,128)(2,1)S(1)} %copy-done.21, ...), custom_call_target="tpu_custom_call" | custom-call | flops 109051904 | bytes 4194304 | tf_op jit(solution)/shard_map/far_round_1/pallas_call | solution.py:244
  75.0 1.9 %collective-permute-start.23 = (bf16[512,128]{1,0:T(8,128)(2,1)}, bf16[512,128]{1,0:T(8,128)(2,1)}, u32[]{:S(2)}, u32[]{:S(2)}) collective-permute-start(bf16[512,128]{1,0:T(8,128)(2,1)} %get-tuple-element.36), channel_id=1, source_target_pairs={{1,0},{2,1},{3,2},{4,3},{5,4},{6,5},{7,6},{8,7},{9,8},{10,9},{11,1... | collective-permute-start | bytes 393224 | tf_op jit(solution)/shard_map/ppermute | solution.py:422
  77.0 1.4 %far_round_2.1 = (f32[13,64,128]{2,1,0:T(8,128)S(1)}, f32[13,64,128]{2,1,0:T(8,128)S(1)}) custom-call(s32[13,16]{1,0:T(8,128)S(1)} %get-tuple-element.44.own_at, s32[13,16]{1,0:T(8,128)S(1)} %collective-permute-done.other_at, bf16[13,64,128]{2,1,0:T(8,128)(2,1)S(1)} %copy-done.29, bf16[13,64,128]{2,1,0:T(8,128)(2,1)S(1)} %copy-done.25, ...), custom_call_target="tpu_custom_call" | custom-call | flops 109051904 | bytes 4194304 | tf_op jit(solution)/shard_map/far_round_2/pallas_call | solution.py:244
  78.5 2.3 %far_round_3.1 = (f32[13,64,128]{2,1,0:T(8,128)S(1)}, f32[13,64,128]{2,1,0:T(8,128)}) custom-call(s32[13,16]{1,0:T(8,128)S(1)} %get-tuple-element.44.own_at, s32[13,16]{1,0:T(8,128)S(1)} %collective-permute-done.other_at, bf16[13,64,128]{2,1,0:T(8,128)(2,1)S(1)} %copy-done.31, bf16[13,64,128]{2,1,0:T(8,128)(2,1)S(1)} %copy-done.23, ...), custom_call_target="tpu_custom_call" | custom-call | flops 109051904 | bytes 4194304 | tf_op jit(solution)/shard_map/far_round_3/pallas_call | solution.py:244
  81.6 3.0 %collective-permute-start.21 = (f32[13,64,128]{2,1,0:T(8,128)}, f32[13,64,128]{2,1,0:T(8,128)}, u32[]{:S(2)}, u32[]{:S(2)}) collective-permute-start(f32[13,64,128]{2,1,0:T(8,128)} %get-tuple-element.33), channel_id=1, source_target_pairs={{0,1},{1,0},{2,3},{3,2},{4,5},{5,4},{6,7},{7,6},{8,9},{9,8},{10,11... | collective-permute-start | bytes 1277960 | tf_op jit(solution)/shard_map/ppermute | solution.py:59
  84.7 8.4 %near_and_turn.2 = (f32[6144,128]{1,0:T(8,128)}, bf16[6144,64]{1,0:T(8,128)(2,1)S(1)}) custom-call(s32[12,2]{1,0:T(8,128)S(1)} %copy.19.mask_ref, s32[12,512]{1,0:T(8,128)S(1)} %copy-done.43, bf16[512,1536]{1,0:T(8,128)(2,1)S(1)} %copy-done.4, bf16[12,64,512]{2,1,0:T(8,128)(2,1)S(1)} %copy-done.7, bf16[6144,128]{1,0:T(8,128)(2,1)S(1)} %copy-done.1, ...), custom_call_target="tpu_custom_call" | custom-call | flops 3221225472 | bytes 4194304 | tf_op jit(solution)/shard_map/near_and_turn/pallas_call | solution.py:323
  93.3 1.4 %copy-done.5 = bf16[512,1536]{1,0:T(8,128)(2,1)S(1)} copy-done((bf16[512,1536]{1,0:T(8,128)(2,1)S(1)}, bf16[512,1536]{1,0:T(8,128)(2,1)}, u32[]{:S(2)}) %copy-start.5) | copy-done | bytes 1572888
  96.6 5.3 %near_and_turn.3 = (f32[6144,128]{1,0:T(8,128)}, bf16[6144,64]{1,0:T(8,128)(2,1)S(1)}) custom-call(s32[12,2]{1,0:T(8,128)S(1)} %copy.19.mask_ref, s32[12,512]{1,0:T(8,128)S(1)} %copy-done.44, bf16[512,1536]{1,0:T(8,128)(2,1)S(1)} %copy-done.5, bf16[12,64,512]{2,1,0:T(8,128)(2,1)S(1)} %copy-done.8, ...), custom_call_target="tpu_custom_call", output_to_operand_aliasing={{0}: (9, {}), {1}: (10, {})} | custom-call | flops 1610612736 | bytes 2097152 | tf_op jit(solution)/shard_map/near_and_turn/pallas_call | solution.py:323
  101.9 1.9 %copy-done.3 = f32[6144,128]{1,0:T(8,128)S(1)} copy-done((f32[6144,128]{1,0:T(8,128)S(1)}, f32[6144,128]{1,0:T(8,128)}, u32[]{:S(2)}) %copy-start.3) | copy-done | bytes 3145752
  103.8 4.5 %local_and_field.1 = bf16[6144,128]{1,0:T(8,128)(2,1)} custom-call(f32[13,64,128]{2,1,0:T(8,128)S(1)} %copy-done.27, f32[13,64,128]{2,1,0:T(8,128)} %collective-permute-done.21.other_ref, bf16[12,64,64]{2,1,0:T(8,128)(2,1)S(1)} %bitcast.9, f32[6144,128]{1,0:T(8,128)S(1)} %copy-done.3, bf16[6144,64]{1,0:T(8,128)(2,1)S(1)} %get-tuple-element.40.turned_ref), custom_call_target="tpu_custom_call" | custom-call | flops 100663296 | bytes 6291456 | tf_op jit(solution)/shard_map/local_and_field/pallas_call | solution.py:364
  (142 shorter events, 36.2 us)
Async XLA Ops:
  9.7 50.0 %collective-permute-start.8 = (bf16[13,64,1024]{2,1,0:T(8,128)(2,1)S(1)}, bf16[13,64,1024]{2,1,0:T(8,128)(2,1)S(1)}, u32[]{:S(2)}, u32[]{:S(2)}) collective-permute-start(bf16[13,64,1024]{2,1,0:T(8,128)(2,1)S(1)} %get-tuple-element.25), channel_id=1, source_target_pairs={{0,1},{1,0},{2,3},{3,2},{4,5},{5,4},{6,7},{7,6},{8,9},{9,8},{10,11... | collective-permute-start | bytes 5111816 | tf_op jit(solution)/shard_map/ppermute | solution.py:59
  18.1 7.0 %collective-permute-start.1 = (bf16[13,64,128]{2,1,0:T(8,128)(2,1)S(1)}, bf16[13,64,128]{2,1,0:T(8,128)(2,1)S(1)}, u32[]{:S(2)}, u32[]{:S(2)}) collective-permute-start(bf16[13,64,128]{2,1,0:T(8,128)(2,1)S(1)} %get-tuple-element.23.line_ref), channel_id=1, source_target_pairs={{0,8},{1,9},{2,10},{3,11},{4,12},{5,13},{6,14},{7,15},{8,24},{9,25... | collective-permute-start | bytes 638984 | tf_op jit(solution)/shard_map/ppermute | solution.py:59
  20.4 17.2 %collective-permute-start.18 = (bf16[13,64,128]{2,1,0:T(8,128)(2,1)S(1)}, bf16[13,64,128]{2,1,0:T(8,128)(2,1)S(1)}, u32[]{:S(2)}, u32[]{:S(2)}) collective-permute-start(bf16[13,64,128]{2,1,0:T(8,128)(2,1)S(1)} %get-tuple-element.23.line_ref), channel_id=1, source_target_pairs={{0,4},{1,5},{2,6},{3,7},{4,0},{5,1},{6,2},{7,3},{8,12},{9,13},{10,... | collective-permute-start | bytes 638984 | tf_op jit(solution)/shard_map/ppermute | solution.py:59
  21.6 13.4 %collective-permute-start.17 = (bf16[13,64,128]{2,1,0:T(8,128)(2,1)S(1)}, bf16[13,64,128]{2,1,0:T(8,128)(2,1)S(1)}, u32[]{:S(2)}, u32[]{:S(2)}) collective-permute-start(bf16[13,64,128]{2,1,0:T(8,128)(2,1)S(1)} %get-tuple-element.23.line_ref), channel_id=1, source_target_pairs={{0,2},{1,3},{2,0},{3,1},{4,6},{5,7},{6,4},{7,5},{8,10},{9,11},{10,... | collective-permute-start | bytes 638984 | tf_op jit(solution)/shard_map/ppermute | solution.py:59
  25.0 6.8 %collective-permute-start.2 = (bf16[13,64,128]{2,1,0:T(8,128)(2,1)S(1)}, bf16[13,64,128]{2,1,0:T(8,128)(2,1)S(1)}, u32[]{:S(2)}, u32[]{:S(2)}) collective-permute-start(bf16[13,64,128]{2,1,0:T(8,128)(2,1)S(1)} %collective-permute-done.1.line_ref), channel_id=1, source_target_pairs={{0,8},{1,9},{2,10},{3,11},{4,12},{5,13},{6,14},{7,15},{8,24},{9,25... | collective-permute-start | bytes 638984 | tf_op jit(solution)/shard_map/ppermute | solution.py:59
  28.1 1.9 %collective-permute-start = (s32[13,16]{1,0:T(8,128)S(1)}, s32[13,16]{1,0:T(8,128)S(1)}, u32[]{:S(2)}, u32[]{:S(2)}) collective-permute-start(s32[13,16]{1,0:T(8,128)S(1)} %get-tuple-element.43), channel_id=1, source_target_pairs={{0,1},{1,0},{2,3},{3,2},{4,5},{5,4},{6,7},{7,6},{8,9},{9,8},{10,11... | collective-permute-start | bytes 2504 | tf_op jit(solution)/shard_map/ppermute | solution.py:59
  30.1 8.5 %collective-permute-start.13 = (bf16[13,64,128]{2,1,0:T(8,128)(2,1)S(1)}, bf16[13,64,128]{2,1,0:T(8,128)(2,1)S(1)}, u32[]{:S(2)}, u32[]{:S(2)}) collective-permute-start(bf16[13,64,128]{2,1,0:T(8,128)(2,1)S(1)} %collective-permute-done.1.line_ref), channel_id=1, source_target_pairs={{0,2},{1,3},{2,0},{3,1},{4,6},{5,7},{6,4},{7,5},{8,10},{9,11},{10,... | collective-permute-start | bytes 638984 | tf_op jit(solution)/shard_map/ppermute | solution.py:59
  31.9 12.7 %collective-permute-start.3 = (bf16[13,64,128]{2,1,0:T(8,128)(2,1)S(1)}, bf16[13,64,128]{2,1,0:T(8,128)(2,1)S(1)}, u32[]{:S(2)}, u32[]{:S(2)}) collective-permute-start(bf16[13,64,128]{2,1,0:T(8,128)(2,1)S(1)} %collective-permute-done.2.line_ref), channel_id=1, source_target_pairs={{0,8},{1,9},{2,10},{3,11},{4,12},{5,13},{6,14},{7,15},{8,24},{9,25... | collective-permute-start | bytes 638984 | tf_op jit(solution)/shard_map/ppermute | solution.py:59
  35.0 10.2 %collective-permute-start.14 = (bf16[13,64,128]{2,1,0:T(8,128)(2,1)S(1)}, bf16[13,64,128]{2,1,0:T(8,128)(2,1)S(1)}, u32[]{:S(2)}, u32[]{:S(2)}) collective-permute-start(bf16[13,64,128]{2,1,0:T(8,128)(2,1)S(1)} %collective-permute-done.1.line_ref), channel_id=1, source_target_pairs={{0,4},{1,5},{2,6},{3,7},{4,0},{5,1},{6,2},{7,3},{8,12},{9,13},{10,... | collective-permute-start | bytes 638984 | tf_op jit(solution)/shard_map/ppermute | solution.py:59
  37.6 4.8 %collective-permute-start.20 = (bf16[6,64,128]{2,1,0:T(8,128)(2,1)S(1)}, bf16[6,64,128]{2,1,0:T(8,128)(2,1)S(1)}, u32[]{:S(2)}, u32[]{:S(2)}) collective-permute-start(bf16[6,64,128]{2,1,0:T(8,128)(2,1)S(1)} %slice.47), channel_id=1, source_target_pairs={{0,4},{1,5},{2,6},{3,7},{4,0},{5,1},{6,2},{7,3},{8,12},{9,13},{10,... | collective-permute-start | bytes 294920 | tf_op jit(solution)/shard_map/ppermute | solution.py:59
  38.6 5.1 %collective-permute-start.19 = (bf16[7,64,128]{2,1,0:T(8,128)(2,1)S(1)}, bf16[7,64,128]{2,1,0:T(8,128)(2,1)S(1)}, u32[]{:S(2)}, u32[]{:S(2)}) collective-permute-start(bf16[7,64,128]{2,1,0:T(8,128)(2,1)S(1)} %slice.46), channel_id=1, source_target_pairs={{0,2},{1,3},{2,0},{3,1},{4,6},{5,7},{6,4},{7,5},{8,10},{9,11},{10,... | collective-permute-start | bytes 344072 | tf_op jit(solution)/shard_map/ppermute | solution.py:59
  43.1 4.0 %collective-permute-start.16 = (bf16[6,64,128]{2,1,0:T(8,128)(2,1)S(1)}, bf16[6,64,128]{2,1,0:T(8,128)(2,1)S(1)}, u32[]{:S(2)}, u32[]{:S(2)}) collective-permute-start(bf16[6,64,128]{2,1,0:T(8,128)(2,1)S(1)} %slice.45), channel_id=1, source_target_pairs={{0,4},{1,5},{2,6},{3,7},{4,0},{5,1},{6,2},{7,3},{8,12},{9,13},{10,... | collective-permute-start | bytes 294920 | tf_op jit(solution)/shard_map/ppermute | solution.py:59
  43.7 6.7 %collective-permute-start.10 = (bf16[13,64,128]{2,1,0:T(8,128)(2,1)S(1)}, bf16[13,64,128]{2,1,0:T(8,128)(2,1)S(1)}, u32[]{:S(2)}, u32[]{:S(2)}) collective-permute-start(bf16[13,64,128]{2,1,0:T(8,128)(2,1)S(1)} %collective-permute-done.2.line_ref), channel_id=1, source_target_pairs={{0,4},{1,5},{2,6},{3,7},{4,0},{5,1},{6,2},{7,3},{8,12},{9,13},{10,... | collective-permute-start | bytes 638984 | tf_op jit(solution)/shard_map/ppermute | solution.py:59
  44.5 9.4 %collective-permute-start.5 = (bf16[13,64,128]{2,1,0:T(8,128)(2,1)S(1)}, bf16[13,64,128]{2,1,0:T(8,128)(2,1)S(1)}, u32[]{:S(2)}, u32[]{:S(2)}) collective-permute-start(bf16[13,64,128]{2,1,0:T(8,128)(2,1)S(1)} %collective-permute-done.3.line_ref), channel_id=1, source_target_pairs={{0,4},{1,5},{2,6},{3,7},{4,0},{5,1},{6,2},{7,3},{8,12},{9,13},{10,... | collective-permute-start | bytes 638984 | tf_op jit(solution)/shard_map/ppermute | solution.py:59
  45.2 11.4 %collective-permute-start.9 = (bf16[13,64,128]{2,1,0:T(8,128)(2,1)S(1)}, bf16[13,64,128]{2,1,0:T(8,128)(2,1)S(1)}, u32[]{:S(2)}, u32[]{:S(2)}) collective-permute-start(bf16[13,64,128]{2,1,0:T(8,128)(2,1)S(1)} %collective-permute-done.2.line_ref), channel_id=1, source_target_pairs={{0,2},{1,3},{2,0},{3,1},{4,6},{5,7},{6,4},{7,5},{8,10},{9,11},{10,... | collective-permute-start | bytes 638984 | tf_op jit(solution)/shard_map/ppermute | solution.py:59
  47.7 10.4 %collective-permute-start.4 = (bf16[13,64,128]{2,1,0:T(8,128)(2,1)S(1)}, bf16[13,64,128]{2,1,0:T(8,128)(2,1)S(1)}, u32[]{:S(2)}, u32[]{:S(2)}) collective-permute-start(bf16[13,64,128]{2,1,0:T(8,128)(2,1)S(1)} %collective-permute-done.3.line_ref), channel_id=1, source_target_pairs={{0,2},{1,3},{2,0},{3,1},{4,6},{5,7},{6,4},{7,5},{8,10},{9,11},{10,... | collective-permute-start | bytes 638984 | tf_op jit(solution)/shard_map/ppermute | solution.py:59
  50.4 15.5 %collective-permute-start.15 = (bf16[7,64,128]{2,1,0:T(8,128)(2,1)}, bf16[7,64,128]{2,1,0:T(8,128)(2,1)}, u32[]{:S(2)}, u32[]{:S(2)}) collective-permute-start(bf16[7,64,128]{2,1,0:T(8,128)(2,1)} %slice.44), channel_id=1, source_target_pairs={{0,2},{1,3},{2,0},{3,1},{4,6},{5,7},{6,4},{7,5},{8,10},{9,11},{10,... | collective-permute-start | bytes 344072 | tf_op jit(solution)/shard_map/ppermute | solution.py:59
  54.0 22.9 %collective-permute-start.11 = (bf16[7,64,128]{2,1,0:T(8,128)(2,1)}, bf16[7,64,128]{2,1,0:T(8,128)(2,1)}, u32[]{:S(2)}, u32[]{:S(2)}) collective-permute-start(bf16[7,64,128]{2,1,0:T(8,128)(2,1)} %slice.42), channel_id=1, source_target_pairs={{0,2},{1,3},{2,0},{3,1},{4,6},{5,7},{6,4},{7,5},{8,10},{9,11},{10,... | collective-permute-start | bytes 344072 | tf_op jit(solution)/shard_map/ppermute | solution.py:59
  56.6 21.9 %collective-permute-start.6 = (bf16[7,64,128]{2,1,0:T(8,128)(2,1)}, bf16[7,64,128]{2,1,0:T(8,128)(2,1)}, u32[]{:S(2)}, u32[]{:S(2)}) collective-permute-start(bf16[7,64,128]{2,1,0:T(8,128)(2,1)} %slice.40), channel_id=1, source_target_pairs={{0,2},{1,3},{2,0},{3,1},{4,6},{5,7},{6,4},{7,5},{8,10},{9,11},{10,... | collective-permute-start | bytes 344072 | tf_op jit(solution)/shard_map/ppermute | solution.py:59
  58.1 16.9 %collective-permute-start.12 = (bf16[6,64,128]{2,1,0:T(8,128)(2,1)}, bf16[6,64,128]{2,1,0:T(8,128)(2,1)}, u32[]{:S(2)}, u32[]{:S(2)}) collective-permute-start(bf16[6,64,128]{2,1,0:T(8,128)(2,1)} %slice.43), channel_id=1, source_target_pairs={{0,4},{1,5},{2,6},{3,7},{4,0},{5,1},{6,2},{7,3},{8,12},{9,13},{10,... | collective-permute-start | bytes 294920 | tf_op jit(solution)/shard_map/ppermute | solution.py:59
  59.7 18.7 %collective-permute-start.7 = (bf16[6,64,128]{2,1,0:T(8,128)(2,1)}, bf16[6,64,128]{2,1,0:T(8,128)(2,1)}, u32[]{:S(2)}, u32[]{:S(2)}) collective-permute-start(bf16[6,64,128]{2,1,0:T(8,128)(2,1)} %slice.41), channel_id=1, source_target_pairs={{0,4},{1,5},{2,6},{3,7},{4,0},{5,1},{6,2},{7,3},{8,12},{9,13},{10,... | collective-permute-start | bytes 294920 | tf_op jit(solution)/shard_map/ppermute | solution.py:59
  65.9 27.3 %collective-permute-start.22 = (bf16[512,128]{1,0:T(8,128)(2,1)}, bf16[512,128]{1,0:T(8,128)(2,1)}, u32[]{:S(2)}, u32[]{:S(2)}) collective-permute-start(bf16[512,128]{1,0:T(8,128)(2,1)} %get-tuple-element.35), channel_id=1, source_target_pairs={{0,1},{1,2},{2,3},{3,4},{4,5},{5,6},{6,7},{7,8},{8,9},{9,10},{10,1... | collective-permute-start | bytes 393224 | tf_op jit(solution)/shard_map/ppermute | solution.py:421
  75.0 18.3 %collective-permute-start.23 = (bf16[512,128]{1,0:T(8,128)(2,1)}, bf16[512,128]{1,0:T(8,128)(2,1)}, u32[]{:S(2)}, u32[]{:S(2)}) collective-permute-start(bf16[512,128]{1,0:T(8,128)(2,1)} %get-tuple-element.36), channel_id=1, source_target_pairs={{1,0},{2,1},{3,2},{4,3},{5,4},{6,5},{7,6},{8,7},{9,8},{10,9},{11,1... | collective-permute-start | bytes 393224 | tf_op jit(solution)/shard_map/ppermute | solution.py:422
  81.6 20.3 %collective-permute-start.21 = (f32[13,64,128]{2,1,0:T(8,128)}, f32[13,64,128]{2,1,0:T(8,128)}, u32[]{:S(2)}, u32[]{:S(2)}) collective-permute-start(f32[13,64,128]{2,1,0:T(8,128)} %get-tuple-element.33), channel_id=1, source_target_pairs={{0,1},{1,0},{2,3},{3,2},{4,5},{5,4},{6,7},{7,6},{8,9},{9,8},{10,11... | collective-permute-start | bytes 1277960 | tf_op jit(solution)/shard_map/ppermute | solution.py:59
  (47 other events, 232.5 us)

commit v3 on v2

v3 whole, which is shorter than its diff:
```python
import functools

import jax
import jax.numpy as jnp
import ml_dtypes
import numpy as np
from jax import lax
from jax.experimental import pallas as pl
from jax.experimental.pallas import tpu as pltpu
from jax.sharding import PartitionSpec as P

COULOMB_SCALE = 0.15
SOFTENING = 0.25
BF = jnp.bfloat16
F32 = jnp.float32
MIB = 1 << 20


def near_tables(leaf_len):
    cells = np.arange(leaf_len)
    along = (cells // 64).astype(np.float32)
    across = (cells // 8 % 8).astype(np.float32)
    height = (cells % 8).astype(np.float32)
    extent = leaf_len // 64
    tables = []
    for offset in (-1, 0, 1):
        delta_x = along[:, None] - along[None, :] - np.float32(offset * extent)
        delta_y = across[:, None] - across[None, :]
        delta_z = height[:, None] - height[None, :]
        square = delta_x * delta_x + delta_y * delta_y + delta_z * delta_z
        value = np.float32(COULOMB_SCALE) / np.sqrt(square + np.float32(SOFTENING))
        tables.append(value.astype(ml_dtypes.bfloat16))
    return np.concatenate(tables, axis=1)


def ring_order(layers):
    return [0] + list(range(1, layers, 2)) + list(range(layers - 2, 0, -2))


def send(block, target):
    count = lax.axis_size("subtree")
    return lax.ppermute(block, "subtree", [(d, target(d)) for d in range(count)])


def over_core(block):
    return send(block, lambda d: d ^ 1)


def over_x(block):
    return send(block, lambda d: d ^ 2)


def over_y(block):
    return send(block, lambda d: d ^ 4)


def onward(block):
    return send(block, lambda d: d ^ (2 if d % 2 else 4))


def along_z(block):
    layers = lax.axis_size("subtree") // 8
    order = ring_order(layers)
    following = {order[i]: order[(i + 1) % layers] for i in range(layers)}
    return send(block, lambda d: following[d // 8] * 8 + d % 8)


def params(mib):
    return pltpu.CompilerParams(vmem_limit_bytes=mib * MIB)


def cost(flops, moved):
    return pl.CostEstimate(flops=flops, bytes_accessed=moved, transcendentals=0)


def whole():
    return pl.BlockSpec(memory_space=pltpu.VMEM)


def scalars():
    return pl.BlockSpec(memory_space=pltpu.SMEM)


def dot(a, b):
    return jnp.dot(a, b, preferred_element_type=F32)


def one_hot_grid(row, leaf_len):
    cells = lax.broadcasted_iota(jnp.int32, (leaf_len, leaf_len), 0)
    return jnp.where(cells == row, 1.0, 0.0).astype(BF)


def skeleton_kernel(per, order_ref, comp_ref, basis_ref, transfer_ref,
                    placed_ref, shared_ref, root_ref):
    step = pl.program_id(0)
    leaf_len = basis_ref.shape[2]

    @pl.when(step == 0)
    def _():
        root_ref[...] = jnp.zeros_like(root_ref)

    for i in range(per):
        leaf = step * per + i
        hot = one_hot_grid(order_ref[pl.ds(leaf, 1), :], leaf_len)
        placed = lax.dot_general(
            basis_ref[i], hot, (((1,), (1,)), ((), ())), preferred_element_type=F32
        ).astype(BF)
        placed_ref[i] = placed
        skeleton = dot(placed, comp_ref[pl.ds(i * leaf_len, leaf_len), :]).astype(BF)
        shared_ref[pl.ds(leaf + 1, 1)] = skeleton[None]
        root_ref[...] += dot(transfer_ref[i], skeleton)

    @pl.when(step == pl.num_programs(0) - 1)
    def _():
        shared_ref[pl.ds(0, 1)] = root_ref[...].astype(BF)[None]


def skeletons(leaf_order, composition, leaf_basis, transfer, per=4):
    leaves, rank, leaf_len = leaf_basis.shape
    fields = composition.shape[1]
    return pl.pallas_call(
        functools.partial(skeleton_kernel, per),
        name="basis_and_skeleton",
        grid=(leaves // per,),
        in_specs=[
            pl.BlockSpec((leaves, leaf_len), lambda s: (0, 0)),
            pl.BlockSpec((per * leaf_len, fields), lambda s: (s, 0)),
            pl.BlockSpec((per, rank, leaf_len), lambda s: (s, 0, 0)),
            pl.BlockSpec((per, rank, rank), lambda s: (s, 0, 0)),
        ],
        out_specs=[
            pl.BlockSpec((per, rank, leaf_len), lambda s: (s, 0, 0)),
            pl.BlockSpec((leaves + 1, rank, fields), lambda s: (0, 0, 0)),
        ],
        out_shape=[
            jax.ShapeDtypeStruct((leaves, rank, leaf_len), BF),
            jax.ShapeDtypeStruct((leaves + 1, rank, fields), BF),
        ],
        scratch_shapes=[pltpu.VMEM((rank, fields), F32)],
        compiler_params=params(16),
        cost_estimate=cost(leaves * leaf_len * leaf_len * rank * 2, 4 * MIB),
    )(leaf_order, composition, leaf_basis, transfer)


def owner_tables(me, layers, owners, blocks):
    leaves, entries = owners.shape
    slots = layers * 4
    rows = leaves + 1
    shape = (rows, 2 * slots)
    lane = lax.broadcasted_iota(jnp.int32, shape, 1)
    plane = (lane >= slots).astype(jnp.int32)
    slot = lane - plane * slots
    layer, chip, core = me // 8, (me // 2) & 3, me & 1
    half = layers // 2
    at = jnp.where(layer & 1 > 0, (layer + 1) // 2, jnp.where(layer > 0, layers - layer // 2, 0))
    back = at - (slot >> 2)
    back = jnp.where(back < 0, back + layers, back)
    source = jnp.where(back == 0, 0, jnp.where(back <= half, 2 * back - 1, 2 * (layers - back)))
    owner = source * 8 + (chip ^ (slot & 3)) * 2 + (core ^ plane)
    row = lax.broadcasted_iota(jnp.int32, shape, 0)
    distant = jnp.abs(owner - me) >= 2
    entry = jnp.where((row == 0) & distant, owner, -1)
    block = jnp.zeros(shape, jnp.int32)
    pad = jnp.full((1, entries), -1, jnp.int32)
    named = jnp.concatenate([pad, owners], axis=0)
    chosen = jnp.concatenate([pad, blocks], axis=0)
    for k in range(entries):
        match = named[:, k:k + 1] == owner
        entry = jnp.where(match, k, entry)
        block = jnp.where(match, chosen[:, k:k + 1] + 1, block)
    return entry, block


def order_kernel(per, layers, me_ref, order_ref, comp_ref, owner_ref, leaf_ref,
                 ordered_ref, first_ref, last_ref, table_ref):
    step = pl.program_id(0)
    leaf_len = order_ref.shape[1]
    for i in range(per):
        row = order_ref[pl.ds(step * per + i, 1), :]
        column = jnp.broadcast_to(row, (128, leaf_len)).T
        lanes = lax.broadcasted_iota(jnp.int32, (leaf_len, 128), 1)
        hot = jnp.concatenate(
            [
                jnp.where(column == lanes + 128 * t, 1.0, 0.0).astype(BF)
                for t in range(leaf_len // 128)
            ],
            axis=1,
        )
        at = pl.ds(i * leaf_len, leaf_len)
        ordered = dot(hot, comp_ref[at, :]).astype(BF)
        ordered_ref[at, :] = ordered
        if i == 0:
            @pl.when(step == 0)
            def _():
                first_ref[...] = ordered
        if i == per - 1:
            @pl.when(step == pl.num_programs(0) - 1)
            def _():
                last_ref[...] = ordered

    @pl.when(step == 0)
    def _():
        entry, block = owner_tables(me_ref[0], layers, owner_ref[...], leaf_ref[...])
        rows = entry.shape[0]
        table_ref[0, :rows, :entry.shape[1]] = entry
        table_ref[1, :rows, :entry.shape[1]] = block


def in_order(me, leaf_order, composition, owners, blocks, layers, per=4):
    leaves, leaf_len = leaf_order.shape
    fields = composition.shape[1]
    entries = owners.shape[1]
    edge = jax.ShapeDtypeStruct((leaf_len, fields), BF)
    return pl.pallas_call(
        functools.partial(order_kernel, per, layers),
        name="cluster_order",
        grid=(leaves // per,),
        in_specs=[
            scalars(),
            pl.BlockSpec((leaves, leaf_len), lambda s: (0, 0)),
            pl.BlockSpec((per * leaf_len, fields), lambda s: (s, 0)),
            pl.BlockSpec((leaves, entries), lambda s: (0, 0)),
            pl.BlockSpec((leaves, entries), lambda s: (0, 0)),
        ],
        out_specs=[
            pl.BlockSpec((per * leaf_len, fields), lambda s: (s, 0)),
            pl.BlockSpec((leaf_len, fields), lambda s: (0, 0)),
            pl.BlockSpec((leaf_len, fields), lambda s: (0, 0)),
            pl.BlockSpec((2, 16, 128), lambda s: (0, 0, 0)),
        ],
        out_shape=[
            jax.ShapeDtypeStruct((leaves * leaf_len, fields), BF),
            edge,
            edge,
            jax.ShapeDtypeStruct((2, 16, 128), jnp.int32),
        ],
        compiler_params=params(16),
        cost_estimate=cost(leaves * leaf_len * leaf_len * fields * 2, 4 * MIB),
    )(me, leaf_order, composition, owners, blocks)


def round_kernel(first, steps, slots, own_at, other_at, line_ref, x_ref, y_ref, far_ref,
                 own_coupling, own_top, other_coupling, other_top, *refs):
    if first:
        own_out, other_out = refs
    else:
        own_in, other_in, own_out, other_out = refs
    rows = own_out.shape[0]
    sides = (line_ref, x_ref, y_ref, far_ref)
    for plane, at_ref, coupling_ref, top_ref, out in (
        (0, own_at, own_coupling, own_top, own_out),
        (1, other_at, other_coupling, other_top, other_out),
    ):
        for row in range(rows):
            value = None
            for place, step in enumerate(steps):
                left, right = [], []
                for q, side in enumerate(sides):
                    lane = plane * slots + step * 4 + q
                    entry = at_ref[0, row, lane]
                    safe = jnp.maximum(entry, 0)
                    block = top_ref[0, safe] if row == 0 else coupling_ref[row - 1, safe]
                    left.append(jnp.where(entry >= 0, block, jnp.zeros_like(block)))
                    right.append(side[place * rows + at_ref[1, row, lane]])
                part = dot(jnp.concatenate(left, axis=1), jnp.concatenate(right, axis=0))
                value = part if value is None else value + part
            if not first:
                value = value + (own_in if plane == 0 else other_in)[row]
            out[row] = value


def far_round(steps, slots, own_at, other_at, parts, couplings, sums):
    rows = couplings[0].shape[0] + 1
    rank, fields = parts[0].shape[1:]
    first = sums is None
    sum_shape = jax.ShapeDtypeStruct((rows, rank, fields), F32)
    args = list(parts) + list(couplings) + ([] if first else list(sums))
    return pl.pallas_call(
        functools.partial(round_kernel, first, steps, slots),
        name="far_round_" + str(steps[0]),
        in_specs=[scalars(), scalars()] + [whole()] * len(args),
        out_specs=[whole(), whole()],
        out_shape=[sum_shape, sum_shape],
        compiler_params=params(16),
        cost_estimate=cost(2 * rows * rank * 4 * rank * fields * 2 * len(steps), 2 * MIB),
    )(own_at, other_at, *args)


def near_kernel(edges, pair_of, last_pair, mask_ref, order_ref, table_ref, placed_ref,
                prev_ref, cur_ref, next_ref, *refs):
    if edges:
        before_ref, after_ref = refs[:2]
    near_ref, turned_ref = refs[-2:]
    pair = pair_of(pl.program_id(0))
    leaf_len = placed_ref.shape[2]
    low, high = cur_ref[:leaf_len, :], cur_ref[leaf_len:, :]
    prev, following = prev_ref[...], next_ref[...]
    if edges:
        prev = jnp.where(pair == 0, before_ref[...], prev)
        following = jnp.where(pair == last_pair, after_ref[...], following)

    def masked(leaf, side, value):
        return jnp.where(mask_ref[leaf, side] > 0, value, jnp.zeros_like(value))

    left = jnp.concatenate(
        [masked(2 * pair, 0, prev), low, masked(2 * pair, 1, high)], axis=0
    )
    right = jnp.concatenate(
        [masked(2 * pair + 1, 0, low), high, masked(2 * pair + 1, 1, following)], axis=0
    )
    near = dot(table_ref[...], jnp.concatenate([left, right], axis=1)).astype(BF)
    fields = cur_ref.shape[1]
    for i in range(2):
        hot = one_hot_grid(order_ref[pl.ds(2 * pair + i, 1), :], leaf_len)
        at = pl.ds(i * leaf_len, leaf_len)
        near_ref[at, :] = dot(hot, near[:, i * fields:(i + 1) * fields]).astype(BF)
        turned_ref[at, :] = placed_ref[i].T


def near_field(pairs, near_list, leaf_order, tables, placed, ordered, halos=None, filled=None):
    leaves, rank, leaf_len = placed.shape
    fields = ordered.shape[1]
    last = leaves // 2 - 1
    gap = pairs[1] - pairs[0] if len(pairs) > 1 else 1

    def pair_of(step):
        return pairs[0] + gap * step

    in_specs = [
        scalars(),
        pl.BlockSpec((leaves, leaf_len), lambda s: (0, 0)),
        pl.BlockSpec(tables.shape, lambda s: (0, 0)),
        pl.BlockSpec((2, rank, leaf_len), lambda s: (pair_of(s), 0, 0)),
        pl.BlockSpec((leaf_len, fields), lambda s: (jnp.maximum(2 * pair_of(s) - 1, 0), 0)),
        pl.BlockSpec((2 * leaf_len, fields), lambda s: (pair_of(s), 0)),
        pl.BlockSpec((leaf_len, fields), lambda s: (jnp.minimum(2 * pair_of(s) + 2, leaves - 1), 0)),
    ]
    args = [near_list, leaf_order, tables, placed, ordered, ordered, ordered]
    aliases = {}
    if halos is not None:
        in_specs += [pl.BlockSpec((leaf_len, fields), lambda s: (0, 0))] * 2
        args += list(halos)
    if filled is not None:
        aliases = {len(args): 0, len(args) + 1: 1}
        in_specs += [pl.BlockSpec(memory_space=pl.ANY)] * 2
        args += list(filled)
    return pl.pallas_call(
        functools.partial(near_kernel, halos is not None, pair_of, last),
        name="near_" + str(pairs[0]),
        grid=(len(pairs),),
        in_specs=in_specs,
        out_specs=[
            pl.BlockSpec((2 * leaf_len, fields), lambda s: (pair_of(s), 0)),
            pl.BlockSpec((2 * leaf_len, rank), lambda s: (pair_of(s), 0)),
        ],
        out_shape=[
            jax.ShapeDtypeStruct((leaves * leaf_len, fields), BF),
            jax.ShapeDtypeStruct((leaves * leaf_len, rank), BF),
        ],
        input_output_aliases=aliases,
        compiler_params=params(16),
        cost_estimate=cost(len(pairs) * 2 * leaf_len * leaf_len * fields * 10, len(pairs) * MIB),
    )(*args)


def field_kernel(per, own_ref, other_ref, turned_transfer_ref, near_ref, turned_ref, out_ref):
    step = pl.program_id(0)
    leaf_len = near_ref.shape[0] // per
    local = own_ref[0] + other_ref[0]
    coarse = local.astype(BF)
    fine = (local - coarse.astype(F32)).astype(BF)
    both = jnp.concatenate([coarse, fine], axis=1)
    fields = local.shape[1]
    for i in range(per):
        leaf = step * per + i
        down = dot(turned_transfer_ref[i], both)
        value = own_ref[leaf + 1] + other_ref[leaf + 1] + (down[:, :fields] + down[:, fields:])
        at = pl.ds(i * leaf_len, leaf_len)
        far = dot(turned_ref[at, :], value.astype(BF))
        out_ref[at, :] = (near_ref[at, :].astype(F32) + far).astype(BF)


def field(own, other, turned_transfer, near, turned, per=4):
    leaves, rank, _ = turned_transfer.shape
    fields = near.shape[1]
    leaf_len = near.shape[0] // leaves
    total = pl.BlockSpec(own.shape, lambda s: (0, 0, 0))
    return pl.pallas_call(
        functools.partial(field_kernel, per),
        name="local_and_field",
        grid=(leaves // per,),
        in_specs=[
            total,
            total,
            pl.BlockSpec((per, rank, rank), lambda s: (s, 0, 0)),
            pl.BlockSpec((per * leaf_len, fields), lambda s: (s, 0)),
            pl.BlockSpec((per * leaf_len, rank), lambda s: (s, 0)),
        ],
        out_specs=pl.BlockSpec((per * leaf_len, fields), lambda s: (s, 0)),
        out_shape=jax.ShapeDtypeStruct(near.shape, BF),
        compiler_params=params(16),
        cost_estimate=cost(leaves * leaf_len * rank * fields * 2, 4 * MIB),
    )(own, other, turned_transfer, near, turned)


def after(block, *others):
    return lax.optimization_barrier((block,) + others)[0]


def on_device(
    composition,
    leaf_basis,
    transfer,
    coupling,
    top_coupling,
    admissible_owner,
    admissible_leaf,
    near_list,
    leaf_order,
):
    leaves, rank, leaf_len = leaf_basis.shape
    count = lax.axis_size("subtree")
    layers = count // 8
    slots = layers * 4
    my_index = lax.axis_index("subtree")
    even = my_index % 2 == 0

    placed, shared = skeletons(leaf_order, composition, leaf_basis, transfer)

    def plane(block):
        from_x, from_y = over_x(block), over_y(block)
        return block, from_x, from_y

    def diagonal(parts, *others):
        chosen = jnp.where(even, parts[1], parts[2])
        return parts + (onward(after(chosen, *others)),)

    near_plane = plane(shared)
    line = along_z(shared)
    ordered, first, last, table = in_order(
        my_index.reshape(1), leaf_order, composition, admissible_owner, admissible_leaf, layers
    )
    line = after(line, table)
    lines = [along_z(line)]
    next_plane = plane(after(line, near_plane[1], near_plane[2]))
    round_0 = diagonal(near_plane)
    for _ in range(layers - 3):
        lines.append(along_z(lines[-1]))
    before = lax.ppermute(last, "subtree", [(d, d + 1) for d in range(count - 1)])
    behind = lax.ppermute(first, "subtree", [(d + 1, d) for d in range(count - 1)])
    couplings = (coupling, top_coupling, over_core(coupling), over_core(top_coupling))
    other_table = over_core(table)

    tables = jnp.asarray(near_tables(leaf_len))
    near_args = (near_list, leaf_order, tables, placed, ordered)
    pairs = leaves // 2
    cut = pairs // 2
    filled = near_field(list(range(1, cut)), *near_args)
    round_1 = diagonal(next_plane, filled[0])
    last_plane = plane(after(jnp.concatenate(lines, axis=0), round_0[3], filled[0]))
    near_args = (near_list, leaf_order, tables, placed, after(ordered, round_1[3]))
    filled = near_field(list(range(cut, pairs - 1)), *near_args, filled=filled)
    sums = far_round([0], slots, table, other_table, round_0, couplings, None)
    sums = far_round([1], slots, table, other_table, round_1, couplings, sums)
    round_2 = diagonal(last_plane, sums[0], filled[0])
    filled = near_field([0, pairs - 1], *near_args, halos=(before, behind), filled=filled)
    round_2 = round_2[:3] + (after(round_2[3], filled[0]),)
    sums = far_round(list(range(2, layers)), slots, table, other_table, round_2, couplings, sums)
    received = over_core(sums[1])
    return field(sums[0], received, transfer.transpose(0, 2, 1), *filled)


def solution(mesh):
    placed = (
        P(("groups", "subtree"), None),
        P("subtree", None, None),
        P("subtree", None, None),
        P("subtree", None, None, None),
        P("subtree", None, None, None),
        P(("groups", "subtree"), None),
        P(("groups", "subtree"), None),
        P(("groups", "subtree"), None),
        P(("groups", "subtree"), None),
    )
    return jax.shard_map(
        on_device,
        mesh=mesh,
        in_specs=placed,
        out_specs=P(("groups", "subtree"), None),
        check_vma=False,
    )
```

time: 109 us -> 90.9 us (0.83)
  the two profiles are of different devices: /device:TPU:9 before, /device:TPU:0 now
where the time goes in v3:
time: 90.9 us; the launch traced here: 89.7 us
  Pallas kernels  32.9 us (36%)
  starting transfers between devices  23.1 us (25%)
  waiting for transfers between devices  20.3 us (22%)
  local copies, waits for them, and re-layouts  12.1 us (13%)
  other arithmetic  1.07 us (1%)
    ppermute x16, starting transfers between devices, send(): lax.ppermute(block, 'subtree', [(d, target(d)) for d in range(count)])  19.7 us
    ppermute x16, waiting for transfers between devices, send(): lax.ppermute(block, 'subtree', [(d, target(d)) for d in range(count)])  18.4 us
    unnamed x44, local copies, waits for them, and re-layouts  12.1 us
    pallas_call x3, Pallas kernels, near_field(): pl.pallas_call(functools.partial(near_kernel, halos is not None, pair_of,...  10.6 us
    pallas_call x3, Pallas kernels, far_round(): pl.pallas_call(functools.partial(round_kernel, first, steps, slots), name...  9.81 us
    pallas_call x1, Pallas kernels, skeletons(): pl.pallas_call(functools.partial(skeleton_kernel, per), name='basis_and_s...  5.87 us
    pallas_call x1, Pallas kernels, in_order(): pl.pallas_call(functools.partial(order_kernel, per, layers), name='cluste...  3.81 us
    pallas_call x1, Pallas kernels, field(): pl.pallas_call(functools.partial(field_kernel, per), name='local_and_fiel...  2.73 us
  transfers between devices with their start and end apart: 18, of which 5 were waited for; matrix products, arithmetic and copies ran while one was open for 2% of the time, Pallas kernels for 16%

profile of v3, /device:TPU:0, one launch (start us, length us, event | category | flops | bytes accessed | tf_op | source)
XLA Modules:
  0.0 89.7 jit_solution(12855837307888801743)
XLA Ops:
  0.0 1.4 %copy-done.10 = bf16[6144,128]{1,0:T(8,128)(2,1)S(1)} copy-done((bf16[6144,128]{1,0:T(8,128)(2,1)S(1)}, bf16[6144,128]{1,0:T(8,128)(2,1)}, u32[]{:S(2)}) %copy-start.10) | copy-done | bytes 1572888
  4.2 5.9 %basis_and_skeleton.1 = (bf16[12,64,512]{2,1,0:T(8,128)(2,1)S(1)}, bf16[13,64,128]{2,1,0:T(8,128)(2,1)}) custom-call(s32[12,512]{1,0:T(8,128)S(1)} %copy-done.15, bf16[6144,128]{1,0:T(8,128)(2,1)S(1)} %copy-done.10, bf16[12,64,512]{2,1,0:T(8,128)(2,1)S(1)} %copy-done.14, bf16[12,64,64]{2,1,0:T(8,128)(2,1)S(1)} %copy-done.12), custom_call_target="tpu_custom_call" | custom-call | flops 402653184 | bytes 4194304 | tf_op jit(solution)/shard_map/basis_and_skeleton/pallas_call | solution.py:121
  11.0 3.0 %collective-permute-start.1 = (bf16[13,64,128]{2,1,0:T(8,128)(2,1)}, bf16[13,64,128]{2,1,0:T(8,128)(2,1)}, u32[]{:S(2)}, u32[]{:S(2)}) collective-permute-start(bf16[13,64,128]{2,1,0:T(8,128)(2,1)} %get-tuple-element.31.line_ref), channel_id=1, source_target_pairs={{0,8},{1,9},{2,10},{3,11},{4,12},{5,13},{6,14},{7,15},{8,24},{9,25... | collective-permute-start | bytes 638984 | tf_op jit(solution)/shard_map/ppermute | solution.py:42
  14.0 1.5 %collective-permute-start.4 = (bf16[13,64,128]{2,1,0:T(8,128)(2,1)}, bf16[13,64,128]{2,1,0:T(8,128)(2,1)S(1)}, u32[]{:S(2)}, u32[]{:S(2)}) collective-permute-start(bf16[13,64,128]{2,1,0:T(8,128)(2,1)} %get-tuple-element.31.line_ref), channel_id=1, source_target_pairs={{0,2},{1,3},{2,0},{3,1},{4,6},{5,7},{6,4},{7,5},{8,10},{9,11},{10,... | collective-permute-start | bytes 638984 | tf_op jit(solution)/shard_map/ppermute | solution.py:42
  15.5 1.5 %collective-permute-start.5 = (bf16[13,64,128]{2,1,0:T(8,128)(2,1)}, bf16[13,64,128]{2,1,0:T(8,128)(2,1)}, u32[]{:S(2)}, u32[]{:S(2)}) collective-permute-start(bf16[13,64,128]{2,1,0:T(8,128)(2,1)} %get-tuple-element.31.line_ref), channel_id=1, source_target_pairs={{0,4},{1,5},{2,6},{3,7},{4,0},{5,1},{6,2},{7,3},{8,12},{9,13},{10,... | collective-permute-start | bytes 638984 | tf_op jit(solution)/shard_map/ppermute | solution.py:42
  17.0 1.4 %copy-done.11 = bf16[6144,128]{1,0:T(8,128)(2,1)S(1)} copy-done((bf16[6144,128]{1,0:T(8,128)(2,1)S(1)}, bf16[6144,128]{1,0:T(8,128)(2,1)}, u32[]{:S(2)}) %copy-start.11) | copy-done | bytes 1572888
  18.4 3.8 %cluster_order.1 = (bf16[6144,128]{1,0:T(8,128)(2,1)S(1)}, bf16[512,128]{1,0:T(8,128)(2,1)S(1)}, bf16[512,128]{1,0:T(8,128)(2,1)S(1)}, s32[2,16,128]{2,1,0:T(8,128)S(1)}) custom-call(s32[1]{0:T(128)} %bitcast.me_ref, s32[12,512]{1,0:T(8,128)S(1)} %copy-done.16, bf16[6144,128]{1,0:T(8,128)(2,1)S(1)} %copy-done.11, s32[12,16]{1,0:T(8,128)S(1)} %copy-done.19, ...), custom_call_target="tpu_custom_call" | custom-call | flops 805306368 | bytes 4194304 | tf_op jit(solution)/shard_map/cluster_order/pallas_call | solution.py:214
  22.9 2.6 %collective-permute-start.2 = (bf16[13,64,128]{2,1,0:T(8,128)(2,1)}, bf16[13,64,128]{2,1,0:T(8,128)(2,1)}, u32[]{:S(2)}, u32[]{:S(2)}) collective-permute-start(bf16[13,64,128]{2,1,0:T(8,128)(2,1)} %collective-permute-done.1.line_ref), channel_id=1, source_target_pairs={{0,8},{1,9},{2,10},{3,11},{4,12},{5,13},{6,14},{7,15},{8,24},{9,25... | collective-permute-start | bytes 638984 | tf_op jit(solution)/shard_map/ppermute | solution.py:42
  27.4 4.4 %collective-permute-done.2 = bf16[13,64,128]{2,1,0:T(8,128)(2,1)} collective-permute-done((bf16[13,64,128]{2,1,0:T(8,128)(2,1)}, bf16[13,64,128]{2,1,0:T(8,128)(2,1)}, u32[]{:S(2)}, u32[]{:S(2)}) %collective-permute-start.2) | collective-permute-done | bytes 213024 | tf_op jit(solution)/shard_map/ppermute | solution.py:42
  31.8 1.7 %collective-permute-start.3 = (bf16[13,64,128]{2,1,0:T(8,128)(2,1)}, bf16[13,64,128]{2,1,0:T(8,128)(2,1)S(1)}, u32[]{:S(2)}, u32[]{:S(2)}) collective-permute-start(bf16[13,64,128]{2,1,0:T(8,128)(2,1)} %collective-permute-done.2), channel_id=1, source_target_pairs={{0,8},{1,9},{2,10},{3,11},{4,12},{5,13},{6,14},{7,15},{8,24},{9,25... | collective-permute-start | bytes 638984 | tf_op jit(solution)/shard_map/ppermute | solution.py:42
  35.2 3.5 %near_1.1 = (bf16[6144,128]{1,0:T(8,128)(2,1)S(1)}, bf16[6144,64]{1,0:T(8,128)(2,1)S(1)}) custom-call(s32[12,2]{1,0:T(8,128)S(1)} %copy.15.mask_ref, s32[12,512]{1,0:T(8,128)S(1)} %copy-done.16, bf16[512,1536]{1,0:T(8,128)(2,1)S(1)} %copy-done.1, bf16[12,64,512]{2,1,0:T(8,128)(2,1)S(1)} %copy-done.7, ...), custom_call_target="tpu_custom_call" | custom-call | flops 1342177280 | bytes 2097152 | tf_op jit(solution)/shard_map/near_1/pallas_call | solution.py:347
  41.9 1.6 %collective-permute-start.11 = (bf16[13,64,128]{2,1,0:T(8,128)(2,1)S(1)}, bf16[13,64,128]{2,1,0:T(8,128)(2,1)S(1)}, u32[]{:S(2)}, u32[]{:S(2)}) collective-permute-start(bf16[13,64,128]{2,1,0:T(8,128)(2,1)S(1)} %broadcast_select_fusion.1), channel_id=1, source_target_pairs={{0,4},{1,3},{2,6},{3,1},{4,0},{5,7},{6,2},{7,5},{8,12},{9,11},{10,... | collective-permute-start | bytes 638984 | tf_op jit(solution)/shard_map/ppermute | solution.py:42
  43.5 11.7 %collective-permute-done.11.far_ref = bf16[13,64,128]{2,1,0:T(8,128)(2,1)S(1)} collective-permute-done((bf16[13,64,128]{2,1,0:T(8,128)(2,1)S(1)}, bf16[13,64,128]{2,1,0:T(8,128)(2,1)S(1)}, u32[]{:S(2)}, u32[]{:S(2)}) %collective-permute-start.11) | collective-permute-done | bytes 213024 | tf_op jit(solution)/shard_map/ppermute | solution.py:42
  55.2 3.6 %near_3.1 = (bf16[6144,128]{1,0:T(8,128)(2,1)S(1)}, bf16[6144,64]{1,0:T(8,128)(2,1)S(1)}) custom-call(s32[12,2]{1,0:T(8,128)S(1)} %copy.15.mask_ref, s32[12,512]{1,0:T(8,128)S(1)} %copy-done.16, bf16[512,1536]{1,0:T(8,128)(2,1)S(1)} %copy-done.1, bf16[12,64,512]{2,1,0:T(8,128)(2,1)S(1)} %copy-done.7, ...), custom_call_target="tpu_custom_call", output_to_operand_aliasing={{0}: (7, {}), {1}: (8, {})} | custom-call | flops 1342177280 | bytes 2097152 | tf_op jit(solution)/shard_map/near_3/pallas_call | solution.py:347
  58.9 2.8 %far_round_0.1 = (f32[13,64,128]{2,1,0:T(8,128)S(1)}, f32[13,64,128]{2,1,0:T(8,128)S(1)}) custom-call(s32[2,16,128]{2,1,0:T(8,128)S(1)} %get-tuple-element.30.own_at, s32[2,16,128]{2,1,0:T(8,128)S(1)} %collective-permute-done.other_at, bf16[13,64,128]{2,1,0:T(8,128)(2,1)} %get-tuple-element.31.line_ref, ...), custom_call_target="tpu_custom_call" | custom-call | flops 109051904 | bytes 2097152 | tf_op jit(solution)/shard_map/far_round_0/pallas_call | solution.py:278
  61.7 2.8 %far_round_1.1 = (f32[13,64,128]{2,1,0:T(8,128)S(1)}, f32[13,64,128]{2,1,0:T(8,128)S(1)}) custom-call(s32[2,16,128]{2,1,0:T(8,128)S(1)} %get-tuple-element.30.own_at, s32[2,16,128]{2,1,0:T(8,128)S(1)} %collective-permute-done.other_at, bf16[13,64,128]{2,1,0:T(8,128)(2,1)} %collective-permute-done.1.line_ref, ...), custom_call_target="tpu_custom_call" | custom-call | flops 109051904 | bytes 2097152 | tf_op jit(solution)/shard_map/far_round_1/pallas_call | solution.py:278
  65.0 2.1 %collective-permute-start.15 = (bf16[512,128]{1,0:T(8,128)(2,1)S(1)}, bf16[512,128]{1,0:T(8,128)(2,1)S(1)}, u32[]{:S(2)}, u32[]{:S(2)}) collective-permute-start(bf16[512,128]{1,0:T(8,128)(2,1)S(1)} %copy-done.18), channel_id=1, source_target_pairs={{0,1},{1,2},{2,3},{3,4},{4,5},{5,6},{6,7},{7,8},{8,9},{9,10},{10,1... | collective-permute-start | bytes 393224 | tf_op jit(solution)/shard_map/ppermute | solution.py:449
  68.5 1.9 %collective-permute-done.16.refs_1_ = bf16[512,128]{1,0:T(8,128)(2,1)S(1)} collective-permute-done((bf16[512,128]{1,0:T(8,128)(2,1)S(1)}, bf16[512,128]{1,0:T(8,128)(2,1)S(1)}, u32[]{:S(2)}, u32[]{:S(2)}) %collective-permute-start.16) | collective-permute-done | bytes 131104 | tf_op jit(solution)/shard_map/ppermute | solution.py:450
  70.4 3.5 %near_0.1 = (bf16[6144,128]{1,0:T(8,128)(2,1)S(1)}, bf16[6144,64]{1,0:T(8,128)(2,1)S(1)}) custom-call(s32[12,2]{1,0:T(8,128)S(1)} %copy.15.mask_ref, s32[12,512]{1,0:T(8,128)S(1)} %copy-done.16, bf16[512,1536]{1,0:T(8,128)(2,1)S(1)} %copy-done.1, bf16[12,64,512]{2,1,0:T(8,128)(2,1)S(1)} %copy-done.8, ...), custom_call_target="tpu_custom_call", output_to_operand_aliasing={{0}: (9, {}), {1}: (10, {})} | custom-call | flops 1342177280 | bytes 2097152 | tf_op jit(solution)/shard_map/near_0/pallas_call | solution.py:347
  74.0 4.3 %far_round_2.1 = (f32[13,64,128]{2,1,0:T(8,128)S(1)}, f32[13,64,128]{2,1,0:T(8,128)S(1)}) custom-call(s32[2,16,128]{2,1,0:T(8,128)S(1)} %get-tuple-element.30.own_at, s32[2,16,128]{2,1,0:T(8,128)S(1)} %collective-permute-done.other_at, bf16[26,64,128]{2,1,0:T(8,128)(2,1)S(1)} %pad_maximum_fusion.line_ref, ...), custom_call_target="tpu_custom_call" | custom-call | flops 218103808 | bytes 2097152 | tf_op jit(solution)/shard_map/far_round_2/pallas_call | solution.py:278
  78.3 4.4 %collective-permute-start.17 = (f32[13,64,128]{2,1,0:T(8,128)S(1)}, f32[13,64,128]{2,1,0:T(8,128)S(1)}, u32[]{:S(2)}, u32[]{:S(2)}) collective-permute-start(f32[13,64,128]{2,1,0:T(8,128)S(1)} %get-tuple-element.53), channel_id=1, source_target_pairs={{0,1},{1,0},{2,3},{3,2},{4,5},{5,4},{6,7},{7,6},{8,9},{9,8},{10,11... | collective-permute-start | bytes 1277960 | tf_op jit(solution)/shard_map/ppermute | solution.py:42
  84.1 1.4 %copy-done.3 = bf16[6144,128]{1,0:T(8,128)(2,1)S(1)} copy-done((bf16[6144,128]{1,0:T(8,128)(2,1)S(1)}, bf16[6144,128]{1,0:T(8,128)(2,1)}, u32[]{:S(2)}) %copy-start.3) | copy-done | bytes 1572888
  85.5 1.4 %copy-done.5 = bf16[6144,64]{1,0:T(8,128)(2,1)S(1)} copy-done((bf16[6144,64]{1,0:T(8,128)(2,1)S(1)}, bf16[6144,64]{1,0:T(8,128)(2,1)}, u32[]{:S(2)}) %copy-start.5) | copy-done | bytes 786456
  87.0 2.7 %local_and_field.1 = bf16[6144,128]{1,0:T(8,128)(2,1)} custom-call(f32[13,64,128]{2,1,0:T(8,128)S(1)} %get-tuple-element.52.own_ref, f32[13,64,128]{2,1,0:T(8,128)S(1)} %collective-permute-done.17.other_ref, bf16[12,64,64]{2,1,0:T(8,128)(2,1)S(1)} %bitcast.2, bf16[6144,128]{1,0:T(8,128)(2,1)S(1)} %copy-done.3, bf16[6144,64]{1,0:T(8,128)(2,1)S(1)} %copy-done.5), custom_call_target="tpu_custom_call" | custom-call | flops 100663296 | bytes 4194304 | tf_op jit(solution)/shard_map/local_and_field/pallas_call | solution.py:388
  (69 shorter events, 14.4 us)
Async XLA Ops:
  4.2 12.8 %copy-start.16 = (s32[12,512]{1,0:T(8,128)S(1)}, s32[12,512]{1,0:T(8,128)}, u32[]{:S(2)}) copy-start(s32[12,512]{1,0:T(8,128)} %order_ref.9) | copy-start | bytes 73732
  4.2 12.8 %copy-start.19 = (s32[12,16]{1,0:T(8,128)S(1)}, s32[12,16]{1,0:T(8,128)}, u32[]{:S(2)}) copy-start(s32[12,16]{1,0:T(8,128)} %owner_ref.1) | copy-start | bytes 2308
  4.2 12.8 %copy-start.20 = (s32[12,16]{1,0:T(8,128)S(1)}, s32[12,16]{1,0:T(8,128)}, u32[]{:S(2)}) copy-start(s32[12,16]{1,0:T(8,128)} %leaf_ref.1) | copy-start | bytes 2308
  11.0 11.9 %collective-permute-start.1 = (bf16[13,64,128]{2,1,0:T(8,128)(2,1)}, bf16[13,64,128]{2,1,0:T(8,128)(2,1)}, u32[]{:S(2)}, u32[]{:S(2)}) collective-permute-start(bf16[13,64,128]{2,1,0:T(8,128)(2,1)} %get-tuple-element.31.line_ref), channel_id=1, source_target_pairs={{0,8},{1,9},{2,10},{3,11},{4,12},{5,13},{6,14},{7,15},{8,24},{9,25... | collective-permute-start | bytes 638984 | tf_op jit(solution)/shard_map/ppermute | solution.py:42
  14.0 12.3 %collective-permute-start.4 = (bf16[13,64,128]{2,1,0:T(8,128)(2,1)}, bf16[13,64,128]{2,1,0:T(8,128)(2,1)S(1)}, u32[]{:S(2)}, u32[]{:S(2)}) collective-permute-start(bf16[13,64,128]{2,1,0:T(8,128)(2,1)} %get-tuple-element.31.line_ref), channel_id=1, source_target_pairs={{0,2},{1,3},{2,0},{3,1},{4,6},{5,7},{6,4},{7,5},{8,10},{9,11},{10,... | collective-permute-start | bytes 638984 | tf_op jit(solution)/shard_map/ppermute | solution.py:42
  15.5 10.8 %collective-permute-start.5 = (bf16[13,64,128]{2,1,0:T(8,128)(2,1)}, bf16[13,64,128]{2,1,0:T(8,128)(2,1)}, u32[]{:S(2)}, u32[]{:S(2)}) collective-permute-start(bf16[13,64,128]{2,1,0:T(8,128)(2,1)} %get-tuple-element.31.line_ref), channel_id=1, source_target_pairs={{0,4},{1,5},{2,6},{3,7},{4,0},{5,1},{6,2},{7,3},{8,12},{9,13},{10,... | collective-permute-start | bytes 638984 | tf_op jit(solution)/shard_map/ppermute | solution.py:42
  17.0 41.8 %collective-permute-start.12 = (bf16[12,16,64,64]{3,2,1,0:T(8,128)(2,1)}, bf16[12,16,64,64]{3,2,1,0:T(8,128)(2,1)}, u32[]{:S(2)}, u32[]{:S(2)}) collective-permute-start(bf16[12,16,64,64]{3,2,1,0:T(8,128)(2,1)} %own_coupling.5), channel_id=1, source_target_pairs={{0,1},{1,0},{2,3},{3,2},{4,5},{5,4},{6,7},{7,6},{8,9},{9,8},{10,11... | collective-permute-start | bytes 4718600 | tf_op jit(solution)/shard_map/ppermute | solution.py:42
  18.4 15.6 %copy-start.1 = (bf16[512,1536]{1,0:T(8,128)(2,1)S(1)}, bf16[512,1536]{1,0:T(8,128)(2,1)}, u32[]{:S(2)}) copy-start(bf16[512,1536]{1,0:T(8,128)(2,1)} %constant.20.clone.table_ref) | copy-start | bytes 4718596
  22.9 8.9 %collective-permute-start.2 = (bf16[13,64,128]{2,1,0:T(8,128)(2,1)}, bf16[13,64,128]{2,1,0:T(8,128)(2,1)}, u32[]{:S(2)}, u32[]{:S(2)}) collective-permute-start(bf16[13,64,128]{2,1,0:T(8,128)(2,1)} %collective-permute-done.1.line_ref), channel_id=1, source_target_pairs={{0,8},{1,9},{2,10},{3,11},{4,12},{5,13},{6,14},{7,15},{8,24},{9,25... | collective-permute-start | bytes 638984 | tf_op jit(solution)/shard_map/ppermute | solution.py:42
  26.3 15.6 %collective-permute-start.10 = (bf16[13,64,128]{2,1,0:T(8,128)(2,1)}, bf16[13,64,128]{2,1,0:T(8,128)(2,1)S(1)}, u32[]{:S(2)}, u32[]{:S(2)}) collective-permute-start(bf16[13,64,128]{2,1,0:T(8,128)(2,1)} %collective-permute-done.1.line_ref), channel_id=1, source_target_pairs={{0,4},{1,5},{2,6},{3,7},{4,0},{5,1},{6,2},{7,3},{8,12},{9,13},{10,... | collective-permute-start | bytes 638984 | tf_op jit(solution)/shard_map/ppermute | solution.py:42
  26.9 15.0 %collective-permute-start.9 = (bf16[13,64,128]{2,1,0:T(8,128)(2,1)}, bf16[13,64,128]{2,1,0:T(8,128)(2,1)S(1)}, u32[]{:S(2)}, u32[]{:S(2)}) collective-permute-start(bf16[13,64,128]{2,1,0:T(8,128)(2,1)} %collective-permute-done.1.line_ref), channel_id=1, source_target_pairs={{0,2},{1,3},{2,0},{3,1},{4,6},{5,7},{6,4},{7,5},{8,10},{9,11},{10,... | collective-permute-start | bytes 638984 | tf_op jit(solution)/shard_map/ppermute | solution.py:42
  31.8 8.0 %collective-permute-start.3 = (bf16[13,64,128]{2,1,0:T(8,128)(2,1)}, bf16[13,64,128]{2,1,0:T(8,128)(2,1)S(1)}, u32[]{:S(2)}, u32[]{:S(2)}) collective-permute-start(bf16[13,64,128]{2,1,0:T(8,128)(2,1)} %collective-permute-done.2), channel_id=1, source_target_pairs={{0,8},{1,9},{2,10},{3,11},{4,12},{5,13},{6,14},{7,15},{8,24},{9,25... | collective-permute-start | bytes 638984 | tf_op jit(solution)/shard_map/ppermute | solution.py:42
  33.5 7.2 %collective-permute-start.6 = (bf16[13,64,128]{2,1,0:T(8,128)(2,1)S(1)}, bf16[13,64,128]{2,1,0:T(8,128)(2,1)S(1)}, u32[]{:S(2)}, u32[]{:S(2)}) collective-permute-start(bf16[13,64,128]{2,1,0:T(8,128)(2,1)S(1)} %broadcast_select_fusion.2), channel_id=1, source_target_pairs={{0,4},{1,3},{2,6},{3,1},{4,0},{5,7},{6,2},{7,5},{8,12},{9,11},{10,... | collective-permute-start | bytes 638984 | tf_op jit(solution)/shard_map/ppermute | solution.py:42
  35.2 20.0 %copy-start.9 = (bf16[1,32,64,64]{3,2,1,0:T(8,128)(2,1)S(1)}, bf16[1,32,64,64]{3,2,1,0:T(8,128)(2,1)}, u32[]{:S(2)}) copy-start(bf16[1,32,64,64]{3,2,1,0:T(8,128)(2,1)} %own_top.5) | copy-start | bytes 786436
  40.8 18.0 %collective-permute-start.7 = (bf16[26,64,128]{2,1,0:T(8,128)(2,1)S(1)}, bf16[26,64,128]{2,1,0:T(8,128)(2,1)S(1)}, u32[]{:S(2)}, u32[]{:S(2)}) collective-permute-start(bf16[26,64,128]{2,1,0:T(8,128)(2,1)S(1)} %pad_maximum_fusion.line_ref), channel_id=1, source_target_pairs={{0,2},{1,3},{2,0},{3,1},{4,6},{5,7},{6,4},{7,5},{8,10},{9,11},{10,... | collective-permute-start | bytes 1277960 | tf_op jit(solution)/shard_map/ppermute | solution.py:42
  41.4 17.4 %collective-permute-start.8 = (bf16[26,64,128]{2,1,0:T(8,128)(2,1)S(1)}, bf16[26,64,128]{2,1,0:T(8,128)(2,1)S(1)}, u32[]{:S(2)}, u32[]{:S(2)}) collective-permute-start(bf16[26,64,128]{2,1,0:T(8,128)(2,1)S(1)} %pad_maximum_fusion.line_ref), channel_id=1, source_target_pairs={{0,4},{1,5},{2,6},{3,7},{4,0},{5,1},{6,2},{7,3},{8,12},{9,13},{10,... | collective-permute-start | bytes 1277960 | tf_op jit(solution)/shard_map/ppermute | solution.py:42
  41.9 13.2 %collective-permute-start.11 = (bf16[13,64,128]{2,1,0:T(8,128)(2,1)S(1)}, bf16[13,64,128]{2,1,0:T(8,128)(2,1)S(1)}, u32[]{:S(2)}, u32[]{:S(2)}) collective-permute-start(bf16[13,64,128]{2,1,0:T(8,128)(2,1)S(1)} %broadcast_select_fusion.1), channel_id=1, source_target_pairs={{0,4},{1,3},{2,6},{3,1},{4,0},{5,7},{6,2},{7,5},{8,12},{9,11},{10,... | collective-permute-start | bytes 638984 | tf_op jit(solution)/shard_map/ppermute | solution.py:42
  43.5 15.3 %collective-permute-start = (s32[2,16,128]{2,1,0:T(8,128)S(1)}, s32[2,16,128]{2,1,0:T(8,128)S(1)}, u32[]{:S(2)}, u32[]{:S(2)}) collective-permute-start(s32[2,16,128]{2,1,0:T(8,128)S(1)} %get-tuple-element.30.own_at), channel_id=1, source_target_pairs={{0,1},{1,0},{2,3},{3,2},{4,5},{5,4},{6,7},{7,6},{8,9},{9,8},{10,11... | collective-permute-start | bytes 49160 | tf_op jit(solution)/shard_map/ppermute | solution.py:42
  55.2 3.7 %collective-permute-start.13 = (bf16[1,32,64,64]{3,2,1,0:T(8,128)(2,1)S(1)}, bf16[1,32,64,64]{3,2,1,0:T(8,128)(2,1)S(1)}, u32[]{:S(2)}, u32[]{:S(2)}) collective-permute-start(bf16[1,32,64,64]{3,2,1,0:T(8,128)(2,1)S(1)} %copy-done.9), channel_id=1, source_target_pairs={{0,1},{1,0},{2,3},{3,2},{4,5},{5,4},{6,7},{7,6},{8,9},{9,8},{10,11... | collective-permute-start | bytes 786440 | tf_op jit(solution)/shard_map/ppermute | solution.py:42
  64.5 9.5 %collective-permute-start.14 = (bf16[26,64,128]{2,1,0:T(8,128)(2,1)S(1)}, bf16[26,64,128]{2,1,0:T(8,128)(2,1)S(1)}, u32[]{:S(2)}, u32[]{:S(2)}) collective-permute-start(bf16[26,64,128]{2,1,0:T(8,128)(2,1)S(1)} %broadcast_select_fusion), channel_id=1, source_target_pairs={{0,4},{1,3},{2,6},{3,1},{4,0},{5,7},{6,2},{7,5},{8,12},{9,11},{10,... | collective-permute-start | bytes 1277960 | tf_op jit(solution)/shard_map/ppermute | solution.py:42
  65.0 3.4 %collective-permute-start.15 = (bf16[512,128]{1,0:T(8,128)(2,1)S(1)}, bf16[512,128]{1,0:T(8,128)(2,1)S(1)}, u32[]{:S(2)}, u32[]{:S(2)}) collective-permute-start(bf16[512,128]{1,0:T(8,128)(2,1)S(1)} %copy-done.18), channel_id=1, source_target_pairs={{0,1},{1,2},{2,3},{3,4},{4,5},{5,6},{6,7},{7,8},{8,9},{9,10},{10,1... | collective-permute-start | bytes 393224 | tf_op jit(solution)/shard_map/ppermute | solution.py:449
  67.2 3.2 %collective-permute-start.16 = (bf16[512,128]{1,0:T(8,128)(2,1)S(1)}, bf16[512,128]{1,0:T(8,128)(2,1)S(1)}, u32[]{:S(2)}, u32[]{:S(2)}) collective-permute-start(bf16[512,128]{1,0:T(8,128)(2,1)S(1)} %get-tuple-element.47), channel_id=1, source_target_pairs={{1,0},{2,1},{3,2},{4,3},{5,4},{6,5},{7,6},{8,7},{9,8},{10,9},{11,1... | collective-permute-start | bytes 393224 | tf_op jit(solution)/shard_map/ppermute | solution.py:450
  74.0 8.7 %copy-start.13 = (bf16[12,64,64]{2,1,0:T(8,128)(2,1)S(1)}, bf16[12,64,64]{2,1,0:T(8,128)(2,1)}, u32[]{:S(2)}) copy-start(bf16[12,64,64]{2,1,0:T(8,128)(2,1)} %transfer_ref.1) | copy-start | bytes 294916
  78.3 5.8 %collective-permute-start.17 = (f32[13,64,128]{2,1,0:T(8,128)S(1)}, f32[13,64,128]{2,1,0:T(8,128)S(1)}, u32[]{:S(2)}, u32[]{:S(2)}) collective-permute-start(f32[13,64,128]{2,1,0:T(8,128)S(1)} %get-tuple-element.53), channel_id=1, source_target_pairs={{0,1},{1,0},{2,3},{3,2},{4,5},{5,4},{6,7},{7,6},{8,9},{9,8},{10,11... | collective-permute-start | bytes 1277960 | tf_op jit(solution)/shard_map/ppermute | solution.py:42
  (15 other events, 35.5 us)

commit v4 on v3

--- a/solution.py
+++ b/solution.py
@@ -33,10 +33,6 @@
     return np.concatenate(tables, axis=1)
 
 
-def ring_order(layers):
-    return [0] + list(range(1, layers, 2)) + list(range(layers - 2, 0, -2))
-
-
 def send(block, target):
     count = lax.axis_size("subtree")
     return lax.ppermute(block, "subtree", [(d, target(d)) for d in range(count)])
@@ -58,11 +54,9 @@
     return send(block, lambda d: d ^ (2 if d % 2 else 4))
 
 
-def along_z(block):
+def along_z(block, step):
     layers = lax.axis_size("subtree") // 8
-    order = ring_order(layers)
-    following = {order[i]: order[(i + 1) % layers] for i in range(layers)}
-    return send(block, lambda d: following[d // 8] * 8 + d % 8)
+    return send(block, lambda d: (d // 8 + step) % layers * 8 + d % 8)
 
 
 def params(mib):
@@ -83,6 +77,26 @@
 
 def dot(a, b):
     return jnp.dot(a, b, preferred_element_type=F32)
+
+
+def in_hbm(*arrays):
+    return [pltpu.with_memory_space_constraint(array, pltpu.HBM) for array in arrays]
+
+
+def hbm(shape, dtype):
+    return pltpu.HBM(shape, dtype)
+
+
+def one_hot_leaf(row, leaf_len):
+    column = jnp.broadcast_to(row, (128, leaf_len)).T
+    lanes = lax.broadcasted_iota(jnp.int32, (leaf_len, 128), 1)
+    return jnp.concatenate(
+        [
+            jnp.where(column == lanes + 128 * t, 1.0, 0.0).astype(BF)
+            for t in range(leaf_len // 128)
+        ],
+        axis=1,
+    )
 
 
 def one_hot_grid(row, leaf_len):
@@ -99,16 +113,17 @@
     def _():
         root_ref[...] = jnp.zeros_like(root_ref)
 
+    hots = [one_hot_leaf(order_ref[pl.ds(step * per + i, 1), :], leaf_len) for i in range(per)]
+    placed = [dot(basis_ref[i], hots[i]).astype(BF) for i in range(per)]
+    skeletons = [
+        dot(placed[i], comp_ref[i * leaf_len:(i + 1) * leaf_len, :]).astype(BF)
+        for i in range(per)
+    ]
+    across = jnp.concatenate([transfer_ref[i] for i in range(per)], axis=1)
+    root_ref[...] += dot(across, jnp.concatenate(skeletons, axis=0))
     for i in range(per):
-        leaf = step * per + i
-        hot = one_hot_grid(order_ref[pl.ds(leaf, 1), :], leaf_len)
-        placed = lax.dot_general(
-            basis_ref[i], hot, (((1,), (1,)), ((), ())), preferred_element_type=F32
-        ).astype(BF)
-        placed_ref[i] = placed
-        skeleton = dot(placed, comp_ref[pl.ds(i * leaf_len, leaf_len), :]).astype(BF)
-        shared_ref[pl.ds(leaf + 1, 1)] = skeleton[None]
-        root_ref[...] += dot(transfer_ref[i], skeleton)
+        placed_ref[i] = placed[i]
+        shared_ref[pl.ds(step * per + i + 1, 1)] = skeletons[i][None]
 
     @pl.when(step == pl.num_programs(0) - 1)
     def _():
@@ -133,13 +148,13 @@
             pl.BlockSpec((leaves + 1, rank, fields), lambda s: (0, 0, 0)),
         ],
         out_shape=[
-            jax.ShapeDtypeStruct((leaves, rank, leaf_len), BF),
+            hbm((leaves, rank, leaf_len), BF),
             jax.ShapeDtypeStruct((leaves + 1, rank, fields), BF),
         ],
         scratch_shapes=[pltpu.VMEM((rank, fields), F32)],
         compiler_params=params(16),
         cost_estimate=cost(leaves * leaf_len * leaf_len * rank * 2, 4 * MIB),
-    )(leaf_order, composition, leaf_basis, transfer)
+    )(*in_hbm(leaf_order, composition, leaf_basis, transfer))
 
 
 def owner_tables(me, layers, owners, blocks):
@@ -151,11 +166,8 @@
     plane = (lane >= slots).astype(jnp.int32)
     slot = lane - plane * slots
     layer, chip, core = me // 8, (me // 2) & 3, me & 1
-    half = layers // 2
-    at = jnp.where(layer & 1 > 0, (layer + 1) // 2, jnp.where(layer > 0, layers - layer // 2, 0))
-    back = at - (slot >> 2)
-    back = jnp.where(back < 0, back + layers, back)
-    source = jnp.where(back == 0, 0, jnp.where(back <= half, 2 * back - 1, 2 * (layers - back)))
+    source = layer - (slot >> 2)
+    source = jnp.where(source < 0, source + layers, source)
     owner = source * 8 + (chip ^ (slot & 3)) * 2 + (core ^ plane)
     row = lax.broadcasted_iota(jnp.int32, shape, 0)
     distant = jnp.abs(owner - me) >= 2
@@ -176,16 +188,7 @@
     step = pl.program_id(0)
     leaf_len = order_ref.shape[1]
     for i in range(per):
-        row = order_ref[pl.ds(step * per + i, 1), :]
-        column = jnp.broadcast_to(row, (128, leaf_len)).T
-        lanes = lax.broadcasted_iota(jnp.int32, (leaf_len, 128), 1)
-        hot = jnp.concatenate(
-            [
-                jnp.where(column == lanes + 128 * t, 1.0, 0.0).astype(BF)
-                for t in range(leaf_len // 128)
-            ],
-            axis=1,
-        )
+        hot = one_hot_leaf(order_ref[pl.ds(step * per + i, 1), :], leaf_len)
         at = pl.ds(i * leaf_len, leaf_len)
         ordered = dot(hot, comp_ref[at, :]).astype(BF)
         ordered_ref[at, :] = ordered
@@ -229,59 +232,98 @@
             pl.BlockSpec((2, 16, 128), lambda s: (0, 0, 0)),
         ],
         out_shape=[
-            jax.ShapeDtypeStruct((leaves * leaf_len, fields), BF),
+            hbm((leaves * leaf_len, fields), BF),
             edge,
             edge,
             jax.ShapeDtypeStruct((2, 16, 128), jnp.int32),
         ],
         compiler_params=params(16),
         cost_estimate=cost(leaves * leaf_len * leaf_len * fields * 2, 4 * MIB),
-    )(me, leaf_order, composition, owners, blocks)
+    )(me, *in_hbm(leaf_order, composition, owners, blocks))
+
+
+def dense_kernel(per, slots, table_ref, coupling_ref, top_ref, own_ref, other_ref):
+    step = pl.program_id(0)
+    rank = coupling_ref.shape[2]
+    leaves = own_ref.shape[0] - 1
+
+    def fill(out_ref, plane, row, entry_row, block_of):
+        for slot in range(0, slots, 2):
+            pair = []
+            for one in (slot, slot + 1):
+                entry = table_ref[0, entry_row, plane * slots + one]
+                block = block_of(jnp.maximum(entry, 0))
+                pair.append(jnp.where(entry >= 0, block, jnp.zeros_like(block)))
+            out_ref[row, :, slot * rank:(slot + 2) * rank] = jnp.concatenate(pair, axis=1)
+
+    for plane, out_ref in ((0, own_ref), (1, other_ref)):
+        for i in range(per):
+            leaf = step * per + i
+            fill(out_ref, plane, leaf, leaf + 1, lambda entry, i=i: coupling_ref[i, entry])
+
+        @pl.when(step == pl.num_programs(0) - 1)
+        def _(plane=plane, out_ref=out_ref):
+            fill(out_ref, plane, leaves, 0, lambda entry: top_ref[0, entry])
+
+
+def dense_couplings(table, coupling, top_coupling, slots, per=4):
+    leaves, entries, rank, _ = coupling.shape
+    shape = jax.ShapeDtypeStruct((leaves + 1, rank, slots * rank), BF)
+    full = pl.BlockSpec((leaves + 1, rank, slots * rank), lambda s: (0, 0, 0))
+    return pl.pallas_call(
+        functools.partial(dense_kernel, per, slots),
+        name="couplings_by_owner",
+        grid=(leaves // per,),
+        in_specs=[
+            scalars(),
+            pl.BlockSpec((per, entries, rank, rank), lambda s: (s, 0, 0, 0)),
+            pl.BlockSpec(top_coupling.shape, lambda s: (0, 0, 0, 0)),
+        ],
+        out_specs=[full, full],
+        out_shape=[shape, shape],
+        compiler_params=params(16 if slots <= 16 else 48),
+        cost_estimate=cost(0, 8 * MIB),
+    )(table, *in_hbm(coupling, top_coupling))
 
 
 def round_kernel(first, steps, slots, own_at, other_at, line_ref, x_ref, y_ref, far_ref,
-                 own_coupling, own_top, other_coupling, other_top, *refs):
+                 own_blocks, other_blocks, *refs):
     if first:
         own_out, other_out = refs
     else:
         own_in, other_in, own_out, other_out = refs
-    rows = own_out.shape[0]
+    rows, rank, _ = own_out.shape
     sides = (line_ref, x_ref, y_ref, far_ref)
-    for plane, at_ref, coupling_ref, top_ref, out in (
-        (0, own_at, own_coupling, own_top, own_out),
-        (1, other_at, other_coupling, other_top, other_out),
+    low, high = steps[0] * 4 * rank, (steps[-1] + 1) * 4 * rank
+    for plane, at_ref, blocks_ref, out in (
+        (0, own_at, own_blocks, own_out),
+        (1, other_at, other_blocks, other_out),
     ):
         for row in range(rows):
-            value = None
-            for place, step in enumerate(steps):
-                left, right = [], []
-                for q, side in enumerate(sides):
-                    lane = plane * slots + step * 4 + q
-                    entry = at_ref[0, row, lane]
-                    safe = jnp.maximum(entry, 0)
-                    block = top_ref[0, safe] if row == 0 else coupling_ref[row - 1, safe]
-                    left.append(jnp.where(entry >= 0, block, jnp.zeros_like(block)))
-                    right.append(side[place * rows + at_ref[1, row, lane]])
-                part = dot(jnp.concatenate(left, axis=1), jnp.concatenate(right, axis=0))
-                value = part if value is None else value + part
+            chosen = [
+                side[place * rows + at_ref[1, (row + 1) % rows, plane * slots + step * 4 + q]]
+                for place, step in enumerate(steps)
+                for q, side in enumerate(sides)
+            ]
+            value = dot(blocks_ref[row, :, low:high], jnp.concatenate(chosen, axis=0))
             if not first:
                 value = value + (own_in if plane == 0 else other_in)[row]
             out[row] = value
 
 
-def far_round(steps, slots, own_at, other_at, parts, couplings, sums):
-    rows = couplings[0].shape[0] + 1
-    rank, fields = parts[0].shape[1:]
+def far_round(steps, slots, own_at, other_at, parts, blocks, sums):
+    rows, rank, _ = blocks[0].shape
+    fields = parts[0].shape[2]
     first = sums is None
     sum_shape = jax.ShapeDtypeStruct((rows, rank, fields), F32)
-    args = list(parts) + list(couplings) + ([] if first else list(sums))
+    args = list(parts) + list(blocks) + ([] if first else list(sums))
     return pl.pallas_call(
         functools.partial(round_kernel, first, steps, slots),
         name="far_round_" + str(steps[0]),
         in_specs=[scalars(), scalars()] + [whole()] * len(args),
         out_specs=[whole(), whole()],
         out_shape=[sum_shape, sum_shape],
-        compiler_params=params(16),
+        compiler_params=params(16 if slots <= 16 else 48),
         cost_estimate=cost(2 * rows * rank * 4 * rank * fields * 2 * len(steps), 2 * MIB),
     )(own_at, other_at, *args)
 
@@ -300,7 +342,7 @@
         following = jnp.where(pair == last_pair, after_ref[...], following)
 
     def masked(leaf, side, value):
-        return jnp.where(mask_ref[leaf, side] > 0, value, jnp.zeros_like(value))
+        return jnp.where(mask_ref[side, leaf] > 0, value, jnp.zeros_like(value))
 
     left = jnp.concatenate(
         [masked(2 * pair, 0, prev), low, masked(2 * pair, 1, high)], axis=0
@@ -335,7 +377,7 @@
         pl.BlockSpec((2 * leaf_len, fields), lambda s: (pair_of(s), 0)),
         pl.BlockSpec((leaf_len, fields), lambda s: (jnp.minimum(2 * pair_of(s) + 2, leaves - 1), 0)),
     ]
-    args = [near_list, leaf_order, tables, placed, ordered, ordered, ordered]
+    args = [near_list.T] + in_hbm(leaf_order, tables, placed, ordered, ordered, ordered)
     aliases = {}
     if halos is not None:
         in_specs += [pl.BlockSpec((leaf_len, fields), lambda s: (0, 0))] * 2
@@ -343,7 +385,7 @@
     if filled is not None:
         aliases = {len(args): 0, len(args) + 1: 1}
         in_specs += [pl.BlockSpec(memory_space=pl.ANY)] * 2
-        args += list(filled)
+        args += in_hbm(*filled)
     return pl.pallas_call(
         functools.partial(near_kernel, halos is not None, pair_of, last),
         name="near_" + str(pairs[0]),
@@ -354,8 +396,8 @@
             pl.BlockSpec((2 * leaf_len, rank), lambda s: (pair_of(s), 0)),
         ],
         out_shape=[
-            jax.ShapeDtypeStruct((leaves * leaf_len, fields), BF),
-            jax.ShapeDtypeStruct((leaves * leaf_len, rank), BF),
+            hbm((leaves * leaf_len, fields), BF),
+            hbm((leaves * leaf_len, rank), BF),
         ],
         input_output_aliases=aliases,
         compiler_params=params(16),
@@ -366,7 +408,8 @@
 def field_kernel(per, own_ref, other_ref, turned_transfer_ref, near_ref, turned_ref, out_ref):
     step = pl.program_id(0)
     leaf_len = near_ref.shape[0] // per
-    local = own_ref[0] + other_ref[0]
+    root = own_ref.shape[0] - 1
+    local = own_ref[root] + other_ref[root]
     coarse = local.astype(BF)
     fine = (local - coarse.astype(F32)).astype(BF)
     both = jnp.concatenate([coarse, fine], axis=1)
@@ -374,7 +417,7 @@
     for i in range(per):
         leaf = step * per + i
         down = dot(turned_transfer_ref[i], both)
-        value = own_ref[leaf + 1] + other_ref[leaf + 1] + (down[:, :fields] + down[:, fields:])
+        value = own_ref[leaf] + other_ref[leaf] + (down[:, :fields] + down[:, fields:])
         at = pl.ds(i * leaf_len, leaf_len)
         far = dot(turned_ref[at, :], value.astype(BF))
         out_ref[at, :] = (near_ref[at, :].astype(F32) + far).astype(BF)
@@ -400,7 +443,7 @@
         out_shape=jax.ShapeDtypeStruct(near.shape, BF),
         compiler_params=params(16),
         cost_estimate=cost(leaves * leaf_len * rank * fields * 2, 4 * MIB),
-    )(own, other, turned_transfer, near, turned)
+    )(own, other, turned_transfer, *in_hbm(near, turned))
 
 
 def after(block, *others):
@@ -435,37 +478,38 @@
         chosen = jnp.where(even, parts[1], parts[2])
         return parts + (onward(after(chosen, *others)),)
 
-    near_plane = plane(shared)
-    line = along_z(shared)
+    half = layers // 2
+    lines = [shared, along_z(shared, 1)]
     ordered, first, last, table = in_order(
         my_index.reshape(1), leaf_order, composition, admissible_owner, admissible_leaf, layers
     )
-    line = after(line, table)
-    lines = [along_z(line)]
-    next_plane = plane(after(line, near_plane[1], near_plane[2]))
-    round_0 = diagonal(near_plane)
-    for _ in range(layers - 3):
-        lines.append(along_z(lines[-1]))
+    for step in range(2, layers):
+        lines.append(along_z(after(shared, table), step))
+    planes = plane(after(jnp.concatenate(lines[:half], axis=0), table))
+    tables = jnp.asarray(near_tables(leaf_len))
+    near_args = (near_list, leaf_order, tables, placed)
+    pairs = leaves // 2
+    cut = pairs // 2
+    filled = near_field(list(range(1, cut)), *near_args, ordered)
+    own_blocks, my_other = dense_couplings(after(table, filled[0]), coupling, top_coupling, slots)
+    other_blocks = over_core(my_other)
+    round_0 = diagonal(planes)
+
+    planes = plane(
+        after(jnp.concatenate(lines[half:], axis=0), planes[1], planes[2], my_other, filled[0])
+    )
+    other_table = over_core(table)
     before = lax.ppermute(last, "subtree", [(d, d + 1) for d in range(count - 1)])
     behind = lax.ppermute(first, "subtree", [(d + 1, d) for d in range(count - 1)])
-    couplings = (coupling, top_coupling, over_core(coupling), over_core(top_coupling))
-    other_table = over_core(table)
-
-    tables = jnp.asarray(near_tables(leaf_len))
-    near_args = (near_list, leaf_order, tables, placed, ordered)
-    pairs = leaves // 2
-    cut = pairs // 2
-    filled = near_field(list(range(1, cut)), *near_args)
-    round_1 = diagonal(next_plane, filled[0])
-    last_plane = plane(after(jnp.concatenate(lines, axis=0), round_0[3], filled[0]))
-    near_args = (near_list, leaf_order, tables, placed, after(ordered, round_1[3]))
-    filled = near_field(list(range(cut, pairs - 1)), *near_args, filled=filled)
-    sums = far_round([0], slots, table, other_table, round_0, couplings, None)
-    sums = far_round([1], slots, table, other_table, round_1, couplings, sums)
-    round_2 = diagonal(last_plane, sums[0], filled[0])
-    filled = near_field([0, pairs - 1], *near_args, halos=(before, behind), filled=filled)
-    round_2 = round_2[:3] + (after(round_2[3], filled[0]),)
-    sums = far_round(list(range(2, layers)), slots, table, other_table, round_2, couplings, sums)
+    blocks = (own_blocks, other_blocks)
+    filled = near_field(
+        list(range(cut, pairs - 1)), *near_args, after(ordered, other_table, before, behind), filled=filled
+    )
+    round_1 = diagonal(planes, filled[0])
+    filled = near_field([0, pairs - 1], *near_args, ordered, halos=(before, behind), filled=filled)
+    sums = far_round(list(range(half)), slots, table, other_table, round_0, blocks, None)
+    round_1 = round_1[:3] + (after(round_1[3], filled[0], sums[0]),)
+    sums = far_round(list(range(half, layers)), slots, table, other_table, round_1, blocks, sums)
     received = over_core(sums[1])
     return field(sums[0], received, transfer.transpose(0, 2, 1), *filled)
 

time: 90.9 us -> 88.1 us (0.969)
  Pallas kernels: 32.9 us -> 41 us
  waiting for transfers between devices: 20.3 us -> 14.2 us
  local copies, waits for them, and re-layouts: 12.1 us -> 6.43 us
  other arithmetic: 1.07 us -> 4 us
  starting transfers between devices: 23.1 us -> 21 us
    pallas_call x3, Pallas kernels: 10.6 us -> 16.3 us  [near_field(): pl.pallas_call(functools.partial(near_kernel, halos is not None, pair_of,...]
    unnamed x44 -> x27, local copies, waits for them, and re-layouts: 12.1 us -> 6.43 us
    pallas_call x3 -> x2, Pallas kernels: 9.81 us -> 4.42 us  [far_round(): pl.pallas_call(functools.partial(round_kernel, first, steps, slots), name...]
    pallas_call x0 -> x1, Pallas kernels: none -> 5.11 us  [dense_couplings(): pl.pallas_call(functools.partial(dense_kernel, per, slots), name='couplin...]
    ppermute x16 -> x12, waiting for transfers between devices: 18.4 us -> 14.2 us  [send(): lax.ppermute(block, 'subtree', [(d, target(d)) for d in range(count)])]
    ppermute x16 -> x12, starting transfers between devices: 19.7 us -> 17.3 us  [send(): lax.ppermute(block, 'subtree', [(d, target(d)) for d in range(count)])]
    select_n x3 -> x2, other arithmetic: 0.1 us -> 2.11 us  [diagonal(): chosen = jnp.where(even, parts[1], parts[2])]
    pallas_call x1, Pallas kernels: 3.81 us -> 5.78 us  [in_order(): pl.pallas_call(functools.partial(order_kernel, per, layers), name='cluste...]
  transfers between devices with their start and end apart: 18 -> 14, of which waited for: 5 -> 4; matrix products, arithmetic and copies ran while one was open for 2% -> 6% of each run, Pallas kernels for 16% -> 33%
where the time goes in v4:
time: 88.1 us; the launch traced here: 86.7 us
  Pallas kernels  41 us (47%)
  starting transfers between devices  21 us (24%)
  waiting for transfers between devices  14.2 us (16%)
  local copies, waits for them, and re-layouts  6.43 us (7%)
  other arithmetic  4 us (5%)
    ppermute x12, starting transfers between devices, send(): lax.ppermute(block, 'subtree', [(d, target(d)) for d in range(count)])  17.3 us
    pallas_call x3, Pallas kernels, near_field(): pl.pallas_call(functools.partial(near_kernel, halos is not None, pair_of,...  16.3 us
    ppermute x12, waiting for transfers between devices, send(): lax.ppermute(block, 'subtree', [(d, target(d)) for d in range(count)])  14.2 us
    unnamed x27, local copies, waits for them, and re-layouts  6.43 us
    pallas_call x1, Pallas kernels, in_order(): pl.pallas_call(functools.partial(order_kernel, per, layers), name='cluste...  5.78 us
    pallas_call x1, Pallas kernels, dense_couplings(): pl.pallas_call(functools.partial(dense_kernel, per, slots), name='couplin...  5.11 us
    pallas_call x1, Pallas kernels, skeletons(): pl.pallas_call(functools.partial(skeleton_kernel, per), name='basis_and_s...  4.79 us
    pallas_call x1, Pallas kernels, field(): pl.pallas_call(functools.partial(field_kernel, per), name='local_and_fiel...  4.53 us
  transfers between devices with their start and end apart: 14, of which 4 were waited for; matrix products, arithmetic and copies ran while one was open for 6% of the time, Pallas kernels for 33%

profile of v4, /device:TPU:0, one launch (start us, length us, event | category | flops | bytes accessed | tf_op | source)
XLA Modules:
  0.0 86.7 jit_solution(8699555581837225535)
XLA Ops:
  0.0 4.8 %basis_and_skeleton.1 = (bf16[12,64,512]{2,1,0:T(8,128)(2,1)}, bf16[13,64,128]{2,1,0:T(8,128)(2,1)}) custom-call(s32[12,512]{1,0:T(8,128)} %order_ref.9, bf16[6144,128]{1,0:T(8,128)(2,1)} %comp_ref.3, bf16[12,64,512]{2,1,0:T(8,128)(2,1)} %basis_ref.1, bf16[12,64,64]{2,1,0:T(8,128)(2,1)} %transfer_ref.1), custom_call_target="tpu_custom_call" | custom-call | flops 402653184 | bytes 4194304 | tf_op jit(solution)/shard_map/basis_and_skeleton/pallas_call | solution.py:136
  4.8 3.1 %collective-permute-start.3 = (bf16[13,64,128]{2,1,0:T(8,128)(2,1)}, bf16[13,64,128]{2,1,0:T(8,128)(2,1)}, u32[]{:S(2)}, u32[]{:S(2)}) collective-permute-start(bf16[13,64,128]{2,1,0:T(8,128)(2,1)} %get-tuple-element.32), channel_id=1, source_target_pairs={{0,8},{1,9},{2,10},{3,11},{4,12},{5,13},{6,14},{7,15},{8,16},{9,17... | collective-permute-start | bytes 638984 | tf_op jit(solution)/shard_map/ppermute | solution.py:38
  7.9 5.8 %cluster_order.1 = (bf16[6144,128]{1,0:T(8,128)(2,1)}, bf16[512,128]{1,0:T(8,128)(2,1)}, bf16[512,128]{1,0:T(8,128)(2,1)}, s32[2,16,128]{2,1,0:T(8,128)S(1)}) custom-call(s32[1]{0:T(128)} %bitcast.me_ref, s32[12,512]{1,0:T(8,128)} %order_ref.9, bf16[6144,128]{1,0:T(8,128)(2,1)} %comp_ref.3, s32[12,16]{1,0:T(8,128)} %owner_ref.1, s32[12,16]{1,0:T(8,128)} %leaf_ref.1), custom_call_target="tpu_custom_call" | custom-call | flops 805306368 | bytes 4194304 | tf_op jit(solution)/shard_map/cluster_order/pallas_call | solution.py:217
  13.7 5.4 %near_1.1 = (bf16[6144,128]{1,0:T(8,128)(2,1)}, bf16[6144,64]{1,0:T(8,128)(2,1)}) custom-call(s32[2,12]{1,0:T(2,128)S(1)} %bitcast.4, s32[12,512]{1,0:T(8,128)} %order_ref.9, bf16[512,1536]{1,0:T(8,128)(2,1)} %constant.20.clone.table_ref, bf16[12,64,512]{2,1,0:T(8,128)(2,1)} %get-tuple-element.34.placed_ref, ...), custom_call_target="tpu_custom_call" | custom-call | flops 1342177280 | bytes 2097152 | tf_op jit(solution)/shard_map/near_1/pallas_call | solution.py:389
  19.1 5.1 %couplings_by_owner.1 = (bf16[13,64,1024]{2,1,0:T(8,128)(2,1)S(1)}, bf16[13,64,1024]{2,1,0:T(8,128)(2,1)}) custom-call(s32[2,16,128]{2,1,0:T(8,128)S(1)} %get-tuple-element.37.table_ref.own_at, bf16[12,16,64,64]{3,2,1,0:T(8,128)(2,1)} %coupling_ref.1, bf16[1,32,64,64]{3,2,1,0:T(8,128)(2,1)} %top_ref.1), custom_call_target="tpu_custom_call" | custom-call | bytes 8388608 | tf_op jit(solution)/shard_map/couplings_by_owner/pallas_call | solution.py:273
  24.2 1.1 %pad_maximum_fusion.1.line_ref = bf16[26,64,128]{2,1,0:T(8,128)(2,1)S(1)} fusion(bf16[13,64,128]{2,1,0:T(8,128)(2,1)} %collective-permute-done.3, bf16[13,64,128]{2,1,0:T(8,128)(2,1)} %get-tuple-element.32), kind=kLoop, calls=%fused_computation.1 | loop fusion | flops 212992 | bytes 851968 | tf_op jit(solution)/shard_map/concatenate | solution.py:488
  25.3 1.6 %collective-permute-start.4 = (bf16[26,64,128]{2,1,0:T(8,128)(2,1)S(1)}, bf16[26,64,128]{2,1,0:T(8,128)(2,1)S(1)}, u32[]{:S(2)}, u32[]{:S(2)}) collective-permute-start(bf16[26,64,128]{2,1,0:T(8,128)(2,1)S(1)} %pad_maximum_fusion.1.line_ref), channel_id=1, source_target_pairs={{0,2},{1,3},{2,0},{3,1},{4,6},{5,7},{6,4},{7,5},{8,10},{9,11},{10,... | collective-permute-start | bytes 1277960 | tf_op jit(solution)/shard_map/ppermute | solution.py:38
  26.9 1.5 %collective-permute-start.5 = (bf16[26,64,128]{2,1,0:T(8,128)(2,1)S(1)}, bf16[26,64,128]{2,1,0:T(8,128)(2,1)S(1)}, u32[]{:S(2)}, u32[]{:S(2)}) collective-permute-start(bf16[26,64,128]{2,1,0:T(8,128)(2,1)S(1)} %pad_maximum_fusion.1.line_ref), channel_id=1, source_target_pairs={{0,4},{1,5},{2,6},{3,7},{4,0},{5,1},{6,2},{7,3},{8,12},{9,13},{10,... | collective-permute-start | bytes 1277960 | tf_op jit(solution)/shard_map/ppermute | solution.py:38
  29.1 2.6 %collective-permute-start.1 = (bf16[13,64,128]{2,1,0:T(8,128)(2,1)}, bf16[13,64,128]{2,1,0:T(8,128)(2,1)S(1)}, u32[]{:S(2)}, u32[]{:S(2)}) collective-permute-start(bf16[13,64,128]{2,1,0:T(8,128)(2,1)} %get-tuple-element.32), channel_id=1, source_target_pairs={{0,16},{1,17},{2,18},{3,19},{4,20},{5,21},{6,22},{7,23},{8,24},{9,... | collective-permute-start | bytes 638984 | tf_op jit(solution)/shard_map/ppermute | solution.py:38
  31.7 1.3 %collective-permute-start.2 = (bf16[13,64,128]{2,1,0:T(8,128)(2,1)}, bf16[13,64,128]{2,1,0:T(8,128)(2,1)S(1)}, u32[]{:S(2)}, u32[]{:S(2)}) collective-permute-start(bf16[13,64,128]{2,1,0:T(8,128)(2,1)} %get-tuple-element.32), channel_id=1, source_target_pairs={{0,24},{1,25},{2,26},{3,27},{4,28},{5,29},{6,30},{7,31},{8,0},{9,1... | collective-permute-start | bytes 638984 | tf_op jit(solution)/shard_map/ppermute | solution.py:38
  33.1 9.9 %collective-permute-done.1 = bf16[13,64,128]{2,1,0:T(8,128)(2,1)S(1)} collective-permute-done((bf16[13,64,128]{2,1,0:T(8,128)(2,1)}, bf16[13,64,128]{2,1,0:T(8,128)(2,1)S(1)}, u32[]{:S(2)}, u32[]{:S(2)}) %collective-permute-start.1) | collective-permute-done | bytes 213024 | tf_op jit(solution)/shard_map/ppermute | solution.py:38
  43.0 2.4 %collective-permute-start.8 = (bf16[512,128]{1,0:T(8,128)(2,1)}, bf16[512,128]{1,0:T(8,128)(2,1)S(1)}, u32[]{:S(2)}, u32[]{:S(2)}) collective-permute-start(bf16[512,128]{1,0:T(8,128)(2,1)} %get-tuple-element.40), channel_id=1, source_target_pairs={{0,1},{1,2},{2,3},{3,4},{4,5},{5,6},{6,7},{7,8},{8,9},{9,10},{10,1... | collective-permute-start | bytes 393224 | tf_op jit(solution)/shard_map/ppermute | solution.py:502
  46.2 1.3 %collective-permute-start.9 = (bf16[512,128]{1,0:T(8,128)(2,1)}, bf16[512,128]{1,0:T(8,128)(2,1)}, u32[]{:S(2)}, u32[]{:S(2)}) collective-permute-start(bf16[512,128]{1,0:T(8,128)(2,1)} %get-tuple-element.41), channel_id=1, source_target_pairs={{1,0},{2,1},{3,2},{4,3},{5,4},{6,5},{7,6},{8,7},{9,8},{10,9},{11,1... | collective-permute-start | bytes 393224 | tf_op jit(solution)/shard_map/ppermute | solution.py:503
  49.0 2.4 %collective-permute-start.6 = (bf16[26,64,128]{2,1,0:T(8,128)(2,1)}, bf16[26,64,128]{2,1,0:T(8,128)(2,1)}, u32[]{:S(2)}, u32[]{:S(2)}) collective-permute-start(bf16[26,64,128]{2,1,0:T(8,128)(2,1)} %pad_maximum_fusion.line_ref), channel_id=1, source_target_pairs={{0,2},{1,3},{2,0},{3,1},{4,6},{5,7},{6,4},{7,5},{8,10},{9,11},{10,... | collective-permute-start | bytes 1277960 | tf_op jit(solution)/shard_map/ppermute | solution.py:38
  54.0 1.2 %collective-permute-start.11 = (bf16[26,64,128]{2,1,0:T(8,128)(2,1)S(1)}, bf16[26,64,128]{2,1,0:T(8,128)(2,1)S(1)}, u32[]{:S(2)}, u32[]{:S(2)}) collective-permute-start(bf16[26,64,128]{2,1,0:T(8,128)(2,1)S(1)} %broadcast_select_fusion), channel_id=1, source_target_pairs={{0,4},{1,3},{2,6},{3,1},{4,0},{5,7},{6,2},{7,5},{8,12},{9,11},{10,... | collective-permute-start | bytes 1277960 | tf_op jit(solution)/shard_map/ppermute | solution.py:38
  55.9 5.4 %near_3.1 = (bf16[6144,128]{1,0:T(8,128)(2,1)}, bf16[6144,64]{1,0:T(8,128)(2,1)}) custom-call(s32[2,12]{1,0:T(2,128)S(1)} %bitcast.5, s32[12,512]{1,0:T(8,128)} %order_ref.9, bf16[512,1536]{1,0:T(8,128)(2,1)} %constant.20.clone.table_ref, bf16[12,64,512]{2,1,0:T(8,128)(2,1)} %get-tuple-element.34.placed_ref, ...), custom_call_target="tpu_custom_call", output_to_operand_aliasing={{0}: (7, {}), {1}: (8, {})} | custom-call | flops 1342177280 | bytes 2097152 | tf_op jit(solution)/shard_map/near_3/pallas_call | solution.py:389
  61.3 2.1 %collective-permute-done.6.x_ref = bf16[26,64,128]{2,1,0:T(8,128)(2,1)} collective-permute-done((bf16[26,64,128]{2,1,0:T(8,128)(2,1)}, bf16[26,64,128]{2,1,0:T(8,128)(2,1)}, u32[]{:S(2)}, u32[]{:S(2)}) %collective-permute-start.6) | collective-permute-done | bytes 426016 | tf_op jit(solution)/shard_map/ppermute | solution.py:38
  65.1 5.5 %near_0.1 = (bf16[6144,128]{1,0:T(8,128)(2,1)}, bf16[6144,64]{1,0:T(8,128)(2,1)}) custom-call(s32[2,12]{1,0:T(2,128)S(1)} %bitcast.6, s32[12,512]{1,0:T(8,128)} %order_ref.9, bf16[512,1536]{1,0:T(8,128)(2,1)} %constant.20.clone.table_ref, bf16[12,64,512]{2,1,0:T(8,128)(2,1)} %get-tuple-element.34.placed_ref, ...), custom_call_target="tpu_custom_call", output_to_operand_aliasing={{0}: (9, {}), {1}: (10, {})} | custom-call | flops 1342177280 | bytes 2097152 | tf_op jit(solution)/shard_map/near_0/pallas_call | solution.py:389
  70.6 1.7 %far_round_0.1 = (f32[13,64,128]{2,1,0:T(8,128)S(1)}, f32[13,64,128]{2,1,0:T(8,128)S(1)}) custom-call(s32[2,16,128]{2,1,0:T(8,128)S(1)} %get-tuple-element.37.table_ref.own_at, s32[2,16,128]{2,1,0:T(8,128)S(1)} %copy-done.9, bf16[26,64,128]{2,1,0:T(8,128)(2,1)S(1)} %copy-done.1, bf16[26,64,128]{2,1,0:T(8,128)(2,1)S(1)} %copy-done.3, ...), custom_call_target="tpu_custom_call" | custom-call | flops 218103808 | bytes 2097152 | tf_op jit(solution)/shard_map/far_round_0/pallas_call | solution.py:320
  72.4 1.7 %collective-permute-done.10.far_ref = bf16[26,64,128]{2,1,0:T(8,128)(2,1)S(1)} collective-permute-done((bf16[26,64,128]{2,1,0:T(8,128)(2,1)S(1)}, bf16[26,64,128]{2,1,0:T(8,128)(2,1)S(1)}, u32[]{:S(2)}, u32[]{:S(2)}) %collective-permute-start.10) | collective-permute-done | bytes 426016 | tf_op jit(solution)/shard_map/ppermute | solution.py:38
  74.1 2.7 %far_round_2.1 = (f32[13,64,128]{2,1,0:T(8,128)S(1)}, f32[13,64,128]{2,1,0:T(8,128)}) custom-call(s32[2,16,128]{2,1,0:T(8,128)S(1)} %get-tuple-element.37.table_ref.own_at, s32[2,16,128]{2,1,0:T(8,128)S(1)} %copy-done.9, bf16[26,64,128]{2,1,0:T(8,128)(2,1)} %pad_maximum_fusion.line_ref, bf16[26,64,128]{2,1,0:T(8,128)(2,1)} %collective-permute-done.6.x_ref, ...), custom_call_target="tpu_custom_call" | custom-call | flops 218103808 | bytes 2097152 | tf_op jit(solution)/shard_map/far_round_2/pallas_call | solution.py:320
  77.5 2.1 %collective-permute-start.13 = (f32[13,64,128]{2,1,0:T(8,128)}, f32[13,64,128]{2,1,0:T(8,128)S(1)}, u32[]{:S(2)}, u32[]{:S(2)}) collective-permute-start(f32[13,64,128]{2,1,0:T(8,128)} %get-tuple-element.53), channel_id=1, source_target_pairs={{0,1},{1,0},{2,3},{3,2},{4,5},{5,4},{6,7},{7,6},{8,9},{9,8},{10,11... | collective-permute-start | bytes 1277960 | tf_op jit(solution)/shard_map/ppermute | solution.py:38
  79.6 1.1 %copy.15 = bf16[12,64,64]{1,2,0:T(8,128)(2,1)S(1)} copy(bf16[12,64,64]{2,1,0:T(8,128)(2,1)} %transfer_ref.1) | data formatting | bytes 196608 | tf_op args[2]
  82.2 4.5 %local_and_field.1 = bf16[6144,128]{1,0:T(8,128)(2,1)} custom-call(f32[13,64,128]{2,1,0:T(8,128)S(1)} %copy-done.7, f32[13,64,128]{2,1,0:T(8,128)S(1)} %collective-permute-done.13.other_ref, bf16[12,64,64]{2,1,0:T(8,128)(2,1)S(1)} %bitcast.3, bf16[6144,128]{1,0:T(8,128)(2,1)} %get-tuple-element.47.near_ref, bf16[6144,64]{1,0:T(8,128)(2,1)} %get-tuple-element.54.turned_ref), custom_call_target="tpu_custom_call" | custom-call | flops 100663296 | bytes 4194304 | tf_op jit(solution)/shard_map/local_and_field/pallas_call | solution.py:431
  (44 shorter events, 10.4 us)
Async XLA Ops:
  4.8 8.9 %copy-start.10 = (s32[12,2]{0,1:T(2,128)S(1)}, s32[12,2]{0,1:T(2,128)}, u32[]{:S(2)}) copy-start(s32[12,2]{0,1:T(2,128)} %param.17) | copy-start | bytes 292
  4.8 19.4 %collective-permute-start.3 = (bf16[13,64,128]{2,1,0:T(8,128)(2,1)}, bf16[13,64,128]{2,1,0:T(8,128)(2,1)}, u32[]{:S(2)}, u32[]{:S(2)}) collective-permute-start(bf16[13,64,128]{2,1,0:T(8,128)(2,1)} %get-tuple-element.32), channel_id=1, source_target_pairs={{0,8},{1,9},{2,10},{3,11},{4,12},{5,13},{6,14},{7,15},{8,16},{9,17... | collective-permute-start | bytes 638984 | tf_op jit(solution)/shard_map/ppermute | solution.py:38
  24.2 46.4 %collective-permute-start.12 = (bf16[13,64,1024]{2,1,0:T(8,128)(2,1)}, bf16[13,64,1024]{2,1,0:T(8,128)(2,1)S(1)}, u32[]{:S(2)}, u32[]{:S(2)}) collective-permute-start(bf16[13,64,1024]{2,1,0:T(8,128)(2,1)} %get-tuple-element.38), channel_id=1, source_target_pairs={{0,1},{1,0},{2,3},{3,2},{4,5},{5,4},{6,7},{7,6},{8,9},{9,8},{10,11... | collective-permute-start | bytes 5111816 | tf_op jit(solution)/shard_map/ppermute | solution.py:38
  25.3 20.1 %collective-permute-start.4 = (bf16[26,64,128]{2,1,0:T(8,128)(2,1)S(1)}, bf16[26,64,128]{2,1,0:T(8,128)(2,1)S(1)}, u32[]{:S(2)}, u32[]{:S(2)}) collective-permute-start(bf16[26,64,128]{2,1,0:T(8,128)(2,1)S(1)} %pad_maximum_fusion.1.line_ref), channel_id=1, source_target_pairs={{0,2},{1,3},{2,0},{3,1},{4,6},{5,7},{6,4},{7,5},{8,10},{9,11},{10,... | collective-permute-start | bytes 1277960 | tf_op jit(solution)/shard_map/ppermute | solution.py:38
  26.9 21.4 %collective-permute-start.5 = (bf16[26,64,128]{2,1,0:T(8,128)(2,1)S(1)}, bf16[26,64,128]{2,1,0:T(8,128)(2,1)S(1)}, u32[]{:S(2)}, u32[]{:S(2)}) collective-permute-start(bf16[26,64,128]{2,1,0:T(8,128)(2,1)S(1)} %pad_maximum_fusion.1.line_ref), channel_id=1, source_target_pairs={{0,4},{1,5},{2,6},{3,7},{4,0},{5,1},{6,2},{7,3},{8,12},{9,13},{10,... | collective-permute-start | bytes 1277960 | tf_op jit(solution)/shard_map/ppermute | solution.py:38
  29.1 13.8 %collective-permute-start.1 = (bf16[13,64,128]{2,1,0:T(8,128)(2,1)}, bf16[13,64,128]{2,1,0:T(8,128)(2,1)S(1)}, u32[]{:S(2)}, u32[]{:S(2)}) collective-permute-start(bf16[13,64,128]{2,1,0:T(8,128)(2,1)} %get-tuple-element.32), channel_id=1, source_target_pairs={{0,16},{1,17},{2,18},{3,19},{4,20},{5,21},{6,22},{7,23},{8,24},{9,... | collective-permute-start | bytes 638984 | tf_op jit(solution)/shard_map/ppermute | solution.py:38
  31.7 11.3 %collective-permute-start.2 = (bf16[13,64,128]{2,1,0:T(8,128)(2,1)}, bf16[13,64,128]{2,1,0:T(8,128)(2,1)S(1)}, u32[]{:S(2)}, u32[]{:S(2)}) collective-permute-start(bf16[13,64,128]{2,1,0:T(8,128)(2,1)} %get-tuple-element.32), channel_id=1, source_target_pairs={{0,24},{1,25},{2,26},{3,27},{4,28},{5,29},{6,30},{7,31},{8,0},{9,1... | collective-permute-start | bytes 638984 | tf_op jit(solution)/shard_map/ppermute | solution.py:38
  43.0 8.5 %collective-permute-start = (s32[2,16,128]{2,1,0:T(8,128)S(1)}, s32[2,16,128]{2,1,0:T(8,128)S(1)}, u32[]{:S(2)}, u32[]{:S(2)}) collective-permute-start(s32[2,16,128]{2,1,0:T(8,128)S(1)} %get-tuple-element.37.table_ref.own_at), channel_id=1, source_target_pairs={{0,1},{1,0},{2,3},{3,2},{4,5},{5,4},{6,7},{7,6},{8,9},{9,8},{10,11... | collective-permute-start | bytes 49160 | tf_op jit(solution)/shard_map/ppermute | solution.py:38
  43.0 9.9 %collective-permute-start.8 = (bf16[512,128]{1,0:T(8,128)(2,1)}, bf16[512,128]{1,0:T(8,128)(2,1)S(1)}, u32[]{:S(2)}, u32[]{:S(2)}) collective-permute-start(bf16[512,128]{1,0:T(8,128)(2,1)} %get-tuple-element.40), channel_id=1, source_target_pairs={{0,1},{1,2},{2,3},{3,4},{4,5},{5,6},{6,7},{7,8},{8,9},{9,10},{10,1... | collective-permute-start | bytes 393224 | tf_op jit(solution)/shard_map/ppermute | solution.py:502
  45.4 0.8 copy-start.2
  46.2 6.8 %collective-permute-start.9 = (bf16[512,128]{1,0:T(8,128)(2,1)}, bf16[512,128]{1,0:T(8,128)(2,1)}, u32[]{:S(2)}, u32[]{:S(2)}) collective-permute-start(bf16[512,128]{1,0:T(8,128)(2,1)} %get-tuple-element.41), channel_id=1, source_target_pairs={{1,0},{2,1},{3,2},{4,3},{5,4},{6,5},{7,6},{8,7},{9,8},{10,9},{11,1... | collective-permute-start | bytes 393224 | tf_op jit(solution)/shard_map/ppermute | solution.py:503
  48.3 0.8 copy-start.4
  49.0 14.3 %collective-permute-start.6 = (bf16[26,64,128]{2,1,0:T(8,128)(2,1)}, bf16[26,64,128]{2,1,0:T(8,128)(2,1)}, u32[]{:S(2)}, u32[]{:S(2)}) collective-permute-start(bf16[26,64,128]{2,1,0:T(8,128)(2,1)} %pad_maximum_fusion.line_ref), channel_id=1, source_target_pairs={{0,2},{1,3},{2,0},{3,1},{4,6},{5,7},{6,4},{7,5},{8,10},{9,11},{10,... | collective-permute-start | bytes 1277960 | tf_op jit(solution)/shard_map/ppermute | solution.py:38
  52.0 11.3 %collective-permute-start.7 = (bf16[26,64,128]{2,1,0:T(8,128)(2,1)}, bf16[26,64,128]{2,1,0:T(8,128)(2,1)}, u32[]{:S(2)}, u32[]{:S(2)}) collective-permute-start(bf16[26,64,128]{2,1,0:T(8,128)(2,1)} %pad_maximum_fusion.line_ref), channel_id=1, source_target_pairs={{0,4},{1,5},{2,6},{3,7},{4,0},{5,1},{6,2},{7,3},{8,12},{9,13},{10,... | collective-permute-start | bytes 1277960 | tf_op jit(solution)/shard_map/ppermute | solution.py:38
  54.0 16.6 %collective-permute-start.11 = (bf16[26,64,128]{2,1,0:T(8,128)(2,1)S(1)}, bf16[26,64,128]{2,1,0:T(8,128)(2,1)S(1)}, u32[]{:S(2)}, u32[]{:S(2)}) collective-permute-start(bf16[26,64,128]{2,1,0:T(8,128)(2,1)S(1)} %broadcast_select_fusion), channel_id=1, source_target_pairs={{0,4},{1,3},{2,6},{3,1},{4,0},{5,7},{6,2},{7,5},{8,12},{9,11},{10,... | collective-permute-start | bytes 1277960 | tf_op jit(solution)/shard_map/ppermute | solution.py:38
  55.9 9.2 %copy-start.12 = (s32[12,2]{0,1:T(2,128)S(1)}, s32[12,2]{0,1:T(2,128)}, u32[]{:S(2)}) copy-start(s32[12,2]{0,1:T(2,128)} %param.17) | copy-start | bytes 292
  64.4 9.6 %collective-permute-start.10 = (bf16[26,64,128]{2,1,0:T(8,128)(2,1)S(1)}, bf16[26,64,128]{2,1,0:T(8,128)(2,1)S(1)}, u32[]{:S(2)}, u32[]{:S(2)}) collective-permute-start(bf16[26,64,128]{2,1,0:T(8,128)(2,1)S(1)} %broadcast_select_fusion.1), channel_id=1, source_target_pairs={{0,4},{1,3},{2,6},{3,1},{4,0},{5,7},{6,2},{7,5},{8,12},{9,11},{10,... | collective-permute-start | bytes 1277960 | tf_op jit(solution)/shard_map/ppermute | solution.py:38
  65.1 5.5 %copy-start.1 = (bf16[26,64,128]{2,1,0:T(8,128)(2,1)S(1)}, bf16[26,64,128]{2,1,0:T(8,128)(2,1)}, u32[]{:S(2)}) copy-start(bf16[26,64,128]{2,1,0:T(8,128)(2,1)} %copy-done) | copy-start | bytes 1277956
  65.1 5.5 %copy-start.3 = (bf16[26,64,128]{2,1,0:T(8,128)(2,1)S(1)}, bf16[26,64,128]{2,1,0:T(8,128)(2,1)}, u32[]{:S(2)}) copy-start(bf16[26,64,128]{2,1,0:T(8,128)(2,1)} %copy-done.2) | copy-start | bytes 1277956
  65.1 5.5 %copy-start.5 = (bf16[26,64,128]{2,1,0:T(8,128)(2,1)S(1)}, bf16[26,64,128]{2,1,0:T(8,128)(2,1)}, u32[]{:S(2)}) copy-start(bf16[26,64,128]{2,1,0:T(8,128)(2,1)} %copy-done.4) | copy-start | bytes 1277956
  65.1 5.5 %copy-start.9 = (s32[2,16,128]{2,1,0:T(8,128)S(1)}, s32[2,16,128]{2,1,0:T(8,128)}, u32[]{:S(2)}) copy-start(s32[2,16,128]{2,1,0:T(8,128)} %copy-done.8) | copy-start | bytes 49156
  76.8 0.8 copy-start.6
  77.5 3.7 %collective-permute-start.13 = (f32[13,64,128]{2,1,0:T(8,128)}, f32[13,64,128]{2,1,0:T(8,128)S(1)}, u32[]{:S(2)}, u32[]{:S(2)}) collective-permute-start(f32[13,64,128]{2,1,0:T(8,128)} %get-tuple-element.53), channel_id=1, source_target_pairs={{0,1},{1,0},{2,3},{3,2},{4,5},{5,4},{6,7},{7,6},{8,9},{9,8},{10,11... | collective-permute-start | bytes 1277960 | tf_op jit(solution)/shard_map/ppermute | solution.py:38
  81.2 1.0 %copy-start.7 = (f32[13,64,128]{2,1,0:T(8,128)S(1)}, f32[13,64,128]{2,1,0:T(8,128)}, u32[]{:S(2)}) copy-start(f32[13,64,128]{2,1,0:T(8,128)} %copy-done.6) | copy-start | bytes 1277956
  (3 other events, 2.0 us)

commit v5 on v4

--- a/solution.py
+++ b/solution.py
@@ -64,7 +64,7 @@
 
 
 def cost(flops, moved):
-    return pl.CostEstimate(flops=flops, bytes_accessed=moved, transcendentals=0)
+    return pl.CostEstimate(flops=flops // 64, bytes_accessed=moved // 64, transcendentals=0)
 
 
 def whole():
@@ -81,10 +81,6 @@
 
 def in_hbm(*arrays):
     return [pltpu.with_memory_space_constraint(array, pltpu.HBM) for array in arrays]
-
-
-def hbm(shape, dtype):
-    return pltpu.HBM(shape, dtype)
 
 
 def one_hot_leaf(row, leaf_len):
@@ -102,59 +98,6 @@
 def one_hot_grid(row, leaf_len):
     cells = lax.broadcasted_iota(jnp.int32, (leaf_len, leaf_len), 0)
     return jnp.where(cells == row, 1.0, 0.0).astype(BF)
-
-
-def skeleton_kernel(per, order_ref, comp_ref, basis_ref, transfer_ref,
-                    placed_ref, shared_ref, root_ref):
-    step = pl.program_id(0)
-    leaf_len = basis_ref.shape[2]
-
-    @pl.when(step == 0)
-    def _():
-        root_ref[...] = jnp.zeros_like(root_ref)
-
-    hots = [one_hot_leaf(order_ref[pl.ds(step * per + i, 1), :], leaf_len) for i in range(per)]
-    placed = [dot(basis_ref[i], hots[i]).astype(BF) for i in range(per)]
-    skeletons = [
-        dot(placed[i], comp_ref[i * leaf_len:(i + 1) * leaf_len, :]).astype(BF)
-        for i in range(per)
-    ]
-    across = jnp.concatenate([transfer_ref[i] for i in range(per)], axis=1)
-    root_ref[...] += dot(across, jnp.concatenate(skeletons, axis=0))
-    for i in range(per):
-        placed_ref[i] = placed[i]
-        shared_ref[pl.ds(step * per + i + 1, 1)] = skeletons[i][None]
-
-    @pl.when(step == pl.num_programs(0) - 1)
-    def _():
-        shared_ref[pl.ds(0, 1)] = root_ref[...].astype(BF)[None]
-
-
-def skeletons(leaf_order, composition, leaf_basis, transfer, per=4):
-    leaves, rank, leaf_len = leaf_basis.shape
-    fields = composition.shape[1]
-    return pl.pallas_call(
-        functools.partial(skeleton_kernel, per),
-        name="basis_and_skeleton",
-        grid=(leaves // per,),
-        in_specs=[
-            pl.BlockSpec((leaves, leaf_len), lambda s: (0, 0)),
-            pl.BlockSpec((per * leaf_len, fields), lambda s: (s, 0)),
-            pl.BlockSpec((per, rank, leaf_len), lambda s: (s, 0, 0)),
-            pl.BlockSpec((per, rank, rank), lambda s: (s, 0, 0)),
-        ],
-        out_specs=[
-            pl.BlockSpec((per, rank, leaf_len), lambda s: (s, 0, 0)),
-            pl.BlockSpec((leaves + 1, rank, fields), lambda s: (0, 0, 0)),
-        ],
-        out_shape=[
-            hbm((leaves, rank, leaf_len), BF),
-            jax.ShapeDtypeStruct((leaves + 1, rank, fields), BF),
-        ],
-        scratch_shapes=[pltpu.VMEM((rank, fields), F32)],
-        compiler_params=params(16),
-        cost_estimate=cost(leaves * leaf_len * leaf_len * rank * 2, 4 * MIB),
-    )(*in_hbm(leaf_order, composition, leaf_basis, transfer))
 
 
 def owner_tables(me, layers, owners, blocks):
@@ -166,7 +109,9 @@
     plane = (lane >= slots).astype(jnp.int32)
     slot = lane - plane * slots
     layer, chip, core = me // 8, (me // 2) & 3, me & 1
-    source = layer - (slot >> 2)
+    turn = slot >> 2
+    shift = jnp.where(turn < 2, turn, jnp.where(turn == 2, layers - 1, turn - 1))
+    source = layer - shift
     source = jnp.where(source < 0, source + layers, source)
     owner = source * 8 + (chip ^ (slot & 3)) * 2 + (core ^ plane)
     row = lax.broadcasted_iota(jnp.int32, shape, 0)
@@ -183,69 +128,133 @@
     return entry, block
 
 
-def order_kernel(per, layers, me_ref, order_ref, comp_ref, owner_ref, leaf_ref,
-                 ordered_ref, first_ref, last_ref, table_ref):
+def skeleton_kernel(per, layers, me_ref, order_ref, comp_ref, basis_ref, transfer_ref,
+                    owner_ref, leaf_ref, ordered_ref, shared_ref, first_ref, last_ref,
+                    table_ref, root_ref):
     step = pl.program_id(0)
-    leaf_len = order_ref.shape[1]
-    for i in range(per):
-        hot = one_hot_leaf(order_ref[pl.ds(step * per + i, 1), :], leaf_len)
-        at = pl.ds(i * leaf_len, leaf_len)
-        ordered = dot(hot, comp_ref[at, :]).astype(BF)
-        ordered_ref[at, :] = ordered
-        if i == 0:
-            @pl.when(step == 0)
-            def _():
-                first_ref[...] = ordered
-        if i == per - 1:
-            @pl.when(step == pl.num_programs(0) - 1)
-            def _():
-                last_ref[...] = ordered
+    leaf_len = basis_ref.shape[2]
 
     @pl.when(step == 0)
     def _():
+        root_ref[...] = jnp.zeros_like(root_ref)
         entry, block = owner_tables(me_ref[0], layers, owner_ref[...], leaf_ref[...])
-        rows = entry.shape[0]
-        table_ref[0, :rows, :entry.shape[1]] = entry
-        table_ref[1, :rows, :entry.shape[1]] = block
-
-
-def in_order(me, leaf_order, composition, owners, blocks, layers, per=4):
-    leaves, leaf_len = leaf_order.shape
+        rows, lanes = entry.shape
+        table_ref[0, :rows, :lanes] = entry
+        table_ref[1, :rows, :lanes] = block
+
+    hots = [one_hot_leaf(order_ref[pl.ds(step * per + i, 1), :], leaf_len) for i in range(per)]
+    ordered = [
+        dot(hots[i], comp_ref[i * leaf_len:(i + 1) * leaf_len, :]).astype(BF) for i in range(per)
+    ]
+    skeletons = [dot(basis_ref[i], ordered[i]).astype(BF) for i in range(per)]
+    across = jnp.concatenate([transfer_ref[i] for i in range(per)], axis=1)
+    root_ref[...] += dot(across, jnp.concatenate(skeletons, axis=0))
+    for i in range(per):
+        ordered_ref[i * leaf_len:(i + 1) * leaf_len, :] = ordered[i]
+        shared_ref[pl.ds(step * per + i + 1, 1)] = skeletons[i][None]
+
+    @pl.when(step == 0)
+    def _():
+        first_ref[...] = ordered[0]
+
+    @pl.when(step == pl.num_programs(0) - 1)
+    def _():
+        last_ref[...] = ordered[-1]
+        shared_ref[pl.ds(0, 1)] = root_ref[...].astype(BF)[None]
+
+
+def skeletons_of(me, leaf_order, composition, leaf_basis, transfer, owners, blocks, layers, per=4):
+    leaves, rank, leaf_len = leaf_basis.shape
     fields = composition.shape[1]
     entries = owners.shape[1]
     edge = jax.ShapeDtypeStruct((leaf_len, fields), BF)
     return pl.pallas_call(
-        functools.partial(order_kernel, per, layers),
-        name="cluster_order",
+        functools.partial(skeleton_kernel, per, layers),
+        name="order_and_skeleton",
         grid=(leaves // per,),
         in_specs=[
             scalars(),
             pl.BlockSpec((leaves, leaf_len), lambda s: (0, 0)),
             pl.BlockSpec((per * leaf_len, fields), lambda s: (s, 0)),
+            pl.BlockSpec((per, rank, leaf_len), lambda s: (s, 0, 0)),
+            pl.BlockSpec((per, rank, rank), lambda s: (s, 0, 0)),
             pl.BlockSpec((leaves, entries), lambda s: (0, 0)),
             pl.BlockSpec((leaves, entries), lambda s: (0, 0)),
         ],
         out_specs=[
             pl.BlockSpec((per * leaf_len, fields), lambda s: (s, 0)),
+            pl.BlockSpec((leaves + 1, rank, fields), lambda s: (0, 0, 0)),
             pl.BlockSpec((leaf_len, fields), lambda s: (0, 0)),
             pl.BlockSpec((leaf_len, fields), lambda s: (0, 0)),
             pl.BlockSpec((2, 16, 128), lambda s: (0, 0, 0)),
         ],
         out_shape=[
-            hbm((leaves * leaf_len, fields), BF),
+            jax.ShapeDtypeStruct((leaves * leaf_len, fields), BF),
+            jax.ShapeDtypeStruct((leaves + 1, rank, fields), BF),
             edge,
             edge,
             jax.ShapeDtypeStruct((2, 16, 128), jnp.int32),
         ],
+        scratch_shapes=[pltpu.VMEM((rank, fields), F32)],
         compiler_params=params(16),
         cost_estimate=cost(leaves * leaf_len * leaf_len * fields * 2, 4 * MIB),
-    )(me, *in_hbm(leaf_order, composition, owners, blocks))
-
-
-def dense_kernel(per, slots, table_ref, coupling_ref, top_ref, own_ref, other_ref):
+    )(me, *in_hbm(leaf_order, composition, leaf_basis, transfer, owners, blocks))
+
+
+def join_kernel(*refs):
+    out = refs[-1]
+    at = 0
+    for ref in refs[:-1]:
+        out[at:at + ref.shape[0]] = ref[...]
+        at += ref.shape[0]
+
+
+def join(parts):
+    if len(parts) == 1:
+        return parts[0]
+    shape = (sum(part.shape[0] for part in parts),) + parts[0].shape[1:]
+    return pl.pallas_call(
+        join_kernel,
+        name="join",
+        in_specs=[whole()] * len(parts),
+        out_specs=whole(),
+        out_shape=jax.ShapeDtypeStruct(shape, BF),
+        compiler_params=params(8 if shape[0] <= 32 else 32),
+        cost_estimate=cost(0, MIB // 2),
+    )(*parts)
+
+
+def choose_kernel(me_ref, *refs):
+    out = refs[-1]
+    number = len(refs) // 2
+    for core in range(2):
+        @pl.when(me_ref[0] % 2 == core)
+        def _(core=core):
+            join_kernel(*refs[core * number:(core + 1) * number], out)
+
+
+def choose(me, from_x, from_y):
+    parts = list(from_x) + list(from_y)
+    shape = (sum(part.shape[0] for part in from_x),) + from_x[0].shape[1:]
+    return pl.pallas_call(
+        choose_kernel,
+        name="choose",
+        in_specs=[scalars()] + [whole()] * len(parts),
+        out_specs=whole(),
+        out_shape=jax.ShapeDtypeStruct(shape, BF),
+        compiler_params=params(8 if shape[0] <= 32 else 32),
+        cost_estimate=cost(0, MIB // 2),
+    )(me, *parts)
+
+
+def dense_kernel(per, slots, table_ref, coupling_ref, top_ref, transfer_ref,
+                 own_ref, other_ref, turned_ref):
     step = pl.program_id(0)
     rank = coupling_ref.shape[2]
     leaves = own_ref.shape[0] - 1
+
+    for i in range(per):
+        turned_ref[step * per + i] = transfer_ref[i].T
 
     def fill(out_ref, plane, row, entry_row, block_of):
         for slot in range(0, slots, 2):
@@ -266,7 +275,7 @@
             fill(out_ref, plane, leaves, 0, lambda entry: top_ref[0, entry])
 
 
-def dense_couplings(table, coupling, top_coupling, slots, per=4):
+def dense_couplings(table, coupling, top_coupling, transfer, slots, per=4):
     leaves, entries, rank, _ = coupling.shape
     shape = jax.ShapeDtypeStruct((leaves + 1, rank, slots * rank), BF)
     full = pl.BlockSpec((leaves + 1, rank, slots * rank), lambda s: (0, 0, 0))
@@ -278,30 +287,42 @@
             scalars(),
             pl.BlockSpec((per, entries, rank, rank), lambda s: (s, 0, 0, 0)),
             pl.BlockSpec(top_coupling.shape, lambda s: (0, 0, 0, 0)),
-        ],
-        out_specs=[full, full],
-        out_shape=[shape, shape],
+            pl.BlockSpec((per, rank, rank), lambda s: (s, 0, 0)),
+        ],
+        out_specs=[full, full, pl.BlockSpec(transfer.shape, lambda s: (0, 0, 0))],
+        out_shape=[shape, shape, jax.ShapeDtypeStruct(transfer.shape, BF)],
         compiler_params=params(16 if slots <= 16 else 48),
         cost_estimate=cost(0, 8 * MIB),
-    )(table, *in_hbm(coupling, top_coupling))
-
-
-def round_kernel(first, steps, slots, own_at, other_at, line_ref, x_ref, y_ref, far_ref,
-                 own_blocks, other_blocks, *refs):
+    )(table, *in_hbm(coupling, top_coupling, transfer))
+
+
+def round_kernel(first, steps, slots, counts, own_at, other_at, *refs):
+    sides = []
+    for number in counts:
+        sides.append(refs[:number])
+        refs = refs[number:]
+    own_blocks, other_blocks = refs[:2]
+    refs = refs[2:]
     if first:
         own_out, other_out = refs
     else:
         own_in, other_in, own_out, other_out = refs
     rows, rank, _ = own_out.shape
-    sides = (line_ref, x_ref, y_ref, far_ref)
     low, high = steps[0] * 4 * rank, (steps[-1] + 1) * 4 * rank
+
+    def block_at(side, base, index):
+        for ref in side:
+            if base < ref.shape[0]:
+                return ref[base + index]
+            base -= ref.shape[0]
+
     for plane, at_ref, blocks_ref, out in (
         (0, own_at, own_blocks, own_out),
         (1, other_at, other_blocks, other_out),
     ):
         for row in range(rows):
             chosen = [
-                side[place * rows + at_ref[1, (row + 1) % rows, plane * slots + step * 4 + q]]
+                block_at(side, place * rows, at_ref[1, (row + 1) % rows, plane * slots + step * 4 + q])
                 for place, step in enumerate(steps)
                 for q, side in enumerate(sides)
             ]
@@ -313,12 +334,12 @@
 
 def far_round(steps, slots, own_at, other_at, parts, blocks, sums):
     rows, rank, _ = blocks[0].shape
-    fields = parts[0].shape[2]
+    fields = parts[0][0].shape[2]
     first = sums is None
     sum_shape = jax.ShapeDtypeStruct((rows, rank, fields), F32)
-    args = list(parts) + list(blocks) + ([] if first else list(sums))
-    return pl.pallas_call(
-        functools.partial(round_kernel, first, steps, slots),
+    args = [part for side in parts for part in side] + list(blocks) + ([] if first else list(sums))
+    return pl.pallas_call(
+        functools.partial(round_kernel, first, steps, slots, [len(side) for side in parts]),
         name="far_round_" + str(steps[0]),
         in_specs=[scalars(), scalars()] + [whole()] * len(args),
         out_specs=[whole(), whole()],
@@ -328,13 +349,13 @@
     )(own_at, other_at, *args)
 
 
-def near_kernel(edges, pair_of, last_pair, mask_ref, order_ref, table_ref, placed_ref,
+def near_kernel(edges, pair_of, last_pair, mask_ref, order_ref, table_ref, basis_ref,
                 prev_ref, cur_ref, next_ref, *refs):
     if edges:
         before_ref, after_ref = refs[:2]
     near_ref, turned_ref = refs[-2:]
     pair = pair_of(pl.program_id(0))
-    leaf_len = placed_ref.shape[2]
+    leaf_len = basis_ref.shape[2]
     low, high = cur_ref[:leaf_len, :], cur_ref[leaf_len:, :]
     prev, following = prev_ref[...], next_ref[...]
     if edges:
@@ -355,12 +376,14 @@
     for i in range(2):
         hot = one_hot_grid(order_ref[pl.ds(2 * pair + i, 1), :], leaf_len)
         at = pl.ds(i * leaf_len, leaf_len)
-        near_ref[at, :] = dot(hot, near[:, i * fields:(i + 1) * fields]).astype(BF)
-        turned_ref[at, :] = placed_ref[i].T
-
-
-def near_field(pairs, near_list, leaf_order, tables, placed, ordered, halos=None, filled=None):
-    leaves, rank, leaf_len = placed.shape
+        both = jnp.concatenate([near[:, i * fields:(i + 1) * fields], basis_ref[i].T], axis=1)
+        moved = dot(hot, both).astype(BF)
+        near_ref[at, :] = moved[:, :fields]
+        turned_ref[at, :] = moved[:, fields:]
+
+
+def near_field(pairs, near_list, leaf_order, tables, basis, ordered, halos=None, filled=None):
+    leaves, rank, leaf_len = basis.shape
     fields = ordered.shape[1]
     last = leaves // 2 - 1
     gap = pairs[1] - pairs[0] if len(pairs) > 1 else 1
@@ -377,7 +400,7 @@
         pl.BlockSpec((2 * leaf_len, fields), lambda s: (pair_of(s), 0)),
         pl.BlockSpec((leaf_len, fields), lambda s: (jnp.minimum(2 * pair_of(s) + 2, leaves - 1), 0)),
     ]
-    args = [near_list.T] + in_hbm(leaf_order, tables, placed, ordered, ordered, ordered)
+    args = [near_list.T, leaf_order, tables, basis, ordered, ordered, ordered]
     aliases = {}
     if halos is not None:
         in_specs += [pl.BlockSpec((leaf_len, fields), lambda s: (0, 0))] * 2
@@ -385,7 +408,7 @@
     if filled is not None:
         aliases = {len(args): 0, len(args) + 1: 1}
         in_specs += [pl.BlockSpec(memory_space=pl.ANY)] * 2
-        args += in_hbm(*filled)
+        args += list(filled)
     return pl.pallas_call(
         functools.partial(near_kernel, halos is not None, pair_of, last),
         name="near_" + str(pairs[0]),
@@ -396,8 +419,8 @@
             pl.BlockSpec((2 * leaf_len, rank), lambda s: (pair_of(s), 0)),
         ],
         out_shape=[
-            hbm((leaves * leaf_len, fields), BF),
-            hbm((leaves * leaf_len, rank), BF),
+            jax.ShapeDtypeStruct((leaves * leaf_len, fields), BF),
+            jax.ShapeDtypeStruct((leaves * leaf_len, rank), BF),
         ],
         input_output_aliases=aliases,
         compiler_params=params(16),
@@ -443,7 +466,7 @@
         out_shape=jax.ShapeDtypeStruct(near.shape, BF),
         compiler_params=params(16),
         cost_estimate=cost(leaves * leaf_len * rank * fields * 2, 4 * MIB),
-    )(own, other, turned_transfer, *in_hbm(near, turned))
+    )(own, other, turned_transfer, near, turned)
 
 
 def after(block, *others):
@@ -465,53 +488,48 @@
     count = lax.axis_size("subtree")
     layers = count // 8
     slots = layers * 4
-    my_index = lax.axis_index("subtree")
-    even = my_index % 2 == 0
-
-    placed, shared = skeletons(leaf_order, composition, leaf_basis, transfer)
-
-    def plane(block):
-        from_x, from_y = over_x(block), over_y(block)
-        return block, from_x, from_y
-
-    def diagonal(parts, *others):
-        chosen = jnp.where(even, parts[1], parts[2])
-        return parts + (onward(after(chosen, *others)),)
-
-    half = layers // 2
-    lines = [shared, along_z(shared, 1)]
-    ordered, first, last, table = in_order(
-        my_index.reshape(1), leaf_order, composition, admissible_owner, admissible_leaf, layers
-    )
-    for step in range(2, layers):
-        lines.append(along_z(after(shared, table), step))
-    planes = plane(after(jnp.concatenate(lines[:half], axis=0), table))
-    tables = jnp.asarray(near_tables(leaf_len))
-    near_args = (near_list, leaf_order, tables, placed)
     pairs = leaves // 2
     cut = pairs // 2
-    filled = near_field(list(range(1, cut)), *near_args, ordered)
-    own_blocks, my_other = dense_couplings(after(table, filled[0]), coupling, top_coupling, slots)
+    me = lax.axis_index("subtree").reshape(1)
+
+    ordered, shared, first, last, table = skeletons_of(
+        me, leaf_order, composition, leaf_basis, transfer, admissible_owner, admissible_leaf, layers
+    )
+    tables = jnp.asarray(near_tables(leaf_len))
+    near_args = (near_list, leaf_order, tables, leaf_basis)
+
+    line = along_z(shared, 1)
+    from_x, from_y = over_x(shared), over_y(shared)
+    own_blocks, my_other, turned_transfer = dense_couplings(
+        table, coupling, top_coupling, transfer, slots
+    )
+    line = after(line, from_x, from_y, my_other)
+    next_x, next_y = over_x(line), over_y(line)
+    lines = [along_z(after(shared, my_other), layers - 1)]
+    for _ in range(layers - 3):
+        lines.append(along_z(line if len(lines) == 1 else lines[-1], 1))
     other_blocks = over_core(my_other)
-    round_0 = diagonal(planes)
-
-    planes = plane(
-        after(jnp.concatenate(lines[half:], axis=0), planes[1], planes[2], my_other, filled[0])
-    )
     other_table = over_core(table)
     before = lax.ppermute(last, "subtree", [(d, d + 1) for d in range(count - 1)])
     behind = lax.ppermute(first, "subtree", [(d + 1, d) for d in range(count - 1)])
+    round_0 = ((shared, line), (from_x, next_x), (from_y, next_y))
+    far = onward(choose(me, (after(from_x, before, behind, other_table, *lines), next_x), round_0[2]))
+    round_0 += ((far,),)
+    held = after(ordered, next_x, next_y, before, behind, other_table, *lines)
+    filled = near_field(list(range(1, cut)), *near_args, held)
+
+    joined = join([after(lines[0], far, filled[0])] + lines[1:])
+    last_x, last_y = over_x(joined), over_y(joined)
+    held = after(ordered, joined)
+    filled = near_field(list(range(cut, pairs - 1)), *near_args, held, filled=filled)
+    filled = near_field([0, pairs - 1], *near_args, ordered, halos=(before, behind), filled=filled)
     blocks = (own_blocks, other_blocks)
-    filled = near_field(
-        list(range(cut, pairs - 1)), *near_args, after(ordered, other_table, before, behind), filled=filled
-    )
-    round_1 = diagonal(planes, filled[0])
-    filled = near_field([0, pairs - 1], *near_args, ordered, halos=(before, behind), filled=filled)
-    sums = far_round(list(range(half)), slots, table, other_table, round_0, blocks, None)
-    round_1 = round_1[:3] + (after(round_1[3], filled[0], sums[0]),)
-    sums = far_round(list(range(half, layers)), slots, table, other_table, round_1, blocks, sums)
+    far = onward(choose(me, (after(last_x, filled[0]),), (last_y,)))
+    sums = far_round([0, 1], slots, table, other_table, round_0, blocks, None)
+    round_1 = ((joined,), (last_x,), (last_y,), (after(far, sums[0]),))
+    sums = far_round(list(range(2, layers)), slots, table, other_table, round_1, blocks, sums)
     received = over_core(sums[1])
-    return field(sums[0], received, transfer.transpose(0, 2, 1), *filled)
+    return field(sums[0], received, turned_transfer, *filled)
 
 
 def solution(mesh):

time: 88.1 us -> 70.6 us (0.80); the launches traced: 86.7 us -> 70.4 us
  Pallas kernels: 41 us -> 25.5 us
  waiting for transfers between devices: 14.2 us -> 26.8 us
  local copies, waits for them, and re-layouts: 6.43 us -> 0.02 us
  other arithmetic: 4 us -> 0 us
  starting transfers between devices: 21 us -> 17.9 us
    ppermute x12 -> x14, waiting for transfers between devices: 14.2 us -> 26.8 us  [send(): lax.ppermute(block, 'subtree', [(d, target(d)) for d in range(count)])]
    pallas_call x4 -> x6, Pallas kernels: 15 us -> 8.29 us  [the longest x1 4.66 us: skeletons_of(): pl.pallas_call(functools.partial(skeleton_kernel, per, layers), name='ord...]
    unnamed x27 -> x8, local copies, waits for them, and re-layouts: 6.43 us -> 0.02 us
    pallas_call x3, Pallas kernels: 16.3 us -> 10.4 us  [near_field(): pl.pallas_call(functools.partial(near_kernel, halos is not None, pair_of,...]
    ppermute x12 -> x14, starting transfers between devices: 17.3 us -> 14.2 us  [send(): lax.ppermute(block, 'subtree', [(d, target(d)) for d in range(count)])]
    select_n x2 -> x0, other arithmetic: 2.11 us -> none  [diagonal(): chosen = jnp.where(even, parts[1], parts[2])]
    concatenate x2 -> x0, other arithmetic: 1.88 us -> none  [the longest x1 1.08 us: on_device(): planes = plane(after(jnp.concatenate(lines[:half], axis=0), table))]
    pallas_call x1, Pallas kernels: 4.53 us -> 2.73 us  [field(): pl.pallas_call(functools.partial(field_kernel, per), name='local_and_fiel...]
  transfers between devices with their start and end apart: 14 -> 16, of which waited for: 4 -> 7; matrix products, arithmetic and copies ran while one was open for 6% -> 0% of each run, Pallas kernels for 33% -> 23%
where the time goes in v5:
time: 70.6 us; the launch traced here: 70.4 us
  waiting for transfers between devices  26.8 us (38%)
  Pallas kernels  25.5 us (36%)
  starting transfers between devices  17.9 us (25%)
    ppermute x14, waiting for transfers between devices, send(): lax.ppermute(block, 'subtree', [(d, target(d)) for d in range(count)])  26.8 us
    ppermute x14, starting transfers between devices, send(): lax.ppermute(block, 'subtree', [(d, target(d)) for d in range(count)])  14.2 us
    pallas_call x3, Pallas kernels, near_field(): pl.pallas_call(functools.partial(near_kernel, halos is not None, pair_of,...  10.4 us
    pallas_call x1, Pallas kernels, skeletons_of(): pl.pallas_call(functools.partial(skeleton_kernel, per, layers), name='ord...  4.66 us
    pallas_call x1, Pallas kernels, dense_couplings(): pl.pallas_call(functools.partial(dense_kernel, per, slots), name='couplin...  4.06 us
    pallas_call x2, Pallas kernels, far_round(): pl.pallas_call(functools.partial(round_kernel, first, steps, slots, [len(...  3.53 us
    pallas_call x1, Pallas kernels, field(): pl.pallas_call(functools.partial(field_kernel, per), name='local_and_fiel...  2.73 us
    ppermute x1, starting transfers between devices, on_device(): lax.ppermute(last, 'subtree', [(d, d + 1) for d in range(count - 1)])  2.4 us
  transfers between devices with their start and end apart: 16, of which 7 were waited for; matrix products, arithmetic and copies ran while one was open for 0% of the time, Pallas kernels for 23%

profile of v5, /device:TPU:0, one launch (start us, length us, event | category | flops | bytes accessed | tf_op | source)
XLA Modules:
  0.0 70.4 jit_solution(4883421474278446756)
XLA Ops:
  0.0 4.7 %order_and_skeleton.1 = (bf16[6144,128]{1,0:T(8,128)(2,1)S(1)}, bf16[13,64,128]{2,1,0:T(8,128)(2,1)S(1)}, bf16[512,128]{1,0:T(8,128)(2,1)S(1)}, bf16[512,128]{1,0:T(8,128)(2,1)S(1)}, s32[2,16,128]{2,1,0:T(8,128)S(1)}) custom-call(s32[1]{0:T(128)} %bitcast.me_ref, s32[12,512]{1,0:T(8,128)} %order_ref.7, bf16[6144,128]{1,0:T(8,128)(2,1)} %comp_ref.1, ...), custom_call_target="tpu_custom_call" | custom-call | flops 12582912 | bytes 65536 | tf_op jit(solution)/shard_map/order_and_skeleton/pallas_call | solution.py:171
  4.7 3.0 %collective-permute-start.6 = (bf16[13,64,128]{2,1,0:T(8,128)(2,1)S(1)}, bf16[13,64,128]{2,1,0:T(8,128)(2,1)S(1)}, u32[]{:S(2)}, u32[]{:S(2)}) collective-permute-start(bf16[13,64,128]{2,1,0:T(8,128)(2,1)S(1)} %get-tuple-element.34.refs_0_), channel_id=1, source_target_pairs={{0,4},{1,5},{2,6},{3,7},{4,0},{5,1},{6,2},{7,3},{8,12},{9,13},{10,... | collective-permute-start | bytes 638984 | tf_op jit(solution)/shard_map/ppermute | solution.py:38
  7.7 1.6 %collective-permute-start.5 = (bf16[13,64,128]{2,1,0:T(8,128)(2,1)S(1)}, bf16[13,64,128]{2,1,0:T(8,128)(2,1)S(1)}, u32[]{:S(2)}, u32[]{:S(2)}) collective-permute-start(bf16[13,64,128]{2,1,0:T(8,128)(2,1)S(1)} %get-tuple-element.34.refs_0_), channel_id=1, source_target_pairs={{0,8},{1,9},{2,10},{3,11},{4,12},{5,13},{6,14},{7,15},{8,16},{9,17... | collective-permute-start | bytes 638984 | tf_op jit(solution)/shard_map/ppermute | solution.py:38
  9.3 1.5 %collective-permute-start.2 = (bf16[13,64,128]{2,1,0:T(8,128)(2,1)S(1)}, bf16[13,64,128]{2,1,0:T(8,128)(2,1)S(1)}, u32[]{:S(2)}, u32[]{:S(2)}) collective-permute-start(bf16[13,64,128]{2,1,0:T(8,128)(2,1)S(1)} %get-tuple-element.34.refs_0_), channel_id=1, source_target_pairs={{0,2},{1,3},{2,0},{3,1},{4,6},{5,7},{6,4},{7,5},{8,10},{9,11},{10,... | collective-permute-start | bytes 638984 | tf_op jit(solution)/shard_map/ppermute | solution.py:38
  10.8 4.1 %couplings_by_owner.1 = (bf16[13,64,1024]{2,1,0:T(8,128)(2,1)S(1)}, bf16[13,64,1024]{2,1,0:T(8,128)(2,1)S(1)}, bf16[12,64,64]{2,1,0:T(8,128)(2,1)S(1)}) custom-call(s32[2,16,128]{2,1,0:T(8,128)S(1)} %get-tuple-element.31.table_ref.own_at, bf16[12,16,64,64]{3,2,1,0:T(8,128)(2,1)} %coupling_ref.1, bf16[1,32,64,64]{3,2,1,0:T(8,128)(2,1)} %top_ref.1, ...), custom_call_target="tpu_custom_call" | custom-call | bytes 131072 | tf_op jit(solution)/shard_map/couplings_by_owner/pallas_call | solution.py:282
  14.9 2.4 %collective-permute-start.3 = (bf16[512,128]{1,0:T(8,128)(2,1)S(1)}, bf16[512,128]{1,0:T(8,128)(2,1)S(1)}, u32[]{:S(2)}, u32[]{:S(2)}) collective-permute-start(bf16[512,128]{1,0:T(8,128)(2,1)S(1)} %get-tuple-element.35), channel_id=1, source_target_pairs={{0,1},{1,2},{2,3},{3,4},{4,5},{5,6},{6,7},{7,8},{8,9},{9,10},{10,1... | collective-permute-start | bytes 393224 | tf_op jit(solution)/shard_map/ppermute | solution.py:513
  17.4 1.3 %collective-permute-start.4 = (bf16[512,128]{1,0:T(8,128)(2,1)S(1)}, bf16[512,128]{1,0:T(8,128)(2,1)S(1)}, u32[]{:S(2)}, u32[]{:S(2)}) collective-permute-start(bf16[512,128]{1,0:T(8,128)(2,1)S(1)} %get-tuple-element.36), channel_id=1, source_target_pairs={{1,0},{2,1},{3,2},{4,3},{5,4},{6,5},{7,6},{8,7},{9,8},{10,9},{11,1... | collective-permute-start | bytes 393224 | tf_op jit(solution)/shard_map/ppermute | solution.py:514
  18.7 1.2 %collective-permute-start = (s32[2,16,128]{2,1,0:T(8,128)S(1)}, s32[2,16,128]{2,1,0:T(8,128)S(1)}, u32[]{:S(2)}, u32[]{:S(2)}) collective-permute-start(s32[2,16,128]{2,1,0:T(8,128)S(1)} %get-tuple-element.31.table_ref.own_at), channel_id=1, source_target_pairs={{0,1},{1,0},{2,3},{3,2},{4,5},{5,4},{6,7},{7,6},{8,9},{9,8},{10,11... | collective-permute-start | bytes 49160 | tf_op jit(solution)/shard_map/ppermute | solution.py:38
  19.9 5.0 %collective-permute-start.1 = (bf16[13,64,128]{2,1,0:T(8,128)(2,1)S(1)}, bf16[13,64,128]{2,1,0:T(8,128)(2,1)S(1)}, u32[]{:S(2)}, u32[]{:S(2)}) collective-permute-start(bf16[13,64,128]{2,1,0:T(8,128)(2,1)S(1)} %get-tuple-element.34.refs_0_), channel_id=1, source_target_pairs={{0,24},{1,25},{2,26},{3,27},{4,28},{5,29},{6,30},{7,31},{8,0},{9,1... | collective-permute-start | bytes 638984 | tf_op jit(solution)/shard_map/ppermute | solution.py:38
  24.9 0.4 collective-permute-start.7
  25.3 0.7 %collective-permute-start.8 = (bf16[13,64,128]{2,1,0:T(8,128)(2,1)S(1)}, bf16[13,64,128]{2,1,0:T(8,128)(2,1)S(1)}, u32[]{:S(2)}, u32[]{:S(2)}) collective-permute-start(bf16[13,64,128]{2,1,0:T(8,128)(2,1)S(1)} %collective-permute-done.5.refs_1_), channel_id=1, source_target_pairs={{0,2},{1,3},{2,0},{3,1},{4,6},{5,7},{6,4},{7,5},{8,10},{9,11},{10,... | collective-permute-start | bytes 638984 | tf_op jit(solution)/shard_map/ppermute | solution.py:38
  26.0 5.4 %collective-permute-done.1.refs_0_ = bf16[13,64,128]{2,1,0:T(8,128)(2,1)S(1)} collective-permute-done((bf16[13,64,128]{2,1,0:T(8,128)(2,1)S(1)}, bf16[13,64,128]{2,1,0:T(8,128)(2,1)S(1)}, u32[]{:S(2)}, u32[]{:S(2)}) %collective-permute-start.1) | collective-permute-done | bytes 213024 | tf_op jit(solution)/shard_map/ppermute | solution.py:38
  31.4 5.5 %collective-permute-done.7.refs_1_ = bf16[13,64,128]{2,1,0:T(8,128)(2,1)S(1)} collective-permute-done((bf16[13,64,128]{2,1,0:T(8,128)(2,1)S(1)}, bf16[13,64,128]{2,1,0:T(8,128)(2,1)S(1)}, u32[]{:S(2)}, u32[]{:S(2)}) %collective-permute-start.7) | collective-permute-done | bytes 213024 | tf_op jit(solution)/shard_map/ppermute | solution.py:38
  37.1 3.5 %near_1.1 = (bf16[6144,128]{1,0:T(8,128)(2,1)S(1)}, bf16[6144,64]{1,0:T(8,128)(2,1)S(1)}) custom-call(s32[2,12]{1,0:T(2,128)S(1)} %bitcast.2, s32[12,512]{1,0:T(8,128)S(1)} %copy-done.2, bf16[512,1536]{1,0:T(8,128)(2,1)S(1)} %copy-done, bf16[12,64,512]{2,1,0:T(8,128)(2,1)S(1)} %copy-done.1, ...), custom_call_target="tpu_custom_call" | custom-call | flops 20971520 | bytes 32768 | tf_op jit(solution)/shard_map/near_1/pallas_call | solution.py:412
  40.5 4.6 %collective-permute-done.10.refs_6_ = bf16[26,64,128]{2,1,0:T(8,128)(2,1)S(1)} collective-permute-done((bf16[26,64,128]{2,1,0:T(8,128)(2,1)S(1)}, bf16[26,64,128]{2,1,0:T(8,128)(2,1)S(1)}, u32[]{:S(2)}, u32[]{:S(2)}) %collective-permute-start.10) | collective-permute-done | bytes 426016 | tf_op jit(solution)/shard_map/ppermute | solution.py:38
  45.3 3.5 %near_3.1 = (bf16[6144,128]{1,0:T(8,128)(2,1)S(1)}, bf16[6144,64]{1,0:T(8,128)(2,1)S(1)}) custom-call(s32[2,12]{1,0:T(2,128)S(1)} %bitcast.3, s32[12,512]{1,0:T(8,128)S(1)} %copy-done.2, bf16[512,1536]{1,0:T(8,128)(2,1)S(1)} %copy-done, bf16[12,64,512]{2,1,0:T(8,128)(2,1)S(1)} %copy-done.1, ...), custom_call_target="tpu_custom_call", output_to_operand_aliasing={{0}: (7, {}), {1}: (8, {})} | custom-call | flops 20971520 | bytes 32768 | tf_op jit(solution)/shard_map/near_3/pallas_call | solution.py:412
  48.8 3.5 %near_0.1 = (bf16[6144,128]{1,0:T(8,128)(2,1)S(1)}, bf16[6144,64]{1,0:T(8,128)(2,1)S(1)}) custom-call(s32[2,12]{1,0:T(2,128)S(1)} %bitcast.4, s32[12,512]{1,0:T(8,128)S(1)} %copy-done.2, bf16[512,1536]{1,0:T(8,128)(2,1)S(1)} %copy-done, bf16[12,64,512]{2,1,0:T(8,128)(2,1)S(1)} %copy-done.1, ...), custom_call_target="tpu_custom_call", output_to_operand_aliasing={{0}: (9, {}), {1}: (10, {})} | custom-call | flops 20971520 | bytes 32768 | tf_op jit(solution)/shard_map/near_0/pallas_call | solution.py:412
  52.3 3.4 %collective-permute-done.11.refs_0_.refs_1_ = bf16[26,64,128]{2,1,0:T(8,128)(2,1)S(1)} collective-permute-done((bf16[26,64,128]{2,1,0:T(8,128)(2,1)S(1)}, bf16[26,64,128]{2,1,0:T(8,128)(2,1)S(1)}, u32[]{:S(2)}, u32[]{:S(2)}) %collective-permute-start.11) | collective-permute-done | bytes 426016 | tf_op jit(solution)/shard_map/ppermute | solution.py:38
  55.8 0.4 collective-permute-start.13
  56.2 1.7 %far_round_0.1 = (f32[13,64,128]{2,1,0:T(8,128)S(1)}, f32[13,64,128]{2,1,0:T(8,128)S(1)}) custom-call(s32[2,16,128]{2,1,0:T(8,128)S(1)} %get-tuple-element.31.table_ref.own_at, s32[2,16,128]{2,1,0:T(8,128)S(1)} %collective-permute-done.other_at, bf16[13,64,128]{2,1,0:T(8,128)(2,1)S(1)} %get-tuple-element.34.refs_0_, ...), custom_call_target="tpu_custom_call" | custom-call | flops 3407872 | bytes 32768 | tf_op jit(solution)/shard_map/far_round_0/pallas_call | solution.py:341
  57.9 6.1 %collective-permute-done.13.refs_3_ = bf16[26,64,128]{2,1,0:T(8,128)(2,1)S(1)} collective-permute-done((bf16[26,64,128]{2,1,0:T(8,128)(2,1)S(1)}, bf16[26,64,128]{2,1,0:T(8,128)(2,1)S(1)}, u32[]{:S(2)}, u32[]{:S(2)}) %collective-permute-start.13) | collective-permute-done | bytes 426016 | tf_op jit(solution)/shard_map/ppermute | solution.py:38
  64.0 1.8 %far_round_2.1 = (f32[13,64,128]{2,1,0:T(8,128)S(1)}, f32[13,64,128]{2,1,0:T(8,128)S(1)}) custom-call(s32[2,16,128]{2,1,0:T(8,128)S(1)} %get-tuple-element.31.table_ref.own_at, s32[2,16,128]{2,1,0:T(8,128)S(1)} %collective-permute-done.other_at, bf16[26,64,128]{2,1,0:T(8,128)(2,1)S(1)} %join.1.refs_0_, ...), custom_call_target="tpu_custom_call" | custom-call | flops 3407872 | bytes 32768 | tf_op jit(solution)/shard_map/far_round_2/pallas_call | solution.py:341
  65.9 1.8 %collective-permute-done.15.other_ref = f32[13,64,128]{2,1,0:T(8,128)S(1)} collective-permute-done((f32[13,64,128]{2,1,0:T(8,128)S(1)}, f32[13,64,128]{2,1,0:T(8,128)S(1)}, u32[]{:S(2)}, u32[]{:S(2)}) %collective-permute-start.15) | collective-permute-done | bytes 426016 | tf_op jit(solution)/shard_map/ppermute | solution.py:38
  67.6 2.7 %local_and_field.1 = bf16[6144,128]{1,0:T(8,128)(2,1)} custom-call(f32[13,64,128]{2,1,0:T(8,128)S(1)} %get-tuple-element.53.own_ref, f32[13,64,128]{2,1,0:T(8,128)S(1)} %collective-permute-done.15.other_ref, bf16[12,64,64]{2,1,0:T(8,128)(2,1)S(1)} %get-tuple-element.55.turned_transfer_ref, bf16[6144,128]{1,0:T(8,128)(2,1)S(1)} %get-tuple-element.47.near_ref, ...), custom_call_target="tpu_custom_call" | custom-call | flops 1572864 | bytes 65536 | tf_op jit(solution)/shard_map/local_and_field/pallas_call | solution.py:454
  (27 shorter events, 0.6 us)
Async XLA Ops:
  4.7 12.7 %collective-permute-start.6 = (bf16[13,64,128]{2,1,0:T(8,128)(2,1)S(1)}, bf16[13,64,128]{2,1,0:T(8,128)(2,1)S(1)}, u32[]{:S(2)}, u32[]{:S(2)}) collective-permute-start(bf16[13,64,128]{2,1,0:T(8,128)(2,1)S(1)} %get-tuple-element.34.refs_0_), channel_id=1, source_target_pairs={{0,4},{1,5},{2,6},{3,7},{4,0},{5,1},{6,2},{7,3},{8,12},{9,13},{10,... | collective-permute-start | bytes 638984 | tf_op jit(solution)/shard_map/ppermute | solution.py:38
  7.7 11.0 %collective-permute-start.5 = (bf16[13,64,128]{2,1,0:T(8,128)(2,1)S(1)}, bf16[13,64,128]{2,1,0:T(8,128)(2,1)S(1)}, u32[]{:S(2)}, u32[]{:S(2)}) collective-permute-start(bf16[13,64,128]{2,1,0:T(8,128)(2,1)S(1)} %get-tuple-element.34.refs_0_), channel_id=1, source_target_pairs={{0,8},{1,9},{2,10},{3,11},{4,12},{5,13},{6,14},{7,15},{8,16},{9,17... | collective-permute-start | bytes 638984 | tf_op jit(solution)/shard_map/ppermute | solution.py:38
  9.3 10.6 %collective-permute-start.2 = (bf16[13,64,128]{2,1,0:T(8,128)(2,1)S(1)}, bf16[13,64,128]{2,1,0:T(8,128)(2,1)S(1)}, u32[]{:S(2)}, u32[]{:S(2)}) collective-permute-start(bf16[13,64,128]{2,1,0:T(8,128)(2,1)S(1)} %get-tuple-element.34.refs_0_), channel_id=1, source_target_pairs={{0,2},{1,3},{2,0},{3,1},{4,6},{5,7},{6,4},{7,5},{8,10},{9,11},{10,... | collective-permute-start | bytes 638984 | tf_op jit(solution)/shard_map/ppermute | solution.py:38
  10.8 26.3 %copy-start = (bf16[512,1536]{1,0:T(8,128)(2,1)S(1)}, bf16[512,1536]{1,0:T(8,128)(2,1)}, u32[]{:S(2)}) copy-start(bf16[512,1536]{1,0:T(8,128)(2,1)} %constant.6.clone.table_ref) | copy-start | bytes 4718596
  10.8 26.3 %copy-start.2 = (s32[12,512]{1,0:T(8,128)S(1)}, s32[12,512]{1,0:T(8,128)}, u32[]{:S(2)}) copy-start(s32[12,512]{1,0:T(8,128)} %order_ref.7) | copy-start | bytes 73732
  10.8 26.3 %copy-start.3 = (s32[12,2]{0,1:T(2,128)S(1)}, s32[12,2]{0,1:T(2,128)}, u32[]{:S(2)}) copy-start(s32[12,2]{0,1:T(2,128)} %param.17) | copy-start | bytes 292
  14.8 22.2 %copy-start.1 = (bf16[12,64,512]{2,1,0:T(8,128)(2,1)S(1)}, bf16[12,64,512]{2,1,0:T(8,128)(2,1)}, u32[]{:S(2)}) copy-start(bf16[12,64,512]{2,1,0:T(8,128)(2,1)} %basis_ref.7) | copy-start | bytes 2359300
  14.9 41.3 %collective-permute-start.14 = (bf16[13,64,1024]{2,1,0:T(8,128)(2,1)S(1)}, bf16[13,64,1024]{2,1,0:T(8,128)(2,1)S(1)}, u32[]{:S(2)}, u32[]{:S(2)}) collective-permute-start(bf16[13,64,1024]{2,1,0:T(8,128)(2,1)S(1)} %get-tuple-element.33), channel_id=1, source_target_pairs={{0,1},{1,0},{2,3},{3,2},{4,5},{5,4},{6,7},{7,6},{8,9},{9,8},{10,11... | collective-permute-start | bytes 5111816 | tf_op jit(solution)/shard_map/ppermute | solution.py:38
  14.9 10.4 %collective-permute-start.3 = (bf16[512,128]{1,0:T(8,128)(2,1)S(1)}, bf16[512,128]{1,0:T(8,128)(2,1)S(1)}, u32[]{:S(2)}, u32[]{:S(2)}) collective-permute-start(bf16[512,128]{1,0:T(8,128)(2,1)S(1)} %get-tuple-element.35), channel_id=1, source_target_pairs={{0,1},{1,2},{2,3},{3,4},{4,5},{5,6},{6,7},{7,8},{8,9},{9,10},{10,1... | collective-permute-start | bytes 393224 | tf_op jit(solution)/shard_map/ppermute | solution.py:513
  17.4 8.0 %collective-permute-start.4 = (bf16[512,128]{1,0:T(8,128)(2,1)S(1)}, bf16[512,128]{1,0:T(8,128)(2,1)S(1)}, u32[]{:S(2)}, u32[]{:S(2)}) collective-permute-start(bf16[512,128]{1,0:T(8,128)(2,1)S(1)} %get-tuple-element.36), channel_id=1, source_target_pairs={{1,0},{2,1},{3,2},{4,3},{5,4},{6,5},{7,6},{8,7},{9,8},{10,9},{11,1... | collective-permute-start | bytes 393224 | tf_op jit(solution)/shard_map/ppermute | solution.py:514
  18.7 6.2 %collective-permute-start = (s32[2,16,128]{2,1,0:T(8,128)S(1)}, s32[2,16,128]{2,1,0:T(8,128)S(1)}, u32[]{:S(2)}, u32[]{:S(2)}) collective-permute-start(s32[2,16,128]{2,1,0:T(8,128)S(1)} %get-tuple-element.31.table_ref.own_at), channel_id=1, source_target_pairs={{0,1},{1,0},{2,3},{3,2},{4,5},{5,4},{6,7},{7,6},{8,9},{9,8},{10,11... | collective-permute-start | bytes 49160 | tf_op jit(solution)/shard_map/ppermute | solution.py:38
  19.9 11.6 %collective-permute-start.1 = (bf16[13,64,128]{2,1,0:T(8,128)(2,1)S(1)}, bf16[13,64,128]{2,1,0:T(8,128)(2,1)S(1)}, u32[]{:S(2)}, u32[]{:S(2)}) collective-permute-start(bf16[13,64,128]{2,1,0:T(8,128)(2,1)S(1)} %get-tuple-element.34.refs_0_), channel_id=1, source_target_pairs={{0,24},{1,25},{2,26},{3,27},{4,28},{5,29},{6,30},{7,31},{8,0},{9,1... | collective-permute-start | bytes 638984 | tf_op jit(solution)/shard_map/ppermute | solution.py:38
  24.9 12.0 %collective-permute-start.7 = (bf16[13,64,128]{2,1,0:T(8,128)(2,1)S(1)}, bf16[13,64,128]{2,1,0:T(8,128)(2,1)S(1)}, u32[]{:S(2)}, u32[]{:S(2)}) collective-permute-start(bf16[13,64,128]{2,1,0:T(8,128)(2,1)S(1)} %collective-permute-done.5.refs_1_), channel_id=1, source_target_pairs={{0,8},{1,9},{2,10},{3,11},{4,12},{5,13},{6,14},{7,15},{8,16},{9,17... | collective-permute-start | bytes 638984 | tf_op jit(solution)/shard_map/ppermute | solution.py:38
  25.3 11.6 %collective-permute-start.9 = (bf16[13,64,128]{2,1,0:T(8,128)(2,1)S(1)}, bf16[13,64,128]{2,1,0:T(8,128)(2,1)S(1)}, u32[]{:S(2)}, u32[]{:S(2)}) collective-permute-start(bf16[13,64,128]{2,1,0:T(8,128)(2,1)S(1)} %collective-permute-done.5.refs_1_), channel_id=1, source_target_pairs={{0,4},{1,5},{2,6},{3,7},{4,0},{5,1},{6,2},{7,3},{8,12},{9,13},{10,... | collective-permute-start | bytes 638984 | tf_op jit(solution)/shard_map/ppermute | solution.py:38
  25.3 11.6 %collective-permute-start.8 = (bf16[13,64,128]{2,1,0:T(8,128)(2,1)S(1)}, bf16[13,64,128]{2,1,0:T(8,128)(2,1)S(1)}, u32[]{:S(2)}, u32[]{:S(2)}) collective-permute-start(bf16[13,64,128]{2,1,0:T(8,128)(2,1)S(1)} %collective-permute-done.5.refs_1_), channel_id=1, source_target_pairs={{0,2},{1,3},{2,0},{3,1},{4,6},{5,7},{6,4},{7,5},{8,10},{9,11},{10,... | collective-permute-start | bytes 638984 | tf_op jit(solution)/shard_map/ppermute | solution.py:38
  37.0 8.2 %collective-permute-start.10 = (bf16[26,64,128]{2,1,0:T(8,128)(2,1)S(1)}, bf16[26,64,128]{2,1,0:T(8,128)(2,1)S(1)}, u32[]{:S(2)}, u32[]{:S(2)}) collective-permute-start(bf16[26,64,128]{2,1,0:T(8,128)(2,1)S(1)} %choose.2), channel_id=1, source_target_pairs={{0,4},{1,3},{2,6},{3,1},{4,0},{5,7},{6,2},{7,5},{8,12},{9,11},{10,... | collective-permute-start | bytes 1277960 | tf_op jit(solution)/shard_map/ppermute | solution.py:38
  45.2 10.5 %collective-permute-start.11 = (bf16[26,64,128]{2,1,0:T(8,128)(2,1)S(1)}, bf16[26,64,128]{2,1,0:T(8,128)(2,1)S(1)}, u32[]{:S(2)}, u32[]{:S(2)}) collective-permute-start(bf16[26,64,128]{2,1,0:T(8,128)(2,1)S(1)} %join.1.refs_0_), channel_id=1, source_target_pairs={{0,2},{1,3},{2,0},{3,1},{4,6},{5,7},{6,4},{7,5},{8,10},{9,11},{10,... | collective-permute-start | bytes 1277960 | tf_op jit(solution)/shard_map/ppermute | solution.py:38
  45.3 10.5 %collective-permute-start.12 = (bf16[26,64,128]{2,1,0:T(8,128)(2,1)S(1)}, bf16[26,64,128]{2,1,0:T(8,128)(2,1)S(1)}, u32[]{:S(2)}, u32[]{:S(2)}) collective-permute-start(bf16[26,64,128]{2,1,0:T(8,128)(2,1)S(1)} %join.1.refs_0_), channel_id=1, source_target_pairs={{0,4},{1,5},{2,6},{3,7},{4,0},{5,1},{6,2},{7,3},{8,12},{9,13},{10,... | collective-permute-start | bytes 1277960 | tf_op jit(solution)/shard_map/ppermute | solution.py:38
  55.8 8.2 %collective-permute-start.13 = (bf16[26,64,128]{2,1,0:T(8,128)(2,1)S(1)}, bf16[26,64,128]{2,1,0:T(8,128)(2,1)S(1)}, u32[]{:S(2)}, u32[]{:S(2)}) collective-permute-start(bf16[26,64,128]{2,1,0:T(8,128)(2,1)S(1)} %choose.3), channel_id=1, source_target_pairs={{0,4},{1,3},{2,6},{3,1},{4,0},{5,7},{6,2},{7,5},{8,12},{9,11},{10,... | collective-permute-start | bytes 1277960 | tf_op jit(solution)/shard_map/ppermute | solution.py:38
  65.8 1.8 %collective-permute-start.15 = (f32[13,64,128]{2,1,0:T(8,128)S(1)}, f32[13,64,128]{2,1,0:T(8,128)S(1)}, u32[]{:S(2)}, u32[]{:S(2)}) collective-permute-start(f32[13,64,128]{2,1,0:T(8,128)S(1)} %get-tuple-element.54), channel_id=1, source_target_pairs={{0,1},{1,0},{2,3},{3,2},{4,5},{5,4},{6,7},{7,6},{8,9},{9,8},{10,11... | collective-permute-start | bytes 1277960 | tf_op jit(solution)/shard_map/ppermute | solution.py:38

commit v6 on v5

--- a/solution.py
+++ b/solution.py
@@ -130,7 +130,7 @@
 
 def skeleton_kernel(per, layers, me_ref, order_ref, comp_ref, basis_ref, transfer_ref,
                     owner_ref, leaf_ref, ordered_ref, shared_ref, first_ref, last_ref,
-                    table_ref, root_ref):
+                    entry_ref, block_ref, root_ref):
     step = pl.program_id(0)
     leaf_len = basis_ref.shape[2]
 
@@ -139,8 +139,8 @@
         root_ref[...] = jnp.zeros_like(root_ref)
         entry, block = owner_tables(me_ref[0], layers, owner_ref[...], leaf_ref[...])
         rows, lanes = entry.shape
-        table_ref[0, :rows, :lanes] = entry
-        table_ref[1, :rows, :lanes] = block
+        entry_ref[:rows, :lanes] = entry
+        block_ref[:rows, :lanes] = block
 
     hots = [one_hot_leaf(order_ref[pl.ds(step * per + i, 1), :], leaf_len) for i in range(per)]
     ordered = [
@@ -186,14 +186,16 @@
             pl.BlockSpec((leaves + 1, rank, fields), lambda s: (0, 0, 0)),
             pl.BlockSpec((leaf_len, fields), lambda s: (0, 0)),
             pl.BlockSpec((leaf_len, fields), lambda s: (0, 0)),
-            pl.BlockSpec((2, 16, 128), lambda s: (0, 0, 0)),
+            pl.BlockSpec((16, 128), lambda s: (0, 0)),
+            pl.BlockSpec((16, 128), lambda s: (0, 0)),
         ],
         out_shape=[
             jax.ShapeDtypeStruct((leaves * leaf_len, fields), BF),
             jax.ShapeDtypeStruct((leaves + 1, rank, fields), BF),
             edge,
             edge,
-            jax.ShapeDtypeStruct((2, 16, 128), jnp.int32),
+            jax.ShapeDtypeStruct((16, 128), jnp.int32),
+            jax.ShapeDtypeStruct((16, 128), jnp.int32),
         ],
         scratch_shapes=[pltpu.VMEM((rank, fields), F32)],
         compiler_params=params(16),
@@ -224,35 +226,42 @@
     )(*parts)
 
 
-def choose_kernel(me_ref, *refs):
-    out = refs[-1]
-    number = len(refs) // 2
+def choose_kernel(number, me_ref, *refs):
+    ins, outs = refs[:2 * number], refs[2 * number:]
     for core in range(2):
         @pl.when(me_ref[0] % 2 == core)
         def _(core=core):
-            join_kernel(*refs[core * number:(core + 1) * number], out)
-
-
-def choose(me, from_x, from_y):
+            at = 0
+            for ref in ins[core * number:(core + 1) * number]:
+                done = 0
+                while done < ref.shape[0]:
+                    out, base = outs[at // outs[0].shape[0]], at % outs[0].shape[0]
+                    size = min(ref.shape[0] - done, out.shape[0] - base)
+                    out[base:base + size] = ref[done:done + size]
+                    done, at = done + size, at + size
+
+
+def choose(me, from_x, from_y, streams):
     parts = list(from_x) + list(from_y)
-    shape = (sum(part.shape[0] for part in from_x),) + from_x[0].shape[1:]
+    total = sum(part.shape[0] for part in from_x)
+    shape = jax.ShapeDtypeStruct((total // streams,) + from_x[0].shape[1:], BF)
     return pl.pallas_call(
-        choose_kernel,
+        functools.partial(choose_kernel, len(from_x)),
         name="choose",
         in_specs=[scalars()] + [whole()] * len(parts),
-        out_specs=whole(),
-        out_shape=jax.ShapeDtypeStruct(shape, BF),
-        compiler_params=params(8 if shape[0] <= 32 else 32),
+        out_specs=[whole()] * streams,
+        out_shape=[shape] * streams,
+        compiler_params=params(8 if total <= 32 else 32),
         cost_estimate=cost(0, MIB // 2),
     )(me, *parts)
 
 
-def dense_kernel(per, slots, table_ref, coupling_ref, top_ref, transfer_ref,
-                 own_ref, other_ref, turned_ref):
+def dense_kernel(per, slots, me_ref, entry_ref, block_ref, first_ref, last_ref, coupling_ref, top_ref,
+                 transfer_ref, own_ref, other_ref, cross_ref, turned_ref):
     step = pl.program_id(0)
     rank = coupling_ref.shape[2]
+    fields = first_ref.shape[1]
     leaves = own_ref.shape[0] - 1
-
     for i in range(per):
         turned_ref[step * per + i] = transfer_ref[i].T
 
@@ -260,7 +269,7 @@
         for slot in range(0, slots, 2):
             pair = []
             for one in (slot, slot + 1):
-                entry = table_ref[0, entry_row, plane * slots + one]
+                entry = entry_ref[entry_row, plane * slots + one]
                 block = block_of(jnp.maximum(entry, 0))
                 pair.append(jnp.where(entry >= 0, block, jnp.zeros_like(block)))
             out_ref[row, :, slot * rank:(slot + 2) * rank] = jnp.concatenate(pair, axis=1)
@@ -274,40 +283,61 @@
         def _(plane=plane, out_ref=out_ref):
             fill(out_ref, plane, leaves, 0, lambda entry: top_ref[0, entry])
 
-
-def dense_couplings(table, coupling, top_coupling, transfer, slots, per=4):
+    @pl.when(step == 0)
+    def _():
+        even = me_ref[0] % 2 == 0
+        first, last = first_ref[...], last_ref[...]
+        cross_ref[...] = jnp.where(even, first, last)
+        inner = jnp.where(even, last, first)
+        for t in range(first.shape[0] // rank):
+            other_ref[leaves + 1, :, t * fields:(t + 1) * fields] = inner[t * rank:(t + 1) * rank]
+        other_ref[leaves + 2] = jnp.zeros(other_ref.shape[1:], BF)
+        blocks = block_ref[...].astype(F32).astype(BF)
+        other_ref[leaves + 2, :blocks.shape[0], :blocks.shape[1]] = blocks
+
+
+def dense_couplings(me, entry, block, first, last, coupling, top_coupling, transfer, slots, per=4):
     leaves, entries, rank, _ = coupling.shape
-    shape = jax.ShapeDtypeStruct((leaves + 1, rank, slots * rank), BF)
-    full = pl.BlockSpec((leaves + 1, rank, slots * rank), lambda s: (0, 0, 0))
+    own = (leaves + 1, rank, slots * rank)
+    other = (leaves + 3, rank, slots * rank)
     return pl.pallas_call(
         functools.partial(dense_kernel, per, slots),
         name="couplings_by_owner",
         grid=(leaves // per,),
         in_specs=[
             scalars(),
+            scalars(),
+            pl.BlockSpec(block.shape, lambda s: (0, 0)),
+            pl.BlockSpec(first.shape, lambda s: (0, 0)),
+            pl.BlockSpec(last.shape, lambda s: (0, 0)),
             pl.BlockSpec((per, entries, rank, rank), lambda s: (s, 0, 0, 0)),
             pl.BlockSpec(top_coupling.shape, lambda s: (0, 0, 0, 0)),
             pl.BlockSpec((per, rank, rank), lambda s: (s, 0, 0)),
         ],
-        out_specs=[full, full, pl.BlockSpec(transfer.shape, lambda s: (0, 0, 0))],
-        out_shape=[shape, shape, jax.ShapeDtypeStruct(transfer.shape, BF)],
+        out_specs=[
+            pl.BlockSpec(own, lambda s: (0, 0, 0)),
+            pl.BlockSpec(other, lambda s: (0, 0, 0)),
+            pl.BlockSpec(first.shape, lambda s: (0, 0)),
+            pl.BlockSpec(transfer.shape, lambda s: (0, 0, 0)),
+        ],
+        out_shape=[
+            jax.ShapeDtypeStruct(own, BF),
+            jax.ShapeDtypeStruct(other, BF),
+            jax.ShapeDtypeStruct(first.shape, BF),
+            jax.ShapeDtypeStruct(transfer.shape, BF),
+        ],
         compiler_params=params(16 if slots <= 16 else 48),
         cost_estimate=cost(0, 8 * MIB),
-    )(table, *in_hbm(coupling, top_coupling, transfer))
-
-
-def round_kernel(first, steps, slots, counts, own_at, other_at, *refs):
+    )(me, entry, block, first, last, *in_hbm(coupling, top_coupling, transfer))
+
+
+def round_kernel(plane, steps, slots, counts, at_ref, *refs):
     sides = []
     for number in counts:
         sides.append(refs[:number])
         refs = refs[number:]
-    own_blocks, other_blocks = refs[:2]
-    refs = refs[2:]
-    if first:
-        own_out, other_out = refs
-    else:
-        own_in, other_in, own_out, other_out = refs
-    rows, rank, _ = own_out.shape
+    blocks_ref, out = refs[0], refs[-1]
+    rows, rank, _ = out.shape
     low, high = steps[0] * 4 * rank, (steps[-1] + 1) * 4 * rank
 
     def block_at(side, base, index):
@@ -316,51 +346,59 @@
                 return ref[base + index]
             base -= ref.shape[0]
 
-    for plane, at_ref, blocks_ref, out in (
-        (0, own_at, own_blocks, own_out),
-        (1, other_at, other_blocks, other_out),
-    ):
-        for row in range(rows):
-            chosen = [
-                block_at(side, place * rows, at_ref[1, (row + 1) % rows, plane * slots + step * 4 + q])
-                for place, step in enumerate(steps)
-                for q, side in enumerate(sides)
-            ]
-            value = dot(blocks_ref[row, :, low:high], jnp.concatenate(chosen, axis=0))
-            if not first:
-                value = value + (own_in if plane == 0 else other_in)[row]
-            out[row] = value
-
-
-def far_round(steps, slots, own_at, other_at, parts, blocks, sums):
-    rows, rank, _ = blocks[0].shape
-    fields = parts[0][0].shape[2]
-    first = sums is None
-    sum_shape = jax.ShapeDtypeStruct((rows, rank, fields), F32)
-    args = [part for side in parts for part in side] + list(blocks) + ([] if first else list(sums))
+    for row in range(rows):
+        chosen = [
+            block_at(side, place * rows, at_ref[(row + 1) % rows, plane * slots + step * 4 + q])
+            for place, step in enumerate(steps)
+            for q, side in enumerate(sides)
+        ]
+        value = dot(blocks_ref[row, :, low:high], jnp.concatenate(chosen, axis=0))
+        if len(refs) > 2:
+            value = value + refs[1][row]
+        out[row] = value
+
+
+def far_round(plane, steps, slots, at, parts, blocks, total=None):
+    rank, fields = parts[0][0].shape[1:]
+    rows = parts[0][0].shape[0] // (1 if len(parts[0]) > 1 else len(steps))
+    args = [part for side in parts for part in side] + [blocks] + ([] if total is None else [total])
     return pl.pallas_call(
-        functools.partial(round_kernel, first, steps, slots, [len(side) for side in parts]),
-        name="far_round_" + str(steps[0]),
-        in_specs=[scalars(), scalars()] + [whole()] * len(args),
-        out_specs=[whole(), whole()],
-        out_shape=[sum_shape, sum_shape],
+        functools.partial(round_kernel, plane, steps, slots, [len(side) for side in parts]),
+        name="far_" + str(plane) + "_" + str(steps[0]),
+        in_specs=[scalars()] + [whole()] * len(args),
+        out_specs=whole(),
+        out_shape=jax.ShapeDtypeStruct((rows, rank, fields), F32),
         compiler_params=params(16 if slots <= 16 else 48),
-        cost_estimate=cost(2 * rows * rank * 4 * rank * fields * 2 * len(steps), 2 * MIB),
-    )(own_at, other_at, *args)
+        cost_estimate=cost(rows * rank * 4 * rank * fields * 2 * len(steps), MIB),
+    )(at, *args)
 
 
 def near_kernel(edges, pair_of, last_pair, mask_ref, order_ref, table_ref, basis_ref,
                 prev_ref, cur_ref, next_ref, *refs):
     if edges:
-        before_ref, after_ref = refs[:2]
-    near_ref, turned_ref = refs[-2:]
+        me_ref, cross_ref, inner_ref, blocks_ref = refs[:4]
+        near_ref, turned_ref, at_ref = refs[-3:]
+    else:
+        near_ref, turned_ref = refs[-2:]
     pair = pair_of(pl.program_id(0))
     leaf_len = basis_ref.shape[2]
     low, high = cur_ref[:leaf_len, :], cur_ref[leaf_len:, :]
     prev, following = prev_ref[...], next_ref[...]
     if edges:
-        prev = jnp.where(pair == 0, before_ref[...], prev)
-        following = jnp.where(pair == last_pair, after_ref[...], following)
+        even = me_ref[0] % 2 == 0
+        cross = cross_ref[...]
+        wide = cross.shape[1]
+        inner = jnp.concatenate(
+            [inner_ref[0, :, t:t + wide] for t in range(0, inner_ref.shape[2], wide)], axis=0
+        )[:leaf_len]
+        prev = jnp.where(pair == 0, jnp.where(even, cross, inner), prev)
+        following = jnp.where(pair == last_pair, jnp.where(even, inner, cross), following)
+
+        @pl.when(pl.program_id(0) == 0)
+        def _():
+            rows, lanes = at_ref.shape
+            at_ref[...] = blocks_ref[0, :rows, :lanes].astype(F32).astype(jnp.int32)
+
 
     def masked(leaf, side, value):
         return jnp.where(mask_ref[side, leaf] > 0, value, jnp.zeros_like(value))
@@ -402,9 +440,18 @@
     ]
     args = [near_list.T, leaf_order, tables, basis, ordered, ordered, ordered]
     aliases = {}
+    extra = []
     if halos is not None:
-        in_specs += [pl.BlockSpec((leaf_len, fields), lambda s: (0, 0))] * 2
-        args += list(halos)
+        me, cross, other = halos
+        row = (1,) + other.shape[1:]
+        in_specs += [
+            scalars(),
+            pl.BlockSpec((leaf_len, fields), lambda s: (0, 0)),
+            pl.BlockSpec(row, lambda s: (leaves + 1, 0, 0)),
+            pl.BlockSpec(row, lambda s: (leaves + 2, 0, 0)),
+        ]
+        args += [me, cross, other, other]
+        extra = [(16, 128)]
     if filled is not None:
         aliases = {len(args): 0, len(args) + 1: 1}
         in_specs += [pl.BlockSpec(memory_space=pl.ANY)] * 2
@@ -417,11 +464,11 @@
         out_specs=[
             pl.BlockSpec((2 * leaf_len, fields), lambda s: (pair_of(s), 0)),
             pl.BlockSpec((2 * leaf_len, rank), lambda s: (pair_of(s), 0)),
-        ],
+        ] + [pl.BlockSpec(shape, lambda s: (0, 0)) for shape in extra],
         out_shape=[
             jax.ShapeDtypeStruct((leaves * leaf_len, fields), BF),
             jax.ShapeDtypeStruct((leaves * leaf_len, rank), BF),
-        ],
+        ] + [jax.ShapeDtypeStruct(shape, jnp.int32) for shape in extra],
         input_output_aliases=aliases,
         compiler_params=params(16),
         cost_estimate=cost(len(pairs) * 2 * leaf_len * leaf_len * fields * 10, len(pairs) * MIB),
@@ -492,7 +539,7 @@
     cut = pairs // 2
     me = lax.axis_index("subtree").reshape(1)
 
-    ordered, shared, first, last, table = skeletons_of(
+    ordered, shared, first, last, entry, own_at = skeletons_of(
         me, leaf_order, composition, leaf_basis, transfer, admissible_owner, admissible_leaf, layers
     )
     tables = jnp.asarray(near_tables(leaf_len))
@@ -500,36 +547,40 @@
 
     line = along_z(shared, 1)
     from_x, from_y = over_x(shared), over_y(shared)
-    own_blocks, my_other, turned_transfer = dense_couplings(
-        table, coupling, top_coupling, transfer, slots
-    )
-    line = after(line, from_x, from_y, my_other)
+    lines = [along_z(shared, layers - 1)]
+    own_blocks, my_other, cross, turned_transfer = dense_couplings(
+        me, entry, own_at, first, last, coupling, top_coupling, transfer, slots
+    )
+    line = after(line, from_x, from_y, lines[0], my_other)
     next_x, next_y = over_x(line), over_y(line)
-    lines = [along_z(after(shared, my_other), layers - 1)]
     for _ in range(layers - 3):
         lines.append(along_z(line if len(lines) == 1 else lines[-1], 1))
-    other_blocks = over_core(my_other)
-    other_table = over_core(table)
-    before = lax.ppermute(last, "subtree", [(d, d + 1) for d in range(count - 1)])
-    behind = lax.ppermute(first, "subtree", [(d + 1, d) for d in range(count - 1)])
+    filled = near_field(list(range(1, cut)), *near_args, after(ordered, line))
+
+    joined = join([after(lines[0], next_x, next_y, filled[0])] + lines[1:])
+    last_x, last_y = over_x(joined), over_y(joined)
     round_0 = ((shared, line), (from_x, next_x), (from_y, next_y))
-    far = onward(choose(me, (after(from_x, before, behind, other_table, *lines), next_x), round_0[2]))
-    round_0 += ((far,),)
-    held = after(ordered, next_x, next_y, before, behind, other_table, *lines)
-    filled = near_field(list(range(1, cut)), *near_args, held)
-
-    joined = join([after(lines[0], far, filled[0])] + lines[1:])
-    last_x, last_y = over_x(joined), over_y(joined)
+    round_0 += (tuple(map(onward, choose(me, *round_0[1:], 1))),)
+    other_blocks = over_core(after(my_other, joined))
+    cross = lax.ppermute(
+        cross,
+        "subtree",
+        [(d, d + 1) for d in range(1, count - 1, 2)] + [(d, d - 1) for d in range(2, count, 2)],
+    )
     held = after(ordered, joined)
     filled = near_field(list(range(cut, pairs - 1)), *near_args, held, filled=filled)
-    filled = near_field([0, pairs - 1], *near_args, ordered, halos=(before, behind), filled=filled)
-    blocks = (own_blocks, other_blocks)
-    far = onward(choose(me, (after(last_x, filled[0]),), (last_y,)))
-    sums = far_round([0, 1], slots, table, other_table, round_0, blocks, None)
-    round_1 = ((joined,), (last_x,), (last_y,), (after(far, sums[0]),))
-    sums = far_round(list(range(2, layers)), slots, table, other_table, round_1, blocks, sums)
-    received = over_core(sums[1])
-    return field(sums[0], received, turned_transfer, *filled)
+    far = tuple(map(onward, choose(me, (after(last_x, filled[0], cross),), (last_y,), 2)))
+    *filled, other_at = near_field(
+        [0, pairs - 1], *near_args, after(ordered, filled[0]), halos=(me, cross, other_blocks), filled=filled
+    )
+    steps = [0, 1]
+    own = far_round(0, steps, slots, own_at, round_0, own_blocks)
+    other = far_round(1, steps, slots, other_at, round_0, other_blocks)
+    steps = list(range(2, layers))
+    round_1 = ((joined,), (last_x,), (last_y,), (after(far[0], own, other),) + far[1:])
+    other = far_round(1, steps, slots, other_at, round_1, other_blocks, other)
+    own = far_round(0, steps, slots, own_at, round_1, own_blocks, own)
+    return field(own, over_core(other), turned_transfer, *filled)
 
 
 def solution(mesh):

time: 70.6 us -> 64.2 us (0.909)
  waiting for transfers between devices: 26.8 us -> 14.1 us
  starting transfers between devices: 17.9 us -> 23 us
  Pallas kernels: 25.5 us -> 26.7 us
    ppermute x14, waiting for transfers between devices: 26.8 us -> 14.1 us  [send(): lax.ppermute(block, 'subtree', [(d, target(d)) for d in range(count)])]
    ppermute x14, starting transfers between devices: 14.2 us -> 22.4 us  [send(): lax.ppermute(block, 'subtree', [(d, target(d)) for d in range(count)])]
    ppermute x2 -> x1, starting transfers between devices: 3.69 us -> 0.66 us  [on_device(): lax.ppermute(cross, 'subtree', [(d, d + 1) for d in range(1, count - 1, 2...]
    pallas_call x4 -> x6, Pallas kernels: 3.6 us -> 4.38 us  [the longest x4 4.31 us: far_round(): pl.pallas_call(functools.partial(round_kernel, plane, steps, slots, [len(...]
  transfers between devices with their start and end apart: 16 -> 15, of which waited for: 7 -> 8; matrix products, arithmetic and copies ran while one was open for 0% -> 0% of each run, Pallas kernels for 23% -> 28%
where the time goes in v6:
time: 64.2 us; the launch traced here: 64 us
  Pallas kernels  26.7 us (42%)
  starting transfers between devices  23 us (36%)
  waiting for transfers between devices  14.1 us (22%)
    ppermute x14, starting transfers between devices, send(): lax.ppermute(block, 'subtree', [(d, target(d)) for d in range(count)])  22.4 us
    ppermute x14, waiting for transfers between devices, send(): lax.ppermute(block, 'subtree', [(d, target(d)) for d in range(count)])  14.1 us
    pallas_call x3, Pallas kernels, near_field(): pl.pallas_call(functools.partial(near_kernel, halos is not None, pair_of,...  10.7 us
    pallas_call x1, Pallas kernels, skeletons_of(): pl.pallas_call(functools.partial(skeleton_kernel, per, layers), name='ord...  4.66 us
    pallas_call x4, Pallas kernels, far_round(): pl.pallas_call(functools.partial(round_kernel, plane, steps, slots, [len(...  4.31 us
    pallas_call x1, Pallas kernels, dense_couplings(): pl.pallas_call(functools.partial(dense_kernel, per, slots), name='couplin...  4.19 us
    pallas_call x1, Pallas kernels, field(): pl.pallas_call(functools.partial(field_kernel, per), name='local_and_fiel...  2.73 us
  transfers between devices with their start and end apart: 15, of which 8 were waited for; matrix products, arithmetic and copies ran while one was open for 0% of the time, Pallas kernels for 28%

profile of v6, /device:TPU:0, one launch (start us, length us, event | category | flops | bytes accessed | tf_op | source)
XLA Modules:
  0.0 64.0 jit_solution(7018947445295116983)
XLA Ops:
  0.0 4.7 %order_and_skeleton.1 = (bf16[6144,128]{1,0:T(8,128)(2,1)S(1)}, bf16[13,64,128]{2,1,0:T(8,128)(2,1)S(1)}, bf16[512,128]{1,0:T(8,128)(2,1)S(1)}, bf16[512,128]{1,...) custom-call(s32[1]{0:T(128)} %bitcast.me_ref.refs_0_, s32[12,512]{1,0:T(8,128)} %order_ref.7, ...), custom_call_target="tpu_custom_call" | custom-call | flops 12582912 | bytes 65536 | tf_op jit(solution)/shard_map/order_and_skeleton/pallas_call | solution.py:171
  4.7 3.0 %collective-permute-start.2 = (bf16[13,64,128]{2,1,0:T(8,128)(2,1)S(1)}, bf16[13,64,128]{2,1,0:T(8,128)(2,1)S(1)}, u32[]{:S(2)}, u32[]{:S(2)}) collective-permute-start(bf16[13,64,128]{2,1,0:T(8,128)(2,1)S(1)} %get-tuple-element.33.refs_0_), channel_id=1, source_target_pairs={{0,2},{1,3},{2,0},{3,1},{4,6},{5,7},{6,4},{7,5},{8,10},{9,11},{10,... | collective-permute-start | bytes 638984 | tf_op jit(solution)/shard_map/ppermute | solution.py:38
  7.7 1.5 %collective-permute-start.3 = (bf16[13,64,128]{2,1,0:T(8,128)(2,1)S(1)}, bf16[13,64,128]{2,1,0:T(8,128)(2,1)S(1)}, u32[]{:S(2)}, u32[]{:S(2)}) collective-permute-start(bf16[13,64,128]{2,1,0:T(8,128)(2,1)S(1)} %get-tuple-element.33.refs_0_), channel_id=1, source_target_pairs={{0,4},{1,5},{2,6},{3,7},{4,0},{5,1},{6,2},{7,3},{8,12},{9,13},{10,... | collective-permute-start | bytes 638984 | tf_op jit(solution)/shard_map/ppermute | solution.py:38
  9.2 3.6 %collective-permute-start = (bf16[13,64,128]{2,1,0:T(8,128)(2,1)S(1)}, bf16[13,64,128]{2,1,0:T(8,128)(2,1)S(1)}, u32[]{:S(2)}, u32[]{:S(2)}) collective-permute-start(bf16[13,64,128]{2,1,0:T(8,128)(2,1)S(1)} %get-tuple-element.33.refs_0_), channel_id=1, source_target_pairs={{0,24},{1,25},{2,26},{3,27},{4,28},{5,29},{6,30},{7,31},{8,0},{9,1... | collective-permute-start | bytes 638984 | tf_op jit(solution)/shard_map/ppermute | solution.py:38
  12.8 4.2 %couplings_by_owner.1 = (bf16[13,64,1024]{2,1,0:T(8,128)(2,1)S(1)}, bf16[15,64,1024]{2,1,0:T(8,128)(2,1)S(1)}, bf16[512,128]{1,0:T(8,128)(2,1)S(1)}, bf16[12,64,64]{2,1,0:T(8,128)(2,1)S(1)}) custom-call(s32[1]{0:T(128)} %bitcast.me_ref.refs_0_, s32[16,128]{1,0:T(8,128)S(1)} %get-tuple-element.34.entry_ref, s32[16,128]{1,0:T(8,128)S(1)} %get-tuple-element.32.block_ref.at_ref, ...), custom_call_target="tpu_custom_call" | custom-call | bytes 131072 | tf_op jit(solution)/shard_map/couplings_by_owner/pallas_call | solution.py:303
  17.0 1.5 %collective-permute-done.refs_0_ = bf16[13,64,128]{2,1,0:T(8,128)(2,1)S(1)} collective-permute-done((bf16[13,64,128]{2,1,0:T(8,128)(2,1)S(1)}, bf16[13,64,128]{2,1,0:T(8,128)(2,1)S(1)}, u32[]{:S(2)}, u32[]{:S(2)}) %collective-permute-start) | collective-permute-done | bytes 213024 | tf_op jit(solution)/shard_map/ppermute | solution.py:38
  18.5 3.7 %collective-permute-done.1.refs_1_ = bf16[13,64,128]{2,1,0:T(8,128)(2,1)S(1)} collective-permute-done((bf16[13,64,128]{2,1,0:T(8,128)(2,1)S(1)}, bf16[13,64,128]{2,1,0:T(8,128)(2,1)S(1)}, u32[]{:S(2)}, u32[]{:S(2)}) %collective-permute-start.1) | collective-permute-done | bytes 213024 | tf_op jit(solution)/shard_map/ppermute | solution.py:38
  23.3 1.6 %collective-permute-start.6 = (bf16[13,64,128]{2,1,0:T(8,128)(2,1)S(1)}, bf16[13,64,128]{2,1,0:T(8,128)(2,1)S(1)}, u32[]{:S(2)}, u32[]{:S(2)}) collective-permute-start(bf16[13,64,128]{2,1,0:T(8,128)(2,1)S(1)} %collective-permute-done.1.refs_1_), channel_id=1, source_target_pairs={{0,8},{1,9},{2,10},{3,11},{4,12},{5,13},{6,14},{7,15},{8,16},{9,17... | collective-permute-start | bytes 638984 | tf_op jit(solution)/shard_map/ppermute | solution.py:38
  24.9 3.5 %near_1.1 = (bf16[6144,128]{1,0:T(8,128)(2,1)S(1)}, bf16[6144,64]{1,0:T(8,128)(2,1)S(1)}) custom-call(s32[2,12]{1,0:T(2,128)S(1)} %bitcast.2, s32[12,512]{1,0:T(8,128)S(1)} %copy-done.2, bf16[512,1536]{1,0:T(8,128)(2,1)S(1)} %copy-done, bf16[12,64,512]{2,1,0:T(8,128)(2,1)S(1)} %copy-done.1, ...), custom_call_target="tpu_custom_call" | custom-call | flops 20971520 | bytes 32768 | tf_op jit(solution)/shard_map/near_1/pallas_call | solution.py:459
  28.6 2.3 %collective-permute-done.6.refs_1_ = bf16[13,64,128]{2,1,0:T(8,128)(2,1)S(1)} collective-permute-done((bf16[13,64,128]{2,1,0:T(8,128)(2,1)S(1)}, bf16[13,64,128]{2,1,0:T(8,128)(2,1)S(1)}, u32[]{:S(2)}, u32[]{:S(2)}) %collective-permute-start.6) | collective-permute-done | bytes 213024 | tf_op jit(solution)/shard_map/ppermute | solution.py:38
  31.0 1.6 %collective-permute-start.7 = (bf16[26,64,128]{2,1,0:T(8,128)(2,1)S(1)}, bf16[26,64,128]{2,1,0:T(8,128)(2,1)S(1)}, u32[]{:S(2)}, u32[]{:S(2)}) collective-permute-start(bf16[26,64,128]{2,1,0:T(8,128)(2,1)S(1)} %join.1.refs_0_), channel_id=1, source_target_pairs={{0,2},{1,3},{2,0},{3,1},{4,6},{5,7},{6,4},{7,5},{8,10},{9,11},{10,... | collective-permute-start | bytes 1277960 | tf_op jit(solution)/shard_map/ppermute | solution.py:38
  32.6 1.5 %collective-permute-start.8 = (bf16[26,64,128]{2,1,0:T(8,128)(2,1)S(1)}, bf16[26,64,128]{2,1,0:T(8,128)(2,1)S(1)}, u32[]{:S(2)}, u32[]{:S(2)}) collective-permute-start(bf16[26,64,128]{2,1,0:T(8,128)(2,1)S(1)} %join.1.refs_0_), channel_id=1, source_target_pairs={{0,4},{1,5},{2,6},{3,7},{4,0},{5,1},{6,2},{7,3},{8,12},{9,13},{10,... | collective-permute-start | bytes 1277960 | tf_op jit(solution)/shard_map/ppermute | solution.py:38
  34.1 0.6 collective-permute-start.11
  34.7 0.7 %collective-permute-start.9 = (bf16[512,128]{1,0:T(8,128)(2,1)S(1)}, bf16[512,128]{1,0:T(8,128)(2,1)S(1)}, u32[]{:S(2)}, u32[]{:S(2)}) collective-permute-start(bf16[512,128]{1,0:T(8,128)(2,1)S(1)} %get-tuple-element.46), channel_id=1, source_target_pairs={{1,2},{3,4},{5,6},{7,8},{9,10},{11,12},{13,14},{15,16},{17,18},{19... | collective-permute-start | bytes 393224 | tf_op jit(solution)/shard_map/ppermute | solution.py:565
  35.4 3.5 %near_3.1 = (bf16[6144,128]{1,0:T(8,128)(2,1)S(1)}, bf16[6144,64]{1,0:T(8,128)(2,1)S(1)}) custom-call(s32[2,12]{1,0:T(2,128)S(1)} %bitcast.3, s32[12,512]{1,0:T(8,128)S(1)} %copy-done.2, bf16[512,1536]{1,0:T(8,128)(2,1)S(1)} %copy-done, bf16[12,64,512]{2,1,0:T(8,128)(2,1)S(1)} %copy-done.1, ...), custom_call_target="tpu_custom_call", output_to_operand_aliasing={{0}: (7, {}), {1}: (8, {})} | custom-call | flops 20971520 | bytes 32768 | tf_op jit(solution)/shard_map/near_3/pallas_call | solution.py:459
  38.9 5.3 %collective-permute-done.7.refs_0_.refs_1_ = bf16[26,64,128]{2,1,0:T(8,128)(2,1)S(1)} collective-permute-done((bf16[26,64,128]{2,1,0:T(8,128)(2,1)S(1)}, bf16[26,64,128]{2,1,0:T(8,128)(2,1)S(1)}, u32[]{:S(2)}, u32[]{:S(2)}) %collective-permute-start.7) | collective-permute-done | bytes 426016 | tf_op jit(solution)/shard_map/ppermute | solution.py:38
  44.5 7.7 %collective-permute-start.10 = (bf16[13,64,128]{2,1,0:T(8,128)(2,1)S(1)}, bf16[13,64,128]{2,1,0:T(8,128)(2,1)S(1)}, u32[]{:S(2)}, u32[]{:S(2)}) collective-permute-start(bf16[13,64,128]{2,1,0:T(8,128)(2,1)S(1)} %get-tuple-element.48), channel_id=1, source_target_pairs={{0,4},{1,3},{2,6},{3,1},{4,0},{5,7},{6,2},{7,5},{8,12},{9,11},{10,... | collective-permute-start | bytes 638984 | tf_op jit(solution)/shard_map/ppermute | solution.py:38
  52.3 1.1 %far_0_0.1.refs_6_ = f32[13,64,128]{2,1,0:T(8,128)S(1)} custom-call(s32[16,128]{1,0:T(8,128)S(1)} %get-tuple-element.32.block_ref.at_ref, bf16[13,64,128]{2,1,0:T(8,128)(2,1)S(1)} %get-tuple-element.33.refs_0_, bf16[13,64,128]{2,1,0:T(8,128)(2,1)S(1)} %collective-permute-done.1.refs_1_, bf16[13,64,128]{2,1,0:T(8,128)(2,1)S(1)} %collective-permute-done.2.refs_0_.refs_2_, ...), custom_call_target="tpu_custom_call" | custom-call | flops 1703936 | bytes 16384 | tf_op jit(solution)/shard_map/far_0_0/pallas_call | solution.py:365
  53.4 3.8 %near_0.1 = (bf16[6144,128]{1,0:T(8,128)(2,1)S(1)}, bf16[6144,64]{1,0:T(8,128)(2,1)S(1)}, s32[16,128]{1,0:T(8,128)S(1)}) custom-call(s32[2,12]{1,0:T(2,128)S(1)} %bitcast.4, s32[12,512]{1,0:T(8,128)S(1)} %copy-done.2, bf16[512,1536]{1,0:T(8,128)(2,1)S(1)} %copy-done, ...), custom_call_target="tpu_custom_call", output_to_operand_aliasing={{0}: (11, {}), {1}: (12, {})} | custom-call | flops 20971520 | bytes 32768 | tf_op jit(solution)/shard_map/near_0/pallas_call | solution.py:459
  57.2 1.1 %far_1_0.1.refs_6_ = f32[13,64,128]{2,1,0:T(8,128)S(1)} custom-call(s32[16,128]{1,0:T(8,128)S(1)} %get-tuple-element.53.at_ref, bf16[13,64,128]{2,1,0:T(8,128)(2,1)S(1)} %get-tuple-element.33.refs_0_, bf16[13,64,128]{2,1,0:T(8,128)(2,1)S(1)} %collective-permute-done.1.refs_1_, bf16[13,64,128]{2,1,0:T(8,128)(2,1)S(1)} %collective-permute-done.2.refs_0_.refs_2_, ...), custom_call_target="tpu_custom_call" | custom-call | flops 1703936 | bytes 16384 | tf_op jit(solution)/shard_map/far_1_0/pallas_call | solution.py:365
  58.3 1.1 %far_1_2.1 = f32[13,64,128]{2,1,0:T(8,128)S(1)} custom-call(s32[16,128]{1,0:T(8,128)S(1)} %get-tuple-element.53.at_ref, bf16[26,64,128]{2,1,0:T(8,128)(2,1)S(1)} %join.1.refs_0_, bf16[26,64,128]{2,1,0:T(8,128)(2,1)S(1)} %collective-permute-done.7.refs_0_.refs_1_, bf16[26,64,128]{2,1,0:T(8,128)(2,1)S(1)} %collective-permute-done.8.refs_1_.refs_2_, ...), custom_call_target="tpu_custom_call" | custom-call | flops 1703936 | bytes 16384 | tf_op jit(solution)/shard_map/far_1_2/pallas_call | solution.py:365
  59.5 1.1 %far_0_2.1.own_ref = f32[13,64,128]{2,1,0:T(8,128)S(1)} custom-call(s32[16,128]{1,0:T(8,128)S(1)} %get-tuple-element.32.block_ref.at_ref, bf16[26,64,128]{2,1,0:T(8,128)(2,1)S(1)} %join.1.refs_0_, bf16[26,64,128]{2,1,0:T(8,128)(2,1)S(1)} %collective-permute-done.7.refs_0_.refs_1_, bf16[26,64,128]{2,1,0:T(8,128)(2,1)S(1)} %collective-permute-done.8.refs_1_.refs_2_, ...), custom_call_target="tpu_custom_call" | custom-call | flops 1703936 | bytes 16384 | tf_op jit(solution)/shard_map/far_0_2/pallas_call | solution.py:365
  60.6 0.7 %collective-permute-done.14.other_ref = f32[13,64,128]{2,1,0:T(8,128)S(1)} collective-permute-done((f32[13,64,128]{2,1,0:T(8,128)S(1)}, f32[13,64,128]{2,1,0:T(8,128)S(1)}, u32[]{:S(2)}, u32[]{:S(2)}) %collective-permute-start.14) | collective-permute-done | bytes 426016 | tf_op jit(solution)/shard_map/ppermute | solution.py:38
  61.2 2.7 %local_and_field.1 = bf16[6144,128]{1,0:T(8,128)(2,1)} custom-call(f32[13,64,128]{2,1,0:T(8,128)S(1)} %far_0_2.1.own_ref, f32[13,64,128]{2,1,0:T(8,128)S(1)} %collective-permute-done.14.other_ref, bf16[12,64,64]{2,1,0:T(8,128)(2,1)S(1)} %get-tuple-element.56.turned_transfer_ref, bf16[6144,128]{1,0:T(8,128)(2,1)S(1)} %get-tuple-element.57.near_ref, ...), custom_call_target="tpu_custom_call" | custom-call | flops 1572864 | bytes 65536 | tf_op jit(solution)/shard_map/local_and_field/pallas_call | solution.py:501
  (27 shorter events, 2.0 us)
Async XLA Ops:
  4.7 12.4 %collective-permute-start.2 = (bf16[13,64,128]{2,1,0:T(8,128)(2,1)S(1)}, bf16[13,64,128]{2,1,0:T(8,128)(2,1)S(1)}, u32[]{:S(2)}, u32[]{:S(2)}) collective-permute-start(bf16[13,64,128]{2,1,0:T(8,128)(2,1)S(1)} %get-tuple-element.33.refs_0_), channel_id=1, source_target_pairs={{0,2},{1,3},{2,0},{3,1},{4,6},{5,7},{6,4},{7,5},{8,10},{9,11},{10,... | collective-permute-start | bytes 638984 | tf_op jit(solution)/shard_map/ppermute | solution.py:38
  7.7 9.4 %collective-permute-start.3 = (bf16[13,64,128]{2,1,0:T(8,128)(2,1)S(1)}, bf16[13,64,128]{2,1,0:T(8,128)(2,1)S(1)}, u32[]{:S(2)}, u32[]{:S(2)}) collective-permute-start(bf16[13,64,128]{2,1,0:T(8,128)(2,1)S(1)} %get-tuple-element.33.refs_0_), channel_id=1, source_target_pairs={{0,4},{1,5},{2,6},{3,7},{4,0},{5,1},{6,2},{7,3},{8,12},{9,13},{10,... | collective-permute-start | bytes 638984 | tf_op jit(solution)/shard_map/ppermute | solution.py:38
  9.2 9.3 %collective-permute-start = (bf16[13,64,128]{2,1,0:T(8,128)(2,1)S(1)}, bf16[13,64,128]{2,1,0:T(8,128)(2,1)S(1)}, u32[]{:S(2)}, u32[]{:S(2)}) collective-permute-start(bf16[13,64,128]{2,1,0:T(8,128)(2,1)S(1)} %get-tuple-element.33.refs_0_), channel_id=1, source_target_pairs={{0,24},{1,25},{2,26},{3,27},{4,28},{5,29},{6,30},{7,31},{8,0},{9,1... | collective-permute-start | bytes 638984 | tf_op jit(solution)/shard_map/ppermute | solution.py:38
  12.8 9.4 %collective-permute-start.1 = (bf16[13,64,128]{2,1,0:T(8,128)(2,1)S(1)}, bf16[13,64,128]{2,1,0:T(8,128)(2,1)S(1)}, u32[]{:S(2)}, u32[]{:S(2)}) collective-permute-start(bf16[13,64,128]{2,1,0:T(8,128)(2,1)S(1)} %get-tuple-element.33.refs_0_), channel_id=1, source_target_pairs={{0,8},{1,9},{2,10},{3,11},{4,12},{5,13},{6,14},{7,15},{8,16},{9,17... | collective-permute-start | bytes 638984 | tf_op jit(solution)/shard_map/ppermute | solution.py:38
  12.8 12.1 %copy-start = (bf16[512,1536]{1,0:T(8,128)(2,1)S(1)}, bf16[512,1536]{1,0:T(8,128)(2,1)}, u32[]{:S(2)}) copy-start(bf16[512,1536]{1,0:T(8,128)(2,1)} %constant.6.clone.table_ref) | copy-start | bytes 4718596
  12.8 12.1 %copy-start.1 = (bf16[12,64,512]{2,1,0:T(8,128)(2,1)S(1)}, bf16[12,64,512]{2,1,0:T(8,128)(2,1)}, u32[]{:S(2)}) copy-start(bf16[12,64,512]{2,1,0:T(8,128)(2,1)} %basis_ref.7) | copy-start | bytes 2359300
  12.8 12.1 %copy-start.2 = (s32[12,512]{1,0:T(8,128)S(1)}, s32[12,512]{1,0:T(8,128)}, u32[]{:S(2)}) copy-start(s32[12,512]{1,0:T(8,128)} %order_ref.7) | copy-start | bytes 73732
  12.8 12.1 %copy-start.3 = (s32[12,2]{0,1:T(2,128)S(1)}, s32[12,2]{0,1:T(2,128)}, u32[]{:S(2)}) copy-start(s32[12,2]{0,1:T(2,128)} %param.17) | copy-start | bytes 292
  22.2 6.1 %collective-permute-start.4 = (bf16[13,64,128]{2,1,0:T(8,128)(2,1)S(1)}, bf16[13,64,128]{2,1,0:T(8,128)(2,1)S(1)}, u32[]{:S(2)}, u32[]{:S(2)}) collective-permute-start(bf16[13,64,128]{2,1,0:T(8,128)(2,1)S(1)} %collective-permute-done.1.refs_1_), channel_id=1, source_target_pairs={{0,2},{1,3},{2,0},{3,1},{4,6},{5,7},{6,4},{7,5},{8,10},{9,11},{10,... | collective-permute-start | bytes 638984 | tf_op jit(solution)/shard_map/ppermute | solution.py:38
  22.7 5.8 %collective-permute-start.5 = (bf16[13,64,128]{2,1,0:T(8,128)(2,1)S(1)}, bf16[13,64,128]{2,1,0:T(8,128)(2,1)S(1)}, u32[]{:S(2)}, u32[]{:S(2)}) collective-permute-start(bf16[13,64,128]{2,1,0:T(8,128)(2,1)S(1)} %collective-permute-done.1.refs_1_), channel_id=1, source_target_pairs={{0,4},{1,5},{2,6},{3,7},{4,0},{5,1},{6,2},{7,3},{8,12},{9,13},{10,... | collective-permute-start | bytes 638984 | tf_op jit(solution)/shard_map/ppermute | solution.py:38
  23.3 7.6 %collective-permute-start.6 = (bf16[13,64,128]{2,1,0:T(8,128)(2,1)S(1)}, bf16[13,64,128]{2,1,0:T(8,128)(2,1)S(1)}, u32[]{:S(2)}, u32[]{:S(2)}) collective-permute-start(bf16[13,64,128]{2,1,0:T(8,128)(2,1)S(1)} %collective-permute-done.1.refs_1_), channel_id=1, source_target_pairs={{0,8},{1,9},{2,10},{3,11},{4,12},{5,13},{6,14},{7,15},{8,16},{9,17... | collective-permute-start | bytes 638984 | tf_op jit(solution)/shard_map/ppermute | solution.py:38
  30.9 22.4 %collective-permute-start.12 = (bf16[15,64,1024]{2,1,0:T(8,128)(2,1)S(1)}, bf16[15,64,1024]{2,1,0:T(8,128)(2,1)S(1)}, u32[]{:S(2)}, u32[]{:S(2)}) collective-permute-start(bf16[15,64,1024]{2,1,0:T(8,128)(2,1)S(1)} %get-tuple-element.51), channel_id=1, source_target_pairs={{0,1},{1,0},{2,3},{3,2},{4,5},{5,4},{6,7},{7,6},{8,9},{9,8},{10,11... | collective-permute-start | bytes 5898248 | tf_op jit(solution)/shard_map/ppermute | solution.py:38
  31.0 13.1 %collective-permute-start.7 = (bf16[26,64,128]{2,1,0:T(8,128)(2,1)S(1)}, bf16[26,64,128]{2,1,0:T(8,128)(2,1)S(1)}, u32[]{:S(2)}, u32[]{:S(2)}) collective-permute-start(bf16[26,64,128]{2,1,0:T(8,128)(2,1)S(1)} %join.1.refs_0_), channel_id=1, source_target_pairs={{0,2},{1,3},{2,0},{3,1},{4,6},{5,7},{6,4},{7,5},{8,10},{9,11},{10,... | collective-permute-start | bytes 1277960 | tf_op jit(solution)/shard_map/ppermute | solution.py:38
  32.6 11.9 %collective-permute-start.8 = (bf16[26,64,128]{2,1,0:T(8,128)(2,1)S(1)}, bf16[26,64,128]{2,1,0:T(8,128)(2,1)S(1)}, u32[]{:S(2)}, u32[]{:S(2)}) collective-permute-start(bf16[26,64,128]{2,1,0:T(8,128)(2,1)S(1)} %join.1.refs_0_), channel_id=1, source_target_pairs={{0,4},{1,5},{2,6},{3,7},{4,0},{5,1},{6,2},{7,3},{8,12},{9,13},{10,... | collective-permute-start | bytes 1277960 | tf_op jit(solution)/shard_map/ppermute | solution.py:38
  34.1 18.1 %collective-permute-start.11 = (bf16[26,64,128]{2,1,0:T(8,128)(2,1)S(1)}, bf16[26,64,128]{2,1,0:T(8,128)(2,1)S(1)}, u32[]{:S(2)}, u32[]{:S(2)}) collective-permute-start(bf16[26,64,128]{2,1,0:T(8,128)(2,1)S(1)} %choose.3), channel_id=1, source_target_pairs={{0,4},{1,3},{2,6},{3,1},{4,0},{5,7},{6,2},{7,5},{8,12},{9,11},{10,... | collective-permute-start | bytes 1277960 | tf_op jit(solution)/shard_map/ppermute | solution.py:38
  34.7 4.1 %collective-permute-start.9 = (bf16[512,128]{1,0:T(8,128)(2,1)S(1)}, bf16[512,128]{1,0:T(8,128)(2,1)S(1)}, u32[]{:S(2)}, u32[]{:S(2)}) collective-permute-start(bf16[512,128]{1,0:T(8,128)(2,1)S(1)} %get-tuple-element.46), channel_id=1, source_target_pairs={{1,2},{3,4},{5,6},{7,8},{9,10},{11,12},{13,14},{15,16},{17,18},{19... | collective-permute-start | bytes 393224 | tf_op jit(solution)/shard_map/ppermute | solution.py:565
  44.5 13.7 %collective-permute-start.10 = (bf16[13,64,128]{2,1,0:T(8,128)(2,1)S(1)}, bf16[13,64,128]{2,1,0:T(8,128)(2,1)S(1)}, u32[]{:S(2)}, u32[]{:S(2)}) collective-permute-start(bf16[13,64,128]{2,1,0:T(8,128)(2,1)S(1)} %get-tuple-element.48), channel_id=1, source_target_pairs={{0,4},{1,3},{2,6},{3,1},{4,0},{5,7},{6,2},{7,5},{8,12},{9,11},{10,... | collective-permute-start | bytes 638984 | tf_op jit(solution)/shard_map/ppermute | solution.py:38
  52.2 6.1 %collective-permute-start.13 = (bf16[13,64,128]{2,1,0:T(8,128)(2,1)S(1)}, bf16[13,64,128]{2,1,0:T(8,128)(2,1)S(1)}, u32[]{:S(2)}, u32[]{:S(2)}) collective-permute-start(bf16[13,64,128]{2,1,0:T(8,128)(2,1)S(1)} %get-tuple-element.55), channel_id=1, source_target_pairs={{0,4},{1,3},{2,6},{3,1},{4,0},{5,7},{6,2},{7,5},{8,12},{9,11},{10,... | collective-permute-start | bytes 638984 | tf_op jit(solution)/shard_map/ppermute | solution.py:38
  59.4 1.8 %collective-permute-start.14 = (f32[13,64,128]{2,1,0:T(8,128)S(1)}, f32[13,64,128]{2,1,0:T(8,128)S(1)}, u32[]{:S(2)}, u32[]{:S(2)}) collective-permute-start(f32[13,64,128]{2,1,0:T(8,128)S(1)} %far_1_2.1), channel_id=1, source_target_pairs={{0,1},{1,0},{2,3},{3,2},{4,5},{5,4},{6,7},{7,6},{8,9},{9,8},{10,11... | collective-permute-start | bytes 1277960 | tf_op jit(solution)/shard_map/ppermute | solution.py:38

commit v7 on v6

--- a/solution.py
+++ b/solution.py
@@ -129,7 +129,7 @@
 
 
 def skeleton_kernel(per, layers, me_ref, order_ref, comp_ref, basis_ref, transfer_ref,
-                    owner_ref, leaf_ref, ordered_ref, shared_ref, first_ref, last_ref,
+                    owner_ref, leaf_ref, ordered_ref, shared_ref, cross_ref, inner_ref,
                     entry_ref, block_ref, root_ref):
     step = pl.program_id(0)
     leaf_len = basis_ref.shape[2]
@@ -153,13 +153,28 @@
         ordered_ref[i * leaf_len:(i + 1) * leaf_len, :] = ordered[i]
         shared_ref[pl.ds(step * per + i + 1, 1)] = skeletons[i][None]
 
-    @pl.when(step == 0)
+    even = me_ref[0] % 2 == 0
+
+    @pl.when((step == 0) & even)
     def _():
-        first_ref[...] = ordered[0]
-
-    @pl.when(step == pl.num_programs(0) - 1)
+        cross_ref[...] = ordered[0]
+
+    @pl.when((step == 0) & ~even)
     def _():
-        last_ref[...] = ordered[-1]
+        inner_ref[...] = ordered[0]
+
+    last = step == pl.num_programs(0) - 1
+
+    @pl.when(last & even)
+    def _():
+        inner_ref[...] = ordered[-1]
+
+    @pl.when(last & ~even)
+    def _():
+        cross_ref[...] = ordered[-1]
+
+    @pl.when(last)
+    def _():
         shared_ref[pl.ds(0, 1)] = root_ref[...].astype(BF)[None]
 
 
@@ -256,11 +271,11 @@
     )(me, *parts)
 
 
-def dense_kernel(per, slots, me_ref, entry_ref, block_ref, first_ref, last_ref, coupling_ref, top_ref,
-                 transfer_ref, own_ref, other_ref, cross_ref, turned_ref):
+def dense_kernel(per, slots, entry_ref, block_ref, inner_ref, coupling_ref, top_ref,
+                 transfer_ref, own_ref, other_ref, turned_ref):
     step = pl.program_id(0)
     rank = coupling_ref.shape[2]
-    fields = first_ref.shape[1]
+    fields = inner_ref.shape[1]
     leaves = own_ref.shape[0] - 1
     for i in range(per):
         turned_ref[step * per + i] = transfer_ref[i].T
@@ -285,18 +300,15 @@
 
     @pl.when(step == 0)
     def _():
-        even = me_ref[0] % 2 == 0
-        first, last = first_ref[...], last_ref[...]
-        cross_ref[...] = jnp.where(even, first, last)
-        inner = jnp.where(even, last, first)
-        for t in range(first.shape[0] // rank):
-            other_ref[leaves + 1, :, t * fields:(t + 1) * fields] = inner[t * rank:(t + 1) * rank]
+        for t in range(inner_ref.shape[0] // rank):
+            part = inner_ref[t * rank:(t + 1) * rank, :]
+            other_ref[leaves + 1, :, t * fields:(t + 1) * fields] = part
         other_ref[leaves + 2] = jnp.zeros(other_ref.shape[1:], BF)
         blocks = block_ref[...].astype(F32).astype(BF)
         other_ref[leaves + 2, :blocks.shape[0], :blocks.shape[1]] = blocks
 
 
-def dense_couplings(me, entry, block, first, last, coupling, top_coupling, transfer, slots, per=4):
+def dense_couplings(entry, block, inner, coupling, top_coupling, transfer, slots, per=4):
     leaves, entries, rank, _ = coupling.shape
     own = (leaves + 1, rank, slots * rank)
     other = (leaves + 3, rank, slots * rank)
@@ -306,10 +318,8 @@
         grid=(leaves // per,),
         in_specs=[
             scalars(),
-            scalars(),
             pl.BlockSpec(block.shape, lambda s: (0, 0)),
-            pl.BlockSpec(first.shape, lambda s: (0, 0)),
-            pl.BlockSpec(last.shape, lambda s: (0, 0)),
+            pl.BlockSpec(inner.shape, lambda s: (0, 0)),
             pl.BlockSpec((per, entries, rank, rank), lambda s: (s, 0, 0, 0)),
             pl.BlockSpec(top_coupling.shape, lambda s: (0, 0, 0, 0)),
             pl.BlockSpec((per, rank, rank), lambda s: (s, 0, 0)),
@@ -317,18 +327,16 @@
         out_specs=[
             pl.BlockSpec(own, lambda s: (0, 0, 0)),
             pl.BlockSpec(other, lambda s: (0, 0, 0)),
-            pl.BlockSpec(first.shape, lambda s: (0, 0)),
             pl.BlockSpec(transfer.shape, lambda s: (0, 0, 0)),
         ],
         out_shape=[
             jax.ShapeDtypeStruct(own, BF),
             jax.ShapeDtypeStruct(other, BF),
-            jax.ShapeDtypeStruct(first.shape, BF),
             jax.ShapeDtypeStruct(transfer.shape, BF),
         ],
         compiler_params=params(16 if slots <= 16 else 48),
         cost_estimate=cost(0, 8 * MIB),
-    )(me, entry, block, first, last, *in_hbm(coupling, top_coupling, transfer))
+    )(entry, block, inner, *in_hbm(coupling, top_coupling, transfer))
 
 
 def round_kernel(plane, steps, slots, counts, at_ref, *refs):
@@ -539,7 +547,7 @@
     cut = pairs // 2
     me = lax.axis_index("subtree").reshape(1)
 
-    ordered, shared, first, last, entry, own_at = skeletons_of(
+    ordered, shared, cross, inner, entry, own_at = skeletons_of(
         me, leaf_order, composition, leaf_basis, transfer, admissible_owner, admissible_leaf, layers
     )
     tables = jnp.asarray(near_tables(leaf_len))
@@ -547,29 +555,30 @@
 
     line = along_z(shared, 1)
     from_x, from_y = over_x(shared), over_y(shared)
-    lines = [along_z(shared, layers - 1)]
-    own_blocks, my_other, cross, turned_transfer = dense_couplings(
-        me, entry, own_at, first, last, coupling, top_coupling, transfer, slots
-    )
-    line = after(line, from_x, from_y, lines[0], my_other)
+    filled = near_field(list(range(1, cut)), *near_args, ordered)
+    line = after(line, from_x, from_y, filled[0])
     next_x, next_y = over_x(line), over_y(line)
+    lines = [along_z(after(shared, line), layers - 1)]
     for _ in range(layers - 3):
         lines.append(along_z(line if len(lines) == 1 else lines[-1], 1))
-    filled = near_field(list(range(1, cut)), *near_args, after(ordered, line))
-
-    joined = join([after(lines[0], next_x, next_y, filled[0])] + lines[1:])
-    last_x, last_y = over_x(joined), over_y(joined)
-    round_0 = ((shared, line), (from_x, next_x), (from_y, next_y))
-    round_0 += (tuple(map(onward, choose(me, *round_0[1:], 1))),)
-    other_blocks = over_core(after(my_other, joined))
     cross = lax.ppermute(
         cross,
         "subtree",
         [(d, d + 1) for d in range(1, count - 1, 2)] + [(d, d - 1) for d in range(2, count, 2)],
     )
+    own_blocks, my_other, turned_transfer = dense_couplings(
+        after(entry, line), own_at, inner, coupling, top_coupling, transfer, slots
+    )
+
+    joined = join([after(lines[0], next_x, next_y, cross, my_other)] + lines[1:])
+    last_x, last_y = over_x(joined), over_y(joined)
+    round_0 = ((shared, line), (from_x, next_x), (from_y, next_y))
+    chosen = choose(me, (after(from_x, joined), next_x), round_0[2], 1)
+    round_0 += (tuple(map(onward, chosen)),)
+    other_blocks = over_core(after(my_other, *chosen))
     held = after(ordered, joined)
     filled = near_field(list(range(cut, pairs - 1)), *near_args, held, filled=filled)
-    far = tuple(map(onward, choose(me, (after(last_x, filled[0], cross),), (last_y,), 2)))
+    far = tuple(map(onward, choose(me, (after(last_x, filled[0]),), (last_y,), 2)))
     *filled, other_at = near_field(
         [0, pairs - 1], *near_args, after(ordered, filled[0]), halos=(me, cross, other_blocks), filled=filled
     )

time: 64.2 us -> 58.8 us (0.916)
  starting transfers between devices: 23 us -> 16.2 us
  waiting for transfers between devices: 14.1 us -> 15.6 us
    ppermute x14, starting transfers between devices: 22.4 us -> 15.5 us  [send(): lax.ppermute(block, 'subtree', [(d, target(d)) for d in range(count)])]
    ppermute x14, waiting for transfers between devices: 14.1 us -> 15.6 us  [send(): lax.ppermute(block, 'subtree', [(d, target(d)) for d in range(count)])]
  transfers between devices with their start and end apart: 15 -> 15, of which waited for: 8 -> 8; matrix products, arithmetic and copies ran while one was open for 0% -> 0% of each run, Pallas kernels for 28% -> 31%
where the time goes in v7:
time: 58.8 us; the launch traced here: 58.6 us
  Pallas kernels  26.6 us (45%)
  starting transfers between devices  16.2 us (28%)
  waiting for transfers between devices  15.6 us (27%)
    ppermute x14, waiting for transfers between devices, send(): lax.ppermute(block, 'subtree', [(d, target(d)) for d in range(count)])  15.6 us
    ppermute x14, starting transfers between devices, send(): lax.ppermute(block, 'subtree', [(d, target(d)) for d in range(count)])  15.5 us
    pallas_call x3, Pallas kernels, near_field(): pl.pallas_call(functools.partial(near_kernel, halos is not None, pair_of,...  10.6 us
    pallas_call x1, Pallas kernels, skeletons_of(): pl.pallas_call(functools.partial(skeleton_kernel, per, layers), name='ord...  4.83 us
    pallas_call x4, Pallas kernels, far_round(): pl.pallas_call(functools.partial(round_kernel, plane, steps, slots, [len(...  4.32 us
    pallas_call x1, Pallas kernels, dense_couplings(): pl.pallas_call(functools.partial(dense_kernel, per, slots), name='couplin...  3.99 us
    pallas_call x1, Pallas kernels, field(): pl.pallas_call(functools.partial(field_kernel, per), name='local_and_fiel...  2.73 us
  transfers between devices with their start and end apart: 15, of which 8 were waited for; matrix products, arithmetic and copies ran while one was open for 0% of the time, Pallas kernels for 31%

profile of v7, /device:TPU:0, one launch (start us, length us, event | category | flops | bytes accessed | tf_op | source)
XLA Modules:
  0.0 58.6 jit_solution(6699503857387210918)
XLA Ops:
  0.0 4.8 %order_and_skeleton.1 = (bf16[6144,128]{1,0:T(8,128)(2,1)S(1)}, bf16[13,64,128]{2,1,0:T(8,128)(2,1)S(1)}, bf16[512,128]{1,0:T(8,128)(2,1)S(1)}, bf16[512,128]{1,...) custom-call(s32[1]{0:T(128)} %bitcast.me_ref.refs_0_, s32[12,512]{1,0:T(8,128)} %order_ref.7, ...), custom_call_target="tpu_custom_call" | custom-call | flops 12582912 | bytes 65536 | tf_op jit(solution)/shard_map/order_and_skeleton/pallas_call | solution.py:186
  4.8 3.0 %collective-permute-start.1 = (bf16[13,64,128]{2,1,0:T(8,128)(2,1)S(1)}, bf16[13,64,128]{2,1,0:T(8,128)(2,1)S(1)}, u32[]{:S(2)}, u32[]{:S(2)}) collective-permute-start(bf16[13,64,128]{2,1,0:T(8,128)(2,1)S(1)} %get-tuple-element.38.refs_0_), channel_id=1, source_target_pairs={{0,2},{1,3},{2,0},{3,1},{4,6},{5,7},{6,4},{7,5},{8,10},{9,11},{10,... | collective-permute-start | bytes 638984 | tf_op jit(solution)/shard_map/ppermute | solution.py:38
  7.9 1.5 %collective-permute-start.2 = (bf16[13,64,128]{2,1,0:T(8,128)(2,1)S(1)}, bf16[13,64,128]{2,1,0:T(8,128)(2,1)S(1)}, u32[]{:S(2)}, u32[]{:S(2)}) collective-permute-start(bf16[13,64,128]{2,1,0:T(8,128)(2,1)S(1)} %get-tuple-element.38.refs_0_), channel_id=1, source_target_pairs={{0,4},{1,5},{2,6},{3,7},{4,0},{5,1},{6,2},{7,3},{8,12},{9,13},{10,... | collective-permute-start | bytes 638984 | tf_op jit(solution)/shard_map/ppermute | solution.py:38
  9.4 1.6 %collective-permute-start = (bf16[13,64,128]{2,1,0:T(8,128)(2,1)S(1)}, bf16[13,64,128]{2,1,0:T(8,128)(2,1)S(1)}, u32[]{:S(2)}, u32[]{:S(2)}) collective-permute-start(bf16[13,64,128]{2,1,0:T(8,128)(2,1)S(1)} %get-tuple-element.38.refs_0_), channel_id=1, source_target_pairs={{0,8},{1,9},{2,10},{3,11},{4,12},{5,13},{6,14},{7,15},{8,16},{9,17... | collective-permute-start | bytes 638984 | tf_op jit(solution)/shard_map/ppermute | solution.py:38
  11.0 3.5 %near_1.1 = (bf16[6144,128]{1,0:T(8,128)(2,1)S(1)}, bf16[6144,64]{1,0:T(8,128)(2,1)S(1)}) custom-call(s32[2,12]{1,0:T(2,128)S(1)} %bitcast.2, s32[12,512]{1,0:T(8,128)S(1)} %copy-done.2, bf16[512,1536]{1,0:T(8,128)(2,1)S(1)} %copy-done, bf16[12,64,512]{2,1,0:T(8,128)(2,1)S(1)} %copy-done.1, ...), custom_call_target="tpu_custom_call" | custom-call | flops 20971520 | bytes 32768 | tf_op jit(solution)/shard_map/near_1/pallas_call | solution.py:467
  14.6 3.1 %collective-permute-done.refs_1_ = bf16[13,64,128]{2,1,0:T(8,128)(2,1)S(1)} collective-permute-done((bf16[13,64,128]{2,1,0:T(8,128)(2,1)S(1)}, bf16[13,64,128]{2,1,0:T(8,128)(2,1)S(1)}, u32[]{:S(2)}, u32[]{:S(2)}) %collective-permute-start) | collective-permute-done | bytes 213024 | tf_op jit(solution)/shard_map/ppermute | solution.py:38
  17.7 1.7 %collective-permute-start.3 = (bf16[13,64,128]{2,1,0:T(8,128)(2,1)S(1)}, bf16[13,64,128]{2,1,0:T(8,128)(2,1)S(1)}, u32[]{:S(2)}, u32[]{:S(2)}) collective-permute-start(bf16[13,64,128]{2,1,0:T(8,128)(2,1)S(1)} %get-tuple-element.38.refs_0_), channel_id=1, source_target_pairs={{0,24},{1,25},{2,26},{3,27},{4,28},{5,29},{6,30},{7,31},{8,0},{9,1... | collective-permute-start | bytes 638984 | tf_op jit(solution)/shard_map/ppermute | solution.py:38
  20.8 0.7 %collective-permute-start.6 = (bf16[512,128]{1,0:T(8,128)(2,1)S(1)}, bf16[512,128]{1,0:T(8,128)(2,1)S(1)}, u32[]{:S(2)}, u32[]{:S(2)}) collective-permute-start(bf16[512,128]{1,0:T(8,128)(2,1)S(1)} %get-tuple-element.39), channel_id=1, source_target_pairs={{1,2},{3,4},{5,6},{7,8},{9,10},{11,12},{13,14},{15,16},{17,18},{19... | collective-permute-start | bytes 393224 | tf_op jit(solution)/shard_map/ppermute | solution.py:564
  21.5 4.0 %couplings_by_owner.1 = (bf16[13,64,1024]{2,1,0:T(8,128)(2,1)S(1)}, bf16[15,64,1024]{2,1,0:T(8,128)(2,1)S(1)}, bf16[12,64,64]{2,1,0:T(8,128)(2,1)S(1)}) custom-call(s32[16,128]{1,0:T(8,128)S(1)} %get-tuple-element.41.entry_ref, s32[16,128]{1,0:T(8,128)S(1)} %get-tuple-element.33.block_ref.at_ref, bf16[512,128]{1,0:T(8,128)(2,1)S(1)} %get-tuple-element.42.inner_ref, ...), custom_call_target="tpu_custom_call" | custom-call | bytes 131072 | tf_op jit(solution)/shard_map/couplings_by_owner/pallas_call | solution.py:315
  25.8 2.6 %collective-permute-done.7.refs_1_ = bf16[13,64,128]{2,1,0:T(8,128)(2,1)S(1)} collective-permute-done((bf16[13,64,128]{2,1,0:T(8,128)(2,1)S(1)}, bf16[13,64,128]{2,1,0:T(8,128)(2,1)S(1)}, u32[]{:S(2)}, u32[]{:S(2)}) %collective-permute-start.7) | collective-permute-done | bytes 213024 | tf_op jit(solution)/shard_map/ppermute | solution.py:38
  28.6 1.4 %collective-permute-start.8 = (bf16[26,64,128]{2,1,0:T(8,128)(2,1)S(1)}, bf16[26,64,128]{2,1,0:T(8,128)(2,1)S(1)}, u32[]{:S(2)}, u32[]{:S(2)}) collective-permute-start(bf16[26,64,128]{2,1,0:T(8,128)(2,1)S(1)} %join.1.refs_0_), channel_id=1, source_target_pairs={{0,2},{1,3},{2,0},{3,1},{4,6},{5,7},{6,4},{7,5},{8,10},{9,11},{10,... | collective-permute-start | bytes 1277960 | tf_op jit(solution)/shard_map/ppermute | solution.py:38
  30.0 2.6 %collective-permute-start.9 = (bf16[26,64,128]{2,1,0:T(8,128)(2,1)S(1)}, bf16[26,64,128]{2,1,0:T(8,128)(2,1)S(1)}, u32[]{:S(2)}, u32[]{:S(2)}) collective-permute-start(bf16[26,64,128]{2,1,0:T(8,128)(2,1)S(1)} %join.1.refs_0_), channel_id=1, source_target_pairs={{0,4},{1,5},{2,6},{3,7},{4,0},{5,1},{6,2},{7,3},{8,12},{9,13},{10,... | collective-permute-start | bytes 1277960 | tf_op jit(solution)/shard_map/ppermute | solution.py:38
  32.7 3.4 %near_3.1 = (bf16[6144,128]{1,0:T(8,128)(2,1)S(1)}, bf16[6144,64]{1,0:T(8,128)(2,1)S(1)}) custom-call(s32[2,12]{1,0:T(2,128)S(1)} %bitcast.3, s32[12,512]{1,0:T(8,128)S(1)} %copy-done.2, bf16[512,1536]{1,0:T(8,128)(2,1)S(1)} %copy-done, bf16[12,64,512]{2,1,0:T(8,128)(2,1)S(1)} %copy-done.1, ...), custom_call_target="tpu_custom_call", output_to_operand_aliasing={{0}: (7, {}), {1}: (8, {})} | custom-call | flops 20971520 | bytes 32768 | tf_op jit(solution)/shard_map/near_3/pallas_call | solution.py:467
  36.1 5.1 %collective-permute-done.8.refs_0_.refs_1_ = bf16[26,64,128]{2,1,0:T(8,128)(2,1)S(1)} collective-permute-done((bf16[26,64,128]{2,1,0:T(8,128)(2,1)S(1)}, bf16[26,64,128]{2,1,0:T(8,128)(2,1)S(1)}, u32[]{:S(2)}, u32[]{:S(2)}) %collective-permute-start.8) | collective-permute-done | bytes 426016 | tf_op jit(solution)/shard_map/ppermute | solution.py:38
  41.3 1.2 %collective-permute-done.9.refs_1_.refs_2_ = bf16[26,64,128]{2,1,0:T(8,128)(2,1)S(1)} collective-permute-done((bf16[26,64,128]{2,1,0:T(8,128)(2,1)S(1)}, bf16[26,64,128]{2,1,0:T(8,128)(2,1)S(1)}, u32[]{:S(2)}, u32[]{:S(2)}) %collective-permute-start.9) | collective-permute-done | bytes 426016 | tf_op jit(solution)/shard_map/ppermute | solution.py:38
  42.5 1.8 %collective-permute-start.10 = (bf16[13,64,128]{2,1,0:T(8,128)(2,1)S(1)}, bf16[13,64,128]{2,1,0:T(8,128)(2,1)S(1)}, u32[]{:S(2)}, u32[]{:S(2)}) collective-permute-start(bf16[13,64,128]{2,1,0:T(8,128)(2,1)S(1)} %get-tuple-element.49), channel_id=1, source_target_pairs={{0,4},{1,3},{2,6},{3,1},{4,0},{5,7},{6,2},{7,5},{8,12},{9,11},{10,... | collective-permute-start | bytes 638984 | tf_op jit(solution)/shard_map/ppermute | solution.py:38
  44.6 2.4 %collective-permute-done.11.refs_6_ = bf16[26,64,128]{2,1,0:T(8,128)(2,1)S(1)} collective-permute-done((bf16[26,64,128]{2,1,0:T(8,128)(2,1)S(1)}, bf16[26,64,128]{2,1,0:T(8,128)(2,1)S(1)}, u32[]{:S(2)}, u32[]{:S(2)}) %collective-permute-start.11) | collective-permute-done | bytes 426016 | tf_op jit(solution)/shard_map/ppermute | solution.py:38
  47.0 1.1 %far_0_0.1.refs_6_ = f32[13,64,128]{2,1,0:T(8,128)S(1)} custom-call(s32[16,128]{1,0:T(8,128)S(1)} %get-tuple-element.33.block_ref.at_ref, bf16[13,64,128]{2,1,0:T(8,128)(2,1)S(1)} %get-tuple-element.38.refs_0_, bf16[13,64,128]{2,1,0:T(8,128)(2,1)S(1)} %collective-permute-done.refs_1_, bf16[13,64,128]{2,1,0:T(8,128)(2,1)S(1)} %collective-permute-done.1.refs_0_.refs_2_, ...), custom_call_target="tpu_custom_call" | custom-call | flops 1703936 | bytes 16384 | tf_op jit(solution)/shard_map/far_0_0/pallas_call | solution.py:373
  48.1 3.8 %near_0.1 = (bf16[6144,128]{1,0:T(8,128)(2,1)S(1)}, bf16[6144,64]{1,0:T(8,128)(2,1)S(1)}, s32[16,128]{1,0:T(8,128)S(1)}) custom-call(s32[2,12]{1,0:T(2,128)S(1)} %bitcast.4, s32[12,512]{1,0:T(8,128)S(1)} %copy-done.2, bf16[512,1536]{1,0:T(8,128)(2,1)S(1)} %copy-done, ...), custom_call_target="tpu_custom_call", output_to_operand_aliasing={{0}: (11, {}), {1}: (12, {})} | custom-call | flops 20971520 | bytes 32768 | tf_op jit(solution)/shard_map/near_0/pallas_call | solution.py:467
  51.8 1.1 %far_1_0.1.refs_6_ = f32[13,64,128]{2,1,0:T(8,128)S(1)} custom-call(s32[16,128]{1,0:T(8,128)S(1)} %get-tuple-element.55.at_ref, bf16[13,64,128]{2,1,0:T(8,128)(2,1)S(1)} %get-tuple-element.38.refs_0_, bf16[13,64,128]{2,1,0:T(8,128)(2,1)S(1)} %collective-permute-done.refs_1_, bf16[13,64,128]{2,1,0:T(8,128)(2,1)S(1)} %collective-permute-done.1.refs_0_.refs_2_, ...), custom_call_target="tpu_custom_call" | custom-call | flops 1703936 | bytes 16384 | tf_op jit(solution)/shard_map/far_1_0/pallas_call | solution.py:373
  52.9 1.1 %far_1_2.1 = f32[13,64,128]{2,1,0:T(8,128)S(1)} custom-call(s32[16,128]{1,0:T(8,128)S(1)} %get-tuple-element.55.at_ref, bf16[26,64,128]{2,1,0:T(8,128)(2,1)S(1)} %join.1.refs_0_, bf16[26,64,128]{2,1,0:T(8,128)(2,1)S(1)} %collective-permute-done.8.refs_0_.refs_1_, bf16[26,64,128]{2,1,0:T(8,128)(2,1)S(1)} %collective-permute-done.9.refs_1_.refs_2_, ...), custom_call_target="tpu_custom_call" | custom-call | flops 1703936 | bytes 16384 | tf_op jit(solution)/shard_map/far_1_2/pallas_call | solution.py:373
  54.1 1.1 %far_0_2.1.own_ref = f32[13,64,128]{2,1,0:T(8,128)S(1)} custom-call(s32[16,128]{1,0:T(8,128)S(1)} %get-tuple-element.33.block_ref.at_ref, bf16[26,64,128]{2,1,0:T(8,128)(2,1)S(1)} %join.1.refs_0_, bf16[26,64,128]{2,1,0:T(8,128)(2,1)S(1)} %collective-permute-done.8.refs_0_.refs_1_, bf16[26,64,128]{2,1,0:T(8,128)(2,1)S(1)} %collective-permute-done.9.refs_1_.refs_2_, ...), custom_call_target="tpu_custom_call" | custom-call | flops 1703936 | bytes 16384 | tf_op jit(solution)/shard_map/far_0_2/pallas_call | solution.py:373
  55.2 0.7 %collective-permute-done.14.other_ref = f32[13,64,128]{2,1,0:T(8,128)S(1)} collective-permute-done((f32[13,64,128]{2,1,0:T(8,128)S(1)}, f32[13,64,128]{2,1,0:T(8,128)S(1)}, u32[]{:S(2)}, u32[]{:S(2)}) %collective-permute-start.14) | collective-permute-done | bytes 426016 | tf_op jit(solution)/shard_map/ppermute | solution.py:38
  55.9 2.7 %local_and_field.1 = bf16[6144,128]{1,0:T(8,128)(2,1)} custom-call(f32[13,64,128]{2,1,0:T(8,128)S(1)} %far_0_2.1.own_ref, f32[13,64,128]{2,1,0:T(8,128)S(1)} %collective-permute-done.14.other_ref, bf16[12,64,64]{2,1,0:T(8,128)(2,1)S(1)} %get-tuple-element.58.turned_transfer_ref, bf16[6144,128]{1,0:T(8,128)(2,1)S(1)} %get-tuple-element.59.near_ref, ...), custom_call_target="tpu_custom_call" | custom-call | flops 1572864 | bytes 65536 | tf_op jit(solution)/shard_map/local_and_field/pallas_call | solution.py:509
  (27 shorter events, 2.5 us)
Async XLA Ops:
  0.0 11.0 %copy-start = (bf16[512,1536]{1,0:T(8,128)(2,1)S(1)}, bf16[512,1536]{1,0:T(8,128)(2,1)}, u32[]{:S(2)}) copy-start(bf16[512,1536]{1,0:T(8,128)(2,1)} %constant.6.clone.table_ref) | copy-start | bytes 4718596
  0.0 11.0 %copy-start.1 = (bf16[12,64,512]{2,1,0:T(8,128)(2,1)S(1)}, bf16[12,64,512]{2,1,0:T(8,128)(2,1)}, u32[]{:S(2)}) copy-start(bf16[12,64,512]{2,1,0:T(8,128)(2,1)} %basis_ref.7) | copy-start | bytes 2359300
  0.0 11.0 %copy-start.2 = (s32[12,512]{1,0:T(8,128)S(1)}, s32[12,512]{1,0:T(8,128)}, u32[]{:S(2)}) copy-start(s32[12,512]{1,0:T(8,128)} %order_ref.7) | copy-start | bytes 73732
  0.0 11.0 %copy-start.3 = (s32[12,2]{0,1:T(2,128)S(1)}, s32[12,2]{0,1:T(2,128)}, u32[]{:S(2)}) copy-start(s32[12,2]{0,1:T(2,128)} %param.17) | copy-start | bytes 292
  4.8 9.6 %collective-permute-start.1 = (bf16[13,64,128]{2,1,0:T(8,128)(2,1)S(1)}, bf16[13,64,128]{2,1,0:T(8,128)(2,1)S(1)}, u32[]{:S(2)}, u32[]{:S(2)}) collective-permute-start(bf16[13,64,128]{2,1,0:T(8,128)(2,1)S(1)} %get-tuple-element.38.refs_0_), channel_id=1, source_target_pairs={{0,2},{1,3},{2,0},{3,1},{4,6},{5,7},{6,4},{7,5},{8,10},{9,11},{10,... | collective-permute-start | bytes 638984 | tf_op jit(solution)/shard_map/ppermute | solution.py:38
  7.9 6.8 %collective-permute-start.2 = (bf16[13,64,128]{2,1,0:T(8,128)(2,1)S(1)}, bf16[13,64,128]{2,1,0:T(8,128)(2,1)S(1)}, u32[]{:S(2)}, u32[]{:S(2)}) collective-permute-start(bf16[13,64,128]{2,1,0:T(8,128)(2,1)S(1)} %get-tuple-element.38.refs_0_), channel_id=1, source_target_pairs={{0,4},{1,5},{2,6},{3,7},{4,0},{5,1},{6,2},{7,3},{8,12},{9,13},{10,... | collective-permute-start | bytes 638984 | tf_op jit(solution)/shard_map/ppermute | solution.py:38
  9.4 8.3 %collective-permute-start = (bf16[13,64,128]{2,1,0:T(8,128)(2,1)S(1)}, bf16[13,64,128]{2,1,0:T(8,128)(2,1)S(1)}, u32[]{:S(2)}, u32[]{:S(2)}) collective-permute-start(bf16[13,64,128]{2,1,0:T(8,128)(2,1)S(1)} %get-tuple-element.38.refs_0_), channel_id=1, source_target_pairs={{0,8},{1,9},{2,10},{3,11},{4,12},{5,13},{6,14},{7,15},{8,16},{9,17... | collective-permute-start | bytes 638984 | tf_op jit(solution)/shard_map/ppermute | solution.py:38
  17.7 7.8 %collective-permute-start.3 = (bf16[13,64,128]{2,1,0:T(8,128)(2,1)S(1)}, bf16[13,64,128]{2,1,0:T(8,128)(2,1)S(1)}, u32[]{:S(2)}, u32[]{:S(2)}) collective-permute-start(bf16[13,64,128]{2,1,0:T(8,128)(2,1)S(1)} %get-tuple-element.38.refs_0_), channel_id=1, source_target_pairs={{0,24},{1,25},{2,26},{3,27},{4,28},{5,29},{6,30},{7,31},{8,0},{9,1... | collective-permute-start | bytes 638984 | tf_op jit(solution)/shard_map/ppermute | solution.py:38
  19.5 6.0 %collective-permute-start.4 = (bf16[13,64,128]{2,1,0:T(8,128)(2,1)S(1)}, bf16[13,64,128]{2,1,0:T(8,128)(2,1)S(1)}, u32[]{:S(2)}, u32[]{:S(2)}) collective-permute-start(bf16[13,64,128]{2,1,0:T(8,128)(2,1)S(1)} %collective-permute-done.refs_1_), channel_id=1, source_target_pairs={{0,2},{1,3},{2,0},{3,1},{4,6},{5,7},{6,4},{7,5},{8,10},{9,11},{10,... | collective-permute-start | bytes 638984 | tf_op jit(solution)/shard_map/ppermute | solution.py:38
  20.0 5.8 %collective-permute-start.5 = (bf16[13,64,128]{2,1,0:T(8,128)(2,1)S(1)}, bf16[13,64,128]{2,1,0:T(8,128)(2,1)S(1)}, u32[]{:S(2)}, u32[]{:S(2)}) collective-permute-start(bf16[13,64,128]{2,1,0:T(8,128)(2,1)S(1)} %collective-permute-done.refs_1_), channel_id=1, source_target_pairs={{0,4},{1,5},{2,6},{3,7},{4,0},{5,1},{6,2},{7,3},{8,12},{9,13},{10,... | collective-permute-start | bytes 638984 | tf_op jit(solution)/shard_map/ppermute | solution.py:38
  20.5 7.9 %collective-permute-start.7 = (bf16[13,64,128]{2,1,0:T(8,128)(2,1)S(1)}, bf16[13,64,128]{2,1,0:T(8,128)(2,1)S(1)}, u32[]{:S(2)}, u32[]{:S(2)}) collective-permute-start(bf16[13,64,128]{2,1,0:T(8,128)(2,1)S(1)} %collective-permute-done.refs_1_), channel_id=1, source_target_pairs={{0,8},{1,9},{2,10},{3,11},{4,12},{5,13},{6,14},{7,15},{8,16},{9,17... | collective-permute-start | bytes 638984 | tf_op jit(solution)/shard_map/ppermute | solution.py:38
  20.8 4.7 %collective-permute-start.6 = (bf16[512,128]{1,0:T(8,128)(2,1)S(1)}, bf16[512,128]{1,0:T(8,128)(2,1)S(1)}, u32[]{:S(2)}, u32[]{:S(2)}) collective-permute-start(bf16[512,128]{1,0:T(8,128)(2,1)S(1)} %get-tuple-element.39), channel_id=1, source_target_pairs={{1,2},{3,4},{5,6},{7,8},{9,10},{11,12},{13,14},{15,16},{17,18},{19... | collective-permute-start | bytes 393224 | tf_op jit(solution)/shard_map/ppermute | solution.py:564
  28.5 19.6 %collective-permute-start.12 = (bf16[15,64,1024]{2,1,0:T(8,128)(2,1)S(1)}, bf16[15,64,1024]{2,1,0:T(8,128)(2,1)S(1)}, u32[]{:S(2)}, u32[]{:S(2)}) collective-permute-start(bf16[15,64,1024]{2,1,0:T(8,128)(2,1)S(1)} %get-tuple-element.53), channel_id=1, source_target_pairs={{0,1},{1,0},{2,3},{3,2},{4,5},{5,4},{6,7},{7,6},{8,9},{9,8},{10,11... | collective-permute-start | bytes 5898248 | tf_op jit(solution)/shard_map/ppermute | solution.py:38
  28.6 12.7 %collective-permute-start.8 = (bf16[26,64,128]{2,1,0:T(8,128)(2,1)S(1)}, bf16[26,64,128]{2,1,0:T(8,128)(2,1)S(1)}, u32[]{:S(2)}, u32[]{:S(2)}) collective-permute-start(bf16[26,64,128]{2,1,0:T(8,128)(2,1)S(1)} %join.1.refs_0_), channel_id=1, source_target_pairs={{0,2},{1,3},{2,0},{3,1},{4,6},{5,7},{6,4},{7,5},{8,10},{9,11},{10,... | collective-permute-start | bytes 1277960 | tf_op jit(solution)/shard_map/ppermute | solution.py:38
  30.0 12.4 %collective-permute-start.9 = (bf16[26,64,128]{2,1,0:T(8,128)(2,1)S(1)}, bf16[26,64,128]{2,1,0:T(8,128)(2,1)S(1)}, u32[]{:S(2)}, u32[]{:S(2)}) collective-permute-start(bf16[26,64,128]{2,1,0:T(8,128)(2,1)S(1)} %join.1.refs_0_), channel_id=1, source_target_pairs={{0,4},{1,5},{2,6},{3,7},{4,0},{5,1},{6,2},{7,3},{8,12},{9,13},{10,... | collective-permute-start | bytes 1277960 | tf_op jit(solution)/shard_map/ppermute | solution.py:38
  32.6 14.3 %collective-permute-start.11 = (bf16[26,64,128]{2,1,0:T(8,128)(2,1)S(1)}, bf16[26,64,128]{2,1,0:T(8,128)(2,1)S(1)}, u32[]{:S(2)}, u32[]{:S(2)}) collective-permute-start(bf16[26,64,128]{2,1,0:T(8,128)(2,1)S(1)} %choose.3), channel_id=1, source_target_pairs={{0,4},{1,3},{2,6},{3,1},{4,0},{5,7},{6,2},{7,5},{8,12},{9,11},{10,... | collective-permute-start | bytes 1277960 | tf_op jit(solution)/shard_map/ppermute | solution.py:38
  42.5 10.4 %collective-permute-start.10 = (bf16[13,64,128]{2,1,0:T(8,128)(2,1)S(1)}, bf16[13,64,128]{2,1,0:T(8,128)(2,1)S(1)}, u32[]{:S(2)}, u32[]{:S(2)}) collective-permute-start(bf16[13,64,128]{2,1,0:T(8,128)(2,1)S(1)} %get-tuple-element.49), channel_id=1, source_target_pairs={{0,4},{1,3},{2,6},{3,1},{4,0},{5,7},{6,2},{7,5},{8,12},{9,11},{10,... | collective-permute-start | bytes 638984 | tf_op jit(solution)/shard_map/ppermute | solution.py:38
  44.3 8.6 %collective-permute-start.13 = (bf16[13,64,128]{2,1,0:T(8,128)(2,1)S(1)}, bf16[13,64,128]{2,1,0:T(8,128)(2,1)S(1)}, u32[]{:S(2)}, u32[]{:S(2)}) collective-permute-start(bf16[13,64,128]{2,1,0:T(8,128)(2,1)S(1)} %get-tuple-element.57), channel_id=1, source_target_pairs={{0,4},{1,3},{2,6},{3,1},{4,0},{5,7},{6,2},{7,5},{8,12},{9,11},{10,... | collective-permute-start | bytes 638984 | tf_op jit(solution)/shard_map/ppermute | solution.py:38
  54.0 1.8 %collective-permute-start.14 = (f32[13,64,128]{2,1,0:T(8,128)S(1)}, f32[13,64,128]{2,1,0:T(8,128)S(1)}, u32[]{:S(2)}, u32[]{:S(2)}) collective-permute-start(f32[13,64,128]{2,1,0:T(8,128)S(1)} %far_1_2.1), channel_id=1, source_target_pairs={{0,1},{1,0},{2,3},{3,2},{4,5},{5,4},{6,7},{7,6},{8,9},{9,8},{10,11... | collective-permute-start | bytes 1277960 | tf_op jit(solution)/shard_map/ppermute | solution.py:38

commit v8 on v7

--- a/solution.py
+++ b/solution.py
@@ -382,7 +382,7 @@
 
 
 def near_kernel(edges, pair_of, last_pair, mask_ref, order_ref, table_ref, basis_ref,
-                prev_ref, cur_ref, next_ref, *refs):
+                ordered_ref, *refs):
     if edges:
         me_ref, cross_ref, inner_ref, blocks_ref = refs[:4]
         near_ref, turned_ref, at_ref = refs[-3:]
@@ -390,8 +390,13 @@
         near_ref, turned_ref = refs[-2:]
     pair = pair_of(pl.program_id(0))
     leaf_len = basis_ref.shape[2]
-    low, high = cur_ref[:leaf_len, :], cur_ref[leaf_len:, :]
-    prev, following = prev_ref[...], next_ref[...]
+    leaves = basis_ref.shape[0]
+
+    def leaf_at(leaf):
+        return ordered_ref[pl.ds(pl.multiple_of(leaf * leaf_len, leaf_len), leaf_len), :]
+
+    low, high = leaf_at(2 * pair), leaf_at(2 * pair + 1)
+    prev, following = leaf_at(jnp.maximum(2 * pair - 1, 0)), leaf_at(jnp.minimum(2 * pair + 2, leaves - 1))
     if edges:
         even = me_ref[0] % 2 == 0
         cross = cross_ref[...]
@@ -418,11 +423,11 @@
         [masked(2 * pair + 1, 0, low), high, masked(2 * pair + 1, 1, following)], axis=0
     )
     near = dot(table_ref[...], jnp.concatenate([left, right], axis=1)).astype(BF)
-    fields = cur_ref.shape[1]
+    fields = ordered_ref.shape[1]
     for i in range(2):
         hot = one_hot_grid(order_ref[pl.ds(2 * pair + i, 1), :], leaf_len)
         at = pl.ds(i * leaf_len, leaf_len)
-        both = jnp.concatenate([near[:, i * fields:(i + 1) * fields], basis_ref[i].T], axis=1)
+        both = jnp.concatenate([near[:, i * fields:(i + 1) * fields], basis_ref[2 * pair + i].T], axis=1)
         moved = dot(hot, both).astype(BF)
         near_ref[at, :] = moved[:, :fields]
         turned_ref[at, :] = moved[:, fields:]
@@ -439,14 +444,12 @@
 
     in_specs = [
         scalars(),
-        pl.BlockSpec((leaves, leaf_len), lambda s: (0, 0)),
-        pl.BlockSpec(tables.shape, lambda s: (0, 0)),
-        pl.BlockSpec((2, rank, leaf_len), lambda s: (pair_of(s), 0, 0)),
-        pl.BlockSpec((leaf_len, fields), lambda s: (jnp.maximum(2 * pair_of(s) - 1, 0), 0)),
-        pl.BlockSpec((2 * leaf_len, fields), lambda s: (pair_of(s), 0)),
-        pl.BlockSpec((leaf_len, fields), lambda s: (jnp.minimum(2 * pair_of(s) + 2, leaves - 1), 0)),
+        whole(),
+        whole(),
+        whole(),
+        whole(),
     ]
-    args = [near_list.T, leaf_order, tables, basis, ordered, ordered, ordered]
+    args = [near_list.T, leaf_order, tables, basis, ordered]
     aliases = {}
     extra = []
     if halos is not None:
@@ -485,7 +488,7 @@
 
 def field_kernel(per, own_ref, other_ref, turned_transfer_ref, near_ref, turned_ref, out_ref):
     step = pl.program_id(0)
-    leaf_len = near_ref.shape[0] // per
+    leaf_len = out_ref.shape[0] // per
     root = own_ref.shape[0] - 1
     local = own_ref[root] + other_ref[root]
     coarse = local.astype(BF)
@@ -494,29 +497,22 @@
     fields = local.shape[1]
     for i in range(per):
         leaf = step * per + i
-        down = dot(turned_transfer_ref[i], both)
+        down = dot(turned_transfer_ref[leaf], both)
         value = own_ref[leaf] + other_ref[leaf] + (down[:, :fields] + down[:, fields:])
-        at = pl.ds(i * leaf_len, leaf_len)
+        at = pl.ds(pl.multiple_of(leaf * leaf_len, leaf_len), leaf_len)
         far = dot(turned_ref[at, :], value.astype(BF))
-        out_ref[at, :] = (near_ref[at, :].astype(F32) + far).astype(BF)
+        out_ref[i * leaf_len:(i + 1) * leaf_len, :] = (near_ref[at, :].astype(F32) + far).astype(BF)
 
 
 def field(own, other, turned_transfer, near, turned, per=4):
     leaves, rank, _ = turned_transfer.shape
     fields = near.shape[1]
     leaf_len = near.shape[0] // leaves
-    total = pl.BlockSpec(own.shape, lambda s: (0, 0, 0))
     return pl.pallas_call(
         functools.partial(field_kernel, per),
         name="local_and_field",
         grid=(leaves // per,),
-        in_specs=[
-            total,
-            total,
-            pl.BlockSpec((per, rank, rank), lambda s: (s, 0, 0)),
-            pl.BlockSpec((per * leaf_len, fields), lambda s: (s, 0)),
-            pl.BlockSpec((per * leaf_len, rank), lambda s: (s, 0)),
-        ],
+        in_specs=[whole()] * 5,
         out_specs=pl.BlockSpec((per * leaf_len, fields), lambda s: (s, 0)),
         out_shape=jax.ShapeDtypeStruct(near.shape, BF),
         compiler_params=params(16),
@@ -556,32 +552,33 @@
     line = along_z(shared, 1)
     from_x, from_y = over_x(shared), over_y(shared)
     filled = near_field(list(range(1, cut)), *near_args, ordered)
-    line = after(line, from_x, from_y, filled[0])
-    next_x, next_y = over_x(line), over_y(line)
-    lines = [along_z(after(shared, line), layers - 1)]
+    line = after(line, filled[0])
+    lines = [along_z(after(shared, filled[0]), layers - 1)]
     for _ in range(layers - 3):
         lines.append(along_z(line if len(lines) == 1 else lines[-1], 1))
+    ready = after(line, from_x, from_y)
+    next_x, next_y = over_x(ready), over_y(ready)
     cross = lax.ppermute(
         cross,
         "subtree",
         [(d, d + 1) for d in range(1, count - 1, 2)] + [(d, d - 1) for d in range(2, count, 2)],
     )
     own_blocks, my_other, turned_transfer = dense_couplings(
-        after(entry, line), own_at, inner, coupling, top_coupling, transfer, slots
-    )
-
-    joined = join([after(lines[0], next_x, next_y, cross, my_other)] + lines[1:])
+        after(entry, ready), own_at, inner, coupling, top_coupling, transfer, slots
+    )
+    round_0 = ((shared, line), (from_x, next_x), (from_y, next_y))
+    chosen = choose(me, (after(from_x, cross, my_other), next_x), round_0[2], 1)
+    round_0 += (tuple(map(onward, chosen)),)
+
+    joined = join([after(lines[0], *chosen)] + lines[1:])
     last_x, last_y = over_x(joined), over_y(joined)
-    round_0 = ((shared, line), (from_x, next_x), (from_y, next_y))
-    chosen = choose(me, (after(from_x, joined), next_x), round_0[2], 1)
-    round_0 += (tuple(map(onward, chosen)),)
     other_blocks = over_core(after(my_other, *chosen))
-    held = after(ordered, joined)
+    held = after(ordered, joined, *round_0[3])
     filled = near_field(list(range(cut, pairs - 1)), *near_args, held, filled=filled)
-    far = tuple(map(onward, choose(me, (after(last_x, filled[0]),), (last_y,), 2)))
     *filled, other_at = near_field(
         [0, pairs - 1], *near_args, after(ordered, filled[0]), halos=(me, cross, other_blocks), filled=filled
     )
+    far = tuple(map(onward, choose(me, (after(last_x, filled[0]),), (last_y,), 2)))
     steps = [0, 1]
     own = far_round(0, steps, slots, own_at, round_0, own_blocks)
     other = far_round(1, steps, slots, other_at, round_0, other_blocks)

time: 58.8 us -> 66.1 us (1.12)
  waiting for transfers between devices: 15.6 us -> 20.2 us
  starting transfers between devices: 16.2 us -> 18.8 us
    ppermute x14, waiting for transfers between devices: 15.6 us -> 20.2 us  [send(): lax.ppermute(block, 'subtree', [(d, target(d)) for d in range(count)])]
    ppermute x14, starting transfers between devices: 15.5 us -> 18.2 us  [send(): lax.ppermute(block, 'subtree', [(d, target(d)) for d in range(count)])]
  transfers between devices with their start and end apart: 15 -> 15, of which waited for: 8 -> 9; matrix products, arithmetic and copies ran while one was open for 0% -> 0% of each run, Pallas kernels for 31% -> 27%
where the time goes in v8:
time: 66.1 us; the launch traced here: 65.9 us
  Pallas kernels  26.7 us (40%)
  waiting for transfers between devices  20.2 us (31%)
  starting transfers between devices  18.8 us (28%)
    ppermute x14, waiting for transfers between devices, send(): lax.ppermute(block, 'subtree', [(d, target(d)) for d in range(count)])  20.2 us
    ppermute x14, starting transfers between devices, send(): lax.ppermute(block, 'subtree', [(d, target(d)) for d in range(count)])  18.2 us
    pallas_call x3, Pallas kernels, near_field(): pl.pallas_call(functools.partial(near_kernel, halos is not None, pair_of,...  10.7 us
    pallas_call x1, Pallas kernels, skeletons_of(): pl.pallas_call(functools.partial(skeleton_kernel, per, layers), name='ord...  4.83 us
    pallas_call x4, Pallas kernels, far_round(): pl.pallas_call(functools.partial(round_kernel, plane, steps, slots, [len(...  4.32 us
    pallas_call x1, Pallas kernels, dense_couplings(): pl.pallas_call(functools.partial(dense_kernel, per, slots), name='couplin...  3.99 us
    pallas_call x1, Pallas kernels, field(): pl.pallas_call(functools.partial(field_kernel, per), name='local_and_fiel...  2.73 us
  transfers between devices with their start and end apart: 15, of which 9 were waited for; matrix products, arithmetic and copies ran while one was open for 0% of the time, Pallas kernels for 27%

profile of v8, /device:TPU:0, one launch (start us, length us, event | category | flops | bytes accessed | tf_op | source)
XLA Modules:
  0.0 65.9 jit_solution(10180332418892123040)
XLA Ops:
  0.0 4.8 %order_and_skeleton.1 = (bf16[6144,128]{1,0:T(8,128)(2,1)S(1)}, bf16[13,64,128]{2,1,0:T(8,128)(2,1)S(1)}, bf16[512,128]{1,0:T(8,128)(2,1)S(1)}, bf16[512,128]{1,...) custom-call(s32[1]{0:T(128)} %bitcast.me_ref.refs_0_, s32[12,512]{1,0:T(8,128)} %order_ref.7, ...), custom_call_target="tpu_custom_call" | custom-call | flops 12582912 | bytes 65536 | tf_op jit(solution)/shard_map/order_and_skeleton/pallas_call | solution.py:186
  4.8 3.1 %collective-permute-start.3 = (bf16[13,64,128]{2,1,0:T(8,128)(2,1)S(1)}, bf16[13,64,128]{2,1,0:T(8,128)(2,1)S(1)}, u32[]{:S(2)}, u32[]{:S(2)}) collective-permute-start(bf16[13,64,128]{2,1,0:T(8,128)(2,1)S(1)} %get-tuple-element.38.refs_0_), channel_id=1, source_target_pairs={{0,8},{1,9},{2,10},{3,11},{4,12},{5,13},{6,14},{7,15},{8,16},{9,17... | collective-permute-start | bytes 638984 | tf_op jit(solution)/shard_map/ppermute | solution.py:38
  7.9 1.5 %collective-permute-start.1 = (bf16[13,64,128]{2,1,0:T(8,128)(2,1)S(1)}, bf16[13,64,128]{2,1,0:T(8,128)(2,1)S(1)}, u32[]{:S(2)}, u32[]{:S(2)}) collective-permute-start(bf16[13,64,128]{2,1,0:T(8,128)(2,1)S(1)} %get-tuple-element.38.refs_0_), channel_id=1, source_target_pairs={{0,2},{1,3},{2,0},{3,1},{4,6},{5,7},{6,4},{7,5},{8,10},{9,11},{10,... | collective-permute-start | bytes 638984 | tf_op jit(solution)/shard_map/ppermute | solution.py:38
  9.4 1.5 %collective-permute-start.4 = (bf16[13,64,128]{2,1,0:T(8,128)(2,1)S(1)}, bf16[13,64,128]{2,1,0:T(8,128)(2,1)S(1)}, u32[]{:S(2)}, u32[]{:S(2)}) collective-permute-start(bf16[13,64,128]{2,1,0:T(8,128)(2,1)S(1)} %get-tuple-element.38.refs_0_), channel_id=1, source_target_pairs={{0,4},{1,5},{2,6},{3,7},{4,0},{5,1},{6,2},{7,3},{8,12},{9,13},{10,... | collective-permute-start | bytes 638984 | tf_op jit(solution)/shard_map/ppermute | solution.py:38
  11.0 3.5 %near_1.1 = (bf16[6144,128]{1,0:T(8,128)(2,1)S(1)}, bf16[6144,64]{1,0:T(8,128)(2,1)S(1)}) custom-call(s32[2,12]{1,0:T(2,128)S(1)} %bitcast.2, s32[12,512]{1,0:T(8,128)S(1)} %copy-done.2, bf16[512,1536]{1,0:T(8,128)(2,1)S(1)} %copy-done, bf16[12,64,512]{2,1,0:T(8,128)(2,1)S(1)} %copy-done.1, bf16[6144,128]{1,0:T(8,128)(2,1)S(1)} %get-tuple-element.51.ordered_ref), custom_call_target="tpu_custom_call" | custom-call | flops 20971520 | bytes 32768 | tf_op jit(solution)/shard_map/near_1/pallas_call | solution.py:470
  16.8 1.5 %collective-permute-start.6 = (bf16[13,64,128]{2,1,0:T(8,128)(2,1)S(1)}, bf16[13,64,128]{2,1,0:T(8,128)(2,1)S(1)}, u32[]{:S(2)}, u32[]{:S(2)}) collective-permute-start(bf16[13,64,128]{2,1,0:T(8,128)(2,1)S(1)} %collective-permute-done.3.refs_1_), channel_id=1, source_target_pairs={{0,4},{1,5},{2,6},{3,7},{4,0},{5,1},{6,2},{7,3},{8,12},{9,13},{10,... | collective-permute-start | bytes 638984 | tf_op jit(solution)/shard_map/ppermute | solution.py:38
  18.9 4.0 %couplings_by_owner.1 = (bf16[13,64,1024]{2,1,0:T(8,128)(2,1)S(1)}, bf16[15,64,1024]{2,1,0:T(8,128)(2,1)S(1)}, bf16[12,64,64]{2,1,0:T(8,128)(2,1)S(1)}) custom-call(s32[16,128]{1,0:T(8,128)S(1)} %get-tuple-element.43.entry_ref, s32[16,128]{1,0:T(8,128)S(1)} %get-tuple-element.34.block_ref.at_ref, bf16[512,128]{1,0:T(8,128)(2,1)S(1)} %get-tuple-element.44.inner_ref, ...), custom_call_target="tpu_custom_call" | custom-call | bytes 131072 | tf_op jit(solution)/shard_map/couplings_by_owner/pallas_call | solution.py:315
  23.0 2.6 %collective-permute-start.11 = (bf16[15,64,1024]{2,1,0:T(8,128)(2,1)S(1)}, bf16[15,64,1024]{2,1,0:T(8,128)(2,1)S(1)}, u32[]{:S(2)}, u32[]{:S(2)}) collective-permute-start(bf16[15,64,1024]{2,1,0:T(8,128)(2,1)S(1)} %get-tuple-element.52), channel_id=1, source_target_pairs={{0,1},{1,0},{2,3},{3,2},{4,5},{5,4},{6,7},{7,6},{8,9},{9,8},{10,11... | collective-permute-start | bytes 5898248 | tf_op jit(solution)/shard_map/ppermute | solution.py:38
  25.6 3.0 %collective-permute-start = (bf16[13,64,128]{2,1,0:T(8,128)(2,1)S(1)}, bf16[13,64,128]{2,1,0:T(8,128)(2,1)S(1)}, u32[]{:S(2)}, u32[]{:S(2)}) collective-permute-start(bf16[13,64,128]{2,1,0:T(8,128)(2,1)S(1)} %get-tuple-element.38.refs_0_), channel_id=1, source_target_pairs={{0,24},{1,25},{2,26},{3,27},{4,28},{5,29},{6,30},{7,31},{8,0},{9,1... | collective-permute-start | bytes 638984 | tf_op jit(solution)/shard_map/ppermute | solution.py:38
  28.6 0.9 %collective-permute-start.10 = (bf16[26,64,128]{2,1,0:T(8,128)(2,1)S(1)}, bf16[26,64,128]{2,1,0:T(8,128)(2,1)S(1)}, u32[]{:S(2)}, u32[]{:S(2)}) collective-permute-start(bf16[26,64,128]{2,1,0:T(8,128)(2,1)S(1)} %choose.2), channel_id=1, source_target_pairs={{0,4},{1,3},{2,6},{3,1},{4,0},{5,7},{6,2},{7,5},{8,12},{9,11},{10,... | collective-permute-start | bytes 1277960 | tf_op jit(solution)/shard_map/ppermute | solution.py:38
  29.5 4.7 %collective-permute-done.refs_0_ = bf16[13,64,128]{2,1,0:T(8,128)(2,1)S(1)} collective-permute-done((bf16[13,64,128]{2,1,0:T(8,128)(2,1)S(1)}, bf16[13,64,128]{2,1,0:T(8,128)(2,1)S(1)}, u32[]{:S(2)}, u32[]{:S(2)}) %collective-permute-start) | collective-permute-done | bytes 213024 | tf_op jit(solution)/shard_map/ppermute | solution.py:38
  34.2 6.2 %collective-permute-done.7.refs_1_ = bf16[13,64,128]{2,1,0:T(8,128)(2,1)S(1)} collective-permute-done((bf16[13,64,128]{2,1,0:T(8,128)(2,1)S(1)}, bf16[13,64,128]{2,1,0:T(8,128)(2,1)S(1)}, u32[]{:S(2)}, u32[]{:S(2)}) %collective-permute-start.7) | collective-permute-done | bytes 213024 | tf_op jit(solution)/shard_map/ppermute | solution.py:38
  41.5 3.4 %near_3.1 = (bf16[6144,128]{1,0:T(8,128)(2,1)S(1)}, bf16[6144,64]{1,0:T(8,128)(2,1)S(1)}) custom-call(s32[2,12]{1,0:T(2,128)S(1)} %bitcast.3, s32[12,512]{1,0:T(8,128)S(1)} %copy-done.2, bf16[512,1536]{1,0:T(8,128)(2,1)S(1)} %copy-done, bf16[12,64,512]{2,1,0:T(8,128)(2,1)S(1)} %copy-done.1, ...), custom_call_target="tpu_custom_call", output_to_operand_aliasing={{0}: (5, {}), {1}: (6, {})} | custom-call | flops 20971520 | bytes 32768 | tf_op jit(solution)/shard_map/near_3/pallas_call | solution.py:470
  45.0 3.8 %near_0.1 = (bf16[6144,128]{1,0:T(8,128)(2,1)S(1)}, bf16[6144,64]{1,0:T(8,128)(2,1)S(1)}, s32[16,128]{1,0:T(8,128)S(1)}) custom-call(s32[2,12]{1,0:T(2,128)S(1)} %bitcast.4, s32[12,512]{1,0:T(8,128)S(1)} %copy-done.2, bf16[512,1536]{1,0:T(8,128)(2,1)S(1)} %copy-done, ...), custom_call_target="tpu_custom_call", output_to_operand_aliasing={{0}: (9, {}), {1}: (10, {})} | custom-call | flops 20971520 | bytes 32768 | tf_op jit(solution)/shard_map/near_0/pallas_call | solution.py:470
  48.7 3.2 %collective-permute-done.8.refs_0_.refs_1_ = bf16[26,64,128]{2,1,0:T(8,128)(2,1)S(1)} collective-permute-done((bf16[26,64,128]{2,1,0:T(8,128)(2,1)S(1)}, bf16[26,64,128]{2,1,0:T(8,128)(2,1)S(1)}, u32[]{:S(2)}, u32[]{:S(2)}) %collective-permute-start.8) | collective-permute-done | bytes 426016 | tf_op jit(solution)/shard_map/ppermute | solution.py:38
  52.0 1.0 %collective-permute-start.12 = (bf16[13,64,128]{2,1,0:T(8,128)(2,1)S(1)}, bf16[13,64,128]{2,1,0:T(8,128)(2,1)S(1)}, u32[]{:S(2)}, u32[]{:S(2)}) collective-permute-start(bf16[13,64,128]{2,1,0:T(8,128)(2,1)S(1)} %get-tuple-element.56), channel_id=1, source_target_pairs={{0,4},{1,3},{2,6},{3,1},{4,0},{5,7},{6,2},{7,5},{8,12},{9,11},{10,... | collective-permute-start | bytes 638984 | tf_op jit(solution)/shard_map/ppermute | solution.py:38
  53.0 1.1 %collective-permute-start.13 = (bf16[13,64,128]{2,1,0:T(8,128)(2,1)S(1)}, bf16[13,64,128]{2,1,0:T(8,128)(2,1)S(1)}, u32[]{:S(2)}, u32[]{:S(2)}) collective-permute-start(bf16[13,64,128]{2,1,0:T(8,128)(2,1)S(1)} %get-tuple-element.60), channel_id=1, source_target_pairs={{0,4},{1,3},{2,6},{3,1},{4,0},{5,7},{6,2},{7,5},{8,12},{9,11},{10,... | collective-permute-start | bytes 638984 | tf_op jit(solution)/shard_map/ppermute | solution.py:38
  54.1 1.1 %far_0_0.1.refs_6_ = f32[13,64,128]{2,1,0:T(8,128)S(1)} custom-call(s32[16,128]{1,0:T(8,128)S(1)} %get-tuple-element.34.block_ref.at_ref, bf16[13,64,128]{2,1,0:T(8,128)(2,1)S(1)} %get-tuple-element.38.refs_0_, bf16[13,64,128]{2,1,0:T(8,128)(2,1)S(1)} %collective-permute-done.3.refs_1_, bf16[13,64,128]{2,1,0:T(8,128)(2,1)S(1)} %collective-permute-done.1.refs_0_.refs_2_, ...), custom_call_target="tpu_custom_call" | custom-call | flops 1703936 | bytes 16384 | tf_op jit(solution)/shard_map/far_0_0/pallas_call | solution.py:373
  55.2 1.1 %far_1_0.1.refs_6_ = f32[13,64,128]{2,1,0:T(8,128)S(1)} custom-call(s32[16,128]{1,0:T(8,128)S(1)} %get-tuple-element.58.at_ref, bf16[13,64,128]{2,1,0:T(8,128)(2,1)S(1)} %get-tuple-element.38.refs_0_, bf16[13,64,128]{2,1,0:T(8,128)(2,1)S(1)} %collective-permute-done.3.refs_1_, bf16[13,64,128]{2,1,0:T(8,128)(2,1)S(1)} %collective-permute-done.1.refs_0_.refs_2_, ...), custom_call_target="tpu_custom_call" | custom-call | flops 1703936 | bytes 16384 | tf_op jit(solution)/shard_map/far_1_0/pallas_call | solution.py:373
  56.3 1.7 %collective-permute-done.12.refs_3_ = bf16[13,64,128]{2,1,0:T(8,128)(2,1)S(1)} collective-permute-done((bf16[13,64,128]{2,1,0:T(8,128)(2,1)S(1)}, bf16[13,64,128]{2,1,0:T(8,128)(2,1)S(1)}, u32[]{:S(2)}, u32[]{:S(2)}) %collective-permute-start.12) | collective-permute-done | bytes 213024 | tf_op jit(solution)/shard_map/ppermute | solution.py:38
  57.9 2.3 %collective-permute-done.13.refs_4_ = bf16[13,64,128]{2,1,0:T(8,128)(2,1)S(1)} collective-permute-done((bf16[13,64,128]{2,1,0:T(8,128)(2,1)S(1)}, bf16[13,64,128]{2,1,0:T(8,128)(2,1)S(1)}, u32[]{:S(2)}, u32[]{:S(2)}) %collective-permute-start.13) | collective-permute-done | bytes 213024 | tf_op jit(solution)/shard_map/ppermute | solution.py:38
  60.2 1.1 %far_1_2.1 = f32[13,64,128]{2,1,0:T(8,128)S(1)} custom-call(s32[16,128]{1,0:T(8,128)S(1)} %get-tuple-element.58.at_ref, bf16[26,64,128]{2,1,0:T(8,128)(2,1)S(1)} %join.1.refs_0_, bf16[26,64,128]{2,1,0:T(8,128)(2,1)S(1)} %collective-permute-done.8.refs_0_.refs_1_, bf16[26,64,128]{2,1,0:T(8,128)(2,1)S(1)} %collective-permute-done.9.refs_1_.refs_2_, ...), custom_call_target="tpu_custom_call" | custom-call | flops 1703936 | bytes 16384 | tf_op jit(solution)/shard_map/far_1_2/pallas_call | solution.py:373
  61.4 1.1 %far_0_2.1.own_ref = f32[13,64,128]{2,1,0:T(8,128)S(1)} custom-call(s32[16,128]{1,0:T(8,128)S(1)} %get-tuple-element.34.block_ref.at_ref, bf16[26,64,128]{2,1,0:T(8,128)(2,1)S(1)} %join.1.refs_0_, bf16[26,64,128]{2,1,0:T(8,128)(2,1)S(1)} %collective-permute-done.8.refs_0_.refs_1_, bf16[26,64,128]{2,1,0:T(8,128)(2,1)S(1)} %collective-permute-done.9.refs_1_.refs_2_, ...), custom_call_target="tpu_custom_call" | custom-call | flops 1703936 | bytes 16384 | tf_op jit(solution)/shard_map/far_0_2/pallas_call | solution.py:373
  63.1 2.7 %local_and_field.1 = bf16[6144,128]{1,0:T(8,128)(2,1)} custom-call(f32[13,64,128]{2,1,0:T(8,128)S(1)} %far_0_2.1.own_ref, f32[13,64,128]{2,1,0:T(8,128)S(1)} %collective-permute-done.14.other_ref, bf16[12,64,64]{2,1,0:T(8,128)(2,1)S(1)} %get-tuple-element.61.turned_transfer_ref, bf16[6144,128]{1,0:T(8,128)(2,1)S(1)} %get-tuple-element.54.near_ref, ...), custom_call_target="tpu_custom_call" | custom-call | flops 1572864 | bytes 65536 | tf_op jit(solution)/shard_map/local_and_field/pallas_call | solution.py:511
  (27 shorter events, 5.0 us)
Async XLA Ops:
  0.0 11.0 %copy-start = (bf16[512,1536]{1,0:T(8,128)(2,1)S(1)}, bf16[512,1536]{1,0:T(8,128)(2,1)}, u32[]{:S(2)}) copy-start(bf16[512,1536]{1,0:T(8,128)(2,1)} %constant.6.clone.table_ref) | copy-start | bytes 4718596
  0.0 11.0 %copy-start.1 = (bf16[12,64,512]{2,1,0:T(8,128)(2,1)S(1)}, bf16[12,64,512]{2,1,0:T(8,128)(2,1)}, u32[]{:S(2)}) copy-start(bf16[12,64,512]{2,1,0:T(8,128)(2,1)} %basis_ref.7) | copy-start | bytes 2359300
  0.0 11.0 %copy-start.2 = (s32[12,512]{1,0:T(8,128)S(1)}, s32[12,512]{1,0:T(8,128)}, u32[]{:S(2)}) copy-start(s32[12,512]{1,0:T(8,128)} %order_ref.7) | copy-start | bytes 73732
  0.0 11.0 %copy-start.3 = (s32[12,2]{0,1:T(2,128)S(1)}, s32[12,2]{0,1:T(2,128)}, u32[]{:S(2)}) copy-start(s32[12,2]{0,1:T(2,128)} %param.17) | copy-start | bytes 292
  4.8 10.4 %collective-permute-start.3 = (bf16[13,64,128]{2,1,0:T(8,128)(2,1)S(1)}, bf16[13,64,128]{2,1,0:T(8,128)(2,1)S(1)}, u32[]{:S(2)}, u32[]{:S(2)}) collective-permute-start(bf16[13,64,128]{2,1,0:T(8,128)(2,1)S(1)} %get-tuple-element.38.refs_0_), channel_id=1, source_target_pairs={{0,8},{1,9},{2,10},{3,11},{4,12},{5,13},{6,14},{7,15},{8,16},{9,17... | collective-permute-start | bytes 638984 | tf_op jit(solution)/shard_map/ppermute | solution.py:38
  7.9 7.3 %collective-permute-start.1 = (bf16[13,64,128]{2,1,0:T(8,128)(2,1)S(1)}, bf16[13,64,128]{2,1,0:T(8,128)(2,1)S(1)}, u32[]{:S(2)}, u32[]{:S(2)}) collective-permute-start(bf16[13,64,128]{2,1,0:T(8,128)(2,1)S(1)} %get-tuple-element.38.refs_0_), channel_id=1, source_target_pairs={{0,2},{1,3},{2,0},{3,1},{4,6},{5,7},{6,4},{7,5},{8,10},{9,11},{10,... | collective-permute-start | bytes 638984 | tf_op jit(solution)/shard_map/ppermute | solution.py:38
  9.4 6.5 %collective-permute-start.4 = (bf16[13,64,128]{2,1,0:T(8,128)(2,1)S(1)}, bf16[13,64,128]{2,1,0:T(8,128)(2,1)S(1)}, u32[]{:S(2)}, u32[]{:S(2)}) collective-permute-start(bf16[13,64,128]{2,1,0:T(8,128)(2,1)S(1)} %get-tuple-element.38.refs_0_), channel_id=1, source_target_pairs={{0,4},{1,5},{2,6},{3,7},{4,0},{5,1},{6,2},{7,3},{8,12},{9,13},{10,... | collective-permute-start | bytes 638984 | tf_op jit(solution)/shard_map/ppermute | solution.py:38
  15.9 7.1 %collective-permute-start.5 = (bf16[13,64,128]{2,1,0:T(8,128)(2,1)S(1)}, bf16[13,64,128]{2,1,0:T(8,128)(2,1)S(1)}, u32[]{:S(2)}, u32[]{:S(2)}) collective-permute-start(bf16[13,64,128]{2,1,0:T(8,128)(2,1)S(1)} %collective-permute-done.3.refs_1_), channel_id=1, source_target_pairs={{0,2},{1,3},{2,0},{3,1},{4,6},{5,7},{6,4},{7,5},{8,10},{9,11},{10,... | collective-permute-start | bytes 638984 | tf_op jit(solution)/shard_map/ppermute | solution.py:38
  16.8 6.2 %collective-permute-start.6 = (bf16[13,64,128]{2,1,0:T(8,128)(2,1)S(1)}, bf16[13,64,128]{2,1,0:T(8,128)(2,1)S(1)}, u32[]{:S(2)}, u32[]{:S(2)}) collective-permute-start(bf16[13,64,128]{2,1,0:T(8,128)(2,1)S(1)} %collective-permute-done.3.refs_1_), channel_id=1, source_target_pairs={{0,4},{1,5},{2,6},{3,7},{4,0},{5,1},{6,2},{7,3},{8,12},{9,13},{10,... | collective-permute-start | bytes 638984 | tf_op jit(solution)/shard_map/ppermute | solution.py:38
  18.3 4.7 %collective-permute-start.2 = (bf16[512,128]{1,0:T(8,128)(2,1)S(1)}, bf16[512,128]{1,0:T(8,128)(2,1)S(1)}, u32[]{:S(2)}, u32[]{:S(2)}) collective-permute-start(bf16[512,128]{1,0:T(8,128)(2,1)S(1)} %get-tuple-element.39), channel_id=1, source_target_pairs={{1,2},{3,4},{5,6},{7,8},{9,10},{11,12},{13,14},{15,16},{17,18},{19... | collective-permute-start | bytes 393224 | tf_op jit(solution)/shard_map/ppermute | solution.py:561
  23.0 21.9 %collective-permute-start.11 = (bf16[15,64,1024]{2,1,0:T(8,128)(2,1)S(1)}, bf16[15,64,1024]{2,1,0:T(8,128)(2,1)S(1)}, u32[]{:S(2)}, u32[]{:S(2)}) collective-permute-start(bf16[15,64,1024]{2,1,0:T(8,128)(2,1)S(1)} %get-tuple-element.52), channel_id=1, source_target_pairs={{0,1},{1,0},{2,3},{3,2},{4,5},{5,4},{6,7},{7,6},{8,9},{9,8},{10,11... | collective-permute-start | bytes 5898248 | tf_op jit(solution)/shard_map/ppermute | solution.py:38
  25.6 8.6 %collective-permute-start = (bf16[13,64,128]{2,1,0:T(8,128)(2,1)S(1)}, bf16[13,64,128]{2,1,0:T(8,128)(2,1)S(1)}, u32[]{:S(2)}, u32[]{:S(2)}) collective-permute-start(bf16[13,64,128]{2,1,0:T(8,128)(2,1)S(1)} %get-tuple-element.38.refs_0_), channel_id=1, source_target_pairs={{0,24},{1,25},{2,26},{3,27},{4,28},{5,29},{6,30},{7,31},{8,0},{9,1... | collective-permute-start | bytes 638984 | tf_op jit(solution)/shard_map/ppermute | solution.py:38
  28.6 11.8 %collective-permute-start.7 = (bf16[13,64,128]{2,1,0:T(8,128)(2,1)S(1)}, bf16[13,64,128]{2,1,0:T(8,128)(2,1)S(1)}, u32[]{:S(2)}, u32[]{:S(2)}) collective-permute-start(bf16[13,64,128]{2,1,0:T(8,128)(2,1)S(1)} %collective-permute-done.3.refs_1_), channel_id=1, source_target_pairs={{0,8},{1,9},{2,10},{3,11},{4,12},{5,13},{6,14},{7,15},{8,16},{9,17... | collective-permute-start | bytes 638984 | tf_op jit(solution)/shard_map/ppermute | solution.py:38
  28.6 12.9 %collective-permute-start.10 = (bf16[26,64,128]{2,1,0:T(8,128)(2,1)S(1)}, bf16[26,64,128]{2,1,0:T(8,128)(2,1)S(1)}, u32[]{:S(2)}, u32[]{:S(2)}) collective-permute-start(bf16[26,64,128]{2,1,0:T(8,128)(2,1)S(1)} %choose.2), channel_id=1, source_target_pairs={{0,4},{1,3},{2,6},{3,1},{4,0},{5,7},{6,2},{7,5},{8,12},{9,11},{10,... | collective-permute-start | bytes 1277960 | tf_op jit(solution)/shard_map/ppermute | solution.py:38
  40.4 11.4 %collective-permute-start.8 = (bf16[26,64,128]{2,1,0:T(8,128)(2,1)S(1)}, bf16[26,64,128]{2,1,0:T(8,128)(2,1)S(1)}, u32[]{:S(2)}, u32[]{:S(2)}) collective-permute-start(bf16[26,64,128]{2,1,0:T(8,128)(2,1)S(1)} %join.1.refs_0_), channel_id=1, source_target_pairs={{0,2},{1,3},{2,0},{3,1},{4,6},{5,7},{6,4},{7,5},{8,10},{9,11},{10,... | collective-permute-start | bytes 1277960 | tf_op jit(solution)/shard_map/ppermute | solution.py:38
  40.6 11.4 %collective-permute-start.9 = (bf16[26,64,128]{2,1,0:T(8,128)(2,1)S(1)}, bf16[26,64,128]{2,1,0:T(8,128)(2,1)S(1)}, u32[]{:S(2)}, u32[]{:S(2)}) collective-permute-start(bf16[26,64,128]{2,1,0:T(8,128)(2,1)S(1)} %join.1.refs_0_), channel_id=1, source_target_pairs={{0,4},{1,5},{2,6},{3,7},{4,0},{5,1},{6,2},{7,3},{8,12},{9,13},{10,... | collective-permute-start | bytes 1277960 | tf_op jit(solution)/shard_map/ppermute | solution.py:38
  52.0 5.9 %collective-permute-start.12 = (bf16[13,64,128]{2,1,0:T(8,128)(2,1)S(1)}, bf16[13,64,128]{2,1,0:T(8,128)(2,1)S(1)}, u32[]{:S(2)}, u32[]{:S(2)}) collective-permute-start(bf16[13,64,128]{2,1,0:T(8,128)(2,1)S(1)} %get-tuple-element.56), channel_id=1, source_target_pairs={{0,4},{1,3},{2,6},{3,1},{4,0},{5,7},{6,2},{7,5},{8,12},{9,11},{10,... | collective-permute-start | bytes 638984 | tf_op jit(solution)/shard_map/ppermute | solution.py:38
  53.0 7.2 %collective-permute-start.13 = (bf16[13,64,128]{2,1,0:T(8,128)(2,1)S(1)}, bf16[13,64,128]{2,1,0:T(8,128)(2,1)S(1)}, u32[]{:S(2)}, u32[]{:S(2)}) collective-permute-start(bf16[13,64,128]{2,1,0:T(8,128)(2,1)S(1)} %get-tuple-element.60), channel_id=1, source_target_pairs={{0,4},{1,3},{2,6},{3,1},{4,0},{5,7},{6,2},{7,5},{8,12},{9,11},{10,... | collective-permute-start | bytes 638984 | tf_op jit(solution)/shard_map/ppermute | solution.py:38
  61.3 1.8 %collective-permute-start.14 = (f32[13,64,128]{2,1,0:T(8,128)S(1)}, f32[13,64,128]{2,1,0:T(8,128)S(1)}, u32[]{:S(2)}, u32[]{:S(2)}) collective-permute-start(f32[13,64,128]{2,1,0:T(8,128)S(1)} %far_1_2.1), channel_id=1, source_target_pairs={{0,1},{1,0},{2,3},{3,2},{4,5},{5,4},{6,7},{7,6},{8,9},{9,8},{10,11... | collective-permute-start | bytes 1277960 | tf_op jit(solution)/shard_map/ppermute | solution.py:38

commit v9 on v8

--- a/solution.py
+++ b/solution.py
@@ -241,34 +241,26 @@
     )(*parts)
 
 
-def choose_kernel(number, me_ref, *refs):
-    ins, outs = refs[:2 * number], refs[2 * number:]
-    for core in range(2):
-        @pl.when(me_ref[0] % 2 == core)
-        def _(core=core):
-            at = 0
-            for ref in ins[core * number:(core + 1) * number]:
-                done = 0
-                while done < ref.shape[0]:
-                    out, base = outs[at // outs[0].shape[0]], at % outs[0].shape[0]
-                    size = min(ref.shape[0] - done, out.shape[0] - base)
-                    out[base:base + size] = ref[done:done + size]
-                    done, at = done + size, at + size
-
-
-def choose(me, from_x, from_y, streams):
-    parts = list(from_x) + list(from_y)
-    total = sum(part.shape[0] for part in from_x)
-    shape = jax.ShapeDtypeStruct((total // streams,) + from_x[0].shape[1:], BF)
+def choose_kernel(me_ref, x_ref, y_ref, out_ref):
+    @pl.when(me_ref[0] % 2 == 0)
+    def _():
+        out_ref[...] = x_ref[...]
+
+    @pl.when(me_ref[0] % 2 == 1)
+    def _():
+        out_ref[...] = y_ref[...]
+
+
+def choose(me, from_x, from_y):
     return pl.pallas_call(
-        functools.partial(choose_kernel, len(from_x)),
+        choose_kernel,
         name="choose",
-        in_specs=[scalars()] + [whole()] * len(parts),
-        out_specs=[whole()] * streams,
-        out_shape=[shape] * streams,
-        compiler_params=params(8 if total <= 32 else 32),
-        cost_estimate=cost(0, MIB // 2),
-    )(me, *parts)
+        in_specs=[scalars(), whole(), whole()],
+        out_specs=whole(),
+        out_shape=jax.ShapeDtypeStruct(from_x.shape, BF),
+        compiler_params=params(8),
+        cost_estimate=cost(0, MIB // 4),
+    )(me, from_x, from_y)
 
 
 def dense_kernel(per, slots, entry_ref, block_ref, inner_ref, coupling_ref, top_ref,
@@ -558,6 +550,7 @@
         lines.append(along_z(line if len(lines) == 1 else lines[-1], 1))
     ready = after(line, from_x, from_y)
     next_x, next_y = over_x(ready), over_y(ready)
+    far = onward(choose(me, after(from_x, ready), from_y))
     cross = lax.ppermute(
         cross,
         "subtree",
@@ -566,24 +559,28 @@
     own_blocks, my_other, turned_transfer = dense_couplings(
         after(entry, ready), own_at, inner, coupling, top_coupling, transfer, slots
     )
-    round_0 = ((shared, line), (from_x, next_x), (from_y, next_y))
-    chosen = choose(me, (after(from_x, cross, my_other), next_x), round_0[2], 1)
-    round_0 += (tuple(map(onward, chosen)),)
-
-    joined = join([after(lines[0], *chosen)] + lines[1:])
+    chosen = choose(me, after(next_x, cross, my_other), next_y)
+    next_far = onward(chosen)
+
+    joined = join([after(lines[0], chosen, far)] + lines[1:])
     last_x, last_y = over_x(joined), over_y(joined)
-    other_blocks = over_core(after(my_other, *chosen))
-    held = after(ordered, joined, *round_0[3])
+    other_blocks = over_core(after(my_other, joined))
+    held = after(ordered, joined)
     filled = near_field(list(range(cut, pairs - 1)), *near_args, held, filled=filled)
+    next_far = after(next_far, filled[0])
+    last_far = [along_z(far, layers - 1)]
+    for _ in range(layers - 3):
+        last_far.append(along_z(next_far if len(last_far) == 1 else last_far[-1], 1))
+    held = after(ordered, filled[0])
     *filled, other_at = near_field(
-        [0, pairs - 1], *near_args, after(ordered, filled[0]), halos=(me, cross, other_blocks), filled=filled
-    )
-    far = tuple(map(onward, choose(me, (after(last_x, filled[0]),), (last_y,), 2)))
+        [0, pairs - 1], *near_args, held, halos=(me, cross, other_blocks), filled=filled
+    )
+    round_0 = ((shared, line), (from_x, next_x), (from_y, next_y), (far, next_far))
     steps = [0, 1]
     own = far_round(0, steps, slots, own_at, round_0, own_blocks)
     other = far_round(1, steps, slots, other_at, round_0, other_blocks)
     steps = list(range(2, layers))
-    round_1 = ((joined,), (last_x,), (last_y,), (after(far[0], own, other),) + far[1:])
+    round_1 = ((joined,), (last_x,), (last_y,), (after(last_far[0], own, other), *last_far[1:]))
     other = far_round(1, steps, slots, other_at, round_1, other_blocks, other)
     own = far_round(0, steps, slots, own_at, round_1, own_blocks, own)
     return field(own, over_core(other), turned_transfer, *filled)

time: 66.1 us -> 54.4 us (0.82)
  waiting for transfers between devices: 20.2 us -> 9.53 us
  starting transfers between devices: 18.8 us -> 17.9 us
    ppermute x14 -> x15, waiting for transfers between devices: 20.2 us -> 9.53 us  [send(): lax.ppermute(block, 'subtree', [(d, target(d)) for d in range(count)])]
    ppermute x14 -> x15, starting transfers between devices: 18.2 us -> 17.2 us  [send(): lax.ppermute(block, 'subtree', [(d, target(d)) for d in range(count)])]
  transfers between devices with their start and end apart: 15 -> 16, of which waited for: 9 -> 7; matrix products, arithmetic and copies ran while one was open for 0% -> 0% of each run, Pallas kernels for 27% -> 33%
where the time goes in v9:
time: 54.4 us; the launch traced here: 54.2 us
  Pallas kernels  26.6 us (49%)
  starting transfers between devices  17.9 us (33%)
  waiting for transfers between devices  9.53 us (18%)
    ppermute x15, starting transfers between devices, send(): lax.ppermute(block, 'subtree', [(d, target(d)) for d in range(count)])  17.2 us
    pallas_call x3, Pallas kernels, near_field(): pl.pallas_call(functools.partial(near_kernel, halos is not None, pair_of,...  10.7 us
    ppermute x15, waiting for transfers between devices, send(): lax.ppermute(block, 'subtree', [(d, target(d)) for d in range(count)])  9.53 us
    pallas_call x1, Pallas kernels, skeletons_of(): pl.pallas_call(functools.partial(skeleton_kernel, per, layers), name='ord...  4.83 us
    pallas_call x4, Pallas kernels, far_round(): pl.pallas_call(functools.partial(round_kernel, plane, steps, slots, [len(...  4.33 us
    pallas_call x1, Pallas kernels, dense_couplings(): pl.pallas_call(functools.partial(dense_kernel, per, slots), name='couplin...  3.98 us
    pallas_call x1, Pallas kernels, field(): pl.pallas_call(functools.partial(field_kernel, per), name='local_and_fiel...  2.73 us
  transfers between devices with their start and end apart: 16, of which 7 were waited for; matrix products, arithmetic and copies ran while one was open for 0% of the time, Pallas kernels for 33%

profile of v9, /device:TPU:0, one launch (start us, length us, event | category | flops | bytes accessed | tf_op | source)
XLA Modules:
  0.0 54.2 jit_solution(13287160846205259500)
XLA Ops:
  0.0 4.8 %order_and_skeleton.1 = (bf16[6144,128]{1,0:T(8,128)(2,1)S(1)}, bf16[13,64,128]{2,1,0:T(8,128)(2,1)S(1)}, bf16[512,128]{1,0:T(8,128)(2,1)S(1)}, bf16[512,128]{1,...) custom-call(s32[1]{0:T(128)} %bitcast.me_ref.refs_0_, s32[12,512]{1,0:T(8,128)} %order_ref.7, ...), custom_call_target="tpu_custom_call" | custom-call | flops 12582912 | bytes 65536 | tf_op jit(solution)/shard_map/order_and_skeleton/pallas_call | solution.py:186
  4.8 3.1 %collective-permute-start.1 = (bf16[13,64,128]{2,1,0:T(8,128)(2,1)S(1)}, bf16[13,64,128]{2,1,0:T(8,128)(2,1)S(1)}, u32[]{:S(2)}, u32[]{:S(2)}) collective-permute-start(bf16[13,64,128]{2,1,0:T(8,128)(2,1)S(1)} %get-tuple-element.37.refs_0_), channel_id=1, source_target_pairs={{0,8},{1,9},{2,10},{3,11},{4,12},{5,13},{6,14},{7,15},{8,16},{9,17... | collective-permute-start | bytes 638984 | tf_op jit(solution)/shard_map/ppermute | solution.py:38
  7.9 1.5 %collective-permute-start.2 = (bf16[13,64,128]{2,1,0:T(8,128)(2,1)S(1)}, bf16[13,64,128]{2,1,0:T(8,128)(2,1)S(1)}, u32[]{:S(2)}, u32[]{:S(2)}) collective-permute-start(bf16[13,64,128]{2,1,0:T(8,128)(2,1)S(1)} %get-tuple-element.37.refs_0_), channel_id=1, source_target_pairs={{0,2},{1,3},{2,0},{3,1},{4,6},{5,7},{6,4},{7,5},{8,10},{9,11},{10,... | collective-permute-start | bytes 638984 | tf_op jit(solution)/shard_map/ppermute | solution.py:38
  9.4 1.5 %collective-permute-start.3 = (bf16[13,64,128]{2,1,0:T(8,128)(2,1)S(1)}, bf16[13,64,128]{2,1,0:T(8,128)(2,1)S(1)}, u32[]{:S(2)}, u32[]{:S(2)}) collective-permute-start(bf16[13,64,128]{2,1,0:T(8,128)(2,1)S(1)} %get-tuple-element.37.refs_0_), channel_id=1, source_target_pairs={{0,4},{1,5},{2,6},{3,7},{4,0},{5,1},{6,2},{7,3},{8,12},{9,13},{10,... | collective-permute-start | bytes 638984 | tf_op jit(solution)/shard_map/ppermute | solution.py:38
  11.7 3.5 %near_1.1 = (bf16[6144,128]{1,0:T(8,128)(2,1)S(1)}, bf16[6144,64]{1,0:T(8,128)(2,1)S(1)}) custom-call(s32[2,12]{1,0:T(2,128)S(1)} %bitcast.2, s32[12,512]{1,0:T(8,128)S(1)} %copy-done.2, bf16[512,1536]{1,0:T(8,128)(2,1)S(1)} %copy-done, bf16[12,64,512]{2,1,0:T(8,128)(2,1)S(1)} %copy-done.1, bf16[6144,128]{1,0:T(8,128)(2,1)S(1)} %get-tuple-element.53.ordered_ref), custom_call_target="tpu_custom_call" | custom-call | flops 20971520 | bytes 32768 | tf_op jit(solution)/shard_map/near_1/pallas_call | solution.py:462
  15.9 1.2 %collective-permute-start.4 = (bf16[13,64,128]{2,1,0:T(8,128)(2,1)S(1)}, bf16[13,64,128]{2,1,0:T(8,128)(2,1)S(1)}, u32[]{:S(2)}, u32[]{:S(2)}) collective-permute-start(bf16[13,64,128]{2,1,0:T(8,128)(2,1)S(1)} %collective-permute-done.1.refs_1_), channel_id=1, source_target_pairs={{0,2},{1,3},{2,0},{3,1},{4,6},{5,7},{6,4},{7,5},{8,10},{9,11},{10,... | collective-permute-start | bytes 638984 | tf_op jit(solution)/shard_map/ppermute | solution.py:38
  17.1 2.4 %collective-permute-start = (bf16[13,64,128]{2,1,0:T(8,128)(2,1)S(1)}, bf16[13,64,128]{2,1,0:T(8,128)(2,1)S(1)}, u32[]{:S(2)}, u32[]{:S(2)}) collective-permute-start(bf16[13,64,128]{2,1,0:T(8,128)(2,1)S(1)} %get-tuple-element.37.refs_0_), channel_id=1, source_target_pairs={{0,24},{1,25},{2,26},{3,27},{4,28},{5,29},{6,30},{7,31},{8,0},{9,1... | collective-permute-start | bytes 638984 | tf_op jit(solution)/shard_map/ppermute | solution.py:38
  19.5 1.6 %collective-permute-start.6 = (bf16[13,64,128]{2,1,0:T(8,128)(2,1)S(1)}, bf16[13,64,128]{2,1,0:T(8,128)(2,1)S(1)}, u32[]{:S(2)}, u32[]{:S(2)}) collective-permute-start(bf16[13,64,128]{2,1,0:T(8,128)(2,1)S(1)} %collective-permute-done.1.refs_1_), channel_id=1, source_target_pairs={{0,4},{1,5},{2,6},{3,7},{4,0},{5,1},{6,2},{7,3},{8,12},{9,13},{10,... | collective-permute-start | bytes 638984 | tf_op jit(solution)/shard_map/ppermute | solution.py:38
  21.6 4.0 %couplings_by_owner.1 = (bf16[13,64,1024]{2,1,0:T(8,128)(2,1)S(1)}, bf16[15,64,1024]{2,1,0:T(8,128)(2,1)S(1)}, bf16[12,64,64]{2,1,0:T(8,128)(2,1)S(1)}) custom-call(s32[16,128]{1,0:T(8,128)S(1)} %get-tuple-element.42.entry_ref, s32[16,128]{1,0:T(8,128)S(1)} %get-tuple-element.33.block_ref.at_ref, bf16[512,128]{1,0:T(8,128)(2,1)S(1)} %get-tuple-element.43.inner_ref, ...), custom_call_target="tpu_custom_call" | custom-call | bytes 131072 | tf_op jit(solution)/shard_map/couplings_by_owner/pallas_call | solution.py:307
  25.6 1.7 %collective-permute-done.6.y_ref.refs_5_ = bf16[13,64,128]{2,1,0:T(8,128)(2,1)S(1)} collective-permute-done((bf16[13,64,128]{2,1,0:T(8,128)(2,1)S(1)}, bf16[13,64,128]{2,1,0:T(8,128)(2,1)S(1)}, u32[]{:S(2)}, u32[]{:S(2)}) %collective-permute-start.6) | collective-permute-done | bytes 213024 | tf_op jit(solution)/shard_map/ppermute | solution.py:38
  27.4 2.2 %collective-permute-done.7.refs_6_ = bf16[13,64,128]{2,1,0:T(8,128)(2,1)S(1)} collective-permute-done((bf16[13,64,128]{2,1,0:T(8,128)(2,1)S(1)}, bf16[13,64,128]{2,1,0:T(8,128)(2,1)S(1)}, u32[]{:S(2)}, u32[]{:S(2)}) %collective-permute-start.7) | collective-permute-done | bytes 213024 | tf_op jit(solution)/shard_map/ppermute | solution.py:38
  29.7 2.0 %collective-permute-done.8.refs_1_ = bf16[13,64,128]{2,1,0:T(8,128)(2,1)S(1)} collective-permute-done((bf16[13,64,128]{2,1,0:T(8,128)(2,1)S(1)}, bf16[13,64,128]{2,1,0:T(8,128)(2,1)S(1)}, u32[]{:S(2)}, u32[]{:S(2)}) %collective-permute-start.8) | collective-permute-done | bytes 213024 | tf_op jit(solution)/shard_map/ppermute | solution.py:38
  31.9 1.5 %collective-permute-start.12 = (bf16[13,64,128]{2,1,0:T(8,128)(2,1)S(1)}, bf16[13,64,128]{2,1,0:T(8,128)(2,1)S(1)}, u32[]{:S(2)}, u32[]{:S(2)}) collective-permute-start(bf16[13,64,128]{2,1,0:T(8,128)(2,1)S(1)} %choose.2), channel_id=1, source_target_pairs={{0,4},{1,3},{2,6},{3,1},{4,0},{5,7},{6,2},{7,5},{8,12},{9,11},{10,... | collective-permute-start | bytes 638984 | tf_op jit(solution)/shard_map/ppermute | solution.py:38
  33.9 0.9 %collective-permute-start.9 = (bf16[26,64,128]{2,1,0:T(8,128)(2,1)S(1)}, bf16[26,64,128]{2,1,0:T(8,128)(2,1)S(1)}, u32[]{:S(2)}, u32[]{:S(2)}) collective-permute-start(bf16[26,64,128]{2,1,0:T(8,128)(2,1)S(1)} %join.1.refs_0_), channel_id=1, source_target_pairs={{0,2},{1,3},{2,0},{3,1},{4,6},{5,7},{6,4},{7,5},{8,10},{9,11},{10,... | collective-permute-start | bytes 1277960 | tf_op jit(solution)/shard_map/ppermute | solution.py:38
  34.8 2.0 %collective-permute-start.11 = (bf16[13,64,128]{2,1,0:T(8,128)(2,1)S(1)}, bf16[13,64,128]{2,1,0:T(8,128)(2,1)S(1)}, u32[]{:S(2)}, u32[]{:S(2)}) collective-permute-start(bf16[13,64,128]{2,1,0:T(8,128)(2,1)S(1)} %collective-permute-done.7.refs_6_), channel_id=1, source_target_pairs={{0,24},{1,25},{2,26},{3,27},{4,28},{5,29},{6,30},{7,31},{8,0},{9,1... | collective-permute-start | bytes 638984 | tf_op jit(solution)/shard_map/ppermute | solution.py:38
  36.8 3.4 %near_3.1 = (bf16[6144,128]{1,0:T(8,128)(2,1)S(1)}, bf16[6144,64]{1,0:T(8,128)(2,1)S(1)}) custom-call(s32[2,12]{1,0:T(2,128)S(1)} %bitcast.3, s32[12,512]{1,0:T(8,128)S(1)} %copy-done.2, bf16[512,1536]{1,0:T(8,128)(2,1)S(1)} %copy-done, bf16[12,64,512]{2,1,0:T(8,128)(2,1)S(1)} %copy-done.1, ...), custom_call_target="tpu_custom_call", output_to_operand_aliasing={{0}: (5, {}), {1}: (6, {})} | custom-call | flops 20971520 | bytes 32768 | tf_op jit(solution)/shard_map/near_3/pallas_call | solution.py:462
  40.5 1.1 %far_0_0.1.refs_6_ = f32[13,64,128]{2,1,0:T(8,128)S(1)} custom-call(s32[16,128]{1,0:T(8,128)S(1)} %get-tuple-element.33.block_ref.at_ref, bf16[13,64,128]{2,1,0:T(8,128)(2,1)S(1)} %get-tuple-element.37.refs_0_, bf16[13,64,128]{2,1,0:T(8,128)(2,1)S(1)} %collective-permute-done.1.refs_1_, bf16[13,64,128]{2,1,0:T(8,128)(2,1)S(1)} %collective-permute-done.2.x_ref.refs_2_, ...), custom_call_target="tpu_custom_call" | custom-call | flops 1703936 | bytes 16384 | tf_op jit(solution)/shard_map/far_0_0/pallas_call | solution.py:365
  41.6 3.8 %near_0.1 = (bf16[6144,128]{1,0:T(8,128)(2,1)S(1)}, bf16[6144,64]{1,0:T(8,128)(2,1)S(1)}, s32[16,128]{1,0:T(8,128)S(1)}) custom-call(s32[2,12]{1,0:T(2,128)S(1)} %bitcast.4, s32[12,512]{1,0:T(8,128)S(1)} %copy-done.2, bf16[512,1536]{1,0:T(8,128)(2,1)S(1)} %copy-done, ...), custom_call_target="tpu_custom_call", output_to_operand_aliasing={{0}: (9, {}), {1}: (10, {})} | custom-call | flops 20971520 | bytes 32768 | tf_op jit(solution)/shard_map/near_0/pallas_call | solution.py:462
  45.4 1.1 %far_1_0.1.refs_6_ = f32[13,64,128]{2,1,0:T(8,128)S(1)} custom-call(s32[16,128]{1,0:T(8,128)S(1)} %get-tuple-element.56.at_ref, bf16[13,64,128]{2,1,0:T(8,128)(2,1)S(1)} %get-tuple-element.37.refs_0_, bf16[13,64,128]{2,1,0:T(8,128)(2,1)S(1)} %collective-permute-done.1.refs_1_, bf16[13,64,128]{2,1,0:T(8,128)(2,1)S(1)} %collective-permute-done.2.x_ref.refs_2_, ...), custom_call_target="tpu_custom_call" | custom-call | flops 1703936 | bytes 16384 | tf_op jit(solution)/shard_map/far_1_0/pallas_call | solution.py:365
  46.5 2.1 %collective-permute-done.14.refs_4_ = bf16[13,64,128]{2,1,0:T(8,128)(2,1)S(1)} collective-permute-done((bf16[13,64,128]{2,1,0:T(8,128)(2,1)S(1)}, bf16[13,64,128]{2,1,0:T(8,128)(2,1)S(1)}, u32[]{:S(2)}, u32[]{:S(2)}) %collective-permute-start.14) | collective-permute-done | bytes 213024 | tf_op jit(solution)/shard_map/ppermute | solution.py:38
  48.6 1.1 %far_1_2.1 = f32[13,64,128]{2,1,0:T(8,128)S(1)} custom-call(s32[16,128]{1,0:T(8,128)S(1)} %get-tuple-element.56.at_ref, bf16[26,64,128]{2,1,0:T(8,128)(2,1)S(1)} %join.1.refs_0_, bf16[26,64,128]{2,1,0:T(8,128)(2,1)S(1)} %collective-permute-done.9.refs_1_, bf16[26,64,128]{2,1,0:T(8,128)(2,1)S(1)} %collective-permute-done.10.refs_2_, ...), custom_call_target="tpu_custom_call" | custom-call | flops 1703936 | bytes 16384 | tf_op jit(solution)/shard_map/far_1_2/pallas_call | solution.py:365
  49.8 1.1 %far_0_2.1.own_ref = f32[13,64,128]{2,1,0:T(8,128)S(1)} custom-call(s32[16,128]{1,0:T(8,128)S(1)} %get-tuple-element.33.block_ref.at_ref, bf16[26,64,128]{2,1,0:T(8,128)(2,1)S(1)} %join.1.refs_0_, bf16[26,64,128]{2,1,0:T(8,128)(2,1)S(1)} %collective-permute-done.9.refs_1_, bf16[26,64,128]{2,1,0:T(8,128)(2,1)S(1)} %collective-permute-done.10.refs_2_, ...), custom_call_target="tpu_custom_call" | custom-call | flops 1703936 | bytes 16384 | tf_op jit(solution)/shard_map/far_0_2/pallas_call | solution.py:365
  50.9 0.7 %collective-permute-done.15.other_ref = f32[13,64,128]{2,1,0:T(8,128)S(1)} collective-permute-done((f32[13,64,128]{2,1,0:T(8,128)S(1)}, f32[13,64,128]{2,1,0:T(8,128)S(1)}, u32[]{:S(2)}, u32[]{:S(2)}) %collective-permute-start.15) | collective-permute-done | bytes 426016 | tf_op jit(solution)/shard_map/ppermute | solution.py:38
  51.5 2.7 %local_and_field.1 = bf16[6144,128]{1,0:T(8,128)(2,1)} custom-call(f32[13,64,128]{2,1,0:T(8,128)S(1)} %far_0_2.1.own_ref, f32[13,64,128]{2,1,0:T(8,128)S(1)} %collective-permute-done.15.other_ref, bf16[12,64,64]{2,1,0:T(8,128)(2,1)S(1)} %get-tuple-element.58.turned_transfer_ref, bf16[6144,128]{1,0:T(8,128)(2,1)S(1)} %get-tuple-element.59.near_ref, ...), custom_call_target="tpu_custom_call" | custom-call | flops 1572864 | bytes 65536 | tf_op jit(solution)/shard_map/local_and_field/pallas_call | solution.py:503
  (29 shorter events, 3.1 us)
Async XLA Ops:
  0.0 11.6 %copy-start = (bf16[512,1536]{1,0:T(8,128)(2,1)S(1)}, bf16[512,1536]{1,0:T(8,128)(2,1)}, u32[]{:S(2)}) copy-start(bf16[512,1536]{1,0:T(8,128)(2,1)} %constant.6.clone.table_ref) | copy-start | bytes 4718596
  0.0 11.6 %copy-start.1 = (bf16[12,64,512]{2,1,0:T(8,128)(2,1)S(1)}, bf16[12,64,512]{2,1,0:T(8,128)(2,1)}, u32[]{:S(2)}) copy-start(bf16[12,64,512]{2,1,0:T(8,128)(2,1)} %basis_ref.7) | copy-start | bytes 2359300
  0.0 11.6 %copy-start.2 = (s32[12,512]{1,0:T(8,128)S(1)}, s32[12,512]{1,0:T(8,128)}, u32[]{:S(2)}) copy-start(s32[12,512]{1,0:T(8,128)} %order_ref.7) | copy-start | bytes 73732
  0.0 11.6 %copy-start.3 = (s32[12,2]{0,1:T(2,128)S(1)}, s32[12,2]{0,1:T(2,128)}, u32[]{:S(2)}) copy-start(s32[12,2]{0,1:T(2,128)} %param.17) | copy-start | bytes 292
  4.8 10.4 %collective-permute-start.1 = (bf16[13,64,128]{2,1,0:T(8,128)(2,1)S(1)}, bf16[13,64,128]{2,1,0:T(8,128)(2,1)S(1)}, u32[]{:S(2)}, u32[]{:S(2)}) collective-permute-start(bf16[13,64,128]{2,1,0:T(8,128)(2,1)S(1)} %get-tuple-element.37.refs_0_), channel_id=1, source_target_pairs={{0,8},{1,9},{2,10},{3,11},{4,12},{5,13},{6,14},{7,15},{8,16},{9,17... | collective-permute-start | bytes 638984 | tf_op jit(solution)/shard_map/ppermute | solution.py:38
  7.9 7.3 %collective-permute-start.2 = (bf16[13,64,128]{2,1,0:T(8,128)(2,1)S(1)}, bf16[13,64,128]{2,1,0:T(8,128)(2,1)S(1)}, u32[]{:S(2)}, u32[]{:S(2)}) collective-permute-start(bf16[13,64,128]{2,1,0:T(8,128)(2,1)S(1)} %get-tuple-element.37.refs_0_), channel_id=1, source_target_pairs={{0,2},{1,3},{2,0},{3,1},{4,6},{5,7},{6,4},{7,5},{8,10},{9,11},{10,... | collective-permute-start | bytes 638984 | tf_op jit(solution)/shard_map/ppermute | solution.py:38
  9.4 6.5 %collective-permute-start.3 = (bf16[13,64,128]{2,1,0:T(8,128)(2,1)S(1)}, bf16[13,64,128]{2,1,0:T(8,128)(2,1)S(1)}, u32[]{:S(2)}, u32[]{:S(2)}) collective-permute-start(bf16[13,64,128]{2,1,0:T(8,128)(2,1)S(1)} %get-tuple-element.37.refs_0_), channel_id=1, source_target_pairs={{0,4},{1,5},{2,6},{3,7},{4,0},{5,1},{6,2},{7,3},{8,12},{9,13},{10,... | collective-permute-start | bytes 638984 | tf_op jit(solution)/shard_map/ppermute | solution.py:38
  11.0 10.7 %collective-permute-start.5 = (bf16[512,128]{1,0:T(8,128)(2,1)S(1)}, bf16[512,128]{1,0:T(8,128)(2,1)S(1)}, u32[]{:S(2)}, u32[]{:S(2)}) collective-permute-start(bf16[512,128]{1,0:T(8,128)(2,1)S(1)} %get-tuple-element.40), channel_id=1, source_target_pairs={{1,2},{3,4},{5,6},{7,8},{9,10},{11,12},{13,14},{15,16},{17,18},{19... | collective-permute-start | bytes 393224 | tf_op jit(solution)/shard_map/ppermute | solution.py:554
  15.9 9.7 %collective-permute-start.4 = (bf16[13,64,128]{2,1,0:T(8,128)(2,1)S(1)}, bf16[13,64,128]{2,1,0:T(8,128)(2,1)S(1)}, u32[]{:S(2)}, u32[]{:S(2)}) collective-permute-start(bf16[13,64,128]{2,1,0:T(8,128)(2,1)S(1)} %collective-permute-done.1.refs_1_), channel_id=1, source_target_pairs={{0,2},{1,3},{2,0},{3,1},{4,6},{5,7},{6,4},{7,5},{8,10},{9,11},{10,... | collective-permute-start | bytes 638984 | tf_op jit(solution)/shard_map/ppermute | solution.py:38
  17.1 10.3 %collective-permute-start = (bf16[13,64,128]{2,1,0:T(8,128)(2,1)S(1)}, bf16[13,64,128]{2,1,0:T(8,128)(2,1)S(1)}, u32[]{:S(2)}, u32[]{:S(2)}) collective-permute-start(bf16[13,64,128]{2,1,0:T(8,128)(2,1)S(1)} %get-tuple-element.37.refs_0_), channel_id=1, source_target_pairs={{0,24},{1,25},{2,26},{3,27},{4,28},{5,29},{6,30},{7,31},{8,0},{9,1... | collective-permute-start | bytes 638984 | tf_op jit(solution)/shard_map/ppermute | solution.py:38
  19.5 7.9 %collective-permute-start.6 = (bf16[13,64,128]{2,1,0:T(8,128)(2,1)S(1)}, bf16[13,64,128]{2,1,0:T(8,128)(2,1)S(1)}, u32[]{:S(2)}, u32[]{:S(2)}) collective-permute-start(bf16[13,64,128]{2,1,0:T(8,128)(2,1)S(1)} %collective-permute-done.1.refs_1_), channel_id=1, source_target_pairs={{0,4},{1,5},{2,6},{3,7},{4,0},{5,1},{6,2},{7,3},{8,12},{9,13},{10,... | collective-permute-start | bytes 638984 | tf_op jit(solution)/shard_map/ppermute | solution.py:38
  21.2 8.5 %collective-permute-start.7 = (bf16[13,64,128]{2,1,0:T(8,128)(2,1)S(1)}, bf16[13,64,128]{2,1,0:T(8,128)(2,1)S(1)}, u32[]{:S(2)}, u32[]{:S(2)}) collective-permute-start(bf16[13,64,128]{2,1,0:T(8,128)(2,1)S(1)} %choose.3), channel_id=1, source_target_pairs={{0,4},{1,3},{2,6},{3,1},{4,0},{5,7},{6,2},{7,5},{8,12},{9,11},{10,... | collective-permute-start | bytes 638984 | tf_op jit(solution)/shard_map/ppermute | solution.py:38
  21.6 10.0 %collective-permute-start.8 = (bf16[13,64,128]{2,1,0:T(8,128)(2,1)S(1)}, bf16[13,64,128]{2,1,0:T(8,128)(2,1)S(1)}, u32[]{:S(2)}, u32[]{:S(2)}) collective-permute-start(bf16[13,64,128]{2,1,0:T(8,128)(2,1)S(1)} %collective-permute-done.1.refs_1_), channel_id=1, source_target_pairs={{0,8},{1,9},{2,10},{3,11},{4,12},{5,13},{6,14},{7,15},{8,16},{9,17... | collective-permute-start | bytes 638984 | tf_op jit(solution)/shard_map/ppermute | solution.py:38
  31.7 9.9 %collective-permute-start.13 = (bf16[15,64,1024]{2,1,0:T(8,128)(2,1)S(1)}, bf16[15,64,1024]{2,1,0:T(8,128)(2,1)S(1)}, u32[]{:S(2)}, u32[]{:S(2)}) collective-permute-start(bf16[15,64,1024]{2,1,0:T(8,128)(2,1)S(1)} %get-tuple-element.54), channel_id=1, source_target_pairs={{0,1},{1,0},{2,3},{3,2},{4,5},{5,4},{6,7},{7,6},{8,9},{9,8},{10,11... | collective-permute-start | bytes 5898248 | tf_op jit(solution)/shard_map/ppermute | solution.py:38
  31.9 8.4 %collective-permute-start.12 = (bf16[13,64,128]{2,1,0:T(8,128)(2,1)S(1)}, bf16[13,64,128]{2,1,0:T(8,128)(2,1)S(1)}, u32[]{:S(2)}, u32[]{:S(2)}) collective-permute-start(bf16[13,64,128]{2,1,0:T(8,128)(2,1)S(1)} %choose.2), channel_id=1, source_target_pairs={{0,4},{1,3},{2,6},{3,1},{4,0},{5,7},{6,2},{7,5},{8,12},{9,11},{10,... | collective-permute-start | bytes 638984 | tf_op jit(solution)/shard_map/ppermute | solution.py:38
  33.4 15.2 %collective-permute-start.10 = (bf16[26,64,128]{2,1,0:T(8,128)(2,1)S(1)}, bf16[26,64,128]{2,1,0:T(8,128)(2,1)S(1)}, u32[]{:S(2)}, u32[]{:S(2)}) collective-permute-start(bf16[26,64,128]{2,1,0:T(8,128)(2,1)S(1)} %join.1.refs_0_), channel_id=1, source_target_pairs={{0,4},{1,5},{2,6},{3,7},{4,0},{5,1},{6,2},{7,3},{8,12},{9,13},{10,... | collective-permute-start | bytes 1277960 | tf_op jit(solution)/shard_map/ppermute | solution.py:38
  33.9 14.7 %collective-permute-start.9 = (bf16[26,64,128]{2,1,0:T(8,128)(2,1)S(1)}, bf16[26,64,128]{2,1,0:T(8,128)(2,1)S(1)}, u32[]{:S(2)}, u32[]{:S(2)}) collective-permute-start(bf16[26,64,128]{2,1,0:T(8,128)(2,1)S(1)} %join.1.refs_0_), channel_id=1, source_target_pairs={{0,2},{1,3},{2,0},{3,1},{4,6},{5,7},{6,4},{7,5},{8,10},{9,11},{10,... | collective-permute-start | bytes 1277960 | tf_op jit(solution)/shard_map/ppermute | solution.py:38
  34.8 11.7 %collective-permute-start.11 = (bf16[13,64,128]{2,1,0:T(8,128)(2,1)S(1)}, bf16[13,64,128]{2,1,0:T(8,128)(2,1)S(1)}, u32[]{:S(2)}, u32[]{:S(2)}) collective-permute-start(bf16[13,64,128]{2,1,0:T(8,128)(2,1)S(1)} %collective-permute-done.7.refs_6_), channel_id=1, source_target_pairs={{0,24},{1,25},{2,26},{3,27},{4,28},{5,29},{6,30},{7,31},{8,0},{9,1... | collective-permute-start | bytes 638984 | tf_op jit(solution)/shard_map/ppermute | solution.py:38
  40.3 8.3 %collective-permute-start.14 = (bf16[13,64,128]{2,1,0:T(8,128)(2,1)S(1)}, bf16[13,64,128]{2,1,0:T(8,128)(2,1)S(1)}, u32[]{:S(2)}, u32[]{:S(2)}) collective-permute-start(bf16[13,64,128]{2,1,0:T(8,128)(2,1)S(1)} %collective-permute-done.12.refs_7_), channel_id=1, source_target_pairs={{0,8},{1,9},{2,10},{3,11},{4,12},{5,13},{6,14},{7,15},{8,16},{9,17... | collective-permute-start | bytes 638984 | tf_op jit(solution)/shard_map/ppermute | solution.py:38
  49.7 1.8 %collective-permute-start.15 = (f32[13,64,128]{2,1,0:T(8,128)S(1)}, f32[13,64,128]{2,1,0:T(8,128)S(1)}, u32[]{:S(2)}, u32[]{:S(2)}) collective-permute-start(f32[13,64,128]{2,1,0:T(8,128)S(1)} %far_1_2.1), channel_id=1, source_target_pairs={{0,1},{1,0},{2,3},{3,2},{4,5},{5,4},{6,7},{7,6},{8,9},{9,8},{10,11... | collective-permute-start | bytes 1277960 | tf_op jit(solution)/shard_map/ppermute | solution.py:38

commit v10 on v9

--- a/solution.py
+++ b/solution.py
@@ -103,29 +103,30 @@
 def owner_tables(me, layers, owners, blocks):
     leaves, entries = owners.shape
     slots = layers * 4
-    rows = leaves + 1
-    shape = (rows, 2 * slots)
+    layer, chip, core = me // 8, (me // 2) & 3, me & 1
+
+    back = layer - owners // 8
+    back = jnp.where(back < 0, back + layers, back)
+    turn = jnp.where(back < 2, back, jnp.where(back == layers - 1, 2, back + 1))
+    slot_of = ((owners & 1) ^ core) * slots + turn * 4 + (((owners // 2) & 3) ^ chip)
+
+    shape = (leaves + 1, 2 * slots)
     lane = lax.broadcasted_iota(jnp.int32, shape, 1)
-    plane = (lane >= slots).astype(jnp.int32)
-    slot = lane - plane * slots
-    layer, chip, core = me // 8, (me // 2) & 3, me & 1
-    turn = slot >> 2
-    shift = jnp.where(turn < 2, turn, jnp.where(turn == 2, layers - 1, turn - 1))
-    source = layer - shift
+    pad = jnp.full((1, entries), -1, jnp.int32)
+    named = jnp.concatenate([pad, slot_of], axis=0)
+    chosen = jnp.concatenate([pad, blocks], axis=0)
+    block = jnp.zeros(shape, jnp.int32)
+    for k in range(entries):
+        block = jnp.where(named[:, k:k + 1] == lane, chosen[:, k:k + 1] + 1, block)
+    return slot_of, block
+
+
+def owner_at(me, layers, plane, slot):
+    turn, side = slot // 4, slot % 4
+    shift = (0, 1, layers - 1)[turn] if turn < 3 else turn - 1
+    source = me // 8 - shift
     source = jnp.where(source < 0, source + layers, source)
-    owner = source * 8 + (chip ^ (slot & 3)) * 2 + (core ^ plane)
-    row = lax.broadcasted_iota(jnp.int32, shape, 0)
-    distant = jnp.abs(owner - me) >= 2
-    entry = jnp.where((row == 0) & distant, owner, -1)
-    block = jnp.zeros(shape, jnp.int32)
-    pad = jnp.full((1, entries), -1, jnp.int32)
-    named = jnp.concatenate([pad, owners], axis=0)
-    chosen = jnp.concatenate([pad, blocks], axis=0)
-    for k in range(entries):
-        match = named[:, k:k + 1] == owner
-        entry = jnp.where(match, k, entry)
-        block = jnp.where(match, chosen[:, k:k + 1] + 1, block)
-    return entry, block
+    return source * 8 + (((me // 2) & 3) ^ side) * 2 + ((me & 1) ^ plane)
 
 
 def skeleton_kernel(per, layers, me_ref, order_ref, comp_ref, basis_ref, transfer_ref,
@@ -137,9 +138,9 @@
     @pl.when(step == 0)
     def _():
         root_ref[...] = jnp.zeros_like(root_ref)
-        entry, block = owner_tables(me_ref[0], layers, owner_ref[...], leaf_ref[...])
-        rows, lanes = entry.shape
-        entry_ref[:rows, :lanes] = entry
+        slot_of, block = owner_tables(me_ref[0], layers, owner_ref[...], leaf_ref[...])
+        rows, lanes = block.shape
+        entry_ref[...] = slot_of
         block_ref[:rows, :lanes] = block
 
     hots = [one_hot_leaf(order_ref[pl.ds(step * per + i, 1), :], leaf_len) for i in range(per)]
@@ -201,7 +202,7 @@
             pl.BlockSpec((leaves + 1, rank, fields), lambda s: (0, 0, 0)),
             pl.BlockSpec((leaf_len, fields), lambda s: (0, 0)),
             pl.BlockSpec((leaf_len, fields), lambda s: (0, 0)),
-            pl.BlockSpec((16, 128), lambda s: (0, 0)),
+            pl.BlockSpec((leaves, entries), lambda s: (0, 0)),
             pl.BlockSpec((16, 128), lambda s: (0, 0)),
         ],
         out_shape=[
@@ -209,7 +210,7 @@
             jax.ShapeDtypeStruct((leaves + 1, rank, fields), BF),
             edge,
             edge,
-            jax.ShapeDtypeStruct((16, 128), jnp.int32),
+            jax.ShapeDtypeStruct((leaves, entries), jnp.int32),
             jax.ShapeDtypeStruct((16, 128), jnp.int32),
         ],
         scratch_shapes=[pltpu.VMEM((rank, fields), F32)],
@@ -263,32 +264,42 @@
     )(me, from_x, from_y)
 
 
-def dense_kernel(per, slots, entry_ref, block_ref, inner_ref, coupling_ref, top_ref,
+def dense_kernel(per, layers, me_ref, slot_ref, block_ref, inner_ref, coupling_ref, top_ref,
                  transfer_ref, own_ref, other_ref, turned_ref):
     step = pl.program_id(0)
-    rank = coupling_ref.shape[2]
+    entries, rank = coupling_ref.shape[1:3]
     fields = inner_ref.shape[1]
     leaves = own_ref.shape[0] - 1
+    slots = layers * 4
+    upper = lax.broadcasted_iota(jnp.int32, (rank, 2 * rank), 1) // rank
     for i in range(per):
-        turned_ref[step * per + i] = transfer_ref[i].T
-
-    def fill(out_ref, plane, row, entry_row, block_of):
-        for slot in range(0, slots, 2):
-            pair = []
-            for one in (slot, slot + 1):
-                entry = entry_ref[entry_row, plane * slots + one]
-                block = block_of(jnp.maximum(entry, 0))
-                pair.append(jnp.where(entry >= 0, block, jnp.zeros_like(block)))
-            out_ref[row, :, slot * rank:(slot + 2) * rank] = jnp.concatenate(pair, axis=1)
-
-    for plane, out_ref in ((0, own_ref), (1, other_ref)):
-        for i in range(per):
-            leaf = step * per + i
-            fill(out_ref, plane, leaf, leaf + 1, lambda entry, i=i: coupling_ref[i, entry])
-
-        @pl.when(step == pl.num_programs(0) - 1)
-        def _(plane=plane, out_ref=out_ref):
-            fill(out_ref, plane, leaves, 0, lambda entry: top_ref[0, entry])
+        leaf = step * per + i
+        turned_ref[leaf] = transfer_ref[i].T
+        own_ref[leaf] = jnp.zeros(own_ref.shape[1:], BF)
+        other_ref[leaf] = jnp.zeros(other_ref.shape[1:], BF)
+        for k in range(entries):
+            slot = slot_ref[leaf, k]
+            block = coupling_ref[i, k]
+            both = jnp.concatenate([block, block], axis=1)
+            for plane, out_ref in ((0, own_ref), (1, other_ref)):
+                here = slot - plane * slots
+
+                @pl.when((here >= 0) & (here < slots))
+                def _(here=here, out_ref=out_ref, both=both, leaf=leaf):
+                    at = pl.ds(pl.multiple_of(here // 2 * 2 * rank, 2 * rank), 2 * rank)
+                    out_ref[leaf, :, at] = jnp.where(upper == here % 2, both, out_ref[leaf, :, at])
+
+    @pl.when(step == pl.num_programs(0) - 1)
+    def _():
+        me = me_ref[0]
+        for plane, out_ref in ((0, own_ref), (1, other_ref)):
+            for slot in range(0, slots, 2):
+                pair = []
+                for one in (slot, slot + 1):
+                    owner = owner_at(me, layers, plane, one)
+                    block = top_ref[0, owner]
+                    pair.append(jnp.where(jnp.abs(owner - me) >= 2, block, jnp.zeros_like(block)))
+                out_ref[leaves, :, slot * rank:(slot + 2) * rank] = jnp.concatenate(pair, axis=1)
 
     @pl.when(step == 0)
     def _():
@@ -300,15 +311,17 @@
         other_ref[leaves + 2, :blocks.shape[0], :blocks.shape[1]] = blocks
 
 
-def dense_couplings(entry, block, inner, coupling, top_coupling, transfer, slots, per=4):
+def dense_couplings(me, slot_of, block, inner, coupling, top_coupling, transfer, layers, per=4):
     leaves, entries, rank, _ = coupling.shape
+    slots = layers * 4
     own = (leaves + 1, rank, slots * rank)
     other = (leaves + 3, rank, slots * rank)
     return pl.pallas_call(
-        functools.partial(dense_kernel, per, slots),
+        functools.partial(dense_kernel, per, layers),
         name="couplings_by_owner",
         grid=(leaves // per,),
         in_specs=[
+            scalars(),
             scalars(),
             pl.BlockSpec(block.shape, lambda s: (0, 0)),
             pl.BlockSpec(inner.shape, lambda s: (0, 0)),
@@ -328,7 +341,7 @@
         ],
         compiler_params=params(16 if slots <= 16 else 48),
         cost_estimate=cost(0, 8 * MIB),
-    )(entry, block, inner, *in_hbm(coupling, top_coupling, transfer))
+    )(me, slot_of, block, inner, *in_hbm(coupling, top_coupling, transfer))
 
 
 def round_kernel(plane, steps, slots, counts, at_ref, *refs):
@@ -416,13 +429,15 @@
     )
     near = dot(table_ref[...], jnp.concatenate([left, right], axis=1)).astype(BF)
     fields = ordered_ref.shape[1]
+    turned = []
     for i in range(2):
         hot = one_hot_grid(order_ref[pl.ds(2 * pair + i, 1), :], leaf_len)
         at = pl.ds(i * leaf_len, leaf_len)
         both = jnp.concatenate([near[:, i * fields:(i + 1) * fields], basis_ref[2 * pair + i].T], axis=1)
         moved = dot(hot, both).astype(BF)
         near_ref[at, :] = moved[:, :fields]
-        turned_ref[at, :] = moved[:, fields:]
+        turned.append(moved[:, fields:])
+    turned_ref[...] = jnp.concatenate(turned, axis=1)
 
 
 def near_field(pairs, near_list, leaf_order, tables, basis, ordered, halos=None, filled=None):
@@ -466,11 +481,11 @@
         in_specs=in_specs,
         out_specs=[
             pl.BlockSpec((2 * leaf_len, fields), lambda s: (pair_of(s), 0)),
-            pl.BlockSpec((2 * leaf_len, rank), lambda s: (pair_of(s), 0)),
+            pl.BlockSpec((leaf_len, 2 * rank), lambda s: (pair_of(s), 0)),
         ] + [pl.BlockSpec(shape, lambda s: (0, 0)) for shape in extra],
         out_shape=[
             jax.ShapeDtypeStruct((leaves * leaf_len, fields), BF),
-            jax.ShapeDtypeStruct((leaves * leaf_len, rank), BF),
+            jax.ShapeDtypeStruct((leaves // 2 * leaf_len, 2 * rank), BF),
         ] + [jax.ShapeDtypeStruct(shape, jnp.int32) for shape in extra],
         input_output_aliases=aliases,
         compiler_params=params(16),
@@ -487,13 +502,27 @@
     fine = (local - coarse.astype(F32)).astype(BF)
     both = jnp.concatenate([coarse, fine], axis=1)
     fields = local.shape[1]
-    for i in range(per):
-        leaf = step * per + i
-        down = dot(turned_transfer_ref[leaf], both)
-        value = own_ref[leaf] + other_ref[leaf] + (down[:, :fields] + down[:, fields:])
-        at = pl.ds(pl.multiple_of(leaf * leaf_len, leaf_len), leaf_len)
-        far = dot(turned_ref[at, :], value.astype(BF))
-        out_ref[i * leaf_len:(i + 1) * leaf_len, :] = (near_ref[at, :].astype(F32) + far).astype(BF)
+    for pair in range(per // 2):
+        values = []
+        for i in range(2):
+            leaf = step * per + 2 * pair + i
+            down = dot(turned_transfer_ref[leaf], both)
+            value = own_ref[leaf] + other_ref[leaf] + (down[:, :fields] + down[:, fields:])
+            values.append(value.astype(BF))
+        zero = jnp.zeros_like(values[0])
+        corner = jnp.concatenate(
+            [
+                jnp.concatenate([values[0], zero], axis=1),
+                jnp.concatenate([zero, values[1]], axis=1),
+            ],
+            axis=0,
+        )
+        at = pl.multiple_of((step * (per // 2) + pair) * leaf_len, leaf_len)
+        far = dot(turned_ref[pl.ds(at, leaf_len), :], corner)
+        for i in range(2):
+            near = near_ref[pl.ds(2 * at + i * leaf_len, leaf_len), :].astype(F32)
+            rows = slice((2 * pair + i) * leaf_len, (2 * pair + i + 1) * leaf_len)
+            out_ref[rows, :] = (near + far[:, i * fields:(i + 1) * fields]).astype(BF)
 
 
 def field(own, other, turned_transfer, near, turned, per=4):
@@ -535,7 +564,7 @@
     cut = pairs // 2
     me = lax.axis_index("subtree").reshape(1)
 
-    ordered, shared, cross, inner, entry, own_at = skeletons_of(
+    ordered, shared, cross, inner, slot_of, own_at = skeletons_of(
         me, leaf_order, composition, leaf_basis, transfer, admissible_owner, admissible_leaf, layers
     )
     tables = jnp.asarray(near_tables(leaf_len))
@@ -545,10 +574,10 @@
     from_x, from_y = over_x(shared), over_y(shared)
     filled = near_field(list(range(1, cut)), *near_args, ordered)
     line = after(line, filled[0])
-    lines = [along_z(after(shared, filled[0]), layers - 1)]
+    lines = [along_z(shared, layers - 1)]
     for _ in range(layers - 3):
         lines.append(along_z(line if len(lines) == 1 else lines[-1], 1))
-    ready = after(line, from_x, from_y)
+    ready = after(line, from_x, from_y, lines[0])
     next_x, next_y = over_x(ready), over_y(ready)
     far = onward(choose(me, after(from_x, ready), from_y))
     cross = lax.ppermute(
@@ -557,14 +586,14 @@
         [(d, d + 1) for d in range(1, count - 1, 2)] + [(d, d - 1) for d in range(2, count, 2)],
     )
     own_blocks, my_other, turned_transfer = dense_couplings(
-        after(entry, ready), own_at, inner, coupling, top_coupling, transfer, slots
-    )
-    chosen = choose(me, after(next_x, cross, my_other), next_y)
+        me, after(slot_of, ready), own_at, inner, coupling, top_coupling, transfer, layers
+    )
+
+    joined = after(join([after(lines[0], my_other)] + lines[1:]), next_x, next_y, far, cross)
+    last_x, last_y = over_x(joined), over_y(joined)
+    chosen = choose(me, after(next_x, joined), next_y)
     next_far = onward(chosen)
-
-    joined = join([after(lines[0], chosen, far)] + lines[1:])
-    last_x, last_y = over_x(joined), over_y(joined)
-    other_blocks = over_core(after(my_other, joined))
+    other_blocks = over_core(after(my_other, chosen))
     held = after(ordered, joined)
     filled = near_field(list(range(cut, pairs - 1)), *near_args, held, filled=filled)
     next_far = after(next_far, filled[0])

time: 54.4 us -> 67.9 us (1.25)
  Pallas kernels: 26.6 us -> 40.4 us
  waiting for transfers between devices: 9.53 us -> 5 us
  starting transfers between devices: 17.9 us -> 22 us
    pallas_call x1, Pallas kernels: 3.98 us -> 17.7 us  [dense_couplings(): pl.pallas_call(functools.partial(dense_kernel, per, layers), name='coupli...]
    ppermute x15, waiting for transfers between devices: 9.53 us -> 4.99 us  [send(): lax.ppermute(block, 'subtree', [(d, target(d)) for d in range(count)])]
    ppermute x15, starting transfers between devices: 17.2 us -> 21.4 us  [send(): lax.ppermute(block, 'subtree', [(d, target(d)) for d in range(count)])]
  transfers between devices with their start and end apart: 16 -> 16, of which waited for: 7 -> 3; matrix products, arithmetic and copies ran while one was open for 0% -> 0% of each run, Pallas kernels for 33% -> 47%
where the time goes in v10:
time: 67.9 us; the launch traced here: 67.7 us
  Pallas kernels  40.4 us (59%)
  starting transfers between devices  22 us (32%)
  waiting for transfers between devices  5 us (7%)
    ppermute x15, starting transfers between devices, send(): lax.ppermute(block, 'subtree', [(d, target(d)) for d in range(count)])  21.4 us
    pallas_call x1, Pallas kernels, dense_couplings(): pl.pallas_call(functools.partial(dense_kernel, per, layers), name='coupli...  17.7 us
    pallas_call x3, Pallas kernels, near_field(): pl.pallas_call(functools.partial(near_kernel, halos is not None, pair_of,...  11 us
    ppermute x15, waiting for transfers between devices, send(): lax.ppermute(block, 'subtree', [(d, target(d)) for d in range(count)])  4.99 us
    pallas_call x1, Pallas kernels, skeletons_of(): pl.pallas_call(functools.partial(skeleton_kernel, per, layers), name='ord...  4.84 us
    pallas_call x4, Pallas kernels, far_round(): pl.pallas_call(functools.partial(round_kernel, plane, steps, slots, [len(...  4.34 us
    pallas_call x1, Pallas kernels, field(): pl.pallas_call(functools.partial(field_kernel, per), name='local_and_fiel...  2.47 us
  transfers between devices with their start and end apart: 16, of which 3 were waited for; matrix products, arithmetic and copies ran while one was open for 0% of the time, Pallas kernels for 47%

profile of v10, /device:TPU:0, one launch (start us, length us, event | category | flops | bytes accessed | tf_op | source)
XLA Modules:
  0.0 67.7 jit_solution(10015640273994601091)
XLA Ops:
  0.0 4.8 %order_and_skeleton.1 = (bf16[6144,128]{1,0:T(8,128)(2,1)S(1)}, bf16[13,64,128]{2,1,0:T(8,128)(2,1)S(1)}, bf16[512,128]{1,0:T(8,128)(2,1)S(1)}, bf16[512,128]{1,...) custom-call(s32[1]{0:T(128)} %bitcast.me_ref.refs_0_, s32[12,512]{1,0:T(8,128)} %order_ref.7, ...), custom_call_target="tpu_custom_call" | custom-call | flops 12582912 | bytes 65536 | tf_op jit(solution)/shard_map/order_and_skeleton/pallas_call | solution.py:187
  4.9 3.1 %collective-permute-start.1 = (bf16[13,64,128]{2,1,0:T(8,128)(2,1)S(1)}, bf16[13,64,128]{2,1,0:T(8,128)(2,1)S(1)}, u32[]{:S(2)}, u32[]{:S(2)}) collective-permute-start(bf16[13,64,128]{2,1,0:T(8,128)(2,1)S(1)} %get-tuple-element.34.refs_0_), channel_id=1, source_target_pairs={{0,8},{1,9},{2,10},{3,11},{4,12},{5,13},{6,14},{7,15},{8,16},{9,17... | collective-permute-start | bytes 638984 | tf_op jit(solution)/shard_map/ppermute | solution.py:38
  8.0 1.5 %collective-permute-start.2 = (bf16[13,64,128]{2,1,0:T(8,128)(2,1)S(1)}, bf16[13,64,128]{2,1,0:T(8,128)(2,1)S(1)}, u32[]{:S(2)}, u32[]{:S(2)}) collective-permute-start(bf16[13,64,128]{2,1,0:T(8,128)(2,1)S(1)} %get-tuple-element.34.refs_0_), channel_id=1, source_target_pairs={{0,2},{1,3},{2,0},{3,1},{4,6},{5,7},{6,4},{7,5},{8,10},{9,11},{10,... | collective-permute-start | bytes 638984 | tf_op jit(solution)/shard_map/ppermute | solution.py:38
  9.4 1.5 %collective-permute-start.3 = (bf16[13,64,128]{2,1,0:T(8,128)(2,1)S(1)}, bf16[13,64,128]{2,1,0:T(8,128)(2,1)S(1)}, u32[]{:S(2)}, u32[]{:S(2)}) collective-permute-start(bf16[13,64,128]{2,1,0:T(8,128)(2,1)S(1)} %get-tuple-element.34.refs_0_), channel_id=1, source_target_pairs={{0,4},{1,5},{2,6},{3,7},{4,0},{5,1},{6,2},{7,3},{8,12},{9,13},{10,... | collective-permute-start | bytes 638984 | tf_op jit(solution)/shard_map/ppermute | solution.py:38
  11.0 2.2 %collective-permute-start = (bf16[13,64,128]{2,1,0:T(8,128)(2,1)S(1)}, bf16[13,64,128]{2,1,0:T(8,128)(2,1)S(1)}, u32[]{:S(2)}, u32[]{:S(2)}) collective-permute-start(bf16[13,64,128]{2,1,0:T(8,128)(2,1)S(1)} %get-tuple-element.34.refs_0_), channel_id=1, source_target_pairs={{0,24},{1,25},{2,26},{3,27},{4,28},{5,29},{6,30},{7,31},{8,0},{9,1... | collective-permute-start | bytes 638984 | tf_op jit(solution)/shard_map/ppermute | solution.py:38
  13.2 3.6 %near_1.1 = (bf16[6144,128]{1,0:T(8,128)(2,1)S(1)}, bf16[3072,128]{1,0:T(8,128)(2,1)S(1)}) custom-call(s32[2,12]{1,0:T(2,128)S(1)} %bitcast.2, s32[12,512]{1,0:T(8,128)S(1)} %copy-done.2, bf16[512,1536]{1,0:T(8,128)(2,1)S(1)} %copy-done, bf16[12,64,512]{2,1,0:T(8,128)(2,1)S(1)} %copy-done.1, bf16[6144,128]{1,0:T(8,128)(2,1)S(1)} %get-tuple-element.53.ordered_ref), custom_call_target="tpu_custom_call" | custom-call | flops 20971520 | bytes 32768 | tf_op jit(solution)/shard_map/near_1/pallas_call | solution.py:477
  16.9 2.9 %collective-permute-done.refs_0_ = bf16[13,64,128]{2,1,0:T(8,128)(2,1)S(1)} collective-permute-done((bf16[13,64,128]{2,1,0:T(8,128)(2,1)S(1)}, bf16[13,64,128]{2,1,0:T(8,128)(2,1)S(1)}, u32[]{:S(2)}, u32[]{:S(2)}) %collective-permute-start) | collective-permute-done | bytes 213024 | tf_op jit(solution)/shard_map/ppermute | solution.py:38
  19.9 2.2 %collective-permute-start.7 = (bf16[13,64,128]{2,1,0:T(8,128)(2,1)S(1)}, bf16[13,64,128]{2,1,0:T(8,128)(2,1)S(1)}, u32[]{:S(2)}, u32[]{:S(2)}) collective-permute-start(bf16[13,64,128]{2,1,0:T(8,128)(2,1)S(1)} %choose.2), channel_id=1, source_target_pairs={{0,4},{1,3},{2,6},{3,1},{4,0},{5,7},{6,2},{7,5},{8,12},{9,11},{10,... | collective-permute-start | bytes 638984 | tf_op jit(solution)/shard_map/ppermute | solution.py:38
  22.1 1.7 %collective-permute-start.5 = (bf16[13,64,128]{2,1,0:T(8,128)(2,1)S(1)}, bf16[13,64,128]{2,1,0:T(8,128)(2,1)S(1)}, u32[]{:S(2)}, u32[]{:S(2)}) collective-permute-start(bf16[13,64,128]{2,1,0:T(8,128)(2,1)S(1)} %collective-permute-done.1.refs_1_), channel_id=1, source_target_pairs={{0,2},{1,3},{2,0},{3,1},{4,6},{5,7},{6,4},{7,5},{8,10},{9,11},{10,... | collective-permute-start | bytes 638984 | tf_op jit(solution)/shard_map/ppermute | solution.py:38
  24.0 0.7 collective-permute-start.8
  24.7 17.7 %couplings_by_owner.1 = (bf16[13,64,1024]{2,1,0:T(8,128)(2,1)S(1)}, bf16[15,64,1024]{2,1,0:T(8,128)(2,1)S(1)}, bf16[12,64,64]{2,1,0:T(8,128)(2,1)S(1)}) custom-call(s32[1]{0:T(128)} %bitcast.me_ref.refs_0_, s32[12,16]{1,0:T(8,128)S(1)} %get-tuple-element.40.slot_ref, s32[16,128]{1,0:T(8,128)S(1)} %get-tuple-element.33.block_ref.at_ref, ...), custom_call_target="tpu_custom_call" | custom-call | bytes 131072 | tf_op jit(solution)/shard_map/couplings_by_owner/pallas_call | solution.py:319
  42.5 1.6 %collective-permute-start.13 = (bf16[15,64,1024]{2,1,0:T(8,128)(2,1)S(1)}, bf16[15,64,1024]{2,1,0:T(8,128)(2,1)S(1)}, u32[]{:S(2)}, u32[]{:S(2)}) collective-permute-start(bf16[15,64,1024]{2,1,0:T(8,128)(2,1)S(1)} %get-tuple-element.54), channel_id=1, source_target_pairs={{0,1},{1,0},{2,3},{3,2},{4,5},{5,4},{6,7},{7,6},{8,9},{9,8},{10,11... | collective-permute-start | bytes 5898248 | tf_op jit(solution)/shard_map/ppermute | solution.py:38
  44.0 2.0 %collective-permute-start.12 = (bf16[13,64,128]{2,1,0:T(8,128)(2,1)S(1)}, bf16[13,64,128]{2,1,0:T(8,128)(2,1)S(1)}, u32[]{:S(2)}, u32[]{:S(2)}) collective-permute-start(bf16[13,64,128]{2,1,0:T(8,128)(2,1)S(1)} %choose.3), channel_id=1, source_target_pairs={{0,4},{1,3},{2,6},{3,1},{4,0},{5,7},{6,2},{7,5},{8,12},{9,11},{10,... | collective-permute-start | bytes 638984 | tf_op jit(solution)/shard_map/ppermute | solution.py:38
  46.1 3.1 %collective-permute-start.9 = (bf16[26,64,128]{2,1,0:T(8,128)(2,1)S(1)}, bf16[26,64,128]{2,1,0:T(8,128)(2,1)S(1)}, u32[]{:S(2)}, u32[]{:S(2)}) collective-permute-start(bf16[26,64,128]{2,1,0:T(8,128)(2,1)S(1)} %join.1.refs_0_), channel_id=1, source_target_pairs={{0,2},{1,3},{2,0},{3,1},{4,6},{5,7},{6,4},{7,5},{8,10},{9,11},{10,... | collective-permute-start | bytes 1277960 | tf_op jit(solution)/shard_map/ppermute | solution.py:38
  49.2 1.8 %collective-permute-start.11 = (bf16[13,64,128]{2,1,0:T(8,128)(2,1)S(1)}, bf16[13,64,128]{2,1,0:T(8,128)(2,1)S(1)}, u32[]{:S(2)}, u32[]{:S(2)}) collective-permute-start(bf16[13,64,128]{2,1,0:T(8,128)(2,1)S(1)} %collective-permute-done.7.refs_6_), channel_id=1, source_target_pairs={{0,24},{1,25},{2,26},{3,27},{4,28},{5,29},{6,30},{7,31},{8,0},{9,1... | collective-permute-start | bytes 638984 | tf_op jit(solution)/shard_map/ppermute | solution.py:38
  51.0 3.6 %near_3.1 = (bf16[6144,128]{1,0:T(8,128)(2,1)S(1)}, bf16[3072,128]{1,0:T(8,128)(2,1)S(1)}) custom-call(s32[2,12]{1,0:T(2,128)S(1)} %bitcast.3, s32[12,512]{1,0:T(8,128)S(1)} %copy-done.2, bf16[512,1536]{1,0:T(8,128)(2,1)S(1)} %copy-done, bf16[12,64,512]{2,1,0:T(8,128)(2,1)S(1)} %copy-done.1, ...), custom_call_target="tpu_custom_call", output_to_operand_aliasing={{0}: (5, {}), {1}: (6, {})} | custom-call | flops 20971520 | bytes 32768 | tf_op jit(solution)/shard_map/near_3/pallas_call | solution.py:477
  54.8 1.1 %far_0_0.1.refs_6_ = f32[13,64,128]{2,1,0:T(8,128)S(1)} custom-call(s32[16,128]{1,0:T(8,128)S(1)} %get-tuple-element.33.block_ref.at_ref, bf16[13,64,128]{2,1,0:T(8,128)(2,1)S(1)} %get-tuple-element.34.refs_0_, bf16[13,64,128]{2,1,0:T(8,128)(2,1)S(1)} %collective-permute-done.1.refs_1_, bf16[13,64,128]{2,1,0:T(8,128)(2,1)S(1)} %collective-permute-done.2.x_ref.refs_2_, ...), custom_call_target="tpu_custom_call" | custom-call | flops 1703936 | bytes 16384 | tf_op jit(solution)/shard_map/far_0_0/pallas_call | solution.py:378
  55.9 3.9 %near_0.1 = (bf16[6144,128]{1,0:T(8,128)(2,1)S(1)}, bf16[3072,128]{1,0:T(8,128)(2,1)S(1)}, s32[16,128]{1,0:T(8,128)S(1)}) custom-call(s32[2,12]{1,0:T(2,128)S(1)} %bitcast.4, s32[12,512]{1,0:T(8,128)S(1)} %copy-done.2, bf16[512,1536]{1,0:T(8,128)(2,1)S(1)} %copy-done, ...), custom_call_target="tpu_custom_call", output_to_operand_aliasing={{0}: (9, {}), {1}: (10, {})} | custom-call | flops 20971520 | bytes 32768 | tf_op jit(solution)/shard_map/near_0/pallas_call | solution.py:477
  59.8 1.1 %far_1_0.1.refs_6_ = f32[13,64,128]{2,1,0:T(8,128)S(1)} custom-call(s32[16,128]{1,0:T(8,128)S(1)} %get-tuple-element.56.at_ref, bf16[13,64,128]{2,1,0:T(8,128)(2,1)S(1)} %get-tuple-element.34.refs_0_, bf16[13,64,128]{2,1,0:T(8,128)(2,1)S(1)} %collective-permute-done.1.refs_1_, bf16[13,64,128]{2,1,0:T(8,128)(2,1)S(1)} %collective-permute-done.2.x_ref.refs_2_, ...), custom_call_target="tpu_custom_call" | custom-call | flops 1703936 | bytes 16384 | tf_op jit(solution)/shard_map/far_1_0/pallas_call | solution.py:378
  60.9 1.4 %collective-permute-done.14.refs_4_ = bf16[13,64,128]{2,1,0:T(8,128)(2,1)S(1)} collective-permute-done((bf16[13,64,128]{2,1,0:T(8,128)(2,1)S(1)}, bf16[13,64,128]{2,1,0:T(8,128)(2,1)S(1)}, u32[]{:S(2)}, u32[]{:S(2)}) %collective-permute-start.14) | collective-permute-done | bytes 213024 | tf_op jit(solution)/shard_map/ppermute | solution.py:38
  62.3 1.1 %far_1_2.1 = f32[13,64,128]{2,1,0:T(8,128)S(1)} custom-call(s32[16,128]{1,0:T(8,128)S(1)} %get-tuple-element.56.at_ref, bf16[26,64,128]{2,1,0:T(8,128)(2,1)S(1)} %join.1.refs_0_, bf16[26,64,128]{2,1,0:T(8,128)(2,1)S(1)} %collective-permute-done.9.refs_1_, bf16[26,64,128]{2,1,0:T(8,128)(2,1)S(1)} %collective-permute-done.10.refs_2_, ...), custom_call_target="tpu_custom_call" | custom-call | flops 1703936 | bytes 16384 | tf_op jit(solution)/shard_map/far_1_2/pallas_call | solution.py:378
  63.5 1.1 %far_0_2.1.own_ref = f32[13,64,128]{2,1,0:T(8,128)S(1)} custom-call(s32[16,128]{1,0:T(8,128)S(1)} %get-tuple-element.33.block_ref.at_ref, bf16[26,64,128]{2,1,0:T(8,128)(2,1)S(1)} %join.1.refs_0_, bf16[26,64,128]{2,1,0:T(8,128)(2,1)S(1)} %collective-permute-done.9.refs_1_, bf16[26,64,128]{2,1,0:T(8,128)(2,1)S(1)} %collective-permute-done.10.refs_2_, ...), custom_call_target="tpu_custom_call" | custom-call | flops 1703936 | bytes 16384 | tf_op jit(solution)/shard_map/far_0_2/pallas_call | solution.py:378
  64.6 0.7 collective-permute-done.15.other_ref
  65.2 2.5 %local_and_field.1 = bf16[6144,128]{1,0:T(8,128)(2,1)} custom-call(f32[13,64,128]{2,1,0:T(8,128)S(1)} %far_0_2.1.own_ref, f32[13,64,128]{2,1,0:T(8,128)S(1)} %collective-permute-done.15.other_ref, bf16[12,64,64]{2,1,0:T(8,128)(2,1)S(1)} %get-tuple-element.58.turned_transfer_ref, bf16[6144,128]{1,0:T(8,128)(2,1)S(1)} %get-tuple-element.59.near_ref, ...), custom_call_target="tpu_custom_call" | custom-call | flops 1572864 | bytes 65536 | tf_op jit(solution)/shard_map/local_and_field/pallas_call | solution.py:532
  (29 shorter events, 0.8 us)
Async XLA Ops:
  0.0 13.2 %copy-start = (bf16[512,1536]{1,0:T(8,128)(2,1)S(1)}, bf16[512,1536]{1,0:T(8,128)(2,1)}, u32[]{:S(2)}) copy-start(bf16[512,1536]{1,0:T(8,128)(2,1)} %constant.6.clone.table_ref) | copy-start | bytes 4718596
  0.0 13.2 %copy-start.1 = (bf16[12,64,512]{2,1,0:T(8,128)(2,1)S(1)}, bf16[12,64,512]{2,1,0:T(8,128)(2,1)}, u32[]{:S(2)}) copy-start(bf16[12,64,512]{2,1,0:T(8,128)(2,1)} %basis_ref.7) | copy-start | bytes 2359300
  0.0 13.2 %copy-start.2 = (s32[12,512]{1,0:T(8,128)S(1)}, s32[12,512]{1,0:T(8,128)}, u32[]{:S(2)}) copy-start(s32[12,512]{1,0:T(8,128)} %order_ref.7) | copy-start | bytes 73732
  0.0 13.2 %copy-start.3 = (s32[12,2]{0,1:T(2,128)S(1)}, s32[12,2]{0,1:T(2,128)}, u32[]{:S(2)}) copy-start(s32[12,2]{0,1:T(2,128)} %param.17) | copy-start | bytes 292
  4.9 12.0 %collective-permute-start.1 = (bf16[13,64,128]{2,1,0:T(8,128)(2,1)S(1)}, bf16[13,64,128]{2,1,0:T(8,128)(2,1)S(1)}, u32[]{:S(2)}, u32[]{:S(2)}) collective-permute-start(bf16[13,64,128]{2,1,0:T(8,128)(2,1)S(1)} %get-tuple-element.34.refs_0_), channel_id=1, source_target_pairs={{0,8},{1,9},{2,10},{3,11},{4,12},{5,13},{6,14},{7,15},{8,16},{9,17... | collective-permute-start | bytes 638984 | tf_op jit(solution)/shard_map/ppermute | solution.py:38
  8.0 8.9 %collective-permute-start.2 = (bf16[13,64,128]{2,1,0:T(8,128)(2,1)S(1)}, bf16[13,64,128]{2,1,0:T(8,128)(2,1)S(1)}, u32[]{:S(2)}, u32[]{:S(2)}) collective-permute-start(bf16[13,64,128]{2,1,0:T(8,128)(2,1)S(1)} %get-tuple-element.34.refs_0_), channel_id=1, source_target_pairs={{0,2},{1,3},{2,0},{3,1},{4,6},{5,7},{6,4},{7,5},{8,10},{9,11},{10,... | collective-permute-start | bytes 638984 | tf_op jit(solution)/shard_map/ppermute | solution.py:38
  9.4 7.5 %collective-permute-start.3 = (bf16[13,64,128]{2,1,0:T(8,128)(2,1)S(1)}, bf16[13,64,128]{2,1,0:T(8,128)(2,1)S(1)}, u32[]{:S(2)}, u32[]{:S(2)}) collective-permute-start(bf16[13,64,128]{2,1,0:T(8,128)(2,1)S(1)} %get-tuple-element.34.refs_0_), channel_id=1, source_target_pairs={{0,4},{1,5},{2,6},{3,7},{4,0},{5,1},{6,2},{7,3},{8,12},{9,13},{10,... | collective-permute-start | bytes 638984 | tf_op jit(solution)/shard_map/ppermute | solution.py:38
  11.0 8.9 %collective-permute-start = (bf16[13,64,128]{2,1,0:T(8,128)(2,1)S(1)}, bf16[13,64,128]{2,1,0:T(8,128)(2,1)S(1)}, u32[]{:S(2)}, u32[]{:S(2)}) collective-permute-start(bf16[13,64,128]{2,1,0:T(8,128)(2,1)S(1)} %get-tuple-element.34.refs_0_), channel_id=1, source_target_pairs={{0,24},{1,25},{2,26},{3,27},{4,28},{5,29},{6,30},{7,31},{8,0},{9,1... | collective-permute-start | bytes 638984 | tf_op jit(solution)/shard_map/ppermute | solution.py:38
  16.8 25.5 %collective-permute-start.4 = (bf16[13,64,128]{2,1,0:T(8,128)(2,1)S(1)}, bf16[13,64,128]{2,1,0:T(8,128)(2,1)S(1)}, u32[]{:S(2)}, u32[]{:S(2)}) collective-permute-start(bf16[13,64,128]{2,1,0:T(8,128)(2,1)S(1)} %collective-permute-done.1.refs_1_), channel_id=1, source_target_pairs={{0,8},{1,9},{2,10},{3,11},{4,12},{5,13},{6,14},{7,15},{8,16},{9,17... | collective-permute-start | bytes 638984 | tf_op jit(solution)/shard_map/ppermute | solution.py:38
  19.9 22.5 %collective-permute-start.7 = (bf16[13,64,128]{2,1,0:T(8,128)(2,1)S(1)}, bf16[13,64,128]{2,1,0:T(8,128)(2,1)S(1)}, u32[]{:S(2)}, u32[]{:S(2)}) collective-permute-start(bf16[13,64,128]{2,1,0:T(8,128)(2,1)S(1)} %choose.2), channel_id=1, source_target_pairs={{0,4},{1,3},{2,6},{3,1},{4,0},{5,7},{6,2},{7,5},{8,12},{9,11},{10,... | collective-permute-start | bytes 638984 | tf_op jit(solution)/shard_map/ppermute | solution.py:38
  22.1 20.3 %collective-permute-start.5 = (bf16[13,64,128]{2,1,0:T(8,128)(2,1)S(1)}, bf16[13,64,128]{2,1,0:T(8,128)(2,1)S(1)}, u32[]{:S(2)}, u32[]{:S(2)}) collective-permute-start(bf16[13,64,128]{2,1,0:T(8,128)(2,1)S(1)} %collective-permute-done.1.refs_1_), channel_id=1, source_target_pairs={{0,2},{1,3},{2,0},{3,1},{4,6},{5,7},{6,4},{7,5},{8,10},{9,11},{10,... | collective-permute-start | bytes 638984 | tf_op jit(solution)/shard_map/ppermute | solution.py:38
  23.8 18.7 %collective-permute-start.6 = (bf16[13,64,128]{2,1,0:T(8,128)(2,1)S(1)}, bf16[13,64,128]{2,1,0:T(8,128)(2,1)S(1)}, u32[]{:S(2)}, u32[]{:S(2)}) collective-permute-start(bf16[13,64,128]{2,1,0:T(8,128)(2,1)S(1)} %collective-permute-done.1.refs_1_), channel_id=1, source_target_pairs={{0,4},{1,5},{2,6},{3,7},{4,0},{5,1},{6,2},{7,3},{8,12},{9,13},{10,... | collective-permute-start | bytes 638984 | tf_op jit(solution)/shard_map/ppermute | solution.py:38
  24.0 18.4 %collective-permute-start.8 = (bf16[512,128]{1,0:T(8,128)(2,1)S(1)}, bf16[512,128]{1,0:T(8,128)(2,1)S(1)}, u32[]{:S(2)}, u32[]{:S(2)}) collective-permute-start(bf16[512,128]{1,0:T(8,128)(2,1)S(1)} %get-tuple-element.45), channel_id=1, source_target_pairs={{1,2},{3,4},{5,6},{7,8},{9,10},{11,12},{13,14},{15,16},{17,18},{19... | collective-permute-start | bytes 393224 | tf_op jit(solution)/shard_map/ppermute | solution.py:583
  42.5 13.4 %collective-permute-start.13 = (bf16[15,64,1024]{2,1,0:T(8,128)(2,1)S(1)}, bf16[15,64,1024]{2,1,0:T(8,128)(2,1)S(1)}, u32[]{:S(2)}, u32[]{:S(2)}) collective-permute-start(bf16[15,64,1024]{2,1,0:T(8,128)(2,1)S(1)} %get-tuple-element.54), channel_id=1, source_target_pairs={{0,1},{1,0},{2,3},{3,2},{4,5},{5,4},{6,7},{7,6},{8,9},{9,8},{10,11... | collective-permute-start | bytes 5898248 | tf_op jit(solution)/shard_map/ppermute | solution.py:38
  44.0 10.5 %collective-permute-start.12 = (bf16[13,64,128]{2,1,0:T(8,128)(2,1)S(1)}, bf16[13,64,128]{2,1,0:T(8,128)(2,1)S(1)}, u32[]{:S(2)}, u32[]{:S(2)}) collective-permute-start(bf16[13,64,128]{2,1,0:T(8,128)(2,1)S(1)} %choose.3), channel_id=1, source_target_pairs={{0,4},{1,3},{2,6},{3,1},{4,0},{5,7},{6,2},{7,5},{8,12},{9,11},{10,... | collective-permute-start | bytes 638984 | tf_op jit(solution)/shard_map/ppermute | solution.py:38
  46.0 16.3 %collective-permute-start.10 = (bf16[26,64,128]{2,1,0:T(8,128)(2,1)S(1)}, bf16[26,64,128]{2,1,0:T(8,128)(2,1)S(1)}, u32[]{:S(2)}, u32[]{:S(2)}) collective-permute-start(bf16[26,64,128]{2,1,0:T(8,128)(2,1)S(1)} %join.1.refs_0_), channel_id=1, source_target_pairs={{0,4},{1,5},{2,6},{3,7},{4,0},{5,1},{6,2},{7,3},{8,12},{9,13},{10,... | collective-permute-start | bytes 1277960 | tf_op jit(solution)/shard_map/ppermute | solution.py:38
  46.1 16.2 %collective-permute-start.9 = (bf16[26,64,128]{2,1,0:T(8,128)(2,1)S(1)}, bf16[26,64,128]{2,1,0:T(8,128)(2,1)S(1)}, u32[]{:S(2)}, u32[]{:S(2)}) collective-permute-start(bf16[26,64,128]{2,1,0:T(8,128)(2,1)S(1)} %join.1.refs_0_), channel_id=1, source_target_pairs={{0,2},{1,3},{2,0},{3,1},{4,6},{5,7},{6,4},{7,5},{8,10},{9,11},{10,... | collective-permute-start | bytes 1277960 | tf_op jit(solution)/shard_map/ppermute | solution.py:38
  49.2 11.7 %collective-permute-start.11 = (bf16[13,64,128]{2,1,0:T(8,128)(2,1)S(1)}, bf16[13,64,128]{2,1,0:T(8,128)(2,1)S(1)}, u32[]{:S(2)}, u32[]{:S(2)}) collective-permute-start(bf16[13,64,128]{2,1,0:T(8,128)(2,1)S(1)} %collective-permute-done.7.refs_6_), channel_id=1, source_target_pairs={{0,24},{1,25},{2,26},{3,27},{4,28},{5,29},{6,30},{7,31},{8,0},{9,1... | collective-permute-start | bytes 638984 | tf_op jit(solution)/shard_map/ppermute | solution.py:38
  54.6 7.7 %collective-permute-start.14 = (bf16[13,64,128]{2,1,0:T(8,128)(2,1)S(1)}, bf16[13,64,128]{2,1,0:T(8,128)(2,1)S(1)}, u32[]{:S(2)}, u32[]{:S(2)}) collective-permute-start(bf16[13,64,128]{2,1,0:T(8,128)(2,1)S(1)} %collective-permute-done.12.refs_7_), channel_id=1, source_target_pairs={{0,8},{1,9},{2,10},{3,11},{4,12},{5,13},{6,14},{7,15},{8,16},{9,17... | collective-permute-start | bytes 638984 | tf_op jit(solution)/shard_map/ppermute | solution.py:38
  63.4 1.8 %collective-permute-start.15 = (f32[13,64,128]{2,1,0:T(8,128)S(1)}, f32[13,64,128]{2,1,0:T(8,128)S(1)}, u32[]{:S(2)}, u32[]{:S(2)}) collective-permute-start(f32[13,64,128]{2,1,0:T(8,128)S(1)} %far_1_2.1), channel_id=1, source_target_pairs={{0,1},{1,0},{2,3},{3,2},{4,5},{5,4},{6,7},{7,6},{8,9},{9,8},{10,11... | collective-permute-start | bytes 1277960 | tf_op jit(solution)/shard_map/ppermute | solution.py:38

commit v11 on v9

--- a/solution.py
+++ b/solution.py
@@ -416,13 +416,15 @@
     )
     near = dot(table_ref[...], jnp.concatenate([left, right], axis=1)).astype(BF)
     fields = ordered_ref.shape[1]
+    turned = []
     for i in range(2):
         hot = one_hot_grid(order_ref[pl.ds(2 * pair + i, 1), :], leaf_len)
         at = pl.ds(i * leaf_len, leaf_len)
         both = jnp.concatenate([near[:, i * fields:(i + 1) * fields], basis_ref[2 * pair + i].T], axis=1)
         moved = dot(hot, both).astype(BF)
         near_ref[at, :] = moved[:, :fields]
-        turned_ref[at, :] = moved[:, fields:]
+        turned.append(moved[:, fields:])
+    turned_ref[...] = jnp.concatenate(turned, axis=1)
 
 
 def near_field(pairs, near_list, leaf_order, tables, basis, ordered, halos=None, filled=None):
@@ -466,11 +468,11 @@
         in_specs=in_specs,
         out_specs=[
             pl.BlockSpec((2 * leaf_len, fields), lambda s: (pair_of(s), 0)),
-            pl.BlockSpec((2 * leaf_len, rank), lambda s: (pair_of(s), 0)),
+            pl.BlockSpec((leaf_len, 2 * rank), lambda s: (pair_of(s), 0)),
         ] + [pl.BlockSpec(shape, lambda s: (0, 0)) for shape in extra],
         out_shape=[
             jax.ShapeDtypeStruct((leaves * leaf_len, fields), BF),
-            jax.ShapeDtypeStruct((leaves * leaf_len, rank), BF),
+            jax.ShapeDtypeStruct((leaves // 2 * leaf_len, 2 * rank), BF),
         ] + [jax.ShapeDtypeStruct(shape, jnp.int32) for shape in extra],
         input_output_aliases=aliases,
         compiler_params=params(16),
@@ -487,13 +489,27 @@
     fine = (local - coarse.astype(F32)).astype(BF)
     both = jnp.concatenate([coarse, fine], axis=1)
     fields = local.shape[1]
-    for i in range(per):
-        leaf = step * per + i
-        down = dot(turned_transfer_ref[leaf], both)
-        value = own_ref[leaf] + other_ref[leaf] + (down[:, :fields] + down[:, fields:])
-        at = pl.ds(pl.multiple_of(leaf * leaf_len, leaf_len), leaf_len)
-        far = dot(turned_ref[at, :], value.astype(BF))
-        out_ref[i * leaf_len:(i + 1) * leaf_len, :] = (near_ref[at, :].astype(F32) + far).astype(BF)
+    for pair in range(per // 2):
+        values = []
+        for i in range(2):
+            leaf = step * per + 2 * pair + i
+            down = dot(turned_transfer_ref[leaf], both)
+            value = own_ref[leaf] + other_ref[leaf] + (down[:, :fields] + down[:, fields:])
+            values.append(value.astype(BF))
+        zero = jnp.zeros_like(values[0])
+        corner = jnp.concatenate(
+            [
+                jnp.concatenate([values[0], zero], axis=1),
+                jnp.concatenate([zero, values[1]], axis=1),
+            ],
+            axis=0,
+        )
+        at = pl.multiple_of((step * (per // 2) + pair) * leaf_len, leaf_len)
+        far = dot(turned_ref[pl.ds(at, leaf_len), :], corner)
+        for i in range(2):
+            near = near_ref[pl.ds(2 * at + i * leaf_len, leaf_len), :].astype(F32)
+            rows = slice((2 * pair + i) * leaf_len, (2 * pair + i + 1) * leaf_len)
+            out_ref[rows, :] = (near + far[:, i * fields:(i + 1) * fields]).astype(BF)
 
 
 def field(own, other, turned_transfer, near, turned, per=4):
@@ -545,12 +561,12 @@
     from_x, from_y = over_x(shared), over_y(shared)
     filled = near_field(list(range(1, cut)), *near_args, ordered)
     line = after(line, filled[0])
-    lines = [along_z(after(shared, filled[0]), layers - 1)]
+    lines = [along_z(shared, layers - 1)]
     for _ in range(layers - 3):
         lines.append(along_z(line if len(lines) == 1 else lines[-1], 1))
     ready = after(line, from_x, from_y)
     next_x, next_y = over_x(ready), over_y(ready)
-    far = onward(choose(me, after(from_x, ready), from_y))
+    far = onward(choose(me, after(from_x, ready, lines[0]), from_y))
     cross = lax.ppermute(
         cross,
         "subtree",
@@ -559,12 +575,12 @@
     own_blocks, my_other, turned_transfer = dense_couplings(
         after(entry, ready), own_at, inner, coupling, top_coupling, transfer, slots
     )
-    chosen = choose(me, after(next_x, cross, my_other), next_y)
+
+    joined = after(join([after(lines[0], my_other)] + lines[1:]), next_x, next_y, cross)
+    last_x, last_y = over_x(joined), over_y(joined)
+    chosen = choose(me, after(next_x, joined, far), next_y)
     next_far = onward(chosen)
-
-    joined = join([after(lines[0], chosen, far)] + lines[1:])
-    last_x, last_y = over_x(joined), over_y(joined)
-    other_blocks = over_core(after(my_other, joined))
+    other_blocks = over_core(after(my_other, chosen))
     held = after(ordered, joined)
     filled = near_field(list(range(cut, pairs - 1)), *near_args, held, filled=filled)
     next_far = after(next_far, filled[0])

time: 54.4 us -> 53 us (0.974)
  waiting for transfers between devices: 9.53 us -> 2.96 us
  starting transfers between devices: 17.9 us -> 22.9 us
    ppermute x15, waiting for transfers between devices: 9.53 us -> 2.96 us  [send(): lax.ppermute(block, 'subtree', [(d, target(d)) for d in range(count)])]
    ppermute x15, starting transfers between devices: 17.2 us -> 22.2 us  [send(): lax.ppermute(block, 'subtree', [(d, target(d)) for d in range(count)])]
  transfers between devices with their start and end apart: 16 -> 16, of which waited for: 7 -> 3; matrix products, arithmetic and copies ran while one was open for 0% -> 0% of each run, Pallas kernels for 33% -> 35%
where the time goes in v11:
time: 53 us; the launch traced here: 52.8 us
  Pallas kernels  26.7 us (50%)
  starting transfers between devices  22.9 us (43%)
  waiting for transfers between devices  2.96 us (6%)
    ppermute x15, starting transfers between devices, send(): lax.ppermute(block, 'subtree', [(d, target(d)) for d in range(count)])  22.2 us
    pallas_call x3, Pallas kernels, near_field(): pl.pallas_call(functools.partial(near_kernel, halos is not None, pair_of,...  11 us
    pallas_call x1, Pallas kernels, skeletons_of(): pl.pallas_call(functools.partial(skeleton_kernel, per, layers), name='ord...  4.83 us
    pallas_call x4, Pallas kernels, far_round(): pl.pallas_call(functools.partial(round_kernel, plane, steps, slots, [len(...  4.34 us
    pallas_call x1, Pallas kernels, dense_couplings(): pl.pallas_call(functools.partial(dense_kernel, per, slots), name='couplin...  3.99 us
    ppermute x15, waiting for transfers between devices, send(): lax.ppermute(block, 'subtree', [(d, target(d)) for d in range(count)])  2.96 us
    pallas_call x1, Pallas kernels, field(): pl.pallas_call(functools.partial(field_kernel, per), name='local_and_fiel...  2.47 us
  transfers between devices with their start and end apart: 16, of which 3 were waited for; matrix products, arithmetic and copies ran while one was open for 0% of the time, Pallas kernels for 35%

profile of v11, /device:TPU:0, one launch (start us, length us, event | category | flops | bytes accessed | tf_op | source)
XLA Modules:
  0.0 52.8 jit_solution(15835037098939558175)
XLA Ops:
  0.0 4.8 %order_and_skeleton.1 = (bf16[6144,128]{1,0:T(8,128)(2,1)S(1)}, bf16[13,64,128]{2,1,0:T(8,128)(2,1)S(1)}, bf16[512,128]{1,0:T(8,128)(2,1)S(1)}, bf16[512,128]{1,...) custom-call(s32[1]{0:T(128)} %bitcast.me_ref.refs_0_, s32[12,512]{1,0:T(8,128)} %order_ref.7, ...), custom_call_target="tpu_custom_call" | custom-call | flops 12582912 | bytes 65536 | tf_op jit(solution)/shard_map/order_and_skeleton/pallas_call | solution.py:186
  4.8 3.1 %collective-permute-start.1 = (bf16[13,64,128]{2,1,0:T(8,128)(2,1)S(1)}, bf16[13,64,128]{2,1,0:T(8,128)(2,1)S(1)}, u32[]{:S(2)}, u32[]{:S(2)}) collective-permute-start(bf16[13,64,128]{2,1,0:T(8,128)(2,1)S(1)} %get-tuple-element.34.refs_0_), channel_id=1, source_target_pairs={{0,8},{1,9},{2,10},{3,11},{4,12},{5,13},{6,14},{7,15},{8,16},{9,17... | collective-permute-start | bytes 638984 | tf_op jit(solution)/shard_map/ppermute | solution.py:38
  7.9 1.5 %collective-permute-start.2 = (bf16[13,64,128]{2,1,0:T(8,128)(2,1)S(1)}, bf16[13,64,128]{2,1,0:T(8,128)(2,1)S(1)}, u32[]{:S(2)}, u32[]{:S(2)}) collective-permute-start(bf16[13,64,128]{2,1,0:T(8,128)(2,1)S(1)} %get-tuple-element.34.refs_0_), channel_id=1, source_target_pairs={{0,2},{1,3},{2,0},{3,1},{4,6},{5,7},{6,4},{7,5},{8,10},{9,11},{10,... | collective-permute-start | bytes 638984 | tf_op jit(solution)/shard_map/ppermute | solution.py:38
  9.4 1.5 %collective-permute-start.3 = (bf16[13,64,128]{2,1,0:T(8,128)(2,1)S(1)}, bf16[13,64,128]{2,1,0:T(8,128)(2,1)S(1)}, u32[]{:S(2)}, u32[]{:S(2)}) collective-permute-start(bf16[13,64,128]{2,1,0:T(8,128)(2,1)S(1)} %get-tuple-element.34.refs_0_), channel_id=1, source_target_pairs={{0,4},{1,5},{2,6},{3,7},{4,0},{5,1},{6,2},{7,3},{8,12},{9,13},{10,... | collective-permute-start | bytes 638984 | tf_op jit(solution)/shard_map/ppermute | solution.py:38
  11.0 2.3 %collective-permute-start = (bf16[13,64,128]{2,1,0:T(8,128)(2,1)S(1)}, bf16[13,64,128]{2,1,0:T(8,128)(2,1)S(1)}, u32[]{:S(2)}, u32[]{:S(2)}) collective-permute-start(bf16[13,64,128]{2,1,0:T(8,128)(2,1)S(1)} %get-tuple-element.34.refs_0_), channel_id=1, source_target_pairs={{0,24},{1,25},{2,26},{3,27},{4,28},{5,29},{6,30},{7,31},{8,0},{9,1... | collective-permute-start | bytes 638984 | tf_op jit(solution)/shard_map/ppermute | solution.py:38
  13.2 3.6 %near_1.1 = (bf16[6144,128]{1,0:T(8,128)(2,1)S(1)}, bf16[3072,128]{1,0:T(8,128)(2,1)S(1)}) custom-call(s32[2,12]{1,0:T(2,128)S(1)} %bitcast.2, s32[12,512]{1,0:T(8,128)S(1)} %copy-done.2, bf16[512,1536]{1,0:T(8,128)(2,1)S(1)} %copy-done, bf16[12,64,512]{2,1,0:T(8,128)(2,1)S(1)} %copy-done.1, bf16[6144,128]{1,0:T(8,128)(2,1)S(1)} %get-tuple-element.53.ordered_ref), custom_call_target="tpu_custom_call" | custom-call | flops 20971520 | bytes 32768 | tf_op jit(solution)/shard_map/near_1/pallas_call | solution.py:464
  16.9 1.0 %collective-permute-start.5 = (bf16[13,64,128]{2,1,0:T(8,128)(2,1)S(1)}, bf16[13,64,128]{2,1,0:T(8,128)(2,1)S(1)}, u32[]{:S(2)}, u32[]{:S(2)}) collective-permute-start(bf16[13,64,128]{2,1,0:T(8,128)(2,1)S(1)} %collective-permute-done.1.refs_1_), channel_id=1, source_target_pairs={{0,2},{1,3},{2,0},{3,1},{4,6},{5,7},{6,4},{7,5},{8,10},{9,11},{10,... | collective-permute-start | bytes 638984 | tf_op jit(solution)/shard_map/ppermute | solution.py:38
  17.9 1.6 %collective-permute-start.6 = (bf16[13,64,128]{2,1,0:T(8,128)(2,1)S(1)}, bf16[13,64,128]{2,1,0:T(8,128)(2,1)S(1)}, u32[]{:S(2)}, u32[]{:S(2)}) collective-permute-start(bf16[13,64,128]{2,1,0:T(8,128)(2,1)S(1)} %collective-permute-done.1.refs_1_), channel_id=1, source_target_pairs={{0,4},{1,5},{2,6},{3,7},{4,0},{5,1},{6,2},{7,3},{8,12},{9,13},{10,... | collective-permute-start | bytes 638984 | tf_op jit(solution)/shard_map/ppermute | solution.py:38
  19.9 2.2 %collective-permute-start.10 = (bf16[13,64,128]{2,1,0:T(8,128)(2,1)S(1)}, bf16[13,64,128]{2,1,0:T(8,128)(2,1)S(1)}, u32[]{:S(2)}, u32[]{:S(2)}) collective-permute-start(bf16[13,64,128]{2,1,0:T(8,128)(2,1)S(1)} %choose.2), channel_id=1, source_target_pairs={{0,4},{1,3},{2,6},{3,1},{4,0},{5,7},{6,2},{7,5},{8,12},{9,11},{10,... | collective-permute-start | bytes 638984 | tf_op jit(solution)/shard_map/ppermute | solution.py:38
  22.1 0.7 %collective-permute-start.7 = (bf16[512,128]{1,0:T(8,128)(2,1)S(1)}, bf16[512,128]{1,0:T(8,128)(2,1)S(1)}, u32[]{:S(2)}, u32[]{:S(2)}) collective-permute-start(bf16[512,128]{1,0:T(8,128)(2,1)S(1)} %get-tuple-element.44), channel_id=1, source_target_pairs={{1,2},{3,4},{5,6},{7,8},{9,10},{11,12},{13,14},{15,16},{17,18},{19... | collective-permute-start | bytes 393224 | tf_op jit(solution)/shard_map/ppermute | solution.py:570
  22.7 4.0 %couplings_by_owner.1 = (bf16[13,64,1024]{2,1,0:T(8,128)(2,1)S(1)}, bf16[15,64,1024]{2,1,0:T(8,128)(2,1)S(1)}, bf16[12,64,64]{2,1,0:T(8,128)(2,1)S(1)}) custom-call(s32[16,128]{1,0:T(8,128)S(1)} %get-tuple-element.40.entry_ref, s32[16,128]{1,0:T(8,128)S(1)} %get-tuple-element.33.block_ref.at_ref, bf16[512,128]{1,0:T(8,128)(2,1)S(1)} %get-tuple-element.41.inner_ref, ...), custom_call_target="tpu_custom_call" | custom-call | bytes 131072 | tf_op jit(solution)/shard_map/couplings_by_owner/pallas_call | solution.py:307
  26.9 3.1 %collective-permute-start.13 = (bf16[15,64,1024]{2,1,0:T(8,128)(2,1)S(1)}, bf16[15,64,1024]{2,1,0:T(8,128)(2,1)S(1)}, u32[]{:S(2)}, u32[]{:S(2)}) collective-permute-start(bf16[15,64,1024]{2,1,0:T(8,128)(2,1)S(1)} %get-tuple-element.54), channel_id=1, source_target_pairs={{0,1},{1,0},{2,3},{3,2},{4,5},{5,4},{6,7},{7,6},{8,9},{9,8},{10,11... | collective-permute-start | bytes 5898248 | tf_op jit(solution)/shard_map/ppermute | solution.py:38
  30.2 2.8 %collective-permute-start.8 = (bf16[26,64,128]{2,1,0:T(8,128)(2,1)S(1)}, bf16[26,64,128]{2,1,0:T(8,128)(2,1)S(1)}, u32[]{:S(2)}, u32[]{:S(2)}) collective-permute-start(bf16[26,64,128]{2,1,0:T(8,128)(2,1)S(1)} %join.1.refs_0_), channel_id=1, source_target_pairs={{0,2},{1,3},{2,0},{3,1},{4,6},{5,7},{6,4},{7,5},{8,10},{9,11},{10,... | collective-permute-start | bytes 1277960 | tf_op jit(solution)/shard_map/ppermute | solution.py:38
  33.0 0.6 %collective-permute-start.9 = (bf16[26,64,128]{2,1,0:T(8,128)(2,1)S(1)}, bf16[26,64,128]{2,1,0:T(8,128)(2,1)S(1)}, u32[]{:S(2)}, u32[]{:S(2)}) collective-permute-start(bf16[26,64,128]{2,1,0:T(8,128)(2,1)S(1)} %join.1.refs_0_), channel_id=1, source_target_pairs={{0,4},{1,5},{2,6},{3,7},{4,0},{5,1},{6,2},{7,3},{8,12},{9,13},{10,... | collective-permute-start | bytes 1277960 | tf_op jit(solution)/shard_map/ppermute | solution.py:38
  33.7 1.9 %collective-permute-start.11 = (bf16[13,64,128]{2,1,0:T(8,128)(2,1)S(1)}, bf16[13,64,128]{2,1,0:T(8,128)(2,1)S(1)}, u32[]{:S(2)}, u32[]{:S(2)}) collective-permute-start(bf16[13,64,128]{2,1,0:T(8,128)(2,1)S(1)} %collective-permute-done.10.refs_6_), channel_id=1, source_target_pairs={{0,24},{1,25},{2,26},{3,27},{4,28},{5,29},{6,30},{7,31},{8,0},{9,1... | collective-permute-start | bytes 638984 | tf_op jit(solution)/shard_map/ppermute | solution.py:38
  35.6 3.6 %near_3.1 = (bf16[6144,128]{1,0:T(8,128)(2,1)S(1)}, bf16[3072,128]{1,0:T(8,128)(2,1)S(1)}) custom-call(s32[2,12]{1,0:T(2,128)S(1)} %bitcast.3, s32[12,512]{1,0:T(8,128)S(1)} %copy-done.2, bf16[512,1536]{1,0:T(8,128)(2,1)S(1)} %copy-done, bf16[12,64,512]{2,1,0:T(8,128)(2,1)S(1)} %copy-done.1, ...), custom_call_target="tpu_custom_call", output_to_operand_aliasing={{0}: (5, {}), {1}: (6, {})} | custom-call | flops 20971520 | bytes 32768 | tf_op jit(solution)/shard_map/near_3/pallas_call | solution.py:464
  39.5 1.1 %far_0_0.1.refs_6_ = f32[13,64,128]{2,1,0:T(8,128)S(1)} custom-call(s32[16,128]{1,0:T(8,128)S(1)} %get-tuple-element.33.block_ref.at_ref, bf16[13,64,128]{2,1,0:T(8,128)(2,1)S(1)} %get-tuple-element.34.refs_0_, bf16[13,64,128]{2,1,0:T(8,128)(2,1)S(1)} %collective-permute-done.1.refs_1_, bf16[13,64,128]{2,1,0:T(8,128)(2,1)S(1)} %collective-permute-done.2.x_ref.refs_2_, ...), custom_call_target="tpu_custom_call" | custom-call | flops 1703936 | bytes 16384 | tf_op jit(solution)/shard_map/far_0_0/pallas_call | solution.py:365
  40.6 3.9 %near_0.1 = (bf16[6144,128]{1,0:T(8,128)(2,1)S(1)}, bf16[3072,128]{1,0:T(8,128)(2,1)S(1)}, s32[16,128]{1,0:T(8,128)S(1)}) custom-call(s32[2,12]{1,0:T(2,128)S(1)} %bitcast.4, s32[12,512]{1,0:T(8,128)S(1)} %copy-done.2, bf16[512,1536]{1,0:T(8,128)(2,1)S(1)} %copy-done, ...), custom_call_target="tpu_custom_call", output_to_operand_aliasing={{0}: (9, {}), {1}: (10, {})} | custom-call | flops 20971520 | bytes 32768 | tf_op jit(solution)/shard_map/near_0/pallas_call | solution.py:464
  44.4 1.1 %far_1_0.1.refs_6_ = f32[13,64,128]{2,1,0:T(8,128)S(1)} custom-call(s32[16,128]{1,0:T(8,128)S(1)} %get-tuple-element.56.at_ref, bf16[13,64,128]{2,1,0:T(8,128)(2,1)S(1)} %get-tuple-element.34.refs_0_, bf16[13,64,128]{2,1,0:T(8,128)(2,1)S(1)} %collective-permute-done.1.refs_1_, bf16[13,64,128]{2,1,0:T(8,128)(2,1)S(1)} %collective-permute-done.2.x_ref.refs_2_, ...), custom_call_target="tpu_custom_call" | custom-call | flops 1703936 | bytes 16384 | tf_op jit(solution)/shard_map/far_1_0/pallas_call | solution.py:365
  45.5 1.9 %collective-permute-done.14.refs_4_ = bf16[13,64,128]{2,1,0:T(8,128)(2,1)S(1)} collective-permute-done((bf16[13,64,128]{2,1,0:T(8,128)(2,1)S(1)}, bf16[13,64,128]{2,1,0:T(8,128)(2,1)S(1)}, u32[]{:S(2)}, u32[]{:S(2)}) %collective-permute-start.14) | collective-permute-done | bytes 213024 | tf_op jit(solution)/shard_map/ppermute | solution.py:38
  47.4 1.1 %far_1_2.1 = f32[13,64,128]{2,1,0:T(8,128)S(1)} custom-call(s32[16,128]{1,0:T(8,128)S(1)} %get-tuple-element.56.at_ref, bf16[26,64,128]{2,1,0:T(8,128)(2,1)S(1)} %join.1.refs_0_, bf16[26,64,128]{2,1,0:T(8,128)(2,1)S(1)} %collective-permute-done.8.refs_1_, bf16[26,64,128]{2,1,0:T(8,128)(2,1)S(1)} %collective-permute-done.9.refs_2_, ...), custom_call_target="tpu_custom_call" | custom-call | flops 1703936 | bytes 16384 | tf_op jit(solution)/shard_map/far_1_2/pallas_call | solution.py:365
  48.6 1.1 %far_0_2.1.own_ref = f32[13,64,128]{2,1,0:T(8,128)S(1)} custom-call(s32[16,128]{1,0:T(8,128)S(1)} %get-tuple-element.33.block_ref.at_ref, bf16[26,64,128]{2,1,0:T(8,128)(2,1)S(1)} %join.1.refs_0_, bf16[26,64,128]{2,1,0:T(8,128)(2,1)S(1)} %collective-permute-done.8.refs_1_, bf16[26,64,128]{2,1,0:T(8,128)(2,1)S(1)} %collective-permute-done.9.refs_2_, ...), custom_call_target="tpu_custom_call" | custom-call | flops 1703936 | bytes 16384 | tf_op jit(solution)/shard_map/far_0_2/pallas_call | solution.py:365
  49.7 0.7 %collective-permute-done.15.other_ref = f32[13,64,128]{2,1,0:T(8,128)S(1)} collective-permute-done((f32[13,64,128]{2,1,0:T(8,128)S(1)}, f32[13,64,128]{2,1,0:T(8,128)S(1)}, u32[]{:S(2)}, u32[]{:S(2)}) %collective-permute-start.15) | collective-permute-done | bytes 426016 | tf_op jit(solution)/shard_map/ppermute | solution.py:38
  50.4 2.5 %local_and_field.1 = bf16[6144,128]{1,0:T(8,128)(2,1)} custom-call(f32[13,64,128]{2,1,0:T(8,128)S(1)} %far_0_2.1.own_ref, f32[13,64,128]{2,1,0:T(8,128)S(1)} %collective-permute-done.15.other_ref, bf16[12,64,64]{2,1,0:T(8,128)(2,1)S(1)} %get-tuple-element.58.turned_transfer_ref, bf16[6144,128]{1,0:T(8,128)(2,1)S(1)} %get-tuple-element.59.near_ref, ...), custom_call_target="tpu_custom_call" | custom-call | flops 1572864 | bytes 65536 | tf_op jit(solution)/shard_map/local_and_field/pallas_call | solution.py:519
  (29 shorter events, 1.2 us)
Async XLA Ops:
  0.0 13.2 %copy-start = (bf16[512,1536]{1,0:T(8,128)(2,1)S(1)}, bf16[512,1536]{1,0:T(8,128)(2,1)}, u32[]{:S(2)}) copy-start(bf16[512,1536]{1,0:T(8,128)(2,1)} %constant.6.clone.table_ref) | copy-start | bytes 4718596
  0.0 13.2 %copy-start.1 = (bf16[12,64,512]{2,1,0:T(8,128)(2,1)S(1)}, bf16[12,64,512]{2,1,0:T(8,128)(2,1)}, u32[]{:S(2)}) copy-start(bf16[12,64,512]{2,1,0:T(8,128)(2,1)} %basis_ref.7) | copy-start | bytes 2359300
  0.0 13.2 %copy-start.2 = (s32[12,512]{1,0:T(8,128)S(1)}, s32[12,512]{1,0:T(8,128)}, u32[]{:S(2)}) copy-start(s32[12,512]{1,0:T(8,128)} %order_ref.7) | copy-start | bytes 73732
  0.0 13.2 %copy-start.3 = (s32[12,2]{0,1:T(2,128)S(1)}, s32[12,2]{0,1:T(2,128)}, u32[]{:S(2)}) copy-start(s32[12,2]{0,1:T(2,128)} %param.17) | copy-start | bytes 292
  4.8 12.0 %collective-permute-start.1 = (bf16[13,64,128]{2,1,0:T(8,128)(2,1)S(1)}, bf16[13,64,128]{2,1,0:T(8,128)(2,1)S(1)}, u32[]{:S(2)}, u32[]{:S(2)}) collective-permute-start(bf16[13,64,128]{2,1,0:T(8,128)(2,1)S(1)} %get-tuple-element.34.refs_0_), channel_id=1, source_target_pairs={{0,8},{1,9},{2,10},{3,11},{4,12},{5,13},{6,14},{7,15},{8,16},{9,17... | collective-permute-start | bytes 638984 | tf_op jit(solution)/shard_map/ppermute | solution.py:38
  7.9 8.9 %collective-permute-start.2 = (bf16[13,64,128]{2,1,0:T(8,128)(2,1)S(1)}, bf16[13,64,128]{2,1,0:T(8,128)(2,1)S(1)}, u32[]{:S(2)}, u32[]{:S(2)}) collective-permute-start(bf16[13,64,128]{2,1,0:T(8,128)(2,1)S(1)} %get-tuple-element.34.refs_0_), channel_id=1, source_target_pairs={{0,2},{1,3},{2,0},{3,1},{4,6},{5,7},{6,4},{7,5},{8,10},{9,11},{10,... | collective-permute-start | bytes 638984 | tf_op jit(solution)/shard_map/ppermute | solution.py:38
  9.4 7.5 %collective-permute-start.3 = (bf16[13,64,128]{2,1,0:T(8,128)(2,1)S(1)}, bf16[13,64,128]{2,1,0:T(8,128)(2,1)S(1)}, u32[]{:S(2)}, u32[]{:S(2)}) collective-permute-start(bf16[13,64,128]{2,1,0:T(8,128)(2,1)S(1)} %get-tuple-element.34.refs_0_), channel_id=1, source_target_pairs={{0,4},{1,5},{2,6},{3,7},{4,0},{5,1},{6,2},{7,3},{8,12},{9,13},{10,... | collective-permute-start | bytes 638984 | tf_op jit(solution)/shard_map/ppermute | solution.py:38
  11.0 8.9 %collective-permute-start = (bf16[13,64,128]{2,1,0:T(8,128)(2,1)S(1)}, bf16[13,64,128]{2,1,0:T(8,128)(2,1)S(1)}, u32[]{:S(2)}, u32[]{:S(2)}) collective-permute-start(bf16[13,64,128]{2,1,0:T(8,128)(2,1)S(1)} %get-tuple-element.34.refs_0_), channel_id=1, source_target_pairs={{0,24},{1,25},{2,26},{3,27},{4,28},{5,29},{6,30},{7,31},{8,0},{9,1... | collective-permute-start | bytes 638984 | tf_op jit(solution)/shard_map/ppermute | solution.py:38
  16.8 9.9 %collective-permute-start.4 = (bf16[13,64,128]{2,1,0:T(8,128)(2,1)S(1)}, bf16[13,64,128]{2,1,0:T(8,128)(2,1)S(1)}, u32[]{:S(2)}, u32[]{:S(2)}) collective-permute-start(bf16[13,64,128]{2,1,0:T(8,128)(2,1)S(1)} %collective-permute-done.1.refs_1_), channel_id=1, source_target_pairs={{0,8},{1,9},{2,10},{3,11},{4,12},{5,13},{6,14},{7,15},{8,16},{9,17... | collective-permute-start | bytes 638984 | tf_op jit(solution)/shard_map/ppermute | solution.py:38
  16.9 9.9 %collective-permute-start.5 = (bf16[13,64,128]{2,1,0:T(8,128)(2,1)S(1)}, bf16[13,64,128]{2,1,0:T(8,128)(2,1)S(1)}, u32[]{:S(2)}, u32[]{:S(2)}) collective-permute-start(bf16[13,64,128]{2,1,0:T(8,128)(2,1)S(1)} %collective-permute-done.1.refs_1_), channel_id=1, source_target_pairs={{0,2},{1,3},{2,0},{3,1},{4,6},{5,7},{6,4},{7,5},{8,10},{9,11},{10,... | collective-permute-start | bytes 638984 | tf_op jit(solution)/shard_map/ppermute | solution.py:38
  17.9 8.9 %collective-permute-start.6 = (bf16[13,64,128]{2,1,0:T(8,128)(2,1)S(1)}, bf16[13,64,128]{2,1,0:T(8,128)(2,1)S(1)}, u32[]{:S(2)}, u32[]{:S(2)}) collective-permute-start(bf16[13,64,128]{2,1,0:T(8,128)(2,1)S(1)} %collective-permute-done.1.refs_1_), channel_id=1, source_target_pairs={{0,4},{1,5},{2,6},{3,7},{4,0},{5,1},{6,2},{7,3},{8,12},{9,13},{10,... | collective-permute-start | bytes 638984 | tf_op jit(solution)/shard_map/ppermute | solution.py:38
  19.9 7.0 %collective-permute-start.10 = (bf16[13,64,128]{2,1,0:T(8,128)(2,1)S(1)}, bf16[13,64,128]{2,1,0:T(8,128)(2,1)S(1)}, u32[]{:S(2)}, u32[]{:S(2)}) collective-permute-start(bf16[13,64,128]{2,1,0:T(8,128)(2,1)S(1)} %choose.2), channel_id=1, source_target_pairs={{0,4},{1,3},{2,6},{3,1},{4,0},{5,7},{6,2},{7,5},{8,12},{9,11},{10,... | collective-permute-start | bytes 638984 | tf_op jit(solution)/shard_map/ppermute | solution.py:38
  22.1 4.7 %collective-permute-start.7 = (bf16[512,128]{1,0:T(8,128)(2,1)S(1)}, bf16[512,128]{1,0:T(8,128)(2,1)S(1)}, u32[]{:S(2)}, u32[]{:S(2)}) collective-permute-start(bf16[512,128]{1,0:T(8,128)(2,1)S(1)} %get-tuple-element.44), channel_id=1, source_target_pairs={{1,2},{3,4},{5,6},{7,8},{9,10},{11,12},{13,14},{15,16},{17,18},{19... | collective-permute-start | bytes 393224 | tf_op jit(solution)/shard_map/ppermute | solution.py:570
  26.9 13.7 %collective-permute-start.13 = (bf16[15,64,1024]{2,1,0:T(8,128)(2,1)S(1)}, bf16[15,64,1024]{2,1,0:T(8,128)(2,1)S(1)}, u32[]{:S(2)}, u32[]{:S(2)}) collective-permute-start(bf16[15,64,1024]{2,1,0:T(8,128)(2,1)S(1)} %get-tuple-element.54), channel_id=1, source_target_pairs={{0,1},{1,0},{2,3},{3,2},{4,5},{5,4},{6,7},{7,6},{8,9},{9,8},{10,11... | collective-permute-start | bytes 5898248 | tf_op jit(solution)/shard_map/ppermute | solution.py:38
  30.0 9.2 %collective-permute-start.12 = (bf16[13,64,128]{2,1,0:T(8,128)(2,1)S(1)}, bf16[13,64,128]{2,1,0:T(8,128)(2,1)S(1)}, u32[]{:S(2)}, u32[]{:S(2)}) collective-permute-start(bf16[13,64,128]{2,1,0:T(8,128)(2,1)S(1)} %choose.3), channel_id=1, source_target_pairs={{0,4},{1,3},{2,6},{3,1},{4,0},{5,7},{6,2},{7,5},{8,12},{9,11},{10,... | collective-permute-start | bytes 638984 | tf_op jit(solution)/shard_map/ppermute | solution.py:38
  30.2 17.2 %collective-permute-start.8 = (bf16[26,64,128]{2,1,0:T(8,128)(2,1)S(1)}, bf16[26,64,128]{2,1,0:T(8,128)(2,1)S(1)}, u32[]{:S(2)}, u32[]{:S(2)}) collective-permute-start(bf16[26,64,128]{2,1,0:T(8,128)(2,1)S(1)} %join.1.refs_0_), channel_id=1, source_target_pairs={{0,2},{1,3},{2,0},{3,1},{4,6},{5,7},{6,4},{7,5},{8,10},{9,11},{10,... | collective-permute-start | bytes 1277960 | tf_op jit(solution)/shard_map/ppermute | solution.py:38
  33.0 14.4 %collective-permute-start.9 = (bf16[26,64,128]{2,1,0:T(8,128)(2,1)S(1)}, bf16[26,64,128]{2,1,0:T(8,128)(2,1)S(1)}, u32[]{:S(2)}, u32[]{:S(2)}) collective-permute-start(bf16[26,64,128]{2,1,0:T(8,128)(2,1)S(1)} %join.1.refs_0_), channel_id=1, source_target_pairs={{0,4},{1,5},{2,6},{3,7},{4,0},{5,1},{6,2},{7,3},{8,12},{9,13},{10,... | collective-permute-start | bytes 1277960 | tf_op jit(solution)/shard_map/ppermute | solution.py:38
  33.7 11.9 %collective-permute-start.11 = (bf16[13,64,128]{2,1,0:T(8,128)(2,1)S(1)}, bf16[13,64,128]{2,1,0:T(8,128)(2,1)S(1)}, u32[]{:S(2)}, u32[]{:S(2)}) collective-permute-start(bf16[13,64,128]{2,1,0:T(8,128)(2,1)S(1)} %collective-permute-done.10.refs_6_), channel_id=1, source_target_pairs={{0,24},{1,25},{2,26},{3,27},{4,28},{5,29},{6,30},{7,31},{8,0},{9,1... | collective-permute-start | bytes 638984 | tf_op jit(solution)/shard_map/ppermute | solution.py:38
  39.1 8.3 %collective-permute-start.14 = (bf16[13,64,128]{2,1,0:T(8,128)(2,1)S(1)}, bf16[13,64,128]{2,1,0:T(8,128)(2,1)S(1)}, u32[]{:S(2)}, u32[]{:S(2)}) collective-permute-start(bf16[13,64,128]{2,1,0:T(8,128)(2,1)S(1)} %collective-permute-done.12.refs_7_), channel_id=1, source_target_pairs={{0,8},{1,9},{2,10},{3,11},{4,12},{5,13},{6,14},{7,15},{8,16},{9,17... | collective-permute-start | bytes 638984 | tf_op jit(solution)/shard_map/ppermute | solution.py:38
  48.5 1.8 %collective-permute-start.15 = (f32[13,64,128]{2,1,0:T(8,128)S(1)}, f32[13,64,128]{2,1,0:T(8,128)S(1)}, u32[]{:S(2)}, u32[]{:S(2)}) collective-permute-start(f32[13,64,128]{2,1,0:T(8,128)S(1)} %far_1_2.1), channel_id=1, source_target_pairs={{0,1},{1,0},{2,3},{3,2},{4,5},{5,4},{6,7},{7,6},{8,9},{9,8},{10,11... | collective-permute-start | bytes 1277960 | tf_op jit(solution)/shard_map/ppermute | solution.py:38

commit v12 on v11

--- a/solution.py
+++ b/solution.py
@@ -273,13 +273,12 @@
         turned_ref[step * per + i] = transfer_ref[i].T
 
     def fill(out_ref, plane, row, entry_row, block_of):
-        for slot in range(0, slots, 2):
-            pair = []
-            for one in (slot, slot + 1):
-                entry = entry_ref[entry_row, plane * slots + one]
-                block = block_of(jnp.maximum(entry, 0))
-                pair.append(jnp.where(entry >= 0, block, jnp.zeros_like(block)))
-            out_ref[row, :, slot * rank:(slot + 2) * rank] = jnp.concatenate(pair, axis=1)
+        blocks = []
+        for slot in range(slots):
+            entry = entry_ref[entry_row, plane * slots + slot]
+            block = block_of(jnp.maximum(entry, 0))
+            blocks.append(jnp.where(entry >= 0, block, jnp.zeros_like(block)))
+        out_ref[row, :, :slots * rank] = jnp.concatenate(blocks, axis=1)
 
     for plane, out_ref in ((0, own_ref), (1, other_ref)):
         for i in range(per):
@@ -346,6 +345,7 @@
                 return ref[base + index]
             base -= ref.shape[0]
 
+    values = []
     for row in range(rows):
         chosen = [
             block_at(side, place * rows, at_ref[(row + 1) % rows, plane * slots + step * 4 + q])
@@ -355,7 +355,9 @@
         value = dot(blocks_ref[row, :, low:high], jnp.concatenate(chosen, axis=0))
         if len(refs) > 2:
             value = value + refs[1][row]
-        out[row] = value
+        values.append(value)
+    for row in range(rows):
+        out[row] = values[row]
 
 
 def far_round(plane, steps, slots, at, parts, blocks, total=None):
@@ -416,15 +418,13 @@
     )
     near = dot(table_ref[...], jnp.concatenate([left, right], axis=1)).astype(BF)
     fields = ordered_ref.shape[1]
-    turned = []
+    moved = []
     for i in range(2):
         hot = one_hot_grid(order_ref[pl.ds(2 * pair + i, 1), :], leaf_len)
-        at = pl.ds(i * leaf_len, leaf_len)
         both = jnp.concatenate([near[:, i * fields:(i + 1) * fields], basis_ref[2 * pair + i].T], axis=1)
-        moved = dot(hot, both).astype(BF)
-        near_ref[at, :] = moved[:, :fields]
-        turned.append(moved[:, fields:])
-    turned_ref[...] = jnp.concatenate(turned, axis=1)
+        moved.append(dot(hot, both).astype(BF))
+    near_ref[...] = jnp.concatenate([part[:, :fields] for part in moved], axis=0)
+    turned_ref[...] = jnp.concatenate([part[:, fields:] for part in moved], axis=1)
 
 
 def near_field(pairs, near_list, leaf_order, tables, basis, ordered, halos=None, filled=None):
@@ -559,8 +559,10 @@
 
     line = along_z(shared, 1)
     from_x, from_y = over_x(shared), over_y(shared)
-    filled = near_field(list(range(1, cut)), *near_args, ordered)
-    line = after(line, filled[0])
+    own_blocks, my_other, turned_transfer = dense_couplings(
+        entry, own_at, inner, coupling, top_coupling, transfer, slots
+    )
+    line = after(line, my_other)
     lines = [along_z(shared, layers - 1)]
     for _ in range(layers - 3):
         lines.append(along_z(line if len(lines) == 1 else lines[-1], 1))
@@ -572,18 +574,15 @@
         "subtree",
         [(d, d + 1) for d in range(1, count - 1, 2)] + [(d, d - 1) for d in range(2, count, 2)],
     )
-    own_blocks, my_other, turned_transfer = dense_couplings(
-        after(entry, ready), own_at, inner, coupling, top_coupling, transfer, slots
-    )
-
-    joined = after(join([after(lines[0], my_other)] + lines[1:]), next_x, next_y, cross)
+
+    joined = after(join(lines), next_x, next_y, cross)
     last_x, last_y = over_x(joined), over_y(joined)
     chosen = choose(me, after(next_x, joined, far), next_y)
     next_far = onward(chosen)
     other_blocks = over_core(after(my_other, chosen))
-    held = after(ordered, joined)
-    filled = near_field(list(range(cut, pairs - 1)), *near_args, held, filled=filled)
+    filled = near_field(list(range(1, cut)), *near_args, after(ordered, joined))
     next_far = after(next_far, filled[0])
+    filled = near_field(list(range(cut, pairs - 1)), *near_args, ordered, filled=filled)
     last_far = [along_z(far, layers - 1)]
     for _ in range(layers - 3):
         last_far.append(along_z(next_far if len(last_far) == 1 else last_far[-1], 1))

time: 53 us -> 54.5 us (1.028)
  waiting for transfers between devices: 2.96 us -> 4.75 us
    ppermute x15, waiting for transfers between devices: 2.96 us -> 4.74 us  [send(): lax.ppermute(block, 'subtree', [(d, target(d)) for d in range(count)])]
  transfers between devices with their start and end apart: 16 -> 16, of which waited for: 3 -> 4; matrix products, arithmetic and copies ran while one was open for 0% -> 0% of each run, Pallas kernels for 35% -> 34%
where the time goes in v12:
time: 54.5 us; the launch traced here: 54.4 us
  Pallas kernels  26.5 us (49%)
  starting transfers between devices  22.8 us (42%)
  waiting for transfers between devices  4.75 us (9%)
    ppermute x15, starting transfers between devices, send(): lax.ppermute(block, 'subtree', [(d, target(d)) for d in range(count)])  22.2 us
    pallas_call x3, Pallas kernels, near_field(): pl.pallas_call(functools.partial(near_kernel, halos is not None, pair_of,...  11 us
    ppermute x15, waiting for transfers between devices, send(): lax.ppermute(block, 'subtree', [(d, target(d)) for d in range(count)])  4.74 us
    pallas_call x1, Pallas kernels, skeletons_of(): pl.pallas_call(functools.partial(skeleton_kernel, per, layers), name='ord...  4.67 us
    pallas_call x4, Pallas kernels, far_round(): pl.pallas_call(functools.partial(round_kernel, plane, steps, slots, [len(...  4.33 us
    pallas_call x1, Pallas kernels, dense_couplings(): pl.pallas_call(functools.partial(dense_kernel, per, slots), name='couplin...  3.96 us
    pallas_call x1, Pallas kernels, field(): pl.pallas_call(functools.partial(field_kernel, per), name='local_and_fiel...  2.48 us
  transfers between devices with their start and end apart: 16, of which 4 were waited for; matrix products, arithmetic and copies ran while one was open for 0% of the time, Pallas kernels for 34%

profile of v12, /device:TPU:0, one launch (start us, length us, event | category | flops | bytes accessed | tf_op | source)
XLA Modules:
  0.0 54.4 jit_solution(14298845155143442092)
XLA Ops:
  0.0 4.7 %order_and_skeleton.1 = (bf16[6144,128]{1,0:T(8,128)(2,1)S(1)}, bf16[13,64,128]{2,1,0:T(8,128)(2,1)S(1)}, bf16[512,128]{1,0:T(8,128)(2,1)S(1)}, bf16[512,128]{1,...) custom-call(s32[1]{0:T(128)} %bitcast.me_ref.refs_0_, s32[12,512]{1,0:T(8,128)} %order_ref.7, ...), custom_call_target="tpu_custom_call" | custom-call | flops 12582912 | bytes 65536 | tf_op jit(solution)/shard_map/order_and_skeleton/pallas_call | solution.py:186
  4.7 3.1 %collective-permute-start.1 = (bf16[13,64,128]{2,1,0:T(8,128)(2,1)S(1)}, bf16[13,64,128]{2,1,0:T(8,128)(2,1)S(1)}, u32[]{:S(2)}, u32[]{:S(2)}) collective-permute-start(bf16[13,64,128]{2,1,0:T(8,128)(2,1)S(1)} %get-tuple-element.32.refs_0_), channel_id=1, source_target_pairs={{0,8},{1,9},{2,10},{3,11},{4,12},{5,13},{6,14},{7,15},{8,16},{9,17... | collective-permute-start | bytes 638984 | tf_op jit(solution)/shard_map/ppermute | solution.py:38
  7.8 1.5 %collective-permute-start.3 = (bf16[13,64,128]{2,1,0:T(8,128)(2,1)S(1)}, bf16[13,64,128]{2,1,0:T(8,128)(2,1)S(1)}, u32[]{:S(2)}, u32[]{:S(2)}) collective-permute-start(bf16[13,64,128]{2,1,0:T(8,128)(2,1)S(1)} %get-tuple-element.32.refs_0_), channel_id=1, source_target_pairs={{0,2},{1,3},{2,0},{3,1},{4,6},{5,7},{6,4},{7,5},{8,10},{9,11},{10,... | collective-permute-start | bytes 638984 | tf_op jit(solution)/shard_map/ppermute | solution.py:38
  9.2 1.5 %collective-permute-start.4 = (bf16[13,64,128]{2,1,0:T(8,128)(2,1)S(1)}, bf16[13,64,128]{2,1,0:T(8,128)(2,1)S(1)}, u32[]{:S(2)}, u32[]{:S(2)}) collective-permute-start(bf16[13,64,128]{2,1,0:T(8,128)(2,1)S(1)} %get-tuple-element.32.refs_0_), channel_id=1, source_target_pairs={{0,4},{1,5},{2,6},{3,7},{4,0},{5,1},{6,2},{7,3},{8,12},{9,13},{10,... | collective-permute-start | bytes 638984 | tf_op jit(solution)/shard_map/ppermute | solution.py:38
  10.8 2.2 %collective-permute-start = (bf16[13,64,128]{2,1,0:T(8,128)(2,1)S(1)}, bf16[13,64,128]{2,1,0:T(8,128)(2,1)S(1)}, u32[]{:S(2)}, u32[]{:S(2)}) collective-permute-start(bf16[13,64,128]{2,1,0:T(8,128)(2,1)S(1)} %get-tuple-element.32.refs_0_), channel_id=1, source_target_pairs={{0,24},{1,25},{2,26},{3,27},{4,28},{5,29},{6,30},{7,31},{8,0},{9,1... | collective-permute-start | bytes 638984 | tf_op jit(solution)/shard_map/ppermute | solution.py:38
  13.0 4.0 %couplings_by_owner.1 = (bf16[13,64,1024]{2,1,0:T(8,128)(2,1)S(1)}, bf16[15,64,1024]{2,1,0:T(8,128)(2,1)S(1)}, bf16[12,64,64]{2,1,0:T(8,128)(2,1)S(1)}) custom-call(s32[16,128]{1,0:T(8,128)S(1)} %get-tuple-element.33.entry_ref, s32[16,128]{1,0:T(8,128)S(1)} %get-tuple-element.31.block_ref.at_ref, bf16[512,128]{1,0:T(8,128)(2,1)S(1)} %get-tuple-element.34.inner_ref, ...), custom_call_target="tpu_custom_call" | custom-call | bytes 131072 | tf_op jit(solution)/shard_map/couplings_by_owner/pallas_call | solution.py:306
  17.7 1.5 %collective-permute-start.6 = (bf16[13,64,128]{2,1,0:T(8,128)(2,1)S(1)}, bf16[13,64,128]{2,1,0:T(8,128)(2,1)S(1)}, u32[]{:S(2)}, u32[]{:S(2)}) collective-permute-start(bf16[13,64,128]{2,1,0:T(8,128)(2,1)S(1)} %collective-permute-done.1.refs_1_), channel_id=1, source_target_pairs={{0,4},{1,5},{2,6},{3,7},{4,0},{5,1},{6,2},{7,3},{8,12},{9,13},{10,... | collective-permute-start | bytes 638984 | tf_op jit(solution)/shard_map/ppermute | solution.py:38
  19.7 1.8 %collective-permute-start.10 = (bf16[13,64,128]{2,1,0:T(8,128)(2,1)S(1)}, bf16[13,64,128]{2,1,0:T(8,128)(2,1)S(1)}, u32[]{:S(2)}, u32[]{:S(2)}) collective-permute-start(bf16[13,64,128]{2,1,0:T(8,128)(2,1)S(1)} %choose.2), channel_id=1, source_target_pairs={{0,4},{1,3},{2,6},{3,1},{4,0},{5,7},{6,2},{7,5},{8,12},{9,11},{10,... | collective-permute-start | bytes 638984 | tf_op jit(solution)/shard_map/ppermute | solution.py:38
  21.5 0.7 %collective-permute-start.7 = (bf16[512,128]{1,0:T(8,128)(2,1)S(1)}, bf16[512,128]{1,0:T(8,128)(2,1)S(1)}, u32[]{:S(2)}, u32[]{:S(2)}) collective-permute-start(bf16[512,128]{1,0:T(8,128)(2,1)S(1)} %get-tuple-element.38), channel_id=1, source_target_pairs={{1,2},{3,4},{5,6},{7,8},{9,10},{11,12},{13,14},{15,16},{17,18},{19... | collective-permute-start | bytes 393224 | tf_op jit(solution)/shard_map/ppermute | solution.py:572
  22.1 2.8 %collective-permute-done.2.refs_1_ = bf16[13,64,128]{2,1,0:T(8,128)(2,1)S(1)} collective-permute-done((bf16[13,64,128]{2,1,0:T(8,128)(2,1)S(1)}, bf16[13,64,128]{2,1,0:T(8,128)(2,1)S(1)}, u32[]{:S(2)}, u32[]{:S(2)}) %collective-permute-start.2) | collective-permute-done | bytes 213024 | tf_op jit(solution)/shard_map/ppermute | solution.py:38
  25.0 0.9 %collective-permute-done.10.refs_6_ = bf16[13,64,128]{2,1,0:T(8,128)(2,1)S(1)} collective-permute-done((bf16[13,64,128]{2,1,0:T(8,128)(2,1)S(1)}, bf16[13,64,128]{2,1,0:T(8,128)(2,1)S(1)}, u32[]{:S(2)}, u32[]{:S(2)}) %collective-permute-start.10) | collective-permute-done | bytes 213024 | tf_op jit(solution)/shard_map/ppermute | solution.py:38
  25.9 3.1 %collective-permute-start.13 = (bf16[15,64,1024]{2,1,0:T(8,128)(2,1)S(1)}, bf16[15,64,1024]{2,1,0:T(8,128)(2,1)S(1)}, u32[]{:S(2)}, u32[]{:S(2)}) collective-permute-start(bf16[15,64,1024]{2,1,0:T(8,128)(2,1)S(1)} %get-tuple-element.50), channel_id=1, source_target_pairs={{0,1},{1,0},{2,3},{3,2},{4,5},{5,4},{6,7},{7,6},{8,9},{9,8},{10,11... | collective-permute-start | bytes 5898248 | tf_op jit(solution)/shard_map/ppermute | solution.py:38
  29.6 1.9 %collective-permute-start.8 = (bf16[26,64,128]{2,1,0:T(8,128)(2,1)S(1)}, bf16[26,64,128]{2,1,0:T(8,128)(2,1)S(1)}, u32[]{:S(2)}, u32[]{:S(2)}) collective-permute-start(bf16[26,64,128]{2,1,0:T(8,128)(2,1)S(1)} %join.1.refs_0_), channel_id=1, source_target_pairs={{0,2},{1,3},{2,0},{3,1},{4,6},{5,7},{6,4},{7,5},{8,10},{9,11},{10,... | collective-permute-start | bytes 1277960 | tf_op jit(solution)/shard_map/ppermute | solution.py:38
  31.5 1.9 %collective-permute-start.9 = (bf16[26,64,128]{2,1,0:T(8,128)(2,1)S(1)}, bf16[26,64,128]{2,1,0:T(8,128)(2,1)S(1)}, u32[]{:S(2)}, u32[]{:S(2)}) collective-permute-start(bf16[26,64,128]{2,1,0:T(8,128)(2,1)S(1)} %join.1.refs_0_), channel_id=1, source_target_pairs={{0,4},{1,5},{2,6},{3,7},{4,0},{5,1},{6,2},{7,3},{8,12},{9,13},{10,... | collective-permute-start | bytes 1277960 | tf_op jit(solution)/shard_map/ppermute | solution.py:38
  33.5 1.8 %collective-permute-start.11 = (bf16[13,64,128]{2,1,0:T(8,128)(2,1)S(1)}, bf16[13,64,128]{2,1,0:T(8,128)(2,1)S(1)}, u32[]{:S(2)}, u32[]{:S(2)}) collective-permute-start(bf16[13,64,128]{2,1,0:T(8,128)(2,1)S(1)} %collective-permute-done.10.refs_6_), channel_id=1, source_target_pairs={{0,24},{1,25},{2,26},{3,27},{4,28},{5,29},{6,30},{7,31},{8,0},{9,1... | collective-permute-start | bytes 638984 | tf_op jit(solution)/shard_map/ppermute | solution.py:38
  35.3 3.6 %near_1.1 = (bf16[6144,128]{1,0:T(8,128)(2,1)S(1)}, bf16[3072,128]{1,0:T(8,128)(2,1)S(1)}) custom-call(s32[2,12]{1,0:T(2,128)S(1)} %bitcast.2, s32[12,512]{1,0:T(8,128)S(1)} %copy-done.2, bf16[512,1536]{1,0:T(8,128)(2,1)S(1)} %copy-done, bf16[12,64,512]{2,1,0:T(8,128)(2,1)S(1)} %copy-done.1, bf16[6144,128]{1,0:T(8,128)(2,1)S(1)} %get-tuple-element.49.ordered_ref), custom_call_target="tpu_custom_call" | custom-call | flops 20971520 | bytes 32768 | tf_op jit(solution)/shard_map/near_1/pallas_call | solution.py:464
  39.3 3.6 %near_3.1 = (bf16[6144,128]{1,0:T(8,128)(2,1)S(1)}, bf16[3072,128]{1,0:T(8,128)(2,1)S(1)}) custom-call(s32[2,12]{1,0:T(2,128)S(1)} %bitcast.3, s32[12,512]{1,0:T(8,128)S(1)} %copy-done.2, bf16[512,1536]{1,0:T(8,128)(2,1)S(1)} %copy-done, bf16[12,64,512]{2,1,0:T(8,128)(2,1)S(1)} %copy-done.1, ...), custom_call_target="tpu_custom_call", output_to_operand_aliasing={{0}: (5, {}), {1}: (6, {})} | custom-call | flops 20971520 | bytes 32768 | tf_op jit(solution)/shard_map/near_3/pallas_call | solution.py:464
  42.8 1.1 %far_0_0.1.refs_6_ = f32[13,64,128]{2,1,0:T(8,128)S(1)} custom-call(s32[16,128]{1,0:T(8,128)S(1)} %get-tuple-element.31.block_ref.at_ref, bf16[13,64,128]{2,1,0:T(8,128)(2,1)S(1)} %get-tuple-element.32.refs_0_, bf16[13,64,128]{2,1,0:T(8,128)(2,1)S(1)} %collective-permute-done.1.refs_1_, bf16[13,64,128]{2,1,0:T(8,128)(2,1)S(1)} %collective-permute-done.3.x_ref.refs_2_, ...), custom_call_target="tpu_custom_call" | custom-call | flops 1703936 | bytes 16384 | tf_op jit(solution)/shard_map/far_0_0/pallas_call | solution.py:367
  43.9 3.9 %near_0.1 = (bf16[6144,128]{1,0:T(8,128)(2,1)S(1)}, bf16[3072,128]{1,0:T(8,128)(2,1)S(1)}, s32[16,128]{1,0:T(8,128)S(1)}) custom-call(s32[2,12]{1,0:T(2,128)S(1)} %bitcast.4, s32[12,512]{1,0:T(8,128)S(1)} %copy-done.2, bf16[512,1536]{1,0:T(8,128)(2,1)S(1)} %copy-done, ...), custom_call_target="tpu_custom_call", output_to_operand_aliasing={{0}: (9, {}), {1}: (10, {})} | custom-call | flops 20971520 | bytes 32768 | tf_op jit(solution)/shard_map/near_0/pallas_call | solution.py:464
  47.8 1.1 %far_1_0.1.refs_6_ = f32[13,64,128]{2,1,0:T(8,128)S(1)} custom-call(s32[16,128]{1,0:T(8,128)S(1)} %get-tuple-element.52.at_ref, bf16[13,64,128]{2,1,0:T(8,128)(2,1)S(1)} %get-tuple-element.32.refs_0_, bf16[13,64,128]{2,1,0:T(8,128)(2,1)S(1)} %collective-permute-done.1.refs_1_, bf16[13,64,128]{2,1,0:T(8,128)(2,1)S(1)} %collective-permute-done.3.x_ref.refs_2_, ...), custom_call_target="tpu_custom_call" | custom-call | flops 1703936 | bytes 16384 | tf_op jit(solution)/shard_map/far_1_0/pallas_call | solution.py:367
  48.9 1.1 %far_1_2.1 = f32[13,64,128]{2,1,0:T(8,128)S(1)} custom-call(s32[16,128]{1,0:T(8,128)S(1)} %get-tuple-element.52.at_ref, bf16[26,64,128]{2,1,0:T(8,128)(2,1)S(1)} %join.1.refs_0_, bf16[26,64,128]{2,1,0:T(8,128)(2,1)S(1)} %collective-permute-done.8.refs_1_, bf16[26,64,128]{2,1,0:T(8,128)(2,1)S(1)} %collective-permute-done.9.refs_2_, ...), custom_call_target="tpu_custom_call" | custom-call | flops 1703936 | bytes 16384 | tf_op jit(solution)/shard_map/far_1_2/pallas_call | solution.py:367
  50.1 1.1 %far_0_2.1.own_ref = f32[13,64,128]{2,1,0:T(8,128)S(1)} custom-call(s32[16,128]{1,0:T(8,128)S(1)} %get-tuple-element.31.block_ref.at_ref, bf16[26,64,128]{2,1,0:T(8,128)(2,1)S(1)} %join.1.refs_0_, bf16[26,64,128]{2,1,0:T(8,128)(2,1)S(1)} %collective-permute-done.8.refs_1_, bf16[26,64,128]{2,1,0:T(8,128)(2,1)S(1)} %collective-permute-done.9.refs_2_, ...), custom_call_target="tpu_custom_call" | custom-call | flops 1703936 | bytes 16384 | tf_op jit(solution)/shard_map/far_0_2/pallas_call | solution.py:367
  51.2 0.7 %collective-permute-done.15.other_ref = f32[13,64,128]{2,1,0:T(8,128)S(1)} collective-permute-done((f32[13,64,128]{2,1,0:T(8,128)S(1)}, f32[13,64,128]{2,1,0:T(8,128)S(1)}, u32[]{:S(2)}, u32[]{:S(2)}) %collective-permute-start.15) | collective-permute-done | bytes 426016 | tf_op jit(solution)/shard_map/ppermute | solution.py:38
  51.9 2.5 %local_and_field.1 = bf16[6144,128]{1,0:T(8,128)(2,1)} custom-call(f32[13,64,128]{2,1,0:T(8,128)S(1)} %far_0_2.1.own_ref, f32[13,64,128]{2,1,0:T(8,128)S(1)} %collective-permute-done.15.other_ref, bf16[12,64,64]{2,1,0:T(8,128)(2,1)S(1)} %get-tuple-element.54.turned_transfer_ref, bf16[6144,128]{1,0:T(8,128)(2,1)S(1)} %get-tuple-element.55.near_ref, ...), custom_call_target="tpu_custom_call" | custom-call | flops 1572864 | bytes 65536 | tf_op jit(solution)/shard_map/local_and_field/pallas_call | solution.py:519
  (29 shorter events, 2.3 us)
Async XLA Ops:
  4.7 12.3 %collective-permute-start.1 = (bf16[13,64,128]{2,1,0:T(8,128)(2,1)S(1)}, bf16[13,64,128]{2,1,0:T(8,128)(2,1)S(1)}, u32[]{:S(2)}, u32[]{:S(2)}) collective-permute-start(bf16[13,64,128]{2,1,0:T(8,128)(2,1)S(1)} %get-tuple-element.32.refs_0_), channel_id=1, source_target_pairs={{0,8},{1,9},{2,10},{3,11},{4,12},{5,13},{6,14},{7,15},{8,16},{9,17... | collective-permute-start | bytes 638984 | tf_op jit(solution)/shard_map/ppermute | solution.py:38
  7.8 9.3 %collective-permute-start.3 = (bf16[13,64,128]{2,1,0:T(8,128)(2,1)S(1)}, bf16[13,64,128]{2,1,0:T(8,128)(2,1)S(1)}, u32[]{:S(2)}, u32[]{:S(2)}) collective-permute-start(bf16[13,64,128]{2,1,0:T(8,128)(2,1)S(1)} %get-tuple-element.32.refs_0_), channel_id=1, source_target_pairs={{0,2},{1,3},{2,0},{3,1},{4,6},{5,7},{6,4},{7,5},{8,10},{9,11},{10,... | collective-permute-start | bytes 638984 | tf_op jit(solution)/shard_map/ppermute | solution.py:38
  9.2 7.9 %collective-permute-start.4 = (bf16[13,64,128]{2,1,0:T(8,128)(2,1)S(1)}, bf16[13,64,128]{2,1,0:T(8,128)(2,1)S(1)}, u32[]{:S(2)}, u32[]{:S(2)}) collective-permute-start(bf16[13,64,128]{2,1,0:T(8,128)(2,1)S(1)} %get-tuple-element.32.refs_0_), channel_id=1, source_target_pairs={{0,4},{1,5},{2,6},{3,7},{4,0},{5,1},{6,2},{7,3},{8,12},{9,13},{10,... | collective-permute-start | bytes 638984 | tf_op jit(solution)/shard_map/ppermute | solution.py:38
  10.8 8.9 %collective-permute-start = (bf16[13,64,128]{2,1,0:T(8,128)(2,1)S(1)}, bf16[13,64,128]{2,1,0:T(8,128)(2,1)S(1)}, u32[]{:S(2)}, u32[]{:S(2)}) collective-permute-start(bf16[13,64,128]{2,1,0:T(8,128)(2,1)S(1)} %get-tuple-element.32.refs_0_), channel_id=1, source_target_pairs={{0,24},{1,25},{2,26},{3,27},{4,28},{5,29},{6,30},{7,31},{8,0},{9,1... | collective-permute-start | bytes 638984 | tf_op jit(solution)/shard_map/ppermute | solution.py:38
  13.0 22.3 %copy-start.1 = (bf16[12,64,512]{2,1,0:T(8,128)(2,1)S(1)}, bf16[12,64,512]{2,1,0:T(8,128)(2,1)}, u32[]{:S(2)}) copy-start(bf16[12,64,512]{2,1,0:T(8,128)(2,1)} %basis_ref.7) | copy-start | bytes 2359300
  17.0 18.3 %copy-start = (bf16[512,1536]{1,0:T(8,128)(2,1)S(1)}, bf16[512,1536]{1,0:T(8,128)(2,1)}, u32[]{:S(2)}) copy-start(bf16[512,1536]{1,0:T(8,128)(2,1)} %constant.6.clone.table_ref) | copy-start | bytes 4718596
  17.0 18.3 %copy-start.2 = (s32[12,512]{1,0:T(8,128)S(1)}, s32[12,512]{1,0:T(8,128)}, u32[]{:S(2)}) copy-start(s32[12,512]{1,0:T(8,128)} %order_ref.7) | copy-start | bytes 73732
  17.0 18.3 %copy-start.3 = (s32[12,2]{0,1:T(2,128)S(1)}, s32[12,2]{0,1:T(2,128)}, u32[]{:S(2)}) copy-start(s32[12,2]{0,1:T(2,128)} %param.17) | copy-start | bytes 292
  17.0 7.9 %collective-permute-start.2 = (bf16[13,64,128]{2,1,0:T(8,128)(2,1)S(1)}, bf16[13,64,128]{2,1,0:T(8,128)(2,1)S(1)}, u32[]{:S(2)}, u32[]{:S(2)}) collective-permute-start(bf16[13,64,128]{2,1,0:T(8,128)(2,1)S(1)} %collective-permute-done.1.refs_1_), channel_id=1, source_target_pairs={{0,8},{1,9},{2,10},{3,11},{4,12},{5,13},{6,14},{7,15},{8,16},{9,17... | collective-permute-start | bytes 638984 | tf_op jit(solution)/shard_map/ppermute | solution.py:38
  17.1 7.9 %collective-permute-start.5 = (bf16[13,64,128]{2,1,0:T(8,128)(2,1)S(1)}, bf16[13,64,128]{2,1,0:T(8,128)(2,1)S(1)}, u32[]{:S(2)}, u32[]{:S(2)}) collective-permute-start(bf16[13,64,128]{2,1,0:T(8,128)(2,1)S(1)} %collective-permute-done.1.refs_1_), channel_id=1, source_target_pairs={{0,2},{1,3},{2,0},{3,1},{4,6},{5,7},{6,4},{7,5},{8,10},{9,11},{10,... | collective-permute-start | bytes 638984 | tf_op jit(solution)/shard_map/ppermute | solution.py:38
  17.7 7.3 %collective-permute-start.6 = (bf16[13,64,128]{2,1,0:T(8,128)(2,1)S(1)}, bf16[13,64,128]{2,1,0:T(8,128)(2,1)S(1)}, u32[]{:S(2)}, u32[]{:S(2)}) collective-permute-start(bf16[13,64,128]{2,1,0:T(8,128)(2,1)S(1)} %collective-permute-done.1.refs_1_), channel_id=1, source_target_pairs={{0,4},{1,5},{2,6},{3,7},{4,0},{5,1},{6,2},{7,3},{8,12},{9,13},{10,... | collective-permute-start | bytes 638984 | tf_op jit(solution)/shard_map/ppermute | solution.py:38
  19.7 6.2 %collective-permute-start.10 = (bf16[13,64,128]{2,1,0:T(8,128)(2,1)S(1)}, bf16[13,64,128]{2,1,0:T(8,128)(2,1)S(1)}, u32[]{:S(2)}, u32[]{:S(2)}) collective-permute-start(bf16[13,64,128]{2,1,0:T(8,128)(2,1)S(1)} %choose.2), channel_id=1, source_target_pairs={{0,4},{1,3},{2,6},{3,1},{4,0},{5,7},{6,2},{7,5},{8,12},{9,11},{10,... | collective-permute-start | bytes 638984 | tf_op jit(solution)/shard_map/ppermute | solution.py:38
  21.5 3.5 %collective-permute-start.7 = (bf16[512,128]{1,0:T(8,128)(2,1)S(1)}, bf16[512,128]{1,0:T(8,128)(2,1)S(1)}, u32[]{:S(2)}, u32[]{:S(2)}) collective-permute-start(bf16[512,128]{1,0:T(8,128)(2,1)S(1)} %get-tuple-element.38), channel_id=1, source_target_pairs={{1,2},{3,4},{5,6},{7,8},{9,10},{11,12},{13,14},{15,16},{17,18},{19... | collective-permute-start | bytes 393224 | tf_op jit(solution)/shard_map/ppermute | solution.py:572
  25.9 18.0 %collective-permute-start.13 = (bf16[15,64,1024]{2,1,0:T(8,128)(2,1)S(1)}, bf16[15,64,1024]{2,1,0:T(8,128)(2,1)S(1)}, u32[]{:S(2)}, u32[]{:S(2)}) collective-permute-start(bf16[15,64,1024]{2,1,0:T(8,128)(2,1)S(1)} %get-tuple-element.50), channel_id=1, source_target_pairs={{0,1},{1,0},{2,3},{3,2},{4,5},{5,4},{6,7},{7,6},{8,9},{9,8},{10,11... | collective-permute-start | bytes 5898248 | tf_op jit(solution)/shard_map/ppermute | solution.py:38
  29.0 9.9 %collective-permute-start.12 = (bf16[13,64,128]{2,1,0:T(8,128)(2,1)S(1)}, bf16[13,64,128]{2,1,0:T(8,128)(2,1)S(1)}, u32[]{:S(2)}, u32[]{:S(2)}) collective-permute-start(bf16[13,64,128]{2,1,0:T(8,128)(2,1)S(1)} %choose.3), channel_id=1, source_target_pairs={{0,4},{1,3},{2,6},{3,1},{4,0},{5,7},{6,2},{7,5},{8,12},{9,11},{10,... | collective-permute-start | bytes 638984 | tf_op jit(solution)/shard_map/ppermute | solution.py:38
  29.6 19.3 %collective-permute-start.8 = (bf16[26,64,128]{2,1,0:T(8,128)(2,1)S(1)}, bf16[26,64,128]{2,1,0:T(8,128)(2,1)S(1)}, u32[]{:S(2)}, u32[]{:S(2)}) collective-permute-start(bf16[26,64,128]{2,1,0:T(8,128)(2,1)S(1)} %join.1.refs_0_), channel_id=1, source_target_pairs={{0,2},{1,3},{2,0},{3,1},{4,6},{5,7},{6,4},{7,5},{8,10},{9,11},{10,... | collective-permute-start | bytes 1277960 | tf_op jit(solution)/shard_map/ppermute | solution.py:38
  31.5 17.4 %collective-permute-start.9 = (bf16[26,64,128]{2,1,0:T(8,128)(2,1)S(1)}, bf16[26,64,128]{2,1,0:T(8,128)(2,1)S(1)}, u32[]{:S(2)}, u32[]{:S(2)}) collective-permute-start(bf16[26,64,128]{2,1,0:T(8,128)(2,1)S(1)} %join.1.refs_0_), channel_id=1, source_target_pairs={{0,4},{1,5},{2,6},{3,7},{4,0},{5,1},{6,2},{7,3},{8,12},{9,13},{10,... | collective-permute-start | bytes 1277960 | tf_op jit(solution)/shard_map/ppermute | solution.py:38
  33.5 15.4 %collective-permute-start.11 = (bf16[13,64,128]{2,1,0:T(8,128)(2,1)S(1)}, bf16[13,64,128]{2,1,0:T(8,128)(2,1)S(1)}, u32[]{:S(2)}, u32[]{:S(2)}) collective-permute-start(bf16[13,64,128]{2,1,0:T(8,128)(2,1)S(1)} %collective-permute-done.10.refs_6_), channel_id=1, source_target_pairs={{0,24},{1,25},{2,26},{3,27},{4,28},{5,29},{6,30},{7,31},{8,0},{9,1... | collective-permute-start | bytes 638984 | tf_op jit(solution)/shard_map/ppermute | solution.py:38
  38.9 10.0 %collective-permute-start.14 = (bf16[13,64,128]{2,1,0:T(8,128)(2,1)S(1)}, bf16[13,64,128]{2,1,0:T(8,128)(2,1)S(1)}, u32[]{:S(2)}, u32[]{:S(2)}) collective-permute-start(bf16[13,64,128]{2,1,0:T(8,128)(2,1)S(1)} %collective-permute-done.12.refs_7_), channel_id=1, source_target_pairs={{0,8},{1,9},{2,10},{3,11},{4,12},{5,13},{6,14},{7,15},{8,16},{9,17... | collective-permute-start | bytes 638984 | tf_op jit(solution)/shard_map/ppermute | solution.py:38
  50.0 1.8 %collective-permute-start.15 = (f32[13,64,128]{2,1,0:T(8,128)S(1)}, f32[13,64,128]{2,1,0:T(8,128)S(1)}, u32[]{:S(2)}, u32[]{:S(2)}) collective-permute-start(f32[13,64,128]{2,1,0:T(8,128)S(1)} %far_1_2.1), channel_id=1, source_target_pairs={{0,1},{1,0},{2,3},{3,2},{4,5},{5,4},{6,7},{7,6},{8,9},{9,8},{10,11... | collective-permute-start | bytes 1277960 | tf_op jit(solution)/shard_map/ppermute | solution.py:38

commit v13 on v11

--- a/solution.py
+++ b/solution.py
@@ -84,11 +84,12 @@
 
 
 def one_hot_leaf(row, leaf_len):
-    column = jnp.broadcast_to(row, (128, leaf_len)).T
+    column = jnp.broadcast_to(row, (128, leaf_len)).T.astype(jnp.int16)
     lanes = lax.broadcasted_iota(jnp.int32, (leaf_len, 128), 1)
+    one, zero = jnp.ones((), BF), jnp.zeros((), BF)
     return jnp.concatenate(
         [
-            jnp.where(column == lanes + 128 * t, 1.0, 0.0).astype(BF)
+            jnp.where(column == (lanes + 128 * t).astype(jnp.int16), one, zero)
             for t in range(leaf_len // 128)
         ],
         axis=1,
@@ -96,8 +97,12 @@
 
 
 def one_hot_grid(row, leaf_len):
-    cells = lax.broadcasted_iota(jnp.int32, (leaf_len, leaf_len), 0)
-    return jnp.where(cells == row, 1.0, 0.0).astype(BF)
+    cells = lax.broadcasted_iota(jnp.int32, (16, leaf_len), 0).astype(jnp.int16)
+    wide = jnp.broadcast_to(row, (16, leaf_len)).astype(jnp.int16)
+    one, zero = jnp.ones((), BF), jnp.zeros((), BF)
+    return jnp.concatenate(
+        [jnp.where(cells + jnp.int16(t) == wide, one, zero) for t in range(0, leaf_len, 16)], axis=0
+    )
 
 
 def owner_tables(me, layers, owners, blocks):

time: 53 us -> 52.9 us (level)
  no operation moved by 1% of the time
where the time goes in v13:
time: 52.9 us; the launch traced here: 52.7 us
  Pallas kernels  26.6 us (50%)
  starting transfers between devices  22.9 us (43%)
  waiting for transfers between devices  3.01 us (6%)
    ppermute x15, starting transfers between devices, send(): lax.ppermute(block, 'subtree', [(d, target(d)) for d in range(count)])  22.2 us
    pallas_call x3, Pallas kernels, near_field(): pl.pallas_call(functools.partial(near_kernel, halos is not None, pair_of,...  11 us
    pallas_call x1, Pallas kernels, skeletons_of(): pl.pallas_call(functools.partial(skeleton_kernel, per, layers), name='ord...  4.69 us
    pallas_call x4, Pallas kernels, far_round(): pl.pallas_call(functools.partial(round_kernel, plane, steps, slots, [len(...  4.34 us
    pallas_call x1, Pallas kernels, dense_couplings(): pl.pallas_call(functools.partial(dense_kernel, per, slots), name='couplin...  3.99 us
    ppermute x15, waiting for transfers between devices, send(): lax.ppermute(block, 'subtree', [(d, target(d)) for d in range(count)])  3.01 us
    pallas_call x1, Pallas kernels, field(): pl.pallas_call(functools.partial(field_kernel, per), name='local_and_fiel...  2.47 us
  transfers between devices with their start and end apart: 16, of which 3 were waited for; matrix products, arithmetic and copies ran while one was open for 0% of the time, Pallas kernels for 35%

profile of v13, /device:TPU:0, one launch (start us, length us, event | category | flops | bytes accessed | tf_op | source)
XLA Modules:
  0.0 52.7 jit_solution(15481216132511839078)
XLA Ops:
  0.0 4.7 %order_and_skeleton.1 = (bf16[6144,128]{1,0:T(8,128)(2,1)S(1)}, bf16[13,64,128]{2,1,0:T(8,128)(2,1)S(1)}, bf16[512,128]{1,0:T(8,128)(2,1)S(1)}, bf16[512,128]{1,...) custom-call(s32[1]{0:T(128)} %bitcast.me_ref.refs_0_, s32[12,512]{1,0:T(8,128)} %order_ref.7, ...), custom_call_target="tpu_custom_call" | custom-call | flops 12582912 | bytes 65536 | tf_op jit(solution)/shard_map/order_and_skeleton/pallas_call | solution.py:191
  4.7 3.1 %collective-permute-start.1 = (bf16[13,64,128]{2,1,0:T(8,128)(2,1)S(1)}, bf16[13,64,128]{2,1,0:T(8,128)(2,1)S(1)}, u32[]{:S(2)}, u32[]{:S(2)}) collective-permute-start(bf16[13,64,128]{2,1,0:T(8,128)(2,1)S(1)} %get-tuple-element.34.refs_0_), channel_id=1, source_target_pairs={{0,8},{1,9},{2,10},{3,11},{4,12},{5,13},{6,14},{7,15},{8,16},{9,17... | collective-permute-start | bytes 638984 | tf_op jit(solution)/shard_map/ppermute | solution.py:38
  7.8 1.5 %collective-permute-start.2 = (bf16[13,64,128]{2,1,0:T(8,128)(2,1)S(1)}, bf16[13,64,128]{2,1,0:T(8,128)(2,1)S(1)}, u32[]{:S(2)}, u32[]{:S(2)}) collective-permute-start(bf16[13,64,128]{2,1,0:T(8,128)(2,1)S(1)} %get-tuple-element.34.refs_0_), channel_id=1, source_target_pairs={{0,2},{1,3},{2,0},{3,1},{4,6},{5,7},{6,4},{7,5},{8,10},{9,11},{10,... | collective-permute-start | bytes 638984 | tf_op jit(solution)/shard_map/ppermute | solution.py:38
  9.3 1.5 %collective-permute-start.3 = (bf16[13,64,128]{2,1,0:T(8,128)(2,1)S(1)}, bf16[13,64,128]{2,1,0:T(8,128)(2,1)S(1)}, u32[]{:S(2)}, u32[]{:S(2)}) collective-permute-start(bf16[13,64,128]{2,1,0:T(8,128)(2,1)S(1)} %get-tuple-element.34.refs_0_), channel_id=1, source_target_pairs={{0,4},{1,5},{2,6},{3,7},{4,0},{5,1},{6,2},{7,3},{8,12},{9,13},{10,... | collective-permute-start | bytes 638984 | tf_op jit(solution)/shard_map/ppermute | solution.py:38
  10.8 2.2 %collective-permute-start = (bf16[13,64,128]{2,1,0:T(8,128)(2,1)S(1)}, bf16[13,64,128]{2,1,0:T(8,128)(2,1)S(1)}, u32[]{:S(2)}, u32[]{:S(2)}) collective-permute-start(bf16[13,64,128]{2,1,0:T(8,128)(2,1)S(1)} %get-tuple-element.34.refs_0_), channel_id=1, source_target_pairs={{0,24},{1,25},{2,26},{3,27},{4,28},{5,29},{6,30},{7,31},{8,0},{9,1... | collective-permute-start | bytes 638984 | tf_op jit(solution)/shard_map/ppermute | solution.py:38
  13.1 3.6 %near_1.1 = (bf16[6144,128]{1,0:T(8,128)(2,1)S(1)}, bf16[3072,128]{1,0:T(8,128)(2,1)S(1)}) custom-call(s32[2,12]{1,0:T(2,128)S(1)} %bitcast.2, s32[12,512]{1,0:T(8,128)S(1)} %copy-done.2, bf16[512,1536]{1,0:T(8,128)(2,1)S(1)} %copy-done, bf16[12,64,512]{2,1,0:T(8,128)(2,1)S(1)} %copy-done.1, bf16[6144,128]{1,0:T(8,128)(2,1)S(1)} %get-tuple-element.53.ordered_ref), custom_call_target="tpu_custom_call" | custom-call | flops 20971520 | bytes 32768 | tf_op jit(solution)/shard_map/near_1/pallas_call | solution.py:469
  16.8 1.0 %collective-permute-start.5 = (bf16[13,64,128]{2,1,0:T(8,128)(2,1)S(1)}, bf16[13,64,128]{2,1,0:T(8,128)(2,1)S(1)}, u32[]{:S(2)}, u32[]{:S(2)}) collective-permute-start(bf16[13,64,128]{2,1,0:T(8,128)(2,1)S(1)} %collective-permute-done.1.refs_1_), channel_id=1, source_target_pairs={{0,2},{1,3},{2,0},{3,1},{4,6},{5,7},{6,4},{7,5},{8,10},{9,11},{10,... | collective-permute-start | bytes 638984 | tf_op jit(solution)/shard_map/ppermute | solution.py:38
  17.7 1.6 %collective-permute-start.6 = (bf16[13,64,128]{2,1,0:T(8,128)(2,1)S(1)}, bf16[13,64,128]{2,1,0:T(8,128)(2,1)S(1)}, u32[]{:S(2)}, u32[]{:S(2)}) collective-permute-start(bf16[13,64,128]{2,1,0:T(8,128)(2,1)S(1)} %collective-permute-done.1.refs_1_), channel_id=1, source_target_pairs={{0,4},{1,5},{2,6},{3,7},{4,0},{5,1},{6,2},{7,3},{8,12},{9,13},{10,... | collective-permute-start | bytes 638984 | tf_op jit(solution)/shard_map/ppermute | solution.py:38
  19.7 2.2 %collective-permute-start.10 = (bf16[13,64,128]{2,1,0:T(8,128)(2,1)S(1)}, bf16[13,64,128]{2,1,0:T(8,128)(2,1)S(1)}, u32[]{:S(2)}, u32[]{:S(2)}) collective-permute-start(bf16[13,64,128]{2,1,0:T(8,128)(2,1)S(1)} %choose.2), channel_id=1, source_target_pairs={{0,4},{1,3},{2,6},{3,1},{4,0},{5,7},{6,2},{7,5},{8,12},{9,11},{10,... | collective-permute-start | bytes 638984 | tf_op jit(solution)/shard_map/ppermute | solution.py:38
  21.9 0.7 %collective-permute-start.7 = (bf16[512,128]{1,0:T(8,128)(2,1)S(1)}, bf16[512,128]{1,0:T(8,128)(2,1)S(1)}, u32[]{:S(2)}, u32[]{:S(2)}) collective-permute-start(bf16[512,128]{1,0:T(8,128)(2,1)S(1)} %get-tuple-element.44), channel_id=1, source_target_pairs={{1,2},{3,4},{5,6},{7,8},{9,10},{11,12},{13,14},{15,16},{17,18},{19... | collective-permute-start | bytes 393224 | tf_op jit(solution)/shard_map/ppermute | solution.py:575
  22.6 4.0 %couplings_by_owner.1 = (bf16[13,64,1024]{2,1,0:T(8,128)(2,1)S(1)}, bf16[15,64,1024]{2,1,0:T(8,128)(2,1)S(1)}, bf16[12,64,64]{2,1,0:T(8,128)(2,1)S(1)}) custom-call(s32[16,128]{1,0:T(8,128)S(1)} %get-tuple-element.40.entry_ref, s32[16,128]{1,0:T(8,128)S(1)} %get-tuple-element.33.block_ref.at_ref, bf16[512,128]{1,0:T(8,128)(2,1)S(1)} %get-tuple-element.41.inner_ref, ...), custom_call_target="tpu_custom_call" | custom-call | bytes 131072 | tf_op jit(solution)/shard_map/couplings_by_owner/pallas_call | solution.py:312
  26.7 3.1 %collective-permute-start.13 = (bf16[15,64,1024]{2,1,0:T(8,128)(2,1)S(1)}, bf16[15,64,1024]{2,1,0:T(8,128)(2,1)S(1)}, u32[]{:S(2)}, u32[]{:S(2)}) collective-permute-start(bf16[15,64,1024]{2,1,0:T(8,128)(2,1)S(1)} %get-tuple-element.54), channel_id=1, source_target_pairs={{0,1},{1,0},{2,3},{3,2},{4,5},{5,4},{6,7},{7,6},{8,9},{9,8},{10,11... | collective-permute-start | bytes 5898248 | tf_op jit(solution)/shard_map/ppermute | solution.py:38
  30.1 2.8 %collective-permute-start.8 = (bf16[26,64,128]{2,1,0:T(8,128)(2,1)S(1)}, bf16[26,64,128]{2,1,0:T(8,128)(2,1)S(1)}, u32[]{:S(2)}, u32[]{:S(2)}) collective-permute-start(bf16[26,64,128]{2,1,0:T(8,128)(2,1)S(1)} %join.1.refs_0_), channel_id=1, source_target_pairs={{0,2},{1,3},{2,0},{3,1},{4,6},{5,7},{6,4},{7,5},{8,10},{9,11},{10,... | collective-permute-start | bytes 1277960 | tf_op jit(solution)/shard_map/ppermute | solution.py:38
  32.8 0.7 %collective-permute-start.9 = (bf16[26,64,128]{2,1,0:T(8,128)(2,1)S(1)}, bf16[26,64,128]{2,1,0:T(8,128)(2,1)S(1)}, u32[]{:S(2)}, u32[]{:S(2)}) collective-permute-start(bf16[26,64,128]{2,1,0:T(8,128)(2,1)S(1)} %join.1.refs_0_), channel_id=1, source_target_pairs={{0,4},{1,5},{2,6},{3,7},{4,0},{5,1},{6,2},{7,3},{8,12},{9,13},{10,... | collective-permute-start | bytes 1277960 | tf_op jit(solution)/shard_map/ppermute | solution.py:38
  33.5 1.9 %collective-permute-start.11 = (bf16[13,64,128]{2,1,0:T(8,128)(2,1)S(1)}, bf16[13,64,128]{2,1,0:T(8,128)(2,1)S(1)}, u32[]{:S(2)}, u32[]{:S(2)}) collective-permute-start(bf16[13,64,128]{2,1,0:T(8,128)(2,1)S(1)} %collective-permute-done.10.refs_6_), channel_id=1, source_target_pairs={{0,24},{1,25},{2,26},{3,27},{4,28},{5,29},{6,30},{7,31},{8,0},{9,1... | collective-permute-start | bytes 638984 | tf_op jit(solution)/shard_map/ppermute | solution.py:38
  35.4 3.6 %near_3.1 = (bf16[6144,128]{1,0:T(8,128)(2,1)S(1)}, bf16[3072,128]{1,0:T(8,128)(2,1)S(1)}) custom-call(s32[2,12]{1,0:T(2,128)S(1)} %bitcast.3, s32[12,512]{1,0:T(8,128)S(1)} %copy-done.2, bf16[512,1536]{1,0:T(8,128)(2,1)S(1)} %copy-done, bf16[12,64,512]{2,1,0:T(8,128)(2,1)S(1)} %copy-done.1, ...), custom_call_target="tpu_custom_call", output_to_operand_aliasing={{0}: (5, {}), {1}: (6, {})} | custom-call | flops 20971520 | bytes 32768 | tf_op jit(solution)/shard_map/near_3/pallas_call | solution.py:469
  39.3 1.1 %far_0_0.1.refs_6_ = f32[13,64,128]{2,1,0:T(8,128)S(1)} custom-call(s32[16,128]{1,0:T(8,128)S(1)} %get-tuple-element.33.block_ref.at_ref, bf16[13,64,128]{2,1,0:T(8,128)(2,1)S(1)} %get-tuple-element.34.refs_0_, bf16[13,64,128]{2,1,0:T(8,128)(2,1)S(1)} %collective-permute-done.1.refs_1_, bf16[13,64,128]{2,1,0:T(8,128)(2,1)S(1)} %collective-permute-done.2.x_ref.refs_2_, ...), custom_call_target="tpu_custom_call" | custom-call | flops 1703936 | bytes 16384 | tf_op jit(solution)/shard_map/far_0_0/pallas_call | solution.py:370
  40.4 3.9 %near_0.1 = (bf16[6144,128]{1,0:T(8,128)(2,1)S(1)}, bf16[3072,128]{1,0:T(8,128)(2,1)S(1)}, s32[16,128]{1,0:T(8,128)S(1)}) custom-call(s32[2,12]{1,0:T(2,128)S(1)} %bitcast.4, s32[12,512]{1,0:T(8,128)S(1)} %copy-done.2, bf16[512,1536]{1,0:T(8,128)(2,1)S(1)} %copy-done, ...), custom_call_target="tpu_custom_call", output_to_operand_aliasing={{0}: (9, {}), {1}: (10, {})} | custom-call | flops 20971520 | bytes 32768 | tf_op jit(solution)/shard_map/near_0/pallas_call | solution.py:469
  44.3 1.1 %far_1_0.1.refs_6_ = f32[13,64,128]{2,1,0:T(8,128)S(1)} custom-call(s32[16,128]{1,0:T(8,128)S(1)} %get-tuple-element.56.at_ref, bf16[13,64,128]{2,1,0:T(8,128)(2,1)S(1)} %get-tuple-element.34.refs_0_, bf16[13,64,128]{2,1,0:T(8,128)(2,1)S(1)} %collective-permute-done.1.refs_1_, bf16[13,64,128]{2,1,0:T(8,128)(2,1)S(1)} %collective-permute-done.2.x_ref.refs_2_, ...), custom_call_target="tpu_custom_call" | custom-call | flops 1703936 | bytes 16384 | tf_op jit(solution)/shard_map/far_1_0/pallas_call | solution.py:370
  45.4 1.9 %collective-permute-done.14.refs_4_ = bf16[13,64,128]{2,1,0:T(8,128)(2,1)S(1)} collective-permute-done((bf16[13,64,128]{2,1,0:T(8,128)(2,1)S(1)}, bf16[13,64,128]{2,1,0:T(8,128)(2,1)S(1)}, u32[]{:S(2)}, u32[]{:S(2)}) %collective-permute-start.14) | collective-permute-done | bytes 213024 | tf_op jit(solution)/shard_map/ppermute | solution.py:38
  47.3 1.1 %far_1_2.1 = f32[13,64,128]{2,1,0:T(8,128)S(1)} custom-call(s32[16,128]{1,0:T(8,128)S(1)} %get-tuple-element.56.at_ref, bf16[26,64,128]{2,1,0:T(8,128)(2,1)S(1)} %join.1.refs_0_, bf16[26,64,128]{2,1,0:T(8,128)(2,1)S(1)} %collective-permute-done.8.refs_1_, bf16[26,64,128]{2,1,0:T(8,128)(2,1)S(1)} %collective-permute-done.9.refs_2_, ...), custom_call_target="tpu_custom_call" | custom-call | flops 1703936 | bytes 16384 | tf_op jit(solution)/shard_map/far_1_2/pallas_call | solution.py:370
  48.5 1.1 %far_0_2.1.own_ref = f32[13,64,128]{2,1,0:T(8,128)S(1)} custom-call(s32[16,128]{1,0:T(8,128)S(1)} %get-tuple-element.33.block_ref.at_ref, bf16[26,64,128]{2,1,0:T(8,128)(2,1)S(1)} %join.1.refs_0_, bf16[26,64,128]{2,1,0:T(8,128)(2,1)S(1)} %collective-permute-done.8.refs_1_, bf16[26,64,128]{2,1,0:T(8,128)(2,1)S(1)} %collective-permute-done.9.refs_2_, ...), custom_call_target="tpu_custom_call" | custom-call | flops 1703936 | bytes 16384 | tf_op jit(solution)/shard_map/far_0_2/pallas_call | solution.py:370
  49.6 0.7 %collective-permute-done.15.other_ref = f32[13,64,128]{2,1,0:T(8,128)S(1)} collective-permute-done((f32[13,64,128]{2,1,0:T(8,128)S(1)}, f32[13,64,128]{2,1,0:T(8,128)S(1)}, u32[]{:S(2)}, u32[]{:S(2)}) %collective-permute-start.15) | collective-permute-done | bytes 426016 | tf_op jit(solution)/shard_map/ppermute | solution.py:38
  50.2 2.5 %local_and_field.1 = bf16[6144,128]{1,0:T(8,128)(2,1)} custom-call(f32[13,64,128]{2,1,0:T(8,128)S(1)} %far_0_2.1.own_ref, f32[13,64,128]{2,1,0:T(8,128)S(1)} %collective-permute-done.15.other_ref, bf16[12,64,64]{2,1,0:T(8,128)(2,1)S(1)} %get-tuple-element.58.turned_transfer_ref, bf16[6144,128]{1,0:T(8,128)(2,1)S(1)} %get-tuple-element.59.near_ref, ...), custom_call_target="tpu_custom_call" | custom-call | flops 1572864 | bytes 65536 | tf_op jit(solution)/shard_map/local_and_field/pallas_call | solution.py:524
  (29 shorter events, 1.2 us)
Async XLA Ops:
  0.0 13.1 %copy-start = (bf16[512,1536]{1,0:T(8,128)(2,1)S(1)}, bf16[512,1536]{1,0:T(8,128)(2,1)}, u32[]{:S(2)}) copy-start(bf16[512,1536]{1,0:T(8,128)(2,1)} %constant.6.clone.table_ref) | copy-start | bytes 4718596
  0.0 13.1 %copy-start.1 = (bf16[12,64,512]{2,1,0:T(8,128)(2,1)S(1)}, bf16[12,64,512]{2,1,0:T(8,128)(2,1)}, u32[]{:S(2)}) copy-start(bf16[12,64,512]{2,1,0:T(8,128)(2,1)} %basis_ref.7) | copy-start | bytes 2359300
  0.0 13.1 %copy-start.2 = (s32[12,512]{1,0:T(8,128)S(1)}, s32[12,512]{1,0:T(8,128)}, u32[]{:S(2)}) copy-start(s32[12,512]{1,0:T(8,128)} %order_ref.7) | copy-start | bytes 73732
  0.0 13.1 %copy-start.3 = (s32[12,2]{0,1:T(2,128)S(1)}, s32[12,2]{0,1:T(2,128)}, u32[]{:S(2)}) copy-start(s32[12,2]{0,1:T(2,128)} %param.17) | copy-start | bytes 292
  4.7 12.0 %collective-permute-start.1 = (bf16[13,64,128]{2,1,0:T(8,128)(2,1)S(1)}, bf16[13,64,128]{2,1,0:T(8,128)(2,1)S(1)}, u32[]{:S(2)}, u32[]{:S(2)}) collective-permute-start(bf16[13,64,128]{2,1,0:T(8,128)(2,1)S(1)} %get-tuple-element.34.refs_0_), channel_id=1, source_target_pairs={{0,8},{1,9},{2,10},{3,11},{4,12},{5,13},{6,14},{7,15},{8,16},{9,17... | collective-permute-start | bytes 638984 | tf_op jit(solution)/shard_map/ppermute | solution.py:38
  7.8 8.9 %collective-permute-start.2 = (bf16[13,64,128]{2,1,0:T(8,128)(2,1)S(1)}, bf16[13,64,128]{2,1,0:T(8,128)(2,1)S(1)}, u32[]{:S(2)}, u32[]{:S(2)}) collective-permute-start(bf16[13,64,128]{2,1,0:T(8,128)(2,1)S(1)} %get-tuple-element.34.refs_0_), channel_id=1, source_target_pairs={{0,2},{1,3},{2,0},{3,1},{4,6},{5,7},{6,4},{7,5},{8,10},{9,11},{10,... | collective-permute-start | bytes 638984 | tf_op jit(solution)/shard_map/ppermute | solution.py:38
  9.3 7.4 %collective-permute-start.3 = (bf16[13,64,128]{2,1,0:T(8,128)(2,1)S(1)}, bf16[13,64,128]{2,1,0:T(8,128)(2,1)S(1)}, u32[]{:S(2)}, u32[]{:S(2)}) collective-permute-start(bf16[13,64,128]{2,1,0:T(8,128)(2,1)S(1)} %get-tuple-element.34.refs_0_), channel_id=1, source_target_pairs={{0,4},{1,5},{2,6},{3,7},{4,0},{5,1},{6,2},{7,3},{8,12},{9,13},{10,... | collective-permute-start | bytes 638984 | tf_op jit(solution)/shard_map/ppermute | solution.py:38
  10.8 8.9 %collective-permute-start = (bf16[13,64,128]{2,1,0:T(8,128)(2,1)S(1)}, bf16[13,64,128]{2,1,0:T(8,128)(2,1)S(1)}, u32[]{:S(2)}, u32[]{:S(2)}) collective-permute-start(bf16[13,64,128]{2,1,0:T(8,128)(2,1)S(1)} %get-tuple-element.34.refs_0_), channel_id=1, source_target_pairs={{0,24},{1,25},{2,26},{3,27},{4,28},{5,29},{6,30},{7,31},{8,0},{9,1... | collective-permute-start | bytes 638984 | tf_op jit(solution)/shard_map/ppermute | solution.py:38
  16.7 9.9 %collective-permute-start.4 = (bf16[13,64,128]{2,1,0:T(8,128)(2,1)S(1)}, bf16[13,64,128]{2,1,0:T(8,128)(2,1)S(1)}, u32[]{:S(2)}, u32[]{:S(2)}) collective-permute-start(bf16[13,64,128]{2,1,0:T(8,128)(2,1)S(1)} %collective-permute-done.1.refs_1_), channel_id=1, source_target_pairs={{0,8},{1,9},{2,10},{3,11},{4,12},{5,13},{6,14},{7,15},{8,16},{9,17... | collective-permute-start | bytes 638984 | tf_op jit(solution)/shard_map/ppermute | solution.py:38
  16.8 9.9 %collective-permute-start.5 = (bf16[13,64,128]{2,1,0:T(8,128)(2,1)S(1)}, bf16[13,64,128]{2,1,0:T(8,128)(2,1)S(1)}, u32[]{:S(2)}, u32[]{:S(2)}) collective-permute-start(bf16[13,64,128]{2,1,0:T(8,128)(2,1)S(1)} %collective-permute-done.1.refs_1_), channel_id=1, source_target_pairs={{0,2},{1,3},{2,0},{3,1},{4,6},{5,7},{6,4},{7,5},{8,10},{9,11},{10,... | collective-permute-start | bytes 638984 | tf_op jit(solution)/shard_map/ppermute | solution.py:38
  17.7 8.9 %collective-permute-start.6 = (bf16[13,64,128]{2,1,0:T(8,128)(2,1)S(1)}, bf16[13,64,128]{2,1,0:T(8,128)(2,1)S(1)}, u32[]{:S(2)}, u32[]{:S(2)}) collective-permute-start(bf16[13,64,128]{2,1,0:T(8,128)(2,1)S(1)} %collective-permute-done.1.refs_1_), channel_id=1, source_target_pairs={{0,4},{1,5},{2,6},{3,7},{4,0},{5,1},{6,2},{7,3},{8,12},{9,13},{10,... | collective-permute-start | bytes 638984 | tf_op jit(solution)/shard_map/ppermute | solution.py:38
  19.7 7.0 %collective-permute-start.10 = (bf16[13,64,128]{2,1,0:T(8,128)(2,1)S(1)}, bf16[13,64,128]{2,1,0:T(8,128)(2,1)S(1)}, u32[]{:S(2)}, u32[]{:S(2)}) collective-permute-start(bf16[13,64,128]{2,1,0:T(8,128)(2,1)S(1)} %choose.2), channel_id=1, source_target_pairs={{0,4},{1,3},{2,6},{3,1},{4,0},{5,7},{6,2},{7,5},{8,12},{9,11},{10,... | collective-permute-start | bytes 638984 | tf_op jit(solution)/shard_map/ppermute | solution.py:38
  21.9 4.7 %collective-permute-start.7 = (bf16[512,128]{1,0:T(8,128)(2,1)S(1)}, bf16[512,128]{1,0:T(8,128)(2,1)S(1)}, u32[]{:S(2)}, u32[]{:S(2)}) collective-permute-start(bf16[512,128]{1,0:T(8,128)(2,1)S(1)} %get-tuple-element.44), channel_id=1, source_target_pairs={{1,2},{3,4},{5,6},{7,8},{9,10},{11,12},{13,14},{15,16},{17,18},{19... | collective-permute-start | bytes 393224 | tf_op jit(solution)/shard_map/ppermute | solution.py:575
  26.7 13.6 %collective-permute-start.13 = (bf16[15,64,1024]{2,1,0:T(8,128)(2,1)S(1)}, bf16[15,64,1024]{2,1,0:T(8,128)(2,1)S(1)}, u32[]{:S(2)}, u32[]{:S(2)}) collective-permute-start(bf16[15,64,1024]{2,1,0:T(8,128)(2,1)S(1)} %get-tuple-element.54), channel_id=1, source_target_pairs={{0,1},{1,0},{2,3},{3,2},{4,5},{5,4},{6,7},{7,6},{8,9},{9,8},{10,11... | collective-permute-start | bytes 5898248 | tf_op jit(solution)/shard_map/ppermute | solution.py:38
  29.8 9.1 %collective-permute-start.12 = (bf16[13,64,128]{2,1,0:T(8,128)(2,1)S(1)}, bf16[13,64,128]{2,1,0:T(8,128)(2,1)S(1)}, u32[]{:S(2)}, u32[]{:S(2)}) collective-permute-start(bf16[13,64,128]{2,1,0:T(8,128)(2,1)S(1)} %choose.3), channel_id=1, source_target_pairs={{0,4},{1,3},{2,6},{3,1},{4,0},{5,7},{6,2},{7,5},{8,12},{9,11},{10,... | collective-permute-start | bytes 638984 | tf_op jit(solution)/shard_map/ppermute | solution.py:38
  30.1 17.2 %collective-permute-start.8 = (bf16[26,64,128]{2,1,0:T(8,128)(2,1)S(1)}, bf16[26,64,128]{2,1,0:T(8,128)(2,1)S(1)}, u32[]{:S(2)}, u32[]{:S(2)}) collective-permute-start(bf16[26,64,128]{2,1,0:T(8,128)(2,1)S(1)} %join.1.refs_0_), channel_id=1, source_target_pairs={{0,2},{1,3},{2,0},{3,1},{4,6},{5,7},{6,4},{7,5},{8,10},{9,11},{10,... | collective-permute-start | bytes 1277960 | tf_op jit(solution)/shard_map/ppermute | solution.py:38
  32.8 14.4 %collective-permute-start.9 = (bf16[26,64,128]{2,1,0:T(8,128)(2,1)S(1)}, bf16[26,64,128]{2,1,0:T(8,128)(2,1)S(1)}, u32[]{:S(2)}, u32[]{:S(2)}) collective-permute-start(bf16[26,64,128]{2,1,0:T(8,128)(2,1)S(1)} %join.1.refs_0_), channel_id=1, source_target_pairs={{0,4},{1,5},{2,6},{3,7},{4,0},{5,1},{6,2},{7,3},{8,12},{9,13},{10,... | collective-permute-start | bytes 1277960 | tf_op jit(solution)/shard_map/ppermute | solution.py:38
  33.5 11.8 %collective-permute-start.11 = (bf16[13,64,128]{2,1,0:T(8,128)(2,1)S(1)}, bf16[13,64,128]{2,1,0:T(8,128)(2,1)S(1)}, u32[]{:S(2)}, u32[]{:S(2)}) collective-permute-start(bf16[13,64,128]{2,1,0:T(8,128)(2,1)S(1)} %collective-permute-done.10.refs_6_), channel_id=1, source_target_pairs={{0,24},{1,25},{2,26},{3,27},{4,28},{5,29},{6,30},{7,31},{8,0},{9,1... | collective-permute-start | bytes 638984 | tf_op jit(solution)/shard_map/ppermute | solution.py:38
  39.0 8.3 %collective-permute-start.14 = (bf16[13,64,128]{2,1,0:T(8,128)(2,1)S(1)}, bf16[13,64,128]{2,1,0:T(8,128)(2,1)S(1)}, u32[]{:S(2)}, u32[]{:S(2)}) collective-permute-start(bf16[13,64,128]{2,1,0:T(8,128)(2,1)S(1)} %collective-permute-done.12.refs_7_), channel_id=1, source_target_pairs={{0,8},{1,9},{2,10},{3,11},{4,12},{5,13},{6,14},{7,15},{8,16},{9,17... | collective-permute-start | bytes 638984 | tf_op jit(solution)/shard_map/ppermute | solution.py:38
  48.4 1.8 %collective-permute-start.15 = (f32[13,64,128]{2,1,0:T(8,128)S(1)}, f32[13,64,128]{2,1,0:T(8,128)S(1)}, u32[]{:S(2)}, u32[]{:S(2)}) collective-permute-start(f32[13,64,128]{2,1,0:T(8,128)S(1)} %far_1_2.1), channel_id=1, source_target_pairs={{0,1},{1,0},{2,3},{3,2},{4,5},{5,4},{6,7},{7,6},{8,9},{9,8},{10,11... | collective-permute-start | bytes 1277960 | tf_op jit(solution)/shard_map/ppermute | solution.py:38

commit v14 on v13

--- a/solution.py
+++ b/solution.py
@@ -84,7 +84,7 @@
 
 
 def one_hot_leaf(row, leaf_len):
-    column = jnp.broadcast_to(row, (128, leaf_len)).T.astype(jnp.int16)
+    column = jnp.broadcast_to(row, (128, leaf_len)).astype(jnp.int16).T
     lanes = lax.broadcasted_iota(jnp.int32, (leaf_len, 128), 1)
     one, zero = jnp.ones((), BF), jnp.zeros((), BF)
     return jnp.concatenate(
@@ -155,7 +155,8 @@
     across = jnp.concatenate([transfer_ref[i] for i in range(per)], axis=1)
     root_ref[...] += dot(across, jnp.concatenate(skeletons, axis=0))
     for i in range(per):
-        ordered_ref[i * leaf_len:(i + 1) * leaf_len, :] = ordered[i]
+        at = pl.multiple_of((step * per + i) * leaf_len, leaf_len)
+        ordered_ref[pl.ds(at, leaf_len), :] = ordered[i]
         shared_ref[pl.ds(step * per + i + 1, 1)] = skeletons[i][None]
 
     even = me_ref[0] % 2 == 0
@@ -201,14 +202,7 @@
             pl.BlockSpec((leaves, entries), lambda s: (0, 0)),
             pl.BlockSpec((leaves, entries), lambda s: (0, 0)),
         ],
-        out_specs=[
-            pl.BlockSpec((per * leaf_len, fields), lambda s: (s, 0)),
-            pl.BlockSpec((leaves + 1, rank, fields), lambda s: (0, 0, 0)),
-            pl.BlockSpec((leaf_len, fields), lambda s: (0, 0)),
-            pl.BlockSpec((leaf_len, fields), lambda s: (0, 0)),
-            pl.BlockSpec((16, 128), lambda s: (0, 0)),
-            pl.BlockSpec((16, 128), lambda s: (0, 0)),
-        ],
+        out_specs=[whole()] * 6,
         out_shape=[
             jax.ShapeDtypeStruct((leaves * leaf_len, fields), BF),
             jax.ShapeDtypeStruct((leaves + 1, rank, fields), BF),
@@ -321,11 +315,7 @@
             pl.BlockSpec(top_coupling.shape, lambda s: (0, 0, 0, 0)),
             pl.BlockSpec((per, rank, rank), lambda s: (s, 0, 0)),
         ],
-        out_specs=[
-            pl.BlockSpec(own, lambda s: (0, 0, 0)),
-            pl.BlockSpec(other, lambda s: (0, 0, 0)),
-            pl.BlockSpec(transfer.shape, lambda s: (0, 0, 0)),
-        ],
+        out_specs=[whole()] * 3,
         out_shape=[
             jax.ShapeDtypeStruct(own, BF),
             jax.ShapeDtypeStruct(other, BF),
@@ -424,12 +414,13 @@
     turned = []
     for i in range(2):
         hot = one_hot_grid(order_ref[pl.ds(2 * pair + i, 1), :], leaf_len)
-        at = pl.ds(i * leaf_len, leaf_len)
+        at = pl.ds(pl.multiple_of((2 * pair + i) * leaf_len, leaf_len), leaf_len)
         both = jnp.concatenate([near[:, i * fields:(i + 1) * fields], basis_ref[2 * pair + i].T], axis=1)
         moved = dot(hot, both).astype(BF)
         near_ref[at, :] = moved[:, :fields]
         turned.append(moved[:, fields:])
-    turned_ref[...] = jnp.concatenate(turned, axis=1)
+    at = pl.multiple_of(pair * leaf_len, leaf_len)
+    turned_ref[pl.ds(at, leaf_len), :] = jnp.concatenate(turned, axis=1)
 
 
 def near_field(pairs, near_list, leaf_order, tables, basis, ordered, halos=None, filled=None):
@@ -464,17 +455,14 @@
         extra = [(16, 128)]
     if filled is not None:
         aliases = {len(args): 0, len(args) + 1: 1}
-        in_specs += [pl.BlockSpec(memory_space=pl.ANY)] * 2
+        in_specs += [whole()] * 2
         args += list(filled)
     return pl.pallas_call(
         functools.partial(near_kernel, halos is not None, pair_of, last),
         name="near_" + str(pairs[0]),
         grid=(len(pairs),),
         in_specs=in_specs,
-        out_specs=[
-            pl.BlockSpec((2 * leaf_len, fields), lambda s: (pair_of(s), 0)),
-            pl.BlockSpec((leaf_len, 2 * rank), lambda s: (pair_of(s), 0)),
-        ] + [pl.BlockSpec(shape, lambda s: (0, 0)) for shape in extra],
+        out_specs=[whole()] * (2 + len(extra)),
         out_shape=[
             jax.ShapeDtypeStruct((leaves * leaf_len, fields), BF),
             jax.ShapeDtypeStruct((leaves // 2 * leaf_len, 2 * rank), BF),
@@ -517,7 +505,7 @@
             out_ref[rows, :] = (near + far[:, i * fields:(i + 1) * fields]).astype(BF)
 
 
-def field(own, other, turned_transfer, near, turned, per=4):
+def field(own, other, turned_transfer, near, turned, per=2):
     leaves, rank, _ = turned_transfer.shape
     fields = near.shape[1]
     leaf_len = near.shape[0] // leaves

time: 52.9 us -> 53.9 us (1.019)
  Pallas kernels: 26.6 us -> 27.7 us
    pallas_call x1, Pallas kernels: 2.47 us -> 3.56 us  [field(): pl.pallas_call(functools.partial(field_kernel, per), name='local_and_fiel...]
  transfers between devices with their start and end apart: 16 -> 16, of which waited for: 3 -> 3; matrix products, arithmetic and copies ran while one was open for 0% -> 0% of each run, Pallas kernels for 35% -> 34%
where the time goes in v14:
time: 53.9 us; the launch traced here: 53.8 us
  Pallas kernels  27.7 us (51%)
  starting transfers between devices  22.8 us (42%)
  waiting for transfers between devices  3.11 us (6%)
    ppermute x15, starting transfers between devices, send(): lax.ppermute(block, 'subtree', [(d, target(d)) for d in range(count)])  22.1 us
    pallas_call x3, Pallas kernels, near_field(): pl.pallas_call(functools.partial(near_kernel, halos is not None, pair_of,...  11 us
    pallas_call x1, Pallas kernels, skeletons_of(): pl.pallas_call(functools.partial(skeleton_kernel, per, layers), name='ord...  4.66 us
    pallas_call x4, Pallas kernels, far_round(): pl.pallas_call(functools.partial(round_kernel, plane, steps, slots, [len(...  4.34 us
    pallas_call x1, Pallas kernels, dense_couplings(): pl.pallas_call(functools.partial(dense_kernel, per, slots), name='couplin...  3.99 us
    pallas_call x1, Pallas kernels, field(): pl.pallas_call(functools.partial(field_kernel, per), name='local_and_fiel...  3.56 us
    ppermute x15, waiting for transfers between devices, send(): lax.ppermute(block, 'subtree', [(d, target(d)) for d in range(count)])  3.1 us
  transfers between devices with their start and end apart: 16, of which 3 were waited for; matrix products, arithmetic and copies ran while one was open for 0% of the time, Pallas kernels for 34%

profile of v14, /device:TPU:0, one launch (start us, length us, event | category | flops | bytes accessed | tf_op | source)
XLA Modules:
  0.0 53.8 jit_solution(11338179290991327881)
XLA Ops:
  0.0 4.7 %order_and_skeleton.1 = (bf16[6144,128]{1,0:T(8,128)(2,1)S(1)}, bf16[13,64,128]{2,1,0:T(8,128)(2,1)S(1)}, bf16[512,128]{1,0:T(8,128)(2,1)S(1)}, bf16[512,128]{1,...) custom-call(s32[1]{0:T(128)} %bitcast.me_ref.refs_0_, s32[12,512]{1,0:T(8,128)} %order_ref.7, ...), custom_call_target="tpu_custom_call" | custom-call | flops 12582912 | bytes 65536 | tf_op jit(solution)/shard_map/order_and_skeleton/pallas_call | solution.py:192
  4.7 3.1 %collective-permute-start.1 = (bf16[13,64,128]{2,1,0:T(8,128)(2,1)S(1)}, bf16[13,64,128]{2,1,0:T(8,128)(2,1)S(1)}, u32[]{:S(2)}, u32[]{:S(2)}) collective-permute-start(bf16[13,64,128]{2,1,0:T(8,128)(2,1)S(1)} %get-tuple-element.34.refs_0_), channel_id=1, source_target_pairs={{0,8},{1,9},{2,10},{3,11},{4,12},{5,13},{6,14},{7,15},{8,16},{9,17... | collective-permute-start | bytes 638984 | tf_op jit(solution)/shard_map/ppermute | solution.py:38
  7.8 1.5 %collective-permute-start.2 = (bf16[13,64,128]{2,1,0:T(8,128)(2,1)S(1)}, bf16[13,64,128]{2,1,0:T(8,128)(2,1)S(1)}, u32[]{:S(2)}, u32[]{:S(2)}) collective-permute-start(bf16[13,64,128]{2,1,0:T(8,128)(2,1)S(1)} %get-tuple-element.34.refs_0_), channel_id=1, source_target_pairs={{0,2},{1,3},{2,0},{3,1},{4,6},{5,7},{6,4},{7,5},{8,10},{9,11},{10,... | collective-permute-start | bytes 638984 | tf_op jit(solution)/shard_map/ppermute | solution.py:38
  9.3 1.5 %collective-permute-start.3 = (bf16[13,64,128]{2,1,0:T(8,128)(2,1)S(1)}, bf16[13,64,128]{2,1,0:T(8,128)(2,1)S(1)}, u32[]{:S(2)}, u32[]{:S(2)}) collective-permute-start(bf16[13,64,128]{2,1,0:T(8,128)(2,1)S(1)} %get-tuple-element.34.refs_0_), channel_id=1, source_target_pairs={{0,4},{1,5},{2,6},{3,7},{4,0},{5,1},{6,2},{7,3},{8,12},{9,13},{10,... | collective-permute-start | bytes 638984 | tf_op jit(solution)/shard_map/ppermute | solution.py:38
  10.8 2.3 %collective-permute-start = (bf16[13,64,128]{2,1,0:T(8,128)(2,1)S(1)}, bf16[13,64,128]{2,1,0:T(8,128)(2,1)S(1)}, u32[]{:S(2)}, u32[]{:S(2)}) collective-permute-start(bf16[13,64,128]{2,1,0:T(8,128)(2,1)S(1)} %get-tuple-element.34.refs_0_), channel_id=1, source_target_pairs={{0,24},{1,25},{2,26},{3,27},{4,28},{5,29},{6,30},{7,31},{8,0},{9,1... | collective-permute-start | bytes 638984 | tf_op jit(solution)/shard_map/ppermute | solution.py:38
  13.0 3.6 %near_1.1 = (bf16[6144,128]{1,0:T(8,128)(2,1)S(1)}, bf16[3072,128]{1,0:T(8,128)(2,1)S(1)}) custom-call(s32[2,12]{1,0:T(2,128)S(1)} %bitcast.2, s32[12,512]{1,0:T(8,128)S(1)} %copy-done.2, bf16[512,1536]{1,0:T(8,128)(2,1)S(1)} %copy-done, bf16[12,64,512]{2,1,0:T(8,128)(2,1)S(1)} %copy-done.1, bf16[6144,128]{1,0:T(8,128)(2,1)S(1)} %get-tuple-element.53.ordered_ref), custom_call_target="tpu_custom_call" | custom-call | flops 20971520 | bytes 32768 | tf_op jit(solution)/shard_map/near_1/pallas_call | solution.py:460
  16.7 1.0 %collective-permute-start.5 = (bf16[13,64,128]{2,1,0:T(8,128)(2,1)S(1)}, bf16[13,64,128]{2,1,0:T(8,128)(2,1)S(1)}, u32[]{:S(2)}, u32[]{:S(2)}) collective-permute-start(bf16[13,64,128]{2,1,0:T(8,128)(2,1)S(1)} %collective-permute-done.1.refs_1_), channel_id=1, source_target_pairs={{0,2},{1,3},{2,0},{3,1},{4,6},{5,7},{6,4},{7,5},{8,10},{9,11},{10,... | collective-permute-start | bytes 638984 | tf_op jit(solution)/shard_map/ppermute | solution.py:38
  17.7 1.6 %collective-permute-start.6 = (bf16[13,64,128]{2,1,0:T(8,128)(2,1)S(1)}, bf16[13,64,128]{2,1,0:T(8,128)(2,1)S(1)}, u32[]{:S(2)}, u32[]{:S(2)}) collective-permute-start(bf16[13,64,128]{2,1,0:T(8,128)(2,1)S(1)} %collective-permute-done.1.refs_1_), channel_id=1, source_target_pairs={{0,4},{1,5},{2,6},{3,7},{4,0},{5,1},{6,2},{7,3},{8,12},{9,13},{10,... | collective-permute-start | bytes 638984 | tf_op jit(solution)/shard_map/ppermute | solution.py:38
  19.7 2.2 %collective-permute-start.10 = (bf16[13,64,128]{2,1,0:T(8,128)(2,1)S(1)}, bf16[13,64,128]{2,1,0:T(8,128)(2,1)S(1)}, u32[]{:S(2)}, u32[]{:S(2)}) collective-permute-start(bf16[13,64,128]{2,1,0:T(8,128)(2,1)S(1)} %choose.2), channel_id=1, source_target_pairs={{0,4},{1,3},{2,6},{3,1},{4,0},{5,7},{6,2},{7,5},{8,12},{9,11},{10,... | collective-permute-start | bytes 638984 | tf_op jit(solution)/shard_map/ppermute | solution.py:38
  21.9 0.7 %collective-permute-start.7 = (bf16[512,128]{1,0:T(8,128)(2,1)S(1)}, bf16[512,128]{1,0:T(8,128)(2,1)S(1)}, u32[]{:S(2)}, u32[]{:S(2)}) collective-permute-start(bf16[512,128]{1,0:T(8,128)(2,1)S(1)} %get-tuple-element.44), channel_id=1, source_target_pairs={{1,2},{3,4},{5,6},{7,8},{9,10},{11,12},{13,14},{15,16},{17,18},{19... | collective-permute-start | bytes 393224 | tf_op jit(solution)/shard_map/ppermute | solution.py:563
  22.6 4.0 %couplings_by_owner.1 = (bf16[13,64,1024]{2,1,0:T(8,128)(2,1)S(1)}, bf16[15,64,1024]{2,1,0:T(8,128)(2,1)S(1)}, bf16[12,64,64]{2,1,0:T(8,128)(2,1)S(1)}) custom-call(s32[16,128]{1,0:T(8,128)S(1)} %get-tuple-element.40.entry_ref, s32[16,128]{1,0:T(8,128)S(1)} %get-tuple-element.33.block_ref.at_ref, bf16[512,128]{1,0:T(8,128)(2,1)S(1)} %get-tuple-element.41.inner_ref, ...), custom_call_target="tpu_custom_call" | custom-call | bytes 131072 | tf_op jit(solution)/shard_map/couplings_by_owner/pallas_call | solution.py:306
  26.7 3.1 %collective-permute-start.13 = (bf16[15,64,1024]{2,1,0:T(8,128)(2,1)S(1)}, bf16[15,64,1024]{2,1,0:T(8,128)(2,1)S(1)}, u32[]{:S(2)}, u32[]{:S(2)}) collective-permute-start(bf16[15,64,1024]{2,1,0:T(8,128)(2,1)S(1)} %get-tuple-element.54), channel_id=1, source_target_pairs={{0,1},{1,0},{2,3},{3,2},{4,5},{5,4},{6,7},{7,6},{8,9},{9,8},{10,11... | collective-permute-start | bytes 5898248 | tf_op jit(solution)/shard_map/ppermute | solution.py:38
  30.0 2.2 %collective-permute-start.8 = (bf16[26,64,128]{2,1,0:T(8,128)(2,1)S(1)}, bf16[26,64,128]{2,1,0:T(8,128)(2,1)S(1)}, u32[]{:S(2)}, u32[]{:S(2)}) collective-permute-start(bf16[26,64,128]{2,1,0:T(8,128)(2,1)S(1)} %join.1.refs_0_), channel_id=1, source_target_pairs={{0,2},{1,3},{2,0},{3,1},{4,6},{5,7},{6,4},{7,5},{8,10},{9,11},{10,... | collective-permute-start | bytes 1277960 | tf_op jit(solution)/shard_map/ppermute | solution.py:38
  32.2 1.3 %collective-permute-start.9 = (bf16[26,64,128]{2,1,0:T(8,128)(2,1)S(1)}, bf16[26,64,128]{2,1,0:T(8,128)(2,1)S(1)}, u32[]{:S(2)}, u32[]{:S(2)}) collective-permute-start(bf16[26,64,128]{2,1,0:T(8,128)(2,1)S(1)} %join.1.refs_0_), channel_id=1, source_target_pairs={{0,4},{1,5},{2,6},{3,7},{4,0},{5,1},{6,2},{7,3},{8,12},{9,13},{10,... | collective-permute-start | bytes 1277960 | tf_op jit(solution)/shard_map/ppermute | solution.py:38
  33.5 1.9 %collective-permute-start.11 = (bf16[13,64,128]{2,1,0:T(8,128)(2,1)S(1)}, bf16[13,64,128]{2,1,0:T(8,128)(2,1)S(1)}, u32[]{:S(2)}, u32[]{:S(2)}) collective-permute-start(bf16[13,64,128]{2,1,0:T(8,128)(2,1)S(1)} %collective-permute-done.10.refs_6_), channel_id=1, source_target_pairs={{0,24},{1,25},{2,26},{3,27},{4,28},{5,29},{6,30},{7,31},{8,0},{9,1... | collective-permute-start | bytes 638984 | tf_op jit(solution)/shard_map/ppermute | solution.py:38
  35.4 3.6 %near_3.1 = (bf16[6144,128]{1,0:T(8,128)(2,1)S(1)}, bf16[3072,128]{1,0:T(8,128)(2,1)S(1)}) custom-call(s32[2,12]{1,0:T(2,128)S(1)} %bitcast.3, s32[12,512]{1,0:T(8,128)S(1)} %copy-done.2, bf16[512,1536]{1,0:T(8,128)(2,1)S(1)} %copy-done, bf16[12,64,512]{2,1,0:T(8,128)(2,1)S(1)} %copy-done.1, ...), custom_call_target="tpu_custom_call", output_to_operand_aliasing={{0}: (5, {}), {1}: (6, {})} | custom-call | flops 20971520 | bytes 32768 | tf_op jit(solution)/shard_map/near_3/pallas_call | solution.py:460
  39.1 1.1 %far_0_0.1.refs_6_ = f32[13,64,128]{2,1,0:T(8,128)S(1)} custom-call(s32[16,128]{1,0:T(8,128)S(1)} %get-tuple-element.33.block_ref.at_ref, bf16[13,64,128]{2,1,0:T(8,128)(2,1)S(1)} %get-tuple-element.34.refs_0_, bf16[13,64,128]{2,1,0:T(8,128)(2,1)S(1)} %collective-permute-done.1.refs_1_, bf16[13,64,128]{2,1,0:T(8,128)(2,1)S(1)} %collective-permute-done.2.x_ref.refs_2_, ...), custom_call_target="tpu_custom_call" | custom-call | flops 1703936 | bytes 16384 | tf_op jit(solution)/shard_map/far_0_0/pallas_call | solution.py:360
  40.2 3.9 %near_0.1 = (bf16[6144,128]{1,0:T(8,128)(2,1)S(1)}, bf16[3072,128]{1,0:T(8,128)(2,1)S(1)}, s32[16,128]{1,0:T(8,128)S(1)}) custom-call(s32[2,12]{1,0:T(2,128)S(1)} %bitcast.4, s32[12,512]{1,0:T(8,128)S(1)} %copy-done.2, bf16[512,1536]{1,0:T(8,128)(2,1)S(1)} %copy-done, ...), custom_call_target="tpu_custom_call", output_to_operand_aliasing={{0}: (9, {}), {1}: (10, {})} | custom-call | flops 20971520 | bytes 32768 | tf_op jit(solution)/shard_map/near_0/pallas_call | solution.py:460
  44.1 1.1 %far_1_0.1.refs_6_ = f32[13,64,128]{2,1,0:T(8,128)S(1)} custom-call(s32[16,128]{1,0:T(8,128)S(1)} %get-tuple-element.56.at_ref, bf16[13,64,128]{2,1,0:T(8,128)(2,1)S(1)} %get-tuple-element.34.refs_0_, bf16[13,64,128]{2,1,0:T(8,128)(2,1)S(1)} %collective-permute-done.1.refs_1_, bf16[13,64,128]{2,1,0:T(8,128)(2,1)S(1)} %collective-permute-done.2.x_ref.refs_2_, ...), custom_call_target="tpu_custom_call" | custom-call | flops 1703936 | bytes 16384 | tf_op jit(solution)/shard_map/far_1_0/pallas_call | solution.py:360
  45.2 2.0 %collective-permute-done.14.refs_4_ = bf16[13,64,128]{2,1,0:T(8,128)(2,1)S(1)} collective-permute-done((bf16[13,64,128]{2,1,0:T(8,128)(2,1)S(1)}, bf16[13,64,128]{2,1,0:T(8,128)(2,1)S(1)}, u32[]{:S(2)}, u32[]{:S(2)}) %collective-permute-start.14) | collective-permute-done | bytes 213024 | tf_op jit(solution)/shard_map/ppermute | solution.py:38
  47.3 1.1 %far_1_2.1 = f32[13,64,128]{2,1,0:T(8,128)S(1)} custom-call(s32[16,128]{1,0:T(8,128)S(1)} %get-tuple-element.56.at_ref, bf16[26,64,128]{2,1,0:T(8,128)(2,1)S(1)} %join.1.refs_0_, bf16[26,64,128]{2,1,0:T(8,128)(2,1)S(1)} %collective-permute-done.8.refs_1_, bf16[26,64,128]{2,1,0:T(8,128)(2,1)S(1)} %collective-permute-done.9.refs_2_, ...), custom_call_target="tpu_custom_call" | custom-call | flops 1703936 | bytes 16384 | tf_op jit(solution)/shard_map/far_1_2/pallas_call | solution.py:360
  48.4 1.1 %far_0_2.1.own_ref = f32[13,64,128]{2,1,0:T(8,128)S(1)} custom-call(s32[16,128]{1,0:T(8,128)S(1)} %get-tuple-element.33.block_ref.at_ref, bf16[26,64,128]{2,1,0:T(8,128)(2,1)S(1)} %join.1.refs_0_, bf16[26,64,128]{2,1,0:T(8,128)(2,1)S(1)} %collective-permute-done.8.refs_1_, bf16[26,64,128]{2,1,0:T(8,128)(2,1)S(1)} %collective-permute-done.9.refs_2_, ...), custom_call_target="tpu_custom_call" | custom-call | flops 1703936 | bytes 16384 | tf_op jit(solution)/shard_map/far_0_2/pallas_call | solution.py:360
  49.5 0.7 %collective-permute-done.15.other_ref = f32[13,64,128]{2,1,0:T(8,128)S(1)} collective-permute-done((f32[13,64,128]{2,1,0:T(8,128)S(1)}, f32[13,64,128]{2,1,0:T(8,128)S(1)}, u32[]{:S(2)}, u32[]{:S(2)}) %collective-permute-start.15) | collective-permute-done | bytes 426016 | tf_op jit(solution)/shard_map/ppermute | solution.py:38
  50.2 3.6 %local_and_field.1 = bf16[6144,128]{1,0:T(8,128)(2,1)} custom-call(f32[13,64,128]{2,1,0:T(8,128)S(1)} %far_0_2.1.own_ref, f32[13,64,128]{2,1,0:T(8,128)S(1)} %collective-permute-done.15.other_ref, bf16[12,64,64]{2,1,0:T(8,128)(2,1)S(1)} %get-tuple-element.58.turned_transfer_ref, bf16[6144,128]{1,0:T(8,128)(2,1)S(1)} %get-tuple-element.59.near_ref, ...), custom_call_target="tpu_custom_call" | custom-call | flops 1572864 | bytes 65536 | tf_op jit(solution)/shard_map/local_and_field/pallas_call | solution.py:512
  (29 shorter events, 1.1 us)
Async XLA Ops:
  0.0 13.0 %copy-start = (bf16[512,1536]{1,0:T(8,128)(2,1)S(1)}, bf16[512,1536]{1,0:T(8,128)(2,1)}, u32[]{:S(2)}) copy-start(bf16[512,1536]{1,0:T(8,128)(2,1)} %constant.6.clone.table_ref) | copy-start | bytes 4718596
  0.0 13.0 %copy-start.1 = (bf16[12,64,512]{2,1,0:T(8,128)(2,1)S(1)}, bf16[12,64,512]{2,1,0:T(8,128)(2,1)}, u32[]{:S(2)}) copy-start(bf16[12,64,512]{2,1,0:T(8,128)(2,1)} %basis_ref.7) | copy-start | bytes 2359300
  0.0 13.0 %copy-start.2 = (s32[12,512]{1,0:T(8,128)S(1)}, s32[12,512]{1,0:T(8,128)}, u32[]{:S(2)}) copy-start(s32[12,512]{1,0:T(8,128)} %order_ref.7) | copy-start | bytes 73732
  0.0 13.0 %copy-start.3 = (s32[12,2]{0,1:T(2,128)S(1)}, s32[12,2]{0,1:T(2,128)}, u32[]{:S(2)}) copy-start(s32[12,2]{0,1:T(2,128)} %param.17) | copy-start | bytes 292
  4.7 12.0 %collective-permute-start.1 = (bf16[13,64,128]{2,1,0:T(8,128)(2,1)S(1)}, bf16[13,64,128]{2,1,0:T(8,128)(2,1)S(1)}, u32[]{:S(2)}, u32[]{:S(2)}) collective-permute-start(bf16[13,64,128]{2,1,0:T(8,128)(2,1)S(1)} %get-tuple-element.34.refs_0_), channel_id=1, source_target_pairs={{0,8},{1,9},{2,10},{3,11},{4,12},{5,13},{6,14},{7,15},{8,16},{9,17... | collective-permute-start | bytes 638984 | tf_op jit(solution)/shard_map/ppermute | solution.py:38
  7.8 8.9 %collective-permute-start.2 = (bf16[13,64,128]{2,1,0:T(8,128)(2,1)S(1)}, bf16[13,64,128]{2,1,0:T(8,128)(2,1)S(1)}, u32[]{:S(2)}, u32[]{:S(2)}) collective-permute-start(bf16[13,64,128]{2,1,0:T(8,128)(2,1)S(1)} %get-tuple-element.34.refs_0_), channel_id=1, source_target_pairs={{0,2},{1,3},{2,0},{3,1},{4,6},{5,7},{6,4},{7,5},{8,10},{9,11},{10,... | collective-permute-start | bytes 638984 | tf_op jit(solution)/shard_map/ppermute | solution.py:38
  9.3 7.5 %collective-permute-start.3 = (bf16[13,64,128]{2,1,0:T(8,128)(2,1)S(1)}, bf16[13,64,128]{2,1,0:T(8,128)(2,1)S(1)}, u32[]{:S(2)}, u32[]{:S(2)}) collective-permute-start(bf16[13,64,128]{2,1,0:T(8,128)(2,1)S(1)} %get-tuple-element.34.refs_0_), channel_id=1, source_target_pairs={{0,4},{1,5},{2,6},{3,7},{4,0},{5,1},{6,2},{7,3},{8,12},{9,13},{10,... | collective-permute-start | bytes 638984 | tf_op jit(solution)/shard_map/ppermute | solution.py:38
  10.8 8.9 %collective-permute-start = (bf16[13,64,128]{2,1,0:T(8,128)(2,1)S(1)}, bf16[13,64,128]{2,1,0:T(8,128)(2,1)S(1)}, u32[]{:S(2)}, u32[]{:S(2)}) collective-permute-start(bf16[13,64,128]{2,1,0:T(8,128)(2,1)S(1)} %get-tuple-element.34.refs_0_), channel_id=1, source_target_pairs={{0,24},{1,25},{2,26},{3,27},{4,28},{5,29},{6,30},{7,31},{8,0},{9,1... | collective-permute-start | bytes 638984 | tf_op jit(solution)/shard_map/ppermute | solution.py:38
  16.6 9.9 %collective-permute-start.4 = (bf16[13,64,128]{2,1,0:T(8,128)(2,1)S(1)}, bf16[13,64,128]{2,1,0:T(8,128)(2,1)S(1)}, u32[]{:S(2)}, u32[]{:S(2)}) collective-permute-start(bf16[13,64,128]{2,1,0:T(8,128)(2,1)S(1)} %collective-permute-done.1.refs_1_), channel_id=1, source_target_pairs={{0,8},{1,9},{2,10},{3,11},{4,12},{5,13},{6,14},{7,15},{8,16},{9,17... | collective-permute-start | bytes 638984 | tf_op jit(solution)/shard_map/ppermute | solution.py:38
  16.7 9.9 %collective-permute-start.5 = (bf16[13,64,128]{2,1,0:T(8,128)(2,1)S(1)}, bf16[13,64,128]{2,1,0:T(8,128)(2,1)S(1)}, u32[]{:S(2)}, u32[]{:S(2)}) collective-permute-start(bf16[13,64,128]{2,1,0:T(8,128)(2,1)S(1)} %collective-permute-done.1.refs_1_), channel_id=1, source_target_pairs={{0,2},{1,3},{2,0},{3,1},{4,6},{5,7},{6,4},{7,5},{8,10},{9,11},{10,... | collective-permute-start | bytes 638984 | tf_op jit(solution)/shard_map/ppermute | solution.py:38
  17.7 8.9 %collective-permute-start.6 = (bf16[13,64,128]{2,1,0:T(8,128)(2,1)S(1)}, bf16[13,64,128]{2,1,0:T(8,128)(2,1)S(1)}, u32[]{:S(2)}, u32[]{:S(2)}) collective-permute-start(bf16[13,64,128]{2,1,0:T(8,128)(2,1)S(1)} %collective-permute-done.1.refs_1_), channel_id=1, source_target_pairs={{0,4},{1,5},{2,6},{3,7},{4,0},{5,1},{6,2},{7,3},{8,12},{9,13},{10,... | collective-permute-start | bytes 638984 | tf_op jit(solution)/shard_map/ppermute | solution.py:38
  19.7 7.0 %collective-permute-start.10 = (bf16[13,64,128]{2,1,0:T(8,128)(2,1)S(1)}, bf16[13,64,128]{2,1,0:T(8,128)(2,1)S(1)}, u32[]{:S(2)}, u32[]{:S(2)}) collective-permute-start(bf16[13,64,128]{2,1,0:T(8,128)(2,1)S(1)} %choose.2), channel_id=1, source_target_pairs={{0,4},{1,3},{2,6},{3,1},{4,0},{5,7},{6,2},{7,5},{8,12},{9,11},{10,... | collective-permute-start | bytes 638984 | tf_op jit(solution)/shard_map/ppermute | solution.py:38
  21.9 4.7 %collective-permute-start.7 = (bf16[512,128]{1,0:T(8,128)(2,1)S(1)}, bf16[512,128]{1,0:T(8,128)(2,1)S(1)}, u32[]{:S(2)}, u32[]{:S(2)}) collective-permute-start(bf16[512,128]{1,0:T(8,128)(2,1)S(1)} %get-tuple-element.44), channel_id=1, source_target_pairs={{1,2},{3,4},{5,6},{7,8},{9,10},{11,12},{13,14},{15,16},{17,18},{19... | collective-permute-start | bytes 393224 | tf_op jit(solution)/shard_map/ppermute | solution.py:563
  26.7 13.5 %collective-permute-start.13 = (bf16[15,64,1024]{2,1,0:T(8,128)(2,1)S(1)}, bf16[15,64,1024]{2,1,0:T(8,128)(2,1)S(1)}, u32[]{:S(2)}, u32[]{:S(2)}) collective-permute-start(bf16[15,64,1024]{2,1,0:T(8,128)(2,1)S(1)} %get-tuple-element.54), channel_id=1, source_target_pairs={{0,1},{1,0},{2,3},{3,2},{4,5},{5,4},{6,7},{7,6},{8,9},{9,8},{10,11... | collective-permute-start | bytes 5898248 | tf_op jit(solution)/shard_map/ppermute | solution.py:38
  29.8 9.1 %collective-permute-start.12 = (bf16[13,64,128]{2,1,0:T(8,128)(2,1)S(1)}, bf16[13,64,128]{2,1,0:T(8,128)(2,1)S(1)}, u32[]{:S(2)}, u32[]{:S(2)}) collective-permute-start(bf16[13,64,128]{2,1,0:T(8,128)(2,1)S(1)} %choose.3), channel_id=1, source_target_pairs={{0,4},{1,3},{2,6},{3,1},{4,0},{5,7},{6,2},{7,5},{8,12},{9,11},{10,... | collective-permute-start | bytes 638984 | tf_op jit(solution)/shard_map/ppermute | solution.py:38
  30.0 17.2 %collective-permute-start.8 = (bf16[26,64,128]{2,1,0:T(8,128)(2,1)S(1)}, bf16[26,64,128]{2,1,0:T(8,128)(2,1)S(1)}, u32[]{:S(2)}, u32[]{:S(2)}) collective-permute-start(bf16[26,64,128]{2,1,0:T(8,128)(2,1)S(1)} %join.1.refs_0_), channel_id=1, source_target_pairs={{0,2},{1,3},{2,0},{3,1},{4,6},{5,7},{6,4},{7,5},{8,10},{9,11},{10,... | collective-permute-start | bytes 1277960 | tf_op jit(solution)/shard_map/ppermute | solution.py:38
  32.2 15.1 %collective-permute-start.9 = (bf16[26,64,128]{2,1,0:T(8,128)(2,1)S(1)}, bf16[26,64,128]{2,1,0:T(8,128)(2,1)S(1)}, u32[]{:S(2)}, u32[]{:S(2)}) collective-permute-start(bf16[26,64,128]{2,1,0:T(8,128)(2,1)S(1)} %join.1.refs_0_), channel_id=1, source_target_pairs={{0,4},{1,5},{2,6},{3,7},{4,0},{5,1},{6,2},{7,3},{8,12},{9,13},{10,... | collective-permute-start | bytes 1277960 | tf_op jit(solution)/shard_map/ppermute | solution.py:38
  33.5 11.7 %collective-permute-start.11 = (bf16[13,64,128]{2,1,0:T(8,128)(2,1)S(1)}, bf16[13,64,128]{2,1,0:T(8,128)(2,1)S(1)}, u32[]{:S(2)}, u32[]{:S(2)}) collective-permute-start(bf16[13,64,128]{2,1,0:T(8,128)(2,1)S(1)} %collective-permute-done.10.refs_6_), channel_id=1, source_target_pairs={{0,24},{1,25},{2,26},{3,27},{4,28},{5,29},{6,30},{7,31},{8,0},{9,1... | collective-permute-start | bytes 638984 | tf_op jit(solution)/shard_map/ppermute | solution.py:38
  39.0 8.3 %collective-permute-start.14 = (bf16[13,64,128]{2,1,0:T(8,128)(2,1)S(1)}, bf16[13,64,128]{2,1,0:T(8,128)(2,1)S(1)}, u32[]{:S(2)}, u32[]{:S(2)}) collective-permute-start(bf16[13,64,128]{2,1,0:T(8,128)(2,1)S(1)} %collective-permute-done.12.refs_7_), channel_id=1, source_target_pairs={{0,8},{1,9},{2,10},{3,11},{4,12},{5,13},{6,14},{7,15},{8,16},{9,17... | collective-permute-start | bytes 638984 | tf_op jit(solution)/shard_map/ppermute | solution.py:38
  48.4 1.8 %collective-permute-start.15 = (f32[13,64,128]{2,1,0:T(8,128)S(1)}, f32[13,64,128]{2,1,0:T(8,128)S(1)}, u32[]{:S(2)}, u32[]{:S(2)}) collective-permute-start(f32[13,64,128]{2,1,0:T(8,128)S(1)} %far_1_2.1), channel_id=1, source_target_pairs={{0,1},{1,0},{2,3},{3,2},{4,5},{5,4},{6,7},{7,6},{8,9},{9,8},{10,11... | collective-permute-start | bytes 1277960 | tf_op jit(solution)/shard_map/ppermute | solution.py:38

commit v15 on v14

--- a/solution.py
+++ b/solution.py
@@ -184,7 +184,7 @@
         shared_ref[pl.ds(0, 1)] = root_ref[...].astype(BF)[None]
 
 
-def skeletons_of(me, leaf_order, composition, leaf_basis, transfer, owners, blocks, layers, per=4):
+def skeletons_of(me, leaf_order, composition, leaf_basis, transfer, owners, blocks, layers, per=6):
     leaves, rank, leaf_len = leaf_basis.shape
     fields = composition.shape[1]
     entries = owners.shape[1]
@@ -299,7 +299,7 @@
         other_ref[leaves + 2, :blocks.shape[0], :blocks.shape[1]] = blocks
 
 
-def dense_couplings(entry, block, inner, coupling, top_coupling, transfer, slots, per=4):
+def dense_couplings(entry, block, inner, coupling, top_coupling, transfer, slots, per=6):
     leaves, entries, rank, _ = coupling.shape
     own = (leaves + 1, rank, slots * rank)
     other = (leaves + 3, rank, slots * rank)
@@ -368,105 +368,79 @@
     )(at, *args)
 
 
-def near_kernel(edges, pair_of, last_pair, mask_ref, order_ref, table_ref, basis_ref,
-                ordered_ref, *refs):
+def near_kernel(edges, pairs, mask_ref, order_ref, table_ref, basis_ref, ordered_ref, *refs):
     if edges:
-        me_ref, cross_ref, inner_ref, blocks_ref = refs[:4]
+        me_ref, cross_ref, inner_ref = refs[:3]
         near_ref, turned_ref, at_ref = refs[-3:]
+        even = me_ref[0] % 2 == 0
     else:
         near_ref, turned_ref = refs[-2:]
-    pair = pair_of(pl.program_id(0))
-    leaf_len = basis_ref.shape[2]
-    leaves = basis_ref.shape[0]
+    leaves, _, leaf_len = basis_ref.shape
+    fields = ordered_ref.shape[1]
+    if edges:
+        rows, rank = at_ref.shape[0], basis_ref.shape[1]
+        blocks = inner_ref[leaves + 2, :rows, :at_ref.shape[1]]
+        at_ref[...] = blocks.astype(F32).astype(jnp.int32)
+        inner = jnp.concatenate(
+            [
+                inner_ref[leaves + 1, :, t * fields:(t + 1) * fields]
+                for t in range(leaf_len // rank)
+            ],
+            axis=0,
+        )
 
     def leaf_at(leaf):
-        return ordered_ref[pl.ds(pl.multiple_of(leaf * leaf_len, leaf_len), leaf_len), :]
-
-    low, high = leaf_at(2 * pair), leaf_at(2 * pair + 1)
-    prev, following = leaf_at(jnp.maximum(2 * pair - 1, 0)), leaf_at(jnp.minimum(2 * pair + 2, leaves - 1))
-    if edges:
-        even = me_ref[0] % 2 == 0
-        cross = cross_ref[...]
-        wide = cross.shape[1]
-        inner = jnp.concatenate(
-            [inner_ref[0, :, t:t + wide] for t in range(0, inner_ref.shape[2], wide)], axis=0
-        )[:leaf_len]
-        prev = jnp.where(pair == 0, jnp.where(even, cross, inner), prev)
-        following = jnp.where(pair == last_pair, jnp.where(even, inner, cross), following)
-
-        @pl.when(pl.program_id(0) == 0)
-        def _():
-            rows, lanes = at_ref.shape
-            at_ref[...] = blocks_ref[0, :rows, :lanes].astype(F32).astype(jnp.int32)
-
-
-    def masked(leaf, side, value):
+        if leaf < 0:
+            return jnp.where(even, cross_ref[...], inner)
+        if leaf >= leaves:
+            return jnp.where(even, inner, cross_ref[...])
+        return ordered_ref[leaf * leaf_len:(leaf + 1) * leaf_len, :]
+
+    def masked(leaf, side):
+        value = leaf_at(leaf - 1 + 2 * side)
         return jnp.where(mask_ref[side, leaf] > 0, value, jnp.zeros_like(value))
 
-    left = jnp.concatenate(
-        [masked(2 * pair, 0, prev), low, masked(2 * pair, 1, high)], axis=0
-    )
-    right = jnp.concatenate(
-        [masked(2 * pair + 1, 0, low), high, masked(2 * pair + 1, 1, following)], axis=0
-    )
-    near = dot(table_ref[...], jnp.concatenate([left, right], axis=1)).astype(BF)
-    fields = ordered_ref.shape[1]
-    turned = []
-    for i in range(2):
-        hot = one_hot_grid(order_ref[pl.ds(2 * pair + i, 1), :], leaf_len)
-        at = pl.ds(pl.multiple_of((2 * pair + i) * leaf_len, leaf_len), leaf_len)
-        both = jnp.concatenate([near[:, i * fields:(i + 1) * fields], basis_ref[2 * pair + i].T], axis=1)
-        moved = dot(hot, both).astype(BF)
-        near_ref[at, :] = moved[:, :fields]
-        turned.append(moved[:, fields:])
-    at = pl.multiple_of(pair * leaf_len, leaf_len)
-    turned_ref[pl.ds(at, leaf_len), :] = jnp.concatenate(turned, axis=1)
+    for pair in pairs:
+        columns = [
+            jnp.concatenate([masked(leaf, 0), leaf_at(leaf), masked(leaf, 1)], axis=0)
+            for leaf in (2 * pair, 2 * pair + 1)
+        ]
+        near = dot(table_ref[...], jnp.concatenate(columns, axis=1)).astype(BF)
+        turned = []
+        for i in range(2):
+            leaf = 2 * pair + i
+            hot = one_hot_grid(order_ref[leaf:leaf + 1, :], leaf_len)
+            both = jnp.concatenate([near[:, i * fields:(i + 1) * fields], basis_ref[leaf].T], axis=1)
+            moved = dot(hot, both).astype(BF)
+            near_ref[leaf * leaf_len:(leaf + 1) * leaf_len, :] = moved[:, :fields]
+            turned.append(moved[:, fields:])
+        turned_ref[pair * leaf_len:(pair + 1) * leaf_len, :] = jnp.concatenate(turned, axis=1)
 
 
 def near_field(pairs, near_list, leaf_order, tables, basis, ordered, halos=None, filled=None):
     leaves, rank, leaf_len = basis.shape
     fields = ordered.shape[1]
-    last = leaves // 2 - 1
-    gap = pairs[1] - pairs[0] if len(pairs) > 1 else 1
-
-    def pair_of(step):
-        return pairs[0] + gap * step
-
-    in_specs = [
-        scalars(),
-        whole(),
-        whole(),
-        whole(),
-        whole(),
+    args = [near_list.T, leaf_order, tables, basis, ordered]
+    in_specs = [scalars()] + [whole()] * 4
+    out_shape = [
+        jax.ShapeDtypeStruct((leaves * leaf_len, fields), BF),
+        jax.ShapeDtypeStruct((leaves // 2 * leaf_len, 2 * rank), BF),
     ]
-    args = [near_list.T, leaf_order, tables, basis, ordered]
     aliases = {}
-    extra = []
     if halos is not None:
-        me, cross, other = halos
-        row = (1,) + other.shape[1:]
-        in_specs += [
-            scalars(),
-            pl.BlockSpec((leaf_len, fields), lambda s: (0, 0)),
-            pl.BlockSpec(row, lambda s: (leaves + 1, 0, 0)),
-            pl.BlockSpec(row, lambda s: (leaves + 2, 0, 0)),
-        ]
-        args += [me, cross, other, other]
-        extra = [(16, 128)]
+        in_specs += [scalars(), whole(), whole()]
+        args += list(halos)
+        out_shape.append(jax.ShapeDtypeStruct((16, 128), jnp.int32))
     if filled is not None:
         aliases = {len(args): 0, len(args) + 1: 1}
         in_specs += [whole()] * 2
         args += list(filled)
     return pl.pallas_call(
-        functools.partial(near_kernel, halos is not None, pair_of, last),
+        functools.partial(near_kernel, halos is not None, tuple(pairs)),
         name="near_" + str(pairs[0]),
-        grid=(len(pairs),),
         in_specs=in_specs,
-        out_specs=[whole()] * (2 + len(extra)),
-        out_shape=[
-            jax.ShapeDtypeStruct((leaves * leaf_len, fields), BF),
-            jax.ShapeDtypeStruct((leaves // 2 * leaf_len, 2 * rank), BF),
-        ] + [jax.ShapeDtypeStruct(shape, jnp.int32) for shape in extra],
+        out_specs=[whole()] * len(out_shape),
+        out_shape=out_shape,
         input_output_aliases=aliases,
         compiler_params=params(16),
         cost_estimate=cost(len(pairs) * 2 * leaf_len * leaf_len * fields * 10, len(pairs) * MIB),
@@ -505,7 +479,7 @@
             out_ref[rows, :] = (near + far[:, i * fields:(i + 1) * fields]).astype(BF)
 
 
-def field(own, other, turned_transfer, near, turned, per=2):
+def field(own, other, turned_transfer, near, turned, per=6):
     leaves, rank, _ = turned_transfer.shape
     fields = near.shape[1]
     leaf_len = near.shape[0] // leaves

time: 53.9 us -> 52.2 us (0.968)
  Pallas kernels: 27.7 us -> 25.2 us
  starting transfers between devices: 22.8 us -> 23.5 us
    pallas_call x1, Pallas kernels: 3.56 us -> 2.23 us  [field(): pl.pallas_call(functools.partial(field_kernel, per), name='local_and_fiel...]
    ppermute x15, starting transfers between devices: 22.1 us -> 22.8 us  [send(): lax.ppermute(block, 'subtree', [(d, target(d)) for d in range(count)])]
where the time goes in v15:
time: 52.2 us; the launch traced here: 52.1 us
  Pallas kernels  25.2 us (48%)
  starting transfers between devices  23.5 us (45%)
  waiting for transfers between devices  3.24 us (6%)
    ppermute x15, starting transfers between devices, send(): lax.ppermute(block, 'subtree', [(d, target(d)) for d in range(count)])  22.8 us
    pallas_call x3, Pallas kernels, near_field(): pl.pallas_call(functools.partial(near_kernel, halos is not None, tuple(pa...  10.7 us
    pallas_call x4, Pallas kernels, far_round(): pl.pallas_call(functools.partial(round_kernel, plane, steps, slots, [len(...  4.34 us
    pallas_call x1, Pallas kernels, skeletons_of(): pl.pallas_call(functools.partial(skeleton_kernel, per, layers), name='ord...  4.29 us
    pallas_call x1, Pallas kernels, dense_couplings(): pl.pallas_call(functools.partial(dense_kernel, per, slots), name='couplin...  3.49 us
    ppermute x15, waiting for transfers between devices, send(): lax.ppermute(block, 'subtree', [(d, target(d)) for d in range(count)])  3.24 us
    pallas_call x1, Pallas kernels, field(): pl.pallas_call(functools.partial(field_kernel, per), name='local_and_fiel...  2.23 us
  transfers between devices with their start and end apart: 16, of which 3 were waited for; matrix products, arithmetic and copies ran while one was open for 0% of the time, Pallas kernels for 34%

profile of v15, /device:TPU:0, one launch (start us, length us, event | category | flops | bytes accessed | tf_op | source)
XLA Modules:
  0.0 52.1 jit_solution(16738742727297626862)
XLA Ops:
  0.0 4.3 %order_and_skeleton.1 = (bf16[6144,128]{1,0:T(8,128)(2,1)S(1)}, bf16[13,64,128]{2,1,0:T(8,128)(2,1)S(1)}, bf16[512,128]{1,0:T(8,128)(2,1)S(1)}, bf16[512,128]{1,...) custom-call(s32[1]{0:T(128)} %bitcast.me_ref.refs_0_, s32[12,512]{1,0:T(8,128)} %order_ref.7, ...), custom_call_target="tpu_custom_call" | custom-call | flops 12582912 | bytes 65536 | tf_op jit(solution)/shard_map/order_and_skeleton/pallas_call | solution.py:192
  4.3 3.1 %collective-permute-start.1 = (bf16[13,64,128]{2,1,0:T(8,128)(2,1)S(1)}, bf16[13,64,128]{2,1,0:T(8,128)(2,1)S(1)}, u32[]{:S(2)}, u32[]{:S(2)}) collective-permute-start(bf16[13,64,128]{2,1,0:T(8,128)(2,1)S(1)} %get-tuple-element.34.refs_0_), channel_id=1, source_target_pairs={{0,8},{1,9},{2,10},{3,11},{4,12},{5,13},{6,14},{7,15},{8,16},{9,17... | collective-permute-start | bytes 638984 | tf_op jit(solution)/shard_map/ppermute | solution.py:38
  7.4 1.5 %collective-permute-start.2 = (bf16[13,64,128]{2,1,0:T(8,128)(2,1)S(1)}, bf16[13,64,128]{2,1,0:T(8,128)(2,1)S(1)}, u32[]{:S(2)}, u32[]{:S(2)}) collective-permute-start(bf16[13,64,128]{2,1,0:T(8,128)(2,1)S(1)} %get-tuple-element.34.refs_0_), channel_id=1, source_target_pairs={{0,2},{1,3},{2,0},{3,1},{4,6},{5,7},{6,4},{7,5},{8,10},{9,11},{10,... | collective-permute-start | bytes 638984 | tf_op jit(solution)/shard_map/ppermute | solution.py:38
  8.9 1.5 %collective-permute-start.3 = (bf16[13,64,128]{2,1,0:T(8,128)(2,1)S(1)}, bf16[13,64,128]{2,1,0:T(8,128)(2,1)S(1)}, u32[]{:S(2)}, u32[]{:S(2)}) collective-permute-start(bf16[13,64,128]{2,1,0:T(8,128)(2,1)S(1)} %get-tuple-element.34.refs_0_), channel_id=1, source_target_pairs={{0,4},{1,5},{2,6},{3,7},{4,0},{5,1},{6,2},{7,3},{8,12},{9,13},{10,... | collective-permute-start | bytes 638984 | tf_op jit(solution)/shard_map/ppermute | solution.py:38
  10.4 2.2 %collective-permute-start = (bf16[13,64,128]{2,1,0:T(8,128)(2,1)S(1)}, bf16[13,64,128]{2,1,0:T(8,128)(2,1)S(1)}, u32[]{:S(2)}, u32[]{:S(2)}) collective-permute-start(bf16[13,64,128]{2,1,0:T(8,128)(2,1)S(1)} %get-tuple-element.34.refs_0_), channel_id=1, source_target_pairs={{0,24},{1,25},{2,26},{3,27},{4,28},{5,29},{6,30},{7,31},{8,0},{9,1... | collective-permute-start | bytes 638984 | tf_op jit(solution)/shard_map/ppermute | solution.py:38
  12.7 3.6 %near_1.1 = (bf16[6144,128]{1,0:T(8,128)(2,1)S(1)}, bf16[3072,128]{1,0:T(8,128)(2,1)S(1)}) custom-call(s32[2,12]{1,0:T(2,128)S(1)} %bitcast.2, s32[12,512]{1,0:T(8,128)S(1)} %copy-done.2, bf16[512,1536]{1,0:T(8,128)(2,1)S(1)} %copy-done, bf16[12,64,512]{2,1,0:T(8,128)(2,1)S(1)} %copy-done.1, bf16[6144,128]{1,0:T(8,128)(2,1)S(1)} %get-tuple-element.53.ordered_ref), custom_call_target="tpu_custom_call" | custom-call | flops 20971520 | bytes 32768 | tf_op jit(solution)/shard_map/near_1/pallas_call | solution.py:438
  16.4 1.0 %collective-permute-start.5 = (bf16[13,64,128]{2,1,0:T(8,128)(2,1)S(1)}, bf16[13,64,128]{2,1,0:T(8,128)(2,1)S(1)}, u32[]{:S(2)}, u32[]{:S(2)}) collective-permute-start(bf16[13,64,128]{2,1,0:T(8,128)(2,1)S(1)} %collective-permute-done.1.refs_1_), channel_id=1, source_target_pairs={{0,2},{1,3},{2,0},{3,1},{4,6},{5,7},{6,4},{7,5},{8,10},{9,11},{10,... | collective-permute-start | bytes 638984 | tf_op jit(solution)/shard_map/ppermute | solution.py:38
  17.3 1.6 %collective-permute-start.6 = (bf16[13,64,128]{2,1,0:T(8,128)(2,1)S(1)}, bf16[13,64,128]{2,1,0:T(8,128)(2,1)S(1)}, u32[]{:S(2)}, u32[]{:S(2)}) collective-permute-start(bf16[13,64,128]{2,1,0:T(8,128)(2,1)S(1)} %collective-permute-done.1.refs_1_), channel_id=1, source_target_pairs={{0,4},{1,5},{2,6},{3,7},{4,0},{5,1},{6,2},{7,3},{8,12},{9,13},{10,... | collective-permute-start | bytes 638984 | tf_op jit(solution)/shard_map/ppermute | solution.py:38
  19.3 2.2 %collective-permute-start.10 = (bf16[13,64,128]{2,1,0:T(8,128)(2,1)S(1)}, bf16[13,64,128]{2,1,0:T(8,128)(2,1)S(1)}, u32[]{:S(2)}, u32[]{:S(2)}) collective-permute-start(bf16[13,64,128]{2,1,0:T(8,128)(2,1)S(1)} %choose.2), channel_id=1, source_target_pairs={{0,4},{1,3},{2,6},{3,1},{4,0},{5,7},{6,2},{7,5},{8,12},{9,11},{10,... | collective-permute-start | bytes 638984 | tf_op jit(solution)/shard_map/ppermute | solution.py:38
  21.5 0.7 %collective-permute-start.7 = (bf16[512,128]{1,0:T(8,128)(2,1)S(1)}, bf16[512,128]{1,0:T(8,128)(2,1)S(1)}, u32[]{:S(2)}, u32[]{:S(2)}) collective-permute-start(bf16[512,128]{1,0:T(8,128)(2,1)S(1)} %get-tuple-element.44), channel_id=1, source_target_pairs={{1,2},{3,4},{5,6},{7,8},{9,10},{11,12},{13,14},{15,16},{17,18},{19... | collective-permute-start | bytes 393224 | tf_op jit(solution)/shard_map/ppermute | solution.py:537
  22.2 3.5 %couplings_by_owner.1 = (bf16[13,64,1024]{2,1,0:T(8,128)(2,1)S(1)}, bf16[15,64,1024]{2,1,0:T(8,128)(2,1)S(1)}, bf16[12,64,64]{2,1,0:T(8,128)(2,1)S(1)}) custom-call(s32[16,128]{1,0:T(8,128)S(1)} %get-tuple-element.40.entry_ref, s32[16,128]{1,0:T(8,128)S(1)} %get-tuple-element.33.block_ref.at_ref, bf16[512,128]{1,0:T(8,128)(2,1)S(1)} %get-tuple-element.41.inner_ref, ...), custom_call_target="tpu_custom_call" | custom-call | bytes 131072 | tf_op jit(solution)/shard_map/couplings_by_owner/pallas_call | solution.py:306
  25.8 3.2 %collective-permute-start.13 = (bf16[15,64,1024]{2,1,0:T(8,128)(2,1)S(1)}, bf16[15,64,1024]{2,1,0:T(8,128)(2,1)S(1)}, u32[]{:S(2)}, u32[]{:S(2)}) collective-permute-start(bf16[15,64,1024]{2,1,0:T(8,128)(2,1)S(1)} %get-tuple-element.54), channel_id=1, source_target_pairs={{0,1},{1,0},{2,3},{3,2},{4,5},{5,4},{6,7},{7,6},{8,9},{9,8},{10,11... | collective-permute-start | bytes 5898248 | tf_op jit(solution)/shard_map/ppermute | solution.py:38
  29.5 2.5 %collective-permute-start.8 = (bf16[26,64,128]{2,1,0:T(8,128)(2,1)S(1)}, bf16[26,64,128]{2,1,0:T(8,128)(2,1)S(1)}, u32[]{:S(2)}, u32[]{:S(2)}) collective-permute-start(bf16[26,64,128]{2,1,0:T(8,128)(2,1)S(1)} %join.1.refs_0_), channel_id=1, source_target_pairs={{0,2},{1,3},{2,0},{3,1},{4,6},{5,7},{6,4},{7,5},{8,10},{9,11},{10,... | collective-permute-start | bytes 1277960 | tf_op jit(solution)/shard_map/ppermute | solution.py:38
  32.0 1.2 %collective-permute-start.9 = (bf16[26,64,128]{2,1,0:T(8,128)(2,1)S(1)}, bf16[26,64,128]{2,1,0:T(8,128)(2,1)S(1)}, u32[]{:S(2)}, u32[]{:S(2)}) collective-permute-start(bf16[26,64,128]{2,1,0:T(8,128)(2,1)S(1)} %join.1.refs_0_), channel_id=1, source_target_pairs={{0,4},{1,5},{2,6},{3,7},{4,0},{5,1},{6,2},{7,3},{8,12},{9,13},{10,... | collective-permute-start | bytes 1277960 | tf_op jit(solution)/shard_map/ppermute | solution.py:38
  33.1 1.7 %collective-permute-start.11 = (bf16[13,64,128]{2,1,0:T(8,128)(2,1)S(1)}, bf16[13,64,128]{2,1,0:T(8,128)(2,1)S(1)}, u32[]{:S(2)}, u32[]{:S(2)}) collective-permute-start(bf16[13,64,128]{2,1,0:T(8,128)(2,1)S(1)} %collective-permute-done.10.refs_6_), channel_id=1, source_target_pairs={{0,24},{1,25},{2,26},{3,27},{4,28},{5,29},{6,30},{7,31},{8,0},{9,1... | collective-permute-start | bytes 638984 | tf_op jit(solution)/shard_map/ppermute | solution.py:38
  34.8 3.6 %near_3.1 = (bf16[6144,128]{1,0:T(8,128)(2,1)S(1)}, bf16[3072,128]{1,0:T(8,128)(2,1)S(1)}) custom-call(s32[2,12]{1,0:T(2,128)S(1)} %bitcast.3, s32[12,512]{1,0:T(8,128)S(1)} %copy-done.2, bf16[512,1536]{1,0:T(8,128)(2,1)S(1)} %copy-done, bf16[12,64,512]{2,1,0:T(8,128)(2,1)S(1)} %copy-done.1, ...), custom_call_target="tpu_custom_call", output_to_operand_aliasing={{0}: (5, {}), {1}: (6, {})} | custom-call | flops 20971520 | bytes 32768 | tf_op jit(solution)/shard_map/near_3/pallas_call | solution.py:438
  38.9 1.1 %far_0_0.1.refs_6_ = f32[13,64,128]{2,1,0:T(8,128)S(1)} custom-call(s32[16,128]{1,0:T(8,128)S(1)} %get-tuple-element.33.block_ref.at_ref, bf16[13,64,128]{2,1,0:T(8,128)(2,1)S(1)} %get-tuple-element.34.refs_0_, bf16[13,64,128]{2,1,0:T(8,128)(2,1)S(1)} %collective-permute-done.1.refs_1_, bf16[13,64,128]{2,1,0:T(8,128)(2,1)S(1)} %collective-permute-done.2.x_ref.refs_2_, ...), custom_call_target="tpu_custom_call" | custom-call | flops 1703936 | bytes 16384 | tf_op jit(solution)/shard_map/far_0_0/pallas_call | solution.py:360
  40.0 3.6 %near_0.1 = (bf16[6144,128]{1,0:T(8,128)(2,1)S(1)}, bf16[3072,128]{1,0:T(8,128)(2,1)S(1)}, s32[16,128]{1,0:T(8,128)S(1)}) custom-call(s32[2,12]{1,0:T(2,128)S(1)} %bitcast.4, s32[12,512]{1,0:T(8,128)S(1)} %copy-done.2, bf16[512,1536]{1,0:T(8,128)(2,1)S(1)} %copy-done, ...), custom_call_target="tpu_custom_call", output_to_operand_aliasing={{0}: (8, {}), {1}: (9, {})} | custom-call | flops 20971520 | bytes 32768 | tf_op jit(solution)/shard_map/near_0/pallas_call | solution.py:438
  43.6 1.1 %far_1_0.1.refs_6_ = f32[13,64,128]{2,1,0:T(8,128)S(1)} custom-call(s32[16,128]{1,0:T(8,128)S(1)} %get-tuple-element.56.at_ref, bf16[13,64,128]{2,1,0:T(8,128)(2,1)S(1)} %get-tuple-element.34.refs_0_, bf16[13,64,128]{2,1,0:T(8,128)(2,1)S(1)} %collective-permute-done.1.refs_1_, bf16[13,64,128]{2,1,0:T(8,128)(2,1)S(1)} %collective-permute-done.2.x_ref.refs_2_, ...), custom_call_target="tpu_custom_call" | custom-call | flops 1703936 | bytes 16384 | tf_op jit(solution)/shard_map/far_1_0/pallas_call | solution.py:360
  44.7 2.2 %collective-permute-done.14.refs_4_ = bf16[13,64,128]{2,1,0:T(8,128)(2,1)S(1)} collective-permute-done((bf16[13,64,128]{2,1,0:T(8,128)(2,1)S(1)}, bf16[13,64,128]{2,1,0:T(8,128)(2,1)S(1)}, u32[]{:S(2)}, u32[]{:S(2)}) %collective-permute-start.14) | collective-permute-done | bytes 213024 | tf_op jit(solution)/shard_map/ppermute | solution.py:38
  46.9 1.1 %far_1_2.1 = f32[13,64,128]{2,1,0:T(8,128)S(1)} custom-call(s32[16,128]{1,0:T(8,128)S(1)} %get-tuple-element.56.at_ref, bf16[26,64,128]{2,1,0:T(8,128)(2,1)S(1)} %join.1.refs_0_, bf16[26,64,128]{2,1,0:T(8,128)(2,1)S(1)} %collective-permute-done.8.refs_1_, bf16[26,64,128]{2,1,0:T(8,128)(2,1)S(1)} %collective-permute-done.9.refs_2_, ...), custom_call_target="tpu_custom_call" | custom-call | flops 1703936 | bytes 16384 | tf_op jit(solution)/shard_map/far_1_2/pallas_call | solution.py:360
  48.1 1.1 %far_0_2.1.own_ref = f32[13,64,128]{2,1,0:T(8,128)S(1)} custom-call(s32[16,128]{1,0:T(8,128)S(1)} %get-tuple-element.33.block_ref.at_ref, bf16[26,64,128]{2,1,0:T(8,128)(2,1)S(1)} %join.1.refs_0_, bf16[26,64,128]{2,1,0:T(8,128)(2,1)S(1)} %collective-permute-done.8.refs_1_, bf16[26,64,128]{2,1,0:T(8,128)(2,1)S(1)} %collective-permute-done.9.refs_2_, ...), custom_call_target="tpu_custom_call" | custom-call | flops 1703936 | bytes 16384 | tf_op jit(solution)/shard_map/far_0_2/pallas_call | solution.py:360
  49.2 0.7 %collective-permute-done.15.other_ref = f32[13,64,128]{2,1,0:T(8,128)S(1)} collective-permute-done((f32[13,64,128]{2,1,0:T(8,128)S(1)}, f32[13,64,128]{2,1,0:T(8,128)S(1)}, u32[]{:S(2)}, u32[]{:S(2)}) %collective-permute-start.15) | collective-permute-done | bytes 426016 | tf_op jit(solution)/shard_map/ppermute | solution.py:38
  49.8 2.2 %local_and_field.1 = bf16[6144,128]{1,0:T(8,128)(2,1)} custom-call(f32[13,64,128]{2,1,0:T(8,128)S(1)} %far_0_2.1.own_ref, f32[13,64,128]{2,1,0:T(8,128)S(1)} %collective-permute-done.15.other_ref, bf16[12,64,64]{2,1,0:T(8,128)(2,1)S(1)} %get-tuple-element.58.turned_transfer_ref, bf16[6144,128]{1,0:T(8,128)(2,1)S(1)} %get-tuple-element.59.near_ref, ...), custom_call_target="tpu_custom_call" | custom-call | flops 1572864 | bytes 65536 | tf_op jit(solution)/shard_map/local_and_field/pallas_call | solution.py:486
  (29 shorter events, 1.7 us)
Async XLA Ops:
  0.0 12.7 %copy-start = (bf16[512,1536]{1,0:T(8,128)(2,1)S(1)}, bf16[512,1536]{1,0:T(8,128)(2,1)}, u32[]{:S(2)}) copy-start(bf16[512,1536]{1,0:T(8,128)(2,1)} %constant.6.clone.table_ref) | copy-start | bytes 4718596
  0.0 12.7 %copy-start.1 = (bf16[12,64,512]{2,1,0:T(8,128)(2,1)S(1)}, bf16[12,64,512]{2,1,0:T(8,128)(2,1)}, u32[]{:S(2)}) copy-start(bf16[12,64,512]{2,1,0:T(8,128)(2,1)} %basis_ref.7) | copy-start | bytes 2359300
  0.0 12.7 %copy-start.2 = (s32[12,512]{1,0:T(8,128)S(1)}, s32[12,512]{1,0:T(8,128)}, u32[]{:S(2)}) copy-start(s32[12,512]{1,0:T(8,128)} %order_ref.7) | copy-start | bytes 73732
  0.0 12.7 %copy-start.3 = (s32[12,2]{0,1:T(2,128)S(1)}, s32[12,2]{0,1:T(2,128)}, u32[]{:S(2)}) copy-start(s32[12,2]{0,1:T(2,128)} %param.17) | copy-start | bytes 292
  4.3 12.0 %collective-permute-start.1 = (bf16[13,64,128]{2,1,0:T(8,128)(2,1)S(1)}, bf16[13,64,128]{2,1,0:T(8,128)(2,1)S(1)}, u32[]{:S(2)}, u32[]{:S(2)}) collective-permute-start(bf16[13,64,128]{2,1,0:T(8,128)(2,1)S(1)} %get-tuple-element.34.refs_0_), channel_id=1, source_target_pairs={{0,8},{1,9},{2,10},{3,11},{4,12},{5,13},{6,14},{7,15},{8,16},{9,17... | collective-permute-start | bytes 638984 | tf_op jit(solution)/shard_map/ppermute | solution.py:38
  7.4 8.9 %collective-permute-start.2 = (bf16[13,64,128]{2,1,0:T(8,128)(2,1)S(1)}, bf16[13,64,128]{2,1,0:T(8,128)(2,1)S(1)}, u32[]{:S(2)}, u32[]{:S(2)}) collective-permute-start(bf16[13,64,128]{2,1,0:T(8,128)(2,1)S(1)} %get-tuple-element.34.refs_0_), channel_id=1, source_target_pairs={{0,2},{1,3},{2,0},{3,1},{4,6},{5,7},{6,4},{7,5},{8,10},{9,11},{10,... | collective-permute-start | bytes 638984 | tf_op jit(solution)/shard_map/ppermute | solution.py:38
  8.9 7.5 %collective-permute-start.3 = (bf16[13,64,128]{2,1,0:T(8,128)(2,1)S(1)}, bf16[13,64,128]{2,1,0:T(8,128)(2,1)S(1)}, u32[]{:S(2)}, u32[]{:S(2)}) collective-permute-start(bf16[13,64,128]{2,1,0:T(8,128)(2,1)S(1)} %get-tuple-element.34.refs_0_), channel_id=1, source_target_pairs={{0,4},{1,5},{2,6},{3,7},{4,0},{5,1},{6,2},{7,3},{8,12},{9,13},{10,... | collective-permute-start | bytes 638984 | tf_op jit(solution)/shard_map/ppermute | solution.py:38
  10.4 8.8 %collective-permute-start = (bf16[13,64,128]{2,1,0:T(8,128)(2,1)S(1)}, bf16[13,64,128]{2,1,0:T(8,128)(2,1)S(1)}, u32[]{:S(2)}, u32[]{:S(2)}) collective-permute-start(bf16[13,64,128]{2,1,0:T(8,128)(2,1)S(1)} %get-tuple-element.34.refs_0_), channel_id=1, source_target_pairs={{0,24},{1,25},{2,26},{3,27},{4,28},{5,29},{6,30},{7,31},{8,0},{9,1... | collective-permute-start | bytes 638984 | tf_op jit(solution)/shard_map/ppermute | solution.py:38
  16.3 9.4 %collective-permute-start.4 = (bf16[13,64,128]{2,1,0:T(8,128)(2,1)S(1)}, bf16[13,64,128]{2,1,0:T(8,128)(2,1)S(1)}, u32[]{:S(2)}, u32[]{:S(2)}) collective-permute-start(bf16[13,64,128]{2,1,0:T(8,128)(2,1)S(1)} %collective-permute-done.1.refs_1_), channel_id=1, source_target_pairs={{0,8},{1,9},{2,10},{3,11},{4,12},{5,13},{6,14},{7,15},{8,16},{9,17... | collective-permute-start | bytes 638984 | tf_op jit(solution)/shard_map/ppermute | solution.py:38
  16.4 9.4 %collective-permute-start.5 = (bf16[13,64,128]{2,1,0:T(8,128)(2,1)S(1)}, bf16[13,64,128]{2,1,0:T(8,128)(2,1)S(1)}, u32[]{:S(2)}, u32[]{:S(2)}) collective-permute-start(bf16[13,64,128]{2,1,0:T(8,128)(2,1)S(1)} %collective-permute-done.1.refs_1_), channel_id=1, source_target_pairs={{0,2},{1,3},{2,0},{3,1},{4,6},{5,7},{6,4},{7,5},{8,10},{9,11},{10,... | collective-permute-start | bytes 638984 | tf_op jit(solution)/shard_map/ppermute | solution.py:38
  17.3 8.4 %collective-permute-start.6 = (bf16[13,64,128]{2,1,0:T(8,128)(2,1)S(1)}, bf16[13,64,128]{2,1,0:T(8,128)(2,1)S(1)}, u32[]{:S(2)}, u32[]{:S(2)}) collective-permute-start(bf16[13,64,128]{2,1,0:T(8,128)(2,1)S(1)} %collective-permute-done.1.refs_1_), channel_id=1, source_target_pairs={{0,4},{1,5},{2,6},{3,7},{4,0},{5,1},{6,2},{7,3},{8,12},{9,13},{10,... | collective-permute-start | bytes 638984 | tf_op jit(solution)/shard_map/ppermute | solution.py:38
  19.3 6.5 %collective-permute-start.10 = (bf16[13,64,128]{2,1,0:T(8,128)(2,1)S(1)}, bf16[13,64,128]{2,1,0:T(8,128)(2,1)S(1)}, u32[]{:S(2)}, u32[]{:S(2)}) collective-permute-start(bf16[13,64,128]{2,1,0:T(8,128)(2,1)S(1)} %choose.2), channel_id=1, source_target_pairs={{0,4},{1,3},{2,6},{3,1},{4,0},{5,7},{6,2},{7,5},{8,12},{9,11},{10,... | collective-permute-start | bytes 638984 | tf_op jit(solution)/shard_map/ppermute | solution.py:38
  21.5 4.2 %collective-permute-start.7 = (bf16[512,128]{1,0:T(8,128)(2,1)S(1)}, bf16[512,128]{1,0:T(8,128)(2,1)S(1)}, u32[]{:S(2)}, u32[]{:S(2)}) collective-permute-start(bf16[512,128]{1,0:T(8,128)(2,1)S(1)} %get-tuple-element.44), channel_id=1, source_target_pairs={{1,2},{3,4},{5,6},{7,8},{9,10},{11,12},{13,14},{15,16},{17,18},{19... | collective-permute-start | bytes 393224 | tf_op jit(solution)/shard_map/ppermute | solution.py:537
  25.8 14.2 %collective-permute-start.13 = (bf16[15,64,1024]{2,1,0:T(8,128)(2,1)S(1)}, bf16[15,64,1024]{2,1,0:T(8,128)(2,1)S(1)}, u32[]{:S(2)}, u32[]{:S(2)}) collective-permute-start(bf16[15,64,1024]{2,1,0:T(8,128)(2,1)S(1)} %get-tuple-element.54), channel_id=1, source_target_pairs={{0,1},{1,0},{2,3},{3,2},{4,5},{5,4},{6,7},{7,6},{8,9},{9,8},{10,11... | collective-permute-start | bytes 5898248 | tf_op jit(solution)/shard_map/ppermute | solution.py:38
  28.9 9.4 %collective-permute-start.12 = (bf16[13,64,128]{2,1,0:T(8,128)(2,1)S(1)}, bf16[13,64,128]{2,1,0:T(8,128)(2,1)S(1)}, u32[]{:S(2)}, u32[]{:S(2)}) collective-permute-start(bf16[13,64,128]{2,1,0:T(8,128)(2,1)S(1)} %choose.3), channel_id=1, source_target_pairs={{0,4},{1,3},{2,6},{3,1},{4,0},{5,7},{6,2},{7,5},{8,12},{9,11},{10,... | collective-permute-start | bytes 638984 | tf_op jit(solution)/shard_map/ppermute | solution.py:38
  29.5 17.4 %collective-permute-start.8 = (bf16[26,64,128]{2,1,0:T(8,128)(2,1)S(1)}, bf16[26,64,128]{2,1,0:T(8,128)(2,1)S(1)}, u32[]{:S(2)}, u32[]{:S(2)}) collective-permute-start(bf16[26,64,128]{2,1,0:T(8,128)(2,1)S(1)} %join.1.refs_0_), channel_id=1, source_target_pairs={{0,2},{1,3},{2,0},{3,1},{4,6},{5,7},{6,4},{7,5},{8,10},{9,11},{10,... | collective-permute-start | bytes 1277960 | tf_op jit(solution)/shard_map/ppermute | solution.py:38
  32.0 14.9 %collective-permute-start.9 = (bf16[26,64,128]{2,1,0:T(8,128)(2,1)S(1)}, bf16[26,64,128]{2,1,0:T(8,128)(2,1)S(1)}, u32[]{:S(2)}, u32[]{:S(2)}) collective-permute-start(bf16[26,64,128]{2,1,0:T(8,128)(2,1)S(1)} %join.1.refs_0_), channel_id=1, source_target_pairs={{0,4},{1,5},{2,6},{3,7},{4,0},{5,1},{6,2},{7,3},{8,12},{9,13},{10,... | collective-permute-start | bytes 1277960 | tf_op jit(solution)/shard_map/ppermute | solution.py:38
  33.1 11.5 %collective-permute-start.11 = (bf16[13,64,128]{2,1,0:T(8,128)(2,1)S(1)}, bf16[13,64,128]{2,1,0:T(8,128)(2,1)S(1)}, u32[]{:S(2)}, u32[]{:S(2)}) collective-permute-start(bf16[13,64,128]{2,1,0:T(8,128)(2,1)S(1)} %collective-permute-done.10.refs_6_), channel_id=1, source_target_pairs={{0,24},{1,25},{2,26},{3,27},{4,28},{5,29},{6,30},{7,31},{8,0},{9,1... | collective-permute-start | bytes 638984 | tf_op jit(solution)/shard_map/ppermute | solution.py:38
  38.4 8.5 %collective-permute-start.14 = (bf16[13,64,128]{2,1,0:T(8,128)(2,1)S(1)}, bf16[13,64,128]{2,1,0:T(8,128)(2,1)S(1)}, u32[]{:S(2)}, u32[]{:S(2)}) collective-permute-start(bf16[13,64,128]{2,1,0:T(8,128)(2,1)S(1)} %collective-permute-done.12.refs_7_), channel_id=1, source_target_pairs={{0,8},{1,9},{2,10},{3,11},{4,12},{5,13},{6,14},{7,15},{8,16},{9,17... | collective-permute-start | bytes 638984 | tf_op jit(solution)/shard_map/ppermute | solution.py:38
  48.0 1.8 %collective-permute-start.15 = (f32[13,64,128]{2,1,0:T(8,128)S(1)}, f32[13,64,128]{2,1,0:T(8,128)S(1)}, u32[]{:S(2)}, u32[]{:S(2)}) collective-permute-start(f32[13,64,128]{2,1,0:T(8,128)S(1)} %far_1_2.1), channel_id=1, source_target_pairs={{0,1},{1,0},{2,3},{3,2},{4,5},{5,4},{6,7},{7,6},{8,9},{9,8},{10,11... | collective-permute-start | bytes 1277960 | tf_op jit(solution)/shard_map/ppermute | solution.py:38

commit v16 on v15

--- a/solution.py
+++ b/solution.py
@@ -368,19 +368,32 @@
     )(at, *args)
 
 
+def table_kernel(row, blocks_ref, at_ref):
+    rows, lanes = at_ref.shape
+    at_ref[...] = blocks_ref[row, :rows, :lanes].astype(F32).astype(jnp.int32)
+
+
+def table_of(other_blocks):
+    return pl.pallas_call(
+        functools.partial(table_kernel, other_blocks.shape[0] - 1),
+        name="table",
+        in_specs=[whole()],
+        out_specs=whole(),
+        out_shape=jax.ShapeDtypeStruct((16, 128), jnp.int32),
+        compiler_params=params(16),
+        cost_estimate=cost(0, MIB // 16),
+    )(other_blocks)
+
+
 def near_kernel(edges, pairs, mask_ref, order_ref, table_ref, basis_ref, ordered_ref, *refs):
     if edges:
         me_ref, cross_ref, inner_ref = refs[:3]
-        near_ref, turned_ref, at_ref = refs[-3:]
         even = me_ref[0] % 2 == 0
-    else:
-        near_ref, turned_ref = refs[-2:]
+    near_ref, turned_ref = refs[-2:]
     leaves, _, leaf_len = basis_ref.shape
     fields = ordered_ref.shape[1]
     if edges:
-        rows, rank = at_ref.shape[0], basis_ref.shape[1]
-        blocks = inner_ref[leaves + 2, :rows, :at_ref.shape[1]]
-        at_ref[...] = blocks.astype(F32).astype(jnp.int32)
+        rank = basis_ref.shape[1]
         inner = jnp.concatenate(
             [
                 inner_ref[leaves + 1, :, t * fields:(t + 1) * fields]
@@ -430,7 +443,6 @@
     if halos is not None:
         in_specs += [scalars(), whole(), whole()]
         args += list(halos)
-        out_shape.append(jax.ShapeDtypeStruct((16, 128), jnp.int32))
     if filled is not None:
         aliases = {len(args): 0, len(args) + 1: 1}
         in_specs += [whole()] * 2
@@ -534,16 +546,16 @@
     ready = after(line, from_x, from_y)
     next_x, next_y = over_x(ready), over_y(ready)
     far = onward(choose(me, after(from_x, ready, lines[0]), from_y))
+    own_blocks, my_other, turned_transfer = dense_couplings(
+        after(entry, ready), own_at, inner, coupling, top_coupling, transfer, slots
+    )
+
+    joined = after(join([after(lines[0], my_other)] + lines[1:]), next_x, next_y)
     cross = lax.ppermute(
-        cross,
+        after(cross, joined),
         "subtree",
         [(d, d + 1) for d in range(1, count - 1, 2)] + [(d, d - 1) for d in range(2, count, 2)],
     )
-    own_blocks, my_other, turned_transfer = dense_couplings(
-        after(entry, ready), own_at, inner, coupling, top_coupling, transfer, slots
-    )
-
-    joined = after(join([after(lines[0], my_other)] + lines[1:]), next_x, next_y, cross)
     last_x, last_y = over_x(joined), over_y(joined)
     chosen = choose(me, after(next_x, joined, far), next_y)
     next_far = onward(chosen)
@@ -554,16 +566,17 @@
     last_far = [along_z(far, layers - 1)]
     for _ in range(layers - 3):
         last_far.append(along_z(next_far if len(last_far) == 1 else last_far[-1], 1))
-    held = after(ordered, filled[0])
-    *filled, other_at = near_field(
-        [0, pairs - 1], *near_args, held, halos=(me, cross, other_blocks), filled=filled
-    )
     round_0 = ((shared, line), (from_x, next_x), (from_y, next_y), (far, next_far))
     steps = [0, 1]
+    other_at = table_of(other_blocks)
     own = far_round(0, steps, slots, own_at, round_0, own_blocks)
     other = far_round(1, steps, slots, other_at, round_0, other_blocks)
+    held = after(ordered, filled[0], last_far[0], own, other)
+    filled = near_field(
+        [0, pairs - 1], *near_args, held, halos=(me, cross, other_blocks), filled=filled
+    )
     steps = list(range(2, layers))
-    round_1 = ((joined,), (last_x,), (last_y,), (after(last_far[0], own, other), *last_far[1:]))
+    round_1 = ((joined,), (last_x,), (last_y,), (after(last_far[0], filled[0]), *last_far[1:]))
     other = far_round(1, steps, slots, other_at, round_1, other_blocks, other)
     own = far_round(0, steps, slots, own_at, round_1, own_blocks, own)
     return field(own, over_core(other), turned_transfer, *filled)

time: 52.2 us -> 54.1 us (1.036)
  the two profiles are of different devices: /device:TPU:0 before, /device:TPU:7 now
where the time goes in v16:
time: 54.1 us; the launch traced here: 54 us
  Pallas kernels  25.1 us (46%)
  starting transfers between devices  18.2 us (34%)
  waiting for transfers between devices  10.5 us (19%)
    ppermute x15, starting transfers between devices, send(): lax.ppermute(block, 'subtree', [(d, target(d)) for d in range(count)])  12.6 us
    pallas_call x3, Pallas kernels, near_field(): pl.pallas_call(functools.partial(near_kernel, halos is not None, tuple(pa...  10.7 us
    ppermute x15, waiting for transfers between devices, send(): lax.ppermute(block, 'subtree', [(d, target(d)) for d in range(count)])  6.57 us
    ppermute x1, starting transfers between devices, on_device(): lax.ppermute(after(cross, joined), 'subtree', [(d, d + 1) for d in range(...  5.57 us
    pallas_call x1, Pallas kernels, skeletons_of(): pl.pallas_call(functools.partial(skeleton_kernel, per, layers), name='ord...  4.29 us
    pallas_call x4, Pallas kernels, far_round(): pl.pallas_call(functools.partial(round_kernel, plane, steps, slots, [len(...  4.29 us
    ppermute x1, waiting for transfers between devices, on_device(): lax.ppermute(after(cross, joined), 'subtree', [(d, d + 1) for d in range(...  3.95 us
    pallas_call x1, Pallas kernels, dense_couplings(): pl.pallas_call(functools.partial(dense_kernel, per, slots), name='couplin...  3.47 us
  transfers between devices with their start and end apart: 16, of which 5 were waited for; matrix products, arithmetic and copies ran while one was open for 0% of the time, Pallas kernels for 32%

profile of v16, /device:TPU:7, one launch (start us, length us, event | category | flops | bytes accessed | tf_op | source)
XLA Modules:
  0.0 54.0 jit_solution(7074504914230062017)
XLA Ops:
  0.0 4.3 %order_and_skeleton.1 = (bf16[6144,128]{1,0:T(8,128)(2,1)S(1)}, bf16[13,64,128]{2,1,0:T(8,128)(2,1)S(1)}, bf16[512,128]{1,0:T(8,128)(2,1)S(1)}, bf16[512,128]{1,...) custom-call(s32[1]{0:T(128)} %bitcast.me_ref.refs_0_, s32[12,512]{1,0:T(8,128)} %order_ref.7, ...), custom_call_target="tpu_custom_call" | custom-call | flops 12582912 | bytes 65536 | tf_op jit(solution)/shard_map/order_and_skeleton/pallas_call | solution.py:192
  4.3 1.3 %collective-permute-start.1 = (bf16[13,64,128]{2,1,0:T(8,128)(2,1)S(1)}, bf16[13,64,128]{2,1,0:T(8,128)(2,1)S(1)}, u32[]{:S(2)}, u32[]{:S(2)}) collective-permute-start(bf16[13,64,128]{2,1,0:T(8,128)(2,1)S(1)} %get-tuple-element.34.refs_0_), channel_id=1, source_target_pairs={{0,8},{1,9},{2,10},{3,11},{4,12},{5,13},{6,14},{7,15},{8,16},{9,17... | collective-permute-start | bytes 638984 | tf_op jit(solution)/shard_map/ppermute | solution.py:38
  6.2 2.1 %collective-permute-start = (bf16[13,64,128]{2,1,0:T(8,128)(2,1)S(1)}, bf16[13,64,128]{2,1,0:T(8,128)(2,1)S(1)}, u32[]{:S(2)}, u32[]{:S(2)}) collective-permute-start(bf16[13,64,128]{2,1,0:T(8,128)(2,1)S(1)} %get-tuple-element.34.refs_0_), channel_id=1, source_target_pairs={{0,24},{1,25},{2,26},{3,27},{4,28},{5,29},{6,30},{7,31},{8,0},{9,1... | collective-permute-start | bytes 638984 | tf_op jit(solution)/shard_map/ppermute | solution.py:38
  8.3 3.6 %near_1.1 = (bf16[6144,128]{1,0:T(8,128)(2,1)S(1)}, bf16[3072,128]{1,0:T(8,128)(2,1)S(1)}) custom-call(s32[2,12]{1,0:T(2,128)S(1)} %bitcast.2, s32[12,512]{1,0:T(8,128)S(1)} %copy-done.2, bf16[512,1536]{1,0:T(8,128)(2,1)S(1)} %copy-done, bf16[12,64,512]{2,1,0:T(8,128)(2,1)S(1)} %copy-done.1, bf16[6144,128]{1,0:T(8,128)(2,1)S(1)} %get-tuple-element.53.ordered_ref), custom_call_target="tpu_custom_call" | custom-call | flops 20971520 | bytes 32768 | tf_op jit(solution)/shard_map/near_1/pallas_call | solution.py:450
  11.9 0.6 %collective-permute-done.1.refs_1_ = bf16[13,64,128]{2,1,0:T(8,128)(2,1)S(1)} collective-permute-done((bf16[13,64,128]{2,1,0:T(8,128)(2,1)S(1)}, bf16[13,64,128]{2,1,0:T(8,128)(2,1)S(1)}, u32[]{:S(2)}, u32[]{:S(2)}) %collective-permute-start.1) | collective-permute-done | bytes 213024 | tf_op jit(solution)/shard_map/ppermute | solution.py:38
  12.5 0.8 %collective-permute-start.5 = (bf16[13,64,128]{2,1,0:T(8,128)(2,1)S(1)}, bf16[13,64,128]{2,1,0:T(8,128)(2,1)S(1)}, u32[]{:S(2)}, u32[]{:S(2)}) collective-permute-start(bf16[13,64,128]{2,1,0:T(8,128)(2,1)S(1)} %collective-permute-done.1.refs_1_), channel_id=1, source_target_pairs={{0,2},{1,3},{2,0},{3,1},{4,6},{5,7},{6,4},{7,5},{8,10},{9,11},{10,... | collective-permute-start | bytes 638984 | tf_op jit(solution)/shard_map/ppermute | solution.py:38
  13.2 1.2 %collective-permute-start.6 = (bf16[13,64,128]{2,1,0:T(8,128)(2,1)S(1)}, bf16[13,64,128]{2,1,0:T(8,128)(2,1)S(1)}, u32[]{:S(2)}, u32[]{:S(2)}) collective-permute-start(bf16[13,64,128]{2,1,0:T(8,128)(2,1)S(1)} %collective-permute-done.1.refs_1_), channel_id=1, source_target_pairs={{0,4},{1,5},{2,6},{3,7},{4,0},{5,1},{6,2},{7,3},{8,12},{9,13},{10,... | collective-permute-start | bytes 638984 | tf_op jit(solution)/shard_map/ppermute | solution.py:38
  14.5 4.0 %collective-permute-done.refs_0_ = bf16[13,64,128]{2,1,0:T(8,128)(2,1)S(1)} collective-permute-done((bf16[13,64,128]{2,1,0:T(8,128)(2,1)S(1)}, bf16[13,64,128]{2,1,0:T(8,128)(2,1)S(1)}, u32[]{:S(2)}, u32[]{:S(2)}) %collective-permute-start) | collective-permute-done | bytes 213024 | tf_op jit(solution)/shard_map/ppermute | solution.py:38
  18.5 0.3 collective-permute-start.9
  18.8 3.5 %couplings_by_owner.1 = (bf16[13,64,1024]{2,1,0:T(8,128)(2,1)S(1)}, bf16[15,64,1024]{2,1,0:T(8,128)(2,1)S(1)}, bf16[12,64,64]{2,1,0:T(8,128)(2,1)S(1)}) custom-call(s32[16,128]{1,0:T(8,128)S(1)} %get-tuple-element.40.entry_ref, s32[16,128]{1,0:T(8,128)S(1)} %get-tuple-element.33.block_ref.at_ref, bf16[512,128]{1,0:T(8,128)(2,1)S(1)} %get-tuple-element.41.inner_ref, ...), custom_call_target="tpu_custom_call" | custom-call | bytes 131072 | tf_op jit(solution)/shard_map/couplings_by_owner/pallas_call | solution.py:306
  22.3 1.2 %collective-permute-done.9.refs_6_ = bf16[13,64,128]{2,1,0:T(8,128)(2,1)S(1)} collective-permute-done((bf16[13,64,128]{2,1,0:T(8,128)(2,1)S(1)}, bf16[13,64,128]{2,1,0:T(8,128)(2,1)S(1)}, u32[]{:S(2)}, u32[]{:S(2)}) %collective-permute-start.9) | collective-permute-done | bytes 213024 | tf_op jit(solution)/shard_map/ppermute | solution.py:38
  23.6 1.8 %collective-permute-start.12 = (bf16[15,64,1024]{2,1,0:T(8,128)(2,1)S(1)}, bf16[15,64,1024]{2,1,0:T(8,128)(2,1)S(1)}, u32[]{:S(2)}, u32[]{:S(2)}) collective-permute-start(bf16[15,64,1024]{2,1,0:T(8,128)(2,1)S(1)} %get-tuple-element.52), channel_id=1, source_target_pairs={{0,1},{1,0},{2,3},{3,2},{4,5},{5,4},{6,7},{7,6},{8,9},{9,8},{10,11... | collective-permute-start | bytes 5898248 | tf_op jit(solution)/shard_map/ppermute | solution.py:38
  25.4 1.5 %collective-permute-start.7 = (bf16[26,64,128]{2,1,0:T(8,128)(2,1)S(1)}, bf16[26,64,128]{2,1,0:T(8,128)(2,1)S(1)}, u32[]{:S(2)}, u32[]{:S(2)}) collective-permute-start(bf16[26,64,128]{2,1,0:T(8,128)(2,1)S(1)} %join.1.refs_0_), channel_id=1, source_target_pairs={{0,2},{1,3},{2,0},{3,1},{4,6},{5,7},{6,4},{7,5},{8,10},{9,11},{10,... | collective-permute-start | bytes 1277960 | tf_op jit(solution)/shard_map/ppermute | solution.py:38
  26.9 2.9 %collective-permute-start.10 = (bf16[13,64,128]{2,1,0:T(8,128)(2,1)S(1)}, bf16[13,64,128]{2,1,0:T(8,128)(2,1)S(1)}, u32[]{:S(2)}, u32[]{:S(2)}) collective-permute-start(bf16[13,64,128]{2,1,0:T(8,128)(2,1)S(1)} %collective-permute-done.9.refs_6_), channel_id=1, source_target_pairs={{0,24},{1,25},{2,26},{3,27},{4,28},{5,29},{6,30},{7,31},{8,0},{9,1... | collective-permute-start | bytes 638984 | tf_op jit(solution)/shard_map/ppermute | solution.py:38
  29.8 3.6 %near_3.1 = (bf16[6144,128]{1,0:T(8,128)(2,1)S(1)}, bf16[3072,128]{1,0:T(8,128)(2,1)S(1)}) custom-call(s32[2,12]{1,0:T(2,128)S(1)} %bitcast.3, s32[12,512]{1,0:T(8,128)S(1)} %copy-done.2, bf16[512,1536]{1,0:T(8,128)(2,1)S(1)} %copy-done, bf16[12,64,512]{2,1,0:T(8,128)(2,1)S(1)} %copy-done.1, ...), custom_call_target="tpu_custom_call", output_to_operand_aliasing={{0}: (5, {}), {1}: (6, {})} | custom-call | flops 20971520 | bytes 32768 | tf_op jit(solution)/shard_map/near_3/pallas_call | solution.py:450
  33.5 5.6 %collective-permute-start.13 = (bf16[512,128]{1,0:T(8,128)(2,1)S(1)}, bf16[512,128]{1,0:T(8,128)(2,1)S(1)}, u32[]{:S(2)}, u32[]{:S(2)}) collective-permute-start(bf16[512,128]{1,0:T(8,128)(2,1)S(1)} %get-tuple-element.55), channel_id=1, source_target_pairs={{1,2},{3,4},{5,6},{7,8},{9,10},{11,12},{13,14},{15,16},{17,18},{19... | collective-permute-start | bytes 393224 | tf_op jit(solution)/shard_map/ppermute | solution.py:554
  39.1 1.1 %far_0_0.1.refs_6_ = f32[13,64,128]{2,1,0:T(8,128)S(1)} custom-call(s32[16,128]{1,0:T(8,128)S(1)} %get-tuple-element.33.block_ref.at_ref, bf16[13,64,128]{2,1,0:T(8,128)(2,1)S(1)} %get-tuple-element.34.refs_0_, bf16[13,64,128]{2,1,0:T(8,128)(2,1)S(1)} %collective-permute-done.1.refs_1_, bf16[13,64,128]{2,1,0:T(8,128)(2,1)S(1)} %collective-permute-done.2.x_ref.refs_2_, ...), custom_call_target="tpu_custom_call" | custom-call | flops 1703936 | bytes 16384 | tf_op jit(solution)/shard_map/far_0_0/pallas_call | solution.py:360
  40.2 1.1 %far_1_0.1.refs_6_ = f32[13,64,128]{2,1,0:T(8,128)S(1)} custom-call(s32[16,128]{1,0:T(8,128)S(1)} %table.1.at_ref, bf16[13,64,128]{2,1,0:T(8,128)(2,1)S(1)} %get-tuple-element.34.refs_0_, bf16[13,64,128]{2,1,0:T(8,128)(2,1)S(1)} %collective-permute-done.1.refs_1_, bf16[13,64,128]{2,1,0:T(8,128)(2,1)S(1)} %collective-permute-done.2.x_ref.refs_2_, ...), custom_call_target="tpu_custom_call" | custom-call | flops 1703936 | bytes 16384 | tf_op jit(solution)/shard_map/far_1_0/pallas_call | solution.py:360
  41.3 4.0 %collective-permute-done.13.refs_1_ = bf16[512,128]{1,0:T(8,128)(2,1)S(1)} collective-permute-done((bf16[512,128]{1,0:T(8,128)(2,1)S(1)}, bf16[512,128]{1,0:T(8,128)(2,1)S(1)}, u32[]{:S(2)}, u32[]{:S(2)}) %collective-permute-start.13) | collective-permute-done | bytes 131104 | tf_op jit(solution)/shard_map/ppermute | solution.py:554
  45.2 3.6 %near_0.1 = (bf16[6144,128]{1,0:T(8,128)(2,1)S(1)}, bf16[3072,128]{1,0:T(8,128)(2,1)S(1)}) custom-call(s32[2,12]{1,0:T(2,128)S(1)} %bitcast.4, s32[12,512]{1,0:T(8,128)S(1)} %copy-done.2, bf16[512,1536]{1,0:T(8,128)(2,1)S(1)} %copy-done, bf16[12,64,512]{2,1,0:T(8,128)(2,1)S(1)} %copy-done.1, ...), custom_call_target="tpu_custom_call", output_to_operand_aliasing={{0}: (8, {}), {1}: (9, {})} | custom-call | flops 20971520 | bytes 32768 | tf_op jit(solution)/shard_map/near_0/pallas_call | solution.py:450
  48.8 1.1 %far_1_2.1 = f32[13,64,128]{2,1,0:T(8,128)S(1)} custom-call(s32[16,128]{1,0:T(8,128)S(1)} %table.1.at_ref, bf16[26,64,128]{2,1,0:T(8,128)(2,1)S(1)} %join.1.refs_0_, bf16[26,64,128]{2,1,0:T(8,128)(2,1)S(1)} %collective-permute-done.7.refs_1_, bf16[26,64,128]{2,1,0:T(8,128)(2,1)S(1)} %collective-permute-done.8.refs_2_, ...), custom_call_target="tpu_custom_call" | custom-call | flops 1703936 | bytes 16384 | tf_op jit(solution)/shard_map/far_1_2/pallas_call | solution.py:360
  50.0 1.1 %far_0_2.1.own_ref = f32[13,64,128]{2,1,0:T(8,128)S(1)} custom-call(s32[16,128]{1,0:T(8,128)S(1)} %get-tuple-element.33.block_ref.at_ref, bf16[26,64,128]{2,1,0:T(8,128)(2,1)S(1)} %join.1.refs_0_, bf16[26,64,128]{2,1,0:T(8,128)(2,1)S(1)} %collective-permute-done.7.refs_1_, bf16[26,64,128]{2,1,0:T(8,128)(2,1)S(1)} %collective-permute-done.8.refs_2_, ...), custom_call_target="tpu_custom_call" | custom-call | flops 1703936 | bytes 16384 | tf_op jit(solution)/shard_map/far_0_2/pallas_call | solution.py:360
  51.1 0.7 %collective-permute-done.15.other_ref = f32[13,64,128]{2,1,0:T(8,128)S(1)} collective-permute-done((f32[13,64,128]{2,1,0:T(8,128)S(1)}, f32[13,64,128]{2,1,0:T(8,128)S(1)}, u32[]{:S(2)}, u32[]{:S(2)}) %collective-permute-start.15) | collective-permute-done | bytes 426016 | tf_op jit(solution)/shard_map/ppermute | solution.py:38
  51.7 2.2 %local_and_field.1 = bf16[6144,128]{1,0:T(8,128)(2,1)} custom-call(f32[13,64,128]{2,1,0:T(8,128)S(1)} %far_0_2.1.own_ref, f32[13,64,128]{2,1,0:T(8,128)S(1)} %collective-permute-done.15.other_ref, bf16[12,64,64]{2,1,0:T(8,128)(2,1)S(1)} %get-tuple-element.59.turned_transfer_ref, bf16[6144,128]{1,0:T(8,128)(2,1)S(1)} %get-tuple-element.57.near_ref, ...), custom_call_target="tpu_custom_call" | custom-call | flops 1572864 | bytes 65536 | tf_op jit(solution)/shard_map/local_and_field/pallas_call | solution.py:498
  (30 shorter events, 0.8 us)
Async XLA Ops:
  0.0 8.3 %copy-start = (bf16[512,1536]{1,0:T(8,128)(2,1)S(1)}, bf16[512,1536]{1,0:T(8,128)(2,1)}, u32[]{:S(2)}) copy-start(bf16[512,1536]{1,0:T(8,128)(2,1)} %constant.6.clone.table_ref) | copy-start | bytes 4718596
  0.0 8.3 %copy-start.1 = (bf16[12,64,512]{2,1,0:T(8,128)(2,1)S(1)}, bf16[12,64,512]{2,1,0:T(8,128)(2,1)}, u32[]{:S(2)}) copy-start(bf16[12,64,512]{2,1,0:T(8,128)(2,1)} %basis_ref.7) | copy-start | bytes 2359300
  0.0 8.3 %copy-start.2 = (s32[12,512]{1,0:T(8,128)S(1)}, s32[12,512]{1,0:T(8,128)}, u32[]{:S(2)}) copy-start(s32[12,512]{1,0:T(8,128)} %order_ref.7) | copy-start | bytes 73732
  0.0 8.3 %copy-start.3 = (s32[12,2]{0,1:T(2,128)S(1)}, s32[12,2]{0,1:T(2,128)}, u32[]{:S(2)}) copy-start(s32[12,2]{0,1:T(2,128)} %param.17) | copy-start | bytes 292
  4.3 8.1 %collective-permute-start.1 = (bf16[13,64,128]{2,1,0:T(8,128)(2,1)S(1)}, bf16[13,64,128]{2,1,0:T(8,128)(2,1)S(1)}, u32[]{:S(2)}, u32[]{:S(2)}) collective-permute-start(bf16[13,64,128]{2,1,0:T(8,128)(2,1)S(1)} %get-tuple-element.34.refs_0_), channel_id=1, source_target_pairs={{0,8},{1,9},{2,10},{3,11},{4,12},{5,13},{6,14},{7,15},{8,16},{9,17... | collective-permute-start | bytes 638984 | tf_op jit(solution)/shard_map/ppermute | solution.py:38
  5.7 6.8 %collective-permute-start.2 = (bf16[13,64,128]{2,1,0:T(8,128)(2,1)S(1)}, bf16[13,64,128]{2,1,0:T(8,128)(2,1)S(1)}, u32[]{:S(2)}, u32[]{:S(2)}) collective-permute-start(bf16[13,64,128]{2,1,0:T(8,128)(2,1)S(1)} %get-tuple-element.34.refs_0_), channel_id=1, source_target_pairs={{0,2},{1,3},{2,0},{3,1},{4,6},{5,7},{6,4},{7,5},{8,10},{9,11},{10,... | collective-permute-start | bytes 638984 | tf_op jit(solution)/shard_map/ppermute | solution.py:38
  5.9 6.5 %collective-permute-start.3 = (bf16[13,64,128]{2,1,0:T(8,128)(2,1)S(1)}, bf16[13,64,128]{2,1,0:T(8,128)(2,1)S(1)}, u32[]{:S(2)}, u32[]{:S(2)}) collective-permute-start(bf16[13,64,128]{2,1,0:T(8,128)(2,1)S(1)} %get-tuple-element.34.refs_0_), channel_id=1, source_target_pairs={{0,4},{1,5},{2,6},{3,7},{4,0},{5,1},{6,2},{7,3},{8,12},{9,13},{10,... | collective-permute-start | bytes 638984 | tf_op jit(solution)/shard_map/ppermute | solution.py:38
  6.2 12.3 %collective-permute-start = (bf16[13,64,128]{2,1,0:T(8,128)(2,1)S(1)}, bf16[13,64,128]{2,1,0:T(8,128)(2,1)S(1)}, u32[]{:S(2)}, u32[]{:S(2)}) collective-permute-start(bf16[13,64,128]{2,1,0:T(8,128)(2,1)S(1)} %get-tuple-element.34.refs_0_), channel_id=1, source_target_pairs={{0,24},{1,25},{2,26},{3,27},{4,28},{5,29},{6,30},{7,31},{8,0},{9,1... | collective-permute-start | bytes 638984 | tf_op jit(solution)/shard_map/ppermute | solution.py:38
  12.5 9.8 %collective-permute-start.4 = (bf16[13,64,128]{2,1,0:T(8,128)(2,1)S(1)}, bf16[13,64,128]{2,1,0:T(8,128)(2,1)S(1)}, u32[]{:S(2)}, u32[]{:S(2)}) collective-permute-start(bf16[13,64,128]{2,1,0:T(8,128)(2,1)S(1)} %collective-permute-done.1.refs_1_), channel_id=1, source_target_pairs={{0,8},{1,9},{2,10},{3,11},{4,12},{5,13},{6,14},{7,15},{8,16},{9,17... | collective-permute-start | bytes 638984 | tf_op jit(solution)/shard_map/ppermute | solution.py:38
  12.5 9.8 %collective-permute-start.5 = (bf16[13,64,128]{2,1,0:T(8,128)(2,1)S(1)}, bf16[13,64,128]{2,1,0:T(8,128)(2,1)S(1)}, u32[]{:S(2)}, u32[]{:S(2)}) collective-permute-start(bf16[13,64,128]{2,1,0:T(8,128)(2,1)S(1)} %collective-permute-done.1.refs_1_), channel_id=1, source_target_pairs={{0,2},{1,3},{2,0},{3,1},{4,6},{5,7},{6,4},{7,5},{8,10},{9,11},{10,... | collective-permute-start | bytes 638984 | tf_op jit(solution)/shard_map/ppermute | solution.py:38
  13.2 9.1 %collective-permute-start.6 = (bf16[13,64,128]{2,1,0:T(8,128)(2,1)S(1)}, bf16[13,64,128]{2,1,0:T(8,128)(2,1)S(1)}, u32[]{:S(2)}, u32[]{:S(2)}) collective-permute-start(bf16[13,64,128]{2,1,0:T(8,128)(2,1)S(1)} %collective-permute-done.1.refs_1_), channel_id=1, source_target_pairs={{0,4},{1,5},{2,6},{3,7},{4,0},{5,1},{6,2},{7,3},{8,12},{9,13},{10,... | collective-permute-start | bytes 638984 | tf_op jit(solution)/shard_map/ppermute | solution.py:38
  18.5 5.1 %collective-permute-start.9 = (bf16[13,64,128]{2,1,0:T(8,128)(2,1)S(1)}, bf16[13,64,128]{2,1,0:T(8,128)(2,1)S(1)}, u32[]{:S(2)}, u32[]{:S(2)}) collective-permute-start(bf16[13,64,128]{2,1,0:T(8,128)(2,1)S(1)} %choose.2), channel_id=1, source_target_pairs={{0,4},{1,3},{2,6},{3,1},{4,0},{5,7},{6,2},{7,5},{8,12},{9,11},{10,... | collective-permute-start | bytes 638984 | tf_op jit(solution)/shard_map/ppermute | solution.py:38
  23.6 9.9 %collective-permute-start.12 = (bf16[15,64,1024]{2,1,0:T(8,128)(2,1)S(1)}, bf16[15,64,1024]{2,1,0:T(8,128)(2,1)S(1)}, u32[]{:S(2)}, u32[]{:S(2)}) collective-permute-start(bf16[15,64,1024]{2,1,0:T(8,128)(2,1)S(1)} %get-tuple-element.52), channel_id=1, source_target_pairs={{0,1},{1,0},{2,3},{3,2},{4,5},{5,4},{6,7},{7,6},{8,9},{9,8},{10,11... | collective-permute-start | bytes 5898248 | tf_op jit(solution)/shard_map/ppermute | solution.py:38
  25.4 8.0 %collective-permute-start.11 = (bf16[13,64,128]{2,1,0:T(8,128)(2,1)S(1)}, bf16[13,64,128]{2,1,0:T(8,128)(2,1)S(1)}, u32[]{:S(2)}, u32[]{:S(2)}) collective-permute-start(bf16[13,64,128]{2,1,0:T(8,128)(2,1)S(1)} %choose.3), channel_id=1, source_target_pairs={{0,4},{1,3},{2,6},{3,1},{4,0},{5,7},{6,2},{7,5},{8,12},{9,11},{10,... | collective-permute-start | bytes 638984 | tf_op jit(solution)/shard_map/ppermute | solution.py:38
  25.4 23.4 %collective-permute-start.7 = (bf16[26,64,128]{2,1,0:T(8,128)(2,1)S(1)}, bf16[26,64,128]{2,1,0:T(8,128)(2,1)S(1)}, u32[]{:S(2)}, u32[]{:S(2)}) collective-permute-start(bf16[26,64,128]{2,1,0:T(8,128)(2,1)S(1)} %join.1.refs_0_), channel_id=1, source_target_pairs={{0,2},{1,3},{2,0},{3,1},{4,6},{5,7},{6,4},{7,5},{8,10},{9,11},{10,... | collective-permute-start | bytes 1277960 | tf_op jit(solution)/shard_map/ppermute | solution.py:38
  26.9 22.0 %collective-permute-start.8 = (bf16[26,64,128]{2,1,0:T(8,128)(2,1)S(1)}, bf16[26,64,128]{2,1,0:T(8,128)(2,1)S(1)}, u32[]{:S(2)}, u32[]{:S(2)}) collective-permute-start(bf16[26,64,128]{2,1,0:T(8,128)(2,1)S(1)} %join.1.refs_0_), channel_id=1, source_target_pairs={{0,4},{1,5},{2,6},{3,7},{4,0},{5,1},{6,2},{7,3},{8,12},{9,13},{10,... | collective-permute-start | bytes 1277960 | tf_op jit(solution)/shard_map/ppermute | solution.py:38
  26.9 14.4 %collective-permute-start.10 = (bf16[13,64,128]{2,1,0:T(8,128)(2,1)S(1)}, bf16[13,64,128]{2,1,0:T(8,128)(2,1)S(1)}, u32[]{:S(2)}, u32[]{:S(2)}) collective-permute-start(bf16[13,64,128]{2,1,0:T(8,128)(2,1)S(1)} %collective-permute-done.9.refs_6_), channel_id=1, source_target_pairs={{0,24},{1,25},{2,26},{3,27},{4,28},{5,29},{6,30},{7,31},{8,0},{9,1... | collective-permute-start | bytes 638984 | tf_op jit(solution)/shard_map/ppermute | solution.py:38
  33.4 15.4 %collective-permute-start.14 = (bf16[13,64,128]{2,1,0:T(8,128)(2,1)S(1)}, bf16[13,64,128]{2,1,0:T(8,128)(2,1)S(1)}, u32[]{:S(2)}, u32[]{:S(2)}) collective-permute-start(bf16[13,64,128]{2,1,0:T(8,128)(2,1)S(1)} %collective-permute-done.11.refs_7_), channel_id=1, source_target_pairs={{0,8},{1,9},{2,10},{3,11},{4,12},{5,13},{6,14},{7,15},{8,16},{9,17... | collective-permute-start | bytes 638984 | tf_op jit(solution)/shard_map/ppermute | solution.py:38
  33.5 11.7 %collective-permute-start.13 = (bf16[512,128]{1,0:T(8,128)(2,1)S(1)}, bf16[512,128]{1,0:T(8,128)(2,1)S(1)}, u32[]{:S(2)}, u32[]{:S(2)}) collective-permute-start(bf16[512,128]{1,0:T(8,128)(2,1)S(1)} %get-tuple-element.55), channel_id=1, source_target_pairs={{1,2},{3,4},{5,6},{7,8},{9,10},{11,12},{13,14},{15,16},{17,18},{19... | collective-permute-start | bytes 393224 | tf_op jit(solution)/shard_map/ppermute | solution.py:554
  49.9 1.8 %collective-permute-start.15 = (f32[13,64,128]{2,1,0:T(8,128)S(1)}, f32[13,64,128]{2,1,0:T(8,128)S(1)}, u32[]{:S(2)}, u32[]{:S(2)}) collective-permute-start(f32[13,64,128]{2,1,0:T(8,128)S(1)} %far_1_2.1), channel_id=1, source_target_pairs={{0,1},{1,0},{2,3},{3,2},{4,5},{5,4},{6,7},{7,6},{8,9},{9,8},{10,11... | collective-permute-start | bytes 1277960 | tf_op jit(solution)/shard_map/ppermute | solution.py:38

commit v17 on v15

--- a/solution.py
+++ b/solution.py
@@ -326,13 +326,15 @@
     )(entry, block, inner, *in_hbm(coupling, top_coupling, transfer))
 
 
-def round_kernel(plane, steps, slots, counts, at_ref, *refs):
+def round_kernel(planes, steps, slots, counts, *refs):
+    number = len(planes)
+    tables, refs = refs[:number], refs[number:]
     sides = []
-    for number in counts:
-        sides.append(refs[:number])
-        refs = refs[number:]
-    blocks_ref, out = refs[0], refs[-1]
-    rows, rank, _ = out.shape
+    for length in counts:
+        sides.append(refs[:length])
+        refs = refs[length:]
+    blocks, totals, outs = refs[:number], refs[number:-number], refs[-number:]
+    rows, rank, _ = outs[0].shape
     low, high = steps[0] * 4 * rank, (steps[-1] + 1) * 4 * rank
 
     def block_at(side, base, index):
@@ -341,31 +343,35 @@
                 return ref[base + index]
             base -= ref.shape[0]
 
-    for row in range(rows):
-        chosen = [
-            block_at(side, place * rows, at_ref[(row + 1) % rows, plane * slots + step * 4 + q])
-            for place, step in enumerate(steps)
-            for q, side in enumerate(sides)
-        ]
-        value = dot(blocks_ref[row, :, low:high], jnp.concatenate(chosen, axis=0))
-        if len(refs) > 2:
-            value = value + refs[1][row]
-        out[row] = value
-
-
-def far_round(plane, steps, slots, at, parts, blocks, total=None):
+    for place, plane in enumerate(planes):
+        for row in range(rows):
+            chosen = [
+                block_at(
+                    side, at * rows, tables[place][(row + 1) % rows, plane * slots + step * 4 + q]
+                )
+                for at, step in enumerate(steps)
+                for q, side in enumerate(sides)
+            ]
+            value = dot(blocks[place][row, :, low:high], jnp.concatenate(chosen, axis=0))
+            if totals:
+                value = value + totals[place][row]
+            outs[place][row] = value
+
+
+def far_rounds(planes, steps, slots, tables, parts, blocks, totals=()):
     rank, fields = parts[0][0].shape[1:]
     rows = parts[0][0].shape[0] // (1 if len(parts[0]) > 1 else len(steps))
-    args = [part for side in parts for part in side] + [blocks] + ([] if total is None else [total])
-    return pl.pallas_call(
-        functools.partial(round_kernel, plane, steps, slots, [len(side) for side in parts]),
-        name="far_" + str(plane) + "_" + str(steps[0]),
-        in_specs=[scalars()] + [whole()] * len(args),
-        out_specs=whole(),
-        out_shape=jax.ShapeDtypeStruct((rows, rank, fields), F32),
+    args = [part for side in parts for part in side] + list(blocks) + list(totals)
+    shape = jax.ShapeDtypeStruct((rows, rank, fields), F32)
+    return pl.pallas_call(
+        functools.partial(round_kernel, planes, steps, slots, [len(side) for side in parts]),
+        name="far_" + str(planes[-1]) + "_" + str(steps[0]),
+        in_specs=[scalars()] * len(planes) + [whole()] * len(args),
+        out_specs=[whole()] * len(planes),
+        out_shape=[shape] * len(planes),
         compiler_params=params(16 if slots <= 16 else 48),
         cost_estimate=cost(rows * rank * 4 * rank * fields * 2 * len(steps), MIB),
-    )(at, *args)
+    )(*tables, *args)
 
 
 def near_kernel(edges, pairs, mask_ref, order_ref, table_ref, basis_ref, ordered_ref, *refs):
@@ -549,23 +555,24 @@
     next_far = onward(chosen)
     other_blocks = over_core(after(my_other, chosen))
     held = after(ordered, joined)
-    filled = near_field(list(range(cut, pairs - 1)), *near_args, held, filled=filled)
+    filled = near_field(list(range(cut, pairs - 2)), *near_args, held, filled=filled)
     next_far = after(next_far, filled[0])
     last_far = [along_z(far, layers - 1)]
     for _ in range(layers - 3):
         last_far.append(along_z(next_far if len(last_far) == 1 else last_far[-1], 1))
+    filled = near_field([pairs - 2], *near_args, ordered, filled=filled)
     held = after(ordered, filled[0])
     *filled, other_at = near_field(
         [0, pairs - 1], *near_args, held, halos=(me, cross, other_blocks), filled=filled
     )
     round_0 = ((shared, line), (from_x, next_x), (from_y, next_y), (far, next_far))
-    steps = [0, 1]
-    own = far_round(0, steps, slots, own_at, round_0, own_blocks)
-    other = far_round(1, steps, slots, other_at, round_0, other_blocks)
+    own, other = far_rounds(
+        (0, 1), [0, 1], slots, (own_at, other_at), round_0, (own_blocks, other_blocks)
+    )
     steps = list(range(2, layers))
-    round_1 = ((joined,), (last_x,), (last_y,), (after(last_far[0], own, other), *last_far[1:]))
-    other = far_round(1, steps, slots, other_at, round_1, other_blocks, other)
-    own = far_round(0, steps, slots, own_at, round_1, own_blocks, own)
+    round_1 = ((joined,), (last_x,), (last_y,), (after(last_far[0], own), *last_far[1:]))
+    (other,) = far_rounds((1,), steps, slots, (other_at,), round_1, (other_blocks,), (other,))
+    (own,) = far_rounds((0,), steps, slots, (own_at,), round_1, (own_blocks,), (own,))
     return field(own, over_core(other), turned_transfer, *filled)
 
 

time: 52.2 us -> 51.4 us (0.985)
  waiting for transfers between devices: 3.24 us -> 1.07 us
  starting transfers between devices: 23.5 us -> 25 us
    ppermute x15, waiting for transfers between devices: 3.24 us -> 1.07 us  [send(): lax.ppermute(block, 'subtree', [(d, target(d)) for d in range(count)])]
    ppermute x15, starting transfers between devices: 22.8 us -> 24.3 us  [send(): lax.ppermute(block, 'subtree', [(d, target(d)) for d in range(count)])]
    pallas_call x4 -> x3, Pallas kernels: 4.34 us -> 3.66 us  [far_rounds(): pl.pallas_call(functools.partial(round_kernel, planes, steps, slots, [len...]
    pallas_call x3 -> x4, Pallas kernels: 10.7 us -> 11.2 us  [near_field(): pl.pallas_call(functools.partial(near_kernel, halos is not None, tuple(pa...]
  transfers between devices with their start and end apart: 16 -> 16, of which waited for: 3 -> 2; matrix products, arithmetic and copies ran while one was open for 0% -> 0% of each run, Pallas kernels for 34% -> 34%
where the time goes in v17:
time: 51.4 us; the launch traced here: 51.2 us
  Pallas kernels  25 us (49%)
  starting transfers between devices  25 us (49%)
  waiting for transfers between devices  1.07 us (2%)
    ppermute x15, starting transfers between devices, send(): lax.ppermute(block, 'subtree', [(d, target(d)) for d in range(count)])  24.3 us
    pallas_call x4, Pallas kernels, near_field(): pl.pallas_call(functools.partial(near_kernel, halos is not None, tuple(pa...  11.2 us
    pallas_call x1, Pallas kernels, skeletons_of(): pl.pallas_call(functools.partial(skeleton_kernel, per, layers), name='ord...  4.29 us
    pallas_call x3, Pallas kernels, far_rounds(): pl.pallas_call(functools.partial(round_kernel, planes, steps, slots, [len...  3.66 us
    pallas_call x1, Pallas kernels, dense_couplings(): pl.pallas_call(functools.partial(dense_kernel, per, slots), name='couplin...  3.49 us
    pallas_call x1, Pallas kernels, field(): pl.pallas_call(functools.partial(field_kernel, per), name='local_and_fiel...  2.21 us
    ppermute x15, waiting for transfers between devices, send(): lax.ppermute(block, 'subtree', [(d, target(d)) for d in range(count)])  1.07 us
  transfers between devices with their start and end apart: 16, of which 2 were waited for; matrix products, arithmetic and copies ran while one was open for 0% of the time, Pallas kernels for 34%

profile of v17, /device:TPU:0, one launch (start us, length us, event | category | flops | bytes accessed | tf_op | source)
XLA Modules:
  0.0 51.2 jit_solution(15577054650441508656)
XLA Ops:
  0.0 4.3 %order_and_skeleton.1 = (bf16[6144,128]{1,0:T(8,128)(2,1)S(1)}, bf16[13,64,128]{2,1,0:T(8,128)(2,1)S(1)}, bf16[512,128]{1,0:T(8,128)(2,1)S(1)}, bf16[512,128]{1,...) custom-call(s32[1]{0:T(128)} %bitcast.me_ref.refs_0_, s32[12,512]{1,0:T(8,128)} %order_ref.9, ...), custom_call_target="tpu_custom_call" | custom-call | flops 12582912 | bytes 65536 | tf_op jit(solution)/shard_map/order_and_skeleton/pallas_call | solution.py:192
  4.3 3.1 %collective-permute-start.1 = (bf16[13,64,128]{2,1,0:T(8,128)(2,1)S(1)}, bf16[13,64,128]{2,1,0:T(8,128)(2,1)S(1)}, u32[]{:S(2)}, u32[]{:S(2)}) collective-permute-start(bf16[13,64,128]{2,1,0:T(8,128)(2,1)S(1)} %get-tuple-element.38.refs_2_), channel_id=1, source_target_pairs={{0,8},{1,9},{2,10},{3,11},{4,12},{5,13},{6,14},{7,15},{8,16},{9,17... | collective-permute-start | bytes 638984 | tf_op jit(solution)/shard_map/ppermute | solution.py:38
  7.4 1.5 %collective-permute-start.2 = (bf16[13,64,128]{2,1,0:T(8,128)(2,1)S(1)}, bf16[13,64,128]{2,1,0:T(8,128)(2,1)S(1)}, u32[]{:S(2)}, u32[]{:S(2)}) collective-permute-start(bf16[13,64,128]{2,1,0:T(8,128)(2,1)S(1)} %get-tuple-element.38.refs_2_), channel_id=1, source_target_pairs={{0,2},{1,3},{2,0},{3,1},{4,6},{5,7},{6,4},{7,5},{8,10},{9,11},{10,... | collective-permute-start | bytes 638984 | tf_op jit(solution)/shard_map/ppermute | solution.py:38
  8.9 1.5 %collective-permute-start.3 = (bf16[13,64,128]{2,1,0:T(8,128)(2,1)S(1)}, bf16[13,64,128]{2,1,0:T(8,128)(2,1)S(1)}, u32[]{:S(2)}, u32[]{:S(2)}) collective-permute-start(bf16[13,64,128]{2,1,0:T(8,128)(2,1)S(1)} %get-tuple-element.38.refs_2_), channel_id=1, source_target_pairs={{0,4},{1,5},{2,6},{3,7},{4,0},{5,1},{6,2},{7,3},{8,12},{9,13},{10,... | collective-permute-start | bytes 638984 | tf_op jit(solution)/shard_map/ppermute | solution.py:38
  10.4 2.2 %collective-permute-start = (bf16[13,64,128]{2,1,0:T(8,128)(2,1)S(1)}, bf16[13,64,128]{2,1,0:T(8,128)(2,1)S(1)}, u32[]{:S(2)}, u32[]{:S(2)}) collective-permute-start(bf16[13,64,128]{2,1,0:T(8,128)(2,1)S(1)} %get-tuple-element.38.refs_2_), channel_id=1, source_target_pairs={{0,24},{1,25},{2,26},{3,27},{4,28},{5,29},{6,30},{7,31},{8,0},{9,1... | collective-permute-start | bytes 638984 | tf_op jit(solution)/shard_map/ppermute | solution.py:38
  12.7 3.6 %near_1.1 = (bf16[6144,128]{1,0:T(8,128)(2,1)S(1)}, bf16[3072,128]{1,0:T(8,128)(2,1)S(1)}) custom-call(s32[2,12]{1,0:T(2,128)S(1)} %bitcast.2, s32[12,512]{1,0:T(8,128)S(1)} %copy-done.2, bf16[512,1536]{1,0:T(8,128)(2,1)S(1)} %copy-done, bf16[12,64,512]{2,1,0:T(8,128)(2,1)S(1)} %copy-done.1, bf16[6144,128]{1,0:T(8,128)(2,1)S(1)} %get-tuple-element.56.ordered_ref), custom_call_target="tpu_custom_call" | custom-call | flops 20971520 | bytes 32768 | tf_op jit(solution)/shard_map/near_1/pallas_call | solution.py:444
  16.4 1.0 %collective-permute-start.5 = (bf16[13,64,128]{2,1,0:T(8,128)(2,1)S(1)}, bf16[13,64,128]{2,1,0:T(8,128)(2,1)S(1)}, u32[]{:S(2)}, u32[]{:S(2)}) collective-permute-start(bf16[13,64,128]{2,1,0:T(8,128)(2,1)S(1)} %collective-permute-done.1.refs_3_), channel_id=1, source_target_pairs={{0,2},{1,3},{2,0},{3,1},{4,6},{5,7},{6,4},{7,5},{8,10},{9,11},{10,... | collective-permute-start | bytes 638984 | tf_op jit(solution)/shard_map/ppermute | solution.py:38
  17.3 1.6 %collective-permute-start.6 = (bf16[13,64,128]{2,1,0:T(8,128)(2,1)S(1)}, bf16[13,64,128]{2,1,0:T(8,128)(2,1)S(1)}, u32[]{:S(2)}, u32[]{:S(2)}) collective-permute-start(bf16[13,64,128]{2,1,0:T(8,128)(2,1)S(1)} %collective-permute-done.1.refs_3_), channel_id=1, source_target_pairs={{0,4},{1,5},{2,6},{3,7},{4,0},{5,1},{6,2},{7,3},{8,12},{9,13},{10,... | collective-permute-start | bytes 638984 | tf_op jit(solution)/shard_map/ppermute | solution.py:38
  19.3 2.2 %collective-permute-start.10 = (bf16[13,64,128]{2,1,0:T(8,128)(2,1)S(1)}, bf16[13,64,128]{2,1,0:T(8,128)(2,1)S(1)}, u32[]{:S(2)}, u32[]{:S(2)}) collective-permute-start(bf16[13,64,128]{2,1,0:T(8,128)(2,1)S(1)} %choose.2), channel_id=1, source_target_pairs={{0,4},{1,3},{2,6},{3,1},{4,0},{5,7},{6,2},{7,5},{8,12},{9,11},{10,... | collective-permute-start | bytes 638984 | tf_op jit(solution)/shard_map/ppermute | solution.py:38
  21.5 0.7 %collective-permute-start.7 = (bf16[512,128]{1,0:T(8,128)(2,1)S(1)}, bf16[512,128]{1,0:T(8,128)(2,1)S(1)}, u32[]{:S(2)}, u32[]{:S(2)}) collective-permute-start(bf16[512,128]{1,0:T(8,128)(2,1)S(1)} %get-tuple-element.48), channel_id=1, source_target_pairs={{1,2},{3,4},{5,6},{7,8},{9,10},{11,12},{13,14},{15,16},{17,18},{19... | collective-permute-start | bytes 393224 | tf_op jit(solution)/shard_map/ppermute | solution.py:543
  22.2 3.5 %couplings_by_owner.1 = (bf16[13,64,1024]{2,1,0:T(8,128)(2,1)S(1)}, bf16[15,64,1024]{2,1,0:T(8,128)(2,1)S(1)}, bf16[12,64,64]{2,1,0:T(8,128)(2,1)S(1)}) custom-call(s32[16,128]{1,0:T(8,128)S(1)} %get-tuple-element.44.entry_ref, s32[16,128]{1,0:T(8,128)S(1)} %get-tuple-element.37.block_ref.refs_0_, bf16[512,128]{1,0:T(8,128)(2,1)S(1)} %get-tuple-element.45.inner_ref, ...), custom_call_target="tpu_custom_call" | custom-call | bytes 131072 | tf_op jit(solution)/shard_map/couplings_by_owner/pallas_call | solution.py:306
  25.8 3.2 %collective-permute-start.12 = (bf16[15,64,1024]{2,1,0:T(8,128)(2,1)S(1)}, bf16[15,64,1024]{2,1,0:T(8,128)(2,1)S(1)}, u32[]{:S(2)}, u32[]{:S(2)}) collective-permute-start(bf16[15,64,1024]{2,1,0:T(8,128)(2,1)S(1)} %get-tuple-element.58), channel_id=1, source_target_pairs={{0,1},{1,0},{2,3},{3,2},{4,5},{5,4},{6,7},{7,6},{8,9},{9,8},{10,11... | collective-permute-start | bytes 5898248 | tf_op jit(solution)/shard_map/ppermute | solution.py:38
  29.5 2.5 %collective-permute-start.8 = (bf16[26,64,128]{2,1,0:T(8,128)(2,1)S(1)}, bf16[26,64,128]{2,1,0:T(8,128)(2,1)S(1)}, u32[]{:S(2)}, u32[]{:S(2)}) collective-permute-start(bf16[26,64,128]{2,1,0:T(8,128)(2,1)S(1)} %join.1.refs_1_), channel_id=1, source_target_pairs={{0,2},{1,3},{2,0},{3,1},{4,6},{5,7},{6,4},{7,5},{8,10},{9,11},{10,... | collective-permute-start | bytes 1277960 | tf_op jit(solution)/shard_map/ppermute | solution.py:38
  32.0 1.2 %collective-permute-start.9 = (bf16[26,64,128]{2,1,0:T(8,128)(2,1)S(1)}, bf16[26,64,128]{2,1,0:T(8,128)(2,1)S(1)}, u32[]{:S(2)}, u32[]{:S(2)}) collective-permute-start(bf16[26,64,128]{2,1,0:T(8,128)(2,1)S(1)} %join.1.refs_1_), channel_id=1, source_target_pairs={{0,4},{1,5},{2,6},{3,7},{4,0},{5,1},{6,2},{7,3},{8,12},{9,13},{10,... | collective-permute-start | bytes 1277960 | tf_op jit(solution)/shard_map/ppermute | solution.py:38
  33.1 1.7 %collective-permute-start.11 = (bf16[13,64,128]{2,1,0:T(8,128)(2,1)S(1)}, bf16[13,64,128]{2,1,0:T(8,128)(2,1)S(1)}, u32[]{:S(2)}, u32[]{:S(2)}) collective-permute-start(bf16[13,64,128]{2,1,0:T(8,128)(2,1)S(1)} %collective-permute-done.10.refs_8_), channel_id=1, source_target_pairs={{0,24},{1,25},{2,26},{3,27},{4,28},{5,29},{6,30},{7,31},{8,0},{9,1... | collective-permute-start | bytes 638984 | tf_op jit(solution)/shard_map/ppermute | solution.py:38
  34.8 2.0 %near_3.1 = (bf16[6144,128]{1,0:T(8,128)(2,1)S(1)}, bf16[3072,128]{1,0:T(8,128)(2,1)S(1)}) custom-call(s32[2,12]{1,0:T(2,128)S(1)} %bitcast.3, s32[12,512]{1,0:T(8,128)S(1)} %copy-done.2, bf16[512,1536]{1,0:T(8,128)(2,1)S(1)} %copy-done, bf16[12,64,512]{2,1,0:T(8,128)(2,1)S(1)} %copy-done.1, ...), custom_call_target="tpu_custom_call", output_to_operand_aliasing={{0}: (5, {}), {1}: (6, {})} | custom-call | flops 10485760 | bytes 16384 | tf_op jit(solution)/shard_map/near_3/pallas_call | solution.py:444
  36.8 2.1 %collective-permute-start.14 = (bf16[13,64,128]{2,1,0:T(8,128)(2,1)S(1)}, bf16[13,64,128]{2,1,0:T(8,128)(2,1)S(1)}, u32[]{:S(2)}, u32[]{:S(2)}) collective-permute-start(bf16[13,64,128]{2,1,0:T(8,128)(2,1)S(1)} %collective-permute-done.13.refs_9_), channel_id=1, source_target_pairs={{0,8},{1,9},{2,10},{3,11},{4,12},{5,13},{6,14},{7,15},{8,16},{9,17... | collective-permute-start | bytes 638984 | tf_op jit(solution)/shard_map/ppermute | solution.py:38
  38.9 2.0 %near_4.1 = (bf16[6144,128]{1,0:T(8,128)(2,1)S(1)}, bf16[3072,128]{1,0:T(8,128)(2,1)S(1)}) custom-call(s32[2,12]{1,0:T(2,128)S(1)} %bitcast.4, s32[12,512]{1,0:T(8,128)S(1)} %copy-done.2, bf16[512,1536]{1,0:T(8,128)(2,1)S(1)} %copy-done, bf16[12,64,512]{2,1,0:T(8,128)(2,1)S(1)} %copy-done.1, ...), custom_call_target="tpu_custom_call", output_to_operand_aliasing={{0}: (5, {}), {1}: (6, {})} | custom-call | flops 10485760 | bytes 16384 | tf_op jit(solution)/shard_map/near_4/pallas_call | solution.py:444
  41.0 3.6 %near_0.1 = (bf16[6144,128]{1,0:T(8,128)(2,1)S(1)}, bf16[3072,128]{1,0:T(8,128)(2,1)S(1)}, s32[16,128]{1,0:T(8,128)S(1)}) custom-call(s32[2,12]{1,0:T(2,128)S(1)} %bitcast.5, s32[12,512]{1,0:T(8,128)S(1)} %copy-done.2, bf16[512,1536]{1,0:T(8,128)(2,1)S(1)} %copy-done, ...), custom_call_target="tpu_custom_call", output_to_operand_aliasing={{0}: (8, {}), {1}: (9, {})} | custom-call | flops 20971520 | bytes 32768 | tf_op jit(solution)/shard_map/near_0/pallas_call | solution.py:444
  44.6 1.5 %far_1_0.1 = (f32[13,64,128]{2,1,0:T(8,128)S(1)}, f32[13,64,128]{2,1,0:T(8,128)S(1)}) custom-call(s32[16,128]{1,0:T(8,128)S(1)} %get-tuple-element.37.block_ref.refs_0_, s32[16,128]{1,0:T(8,128)S(1)} %get-tuple-element.60.refs_1_.refs_0_, bf16[13,64,128]{2,1,0:T(8,128)(2,1)S(1)} %get-tuple-element.38.refs_2_, ...), custom_call_target="tpu_custom_call" | custom-call | flops 1703936 | bytes 16384 | tf_op jit(solution)/shard_map/far_1_0/pallas_call | solution.py:366
  46.1 1.1 %far_1_2.1 = f32[13,64,128]{2,1,0:T(8,128)S(1)} custom-call(s32[16,128]{1,0:T(8,128)S(1)} %get-tuple-element.60.refs_1_.refs_0_, bf16[26,64,128]{2,1,0:T(8,128)(2,1)S(1)} %join.1.refs_1_, bf16[26,64,128]{2,1,0:T(8,128)(2,1)S(1)} %collective-permute-done.8.refs_2_, bf16[26,64,128]{2,1,0:T(8,128)(2,1)S(1)} %collective-permute-done.9.refs_3_, ...), custom_call_target="tpu_custom_call" | custom-call | flops 1703936 | bytes 16384 | tf_op jit(solution)/shard_map/far_1_2/pallas_call | solution.py:366
  47.3 1.1 %far_0_2.1.own_ref = f32[13,64,128]{2,1,0:T(8,128)S(1)} custom-call(s32[16,128]{1,0:T(8,128)S(1)} %get-tuple-element.37.block_ref.refs_0_, bf16[26,64,128]{2,1,0:T(8,128)(2,1)S(1)} %join.1.refs_1_, bf16[26,64,128]{2,1,0:T(8,128)(2,1)S(1)} %collective-permute-done.8.refs_2_, bf16[26,64,128]{2,1,0:T(8,128)(2,1)S(1)} %collective-permute-done.9.refs_3_, ...), custom_call_target="tpu_custom_call" | custom-call | flops 1703936 | bytes 16384 | tf_op jit(solution)/shard_map/far_0_2/pallas_call | solution.py:366
  48.4 0.7 %collective-permute-done.15.other_ref = f32[13,64,128]{2,1,0:T(8,128)S(1)} collective-permute-done((f32[13,64,128]{2,1,0:T(8,128)S(1)}, f32[13,64,128]{2,1,0:T(8,128)S(1)}, u32[]{:S(2)}, u32[]{:S(2)}) %collective-permute-start.15) | collective-permute-done | bytes 426016 | tf_op jit(solution)/shard_map/ppermute | solution.py:38
  49.0 2.2 %local_and_field.1 = bf16[6144,128]{1,0:T(8,128)(2,1)} custom-call(f32[13,64,128]{2,1,0:T(8,128)S(1)} %far_0_2.1.own_ref, f32[13,64,128]{2,1,0:T(8,128)S(1)} %collective-permute-done.15.other_ref, bf16[12,64,64]{2,1,0:T(8,128)(2,1)S(1)} %get-tuple-element.66.turned_transfer_ref, bf16[6144,128]{1,0:T(8,128)(2,1)S(1)} %get-tuple-element.67.near_ref, ...), custom_call_target="tpu_custom_call" | custom-call | flops 1572864 | bytes 65536 | tf_op jit(solution)/shard_map/local_and_field/pallas_call | solution.py:492
  (29 shorter events, 1.2 us)
Async XLA Ops:
  0.0 12.7 %copy-start = (bf16[512,1536]{1,0:T(8,128)(2,1)S(1)}, bf16[512,1536]{1,0:T(8,128)(2,1)}, u32[]{:S(2)}) copy-start(bf16[512,1536]{1,0:T(8,128)(2,1)} %constant.6.clone.table_ref) | copy-start | bytes 4718596
  0.0 12.7 %copy-start.1 = (bf16[12,64,512]{2,1,0:T(8,128)(2,1)S(1)}, bf16[12,64,512]{2,1,0:T(8,128)(2,1)}, u32[]{:S(2)}) copy-start(bf16[12,64,512]{2,1,0:T(8,128)(2,1)} %basis_ref.9) | copy-start | bytes 2359300
  0.0 12.7 %copy-start.2 = (s32[12,512]{1,0:T(8,128)S(1)}, s32[12,512]{1,0:T(8,128)}, u32[]{:S(2)}) copy-start(s32[12,512]{1,0:T(8,128)} %order_ref.9) | copy-start | bytes 73732
  0.0 12.7 %copy-start.3 = (s32[12,2]{0,1:T(2,128)S(1)}, s32[12,2]{0,1:T(2,128)}, u32[]{:S(2)}) copy-start(s32[12,2]{0,1:T(2,128)} %param.17) | copy-start | bytes 292
  4.3 12.0 %collective-permute-start.1 = (bf16[13,64,128]{2,1,0:T(8,128)(2,1)S(1)}, bf16[13,64,128]{2,1,0:T(8,128)(2,1)S(1)}, u32[]{:S(2)}, u32[]{:S(2)}) collective-permute-start(bf16[13,64,128]{2,1,0:T(8,128)(2,1)S(1)} %get-tuple-element.38.refs_2_), channel_id=1, source_target_pairs={{0,8},{1,9},{2,10},{3,11},{4,12},{5,13},{6,14},{7,15},{8,16},{9,17... | collective-permute-start | bytes 638984 | tf_op jit(solution)/shard_map/ppermute | solution.py:38
  7.4 8.9 %collective-permute-start.2 = (bf16[13,64,128]{2,1,0:T(8,128)(2,1)S(1)}, bf16[13,64,128]{2,1,0:T(8,128)(2,1)S(1)}, u32[]{:S(2)}, u32[]{:S(2)}) collective-permute-start(bf16[13,64,128]{2,1,0:T(8,128)(2,1)S(1)} %get-tuple-element.38.refs_2_), channel_id=1, source_target_pairs={{0,2},{1,3},{2,0},{3,1},{4,6},{5,7},{6,4},{7,5},{8,10},{9,11},{10,... | collective-permute-start | bytes 638984 | tf_op jit(solution)/shard_map/ppermute | solution.py:38
  8.9 7.5 %collective-permute-start.3 = (bf16[13,64,128]{2,1,0:T(8,128)(2,1)S(1)}, bf16[13,64,128]{2,1,0:T(8,128)(2,1)S(1)}, u32[]{:S(2)}, u32[]{:S(2)}) collective-permute-start(bf16[13,64,128]{2,1,0:T(8,128)(2,1)S(1)} %get-tuple-element.38.refs_2_), channel_id=1, source_target_pairs={{0,4},{1,5},{2,6},{3,7},{4,0},{5,1},{6,2},{7,3},{8,12},{9,13},{10,... | collective-permute-start | bytes 638984 | tf_op jit(solution)/shard_map/ppermute | solution.py:38
  10.4 8.8 %collective-permute-start = (bf16[13,64,128]{2,1,0:T(8,128)(2,1)S(1)}, bf16[13,64,128]{2,1,0:T(8,128)(2,1)S(1)}, u32[]{:S(2)}, u32[]{:S(2)}) collective-permute-start(bf16[13,64,128]{2,1,0:T(8,128)(2,1)S(1)} %get-tuple-element.38.refs_2_), channel_id=1, source_target_pairs={{0,24},{1,25},{2,26},{3,27},{4,28},{5,29},{6,30},{7,31},{8,0},{9,1... | collective-permute-start | bytes 638984 | tf_op jit(solution)/shard_map/ppermute | solution.py:38
  16.3 9.4 %collective-permute-start.4 = (bf16[13,64,128]{2,1,0:T(8,128)(2,1)S(1)}, bf16[13,64,128]{2,1,0:T(8,128)(2,1)S(1)}, u32[]{:S(2)}, u32[]{:S(2)}) collective-permute-start(bf16[13,64,128]{2,1,0:T(8,128)(2,1)S(1)} %collective-permute-done.1.refs_3_), channel_id=1, source_target_pairs={{0,8},{1,9},{2,10},{3,11},{4,12},{5,13},{6,14},{7,15},{8,16},{9,17... | collective-permute-start | bytes 638984 | tf_op jit(solution)/shard_map/ppermute | solution.py:38
  16.4 9.4 %collective-permute-start.5 = (bf16[13,64,128]{2,1,0:T(8,128)(2,1)S(1)}, bf16[13,64,128]{2,1,0:T(8,128)(2,1)S(1)}, u32[]{:S(2)}, u32[]{:S(2)}) collective-permute-start(bf16[13,64,128]{2,1,0:T(8,128)(2,1)S(1)} %collective-permute-done.1.refs_3_), channel_id=1, source_target_pairs={{0,2},{1,3},{2,0},{3,1},{4,6},{5,7},{6,4},{7,5},{8,10},{9,11},{10,... | collective-permute-start | bytes 638984 | tf_op jit(solution)/shard_map/ppermute | solution.py:38
  17.3 8.4 %collective-permute-start.6 = (bf16[13,64,128]{2,1,0:T(8,128)(2,1)S(1)}, bf16[13,64,128]{2,1,0:T(8,128)(2,1)S(1)}, u32[]{:S(2)}, u32[]{:S(2)}) collective-permute-start(bf16[13,64,128]{2,1,0:T(8,128)(2,1)S(1)} %collective-permute-done.1.refs_3_), channel_id=1, source_target_pairs={{0,4},{1,5},{2,6},{3,7},{4,0},{5,1},{6,2},{7,3},{8,12},{9,13},{10,... | collective-permute-start | bytes 638984 | tf_op jit(solution)/shard_map/ppermute | solution.py:38
  19.3 6.5 %collective-permute-start.10 = (bf16[13,64,128]{2,1,0:T(8,128)(2,1)S(1)}, bf16[13,64,128]{2,1,0:T(8,128)(2,1)S(1)}, u32[]{:S(2)}, u32[]{:S(2)}) collective-permute-start(bf16[13,64,128]{2,1,0:T(8,128)(2,1)S(1)} %choose.2), channel_id=1, source_target_pairs={{0,4},{1,3},{2,6},{3,1},{4,0},{5,7},{6,2},{7,5},{8,12},{9,11},{10,... | collective-permute-start | bytes 638984 | tf_op jit(solution)/shard_map/ppermute | solution.py:38
  21.5 4.2 %collective-permute-start.7 = (bf16[512,128]{1,0:T(8,128)(2,1)S(1)}, bf16[512,128]{1,0:T(8,128)(2,1)S(1)}, u32[]{:S(2)}, u32[]{:S(2)}) collective-permute-start(bf16[512,128]{1,0:T(8,128)(2,1)S(1)} %get-tuple-element.48), channel_id=1, source_target_pairs={{1,2},{3,4},{5,6},{7,8},{9,10},{11,12},{13,14},{15,16},{17,18},{19... | collective-permute-start | bytes 393224 | tf_op jit(solution)/shard_map/ppermute | solution.py:543
  25.8 15.2 %collective-permute-start.12 = (bf16[15,64,1024]{2,1,0:T(8,128)(2,1)S(1)}, bf16[15,64,1024]{2,1,0:T(8,128)(2,1)S(1)}, u32[]{:S(2)}, u32[]{:S(2)}) collective-permute-start(bf16[15,64,1024]{2,1,0:T(8,128)(2,1)S(1)} %get-tuple-element.58), channel_id=1, source_target_pairs={{0,1},{1,0},{2,3},{3,2},{4,5},{5,4},{6,7},{7,6},{8,9},{9,8},{10,11... | collective-permute-start | bytes 5898248 | tf_op jit(solution)/shard_map/ppermute | solution.py:38
  28.9 7.9 %collective-permute-start.13 = (bf16[13,64,128]{2,1,0:T(8,128)(2,1)S(1)}, bf16[13,64,128]{2,1,0:T(8,128)(2,1)S(1)}, u32[]{:S(2)}, u32[]{:S(2)}) collective-permute-start(bf16[13,64,128]{2,1,0:T(8,128)(2,1)S(1)} %choose.3), channel_id=1, source_target_pairs={{0,4},{1,3},{2,6},{3,1},{4,0},{5,7},{6,2},{7,5},{8,12},{9,11},{10,... | collective-permute-start | bytes 638984 | tf_op jit(solution)/shard_map/ppermute | solution.py:38
  29.5 16.6 %collective-permute-start.8 = (bf16[26,64,128]{2,1,0:T(8,128)(2,1)S(1)}, bf16[26,64,128]{2,1,0:T(8,128)(2,1)S(1)}, u32[]{:S(2)}, u32[]{:S(2)}) collective-permute-start(bf16[26,64,128]{2,1,0:T(8,128)(2,1)S(1)} %join.1.refs_1_), channel_id=1, source_target_pairs={{0,2},{1,3},{2,0},{3,1},{4,6},{5,7},{6,4},{7,5},{8,10},{9,11},{10,... | collective-permute-start | bytes 1277960 | tf_op jit(solution)/shard_map/ppermute | solution.py:38
  32.0 14.1 %collective-permute-start.9 = (bf16[26,64,128]{2,1,0:T(8,128)(2,1)S(1)}, bf16[26,64,128]{2,1,0:T(8,128)(2,1)S(1)}, u32[]{:S(2)}, u32[]{:S(2)}) collective-permute-start(bf16[26,64,128]{2,1,0:T(8,128)(2,1)S(1)} %join.1.refs_1_), channel_id=1, source_target_pairs={{0,4},{1,5},{2,6},{3,7},{4,0},{5,1},{6,2},{7,3},{8,12},{9,13},{10,... | collective-permute-start | bytes 1277960 | tf_op jit(solution)/shard_map/ppermute | solution.py:38
  33.1 12.9 %collective-permute-start.11 = (bf16[13,64,128]{2,1,0:T(8,128)(2,1)S(1)}, bf16[13,64,128]{2,1,0:T(8,128)(2,1)S(1)}, u32[]{:S(2)}, u32[]{:S(2)}) collective-permute-start(bf16[13,64,128]{2,1,0:T(8,128)(2,1)S(1)} %collective-permute-done.10.refs_8_), channel_id=1, source_target_pairs={{0,24},{1,25},{2,26},{3,27},{4,28},{5,29},{6,30},{7,31},{8,0},{9,1... | collective-permute-start | bytes 638984 | tf_op jit(solution)/shard_map/ppermute | solution.py:38
  36.8 9.3 %collective-permute-start.14 = (bf16[13,64,128]{2,1,0:T(8,128)(2,1)S(1)}, bf16[13,64,128]{2,1,0:T(8,128)(2,1)S(1)}, u32[]{:S(2)}, u32[]{:S(2)}) collective-permute-start(bf16[13,64,128]{2,1,0:T(8,128)(2,1)S(1)} %collective-permute-done.13.refs_9_), channel_id=1, source_target_pairs={{0,8},{1,9},{2,10},{3,11},{4,12},{5,13},{6,14},{7,15},{8,16},{9,17... | collective-permute-start | bytes 638984 | tf_op jit(solution)/shard_map/ppermute | solution.py:38
  47.2 1.8 %collective-permute-start.15 = (f32[13,64,128]{2,1,0:T(8,128)S(1)}, f32[13,64,128]{2,1,0:T(8,128)S(1)}, u32[]{:S(2)}, u32[]{:S(2)}) collective-permute-start(f32[13,64,128]{2,1,0:T(8,128)S(1)} %far_1_2.1), channel_id=1, source_target_pairs={{0,1},{1,0},{2,3},{3,2},{4,5},{5,4},{6,7},{7,6},{8,9},{9,8},{10,11... | collective-permute-start | bytes 1277960 | tf_op jit(solution)/shard_map/ppermute | solution.py:38

commit v18 on v17

--- a/solution.py
+++ b/solution.py
@@ -406,20 +406,20 @@
         value = leaf_at(leaf - 1 + 2 * side)
         return jnp.where(mask_ref[side, leaf] > 0, value, jnp.zeros_like(value))
 
-    for pair in pairs:
-        columns = [
-            jnp.concatenate([masked(leaf, 0), leaf_at(leaf), masked(leaf, 1)], axis=0)
-            for leaf in (2 * pair, 2 * pair + 1)
-        ]
-        near = dot(table_ref[...], jnp.concatenate(columns, axis=1)).astype(BF)
-        turned = []
-        for i in range(2):
-            leaf = 2 * pair + i
-            hot = one_hot_grid(order_ref[leaf:leaf + 1, :], leaf_len)
-            both = jnp.concatenate([near[:, i * fields:(i + 1) * fields], basis_ref[leaf].T], axis=1)
-            moved = dot(hot, both).astype(BF)
-            near_ref[leaf * leaf_len:(leaf + 1) * leaf_len, :] = moved[:, :fields]
-            turned.append(moved[:, fields:])
+    near_leaves = [leaf for pair in pairs for leaf in (2 * pair, 2 * pair + 1)]
+    columns = [
+        jnp.concatenate([masked(leaf, 0), leaf_at(leaf), masked(leaf, 1)], axis=0)
+        for leaf in near_leaves
+    ]
+    near = dot(table_ref[...], jnp.concatenate(columns, axis=1)).astype(BF)
+    moved = []
+    for i, leaf in enumerate(near_leaves):
+        hot = one_hot_grid(order_ref[leaf:leaf + 1, :], leaf_len)
+        both = jnp.concatenate([near[:, i * fields:(i + 1) * fields], basis_ref[leaf].T], axis=1)
+        moved.append(dot(hot, both).astype(BF))
+        near_ref[leaf * leaf_len:(leaf + 1) * leaf_len, :] = moved[i][:, :fields]
+    for i, pair in enumerate(pairs):
+        turned = [part[:, fields:] for part in moved[2 * i:2 * i + 2]]
         turned_ref[pair * leaf_len:(pair + 1) * leaf_len, :] = jnp.concatenate(turned, axis=1)
 
 
@@ -555,12 +555,11 @@
     next_far = onward(chosen)
     other_blocks = over_core(after(my_other, chosen))
     held = after(ordered, joined)
-    filled = near_field(list(range(cut, pairs - 2)), *near_args, held, filled=filled)
+    filled = near_field(list(range(cut, pairs - 1)), *near_args, held, filled=filled)
     next_far = after(next_far, filled[0])
     last_far = [along_z(far, layers - 1)]
     for _ in range(layers - 3):
         last_far.append(along_z(next_far if len(last_far) == 1 else last_far[-1], 1))
-    filled = near_field([pairs - 2], *near_args, ordered, filled=filled)
     held = after(ordered, filled[0])
     *filled, other_at = near_field(
         [0, pairs - 1], *near_args, held, halos=(me, cross, other_blocks), filled=filled

time: 51.4 us -> 51.4 us (level)
  waiting for transfers between devices: 1.07 us -> 5.68 us
  Pallas kernels: 25 us -> 20.4 us
    ppermute x15, waiting for transfers between devices: 1.07 us -> 5.68 us  [send(): lax.ppermute(block, 'subtree', [(d, target(d)) for d in range(count)])]
    pallas_call x4 -> x3, Pallas kernels: 11.2 us -> 6.7 us  [near_field(): pl.pallas_call(functools.partial(near_kernel, halos is not None, tuple(pa...]
  transfers between devices with their start and end apart: 16 -> 16, of which waited for: 2 -> 4; matrix products, arithmetic and copies ran while one was open for 0% -> 0% of each run, Pallas kernels for 34% -> 25%
where the time goes in v18:
time: 51.4 us; the launch traced here: 51.2 us
  starting transfers between devices  25 us (49%)
  Pallas kernels  20.4 us (40%)
  waiting for transfers between devices  5.68 us (11%)
    ppermute x15, starting transfers between devices, send(): lax.ppermute(block, 'subtree', [(d, target(d)) for d in range(count)])  24.3 us
    pallas_call x3, Pallas kernels, near_field(): pl.pallas_call(functools.partial(near_kernel, halos is not None, tuple(pa...  6.7 us
    ppermute x15, waiting for transfers between devices, send(): lax.ppermute(block, 'subtree', [(d, target(d)) for d in range(count)])  5.68 us
    pallas_call x1, Pallas kernels, skeletons_of(): pl.pallas_call(functools.partial(skeleton_kernel, per, layers), name='ord...  4.29 us
    pallas_call x3, Pallas kernels, far_rounds(): pl.pallas_call(functools.partial(round_kernel, planes, steps, slots, [len...  3.67 us
    pallas_call x1, Pallas kernels, dense_couplings(): pl.pallas_call(functools.partial(dense_kernel, per, slots), name='couplin...  3.49 us
    pallas_call x1, Pallas kernels, field(): pl.pallas_call(functools.partial(field_kernel, per), name='local_and_fiel...  2.2 us
  transfers between devices with their start and end apart: 16, of which 4 were waited for; matrix products, arithmetic and copies ran while one was open for 0% of the time, Pallas kernels for 25%

profile of v18, /device:TPU:0, one launch (start us, length us, event | category | flops | bytes accessed | tf_op | source)
XLA Modules:
  0.0 51.2 jit_solution(9140084346292474659)
XLA Ops:
  0.0 4.3 %order_and_skeleton.1 = (bf16[6144,128]{1,0:T(8,128)(2,1)S(1)}, bf16[13,64,128]{2,1,0:T(8,128)(2,1)S(1)}, bf16[512,128]{1,0:T(8,128)(2,1)S(1)}, bf16[512,128]{1,...) custom-call(s32[1]{0:T(128)} %bitcast.me_ref.refs_0_, s32[12,512]{1,0:T(8,128)} %order_ref.7, ...), custom_call_target="tpu_custom_call" | custom-call | flops 12582912 | bytes 65536 | tf_op jit(solution)/shard_map/order_and_skeleton/pallas_call | solution.py:192
  4.3 3.1 %collective-permute-start.1 = (bf16[13,64,128]{2,1,0:T(8,128)(2,1)S(1)}, bf16[13,64,128]{2,1,0:T(8,128)(2,1)S(1)}, u32[]{:S(2)}, u32[]{:S(2)}) collective-permute-start(bf16[13,64,128]{2,1,0:T(8,128)(2,1)S(1)} %get-tuple-element.36.refs_2_), channel_id=1, source_target_pairs={{0,8},{1,9},{2,10},{3,11},{4,12},{5,13},{6,14},{7,15},{8,16},{9,17... | collective-permute-start | bytes 638984 | tf_op jit(solution)/shard_map/ppermute | solution.py:38
  7.4 1.5 %collective-permute-start.2 = (bf16[13,64,128]{2,1,0:T(8,128)(2,1)S(1)}, bf16[13,64,128]{2,1,0:T(8,128)(2,1)S(1)}, u32[]{:S(2)}, u32[]{:S(2)}) collective-permute-start(bf16[13,64,128]{2,1,0:T(8,128)(2,1)S(1)} %get-tuple-element.36.refs_2_), channel_id=1, source_target_pairs={{0,2},{1,3},{2,0},{3,1},{4,6},{5,7},{6,4},{7,5},{8,10},{9,11},{10,... | collective-permute-start | bytes 638984 | tf_op jit(solution)/shard_map/ppermute | solution.py:38
  8.9 1.5 %collective-permute-start.3 = (bf16[13,64,128]{2,1,0:T(8,128)(2,1)S(1)}, bf16[13,64,128]{2,1,0:T(8,128)(2,1)S(1)}, u32[]{:S(2)}, u32[]{:S(2)}) collective-permute-start(bf16[13,64,128]{2,1,0:T(8,128)(2,1)S(1)} %get-tuple-element.36.refs_2_), channel_id=1, source_target_pairs={{0,4},{1,5},{2,6},{3,7},{4,0},{5,1},{6,2},{7,3},{8,12},{9,13},{10,... | collective-permute-start | bytes 638984 | tf_op jit(solution)/shard_map/ppermute | solution.py:38
  10.4 2.2 %collective-permute-start = (bf16[13,64,128]{2,1,0:T(8,128)(2,1)S(1)}, bf16[13,64,128]{2,1,0:T(8,128)(2,1)S(1)}, u32[]{:S(2)}, u32[]{:S(2)}) collective-permute-start(bf16[13,64,128]{2,1,0:T(8,128)(2,1)S(1)} %get-tuple-element.36.refs_2_), channel_id=1, source_target_pairs={{0,24},{1,25},{2,26},{3,27},{4,28},{5,29},{6,30},{7,31},{8,0},{9,1... | collective-permute-start | bytes 638984 | tf_op jit(solution)/shard_map/ppermute | solution.py:38
  12.7 2.2 %near_1.1 = (bf16[6144,128]{1,0:T(8,128)(2,1)S(1)}, bf16[3072,128]{1,0:T(8,128)(2,1)S(1)}) custom-call(s32[2,12]{1,0:T(2,128)S(1)} %bitcast.2, s32[12,512]{1,0:T(8,128)S(1)} %copy-done.2, bf16[512,1536]{1,0:T(8,128)(2,1)S(1)} %copy-done, bf16[12,64,512]{2,1,0:T(8,128)(2,1)S(1)} %copy-done.1, bf16[6144,128]{1,0:T(8,128)(2,1)S(1)} %get-tuple-element.52.ordered_ref), custom_call_target="tpu_custom_call" | custom-call | flops 20971520 | bytes 32768 | tf_op jit(solution)/shard_map/near_1/pallas_call | solution.py:444
  15.3 2.0 %collective-permute-start.5 = (bf16[13,64,128]{2,1,0:T(8,128)(2,1)S(1)}, bf16[13,64,128]{2,1,0:T(8,128)(2,1)S(1)}, u32[]{:S(2)}, u32[]{:S(2)}) collective-permute-start(bf16[13,64,128]{2,1,0:T(8,128)(2,1)S(1)} %collective-permute-done.1.refs_3_), channel_id=1, source_target_pairs={{0,2},{1,3},{2,0},{3,1},{4,6},{5,7},{6,4},{7,5},{8,10},{9,11},{10,... | collective-permute-start | bytes 638984 | tf_op jit(solution)/shard_map/ppermute | solution.py:38
  17.3 1.6 %collective-permute-start.6 = (bf16[13,64,128]{2,1,0:T(8,128)(2,1)S(1)}, bf16[13,64,128]{2,1,0:T(8,128)(2,1)S(1)}, u32[]{:S(2)}, u32[]{:S(2)}) collective-permute-start(bf16[13,64,128]{2,1,0:T(8,128)(2,1)S(1)} %collective-permute-done.1.refs_3_), channel_id=1, source_target_pairs={{0,4},{1,5},{2,6},{3,7},{4,0},{5,1},{6,2},{7,3},{8,12},{9,13},{10,... | collective-permute-start | bytes 638984 | tf_op jit(solution)/shard_map/ppermute | solution.py:38
  18.9 1.2 %collective-permute-done.refs_0_ = bf16[13,64,128]{2,1,0:T(8,128)(2,1)S(1)} collective-permute-done((bf16[13,64,128]{2,1,0:T(8,128)(2,1)S(1)}, bf16[13,64,128]{2,1,0:T(8,128)(2,1)S(1)}, u32[]{:S(2)}, u32[]{:S(2)}) %collective-permute-start) | collective-permute-done | bytes 213024 | tf_op jit(solution)/shard_map/ppermute | solution.py:38
  20.1 1.8 %collective-permute-start.10 = (bf16[13,64,128]{2,1,0:T(8,128)(2,1)S(1)}, bf16[13,64,128]{2,1,0:T(8,128)(2,1)S(1)}, u32[]{:S(2)}, u32[]{:S(2)}) collective-permute-start(bf16[13,64,128]{2,1,0:T(8,128)(2,1)S(1)} %choose.2), channel_id=1, source_target_pairs={{0,4},{1,3},{2,6},{3,1},{4,0},{5,7},{6,2},{7,5},{8,12},{9,11},{10,... | collective-permute-start | bytes 638984 | tf_op jit(solution)/shard_map/ppermute | solution.py:38
  22.6 3.5 %couplings_by_owner.1 = (bf16[13,64,1024]{2,1,0:T(8,128)(2,1)S(1)}, bf16[15,64,1024]{2,1,0:T(8,128)(2,1)S(1)}, bf16[12,64,64]{2,1,0:T(8,128)(2,1)S(1)}) custom-call(s32[16,128]{1,0:T(8,128)S(1)} %get-tuple-element.42.entry_ref, s32[16,128]{1,0:T(8,128)S(1)} %get-tuple-element.35.block_ref.refs_0_, bf16[512,128]{1,0:T(8,128)(2,1)S(1)} %get-tuple-element.43.inner_ref, ...), custom_call_target="tpu_custom_call" | custom-call | bytes 131072 | tf_op jit(solution)/shard_map/couplings_by_owner/pallas_call | solution.py:306
  26.2 3.0 %collective-permute-start.12 = (bf16[15,64,1024]{2,1,0:T(8,128)(2,1)S(1)}, bf16[15,64,1024]{2,1,0:T(8,128)(2,1)S(1)}, u32[]{:S(2)}, u32[]{:S(2)}) collective-permute-start(bf16[15,64,1024]{2,1,0:T(8,128)(2,1)S(1)} %get-tuple-element.54), channel_id=1, source_target_pairs={{0,1},{1,0},{2,3},{3,2},{4,5},{5,4},{6,7},{7,6},{8,9},{9,8},{10,11... | collective-permute-start | bytes 5898248 | tf_op jit(solution)/shard_map/ppermute | solution.py:38
  29.3 1.6 %collective-permute-start.13 = (bf16[13,64,128]{2,1,0:T(8,128)(2,1)S(1)}, bf16[13,64,128]{2,1,0:T(8,128)(2,1)S(1)}, u32[]{:S(2)}, u32[]{:S(2)}) collective-permute-start(bf16[13,64,128]{2,1,0:T(8,128)(2,1)S(1)} %choose.3), channel_id=1, source_target_pairs={{0,4},{1,3},{2,6},{3,1},{4,0},{5,7},{6,2},{7,5},{8,12},{9,11},{10,... | collective-permute-start | bytes 638984 | tf_op jit(solution)/shard_map/ppermute | solution.py:38
  30.8 1.2 %collective-permute-start.8 = (bf16[26,64,128]{2,1,0:T(8,128)(2,1)S(1)}, bf16[26,64,128]{2,1,0:T(8,128)(2,1)S(1)}, u32[]{:S(2)}, u32[]{:S(2)}) collective-permute-start(bf16[26,64,128]{2,1,0:T(8,128)(2,1)S(1)} %join.1.refs_1_), channel_id=1, source_target_pairs={{0,2},{1,3},{2,0},{3,1},{4,6},{5,7},{6,4},{7,5},{8,10},{9,11},{10,... | collective-permute-start | bytes 1277960 | tf_op jit(solution)/shard_map/ppermute | solution.py:38
  32.0 1.2 %collective-permute-start.9 = (bf16[26,64,128]{2,1,0:T(8,128)(2,1)S(1)}, bf16[26,64,128]{2,1,0:T(8,128)(2,1)S(1)}, u32[]{:S(2)}, u32[]{:S(2)}) collective-permute-start(bf16[26,64,128]{2,1,0:T(8,128)(2,1)S(1)} %join.1.refs_1_), channel_id=1, source_target_pairs={{0,4},{1,5},{2,6},{3,7},{4,0},{5,1},{6,2},{7,3},{8,12},{9,13},{10,... | collective-permute-start | bytes 1277960 | tf_op jit(solution)/shard_map/ppermute | solution.py:38
  33.1 1.7 %collective-permute-start.11 = (bf16[13,64,128]{2,1,0:T(8,128)(2,1)S(1)}, bf16[13,64,128]{2,1,0:T(8,128)(2,1)S(1)}, u32[]{:S(2)}, u32[]{:S(2)}) collective-permute-start(bf16[13,64,128]{2,1,0:T(8,128)(2,1)S(1)} %collective-permute-done.10.refs_8_), channel_id=1, source_target_pairs={{0,24},{1,25},{2,26},{3,27},{4,28},{5,29},{6,30},{7,31},{8,0},{9,1... | collective-permute-start | bytes 638984 | tf_op jit(solution)/shard_map/ppermute | solution.py:38
  34.8 2.2 %near_3.1 = (bf16[6144,128]{1,0:T(8,128)(2,1)S(1)}, bf16[3072,128]{1,0:T(8,128)(2,1)S(1)}) custom-call(s32[2,12]{1,0:T(2,128)S(1)} %bitcast.3, s32[12,512]{1,0:T(8,128)S(1)} %copy-done.2, bf16[512,1536]{1,0:T(8,128)(2,1)S(1)} %copy-done, bf16[12,64,512]{2,1,0:T(8,128)(2,1)S(1)} %copy-done.1, ...), custom_call_target="tpu_custom_call", output_to_operand_aliasing={{0}: (5, {}), {1}: (6, {})} | custom-call | flops 20971520 | bytes 32768 | tf_op jit(solution)/shard_map/near_3/pallas_call | solution.py:444
  37.0 1.9 %collective-permute-start.14 = (bf16[13,64,128]{2,1,0:T(8,128)(2,1)S(1)}, bf16[13,64,128]{2,1,0:T(8,128)(2,1)S(1)}, u32[]{:S(2)}, u32[]{:S(2)}) collective-permute-start(bf16[13,64,128]{2,1,0:T(8,128)(2,1)S(1)} %collective-permute-done.13.refs_9_), channel_id=1, source_target_pairs={{0,8},{1,9},{2,10},{3,11},{4,12},{5,13},{6,14},{7,15},{8,16},{9,17... | collective-permute-start | bytes 638984 | tf_op jit(solution)/shard_map/ppermute | solution.py:38
  38.9 2.2 %near_0.1 = (bf16[6144,128]{1,0:T(8,128)(2,1)S(1)}, bf16[3072,128]{1,0:T(8,128)(2,1)S(1)}, s32[16,128]{1,0:T(8,128)S(1)}) custom-call(s32[2,12]{1,0:T(2,128)S(1)} %bitcast.4, s32[12,512]{1,0:T(8,128)S(1)} %copy-done.2, bf16[512,1536]{1,0:T(8,128)(2,1)S(1)} %copy-done, ...), custom_call_target="tpu_custom_call", output_to_operand_aliasing={{0}: (8, {}), {1}: (9, {})} | custom-call | flops 20971520 | bytes 32768 | tf_op jit(solution)/shard_map/near_0/pallas_call | solution.py:444
  41.2 1.5 %far_1_0.1 = (f32[13,64,128]{2,1,0:T(8,128)S(1)}, f32[13,64,128]{2,1,0:T(8,128)S(1)}) custom-call(s32[16,128]{1,0:T(8,128)S(1)} %get-tuple-element.35.block_ref.refs_0_, s32[16,128]{1,0:T(8,128)S(1)} %get-tuple-element.56.refs_1_.refs_0_, bf16[13,64,128]{2,1,0:T(8,128)(2,1)S(1)} %get-tuple-element.36.refs_2_, ...), custom_call_target="tpu_custom_call" | custom-call | flops 1703936 | bytes 16384 | tf_op jit(solution)/shard_map/far_1_0/pallas_call | solution.py:366
  42.7 3.4 %collective-permute-done.14.refs_5_ = bf16[13,64,128]{2,1,0:T(8,128)(2,1)S(1)} collective-permute-done((bf16[13,64,128]{2,1,0:T(8,128)(2,1)S(1)}, bf16[13,64,128]{2,1,0:T(8,128)(2,1)S(1)}, u32[]{:S(2)}, u32[]{:S(2)}) %collective-permute-start.14) | collective-permute-done | bytes 213024 | tf_op jit(solution)/shard_map/ppermute | solution.py:38
  46.1 1.1 %far_1_2.1 = f32[13,64,128]{2,1,0:T(8,128)S(1)} custom-call(s32[16,128]{1,0:T(8,128)S(1)} %get-tuple-element.56.refs_1_.refs_0_, bf16[26,64,128]{2,1,0:T(8,128)(2,1)S(1)} %join.1.refs_1_, bf16[26,64,128]{2,1,0:T(8,128)(2,1)S(1)} %collective-permute-done.8.refs_2_, bf16[26,64,128]{2,1,0:T(8,128)(2,1)S(1)} %collective-permute-done.9.refs_3_, ...), custom_call_target="tpu_custom_call" | custom-call | flops 1703936 | bytes 16384 | tf_op jit(solution)/shard_map/far_1_2/pallas_call | solution.py:366
  47.3 1.1 %far_0_2.1.own_ref = f32[13,64,128]{2,1,0:T(8,128)S(1)} custom-call(s32[16,128]{1,0:T(8,128)S(1)} %get-tuple-element.35.block_ref.refs_0_, bf16[26,64,128]{2,1,0:T(8,128)(2,1)S(1)} %join.1.refs_1_, bf16[26,64,128]{2,1,0:T(8,128)(2,1)S(1)} %collective-permute-done.8.refs_2_, bf16[26,64,128]{2,1,0:T(8,128)(2,1)S(1)} %collective-permute-done.9.refs_3_, ...), custom_call_target="tpu_custom_call" | custom-call | flops 1703936 | bytes 16384 | tf_op jit(solution)/shard_map/far_0_2/pallas_call | solution.py:366
  49.0 2.2 %local_and_field.1 = bf16[6144,128]{1,0:T(8,128)(2,1)} custom-call(f32[13,64,128]{2,1,0:T(8,128)S(1)} %far_0_2.1.own_ref, f32[13,64,128]{2,1,0:T(8,128)S(1)} %collective-permute-done.15.other_ref, bf16[12,64,64]{2,1,0:T(8,128)(2,1)S(1)} %get-tuple-element.62.turned_transfer_ref, bf16[6144,128]{1,0:T(8,128)(2,1)S(1)} %get-tuple-element.63.near_ref, ...), custom_call_target="tpu_custom_call" | custom-call | flops 1572864 | bytes 65536 | tf_op jit(solution)/shard_map/local_and_field/pallas_call | solution.py:492
  (28 shorter events, 1.9 us)
Async XLA Ops:
  0.0 12.7 %copy-start = (bf16[512,1536]{1,0:T(8,128)(2,1)S(1)}, bf16[512,1536]{1,0:T(8,128)(2,1)}, u32[]{:S(2)}) copy-start(bf16[512,1536]{1,0:T(8,128)(2,1)} %constant.6.clone.table_ref) | copy-start | bytes 4718596
  0.0 12.7 %copy-start.1 = (bf16[12,64,512]{2,1,0:T(8,128)(2,1)S(1)}, bf16[12,64,512]{2,1,0:T(8,128)(2,1)}, u32[]{:S(2)}) copy-start(bf16[12,64,512]{2,1,0:T(8,128)(2,1)} %basis_ref.7) | copy-start | bytes 2359300
  0.0 12.7 %copy-start.2 = (s32[12,512]{1,0:T(8,128)S(1)}, s32[12,512]{1,0:T(8,128)}, u32[]{:S(2)}) copy-start(s32[12,512]{1,0:T(8,128)} %order_ref.7) | copy-start | bytes 73732
  0.0 12.7 %copy-start.3 = (s32[12,2]{0,1:T(2,128)S(1)}, s32[12,2]{0,1:T(2,128)}, u32[]{:S(2)}) copy-start(s32[12,2]{0,1:T(2,128)} %param.17) | copy-start | bytes 292
  4.3 11.0 %collective-permute-start.1 = (bf16[13,64,128]{2,1,0:T(8,128)(2,1)S(1)}, bf16[13,64,128]{2,1,0:T(8,128)(2,1)S(1)}, u32[]{:S(2)}, u32[]{:S(2)}) collective-permute-start(bf16[13,64,128]{2,1,0:T(8,128)(2,1)S(1)} %get-tuple-element.36.refs_2_), channel_id=1, source_target_pairs={{0,8},{1,9},{2,10},{3,11},{4,12},{5,13},{6,14},{7,15},{8,16},{9,17... | collective-permute-start | bytes 638984 | tf_op jit(solution)/shard_map/ppermute | solution.py:38
  7.4 7.9 %collective-permute-start.2 = (bf16[13,64,128]{2,1,0:T(8,128)(2,1)S(1)}, bf16[13,64,128]{2,1,0:T(8,128)(2,1)S(1)}, u32[]{:S(2)}, u32[]{:S(2)}) collective-permute-start(bf16[13,64,128]{2,1,0:T(8,128)(2,1)S(1)} %get-tuple-element.36.refs_2_), channel_id=1, source_target_pairs={{0,2},{1,3},{2,0},{3,1},{4,6},{5,7},{6,4},{7,5},{8,10},{9,11},{10,... | collective-permute-start | bytes 638984 | tf_op jit(solution)/shard_map/ppermute | solution.py:38
  8.9 6.4 %collective-permute-start.3 = (bf16[13,64,128]{2,1,0:T(8,128)(2,1)S(1)}, bf16[13,64,128]{2,1,0:T(8,128)(2,1)S(1)}, u32[]{:S(2)}, u32[]{:S(2)}) collective-permute-start(bf16[13,64,128]{2,1,0:T(8,128)(2,1)S(1)} %get-tuple-element.36.refs_2_), channel_id=1, source_target_pairs={{0,4},{1,5},{2,6},{3,7},{4,0},{5,1},{6,2},{7,3},{8,12},{9,13},{10,... | collective-permute-start | bytes 638984 | tf_op jit(solution)/shard_map/ppermute | solution.py:38
  10.4 9.7 %collective-permute-start = (bf16[13,64,128]{2,1,0:T(8,128)(2,1)S(1)}, bf16[13,64,128]{2,1,0:T(8,128)(2,1)S(1)}, u32[]{:S(2)}, u32[]{:S(2)}) collective-permute-start(bf16[13,64,128]{2,1,0:T(8,128)(2,1)S(1)} %get-tuple-element.36.refs_2_), channel_id=1, source_target_pairs={{0,24},{1,25},{2,26},{3,27},{4,28},{5,29},{6,30},{7,31},{8,0},{9,1... | collective-permute-start | bytes 638984 | tf_op jit(solution)/shard_map/ppermute | solution.py:38
  15.3 10.8 %collective-permute-start.4 = (bf16[13,64,128]{2,1,0:T(8,128)(2,1)S(1)}, bf16[13,64,128]{2,1,0:T(8,128)(2,1)S(1)}, u32[]{:S(2)}, u32[]{:S(2)}) collective-permute-start(bf16[13,64,128]{2,1,0:T(8,128)(2,1)S(1)} %collective-permute-done.1.refs_3_), channel_id=1, source_target_pairs={{0,8},{1,9},{2,10},{3,11},{4,12},{5,13},{6,14},{7,15},{8,16},{9,17... | collective-permute-start | bytes 638984 | tf_op jit(solution)/shard_map/ppermute | solution.py:38
  15.3 10.8 %collective-permute-start.5 = (bf16[13,64,128]{2,1,0:T(8,128)(2,1)S(1)}, bf16[13,64,128]{2,1,0:T(8,128)(2,1)S(1)}, u32[]{:S(2)}, u32[]{:S(2)}) collective-permute-start(bf16[13,64,128]{2,1,0:T(8,128)(2,1)S(1)} %collective-permute-done.1.refs_3_), channel_id=1, source_target_pairs={{0,2},{1,3},{2,0},{3,1},{4,6},{5,7},{6,4},{7,5},{8,10},{9,11},{10,... | collective-permute-start | bytes 638984 | tf_op jit(solution)/shard_map/ppermute | solution.py:38
  17.3 8.8 %collective-permute-start.6 = (bf16[13,64,128]{2,1,0:T(8,128)(2,1)S(1)}, bf16[13,64,128]{2,1,0:T(8,128)(2,1)S(1)}, u32[]{:S(2)}, u32[]{:S(2)}) collective-permute-start(bf16[13,64,128]{2,1,0:T(8,128)(2,1)S(1)} %collective-permute-done.1.refs_3_), channel_id=1, source_target_pairs={{0,4},{1,5},{2,6},{3,7},{4,0},{5,1},{6,2},{7,3},{8,12},{9,13},{10,... | collective-permute-start | bytes 638984 | tf_op jit(solution)/shard_map/ppermute | solution.py:38
  20.1 6.1 %collective-permute-start.10 = (bf16[13,64,128]{2,1,0:T(8,128)(2,1)S(1)}, bf16[13,64,128]{2,1,0:T(8,128)(2,1)S(1)}, u32[]{:S(2)}, u32[]{:S(2)}) collective-permute-start(bf16[13,64,128]{2,1,0:T(8,128)(2,1)S(1)} %choose.2), channel_id=1, source_target_pairs={{0,4},{1,3},{2,6},{3,1},{4,0},{5,7},{6,2},{7,5},{8,12},{9,11},{10,... | collective-permute-start | bytes 638984 | tf_op jit(solution)/shard_map/ppermute | solution.py:38
  21.9 4.2 %collective-permute-start.7 = (bf16[512,128]{1,0:T(8,128)(2,1)S(1)}, bf16[512,128]{1,0:T(8,128)(2,1)S(1)}, u32[]{:S(2)}, u32[]{:S(2)}) collective-permute-start(bf16[512,128]{1,0:T(8,128)(2,1)S(1)} %get-tuple-element.46), channel_id=1, source_target_pairs={{1,2},{3,4},{5,6},{7,8},{9,10},{11,12},{13,14},{15,16},{17,18},{19... | collective-permute-start | bytes 393224 | tf_op jit(solution)/shard_map/ppermute | solution.py:543
  26.2 12.7 %collective-permute-start.12 = (bf16[15,64,1024]{2,1,0:T(8,128)(2,1)S(1)}, bf16[15,64,1024]{2,1,0:T(8,128)(2,1)S(1)}, u32[]{:S(2)}, u32[]{:S(2)}) collective-permute-start(bf16[15,64,1024]{2,1,0:T(8,128)(2,1)S(1)} %get-tuple-element.54), channel_id=1, source_target_pairs={{0,1},{1,0},{2,3},{3,2},{4,5},{5,4},{6,7},{7,6},{8,9},{9,8},{10,11... | collective-permute-start | bytes 5898248 | tf_op jit(solution)/shard_map/ppermute | solution.py:38
  29.3 7.8 %collective-permute-start.13 = (bf16[13,64,128]{2,1,0:T(8,128)(2,1)S(1)}, bf16[13,64,128]{2,1,0:T(8,128)(2,1)S(1)}, u32[]{:S(2)}, u32[]{:S(2)}) collective-permute-start(bf16[13,64,128]{2,1,0:T(8,128)(2,1)S(1)} %choose.3), channel_id=1, source_target_pairs={{0,4},{1,3},{2,6},{3,1},{4,0},{5,7},{6,2},{7,5},{8,12},{9,11},{10,... | collective-permute-start | bytes 638984 | tf_op jit(solution)/shard_map/ppermute | solution.py:38
  30.8 15.3 %collective-permute-start.8 = (bf16[26,64,128]{2,1,0:T(8,128)(2,1)S(1)}, bf16[26,64,128]{2,1,0:T(8,128)(2,1)S(1)}, u32[]{:S(2)}, u32[]{:S(2)}) collective-permute-start(bf16[26,64,128]{2,1,0:T(8,128)(2,1)S(1)} %join.1.refs_1_), channel_id=1, source_target_pairs={{0,2},{1,3},{2,0},{3,1},{4,6},{5,7},{6,4},{7,5},{8,10},{9,11},{10,... | collective-permute-start | bytes 1277960 | tf_op jit(solution)/shard_map/ppermute | solution.py:38
  32.0 14.1 %collective-permute-start.9 = (bf16[26,64,128]{2,1,0:T(8,128)(2,1)S(1)}, bf16[26,64,128]{2,1,0:T(8,128)(2,1)S(1)}, u32[]{:S(2)}, u32[]{:S(2)}) collective-permute-start(bf16[26,64,128]{2,1,0:T(8,128)(2,1)S(1)} %join.1.refs_1_), channel_id=1, source_target_pairs={{0,4},{1,5},{2,6},{3,7},{4,0},{5,1},{6,2},{7,3},{8,12},{9,13},{10,... | collective-permute-start | bytes 1277960 | tf_op jit(solution)/shard_map/ppermute | solution.py:38
  33.1 9.5 %collective-permute-start.11 = (bf16[13,64,128]{2,1,0:T(8,128)(2,1)S(1)}, bf16[13,64,128]{2,1,0:T(8,128)(2,1)S(1)}, u32[]{:S(2)}, u32[]{:S(2)}) collective-permute-start(bf16[13,64,128]{2,1,0:T(8,128)(2,1)S(1)} %collective-permute-done.10.refs_8_), channel_id=1, source_target_pairs={{0,24},{1,25},{2,26},{3,27},{4,28},{5,29},{6,30},{7,31},{8,0},{9,1... | collective-permute-start | bytes 638984 | tf_op jit(solution)/shard_map/ppermute | solution.py:38
  37.0 9.1 %collective-permute-start.14 = (bf16[13,64,128]{2,1,0:T(8,128)(2,1)S(1)}, bf16[13,64,128]{2,1,0:T(8,128)(2,1)S(1)}, u32[]{:S(2)}, u32[]{:S(2)}) collective-permute-start(bf16[13,64,128]{2,1,0:T(8,128)(2,1)S(1)} %collective-permute-done.13.refs_9_), channel_id=1, source_target_pairs={{0,8},{1,9},{2,10},{3,11},{4,12},{5,13},{6,14},{7,15},{8,16},{9,17... | collective-permute-start | bytes 638984 | tf_op jit(solution)/shard_map/ppermute | solution.py:38
  47.2 1.8 %collective-permute-start.15 = (f32[13,64,128]{2,1,0:T(8,128)S(1)}, f32[13,64,128]{2,1,0:T(8,128)S(1)}, u32[]{:S(2)}, u32[]{:S(2)}) collective-permute-start(f32[13,64,128]{2,1,0:T(8,128)S(1)} %far_1_2.1), channel_id=1, source_target_pairs={{0,1},{1,0},{2,3},{3,2},{4,5},{5,4},{6,7},{7,6},{8,9},{9,8},{10,11... | collective-permute-start | bytes 1277960 | tf_op jit(solution)/shard_map/ppermute | solution.py:38

commit v19 on v18

--- a/solution.py
+++ b/solution.py
@@ -462,27 +462,28 @@
     fine = (local - coarse.astype(F32)).astype(BF)
     both = jnp.concatenate([coarse, fine], axis=1)
     fields = local.shape[1]
-    for pair in range(per // 2):
-        values = []
-        for i in range(2):
-            leaf = step * per + 2 * pair + i
+    for start in range(0, per, 4):
+        size = min(4, per - start)
+        rows = []
+        for i in range(size):
+            leaf = step * per + start + i
             down = dot(turned_transfer_ref[leaf], both)
             value = own_ref[leaf] + other_ref[leaf] + (down[:, :fields] + down[:, fields:])
-            values.append(value.astype(BF))
-        zero = jnp.zeros_like(values[0])
-        corner = jnp.concatenate(
-            [
-                jnp.concatenate([values[0], zero], axis=1),
-                jnp.concatenate([zero, values[1]], axis=1),
-            ],
-            axis=0,
-        )
-        at = pl.multiple_of((step * (per // 2) + pair) * leaf_len, leaf_len)
-        far = dot(turned_ref[pl.ds(at, leaf_len), :], corner)
-        for i in range(2):
-            near = near_ref[pl.ds(2 * at + i * leaf_len, leaf_len), :].astype(F32)
-            rows = slice((2 * pair + i) * leaf_len, (2 * pair + i + 1) * leaf_len)
-            out_ref[rows, :] = (near + far[:, i * fields:(i + 1) * fields]).astype(BF)
+            parts = [jnp.zeros(value.shape, BF)] * size
+            parts[i] = value.astype(BF)
+            rows.append(jnp.concatenate(parts, axis=1))
+        first = step * per + start
+        turned = [
+            turned_ref[pl.ds(pl.multiple_of((first // 2 + i) * leaf_len, leaf_len), leaf_len), :]
+            for i in range(size // 2)
+        ]
+        far = dot(jnp.concatenate(turned, axis=1), jnp.concatenate(rows, axis=0))
+        for i in range(size):
+            at = pl.multiple_of((first + i) * leaf_len, leaf_len)
+            near = near_ref[pl.ds(at, leaf_len), :].astype(F32)
+            out_ref[(start + i) * leaf_len:(start + i + 1) * leaf_len, :] = (
+                near + far[:, i * fields:(i + 1) * fields]
+            ).astype(BF)
 
 
 def field(own, other, turned_transfer, near, turned, per=6):
@@ -556,7 +557,6 @@
     other_blocks = over_core(after(my_other, chosen))
     held = after(ordered, joined)
     filled = near_field(list(range(cut, pairs - 1)), *near_args, held, filled=filled)
-    next_far = after(next_far, filled[0])
     last_far = [along_z(far, layers - 1)]
     for _ in range(layers - 3):
         last_far.append(along_z(next_far if len(last_far) == 1 else last_far[-1], 1))

time: 51.4 us -> 51.6 us (level)
  waiting for transfers between devices: 5.68 us -> 4.96 us
  starting transfers between devices: 25 us -> 25.7 us
    ppermute x15, waiting for transfers between devices: 5.68 us -> 4.96 us  [send(): lax.ppermute(block, 'subtree', [(d, target(d)) for d in range(count)])]
    ppermute x15, starting transfers between devices: 24.3 us -> 25 us  [send(): lax.ppermute(block, 'subtree', [(d, target(d)) for d in range(count)])]
  transfers between devices with their start and end apart: 16 -> 16, of which waited for: 4 -> 5; matrix products, arithmetic and copies ran while one was open for 0% -> 0% of each run, Pallas kernels for 25% -> 25%
where the time goes in v19:
time: 51.6 us; the launch traced here: 51.5 us
  starting transfers between devices  25.7 us (50%)
  Pallas kernels  20.7 us (40%)
  waiting for transfers between devices  4.96 us (10%)
    ppermute x15, starting transfers between devices, send(): lax.ppermute(block, 'subtree', [(d, target(d)) for d in range(count)])  25 us
    pallas_call x3, Pallas kernels, near_field(): pl.pallas_call(functools.partial(near_kernel, halos is not None, tuple(pa...  6.7 us
    ppermute x15, waiting for transfers between devices, send(): lax.ppermute(block, 'subtree', [(d, target(d)) for d in range(count)])  4.96 us
    pallas_call x1, Pallas kernels, skeletons_of(): pl.pallas_call(functools.partial(skeleton_kernel, per, layers), name='ord...  4.29 us
    pallas_call x3, Pallas kernels, far_rounds(): pl.pallas_call(functools.partial(round_kernel, planes, steps, slots, [len...  3.66 us
    pallas_call x1, Pallas kernels, dense_couplings(): pl.pallas_call(functools.partial(dense_kernel, per, slots), name='couplin...  3.49 us
    pallas_call x1, Pallas kernels, field(): pl.pallas_call(functools.partial(field_kernel, per), name='local_and_fiel...  2.43 us
  transfers between devices with their start and end apart: 16, of which 5 were waited for; matrix products, arithmetic and copies ran while one was open for 0% of the time, Pallas kernels for 25%

profile of v19, /device:TPU:0, one launch (start us, length us, event | category | flops | bytes accessed | tf_op | source)
XLA Modules:
  0.0 51.5 jit_solution(12398819100507432523)
XLA Ops:
  0.0 4.3 %order_and_skeleton.1 = (bf16[6144,128]{1,0:T(8,128)(2,1)S(1)}, bf16[13,64,128]{2,1,0:T(8,128)(2,1)S(1)}, bf16[512,128]{1,0:T(8,128)(2,1)S(1)}, bf16[512,128]{1,...) custom-call(s32[1]{0:T(128)} %bitcast.me_ref.refs_0_, s32[12,512]{1,0:T(8,128)} %order_ref.7, ...), custom_call_target="tpu_custom_call" | custom-call | flops 12582912 | bytes 65536 | tf_op jit(solution)/shard_map/order_and_skeleton/pallas_call | solution.py:192
  4.3 3.1 %collective-permute-start.1 = (bf16[13,64,128]{2,1,0:T(8,128)(2,1)S(1)}, bf16[13,64,128]{2,1,0:T(8,128)(2,1)S(1)}, u32[]{:S(2)}, u32[]{:S(2)}) collective-permute-start(bf16[13,64,128]{2,1,0:T(8,128)(2,1)S(1)} %get-tuple-element.35.refs_2_), channel_id=1, source_target_pairs={{0,8},{1,9},{2,10},{3,11},{4,12},{5,13},{6,14},{7,15},{8,16},{9,17... | collective-permute-start | bytes 638984 | tf_op jit(solution)/shard_map/ppermute | solution.py:38
  7.4 1.5 %collective-permute-start.2 = (bf16[13,64,128]{2,1,0:T(8,128)(2,1)S(1)}, bf16[13,64,128]{2,1,0:T(8,128)(2,1)S(1)}, u32[]{:S(2)}, u32[]{:S(2)}) collective-permute-start(bf16[13,64,128]{2,1,0:T(8,128)(2,1)S(1)} %get-tuple-element.35.refs_2_), channel_id=1, source_target_pairs={{0,2},{1,3},{2,0},{3,1},{4,6},{5,7},{6,4},{7,5},{8,10},{9,11},{10,... | collective-permute-start | bytes 638984 | tf_op jit(solution)/shard_map/ppermute | solution.py:38
  8.9 1.5 %collective-permute-start.3 = (bf16[13,64,128]{2,1,0:T(8,128)(2,1)S(1)}, bf16[13,64,128]{2,1,0:T(8,128)(2,1)S(1)}, u32[]{:S(2)}, u32[]{:S(2)}) collective-permute-start(bf16[13,64,128]{2,1,0:T(8,128)(2,1)S(1)} %get-tuple-element.35.refs_2_), channel_id=1, source_target_pairs={{0,4},{1,5},{2,6},{3,7},{4,0},{5,1},{6,2},{7,3},{8,12},{9,13},{10,... | collective-permute-start | bytes 638984 | tf_op jit(solution)/shard_map/ppermute | solution.py:38
  10.4 2.2 %collective-permute-start = (bf16[13,64,128]{2,1,0:T(8,128)(2,1)S(1)}, bf16[13,64,128]{2,1,0:T(8,128)(2,1)S(1)}, u32[]{:S(2)}, u32[]{:S(2)}) collective-permute-start(bf16[13,64,128]{2,1,0:T(8,128)(2,1)S(1)} %get-tuple-element.35.refs_2_), channel_id=1, source_target_pairs={{0,24},{1,25},{2,26},{3,27},{4,28},{5,29},{6,30},{7,31},{8,0},{9,1... | collective-permute-start | bytes 638984 | tf_op jit(solution)/shard_map/ppermute | solution.py:38
  12.7 2.2 %near_1.1 = (bf16[6144,128]{1,0:T(8,128)(2,1)S(1)}, bf16[3072,128]{1,0:T(8,128)(2,1)S(1)}) custom-call(s32[2,12]{1,0:T(2,128)S(1)} %bitcast.2, s32[12,512]{1,0:T(8,128)S(1)} %copy-done.2, bf16[512,1536]{1,0:T(8,128)(2,1)S(1)} %copy-done, bf16[12,64,512]{2,1,0:T(8,128)(2,1)S(1)} %copy-done.1, bf16[6144,128]{1,0:T(8,128)(2,1)S(1)} %get-tuple-element.51.ordered_ref), custom_call_target="tpu_custom_call" | custom-call | flops 20971520 | bytes 32768 | tf_op jit(solution)/shard_map/near_1/pallas_call | solution.py:444
  15.3 2.0 %collective-permute-start.5 = (bf16[13,64,128]{2,1,0:T(8,128)(2,1)S(1)}, bf16[13,64,128]{2,1,0:T(8,128)(2,1)S(1)}, u32[]{:S(2)}, u32[]{:S(2)}) collective-permute-start(bf16[13,64,128]{2,1,0:T(8,128)(2,1)S(1)} %collective-permute-done.1.refs_3_), channel_id=1, source_target_pairs={{0,2},{1,3},{2,0},{3,1},{4,6},{5,7},{6,4},{7,5},{8,10},{9,11},{10,... | collective-permute-start | bytes 638984 | tf_op jit(solution)/shard_map/ppermute | solution.py:38
  17.3 1.6 %collective-permute-start.6 = (bf16[13,64,128]{2,1,0:T(8,128)(2,1)S(1)}, bf16[13,64,128]{2,1,0:T(8,128)(2,1)S(1)}, u32[]{:S(2)}, u32[]{:S(2)}) collective-permute-start(bf16[13,64,128]{2,1,0:T(8,128)(2,1)S(1)} %collective-permute-done.1.refs_3_), channel_id=1, source_target_pairs={{0,4},{1,5},{2,6},{3,7},{4,0},{5,1},{6,2},{7,3},{8,12},{9,13},{10,... | collective-permute-start | bytes 638984 | tf_op jit(solution)/shard_map/ppermute | solution.py:38
  18.9 1.2 %collective-permute-done.refs_0_ = bf16[13,64,128]{2,1,0:T(8,128)(2,1)S(1)} collective-permute-done((bf16[13,64,128]{2,1,0:T(8,128)(2,1)S(1)}, bf16[13,64,128]{2,1,0:T(8,128)(2,1)S(1)}, u32[]{:S(2)}, u32[]{:S(2)}) %collective-permute-start) | collective-permute-done | bytes 213024 | tf_op jit(solution)/shard_map/ppermute | solution.py:38
  20.1 1.8 %collective-permute-start.10 = (bf16[13,64,128]{2,1,0:T(8,128)(2,1)S(1)}, bf16[13,64,128]{2,1,0:T(8,128)(2,1)S(1)}, u32[]{:S(2)}, u32[]{:S(2)}) collective-permute-start(bf16[13,64,128]{2,1,0:T(8,128)(2,1)S(1)} %choose.2), channel_id=1, source_target_pairs={{0,4},{1,3},{2,6},{3,1},{4,0},{5,7},{6,2},{7,5},{8,12},{9,11},{10,... | collective-permute-start | bytes 638984 | tf_op jit(solution)/shard_map/ppermute | solution.py:38
  22.6 3.5 %couplings_by_owner.1 = (bf16[13,64,1024]{2,1,0:T(8,128)(2,1)S(1)}, bf16[15,64,1024]{2,1,0:T(8,128)(2,1)S(1)}, bf16[12,64,64]{2,1,0:T(8,128)(2,1)S(1)}) custom-call(s32[16,128]{1,0:T(8,128)S(1)} %get-tuple-element.41.entry_ref, s32[16,128]{1,0:T(8,128)S(1)} %get-tuple-element.34.block_ref.refs_0_, bf16[512,128]{1,0:T(8,128)(2,1)S(1)} %get-tuple-element.42.inner_ref, ...), custom_call_target="tpu_custom_call" | custom-call | bytes 131072 | tf_op jit(solution)/shard_map/couplings_by_owner/pallas_call | solution.py:306
  26.2 3.0 %collective-permute-start.12 = (bf16[15,64,1024]{2,1,0:T(8,128)(2,1)S(1)}, bf16[15,64,1024]{2,1,0:T(8,128)(2,1)S(1)}, u32[]{:S(2)}, u32[]{:S(2)}) collective-permute-start(bf16[15,64,1024]{2,1,0:T(8,128)(2,1)S(1)} %get-tuple-element.53), channel_id=1, source_target_pairs={{0,1},{1,0},{2,3},{3,2},{4,5},{5,4},{6,7},{7,6},{8,9},{9,8},{10,11... | collective-permute-start | bytes 5898248 | tf_op jit(solution)/shard_map/ppermute | solution.py:38
  29.3 1.6 %collective-permute-start.13 = (bf16[13,64,128]{2,1,0:T(8,128)(2,1)S(1)}, bf16[13,64,128]{2,1,0:T(8,128)(2,1)S(1)}, u32[]{:S(2)}, u32[]{:S(2)}) collective-permute-start(bf16[13,64,128]{2,1,0:T(8,128)(2,1)S(1)} %choose.3), channel_id=1, source_target_pairs={{0,4},{1,3},{2,6},{3,1},{4,0},{5,7},{6,2},{7,5},{8,12},{9,11},{10,... | collective-permute-start | bytes 638984 | tf_op jit(solution)/shard_map/ppermute | solution.py:38
  30.8 1.2 %collective-permute-start.8 = (bf16[26,64,128]{2,1,0:T(8,128)(2,1)S(1)}, bf16[26,64,128]{2,1,0:T(8,128)(2,1)S(1)}, u32[]{:S(2)}, u32[]{:S(2)}) collective-permute-start(bf16[26,64,128]{2,1,0:T(8,128)(2,1)S(1)} %join.1.refs_1_), channel_id=1, source_target_pairs={{0,2},{1,3},{2,0},{3,1},{4,6},{5,7},{6,4},{7,5},{8,10},{9,11},{10,... | collective-permute-start | bytes 1277960 | tf_op jit(solution)/shard_map/ppermute | solution.py:38
  32.0 1.2 %collective-permute-start.9 = (bf16[26,64,128]{2,1,0:T(8,128)(2,1)S(1)}, bf16[26,64,128]{2,1,0:T(8,128)(2,1)S(1)}, u32[]{:S(2)}, u32[]{:S(2)}) collective-permute-start(bf16[26,64,128]{2,1,0:T(8,128)(2,1)S(1)} %join.1.refs_1_), channel_id=1, source_target_pairs={{0,4},{1,5},{2,6},{3,7},{4,0},{5,1},{6,2},{7,3},{8,12},{9,13},{10,... | collective-permute-start | bytes 1277960 | tf_op jit(solution)/shard_map/ppermute | solution.py:38
  33.1 1.7 %collective-permute-start.11 = (bf16[13,64,128]{2,1,0:T(8,128)(2,1)S(1)}, bf16[13,64,128]{2,1,0:T(8,128)(2,1)S(1)}, u32[]{:S(2)}, u32[]{:S(2)}) collective-permute-start(bf16[13,64,128]{2,1,0:T(8,128)(2,1)S(1)} %collective-permute-done.10.refs_8_), channel_id=1, source_target_pairs={{0,24},{1,25},{2,26},{3,27},{4,28},{5,29},{6,30},{7,31},{8,0},{9,1... | collective-permute-start | bytes 638984 | tf_op jit(solution)/shard_map/ppermute | solution.py:38
  34.8 1.5 %collective-permute-done.13.refs_9_ = bf16[13,64,128]{2,1,0:T(8,128)(2,1)S(1)} collective-permute-done((bf16[13,64,128]{2,1,0:T(8,128)(2,1)S(1)}, bf16[13,64,128]{2,1,0:T(8,128)(2,1)S(1)}, u32[]{:S(2)}, u32[]{:S(2)}) %collective-permute-start.13) | collective-permute-done | bytes 213024 | tf_op jit(solution)/shard_map/ppermute | solution.py:38
  36.3 2.6 %collective-permute-start.14 = (bf16[13,64,128]{2,1,0:T(8,128)(2,1)S(1)}, bf16[13,64,128]{2,1,0:T(8,128)(2,1)S(1)}, u32[]{:S(2)}, u32[]{:S(2)}) collective-permute-start(bf16[13,64,128]{2,1,0:T(8,128)(2,1)S(1)} %collective-permute-done.13.refs_9_), channel_id=1, source_target_pairs={{0,8},{1,9},{2,10},{3,11},{4,12},{5,13},{6,14},{7,15},{8,16},{9,17... | collective-permute-start | bytes 638984 | tf_op jit(solution)/shard_map/ppermute | solution.py:38
  38.9 2.2 %near_3.1 = (bf16[6144,128]{1,0:T(8,128)(2,1)S(1)}, bf16[3072,128]{1,0:T(8,128)(2,1)S(1)}) custom-call(s32[2,12]{1,0:T(2,128)S(1)} %bitcast.3, s32[12,512]{1,0:T(8,128)S(1)} %copy-done.2, bf16[512,1536]{1,0:T(8,128)(2,1)S(1)} %copy-done, bf16[12,64,512]{2,1,0:T(8,128)(2,1)S(1)} %copy-done.1, ...), custom_call_target="tpu_custom_call", output_to_operand_aliasing={{0}: (5, {}), {1}: (6, {})} | custom-call | flops 20971520 | bytes 32768 | tf_op jit(solution)/shard_map/near_3/pallas_call | solution.py:444
  41.2 2.2 %near_0.1 = (bf16[6144,128]{1,0:T(8,128)(2,1)S(1)}, bf16[3072,128]{1,0:T(8,128)(2,1)S(1)}, s32[16,128]{1,0:T(8,128)S(1)}) custom-call(s32[2,12]{1,0:T(2,128)S(1)} %bitcast.4, s32[12,512]{1,0:T(8,128)S(1)} %copy-done.2, bf16[512,1536]{1,0:T(8,128)(2,1)S(1)} %copy-done, ...), custom_call_target="tpu_custom_call", output_to_operand_aliasing={{0}: (8, {}), {1}: (9, {})} | custom-call | flops 20971520 | bytes 32768 | tf_op jit(solution)/shard_map/near_0/pallas_call | solution.py:444
  43.4 1.5 %far_1_0.1 = (f32[13,64,128]{2,1,0:T(8,128)S(1)}, f32[13,64,128]{2,1,0:T(8,128)S(1)}) custom-call(s32[16,128]{1,0:T(8,128)S(1)} %get-tuple-element.34.block_ref.refs_0_, s32[16,128]{1,0:T(8,128)S(1)} %get-tuple-element.55.refs_1_.refs_0_, bf16[13,64,128]{2,1,0:T(8,128)(2,1)S(1)} %get-tuple-element.35.refs_2_, ...), custom_call_target="tpu_custom_call" | custom-call | flops 1703936 | bytes 16384 | tf_op jit(solution)/shard_map/far_1_0/pallas_call | solution.py:366
  44.9 1.2 %collective-permute-done.14.refs_5_ = bf16[13,64,128]{2,1,0:T(8,128)(2,1)S(1)} collective-permute-done((bf16[13,64,128]{2,1,0:T(8,128)(2,1)S(1)}, bf16[13,64,128]{2,1,0:T(8,128)(2,1)S(1)}, u32[]{:S(2)}, u32[]{:S(2)}) %collective-permute-start.14) | collective-permute-done | bytes 213024 | tf_op jit(solution)/shard_map/ppermute | solution.py:38
  46.1 1.1 %far_1_2.1 = f32[13,64,128]{2,1,0:T(8,128)S(1)} custom-call(s32[16,128]{1,0:T(8,128)S(1)} %get-tuple-element.55.refs_1_.refs_0_, bf16[26,64,128]{2,1,0:T(8,128)(2,1)S(1)} %join.1.refs_1_, bf16[26,64,128]{2,1,0:T(8,128)(2,1)S(1)} %collective-permute-done.8.refs_2_, bf16[26,64,128]{2,1,0:T(8,128)(2,1)S(1)} %collective-permute-done.9.refs_3_, ...), custom_call_target="tpu_custom_call" | custom-call | flops 1703936 | bytes 16384 | tf_op jit(solution)/shard_map/far_1_2/pallas_call | solution.py:366
  49.0 2.4 %local_and_field.1 = bf16[6144,128]{1,0:T(8,128)(2,1)} custom-call(f32[13,64,128]{2,1,0:T(8,128)S(1)} %far_0_2.1.own_ref, f32[13,64,128]{2,1,0:T(8,128)S(1)} %collective-permute-done.15.other_ref, bf16[12,64,64]{2,1,0:T(8,128)(2,1)S(1)} %get-tuple-element.60.turned_transfer_ref, bf16[6144,128]{1,0:T(8,128)(2,1)S(1)} %get-tuple-element.61.near_ref, ...), custom_call_target="tpu_custom_call" | custom-call | flops 1572864 | bytes 65536 | tf_op jit(solution)/shard_map/local_and_field/pallas_call | solution.py:493
  (28 shorter events, 3.0 us)
Async XLA Ops:
  0.0 12.7 %copy-start = (bf16[512,1536]{1,0:T(8,128)(2,1)S(1)}, bf16[512,1536]{1,0:T(8,128)(2,1)}, u32[]{:S(2)}) copy-start(bf16[512,1536]{1,0:T(8,128)(2,1)} %constant.6.clone.table_ref) | copy-start | bytes 4718596
  0.0 12.7 %copy-start.1 = (bf16[12,64,512]{2,1,0:T(8,128)(2,1)S(1)}, bf16[12,64,512]{2,1,0:T(8,128)(2,1)}, u32[]{:S(2)}) copy-start(bf16[12,64,512]{2,1,0:T(8,128)(2,1)} %basis_ref.7) | copy-start | bytes 2359300
  0.0 12.7 %copy-start.2 = (s32[12,512]{1,0:T(8,128)S(1)}, s32[12,512]{1,0:T(8,128)}, u32[]{:S(2)}) copy-start(s32[12,512]{1,0:T(8,128)} %order_ref.7) | copy-start | bytes 73732
  0.0 12.7 %copy-start.3 = (s32[12,2]{0,1:T(2,128)S(1)}, s32[12,2]{0,1:T(2,128)}, u32[]{:S(2)}) copy-start(s32[12,2]{0,1:T(2,128)} %param.17) | copy-start | bytes 292
  4.3 11.0 %collective-permute-start.1 = (bf16[13,64,128]{2,1,0:T(8,128)(2,1)S(1)}, bf16[13,64,128]{2,1,0:T(8,128)(2,1)S(1)}, u32[]{:S(2)}, u32[]{:S(2)}) collective-permute-start(bf16[13,64,128]{2,1,0:T(8,128)(2,1)S(1)} %get-tuple-element.35.refs_2_), channel_id=1, source_target_pairs={{0,8},{1,9},{2,10},{3,11},{4,12},{5,13},{6,14},{7,15},{8,16},{9,17... | collective-permute-start | bytes 638984 | tf_op jit(solution)/shard_map/ppermute | solution.py:38
  7.4 7.9 %collective-permute-start.2 = (bf16[13,64,128]{2,1,0:T(8,128)(2,1)S(1)}, bf16[13,64,128]{2,1,0:T(8,128)(2,1)S(1)}, u32[]{:S(2)}, u32[]{:S(2)}) collective-permute-start(bf16[13,64,128]{2,1,0:T(8,128)(2,1)S(1)} %get-tuple-element.35.refs_2_), channel_id=1, source_target_pairs={{0,2},{1,3},{2,0},{3,1},{4,6},{5,7},{6,4},{7,5},{8,10},{9,11},{10,... | collective-permute-start | bytes 638984 | tf_op jit(solution)/shard_map/ppermute | solution.py:38
  8.9 6.4 %collective-permute-start.3 = (bf16[13,64,128]{2,1,0:T(8,128)(2,1)S(1)}, bf16[13,64,128]{2,1,0:T(8,128)(2,1)S(1)}, u32[]{:S(2)}, u32[]{:S(2)}) collective-permute-start(bf16[13,64,128]{2,1,0:T(8,128)(2,1)S(1)} %get-tuple-element.35.refs_2_), channel_id=1, source_target_pairs={{0,4},{1,5},{2,6},{3,7},{4,0},{5,1},{6,2},{7,3},{8,12},{9,13},{10,... | collective-permute-start | bytes 638984 | tf_op jit(solution)/shard_map/ppermute | solution.py:38
  10.4 9.7 %collective-permute-start = (bf16[13,64,128]{2,1,0:T(8,128)(2,1)S(1)}, bf16[13,64,128]{2,1,0:T(8,128)(2,1)S(1)}, u32[]{:S(2)}, u32[]{:S(2)}) collective-permute-start(bf16[13,64,128]{2,1,0:T(8,128)(2,1)S(1)} %get-tuple-element.35.refs_2_), channel_id=1, source_target_pairs={{0,24},{1,25},{2,26},{3,27},{4,28},{5,29},{6,30},{7,31},{8,0},{9,1... | collective-permute-start | bytes 638984 | tf_op jit(solution)/shard_map/ppermute | solution.py:38
  15.3 10.8 %collective-permute-start.4 = (bf16[13,64,128]{2,1,0:T(8,128)(2,1)S(1)}, bf16[13,64,128]{2,1,0:T(8,128)(2,1)S(1)}, u32[]{:S(2)}, u32[]{:S(2)}) collective-permute-start(bf16[13,64,128]{2,1,0:T(8,128)(2,1)S(1)} %collective-permute-done.1.refs_3_), channel_id=1, source_target_pairs={{0,8},{1,9},{2,10},{3,11},{4,12},{5,13},{6,14},{7,15},{8,16},{9,17... | collective-permute-start | bytes 638984 | tf_op jit(solution)/shard_map/ppermute | solution.py:38
  15.3 10.8 %collective-permute-start.5 = (bf16[13,64,128]{2,1,0:T(8,128)(2,1)S(1)}, bf16[13,64,128]{2,1,0:T(8,128)(2,1)S(1)}, u32[]{:S(2)}, u32[]{:S(2)}) collective-permute-start(bf16[13,64,128]{2,1,0:T(8,128)(2,1)S(1)} %collective-permute-done.1.refs_3_), channel_id=1, source_target_pairs={{0,2},{1,3},{2,0},{3,1},{4,6},{5,7},{6,4},{7,5},{8,10},{9,11},{10,... | collective-permute-start | bytes 638984 | tf_op jit(solution)/shard_map/ppermute | solution.py:38
  17.3 8.8 %collective-permute-start.6 = (bf16[13,64,128]{2,1,0:T(8,128)(2,1)S(1)}, bf16[13,64,128]{2,1,0:T(8,128)(2,1)S(1)}, u32[]{:S(2)}, u32[]{:S(2)}) collective-permute-start(bf16[13,64,128]{2,1,0:T(8,128)(2,1)S(1)} %collective-permute-done.1.refs_3_), channel_id=1, source_target_pairs={{0,4},{1,5},{2,6},{3,7},{4,0},{5,1},{6,2},{7,3},{8,12},{9,13},{10,... | collective-permute-start | bytes 638984 | tf_op jit(solution)/shard_map/ppermute | solution.py:38
  20.1 6.1 %collective-permute-start.10 = (bf16[13,64,128]{2,1,0:T(8,128)(2,1)S(1)}, bf16[13,64,128]{2,1,0:T(8,128)(2,1)S(1)}, u32[]{:S(2)}, u32[]{:S(2)}) collective-permute-start(bf16[13,64,128]{2,1,0:T(8,128)(2,1)S(1)} %choose.2), channel_id=1, source_target_pairs={{0,4},{1,3},{2,6},{3,1},{4,0},{5,7},{6,2},{7,5},{8,12},{9,11},{10,... | collective-permute-start | bytes 638984 | tf_op jit(solution)/shard_map/ppermute | solution.py:38
  21.9 4.2 %collective-permute-start.7 = (bf16[512,128]{1,0:T(8,128)(2,1)S(1)}, bf16[512,128]{1,0:T(8,128)(2,1)S(1)}, u32[]{:S(2)}, u32[]{:S(2)}) collective-permute-start(bf16[512,128]{1,0:T(8,128)(2,1)S(1)} %get-tuple-element.45), channel_id=1, source_target_pairs={{1,2},{3,4},{5,6},{7,8},{9,10},{11,12},{13,14},{15,16},{17,18},{19... | collective-permute-start | bytes 393224 | tf_op jit(solution)/shard_map/ppermute | solution.py:544
  26.2 14.9 %collective-permute-start.12 = (bf16[15,64,1024]{2,1,0:T(8,128)(2,1)S(1)}, bf16[15,64,1024]{2,1,0:T(8,128)(2,1)S(1)}, u32[]{:S(2)}, u32[]{:S(2)}) collective-permute-start(bf16[15,64,1024]{2,1,0:T(8,128)(2,1)S(1)} %get-tuple-element.53), channel_id=1, source_target_pairs={{0,1},{1,0},{2,3},{3,2},{4,5},{5,4},{6,7},{7,6},{8,9},{9,8},{10,11... | collective-permute-start | bytes 5898248 | tf_op jit(solution)/shard_map/ppermute | solution.py:38
  29.3 7.1 %collective-permute-start.13 = (bf16[13,64,128]{2,1,0:T(8,128)(2,1)S(1)}, bf16[13,64,128]{2,1,0:T(8,128)(2,1)S(1)}, u32[]{:S(2)}, u32[]{:S(2)}) collective-permute-start(bf16[13,64,128]{2,1,0:T(8,128)(2,1)S(1)} %choose.3), channel_id=1, source_target_pairs={{0,4},{1,3},{2,6},{3,1},{4,0},{5,7},{6,2},{7,5},{8,12},{9,11},{10,... | collective-permute-start | bytes 638984 | tf_op jit(solution)/shard_map/ppermute | solution.py:38
  30.8 15.3 %collective-permute-start.8 = (bf16[26,64,128]{2,1,0:T(8,128)(2,1)S(1)}, bf16[26,64,128]{2,1,0:T(8,128)(2,1)S(1)}, u32[]{:S(2)}, u32[]{:S(2)}) collective-permute-start(bf16[26,64,128]{2,1,0:T(8,128)(2,1)S(1)} %join.1.refs_1_), channel_id=1, source_target_pairs={{0,2},{1,3},{2,0},{3,1},{4,6},{5,7},{6,4},{7,5},{8,10},{9,11},{10,... | collective-permute-start | bytes 1277960 | tf_op jit(solution)/shard_map/ppermute | solution.py:38
  32.0 14.1 %collective-permute-start.9 = (bf16[26,64,128]{2,1,0:T(8,128)(2,1)S(1)}, bf16[26,64,128]{2,1,0:T(8,128)(2,1)S(1)}, u32[]{:S(2)}, u32[]{:S(2)}) collective-permute-start(bf16[26,64,128]{2,1,0:T(8,128)(2,1)S(1)} %join.1.refs_1_), channel_id=1, source_target_pairs={{0,4},{1,5},{2,6},{3,7},{4,0},{5,1},{6,2},{7,3},{8,12},{9,13},{10,... | collective-permute-start | bytes 1277960 | tf_op jit(solution)/shard_map/ppermute | solution.py:38
  33.1 11.8 %collective-permute-start.11 = (bf16[13,64,128]{2,1,0:T(8,128)(2,1)S(1)}, bf16[13,64,128]{2,1,0:T(8,128)(2,1)S(1)}, u32[]{:S(2)}, u32[]{:S(2)}) collective-permute-start(bf16[13,64,128]{2,1,0:T(8,128)(2,1)S(1)} %collective-permute-done.10.refs_8_), channel_id=1, source_target_pairs={{0,24},{1,25},{2,26},{3,27},{4,28},{5,29},{6,30},{7,31},{8,0},{9,1... | collective-permute-start | bytes 638984 | tf_op jit(solution)/shard_map/ppermute | solution.py:38
  36.3 9.8 %collective-permute-start.14 = (bf16[13,64,128]{2,1,0:T(8,128)(2,1)S(1)}, bf16[13,64,128]{2,1,0:T(8,128)(2,1)S(1)}, u32[]{:S(2)}, u32[]{:S(2)}) collective-permute-start(bf16[13,64,128]{2,1,0:T(8,128)(2,1)S(1)} %collective-permute-done.13.refs_9_), channel_id=1, source_target_pairs={{0,8},{1,9},{2,10},{3,11},{4,12},{5,13},{6,14},{7,15},{8,16},{9,17... | collective-permute-start | bytes 638984 | tf_op jit(solution)/shard_map/ppermute | solution.py:38
  47.2 1.8 %collective-permute-start.15 = (f32[13,64,128]{2,1,0:T(8,128)S(1)}, f32[13,64,128]{2,1,0:T(8,128)S(1)}, u32[]{:S(2)}, u32[]{:S(2)}) collective-permute-start(f32[13,64,128]{2,1,0:T(8,128)S(1)} %far_1_2.1), channel_id=1, source_target_pairs={{0,1},{1,0},{2,3},{3,2},{4,5},{5,4},{6,7},{7,6},{8,9},{9,8},{10,11... | collective-permute-start | bytes 1277960 | tf_op jit(solution)/shard_map/ppermute | solution.py:38

commit v20 on v18

--- a/solution.py
+++ b/solution.py
@@ -533,30 +533,29 @@
     line = along_z(shared, 1)
     from_x, from_y = over_x(shared), over_y(shared)
     filled = near_field(list(range(1, cut)), *near_args, ordered)
-    line = after(line, filled[0])
+    cross = lax.ppermute(
+        cross,
+        "subtree",
+        [(d, d + 1) for d in range(1, count - 1, 2)] + [(d, d - 1) for d in range(2, count, 2)],
+    )
+    line = after(line, filled[0], cross)
     lines = [along_z(shared, layers - 1)]
     for _ in range(layers - 3):
         lines.append(along_z(line if len(lines) == 1 else lines[-1], 1))
     ready = after(line, from_x, from_y)
     next_x, next_y = over_x(ready), over_y(ready)
     far = onward(choose(me, after(from_x, ready, lines[0]), from_y))
-    cross = lax.ppermute(
-        cross,
-        "subtree",
-        [(d, d + 1) for d in range(1, count - 1, 2)] + [(d, d - 1) for d in range(2, count, 2)],
-    )
     own_blocks, my_other, turned_transfer = dense_couplings(
         after(entry, ready), own_at, inner, coupling, top_coupling, transfer, slots
     )
 
-    joined = after(join([after(lines[0], my_other)] + lines[1:]), next_x, next_y, cross)
+    joined = after(join([after(lines[0], my_other)] + lines[1:]), next_x, next_y)
     last_x, last_y = over_x(joined), over_y(joined)
     chosen = choose(me, after(next_x, joined, far), next_y)
     next_far = onward(chosen)
     other_blocks = over_core(after(my_other, chosen))
     held = after(ordered, joined)
     filled = near_field(list(range(cut, pairs - 1)), *near_args, held, filled=filled)
-    next_far = after(next_far, filled[0])
     last_far = [along_z(far, layers - 1)]
     for _ in range(layers - 3):
         last_far.append(along_z(next_far if len(last_far) == 1 else last_far[-1], 1))

time: 51.4 us -> 52.3 us (1.018)
  waiting for transfers between devices: 5.68 us -> 7.28 us
  starting transfers between devices: 25 us -> 24.3 us
    ppermute x15, waiting for transfers between devices: 5.68 us -> 7.28 us  [send(): lax.ppermute(block, 'subtree', [(d, target(d)) for d in range(count)])]
    ppermute x15, starting transfers between devices: 24.3 us -> 23.6 us  [send(): lax.ppermute(block, 'subtree', [(d, target(d)) for d in range(count)])]
  transfers between devices with their start and end apart: 16 -> 16, of which waited for: 4 -> 6; matrix products, arithmetic and copies ran while one was open for 0% -> 0% of each run, Pallas kernels for 25% -> 25%
where the time goes in v20:
time: 52.3 us; the launch traced here: 52.2 us
  starting transfers between devices  24.3 us (46%)
  Pallas kernels  20.4 us (39%)
  waiting for transfers between devices  7.28 us (14%)
    ppermute x15, starting transfers between devices, send(): lax.ppermute(block, 'subtree', [(d, target(d)) for d in range(count)])  23.6 us
    ppermute x15, waiting for transfers between devices, send(): lax.ppermute(block, 'subtree', [(d, target(d)) for d in range(count)])  7.28 us
    pallas_call x3, Pallas kernels, near_field(): pl.pallas_call(functools.partial(near_kernel, halos is not None, tuple(pa...  6.71 us
    pallas_call x1, Pallas kernels, skeletons_of(): pl.pallas_call(functools.partial(skeleton_kernel, per, layers), name='ord...  4.29 us
    pallas_call x3, Pallas kernels, far_rounds(): pl.pallas_call(functools.partial(round_kernel, planes, steps, slots, [len...  3.66 us
    pallas_call x1, Pallas kernels, dense_couplings(): pl.pallas_call(functools.partial(dense_kernel, per, slots), name='couplin...  3.47 us
    pallas_call x1, Pallas kernels, field(): pl.pallas_call(functools.partial(field_kernel, per), name='local_and_fiel...  2.2 us
  transfers between devices with their start and end apart: 16, of which 6 were waited for; matrix products, arithmetic and copies ran while one was open for 0% of the time, Pallas kernels for 25%

profile of v20, /device:TPU:0, one launch (start us, length us, event | category | flops | bytes accessed | tf_op | source)
XLA Modules:
  0.0 52.2 jit_solution(14721197198426574746)
XLA Ops:
  0.0 4.3 %order_and_skeleton.1 = (bf16[6144,128]{1,0:T(8,128)(2,1)S(1)}, bf16[13,64,128]{2,1,0:T(8,128)(2,1)S(1)}, bf16[512,128]{1,0:T(8,128)(2,1)S(1)}, bf16[512,128]{1,...) custom-call(s32[1]{0:T(128)} %bitcast.me_ref.refs_0_, s32[12,512]{1,0:T(8,128)} %order_ref.7, ...), custom_call_target="tpu_custom_call" | custom-call | flops 12582912 | bytes 65536 | tf_op jit(solution)/shard_map/order_and_skeleton/pallas_call | solution.py:192
  4.3 3.1 %collective-permute-start.1 = (bf16[13,64,128]{2,1,0:T(8,128)(2,1)S(1)}, bf16[13,64,128]{2,1,0:T(8,128)(2,1)S(1)}, u32[]{:S(2)}, u32[]{:S(2)}) collective-permute-start(bf16[13,64,128]{2,1,0:T(8,128)(2,1)S(1)} %get-tuple-element.35.refs_2_), channel_id=1, source_target_pairs={{0,8},{1,9},{2,10},{3,11},{4,12},{5,13},{6,14},{7,15},{8,16},{9,17... | collective-permute-start | bytes 638984 | tf_op jit(solution)/shard_map/ppermute | solution.py:38
  7.4 1.5 %collective-permute-start.3 = (bf16[13,64,128]{2,1,0:T(8,128)(2,1)S(1)}, bf16[13,64,128]{2,1,0:T(8,128)(2,1)S(1)}, u32[]{:S(2)}, u32[]{:S(2)}) collective-permute-start(bf16[13,64,128]{2,1,0:T(8,128)(2,1)S(1)} %get-tuple-element.35.refs_2_), channel_id=1, source_target_pairs={{0,2},{1,3},{2,0},{3,1},{4,6},{5,7},{6,4},{7,5},{8,10},{9,11},{10,... | collective-permute-start | bytes 638984 | tf_op jit(solution)/shard_map/ppermute | solution.py:38
  8.9 1.5 %collective-permute-start.4 = (bf16[13,64,128]{2,1,0:T(8,128)(2,1)S(1)}, bf16[13,64,128]{2,1,0:T(8,128)(2,1)S(1)}, u32[]{:S(2)}, u32[]{:S(2)}) collective-permute-start(bf16[13,64,128]{2,1,0:T(8,128)(2,1)S(1)} %get-tuple-element.35.refs_2_), channel_id=1, source_target_pairs={{0,4},{1,5},{2,6},{3,7},{4,0},{5,1},{6,2},{7,3},{8,12},{9,13},{10,... | collective-permute-start | bytes 638984 | tf_op jit(solution)/shard_map/ppermute | solution.py:38
  10.4 2.2 %collective-permute-start = (bf16[13,64,128]{2,1,0:T(8,128)(2,1)S(1)}, bf16[13,64,128]{2,1,0:T(8,128)(2,1)S(1)}, u32[]{:S(2)}, u32[]{:S(2)}) collective-permute-start(bf16[13,64,128]{2,1,0:T(8,128)(2,1)S(1)} %get-tuple-element.35.refs_2_), channel_id=1, source_target_pairs={{0,24},{1,25},{2,26},{3,27},{4,28},{5,29},{6,30},{7,31},{8,0},{9,1... | collective-permute-start | bytes 638984 | tf_op jit(solution)/shard_map/ppermute | solution.py:38
  12.7 0.7 %collective-permute-start.2 = (bf16[512,128]{1,0:T(8,128)(2,1)S(1)}, bf16[512,128]{1,0:T(8,128)(2,1)S(1)}, u32[]{:S(2)}, u32[]{:S(2)}) collective-permute-start(bf16[512,128]{1,0:T(8,128)(2,1)S(1)} %get-tuple-element.39), channel_id=1, source_target_pairs={{1,2},{3,4},{5,6},{7,8},{9,10},{11,12},{13,14},{15,16},{17,18},{19... | collective-permute-start | bytes 393224 | tf_op jit(solution)/shard_map/ppermute | solution.py:536
  13.4 2.2 %near_1.1 = (bf16[6144,128]{1,0:T(8,128)(2,1)S(1)}, bf16[3072,128]{1,0:T(8,128)(2,1)S(1)}) custom-call(s32[2,12]{1,0:T(2,128)S(1)} %bitcast.2, s32[12,512]{1,0:T(8,128)S(1)} %copy-done.2, bf16[512,1536]{1,0:T(8,128)(2,1)S(1)} %copy-done, bf16[12,64,512]{2,1,0:T(8,128)(2,1)S(1)} %copy-done.1, bf16[6144,128]{1,0:T(8,128)(2,1)S(1)} %get-tuple-element.51.ordered_ref), custom_call_target="tpu_custom_call" | custom-call | flops 20971520 | bytes 32768 | tf_op jit(solution)/shard_map/near_1/pallas_call | solution.py:444
  15.6 6.7 %collective-permute-start.5 = (bf16[13,64,128]{2,1,0:T(8,128)(2,1)S(1)}, bf16[13,64,128]{2,1,0:T(8,128)(2,1)S(1)}, u32[]{:S(2)}, u32[]{:S(2)}) collective-permute-start(bf16[13,64,128]{2,1,0:T(8,128)(2,1)S(1)} %collective-permute-done.1.refs_3_), channel_id=1, source_target_pairs={{0,8},{1,9},{2,10},{3,11},{4,12},{5,13},{6,14},{7,15},{8,16},{9,17... | collective-permute-start | bytes 638984 | tf_op jit(solution)/shard_map/ppermute | solution.py:38
  22.4 2.1 %collective-permute-start.10 = (bf16[13,64,128]{2,1,0:T(8,128)(2,1)S(1)}, bf16[13,64,128]{2,1,0:T(8,128)(2,1)S(1)}, u32[]{:S(2)}, u32[]{:S(2)}) collective-permute-start(bf16[13,64,128]{2,1,0:T(8,128)(2,1)S(1)} %choose.2), channel_id=1, source_target_pairs={{0,4},{1,3},{2,6},{3,1},{4,0},{5,7},{6,2},{7,5},{8,12},{9,11},{10,... | collective-permute-start | bytes 638984 | tf_op jit(solution)/shard_map/ppermute | solution.py:38
  24.5 3.5 %couplings_by_owner.1 = (bf16[13,64,1024]{2,1,0:T(8,128)(2,1)S(1)}, bf16[15,64,1024]{2,1,0:T(8,128)(2,1)S(1)}, bf16[12,64,64]{2,1,0:T(8,128)(2,1)S(1)}) custom-call(s32[16,128]{1,0:T(8,128)S(1)} %get-tuple-element.42.entry_ref, s32[16,128]{1,0:T(8,128)S(1)} %get-tuple-element.34.block_ref.refs_0_, bf16[512,128]{1,0:T(8,128)(2,1)S(1)} %get-tuple-element.43.inner_ref, ...), custom_call_target="tpu_custom_call" | custom-call | bytes 131072 | tf_op jit(solution)/shard_map/couplings_by_owner/pallas_call | solution.py:306
  28.1 2.2 %collective-permute-done.6.x_ref.refs_5_ = bf16[13,64,128]{2,1,0:T(8,128)(2,1)S(1)} collective-permute-done((bf16[13,64,128]{2,1,0:T(8,128)(2,1)S(1)}, bf16[13,64,128]{2,1,0:T(8,128)(2,1)S(1)}, u32[]{:S(2)}, u32[]{:S(2)}) %collective-permute-start.6) | collective-permute-done | bytes 213024 | tf_op jit(solution)/shard_map/ppermute | solution.py:38
  30.4 0.7 %collective-permute-done.10.refs_8_ = bf16[13,64,128]{2,1,0:T(8,128)(2,1)S(1)} collective-permute-done((bf16[13,64,128]{2,1,0:T(8,128)(2,1)S(1)}, bf16[13,64,128]{2,1,0:T(8,128)(2,1)S(1)}, u32[]{:S(2)}, u32[]{:S(2)}) %collective-permute-start.10) | collective-permute-done | bytes 213024 | tf_op jit(solution)/shard_map/ppermute | solution.py:38
  31.2 1.7 %collective-permute-start.13 = (bf16[13,64,128]{2,1,0:T(8,128)(2,1)S(1)}, bf16[13,64,128]{2,1,0:T(8,128)(2,1)S(1)}, u32[]{:S(2)}, u32[]{:S(2)}) collective-permute-start(bf16[13,64,128]{2,1,0:T(8,128)(2,1)S(1)} %choose.3), channel_id=1, source_target_pairs={{0,4},{1,3},{2,6},{3,1},{4,0},{5,7},{6,2},{7,5},{8,12},{9,11},{10,... | collective-permute-start | bytes 638984 | tf_op jit(solution)/shard_map/ppermute | solution.py:38
  33.4 1.3 %collective-permute-start.9 = (bf16[26,64,128]{2,1,0:T(8,128)(2,1)S(1)}, bf16[26,64,128]{2,1,0:T(8,128)(2,1)S(1)}, u32[]{:S(2)}, u32[]{:S(2)}) collective-permute-start(bf16[26,64,128]{2,1,0:T(8,128)(2,1)S(1)} %join.1.refs_1_), channel_id=1, source_target_pairs={{0,4},{1,5},{2,6},{3,7},{4,0},{5,1},{6,2},{7,3},{8,12},{9,13},{10,... | collective-permute-start | bytes 1277960 | tf_op jit(solution)/shard_map/ppermute | solution.py:38
  34.7 2.3 %collective-permute-start.11 = (bf16[13,64,128]{2,1,0:T(8,128)(2,1)S(1)}, bf16[13,64,128]{2,1,0:T(8,128)(2,1)S(1)}, u32[]{:S(2)}, u32[]{:S(2)}) collective-permute-start(bf16[13,64,128]{2,1,0:T(8,128)(2,1)S(1)} %collective-permute-done.10.refs_8_), channel_id=1, source_target_pairs={{0,24},{1,25},{2,26},{3,27},{4,28},{5,29},{6,30},{7,31},{8,0},{9,1... | collective-permute-start | bytes 638984 | tf_op jit(solution)/shard_map/ppermute | solution.py:38
  36.9 1.6 %collective-permute-done.13.refs_9_ = bf16[13,64,128]{2,1,0:T(8,128)(2,1)S(1)} collective-permute-done((bf16[13,64,128]{2,1,0:T(8,128)(2,1)S(1)}, bf16[13,64,128]{2,1,0:T(8,128)(2,1)S(1)}, u32[]{:S(2)}, u32[]{:S(2)}) %collective-permute-start.13) | collective-permute-done | bytes 213024 | tf_op jit(solution)/shard_map/ppermute | solution.py:38
  39.1 2.2 %near_3.1 = (bf16[6144,128]{1,0:T(8,128)(2,1)S(1)}, bf16[3072,128]{1,0:T(8,128)(2,1)S(1)}) custom-call(s32[2,12]{1,0:T(2,128)S(1)} %bitcast.3, s32[12,512]{1,0:T(8,128)S(1)} %copy-done.2, bf16[512,1536]{1,0:T(8,128)(2,1)S(1)} %copy-done, bf16[12,64,512]{2,1,0:T(8,128)(2,1)S(1)} %copy-done.1, ...), custom_call_target="tpu_custom_call", output_to_operand_aliasing={{0}: (5, {}), {1}: (6, {})} | custom-call | flops 20971520 | bytes 32768 | tf_op jit(solution)/shard_map/near_3/pallas_call | solution.py:444
  41.4 2.2 %near_0.1 = (bf16[6144,128]{1,0:T(8,128)(2,1)S(1)}, bf16[3072,128]{1,0:T(8,128)(2,1)S(1)}, s32[16,128]{1,0:T(8,128)S(1)}) custom-call(s32[2,12]{1,0:T(2,128)S(1)} %bitcast.4, s32[12,512]{1,0:T(8,128)S(1)} %copy-done.2, bf16[512,1536]{1,0:T(8,128)(2,1)S(1)} %copy-done, ...), custom_call_target="tpu_custom_call", output_to_operand_aliasing={{0}: (8, {}), {1}: (9, {})} | custom-call | flops 20971520 | bytes 32768 | tf_op jit(solution)/shard_map/near_0/pallas_call | solution.py:444
  43.6 1.5 %far_1_0.1 = (f32[13,64,128]{2,1,0:T(8,128)S(1)}, f32[13,64,128]{2,1,0:T(8,128)S(1)}) custom-call(s32[16,128]{1,0:T(8,128)S(1)} %get-tuple-element.34.block_ref.refs_0_, s32[16,128]{1,0:T(8,128)S(1)} %get-tuple-element.55.refs_1_.refs_0_, bf16[13,64,128]{2,1,0:T(8,128)(2,1)S(1)} %get-tuple-element.35.refs_2_, ...), custom_call_target="tpu_custom_call" | custom-call | flops 1703936 | bytes 16384 | tf_op jit(solution)/shard_map/far_1_0/pallas_call | solution.py:366
  45.1 1.9 %collective-permute-done.14.refs_5_ = bf16[13,64,128]{2,1,0:T(8,128)(2,1)S(1)} collective-permute-done((bf16[13,64,128]{2,1,0:T(8,128)(2,1)S(1)}, bf16[13,64,128]{2,1,0:T(8,128)(2,1)S(1)}, u32[]{:S(2)}, u32[]{:S(2)}) %collective-permute-start.14) | collective-permute-done | bytes 213024 | tf_op jit(solution)/shard_map/ppermute | solution.py:38
  47.1 1.1 %far_1_2.1 = f32[13,64,128]{2,1,0:T(8,128)S(1)} custom-call(s32[16,128]{1,0:T(8,128)S(1)} %get-tuple-element.55.refs_1_.refs_0_, bf16[26,64,128]{2,1,0:T(8,128)(2,1)S(1)} %join.1.refs_1_, bf16[26,64,128]{2,1,0:T(8,128)(2,1)S(1)} %collective-permute-done.8.refs_2_, bf16[26,64,128]{2,1,0:T(8,128)(2,1)S(1)} %collective-permute-done.9.refs_3_, ...), custom_call_target="tpu_custom_call" | custom-call | flops 1703936 | bytes 16384 | tf_op jit(solution)/shard_map/far_1_2/pallas_call | solution.py:366
  48.2 1.1 %far_0_2.1.own_ref = f32[13,64,128]{2,1,0:T(8,128)S(1)} custom-call(s32[16,128]{1,0:T(8,128)S(1)} %get-tuple-element.34.block_ref.refs_0_, bf16[26,64,128]{2,1,0:T(8,128)(2,1)S(1)} %join.1.refs_1_, bf16[26,64,128]{2,1,0:T(8,128)(2,1)S(1)} %collective-permute-done.8.refs_2_, bf16[26,64,128]{2,1,0:T(8,128)(2,1)S(1)} %collective-permute-done.9.refs_3_, ...), custom_call_target="tpu_custom_call" | custom-call | flops 1703936 | bytes 16384 | tf_op jit(solution)/shard_map/far_0_2/pallas_call | solution.py:366
  49.3 0.7 %collective-permute-done.15.other_ref = f32[13,64,128]{2,1,0:T(8,128)S(1)} collective-permute-done((f32[13,64,128]{2,1,0:T(8,128)S(1)}, f32[13,64,128]{2,1,0:T(8,128)S(1)}, u32[]{:S(2)}, u32[]{:S(2)}) %collective-permute-start.15) | collective-permute-done | bytes 426016 | tf_op jit(solution)/shard_map/ppermute | solution.py:38
  50.0 2.2 %local_and_field.1 = bf16[6144,128]{1,0:T(8,128)(2,1)} custom-call(f32[13,64,128]{2,1,0:T(8,128)S(1)} %far_0_2.1.own_ref, f32[13,64,128]{2,1,0:T(8,128)S(1)} %collective-permute-done.15.other_ref, bf16[12,64,64]{2,1,0:T(8,128)(2,1)S(1)} %get-tuple-element.60.turned_transfer_ref, bf16[6144,128]{1,0:T(8,128)(2,1)S(1)} %get-tuple-element.61.near_ref, ...), custom_call_target="tpu_custom_call" | custom-call | flops 1572864 | bytes 65536 | tf_op jit(solution)/shard_map/local_and_field/pallas_call | solution.py:492
  (28 shorter events, 1.5 us)
Async XLA Ops:
  0.0 13.3 %copy-start = (bf16[512,1536]{1,0:T(8,128)(2,1)S(1)}, bf16[512,1536]{1,0:T(8,128)(2,1)}, u32[]{:S(2)}) copy-start(bf16[512,1536]{1,0:T(8,128)(2,1)} %constant.6.clone.table_ref) | copy-start | bytes 4718596
  0.0 13.3 %copy-start.1 = (bf16[12,64,512]{2,1,0:T(8,128)(2,1)S(1)}, bf16[12,64,512]{2,1,0:T(8,128)(2,1)}, u32[]{:S(2)}) copy-start(bf16[12,64,512]{2,1,0:T(8,128)(2,1)} %basis_ref.7) | copy-start | bytes 2359300
  0.0 13.3 %copy-start.2 = (s32[12,512]{1,0:T(8,128)S(1)}, s32[12,512]{1,0:T(8,128)}, u32[]{:S(2)}) copy-start(s32[12,512]{1,0:T(8,128)} %order_ref.7) | copy-start | bytes 73732
  0.0 13.4 %copy-start.3 = (s32[12,2]{0,1:T(2,128)S(1)}, s32[12,2]{0,1:T(2,128)}, u32[]{:S(2)}) copy-start(s32[12,2]{0,1:T(2,128)} %param.17) | copy-start | bytes 292
  4.3 11.3 %collective-permute-start.1 = (bf16[13,64,128]{2,1,0:T(8,128)(2,1)S(1)}, bf16[13,64,128]{2,1,0:T(8,128)(2,1)S(1)}, u32[]{:S(2)}, u32[]{:S(2)}) collective-permute-start(bf16[13,64,128]{2,1,0:T(8,128)(2,1)S(1)} %get-tuple-element.35.refs_2_), channel_id=1, source_target_pairs={{0,8},{1,9},{2,10},{3,11},{4,12},{5,13},{6,14},{7,15},{8,16},{9,17... | collective-permute-start | bytes 638984 | tf_op jit(solution)/shard_map/ppermute | solution.py:38
  7.4 14.9 %collective-permute-start.3 = (bf16[13,64,128]{2,1,0:T(8,128)(2,1)S(1)}, bf16[13,64,128]{2,1,0:T(8,128)(2,1)S(1)}, u32[]{:S(2)}, u32[]{:S(2)}) collective-permute-start(bf16[13,64,128]{2,1,0:T(8,128)(2,1)S(1)} %get-tuple-element.35.refs_2_), channel_id=1, source_target_pairs={{0,2},{1,3},{2,0},{3,1},{4,6},{5,7},{6,4},{7,5},{8,10},{9,11},{10,... | collective-permute-start | bytes 638984 | tf_op jit(solution)/shard_map/ppermute | solution.py:38
  8.9 13.4 %collective-permute-start.4 = (bf16[13,64,128]{2,1,0:T(8,128)(2,1)S(1)}, bf16[13,64,128]{2,1,0:T(8,128)(2,1)S(1)}, u32[]{:S(2)}, u32[]{:S(2)}) collective-permute-start(bf16[13,64,128]{2,1,0:T(8,128)(2,1)S(1)} %get-tuple-element.35.refs_2_), channel_id=1, source_target_pairs={{0,4},{1,5},{2,6},{3,7},{4,0},{5,1},{6,2},{7,3},{8,12},{9,13},{10,... | collective-permute-start | bytes 638984 | tf_op jit(solution)/shard_map/ppermute | solution.py:38
  10.4 12.0 %collective-permute-start = (bf16[13,64,128]{2,1,0:T(8,128)(2,1)S(1)}, bf16[13,64,128]{2,1,0:T(8,128)(2,1)S(1)}, u32[]{:S(2)}, u32[]{:S(2)}) collective-permute-start(bf16[13,64,128]{2,1,0:T(8,128)(2,1)S(1)} %get-tuple-element.35.refs_2_), channel_id=1, source_target_pairs={{0,24},{1,25},{2,26},{3,27},{4,28},{5,29},{6,30},{7,31},{8,0},{9,1... | collective-permute-start | bytes 638984 | tf_op jit(solution)/shard_map/ppermute | solution.py:38
  12.7 2.9 %collective-permute-start.2 = (bf16[512,128]{1,0:T(8,128)(2,1)S(1)}, bf16[512,128]{1,0:T(8,128)(2,1)S(1)}, u32[]{:S(2)}, u32[]{:S(2)}) collective-permute-start(bf16[512,128]{1,0:T(8,128)(2,1)S(1)} %get-tuple-element.39), channel_id=1, source_target_pairs={{1,2},{3,4},{5,6},{7,8},{9,10},{11,12},{13,14},{15,16},{17,18},{19... | collective-permute-start | bytes 393224 | tf_op jit(solution)/shard_map/ppermute | solution.py:536
  15.6 12.5 %collective-permute-start.5 = (bf16[13,64,128]{2,1,0:T(8,128)(2,1)S(1)}, bf16[13,64,128]{2,1,0:T(8,128)(2,1)S(1)}, u32[]{:S(2)}, u32[]{:S(2)}) collective-permute-start(bf16[13,64,128]{2,1,0:T(8,128)(2,1)S(1)} %collective-permute-done.1.refs_3_), channel_id=1, source_target_pairs={{0,8},{1,9},{2,10},{3,11},{4,12},{5,13},{6,14},{7,15},{8,16},{9,17... | collective-permute-start | bytes 638984 | tf_op jit(solution)/shard_map/ppermute | solution.py:38
  22.3 8.1 %collective-permute-start.6 = (bf16[13,64,128]{2,1,0:T(8,128)(2,1)S(1)}, bf16[13,64,128]{2,1,0:T(8,128)(2,1)S(1)}, u32[]{:S(2)}, u32[]{:S(2)}) collective-permute-start(bf16[13,64,128]{2,1,0:T(8,128)(2,1)S(1)} %collective-permute-done.1.refs_3_), channel_id=1, source_target_pairs={{0,2},{1,3},{2,0},{3,1},{4,6},{5,7},{6,4},{7,5},{8,10},{9,11},{10,... | collective-permute-start | bytes 638984 | tf_op jit(solution)/shard_map/ppermute | solution.py:38
  22.3 8.1 %collective-permute-start.7 = (bf16[13,64,128]{2,1,0:T(8,128)(2,1)S(1)}, bf16[13,64,128]{2,1,0:T(8,128)(2,1)S(1)}, u32[]{:S(2)}, u32[]{:S(2)}) collective-permute-start(bf16[13,64,128]{2,1,0:T(8,128)(2,1)S(1)} %collective-permute-done.1.refs_3_), channel_id=1, source_target_pairs={{0,4},{1,5},{2,6},{3,7},{4,0},{5,1},{6,2},{7,3},{8,12},{9,13},{10,... | collective-permute-start | bytes 638984 | tf_op jit(solution)/shard_map/ppermute | solution.py:38
  22.4 8.7 %collective-permute-start.10 = (bf16[13,64,128]{2,1,0:T(8,128)(2,1)S(1)}, bf16[13,64,128]{2,1,0:T(8,128)(2,1)S(1)}, u32[]{:S(2)}, u32[]{:S(2)}) collective-permute-start(bf16[13,64,128]{2,1,0:T(8,128)(2,1)S(1)} %choose.2), channel_id=1, source_target_pairs={{0,4},{1,3},{2,6},{3,1},{4,0},{5,7},{6,2},{7,5},{8,12},{9,11},{10,... | collective-permute-start | bytes 638984 | tf_op jit(solution)/shard_map/ppermute | solution.py:38
  31.1 10.2 %collective-permute-start.12 = (bf16[15,64,1024]{2,1,0:T(8,128)(2,1)S(1)}, bf16[15,64,1024]{2,1,0:T(8,128)(2,1)S(1)}, u32[]{:S(2)}, u32[]{:S(2)}) collective-permute-start(bf16[15,64,1024]{2,1,0:T(8,128)(2,1)S(1)} %get-tuple-element.53), channel_id=1, source_target_pairs={{0,1},{1,0},{2,3},{3,2},{4,5},{5,4},{6,7},{7,6},{8,9},{9,8},{10,11... | collective-permute-start | bytes 5898248 | tf_op jit(solution)/shard_map/ppermute | solution.py:38
  31.2 7.3 %collective-permute-start.13 = (bf16[13,64,128]{2,1,0:T(8,128)(2,1)S(1)}, bf16[13,64,128]{2,1,0:T(8,128)(2,1)S(1)}, u32[]{:S(2)}, u32[]{:S(2)}) collective-permute-start(bf16[13,64,128]{2,1,0:T(8,128)(2,1)S(1)} %choose.3), channel_id=1, source_target_pairs={{0,4},{1,3},{2,6},{3,1},{4,0},{5,7},{6,2},{7,5},{8,12},{9,11},{10,... | collective-permute-start | bytes 638984 | tf_op jit(solution)/shard_map/ppermute | solution.py:38
  33.0 14.1 %collective-permute-start.8 = (bf16[26,64,128]{2,1,0:T(8,128)(2,1)S(1)}, bf16[26,64,128]{2,1,0:T(8,128)(2,1)S(1)}, u32[]{:S(2)}, u32[]{:S(2)}) collective-permute-start(bf16[26,64,128]{2,1,0:T(8,128)(2,1)S(1)} %join.1.refs_1_), channel_id=1, source_target_pairs={{0,2},{1,3},{2,0},{3,1},{4,6},{5,7},{6,4},{7,5},{8,10},{9,11},{10,... | collective-permute-start | bytes 1277960 | tf_op jit(solution)/shard_map/ppermute | solution.py:38
  33.4 13.7 %collective-permute-start.9 = (bf16[26,64,128]{2,1,0:T(8,128)(2,1)S(1)}, bf16[26,64,128]{2,1,0:T(8,128)(2,1)S(1)}, u32[]{:S(2)}, u32[]{:S(2)}) collective-permute-start(bf16[26,64,128]{2,1,0:T(8,128)(2,1)S(1)} %join.1.refs_1_), channel_id=1, source_target_pairs={{0,4},{1,5},{2,6},{3,7},{4,0},{5,1},{6,2},{7,3},{8,12},{9,13},{10,... | collective-permute-start | bytes 1277960 | tf_op jit(solution)/shard_map/ppermute | solution.py:38
  34.7 10.4 %collective-permute-start.11 = (bf16[13,64,128]{2,1,0:T(8,128)(2,1)S(1)}, bf16[13,64,128]{2,1,0:T(8,128)(2,1)S(1)}, u32[]{:S(2)}, u32[]{:S(2)}) collective-permute-start(bf16[13,64,128]{2,1,0:T(8,128)(2,1)S(1)} %collective-permute-done.10.refs_8_), channel_id=1, source_target_pairs={{0,24},{1,25},{2,26},{3,27},{4,28},{5,29},{6,30},{7,31},{8,0},{9,1... | collective-permute-start | bytes 638984 | tf_op jit(solution)/shard_map/ppermute | solution.py:38
  38.5 8.6 %collective-permute-start.14 = (bf16[13,64,128]{2,1,0:T(8,128)(2,1)S(1)}, bf16[13,64,128]{2,1,0:T(8,128)(2,1)S(1)}, u32[]{:S(2)}, u32[]{:S(2)}) collective-permute-start(bf16[13,64,128]{2,1,0:T(8,128)(2,1)S(1)} %collective-permute-done.13.refs_9_), channel_id=1, source_target_pairs={{0,8},{1,9},{2,10},{3,11},{4,12},{5,13},{6,14},{7,15},{8,16},{9,17... | collective-permute-start | bytes 638984 | tf_op jit(solution)/shard_map/ppermute | solution.py:38
  48.2 1.8 %collective-permute-start.15 = (f32[13,64,128]{2,1,0:T(8,128)S(1)}, f32[13,64,128]{2,1,0:T(8,128)S(1)}, u32[]{:S(2)}, u32[]{:S(2)}) collective-permute-start(f32[13,64,128]{2,1,0:T(8,128)S(1)} %far_1_2.1), channel_id=1, source_target_pairs={{0,1},{1,0},{2,3},{3,2},{4,5},{5,4},{6,7},{7,6},{8,9},{9,8},{10,11... | collective-permute-start | bytes 1277960 | tf_op jit(solution)/shard_map/ppermute | solution.py:38
